TPU v7x, 32 devices: a whole 2x2x4 slice. The times are simulated.
32 devices in a mesh: section: 2 (over y), dp: 16 (over z, x, core).
Axes of the slice: x: 2, y: 2, z: 4, core: 2. Of those that a mesh axis runs over, the one named last changes fastest.
Arguments:
- tokens_in: bfloat16 [2, 1024, 768], P(None, 'dp'), may hold values from -6 to 6
- segment_ids: int32 [2, 1024], P(None, 'dp'), may hold values from 0 to 6, as said below
- out_grad: bfloat16 [2, 1024, 768], P(None, 'dp'), may hold values from -6 to 6
- qkv_weight: bfloat16 [2, 768, 2304], P('section', 'dp'), may hold values from -0.21875 to 0.21875
- attn_out_weight: bfloat16 [2, 768, 768], P('section', 'dp'), may hold values from -1.75 to 1.75
- mlp_in_weight: bfloat16 [2, 768, 2304], P('section', 'dp'), may hold values from -0.21875 to 0.21875
- mlp_out_weight: bfloat16 [2, 1152, 768], P('section', 'dp'), may hold values from -0.1875 to 0.1875
- attn_gain: bfloat16 [2, 768], P('section', 'dp'), may hold values from 0.25 to 1.75
- mlp_gain: bfloat16 [2, 768], P('section', 'dp'), may hold values from 0.25 to 1.75
Outputs:
- layer_outputs: bfloat16 [2, 2, 1024, 768], P('section', None, 'dp')
- input_grads: bfloat16 [2, 2, 1024, 768], P('section', None, 'dp')
- qkv_grad: float32 [2, 768, 2304], P('section', 'dp')
- attn_out_grad: float32 [2, 768, 768], P('section', 'dp')
- mlp_in_grad: float32 [2, 768, 2304], P('section', 'dp')
- mlp_out_grad: float32 [2, 1152, 768], P('section', 'dp')
- attn_gain_grad: float32 [2, 768], P('section', 'dp')
- mlp_gain_grad: float32 [2, 768], P('section', 'dp')
Inputs may be any that keep to these rules, and one draw needn't show every extreme that they name: `segment_ids`: within each sequence of 1024 tokens the numbers start at 0, never fall and rise by exactly one at each document start: 3 starts lie among positions 1 to 62 and 3 among positions 962 to 1023 of the sequence, none elsewhere.
All inputs are finite; a program needn't handle non-finite values.
Results may differ from a plain program's by a relative error of at most 0.024.
Values may be sent and summed in bfloat16 or wider, within the bound.
No kernel may reach another device: no remote copies, remote signals or barrier semaphores. Data moves between devices by JAX's collectives and lax.ppermute only.
A program may use at most 192 MiB of HBM per device.

v0:
```python
import math

import jax
import jax.numpy as jnp
from jax import lax
from jax.experimental import pallas as pl
from jax.experimental.pallas import tpu as pltpu
from jax.sharding import PartitionSpec as P

HEAD_DIM = 64
GROUP = 16
HALF_WIN = 64
LANES = 128
TILE = 256

local_log_base = math.log(10000.0)
global_log_base = math.log(160000.0)
masked_score = -1e30
SCALE = 1.0 / math.sqrt(HEAD_DIM)
BF = jnp.bfloat16
F32 = jnp.float32


def dot(left, right):
    return jnp.dot(left, right, preferred_element_type=F32)


def dot_bt(left, right):
    return lax.dot_general(left, right, (((1,), (1,)), ((), ())), preferred_element_type=F32)


def dot_at(left, right):
    return lax.dot_general(left, right, (((0,), (0,)), ((), ())), preferred_element_type=F32)


def moments(values):
    center = values - jnp.mean(values, -1, keepdims=True)
    scale = lax.rsqrt(jnp.mean(center * center, -1, keepdims=True) + 1e-05)
    return center * scale, scale


def norm_back(grad_out, gain_row, xhat, scale):
    scaled = grad_out * gain_row
    mean_grad = jnp.mean(scaled, -1, keepdims=True)
    mean_dot = jnp.mean(scaled * xhat, -1, keepdims=True)
    return (scaled - mean_grad - xhat * mean_dot) * scale


def angles(positions, log_base):
    half_dim = HEAD_DIM // 2
    fraction = (2 * jnp.arange(half_dim)).astype(F32) / HEAD_DIM
    inverse = jnp.exp(-fraction * log_base)
    table = positions.astype(F32)[:, None] * inverse[None, :]
    cosine, sine = jnp.cos(table), jnp.sin(table)
    none = jnp.zeros_like(sine)
    cosine = jnp.concatenate([cosine, cosine], 1)
    to_first = jnp.concatenate([-sine, none], 1)
    to_second = jnp.concatenate([none, sine], 1)
    return jnp.tile(jnp.stack([cosine, to_first, to_second]), (1, 2, 2))


def on_core(body, outs, args, scratch=()):
    return pl.pallas_call(
        body,
        out_shape=[jax.ShapeDtypeStruct(shape, dtype) for shape, dtype in outs],
        in_specs=[pl.BlockSpec(memory_space=pltpu.VMEM)] * len(args),
        out_specs=[pl.BlockSpec(memory_space=pltpu.VMEM)] * len(outs),
        scratch_shapes=scratch,
        compiler_params=pltpu.CompilerParams(vmem_limit_bytes=48 * 2**20),
    )(*args)


def low_lanes():
    return lax.broadcasted_iota(jnp.int32, (1, LANES), 1) < HEAD_DIM


def swap(chunk):
    return pltpu.roll(chunk, HEAD_DIM, 1)


def chunks_of(rows):
    return [rows[:, c : c + LANES] for c in range(0, rows.shape[1], LANES)]


def rotate(chunk, tables):
    cosine, to_first, to_second = tables
    quarter = HEAD_DIM // 2
    return (
        chunk * cosine
        + pltpu.roll(chunk, LANES - quarter, 1) * to_first
        + pltpu.roll(chunk, quarter, 1) * to_second
    )


def unrotate(chunk, tables):
    cosine, to_first, to_second = tables
    quarter = HEAD_DIM // 2
    return (
        chunk * cosine
        - pltpu.roll(chunk, LANES - quarter, 1) * to_first
        - pltpu.roll(chunk, quarter, 1) * to_second
    )


def low_and_high(chunks):
    swapped = [swap(chunk) for chunk in chunks]
    low = [(swapped if h % 2 else chunks)[h // 2] for h in range(2 * len(chunks))]
    high = [(chunks if h % 2 else swapped)[h // 2] for h in range(2 * len(chunks))]
    return low, high


def targets():
    for d in range(GROUP):
        micro, chip, half = d // 8, d % 8 // 2, d % 2
        yield d, micro, 3 * chip + 2 * half, 3 * chip + 1, half


def pack_folded(chunks, ref, base):
    low, high = low_and_high(chunks)
    first = low_lanes()
    rows = chunks[0].shape[0] // 2
    half, fold = rows // 2, rows * 3 // 4
    for d, micro, own, shared, side in targets():
        start = micro * rows
        part = start + side * half
        upper = jnp.concatenate(
            [high[own][start + fold : start + rows], high[shared][part : part + half]], 0
        )
        ref[d, base : base + fold] = jnp.where(
            first, low[own][start : start + fold], upper
        ).astype(BF)


def pack_pairs(lefts, rights, ref):
    low, high = low_and_high(lefts)[0], low_and_high(rights)[1]
    first = low_lanes()
    rows = lefts[0].shape[0] // 2
    half = rows // 2
    for d, micro, own, shared, side in targets():
        start = micro * rows
        part = start + side * half
        ref[d, 0:rows] = jnp.where(
            first, low[own][start : start + rows], high[own][start : start + rows]
        ).astype(BF)
        ref[d, rows : rows + half] = jnp.where(
            first, low[shared][part : part + half], high[shared][part : part + half]
        ).astype(BF)


def unpack_folded(ref, base, rows):
    first = low_lanes()
    fold = rows * 3 // 4
    low, high = {}, {}
    shared_parts = {}
    for d, micro, own, shared, side in targets():
        block = ref[d, base : base + fold].astype(F32)
        mine = jnp.concatenate([block, swap(block[: rows - fold])], 0)
        if own % 2:
            high[micro, own] = swap(mine)
        else:
            low[micro, own] = mine
        shared_parts[micro, shared, side] = block[rows - fold :]
        if side:
            both = jnp.concatenate([shared_parts[micro, shared, 0], block[rows - fold :]], 0)
            if shared % 2:
                high[micro, shared] = both
            else:
                low[micro, shared] = swap(both)
    heads = GROUP // 4 * 3
    return [
        jnp.concatenate(
            [jnp.where(first, low[m, h], high[m, h + 1]) for m in range(2)], 0
        )
        for h in range(0, heads, 2)
    ]


def unpack_pairs(ref, rows):
    first = low_lanes()
    half = rows // 2
    pairs = {}
    parts = {}
    for d, micro, own, shared, side in targets():
        pairs[micro, own] = ref[d, 0:rows].astype(F32)
        parts[side] = ref[d, rows : rows + half].astype(F32)
        if side:
            pairs[micro, shared] = jnp.concatenate([parts[0], parts[1]], 0)
    heads = GROUP // 4 * 3
    lefts, rights = [], []
    for h in range(0, heads, 2):
        even, odd = [pairs[m, h] for m in range(2)], [pairs[m, h + 1] for m in range(2)]
        lefts.append(
            jnp.concatenate([jnp.where(first, a, swap(b)) for a, b in zip(even, odd)], 0)
        )
        rights.append(
            jnp.concatenate([jnp.where(first, swap(a), b) for a, b in zip(even, odd)], 0)
        )
    return lefts, rights


def mlp_forward(layer_in, attended, gain, wide_ref, out_ref):
    width = layer_in.shape[1]
    inner = wide_ref.shape[1] - width - out_ref.shape[0] * width // wide_ref.shape[0]
    middle = layer_in + dot(attended, wide_ref[:, :width])
    xhat, _ = moments(middle)
    normed = (xhat * gain).astype(BF)
    gate_up = dot(normed, wide_ref[:, width : width + inner])
    gate, up = gate_up[:, : inner // 2], gate_up[:, inner // 2 :]
    cdf = 0.5 * (1.0 + lax.erf(gate * math.sqrt(0.5)))
    mixed = (gate * cdf * up).astype(BF)
    result = (middle + dot(mixed, out_ref[...])).astype(BF)
    return middle, normed, gate, up, mixed, result


def mlp_backward(upstream, middle, gate, up, gain, wide_ref, out_ref):
    width = middle.shape[1]
    inner = 2 * gate.shape[1]
    d_mixed = dot_bt(upstream, out_ref[...])
    cdf = 0.5 * (1.0 + lax.erf(gate * math.sqrt(0.5)))
    density = jnp.exp(-0.5 * gate * gate) * (1.0 / math.sqrt(2.0 * math.pi))
    d_gate = d_mixed * up * (cdf + gate * density)
    d_up = d_mixed * gate * cdf
    d_gate_up = jnp.concatenate([d_gate.astype(BF), d_up.astype(BF)], 1)
    d_normed = dot_bt(d_gate_up, wide_ref[:, width : width + inner])
    xhat, scale = moments(middle)
    gain_grad = jnp.sum(d_normed * xhat, 0, keepdims=True)
    d_middle = upstream.astype(F32) + norm_back(d_normed, gain, xhat, scale)
    d_attn = d_middle.astype(BF)
    d_attended = dot_bt(d_attn, wide_ref[:, :width])
    return d_gate_up, gain_grad, d_middle, d_attn, d_attended


def project(x_ref, gain_ref, first_ref, table_ref, normed_ref):
    width = x_ref.shape[1]
    xhat, _ = moments(x_ref[...].astype(F32))
    normed = (xhat * gain_ref[...]).astype(BF)
    normed_ref[...] = normed
    tables = [table_ref[i] for i in range(3)]
    queries = chunks_of(dot(normed, first_ref[:, :width]))
    keys = chunks_of(dot(normed, first_ref[:, width : 2 * width]))
    values = dot(normed, first_ref[:, 2 * width : 3 * width])
    return [rotate(c, tables) for c in queries], [rotate(c, tables) for c in keys], values


def input_backward(d_middle, d_projected, x_ref, gain_ref, first_ref, grad_ref, gain_out_ref):
    d_normed = dot_bt(d_projected, first_ref[:, : d_projected.shape[1]])
    xhat, scale = moments(x_ref[...].astype(F32))
    gain_out_ref[...] = jnp.sum(d_normed * xhat, 0, keepdims=True)
    grad_ref[...] = (d_middle + norm_back(d_normed, gain_ref[...], xhat, scale)).astype(BF)


def local_project_body(x_ref, gain_ref, first_ref, table_ref, normed_ref, q_ref, kv_ref):
    queries, keys, values = project(x_ref, gain_ref, first_ref, table_ref, normed_ref)
    width = values.shape[1]
    for j, (q, k) in enumerate(zip(queries, keys)):
        q_ref[:, LANES * j : LANES * (j + 1)] = q.astype(BF)
        kv_ref[:, LANES * j : LANES * (j + 1)] = k.astype(BF)
    kv_ref[:, width:] = values.astype(BF)


def two_heads(chunk):
    first = low_lanes()
    wide = chunk.astype(F32)
    return jnp.concatenate([jnp.where(first, wide, 0.0), jnp.where(first, 0.0, wide)], 0)


def pick_heads(rows):
    half = rows.shape[0] // 2
    return jnp.where(low_lanes(), rows[:half], rows[half:])


def local_parts(q_ref, before_ref, own_ref, after_ref):
    rows = q_ref.shape[0] // 2
    width = q_ref.shape[1]
    for micro in range(2):
        for j in range(width // LANES):
            here = slice(micro * rows, (micro + 1) * rows)
            lanes = slice(LANES * j, LANES * (j + 1))
            more = slice(width + LANES * j, width + LANES * (j + 1))
            keys, values = (
                jnp.concatenate([ref[here, part] for ref in (before_ref, own_ref, after_ref)], 0)
                for part in (lanes, more)
            )
            queries = (two_heads(q_ref[here, lanes]) * SCALE).astype(BF)
            yield micro * (width // LANES) + j, micro, here, lanes, more, queries, keys, values


def local_forward_body(q_ref, before_ref, own_ref, after_ref, bias_ref, att_ref, total_ref):
    parts = local_parts(q_ref, before_ref, own_ref, after_ref)
    for index, micro, here, lanes, _, queries, keys, values in parts:
        scores = dot_bt(keys, queries) + bias_ref[micro]
        peak = jnp.max(scores, 0, keepdims=True)
        weights = jnp.exp(scores - peak)
        total = jnp.sum(weights, 0, keepdims=True)
        total_ref[index] = peak + jnp.log(total)
        probs = (weights * (1.0 / total)).astype(BF)
        att_ref[here, lanes] = pick_heads(dot_at(probs, values)).astype(BF)


def local_backward_body(
    q_ref, before_ref, own_ref, after_ref, bias_ref, total_ref, d_ref, table_ref,
    dq_ref, d_own_ref, d_before_ref, d_after_ref,
):
    tables = [table_ref[i] for i in range(3)]
    parts = local_parts(q_ref, before_ref, own_ref, after_ref)
    rows = q_ref.shape[0] // 2
    for index, micro, here, lanes, more, queries, keys, values in parts:
        d_out = two_heads(d_ref[here, lanes]).astype(BF)
        probs = jnp.exp(dot_bt(keys, queries) + bias_ref[micro] - total_ref[index])
        d_probs = dot_bt(values, d_out)
        product = probs * d_probs
        delta = jnp.sum(product, 0, keepdims=True)
        d_scores = (product - probs * delta).astype(BF)
        d_queries = pick_heads(dot_at(d_scores, keys)) * SCALE
        local_tables = [table[here] for table in tables]
        dq_ref[here, lanes] = unrotate(d_queries, local_tables).astype(BF)
        for part, grads in ((lanes, dot(d_scores, queries)), (more, dot(probs.astype(BF), d_out))):
            d_before_ref[here, part] = grads[:rows].astype(BF)
            d_own_ref[here, part] = grads[rows : 2 * rows]
            d_after_ref[here, part] = grads[2 * rows :].astype(BF)


def local_join_body(dq_ref, own_ref, low_ref, high_ref, table_ref, out_ref):
    tables = [table_ref[i] for i in range(3)]
    width = dq_ref.shape[1]
    out_ref[:, :width] = dq_ref[...]
    total = own_ref[...] + low_ref[...].astype(F32) + high_ref[...].astype(F32)
    for j, chunk in enumerate(chunks_of(total[:, :width])):
        start = width + LANES * j
        out_ref[:, start : start + LANES] = unrotate(chunk, tables).astype(BF)
    out_ref[:, 2 * width :] = total[:, width:].astype(BF)


def local_middle_body(
    x_ref, att_ref, gain_ref, wide_ref, w_out_ref, out_ref, normed_ref, mixed_ref, middle_ref, gate_up_ref
):
    middle, normed, gate, up, mixed, result = mlp_forward(
        x_ref[...].astype(F32), att_ref[...], gain_ref[...], wide_ref, w_out_ref
    )
    out_ref[...] = result
    normed_ref[...] = normed
    mixed_ref[...] = mixed
    middle_ref[...] = middle
    half = gate.shape[1]
    gate_up_ref[:, :half] = gate
    gate_up_ref[:, half:] = up


def local_back_middle_body(
    up_ref, middle_ref, gate_up_ref, gain_ref, wide_ref, w_out_ref,
    d_gate_up_ref, gain_out_ref, d_middle_ref, d_attn_ref, d_att_ref,
):
    half = gate_up_ref.shape[1] // 2
    d_gate_up, gain_grad, d_middle, d_attn, d_attended = mlp_backward(
        up_ref[...], middle_ref[...], gate_up_ref[:, :half], gate_up_ref[:, half:],
        gain_ref[...], wide_ref, w_out_ref,
    )
    d_gate_up_ref[...] = d_gate_up
    gain_out_ref[...] = gain_grad
    d_middle_ref[...] = d_middle
    d_attn_ref[...] = d_attn
    d_att_ref[...] = d_attended.astype(BF)


def input_backward_body(
    d_middle_ref, d_proj_ref, x_ref, gain_ref, first_ref, grad_ref, gain_out_ref
):
    input_backward(
        d_middle_ref[...], d_proj_ref[...], x_ref, gain_ref, first_ref, grad_ref, gain_out_ref
    )


def global_project_body(x_ref, gain_ref, first_ref, table_ref, normed_ref, sent_ref):
    queries, keys, values = project(x_ref, gain_ref, first_ref, table_ref, normed_ref)
    pack_pairs(queries, keys, sent_ref)
    pack_folded(chunks_of(values), sent_ref, sent_ref.shape[1] * 2 // 3)


def flat(blocks):
    return blocks.reshape(-1, LANES)


def own_unfolded(ref, base, rows):
    fold = rows * 3 // 4
    block = ref[:, base : base + fold].astype(F32)
    rest = swap(flat(block[:, : rows - fold])).reshape(GROUP, rows - fold, LANES)
    return flat(jnp.concatenate([block, rest], 1))


def shared_unfolded(ref, start, rows):
    return swap(flat(ref[:, start : start + rows // 2].astype(F32)))


def fill_heads(got_ref, other_ref, own_seg_ref, shared_seg_ref, q_scr, k_scr, v_scr):
    rows = got_ref.shape[1] * 4 // 9
    half = rows // 2
    first = low_lanes()
    lane = lax.broadcasted_iota(jnp.int32, (1, LANES), 1) - HEAD_DIM
    own = flat(got_ref[:, 0:rows].astype(F32))
    shared = flat(got_ref[:, rows : rows + half].astype(F32))
    other = flat(other_ref[:, 0:half].astype(F32))
    count = own.shape[0]
    own_hit = lane == own_seg_ref[...]
    shared_hit = lane == shared_seg_ref[...]
    both = jnp.concatenate([shared, other], 0)
    for start, pairs, hit in (
        (0, own, own_hit),
        (count, shared, shared_hit[: count // 2]),
    ):
        marked = jnp.where(hit, 1.0, 0.0)
        q_scr[start : start + pairs.shape[0]] = jnp.where(first, pairs * SCALE, marked).astype(BF)
    for unit, pairs, hit in ((0, own, own_hit), (1, both, shared_hit)):
        marked = jnp.where(hit, 0.0, masked_score)
        k_scr[unit] = jnp.where(first, swap(pairs), marked).astype(BF)
    base = rows + half
    v_scr[0] = jnp.where(first, own_unfolded(got_ref, base, rows), 0.0).astype(BF)
    start = base + rows - rows * 3 // 4
    shared_v = jnp.concatenate(
        [shared_unfolded(got_ref, start, rows), shared_unfolded(other_ref, half, rows)], 0
    )
    v_scr[1] = jnp.where(first, shared_v, 0.0).astype(BF)


def fold_out(own, shared, rows, ref, base):
    fold = rows * 3 // 4
    blocks = own.reshape(GROUP, rows, LANES)
    swapped = swap(own).reshape(GROUP, rows, LANES)
    upper = jnp.concatenate(
        [swapped[:, fold:], swap(shared).reshape(GROUP, rows // 2, LANES)], 1
    )
    ref[:, base : base + fold] = jnp.where(low_lanes(), blocks[:, :fold], upper).astype(BF)


def global_forward_body(
    got_ref, other_ref, own_seg_ref, shared_seg_ref, out_ref, total_ref,
    q_scr, k_scr, v_scr, vt_scr, o_scr,
):
    fill_heads(got_ref, other_ref, own_seg_ref, shared_seg_ref, q_scr, k_scr, v_scr)
    for unit in range(2):
        vt_scr[unit] = v_scr[unit].astype(F32).T.astype(BF)
    count = k_scr.shape[1]

    def step(tile, carry):
        unit = tile // (count // TILE)
        rows = pl.ds(pl.multiple_of(tile * TILE, TILE), TILE)
        scores = dot_bt(k_scr[unit], q_scr[rows])
        peak = jnp.max(scores, 0, keepdims=True)
        weights = jnp.exp(scores - peak)
        total = jnp.sum(weights, 0, keepdims=True)
        total_ref[tile] = peak + jnp.log(total)
        out = dot(vt_scr[unit], weights.astype(BF)) * (1.0 / total)
        o_scr[rows] = out.T
        return carry

    lax.fori_loop(0, q_scr.shape[0] // TILE, step, 0)
    rows = got_ref.shape[1] * 4 // 9
    fold_out(o_scr[:count], o_scr[count:], rows, out_ref, 0)


def global_backward_body(
    got_ref, other_ref, own_seg_ref, shared_seg_ref, total_ref, d_ref, sent_ref, to_other_ref,
    q_scr, k_scr, v_scr, kt_scr, d_scr, dq_scr, dk_scr, dv_scr,
):
    fill_heads(got_ref, other_ref, own_seg_ref, shared_seg_ref, q_scr, k_scr, v_scr)
    first = low_lanes()
    rows = got_ref.shape[1] * 4 // 9
    half = rows // 2
    for unit in range(2):
        keys = jnp.where(first, k_scr[unit].astype(F32), 0.0)
        kt_scr[unit] = keys.T.astype(BF)
    count = k_scr.shape[1]
    d_scr[:count] = jnp.where(first, own_unfolded(d_ref, 0, rows), 0.0).astype(BF)
    d_scr[count:] = jnp.where(
        first, shared_unfolded(d_ref, rows - rows * 3 // 4, rows), 0.0
    ).astype(BF)
    dk_scr[...] = jnp.zeros_like(dk_scr)
    dv_scr[...] = jnp.zeros_like(dv_scr)

    def step(tile, carry):
        unit = tile // (count // TILE)
        here = pl.ds(pl.multiple_of(tile * TILE, TILE), TILE)
        queries, d_out = q_scr[here], d_scr[here]
        probs = jnp.exp(dot_bt(k_scr[unit], queries) - total_ref[tile])
        d_probs = dot_bt(v_scr[unit], d_out)
        product = probs * d_probs
        delta = jnp.sum(product, 0, keepdims=True)
        d_scores = (product - probs * delta).astype(BF)
        dv_scr[unit] += dot(probs.astype(BF), d_out)
        dk_scr[unit] += dot(d_scores, queries)
        dq_scr[here] = dot(kt_scr[unit], d_scores).T * SCALE
        return carry

    lax.fori_loop(0, q_scr.shape[0] // TILE, step, 0)
    mine = count // 2
    own = jnp.where(first, dq_scr[:count], swap(dk_scr[0]))
    sent_ref[:, 0:rows] = own.reshape(GROUP, rows, LANES).astype(BF)
    shared_k, shared_v = dk_scr[1], dv_scr[1]
    shared = jnp.where(first, dq_scr[count:], swap(shared_k[:mine]))
    sent_ref[:, rows : rows + half] = shared.reshape(GROUP, half, LANES).astype(BF)
    fold_out(dv_scr[0], shared_v[:mine], rows, sent_ref, rows + half)
    for place, grads in enumerate((shared_k, shared_v)):
        other = jnp.where(first, 0.0, swap(grads[mine:])).reshape(GROUP, half, LANES)
        to_other_ref[:, place * half : (place + 1) * half] = other.astype(BF)


def global_middle_body(
    got_ref, x_ref, up_ref, gain_ref, wide_ref, w_out_ref,
    out_ref, att_ref, normed_ref, mixed_ref, d_gate_up_ref, gain_out_ref, d_middle_ref, d_attn_ref, sent_ref,
):
    rows = x_ref.shape[0] // 2
    attended = jnp.concatenate([c.astype(BF) for c in unpack_folded(got_ref, 0, rows)], 1)
    att_ref[...] = attended
    gain = gain_ref[...]
    middle, normed, gate, up, mixed, result = mlp_forward(
        x_ref[...].astype(F32), attended, gain, wide_ref, w_out_ref
    )
    out_ref[...] = result
    normed_ref[...] = normed
    mixed_ref[...] = mixed
    d_gate_up, gain_grad, d_middle, d_attn, d_attended = mlp_backward(
        up_ref[...], middle, gate, up, gain, wide_ref, w_out_ref
    )
    d_gate_up_ref[...] = d_gate_up
    gain_out_ref[...] = gain_grad
    d_middle_ref[...] = d_middle
    d_attn_ref[...] = d_attn
    pack_folded(chunks_of(d_attended), sent_ref, 0)


def global_finish_body(
    got_ref, d_middle_ref, x_ref, gain_ref, first_ref, table_ref, d_proj_ref, grad_ref, gain_out_ref
):
    tables = [table_ref[i] for i in range(3)]
    rows = x_ref.shape[0] // 2
    width = x_ref.shape[1]
    d_queries, d_keys = unpack_pairs(got_ref, rows)
    d_values = unpack_folded(got_ref, rows * 3 // 2, rows)
    parts = [unrotate(c, tables).astype(BF) for c in d_queries + d_keys]
    d_projected = jnp.concatenate(parts + [c.astype(BF) for c in d_values], 1)
    d_proj_ref[...] = d_projected
    input_backward(
        d_middle_ref[...], d_projected, x_ref, gain_ref, first_ref, grad_ref, gain_out_ref
    )


def neighbours(count, step):
    return [
        (i, i + step)
        for i in range(count)
        if 0 <= i + step < count and i // GROUP == (i + step) // GROUP
    ]


def exchange(blocks, count):
    groups = [list(range(s, s + GROUP)) for s in range(0, count, GROUP)]
    return lax.all_to_all(blocks, "dp", 0, 0, axis_index_groups=groups)


def to_other_section(rows, step):
    return lax.ppermute(rows, "section", [(0, 1)] if step > 0 else [(1, 0)])


def partner(rows, apart, count):
    return lax.ppermute(rows, "dp", [(i, i ^ apart) for i in range(count)])


def gather_group(piece, group_pos, count):
    pieces = {0: piece}
    for apart in (4, 8, 12):
        pieces[apart] = partner(piece, apart, count)
    for apart in (0, 4, 8, 12):
        pieces[apart + 2] = partner(pieces[apart], 2, count)
    for apart in range(0, GROUP, 2):
        pieces[apart + 1] = partner(pieces[apart], 1, count)
    whole = jnp.zeros((GROUP,) + piece.shape, piece.dtype)
    for apart, item in pieces.items():
        start = (group_pos ^ apart,) + (0,) * piece.ndim
        whole = lax.dynamic_update_slice(whole, item[None], start)
    return whole


def gather_rows(piece, group_pos, count):
    whole = gather_group(piece, group_pos, count)
    if count > GROUP:
        groups = [list(range(s, count, GROUP)) for s in range(GROUP)]
        whole = lax.all_gather(whole, "dp", axis=0, tiled=True, axis_index_groups=groups)
    return whole.reshape(-1, piece.shape[-1])


def plane_rows(rows, group_pos, count):
    parts = rows.reshape(count // GROUP, 4, 4, *rows.shape[1:])
    place = group_pos % 4
    taken = []
    for apart in range(4):
        block = lax.dynamic_index_in_dim(parts, place ^ apart, 2, keepdims=False)
        taken.append(partner(block, apart, count) if apart else block)
    return jnp.concatenate(taken, -1).swapaxes(0, 1)


def plane_tokens(rows, count):
    across = partner(rows, 2, count)
    beside = partner(rows, 1, count)
    return jnp.concatenate([rows, beside, across, partner(across, 1, count)], 0)


def plane_product(left, right):
    planes, groups, rows, tokens = left.shape
    product = dot(left.reshape(-1, tokens), right)
    return product.reshape(planes, groups, rows, -1)


def stacked_columns(blocks, width):
    return jnp.concatenate(
        [blocks[..., c : c + width] for c in range(0, blocks.shape[-1], width)], -2
    )


def sum_planes(blocks, count):
    groups = [
        [s + 4 * z + k for z in range(4)] for s in range(0, count, GROUP) for k in range(4)
    ]
    got = lax.all_to_all(blocks.astype(BF), "dp", 0, 0, axis_index_groups=groups)
    total = jnp.sum(got.astype(F32), 0)
    if count > GROUP:
        apart = [list(range(s, count, GROUP)) for s in range(GROUP)]
        total = lax.psum_scatter(total, "dp", scatter_dimension=0, axis_index_groups=apart)
        return total
    return total[0]


def on_device(
    tokens_in,
    segment_ids,
    out_grad,
    qkv_weight,
    attn_out_weight,
    mlp_in_weight,
    mlp_out_weight,
    attn_gain,
    mlp_gain,
):
    lower = lax.axis_index("section") == 0
    count = lax.axis_size("dp")
    replica = lax.axis_index("dp")
    group_pos = replica % GROUP
    micro_count, row_count, width = tokens_in.shape
    shard = qkv_weight.shape[1]
    wide = mlp_out_weight.shape[1] * width // shard
    own_ids = segment_ids.reshape(-1)
    id_columns = -(-own_ids.size // shard)
    ids = jnp.pad(own_ids.astype(BF), (0, id_columns * shard - own_ids.size))
    extra = jnp.concatenate(
        [attn_gain[0][:, None], mlp_gain[0][:, None], ids.reshape(shard, id_columns)], 1
    )
    extra = jnp.pad(extra, ((0, 0), (0, 128 - extra.shape[1])))
    second = lax.all_gather(
        jnp.concatenate(
            [attn_out_weight[0], mlp_in_weight[0], mlp_out_weight[0].reshape(shard, wide)], 1
        ),
        "dp",
        axis=0,
        tiled=True,
    )
    first = gather_rows(jnp.concatenate([qkv_weight[0], extra], 1), group_pos, count)
    gain_attn = first[:, 3 * width].astype(F32)[None]
    gain_mlp = first[:, 3 * width + 1].astype(F32)[None]
    w_out = second[:, second.shape[1] - wide :].reshape(-1, width)
    all_ids = first[:, 3 * width + 2 : 3 * width + 2 + id_columns].reshape(count, -1)
    all_ids = lax.dynamic_slice_in_dim(all_ids, replica - group_pos, GROUP, 0)
    all_ids = all_ids[:, : own_ids.size].reshape(GROUP, micro_count, row_count)
    segments = all_ids.swapaxes(0, 1).reshape(micro_count, GROUP * row_count).astype(jnp.int32)

    positions = group_pos * row_count + jnp.arange(row_count)
    local_tables = angles(positions, local_log_base)
    global_tables = angles(positions, global_log_base)

    key_pos = positions[0] - row_count + jnp.arange(3 * row_count)
    around = jnp.pad(segments, ((0, 0), (row_count, row_count)), constant_values=-1)
    key_seg = lax.dynamic_slice_in_dim(around, group_pos * row_count, 3 * row_count, 1)
    visible = (key_seg[:, :, None] == segment_ids[:, None, :]) & (
        jnp.abs(positions[None, :] - key_pos[:, None]) <= HALF_WIN
    )[None]
    bias = jnp.tile(jnp.where(visible, 0.0, masked_score), (1, 1, 2))

    own_seg = lax.dynamic_index_in_dim(segments, group_pos // 8, 0, keepdims=False)
    halves = own_seg.reshape(GROUP, 2, row_count // 2)
    mine = lax.dynamic_index_in_dim(halves, group_pos % 2, 1, keepdims=False).reshape(-1)
    theirs = lax.dynamic_index_in_dim(halves, 1 - group_pos % 2, 1, keepdims=False).reshape(-1)
    shared_seg = jnp.concatenate([mine, theirs])[:, None]
    own_seg = own_seg[:, None]

    rows = micro_count * row_count
    inner = second.shape[1] - width - wide
    hidden = w_out.shape[0]
    pairs = rows * width // (row_count * LANES)
    in_0 = tokens_in.reshape(rows, width)
    normed_0, q_0, kv_0 = on_core(
        local_project_body,
        [((rows, width), BF), ((rows, width), BF), ((rows, 2 * width), BF)],
        (in_0, gain_attn, first, local_tables),
    )
    up_pairs, down_pairs = neighbours(count, 1), neighbours(count, -1)
    around_0 = (
        lax.ppermute(kv_0, "dp", up_pairs),
        kv_0,
        lax.ppermute(kv_0, "dp", down_pairs),
    )
    att_0, total_0 = on_core(
        local_forward_body,
        [((rows, width), BF), ((pairs, 1, LANES), F32)],
        (q_0, *around_0, bias),
    )
    out_0, n2_0, mixed_0, middle_0, gate_up_0 = on_core(
        local_middle_body,
        [
            ((rows, width), BF),
            ((rows, width), BF),
            ((rows, hidden), BF),
            ((rows, width), F32),
            ((rows, inner), F32),
        ],
        (in_0, att_0, gain_mlp, second, w_out),
    )

    in_1 = to_other_section(out_0, 1)
    fold = row_count * 3 // 4
    half = row_count // 2
    normed_1, sent = on_core(
        global_project_body,
        [((rows, width), BF), ((GROUP, 3 * fold, LANES), BF)],
        (in_1, gain_attn, first, global_tables),
    )
    got = exchange(sent, count)
    beside = jnp.concatenate(
        [got[:, row_count : row_count + half], got[:, 3 * fold - half :]], 1
    )
    beside = partner(beside, 1, count)
    keys = GROUP * row_count
    tiles = keys * 3 // 2 // TILE
    head_scratch = [
        pltpu.VMEM((keys * 3 // 2, LANES), BF),
        pltpu.VMEM((2, keys, LANES), BF),
        pltpu.VMEM((2, keys, LANES), BF),
        pltpu.VMEM((2, LANES, keys), BF),
    ]
    folded, total_1 = on_core(
        global_forward_body,
        [((GROUP, fold, LANES), BF), ((tiles, 1, TILE), F32)],
        (got, beside, own_seg, shared_seg),
        head_scratch + [pltpu.VMEM((keys * 3 // 2, LANES), F32)],
    )
    folded = exchange(folded, count)

    up_1 = out_grad.reshape(rows, width)
    out_1, att_1, n2_1, mixed_1, d_gu_1, gain_mlp_1, d_mid_1, d_attn_1, sent = on_core(
        global_middle_body,
        [
            ((rows, width), BF),
            ((rows, width), BF),
            ((rows, width), BF),
            ((rows, hidden), BF),
            ((rows, inner), BF),
            ((1, width), F32),
            ((rows, width), F32),
            ((rows, width), BF),
            ((GROUP, fold, LANES), BF),
        ],
        (folded, in_1, up_1, gain_mlp, second, w_out),
    )
    d_folded = exchange(sent, count)
    sent, to_beside = on_core(
        global_backward_body,
        [((GROUP, 3 * fold, LANES), BF), ((GROUP, 2 * half, LANES), BF)],
        (got, beside, own_seg, shared_seg, total_1, d_folded),
        head_scratch
        + [
            pltpu.VMEM((keys * 3 // 2, LANES), BF),
            pltpu.VMEM((keys * 3 // 2, LANES), F32),
            pltpu.VMEM((2, keys, LANES), F32),
            pltpu.VMEM((2, keys, LANES), F32),
        ],
    )
    back = partner(to_beside, 1, count)
    gap = 3 * fold - half - row_count - half
    back = jnp.concatenate(
        [
            jnp.zeros((GROUP, row_count, LANES), BF),
            back[:, :half],
            jnp.zeros((GROUP, gap, LANES), BF),
            back[:, half:],
        ],
        1,
    )
    sent = (sent.astype(F32) + back.astype(F32)).astype(BF)
    got = exchange(sent, count)
    d_proj_1, grad_1, gain_attn_1 = on_core(
        global_finish_body,
        [((rows, 3 * width), BF), ((rows, width), BF), ((1, width), F32)],
        (got, d_mid_1, in_1, gain_attn, first, global_tables),
    )

    n1, att, n2, mixed = (
        jnp.where(lower, a, b).T.reshape(count, -1, micro_count * row_count)
        for a, b in (
            (normed_0, normed_1),
            (att_0, att_1),
            (n2_0, n2_1),
            (mixed_0, mixed_1),
        )
    )
    left = plane_rows(jnp.concatenate([n1, att, n2, mixed], 1), group_pos, count)

    up_0 = to_other_section(grad_1, -1)
    d_gu_0, gain_mlp_0, d_mid_0, d_attn_0, d_att_0 = on_core(
        local_back_middle_body,
        [
            ((rows, inner), BF),
            ((1, width), F32),
            ((rows, width), F32),
            ((rows, width), BF),
            ((rows, width), BF),
        ],
        (up_0, middle_0, gate_up_0, gain_mlp, second, w_out),
    )
    d_gu, d_mlp, d_attn = (
        jnp.where(lower, a, b)
        for a, b in ((d_gu_0, d_gu_1), (up_0, up_1), (d_attn_0, d_attn_1))
    )
    right = plane_tokens(jnp.concatenate([d_gu, d_mlp, d_attn], 1), count)
    early = jnp.concatenate(
        [
            stacked_columns(
                plane_product(left[:, :, 2 * shard : 3 * shard], right[:, :inner]), width
            ),
            plane_product(left[:, :, 3 * shard :], right[:, inner : inner + width]),
            plane_product(left[:, :, shard : 2 * shard], right[:, inner + width :]),
        ],
        2,
    )
    dq_0, d_own, d_before, d_after = on_core(
        local_backward_body,
        [
            ((rows, width), BF),
            ((rows, 2 * width), F32),
            ((rows, 2 * width), BF),
            ((rows, 2 * width), BF),
        ],
        (q_0, *around_0, bias, total_0, d_att_0, local_tables),
    )
    from_after = lax.ppermute(d_before, "dp", down_pairs)
    from_before = lax.ppermute(d_after, "dp", up_pairs)
    (d_proj_0,) = on_core(
        local_join_body,
        [((rows, 3 * width), BF)],
        (dq_0, d_own, from_after, from_before, local_tables),
    )
    d_proj = jnp.where(lower, d_proj_0, d_proj_1)
    d_proj, early = lax.optimization_barrier((d_proj, early))
    early = sum_planes(early, count)
    late = stacked_columns(
        plane_product(left[:, :, :shard], plane_tokens(d_proj, count)), width
    )
    grad_0, gain_attn_0 = on_core(
        input_backward_body,
        [((rows, width), BF), ((1, width), F32)],
        (d_mid_0, d_proj_0, in_0, gain_attn, first),
    )

    gains = jnp.where(
        lower,
        jnp.concatenate([gain_attn_0, gain_mlp_0]),
        jnp.concatenate([gain_attn_1, gain_mlp_1]),
    )
    gains = gains + partner(gains, 1, count)
    gains = gains + partner(gains, 2, count)
    gains = gains.reshape(2, count // GROUP, 4, 4, shard)
    gains = lax.dynamic_index_in_dim(gains, group_pos % 4, 3, keepdims=False)
    gains = jnp.pad(
        gains.transpose(2, 1, 0, 3), ((0, 0), (0, 0), (0, 14), (0, width - shard))
    )
    late = sum_planes(jnp.concatenate([late, gains], 2), count)

    def columns(rows, parts):
        return jnp.concatenate([rows[p * shard : (p + 1) * shard] for p in range(parts)], 1)[None]

    parts = inner // width
    return (
        jnp.where(lower, out_0, out_1).reshape(1, micro_count, row_count, width),
        jnp.where(lower, grad_0, grad_1).reshape(1, micro_count, row_count, width),
        columns(late, 3),
        early[early.shape[0] - shard :][None],
        columns(early, parts),
        early[parts * shard : early.shape[0] - shard][None],
        late[3 * shard, :shard][None],
        late[3 * shard + 1, :shard][None],
    )


def solution(mesh):
    in_specs = (
        P(None, "dp", None),
        P(None, "dp"),
        P(None, "dp", None),
        P("section", "dp", None),
        P("section", "dp", None),
        P("section", "dp", None),
        P("section", "dp", None),
        P("section", "dp"),
        P("section", "dp"),
    )
    out_specs = (
        P("section", None, "dp", None),
        P("section", None, "dp", None),
        P("section", "dp", None),
        P("section", "dp", None),
        P("section", "dp", None),
        P("section", "dp", None),
        P("section", "dp"),
        P("section", "dp"),
    )
    return jax.shard_map(
        on_device, mesh=mesh, in_specs=in_specs, out_specs=out_specs, check_vma=False
    )
```

profile of v0, /device:TPU:0, one launch (start us, length us, event | category | flops | bytes accessed | tf_op | source)
XLA Modules:
  0.0 367.9 jit_solution(1216042377584419763)
XLA Ops:
  10.0 3.1 collective-permute-start
  13.1 2.6 collective-permute-start.1
  15.7 1.7 collective-permute-start.3
  18.4 1.8 pad_maximum_fusion.3
  20.9 2.1 broadcast_in_dim.90
  24.7 7.9 %collective-permute-done.1 = bf16[48,2432]{1,0:T(8,128)(2,1)S(1)} collective-permute-done((bf16[48,2432]{1,0:T(8,128)(2,1)S(1)}, bf16[48,2432]{1,0:T(8,128)(2,1)S(1)}, u32[]{:S(2)}, u32[]{:S(2)}) %collective-permute-start.1) | collective-permute-done | bytes 233504 | tf_op jit(solution)/shard_map/ppermute | solution.py:564
  38.7 4.2 %collective-permute-done.5 = bf16[48,2432]{1,0:T(8,128)(2,1)S(1)} collective-permute-done((bf16[48,2432]{1,0:T(8,128)(2,1)S(1)}, bf16[48,2432]{1,0:T(8,128)(2,1)S(1)}, u32[]{:S(2)}, u32[]{:S(2)}) %collective-permute-start.5) | collective-permute-done | bytes 233504 | tf_op jit(solution)/shard_map/ppermute | solution.py:564
  43.6 3.2 collective-permute-done.6
  55.9 3.0 shard_map.152
  59.5 1.8 collective-permute-start.15
  65.7 3.6 shard_map.153
  69.9 23.0 %all-gather.2.cloned.1.call-done.wide_ref = bf16[768,4224]{1,0:T(8,128)(2,1)} async-done(((bf16[48,4224]{1,0:T(8,128)(2,1)}), bf16[768,4224]{1,0:T(8,128)(2,1)}) %all-gather.2.cloned.1.call-update) | async-done | bytes 6488080 | tf_op jit(solution)/shard_map/all_gather | solution.py:656
  93.0 2.9 slice.165
  95.9 2.9 reshape.275.w_out_ref
  98.8 4.3 %shard_map.154 = (bf16[128,768]{1,0:T(8,128)(2,1)S(1)}, bf16[128,768]{1,0:T(8,128)(2,1)S(1)}, bf16[128,1152]{1,0:T(8,128)(2,1)S(1)}, f32[128,768]{1,0:T(8,128)S(1)}, f32[128,2304]{1,0:T(8,128)S(1)}) custom-call(bf16[128,768]{1,0:T(8,128)(2,1)S(1)} %bitcast.151, bf16[128,768]{1,0:T(8,128)(2,1)S(1)} %get-tuple-element.51.att_ref, ...), custom_call_target="tpu_custom_call" | custom-call | tf_op jit(solution)/shard_map/pallas_call | solution.py:63
  106.4 3.4 collective-permute-start.17
  110.1 4.2 %collective-permute-done.17.x_ref = bf16[128,768]{1,0:T(8,128)(2,1)S(1)} collective-permute-done((bf16[128,768]{1,0:T(8,128)(2,1)S(1)}, bf16[128,768]{1,0:T(8,128)(2,1)S(1)}, u32[]{:S(2)}, u32[]{:S(2)}) %collective-permute-start.17) | collective-permute-done | bytes 196640 | tf_op jit(solution)/shard_map/ppermute | solution.py:560
  114.3 3.2 shard_map.155
  117.6 22.6 %all_to_all.30.got_ref = bf16[16,144,128]{2,1,0:T(8,128)(2,1)S(1)} all-to-all(bf16[16,144,128]{2,1,0:T(8,128)(2,1)S(1)} %get-tuple-element.53), channel_id=1, replica_groups={{0,1,2,3,4,5,6,7,8,9,10,11,12,13,14,15},{16,17,18,19,20,21,22,23,24,25,..., dimensions={0} | all-to-all | bytes 1179648 | tf_op jit(solution)/shard_map/all_to_all | solution.py:556
  142.8 7.0 %shard_map.156 = (bf16[16,48,128]{2,1,0:T(8,128)(2,1)S(1)}, f32[6,1,256]{2,1,0:T(1,128)S(1)}) custom-call(bf16[16,144,128]{2,1,0:T(8,128)(2,1)S(1)} %all_to_all.30.got_ref, bf16[16,64,128]{2,1,0:T(8,128)(2,1)} %collective-permute-done.18.other_ref, s32[1024,1]{1,0:T(8,128)S(1)} %copy.42.own_seg_ref, s32[1024,1]{1,0:T(8,128)S(1)} %copy.43.shared_seg_ref), custom_call_target="tpu_custom_call" | custom-call | tf_op jit(solution)/shard_map/pallas_call | solution.py:63
  149.8 11.8 %all_to_all.31.got_ref = bf16[16,48,128]{2,1,0:T(8,128)(2,1)S(1)} all-to-all(bf16[16,48,128]{2,1,0:T(8,128)(2,1)S(1)} %get-tuple-element.54), channel_id=1, replica_groups={{0,1,2,3,4,5,6,7,8,9,10,11,12,13,14,15},{16,17,18,19,20,21,22,23,24,25,..., dimensions={0} | all-to-all | bytes 393216 | tf_op jit(solution)/shard_map/all_to_all | solution.py:556
  161.6 7.0 %shard_map.157 = (bf16[128,768]{1,0:T(8,128)(2,1)S(1)}, bf16[128,768]{1,0:T(8,128)(2,1)S(1)}, bf16[128,768]{1,0:T(8,128)(2,1)S(1)}, bf16[128,1152]{1,0:T(8,128)(...) custom-call(bf16[16,48,128]{2,1,0:T(8,128)(2,1)S(1)} %all_to_all.31., ...), custom_call_target="tpu_custom_call" | custom-call | tf_op jit(solution)/shard_map/pallas_call | solution.py:63
  170.6 11.6 %all_to_all.32.d_ref = bf16[16,48,128]{2,1,0:T(8,128)(2,1)S(1)} all-to-all(bf16[16,48,128]{2,1,0:T(8,128)(2,1)S(1)} %get-tuple-element.57), channel_id=1, replica_groups={{0,1,2,3,4,5,6,7,8,9,10,11,12,13,14,15},{16,17,18,19,20,21,22,23,24,25,..., dimensions={0} | all-to-all | bytes 393216 | tf_op jit(solution)/shard_map/all_to_all | solution.py:556
  182.2 8.3 %shard_map.158 = (bf16[16,144,128]{2,1,0:T(8,128)(2,1)S(1)}, bf16[16,64,128]{2,1,0:T(8,128)(2,1)S(1)}) custom-call(bf16[16,144,128]{2,1,0:T(8,128)(2,1)S(1)} %all_to_all.30.got_ref, bf16[16,64,128]{2,1,0:T(8,128)(2,1)} %collective-permute-done.18.other_ref, s32[1024,1]{1,0:T(8,128)S(1)} %copy.42.own_seg_ref, s32[1024,1]{1,0:T(8,128)S(1)} %copy.43.shared_seg_ref, ...), custom_call_target="tpu_custom_call" | custom-call | tf_op jit(solution)/shard_map/pallas_call | solution.py:63
  193.3 3.6 all-to-all-start.3
  197.7 1.7 copy.47
  200.3 12.2 %all-to-all-done.3.got_ref = bf16[16,144,128]{2,1,0:T(8,128)(2,1)S(1)} async-done(((bf16[16,144,128]{2,1,0:T(8,128)(2,1)}), bf16[16,144,128]{2,1,0:T(8,128)(2,1)S(1)}, u32[]{:S(2)}, u32[]{:S(2)}) %all-to-all-start.3) | async-done | bytes 589856 | tf_op jit(solution)/shard_map/all_to_all | solution.py:556
  213.4 3.7 shard_map.159
  219.5 6.5 %collective-permute-done.20.up_ref = bf16[128,768]{1,0:T(8,128)(2,1)S(1)} collective-permute-done((bf16[128,768]{1,0:T(8,128)(2,1)S(1)}, bf16[128,768]{1,0:T(8,128)(2,1)S(1)}, u32[]{:S(2)}, u32[]{:S(2)}) %collective-permute-start.20) | collective-permute-done | bytes 196640 | tf_op jit(solution)/shard_map/ppermute | solution.py:560
  228.3 5.7 %shard_map.160 = (bf16[128,2304]{1,0:T(8,128)(2,1)S(1)}, f32[1,768]{1,0:T(1,128)S(1)}, f32[128,768]{1,0:T(8,128)S(1)}, bf16[128,768]{1,0:T(8,128)(2,1)S(1)}, bf16[128,768]{1,0:T(8,128)(2,1)S(1)}) custom-call(bf16[128,768]{1,0:T(8,128)(2,1)S(1)} %collective-permute-done.20.up_ref, f32[128,768]{1,0:T(8,128)S(1)} %copy-done.28, f32[128,2304]{1,0:T(8,128)S(1)} %copy-done.18, ...), custom_call_target="tpu_custom_call" | custom-call | tf_op jit(solution)/shard_map/pallas_call | solution.py:63
  241.6 3.5 shard_map.161
  246.4 3.1 collective-permute-start.22
  249.5 3.3 collective-permute-start.25
  252.7 15.9 %collective-permute-done.24 = bf16[1,4,216,128]{3,2,1,0:T(8,128)(2,1)S(1)} collective-permute-done((bf16[1,4,216,128]{3,2,1,0:T(8,128)(2,1)S(1)}, bf16[1,4,216,128]{3,2,1,0:T(8,128)(2,1)S(1)}, u32[]{:S(2)}, u32[]{:S(2)}) %collective-permute-start.24) | collective-permute-done | bytes 221216 | tf_op jit(solution)/shard_map/ppermute | solution.py:564
  269.1 4.2 %collective-permute-done.25 = bf16[1,4,216,128]{3,2,1,0:T(8,128)(2,1)S(1)} collective-permute-done((bf16[1,4,216,128]{3,2,1,0:T(8,128)(2,1)S(1)}, bf16[1,4,216,128]{3,2,1,0:T(8,128)(2,1)S(1)}, u32[]{:S(2)}, u32[]{:S(2)}) %collective-permute-start.25) | collective-permute-done | bytes 221216 | tf_op jit(solution)/shard_map/ppermute | solution.py:564
  275.2 5.4 %pad_maximum_fusion = bf16[512,3840]{1,0:T(8,128)(2,1)S(1)} fusion(bf16[128,3840]{1,0:T(8,128)(2,1)S(1)} %collective-permute-done.28, bf16[128,3840]{1,0:T(8,128)(2,1)} %collective-permute-done.27, bf16[128,3840]{1,0:T(8,128)(2,1)S(1)} %collective-permute-done.26, bf16[128,768]{1,0:T(8,128)(2,1)S(1)} %copy-done.60, bf16[128,768]{1,0:T(8,128)(2,1)S(1)} %copy-done.62, ...), kind=kLoop, calls=%fused_computation | loop fusion | flops 23592960 | bytes 7864320 | tf_op jit(solution)/shard_map/concatenate | solution.py:603
  283.5 2.1 fusion.8
  285.6 2.0 fusion.9
  287.6 4.5 %all-to-all-start.5 = ((bf16[4,1,264,768]{3,2,1,0:T(8,128)(2,1)}), bf16[4,1,264,768]{3,2,1,0:T(8,128)(2,1)}, u32[]{:S(2)}, u32[]{:S(2)}) async-start(bf16[4,1,264,768]{3,2,1,0:T(8,128)(2,1)} %bitcast.146), calls=%async_computation.5 | async-start | bytes 3244032 | tf_op jit(solution)/shard_map/all_to_all | solution.py:622
  292.1 5.9 %collective-permute-start.30 = (bf16[128,2304]{1,0:T(8,128)(2,1)S(1)}, bf16[128,2304]{1,0:T(8,128)(2,1)S(1)}, u32[]{:S(2)}, u32[]{:S(2)}) collective-permute-start(bf16[128,2304]{1,0:T(8,128)(2,1)S(1)} %copy-done.65), channel_id=1, source_target_pairs={{0,2},{1,3},{2,0},{3,1},{4,6},{5,7},{6,4},{7,5},{8,10},{9,11},{10,... | collective-permute-start | bytes 1769480 | tf_op jit(solution)/shard_map/ppermute | solution.py:564
  297.9 3.5 shard_map.163
  301.5 9.3 %collective-permute-done.30 = bf16[128,2304]{1,0:T(8,128)(2,1)S(1)} collective-permute-done((bf16[128,2304]{1,0:T(8,128)(2,1)S(1)}, bf16[128,2304]{1,0:T(8,128)(2,1)S(1)}, u32[]{:S(2)}, u32[]{:S(2)}) %collective-permute-start.30) | collective-permute-done | bytes 589856 | tf_op jit(solution)/shard_map/ppermute | solution.py:564
  313.2 3.3 collective-permute-done.33
  316.7 1.6 fusion
  319.4 11.0 %all-to-all-done.5 = bf16[4,1,264,768]{3,2,1,0:T(8,128)(2,1)} async-done(((bf16[4,1,264,768]{3,2,1,0:T(8,128)(2,1)}), bf16[4,1,264,768]{3,2,1,0:T(8,128)(2,1)}, u32[]{:S(2)}, u32[]{:S(2)}) %all-to-all-start.5) | async-done | bytes 1622048 | tf_op jit(solution)/shard_map/all_to_all | solution.py:622
  330.5 3.5 all-to-all-start.4
  335.4 1.8 convert_reduce_fusion
  339.4 20.2 %all-to-all-done.4 = bf16[4,1,160,768]{3,2,1,0:T(8,128)(2,1)S(1)} async-done(((bf16[4,1,160,768]{3,2,1,0:T(8,128)(2,1)}), bf16[4,1,160,768]{3,2,1,0:T(8,128)(2,1)S(1)}, u32[]{:S(2)}, u32[]{:S(2)}) %all-to-all-start.4) | async-done | bytes 983072 | tf_op jit(solution)/shard_map/all_to_all | solution.py:622
  (295 shorter events, 68.0 us)
Async XLA Ops:
  7.2 85.8 %all-gather.2.cloned.1.call-start = ((), (), s32[]{:S(2)}) async-start(), calls=%async_computation.6 | async-start | bytes 6893568 | tf_op jit(solution)/shard_map/all_gather | solution.py:656
  10.0 14.4 %collective-permute-start = (bf16[48,2432]{1,0:T(8,128)(2,1)S(1)}, bf16[48,2432]{1,0:T(8,128)(2,1)S(1)}, u32[]{:S(2)}, u32[]{:S(2)}) collective-permute-start(bf16[48,2432]{1,0:T(8,128)(2,1)S(1)} %fusion.33), channel_id=1, source_target_pairs={{0,4},{1,5},{2,6},{3,7},{4,0},{5,1},{6,2},{7,3},{8,12},{9,13},{10,... | collective-permute-start | bytes 700424 | tf_op jit(solution)/shard_map/ppermute | solution.py:564
  13.1 19.5 %collective-permute-start.1 = (bf16[48,2432]{1,0:T(8,128)(2,1)S(1)}, bf16[48,2432]{1,0:T(8,128)(2,1)S(1)}, u32[]{:S(2)}, u32[]{:S(2)}) collective-permute-start(bf16[48,2432]{1,0:T(8,128)(2,1)S(1)} %fusion.33), channel_id=1, source_target_pairs={{0,8},{1,9},{2,10},{3,11},{4,12},{5,13},{6,14},{7,15},{8,0},{9,1},... | collective-permute-start | bytes 700424 | tf_op jit(solution)/shard_map/ppermute | solution.py:564
  15.7 18.4 %collective-permute-start.2 = (bf16[48,2432]{1,0:T(8,128)(2,1)S(1)}, bf16[48,2432]{1,0:T(8,128)(2,1)S(1)}, u32[]{:S(2)}, u32[]{:S(2)}) collective-permute-start(bf16[48,2432]{1,0:T(8,128)(2,1)S(1)} %fusion.33), channel_id=1, source_target_pairs={{0,12},{1,13},{2,14},{3,15},{4,8},{5,9},{6,10},{7,11},{8,4},{9,5},... | collective-permute-start | bytes 700424 | tf_op jit(solution)/shard_map/ppermute | solution.py:564
  15.7 19.0 %collective-permute-start.3 = (bf16[48,2432]{1,0:T(8,128)(2,1)S(1)}, bf16[48,2432]{1,0:T(8,128)(2,1)S(1)}, u32[]{:S(2)}, u32[]{:S(2)}) collective-permute-start(bf16[48,2432]{1,0:T(8,128)(2,1)S(1)} %fusion.33), channel_id=1, source_target_pairs={{0,2},{1,3},{2,0},{3,1},{4,6},{5,7},{6,4},{7,5},{8,10},{9,11},{10,... | collective-permute-start | bytes 700424 | tf_op jit(solution)/shard_map/ppermute | solution.py:564
  17.4 30.2 %collective-permute-start.7 = (bf16[48,2432]{1,0:T(8,128)(2,1)S(1)}, bf16[48,2432]{1,0:T(8,128)(2,1)S(1)}, u32[]{:S(2)}, u32[]{:S(2)}) collective-permute-start(bf16[48,2432]{1,0:T(8,128)(2,1)S(1)} %fusion.33), channel_id=1, source_target_pairs={{0,1},{1,0},{2,3},{3,2},{4,5},{5,4},{6,7},{7,6},{8,9},{9,8},{10,11... | collective-permute-start | bytes 700424 | tf_op jit(solution)/shard_map/ppermute | solution.py:564
  24.2 31.7 %copy-start = (f32[3,128,128]{2,1,0:T(8,128)}, f32[3,128,128]{2,1,0:T(8,128)S(1)}, u32[]{:S(2)}) copy-start(f32[3,128,128]{2,1,0:T(8,128)S(1)} %tile.13.table_ref) | copy-start | bytes 589828
  24.4 13.1 %collective-permute-start.4 = (bf16[48,2432]{1,0:T(8,128)(2,1)S(1)}, bf16[48,2432]{1,0:T(8,128)(2,1)S(1)}, u32[]{:S(2)}, u32[]{:S(2)}) collective-permute-start(bf16[48,2432]{1,0:T(8,128)(2,1)S(1)} %collective-permute-done), channel_id=1, source_target_pairs={{0,2},{1,3},{2,0},{3,1},{4,6},{5,7},{6,4},{7,5},{8,10},{9,11},{10,... | collective-permute-start | bytes 700424 | tf_op jit(solution)/shard_map/ppermute | solution.py:564
  32.6 10.3 %collective-permute-start.5 = (bf16[48,2432]{1,0:T(8,128)(2,1)S(1)}, bf16[48,2432]{1,0:T(8,128)(2,1)S(1)}, u32[]{:S(2)}, u32[]{:S(2)}) collective-permute-start(bf16[48,2432]{1,0:T(8,128)(2,1)S(1)} %collective-permute-done.1), channel_id=1, source_target_pairs={{0,2},{1,3},{2,0},{3,1},{4,6},{5,7},{6,4},{7,5},{8,10},{9,11},{10,... | collective-permute-start | bytes 700424 | tf_op jit(solution)/shard_map/ppermute | solution.py:564
  34.1 12.8 %collective-permute-start.6 = (bf16[48,2432]{1,0:T(8,128)(2,1)S(1)}, bf16[48,2432]{1,0:T(8,128)(2,1)S(1)}, u32[]{:S(2)}, u32[]{:S(2)}) collective-permute-start(bf16[48,2432]{1,0:T(8,128)(2,1)S(1)} %collective-permute-done.2), channel_id=1, source_target_pairs={{0,2},{1,3},{2,0},{3,1},{4,6},{5,7},{6,4},{7,5},{8,10},{9,11},{10,... | collective-permute-start | bytes 700424 | tf_op jit(solution)/shard_map/ppermute | solution.py:564
  34.6 14.2 %collective-permute-start.8 = (bf16[48,2432]{1,0:T(8,128)(2,1)S(1)}, bf16[48,2432]{1,0:T(8,128)(2,1)S(1)}, u32[]{:S(2)}, u32[]{:S(2)}) collective-permute-start(bf16[48,2432]{1,0:T(8,128)(2,1)S(1)} %collective-permute-done.3), channel_id=1, source_target_pairs={{0,1},{1,0},{2,3},{3,2},{4,5},{5,4},{6,7},{7,6},{8,9},{9,8},{10,11... | collective-permute-start | bytes 700424 | tf_op jit(solution)/shard_map/ppermute | solution.py:564
  37.5 12.1 %collective-permute-start.9 = (bf16[48,2432]{1,0:T(8,128)(2,1)S(1)}, bf16[48,2432]{1,0:T(8,128)(2,1)S(1)}, u32[]{:S(2)}, u32[]{:S(2)}) collective-permute-start(bf16[48,2432]{1,0:T(8,128)(2,1)S(1)} %collective-permute-done), channel_id=1, source_target_pairs={{0,1},{1,0},{2,3},{3,2},{4,5},{5,4},{6,7},{7,6},{8,9},{9,8},{10,11... | collective-permute-start | bytes 700424 | tf_op jit(solution)/shard_map/ppermute | solution.py:564
  42.9 8.6 %collective-permute-start.11 = (bf16[48,2432]{1,0:T(8,128)(2,1)S(1)}, bf16[48,2432]{1,0:T(8,128)(2,1)S(1)}, u32[]{:S(2)}, u32[]{:S(2)}) collective-permute-start(bf16[48,2432]{1,0:T(8,128)(2,1)S(1)} %collective-permute-done.1), channel_id=1, source_target_pairs={{0,1},{1,0},{2,3},{3,2},{4,5},{5,4},{6,7},{7,6},{8,9},{9,8},{10,11... | collective-permute-start | bytes 700424 | tf_op jit(solution)/shard_map/ppermute | solution.py:564
  46.9 6.0 %collective-permute-start.13 = (bf16[48,2432]{1,0:T(8,128)(2,1)S(1)}, bf16[48,2432]{1,0:T(8,128)(2,1)S(1)}, u32[]{:S(2)}, u32[]{:S(2)}) collective-permute-start(bf16[48,2432]{1,0:T(8,128)(2,1)S(1)} %collective-permute-done.2), channel_id=1, source_target_pairs={{0,1},{1,0},{2,3},{3,2},{4,5},{5,4},{6,7},{7,6},{8,9},{9,8},{10,11... | collective-permute-start | bytes 700424 | tf_op jit(solution)/shard_map/ppermute | solution.py:564
  47.6 3.2 collective-permute-start.10
  48.8 3.4 collective-permute-start.12
  49.6 4.0 %collective-permute-start.14 = (bf16[48,2432]{1,0:T(8,128)(2,1)S(1)}, bf16[48,2432]{1,0:T(8,128)(2,1)S(1)}, u32[]{:S(2)}, u32[]{:S(2)}) collective-permute-start(bf16[48,2432]{1,0:T(8,128)(2,1)S(1)} %collective-permute-done.6), channel_id=1, source_target_pairs={{0,1},{1,0},{2,3},{3,2},{4,5},{5,4},{6,7},{7,6},{8,9},{9,8},{10,11... | collective-permute-start | bytes 700424 | tf_op jit(solution)/shard_map/ppermute | solution.py:564
  59.5 33.5 %copy-start.11 = (bf16[128,1536]{1,0:T(8,128)(2,1)}, bf16[128,1536]{1,0:T(8,128)(2,1)S(1)}, u32[]{:S(2)}) copy-start(bf16[128,1536]{1,0:T(8,128)(2,1)S(1)} %get-tuple-element.50.own_ref) | copy-start | bytes 1179652
  59.5 33.5 %copy-start.19 = (bf16[128,768]{1,0:T(8,128)(2,1)}, bf16[128,768]{1,0:T(8,128)(2,1)S(1)}, u32[]{:S(2)}) copy-start(bf16[128,768]{1,0:T(8,128)(2,1)S(1)} %get-tuple-element.49.q_ref) | copy-start | bytes 589828
  59.5 4.9 %collective-permute-start.15 = (bf16[128,1536]{1,0:T(8,128)(2,1)S(1)}, bf16[128,1536]{1,0:T(8,128)(2,1)S(1)}, u32[]{:S(2)}, u32[]{:S(2)}) collective-permute-start(bf16[128,1536]{1,0:T(8,128)(2,1)S(1)} %get-tuple-element.50.own_ref), channel_id=1, source_target_pairs={{0,1},{1,2},{2,3},{3,4},{4,5},{5,6},{6,7},{7,8},{8,9},{9,10},{10,1... | collective-permute-start | bytes 1179656 | tf_op jit(solution)/shard_map/ppermute | solution.py:704
  61.3 4.3 %collective-permute-start.16 = (bf16[128,1536]{1,0:T(8,128)(2,1)S(1)}, bf16[128,1536]{1,0:T(8,128)(2,1)S(1)}, u32[]{:S(2)}, u32[]{:S(2)}) collective-permute-start(bf16[128,1536]{1,0:T(8,128)(2,1)S(1)} %get-tuple-element.50.own_ref), channel_id=1, source_target_pairs={{1,0},{2,1},{3,2},{4,3},{5,4},{6,5},{7,6},{8,7},{9,8},{10,9},{11,1... | collective-permute-start | bytes 1179656 | tf_op jit(solution)/shard_map/ppermute | solution.py:706
  64.4 28.6 %copy-start.4 = (f32[2,192,128]{2,1,0:T(8,128)}, f32[2,192,128]{2,1,0:T(8,128)S(1)}, u32[]{:S(2)}) copy-start(f32[2,192,128]{2,1,0:T(8,128)S(1)} %copy.41.bias_ref) | copy-start | bytes 589828
  64.5 28.5 %copy-start.13 = (bf16[128,1536]{1,0:T(8,128)(2,1)}, bf16[128,1536]{1,0:T(8,128)(2,1)S(1)}, u32[]{:S(2)}) copy-start(bf16[128,1536]{1,0:T(8,128)(2,1)S(1)} %collective-permute-done.15.before_ref) | copy-start | bytes 1179652
  65.7 27.3 %copy-start.15 = (bf16[128,1536]{1,0:T(8,128)(2,1)}, bf16[128,1536]{1,0:T(8,128)(2,1)S(1)}, u32[]{:S(2)}) copy-start(bf16[128,1536]{1,0:T(8,128)(2,1)S(1)} %collective-permute-done.16.after_ref) | copy-start | bytes 1179652
  69.9 28.9 %copy-start.23 = (bf16[128,768]{1,0:T(8,128)(2,1)}, bf16[128,768]{1,0:T(8,128)(2,1)S(1)}, u32[]{:S(2)}) copy-start(bf16[128,768]{1,0:T(8,128)(2,1)S(1)} %get-tuple-element.51.att_ref) | copy-start | bytes 589828
  106.4 7.9 %collective-permute-start.17 = (bf16[128,768]{1,0:T(8,128)(2,1)S(1)}, bf16[128,768]{1,0:T(8,128)(2,1)S(1)}, u32[]{:S(2)}, u32[]{:S(2)}) collective-permute-start(bf16[128,768]{1,0:T(8,128)(2,1)S(1)} %get-tuple-element.52), channel_id=1, source_target_pairs={{0,16},{1,17},{2,18},{3,19},{4,20},{5,21},{6,22},{7,23},{8,24},{9,... | collective-permute-start | bytes 589832 | tf_op jit(solution)/shard_map/ppermute | solution.py:560
  117.5 22.7 %copy-start.45 = (bf16[128,768]{1,0:T(8,128)(2,1)}, bf16[128,768]{1,0:T(8,128)(2,1)S(1)}, u32[]{:S(2)}) copy-start(bf16[128,768]{1,0:T(8,128)(2,1)S(1)} %get-tuple-element.73) | copy-start | bytes 589828
  141.0 1.9 collective-permute-start.18
  170.6 21.6 %copy-start.37 = (bf16[128,768]{1,0:T(8,128)(2,1)}, bf16[128,768]{1,0:T(8,128)(2,1)S(1)}, u32[]{:S(2)}) copy-start(bf16[128,768]{1,0:T(8,128)(2,1)S(1)} %get-tuple-element.55) | copy-start | bytes 589828
  170.6 21.6 %copy-start.51 = (bf16[128,768]{1,0:T(8,128)(2,1)}, bf16[128,768]{1,0:T(8,128)(2,1)S(1)}, u32[]{:S(2)}) copy-start(bf16[128,768]{1,0:T(8,128)(2,1)S(1)} %get-tuple-element.74) | copy-start | bytes 589828
  190.6 1.6 collective-permute-start.19
  193.3 19.1 %all-to-all-start.3 = ((bf16[16,144,128]{2,1,0:T(8,128)(2,1)}), bf16[16,144,128]{2,1,0:T(8,128)(2,1)S(1)}, u32[]{:S(2)}, u32[]{:S(2)}) async-start(bf16[16,144,128]{2,1,0:T(8,128)(2,1)} %add_convert_fusion), calls=%async_computation.3 | async-start | bytes 1179648 | tf_op jit(solution)/shard_map/all_to_all | solution.py:556
  217.1 8.9 %collective-permute-start.20 = (bf16[128,768]{1,0:T(8,128)(2,1)S(1)}, bf16[128,768]{1,0:T(8,128)(2,1)S(1)}, u32[]{:S(2)}, u32[]{:S(2)}) collective-permute-start(bf16[128,768]{1,0:T(8,128)(2,1)S(1)} %get-tuple-element.61), channel_id=1, source_target_pairs={{16,0},{17,1},{18,2},{19,3},{20,4},{21,5},{22,6},{23,7},{24,8},{25... | collective-permute-start | bytes 589832 | tf_op jit(solution)/shard_map/ppermute | solution.py:560
  236.0 32.6 %collective-permute-start.27 = (bf16[128,3840]{1,0:T(8,128)(2,1)}, bf16[128,3840]{1,0:T(8,128)(2,1)}, u32[]{:S(2)}, u32[]{:S(2)}) collective-permute-start(bf16[128,3840]{1,0:T(8,128)(2,1)} %pad_maximum_fusion.1), channel_id=1, source_target_pairs={{0,2},{1,3},{2,0},{3,1},{4,6},{5,7},{6,4},{7,5},{8,10},{9,11},{10,... | collective-permute-start | bytes 2949128 | tf_op jit(solution)/shard_map/ppermute | solution.py:564
  240.7 8.8 %collective-permute-start.23 = (bf16[1,4,216,128]{3,2,1,0:T(8,128)(2,1)S(1)}, bf16[1,4,216,128]{3,2,1,0:T(8,128)(2,1)S(1)}, u32[]{:S(2)}, u32[]{:S(2)}) collective-permute-start(bf16[1,4,216,128]{3,2,1,0:T(8,128)(2,1)S(1)} %get-tuple-element.100), channel_id=1, source_target_pairs={{0,1},{1,0},{2,3},{3,2},{4,5},{5,4},{6,7},{7,6},{8,9},{9,8},{10,11... | collective-permute-start | bytes 663560 | tf_op jit(solution)/shard_map/ppermute | solution.py:564
  240.7 27.9 %collective-permute-start.24 = (bf16[1,4,216,128]{3,2,1,0:T(8,128)(2,1)S(1)}, bf16[1,4,216,128]{3,2,1,0:T(8,128)(2,1)S(1)}, u32[]{:S(2)}, u32[]{:S(2)}) collective-permute-start(bf16[1,4,216,128]{3,2,1,0:T(8,128)(2,1)S(1)} %get-tuple-element.99), channel_id=1, source_target_pairs={{0,2},{1,3},{2,0},{3,1},{4,6},{5,7},{6,4},{7,5},{8,10},{9,11},{10,... | collective-permute-start | bytes 663560 | tf_op jit(solution)/shard_map/ppermute | solution.py:564
  245.1 28.4 %collective-permute-start.21 = (bf16[128,1536]{1,0:T(8,128)(2,1)S(1)}, bf16[128,1536]{1,0:T(8,128)(2,1)S(1)}, u32[]{:S(2)}, u32[]{:S(2)}) collective-permute-start(bf16[128,1536]{1,0:T(8,128)(2,1)S(1)} %get-tuple-element.69), channel_id=1, source_target_pairs={{1,0},{2,1},{3,2},{4,3},{5,4},{6,5},{7,6},{8,7},{9,8},{10,9},{11,1... | collective-permute-start | bytes 1179656 | tf_op jit(solution)/shard_map/ppermute | solution.py:850
  246.4 27.1 %collective-permute-start.22 = (bf16[128,1536]{1,0:T(8,128)(2,1)S(1)}, bf16[128,1536]{1,0:T(8,128)(2,1)S(1)}, u32[]{:S(2)}, u32[]{:S(2)}) collective-permute-start(bf16[128,1536]{1,0:T(8,128)(2,1)S(1)} %get-tuple-element.70), channel_id=1, source_target_pairs={{0,1},{1,2},{2,3},{3,4},{4,5},{5,6},{6,7},{7,8},{8,9},{9,10},{10,1... | collective-permute-start | bytes 1179656 | tf_op jit(solution)/shard_map/ppermute | solution.py:851
  249.5 23.9 %collective-permute-start.25 = (bf16[1,4,216,128]{3,2,1,0:T(8,128)(2,1)S(1)}, bf16[1,4,216,128]{3,2,1,0:T(8,128)(2,1)S(1)}, u32[]{:S(2)}, u32[]{:S(2)}) collective-permute-start(bf16[1,4,216,128]{3,2,1,0:T(8,128)(2,1)S(1)} %get-tuple-element.98), channel_id=1, source_target_pairs={{0,3},{1,2},{2,1},{3,0},{4,7},{5,6},{6,5},{7,4},{8,11},{9,10},{10,... | collective-permute-start | bytes 663560 | tf_op jit(solution)/shard_map/ppermute | solution.py:564
  268.6 6.2 %collective-permute-start.26 = (bf16[128,3840]{1,0:T(8,128)(2,1)}, bf16[128,3840]{1,0:T(8,128)(2,1)S(1)}, u32[]{:S(2)}, u32[]{:S(2)}) collective-permute-start(bf16[128,3840]{1,0:T(8,128)(2,1)} %pad_maximum_fusion.1), channel_id=1, source_target_pairs={{0,1},{1,0},{2,3},{3,2},{4,5},{5,4},{6,7},{7,6},{8,9},{9,8},{10,11... | collective-permute-start | bytes 2949128 | tf_op jit(solution)/shard_map/ppermute | solution.py:564
  268.6 6.2 %collective-permute-start.28 = (bf16[128,3840]{1,0:T(8,128)(2,1)}, bf16[128,3840]{1,0:T(8,128)(2,1)S(1)}, u32[]{:S(2)}, u32[]{:S(2)}) collective-permute-start(bf16[128,3840]{1,0:T(8,128)(2,1)} %collective-permute-done.27), channel_id=1, source_target_pairs={{0,1},{1,0},{2,3},{3,2},{4,5},{5,4},{6,7},{7,6},{8,9},{9,8},{10,11... | collective-permute-start | bytes 2949128 | tf_op jit(solution)/shard_map/ppermute | solution.py:564
  287.6 42.9 %all-to-all-start.5 = ((bf16[4,1,264,768]{3,2,1,0:T(8,128)(2,1)}), bf16[4,1,264,768]{3,2,1,0:T(8,128)(2,1)}, u32[]{:S(2)}, u32[]{:S(2)}) async-start(bf16[4,1,264,768]{3,2,1,0:T(8,128)(2,1)} %bitcast.146), calls=%async_computation.5 | async-start | bytes 3244032 | tf_op jit(solution)/shard_map/all_to_all | solution.py:622
  292.1 18.7 %collective-permute-start.30 = (bf16[128,2304]{1,0:T(8,128)(2,1)S(1)}, bf16[128,2304]{1,0:T(8,128)(2,1)S(1)}, u32[]{:S(2)}, u32[]{:S(2)}) collective-permute-start(bf16[128,2304]{1,0:T(8,128)(2,1)S(1)} %copy-done.65), channel_id=1, source_target_pairs={{0,2},{1,3},{2,0},{3,1},{4,6},{5,7},{6,4},{7,5},{8,10},{9,11},{10,... | collective-permute-start | bytes 1769480 | tf_op jit(solution)/shard_map/ppermute | solution.py:564
  301.5 15.2 %collective-permute-start.29 = (bf16[128,2304]{1,0:T(8,128)(2,1)S(1)}, bf16[128,2304]{1,0:T(8,128)(2,1)S(1)}, u32[]{:S(2)}, u32[]{:S(2)}) collective-permute-start(bf16[128,2304]{1,0:T(8,128)(2,1)S(1)} %copy-done.65), channel_id=1, source_target_pairs={{0,1},{1,0},{2,3},{3,2},{4,5},{5,4},{6,7},{7,6},{8,9},{9,8},{10,11... | collective-permute-start | bytes 1769480 | tf_op jit(solution)/shard_map/ppermute | solution.py:564
  310.8 5.9 %collective-permute-start.31 = (bf16[128,2304]{1,0:T(8,128)(2,1)S(1)}, bf16[128,2304]{1,0:T(8,128)(2,1)S(1)}, u32[]{:S(2)}, u32[]{:S(2)}) collective-permute-start(bf16[128,2304]{1,0:T(8,128)(2,1)S(1)} %collective-permute-done.30), channel_id=1, source_target_pairs={{0,1},{1,0},{2,3},{3,2},{4,5},{5,4},{6,7},{7,6},{8,9},{9,8},{10,11... | collective-permute-start | bytes 1769480 | tf_op jit(solution)/shard_map/ppermute | solution.py:564
  310.8 2.0 collective-permute-start.32
  312.8 3.7 %collective-permute-start.33 = (f32[2,768]{1,0:T(2,128)S(1)}, f32[2,768]{1,0:T(2,128)S(1)}, u32[]{:S(2)}, u32[]{:S(2)}) collective-permute-start(f32[2,768]{1,0:T(2,128)S(1)} %fusion.47), channel_id=1, source_target_pairs={{0,2},{1,3},{2,0},{3,1},{4,6},{5,7},{6,4},{7,5},{8,10},{9,11},{10,... | collective-permute-start | bytes 18440 | tf_op jit(solution)/shard_map/ppermute | solution.py:564
  330.5 29.1 %all-to-all-start.4 = ((bf16[4,1,160,768]{3,2,1,0:T(8,128)(2,1)}), bf16[4,1,160,768]{3,2,1,0:T(8,128)(2,1)S(1)}, u32[]{:S(2)}, u32[]{:S(2)}) async-start(bf16[4,1,160,768]{3,2,1,0:T(8,128)(2,1)} %fusion.11), calls=%async_computation.4 | async-start | bytes 1966080 | tf_op jit(solution)/shard_map/all_to_all | solution.py:622
  (57 other events, 376.9 us)
Sparse Core Ops, SparseCore 0:
  20.3 72.6 all-gather.1
where the time goes:
time: 369 us; the launch traced here: 368 us
  waiting for transfers between devices  130 us (35%)
  Pallas kernels  53.1 us (14%)
  starting transfers between devices  48.2 us (13%)
  blocking collectives  46 us (12%)
  local copies, waits for them, and re-layouts  43.6 us (12%)
  other arithmetic  25.1 us (7%)
  between operations  15.4 us (4%)
  matrix products  6.26 us (2%)
    pallas_call x12, Pallas kernels, on_core(): pl.pallas_call(body, out_shape=[jax.ShapeDtypeStruct(shape, dtype) for sh...  53.1 us
    ppermute x28, waiting for transfers between devices, partner(): return lax.ppermute(rows, 'dp', [(i, i ^ apart) for i in range(count)])  51.8 us
    all_to_all x3, blocking collectives, exchange(): return lax.all_to_all(blocks, 'dp', 0, 0, axis_index_groups=groups)  46 us
    all_to_all x2, waiting for transfers between devices, sum_planes(): lax.all_to_all(blocks.astype(BF), 'dp', 0, 0, axis_index_groups=groups)  31.3 us
    ppermute x28, starting transfers between devices, partner(): return lax.ppermute(rows, 'dp', [(i, i ^ apart) for i in range(count)])  24.3 us
    all_gather x1, waiting for transfers between devices, on_device(): lax.all_gather(jnp.concatenate([attn_out_weight[0], mlp_in_weight[0], mlp...  23 us
    unnamed x139, local copies, waits for them, and re-layouts  13.5 us
    all_to_all x1, waiting for transfers between devices, exchange(): return lax.all_to_all(blocks, 'dp', 0, 0, axis_index_groups=groups)  12.2 us
  transfers between devices with their start and end apart: 38, of which 17 were waited for; matrix products, arithmetic and copies ran while one was open for 10% of the time, Pallas kernels for 4%

commit v1 on v0

--- a/solution.py
+++ b/solution.py
@@ -59,14 +59,16 @@
     return jnp.tile(jnp.stack([cosine, to_first, to_second]), (1, 2, 2))
 
 
-def on_core(body, outs, args, scratch=()):
+def on_core(body, outs, args, scratch=(), spaces=None):
     return pl.pallas_call(
         body,
         out_shape=[jax.ShapeDtypeStruct(shape, dtype) for shape, dtype in outs],
-        in_specs=[pl.BlockSpec(memory_space=pltpu.VMEM)] * len(args),
+        in_specs=[
+            pl.BlockSpec(memory_space=space) for space in spaces or [pltpu.VMEM] * len(args)
+        ],
         out_specs=[pl.BlockSpec(memory_space=pltpu.VMEM)] * len(outs),
         scratch_shapes=scratch,
-        compiler_params=pltpu.CompilerParams(vmem_limit_bytes=48 * 2**20),
+        compiler_params=pltpu.CompilerParams(vmem_limit_bytes=24 * 2**20),
     )(*args)
 
 
@@ -200,7 +202,7 @@
 
 def mlp_forward(layer_in, attended, gain, wide_ref, out_ref):
     width = layer_in.shape[1]
-    inner = wide_ref.shape[1] - width - out_ref.shape[0] * width // wide_ref.shape[0]
+    inner = wide_ref.shape[1] - width
     middle = layer_in + dot(attended, wide_ref[:, :width])
     xhat, _ = moments(middle)
     normed = (xhat * gain).astype(BF)
@@ -230,10 +232,9 @@
     return d_gate_up, gain_grad, d_middle, d_attn, d_attended
 
 
-def project(x_ref, gain_ref, first_ref, table_ref, normed_ref):
-    width = x_ref.shape[1]
-    xhat, _ = moments(x_ref[...].astype(F32))
-    normed = (xhat * gain_ref[...]).astype(BF)
+def project(xhat, gain, first_ref, table_ref, normed_ref):
+    width = xhat.shape[1]
+    normed = (xhat * gain).astype(BF)
     normed_ref[...] = normed
     tables = [table_ref[i] for i in range(3)]
     queries = chunks_of(dot(normed, first_ref[:, :width]))
@@ -249,8 +250,22 @@
     grad_ref[...] = (d_middle + norm_back(d_normed, gain_ref[...], xhat, scale)).astype(BF)
 
 
-def local_project_body(x_ref, gain_ref, first_ref, table_ref, normed_ref, q_ref, kv_ref):
-    queries, keys, values = project(x_ref, gain_ref, first_ref, table_ref, normed_ref)
+def local_project_body(place_ref, x_ref, table_ref, *refs):
+    pieces, (first_ref, extra_ref, normed_ref, q_ref, kv_ref, sem) = refs[:-6], refs[-6:]
+    rows = pieces[0].shape[0]
+    copies = []
+    for apart, piece in enumerate(pieces):
+        start = pl.multiple_of((place_ref[0] ^ apart) * rows, rows) if len(pieces) > 1 else 0
+        copies.append(
+            pltpu.make_async_copy(piece, first_ref.at[pl.ds(start, rows)], sem.at[apart])
+        )
+        copies[-1].start()
+    xhat, _ = moments(x_ref[...].astype(F32))
+    for copy in copies:
+        copy.wait()
+    extra = first_ref[:, first_ref.shape[1] - LANES :].astype(F32).T
+    extra_ref[...] = extra[: extra_ref.shape[0]]
+    queries, keys, values = project(xhat, extra[:1], first_ref, table_ref, normed_ref)
     width = values.shape[1]
     for j, (q, k) in enumerate(zip(queries, keys)):
         q_ref[:, LANES * j : LANES * (j + 1)] = q.astype(BF)
@@ -371,7 +386,8 @@
 
 
 def global_project_body(x_ref, gain_ref, first_ref, table_ref, normed_ref, sent_ref):
-    queries, keys, values = project(x_ref, gain_ref, first_ref, table_ref, normed_ref)
+    xhat, _ = moments(x_ref[...].astype(F32))
+    queries, keys, values = project(xhat, gain_ref[...], first_ref, table_ref, normed_ref)
     pack_pairs(queries, keys, sent_ref)
     pack_folded(chunks_of(values), sent_ref, sent_ref.shape[1] * 2 // 3)
 
@@ -564,27 +580,32 @@
     return lax.ppermute(rows, "dp", [(i, i ^ apart) for i in range(count)])
 
 
-def gather_group(piece, group_pos, count):
+def group_pieces(piece, count, hold=None):
     pieces = {0: piece}
     for apart in (4, 8, 12):
         pieces[apart] = partner(piece, apart, count)
+    held = [pieces[apart] for apart in (4, 8, 12)]
+    if hold is not None:
+        held, hold = lax.optimization_barrier((held, hold))
+        for apart, item in zip((4, 8, 12), held):
+            pieces[apart] = item
     for apart in (0, 4, 8, 12):
         pieces[apart + 2] = partner(pieces[apart], 2, count)
     for apart in range(0, GROUP, 2):
         pieces[apart + 1] = partner(pieces[apart], 1, count)
-    whole = jnp.zeros((GROUP,) + piece.shape, piece.dtype)
-    for apart, item in pieces.items():
-        start = (group_pos ^ apart,) + (0,) * piece.ndim
+    return [pieces[apart] for apart in range(GROUP)], hold
+
+
+def in_order(pieces, group_pos, count):
+    shape = pieces[0].shape
+    whole = jnp.zeros((GROUP,) + shape, pieces[0].dtype)
+    for apart, item in enumerate(pieces):
+        start = (group_pos ^ apart,) + (0,) * len(shape)
         whole = lax.dynamic_update_slice(whole, item[None], start)
-    return whole
-
-
-def gather_rows(piece, group_pos, count):
-    whole = gather_group(piece, group_pos, count)
     if count > GROUP:
         groups = [list(range(s, count, GROUP)) for s in range(GROUP)]
         whole = lax.all_gather(whole, "dp", axis=0, tiled=True, axis_index_groups=groups)
-    return whole.reshape(-1, piece.shape[-1])
+    return whole.reshape(-1, shape[-1])
 
 
 def plane_rows(rows, group_pos, count):
@@ -593,38 +614,42 @@
     taken = []
     for apart in range(4):
         block = lax.dynamic_index_in_dim(parts, place ^ apart, 2, keepdims=False)
-        taken.append(partner(block, apart, count) if apart else block)
-    return jnp.concatenate(taken, -1).swapaxes(0, 1)
-
-
-def plane_tokens(rows, count):
-    across = partner(rows, 2, count)
-    beside = partner(rows, 1, count)
-    return jnp.concatenate([rows, beside, across, partner(across, 1, count)], 0)
-
-
-def plane_product(left, right):
-    planes, groups, rows, tokens = left.shape
-    product = dot(left.reshape(-1, tokens), right)
-    return product.reshape(planes, groups, rows, -1)
-
-
-def stacked_columns(blocks, width):
-    return jnp.concatenate(
-        [blocks[..., c : c + width] for c in range(0, blocks.shape[-1], width)], -2
-    )
+        taken.append((partner(block, apart, count) if apart else block).swapaxes(0, 1))
+    return taken
+
+
+def product_body(*refs):
+    out_ref = refs[-1]
+    column = 0
+    for start in range(0, len(refs) - 1, 8):
+        left = jnp.concatenate([ref[...] for ref in refs[start : start + 4]], 1)
+        right = jnp.concatenate([ref[...] for ref in refs[start + 4 : start + 8]], 0)
+        end = column + right.shape[1]
+        out_ref[:, column:end] = dot(left, right).astype(BF)
+        column = end
+
+
+def plane_product(terms):
+    planes, groups, rows, tokens = terms[0][0][0].shape
+    args = [
+        part
+        for lefts, rights in terms
+        for part in [item.reshape(-1, tokens) for item in lefts] + list(rights)
+    ]
+    columns = sum(rights[0].shape[1] for _, rights in terms)
+    (product,) = on_core(product_body, [((planes * groups * rows, columns), BF)], args)
+    return product.reshape(planes, groups, rows, columns)
 
 
 def sum_planes(blocks, count):
     groups = [
         [s + 4 * z + k for z in range(4)] for s in range(0, count, GROUP) for k in range(4)
     ]
-    got = lax.all_to_all(blocks.astype(BF), "dp", 0, 0, axis_index_groups=groups)
+    got = lax.all_to_all(blocks, "dp", 0, 0, axis_index_groups=groups)
     total = jnp.sum(got.astype(F32), 0)
     if count > GROUP:
         apart = [list(range(s, count, GROUP)) for s in range(GROUP)]
-        total = lax.psum_scatter(total, "dp", scatter_dimension=0, axis_index_groups=apart)
-        return total
+        return lax.psum_scatter(total, "dp", scatter_dimension=0, axis_index_groups=apart)
     return total[0]
 
 
@@ -645,34 +670,52 @@
     group_pos = replica % GROUP
     micro_count, row_count, width = tokens_in.shape
     shard = qkv_weight.shape[1]
-    wide = mlp_out_weight.shape[1] * width // shard
     own_ids = segment_ids.reshape(-1)
     id_columns = -(-own_ids.size // shard)
     ids = jnp.pad(own_ids.astype(BF), (0, id_columns * shard - own_ids.size))
     extra = jnp.concatenate(
         [attn_gain[0][:, None], mlp_gain[0][:, None], ids.reshape(shard, id_columns)], 1
     )
-    extra = jnp.pad(extra, ((0, 0), (0, 128 - extra.shape[1])))
+    extra = jnp.pad(extra, ((0, 0), (0, LANES - extra.shape[1])))
     second = lax.all_gather(
-        jnp.concatenate(
-            [attn_out_weight[0], mlp_in_weight[0], mlp_out_weight[0].reshape(shard, wide)], 1
-        ),
-        "dp",
-        axis=0,
-        tiled=True,
-    )
-    first = gather_rows(jnp.concatenate([qkv_weight[0], extra], 1), group_pos, count)
-    gain_attn = first[:, 3 * width].astype(F32)[None]
-    gain_mlp = first[:, 3 * width + 1].astype(F32)[None]
-    w_out = second[:, second.shape[1] - wide :].reshape(-1, width)
-    all_ids = first[:, 3 * width + 2 : 3 * width + 2 + id_columns].reshape(count, -1)
-    all_ids = lax.dynamic_slice_in_dim(all_ids, replica - group_pos, GROUP, 0)
-    all_ids = all_ids[:, : own_ids.size].reshape(GROUP, micro_count, row_count)
-    segments = all_ids.swapaxes(0, 1).reshape(micro_count, GROUP * row_count).astype(jnp.int32)
+        jnp.concatenate([attn_out_weight[0], mlp_in_weight[0]], 1), "dp", axis=0, tiled=True
+    )
+    pieces, late_weight = group_pieces(
+        jnp.concatenate([qkv_weight[0], extra], 1), count, mlp_out_weight[0]
+    )
+    if count > GROUP:
+        pieces = [in_order(pieces, group_pos, count)]
+    w_out = in_order(group_pieces(late_weight, count)[0], group_pos, count)
 
     positions = group_pos * row_count + jnp.arange(row_count)
     local_tables = angles(positions, local_log_base)
     global_tables = angles(positions, global_log_base)
+
+    rows = micro_count * row_count
+    inner = second.shape[1] - width
+    hidden = w_out.shape[0]
+    pairs = rows * width // (row_count * LANES)
+    in_0 = tokens_in.reshape(rows, width)
+    extra_rows = -(-(2 + id_columns) // 8) * 8
+    first, extra, normed_0, q_0, kv_0 = on_core(
+        local_project_body,
+        [
+            ((width, 3 * width + LANES), BF),
+            ((extra_rows, width), F32),
+            ((rows, width), BF),
+            ((rows, width), BF),
+            ((rows, 2 * width), BF),
+        ],
+        (group_pos[None], in_0, local_tables, *pieces),
+        [pltpu.SemaphoreType.DMA((len(pieces),))],
+        [pltpu.SMEM, pltpu.VMEM, pltpu.VMEM] + [pl.ANY] * len(pieces),
+    )
+    gain_attn, gain_mlp = extra[:1], extra[1:2]
+    all_ids = extra[2 : 2 + id_columns].reshape(id_columns, count, shard)
+    all_ids = lax.dynamic_slice_in_dim(all_ids, replica - group_pos, GROUP, 1)
+    all_ids = all_ids.transpose(1, 2, 0).reshape(GROUP, -1)
+    all_ids = all_ids[:, : own_ids.size].reshape(GROUP, micro_count, row_count)
+    segments = all_ids.swapaxes(0, 1).reshape(micro_count, GROUP * row_count).astype(jnp.int32)
 
     key_pos = positions[0] - row_count + jnp.arange(3 * row_count)
     around = jnp.pad(segments, ((0, 0), (row_count, row_count)), constant_values=-1)
@@ -689,16 +732,6 @@
     shared_seg = jnp.concatenate([mine, theirs])[:, None]
     own_seg = own_seg[:, None]
 
-    rows = micro_count * row_count
-    inner = second.shape[1] - width - wide
-    hidden = w_out.shape[0]
-    pairs = rows * width // (row_count * LANES)
-    in_0 = tokens_in.reshape(rows, width)
-    normed_0, q_0, kv_0 = on_core(
-        local_project_body,
-        [((rows, width), BF), ((rows, width), BF), ((rows, 2 * width), BF)],
-        (in_0, gain_attn, first, local_tables),
-    )
     up_pairs, down_pairs = neighbours(count, 1), neighbours(count, -1)
     around_0 = (
         lax.ppermute(kv_0, "dp", up_pairs),
@@ -793,11 +826,6 @@
     )
     sent = (sent.astype(F32) + back.astype(F32)).astype(BF)
     got = exchange(sent, count)
-    d_proj_1, grad_1, gain_attn_1 = on_core(
-        global_finish_body,
-        [((rows, 3 * width), BF), ((rows, width), BF), ((1, width), F32)],
-        (got, d_mid_1, in_1, gain_attn, first, global_tables),
-    )
 
     n1, att, n2, mixed = (
         jnp.where(lower, a, b).T.reshape(count, -1, micro_count * row_count)
@@ -808,9 +836,29 @@
             (mixed_0, mixed_1),
         )
     )
-    left = plane_rows(jnp.concatenate([n1, att, n2, mixed], 1), group_pos, count)
+    left = jnp.concatenate([n1, att, n2, mixed], 1)
+    left, got = lax.optimization_barrier((left, got))
+    left = plane_rows(left, group_pos, count)
+    n1, att, n2, mixed = (
+        [part[:, :, start:end] for part in left]
+        for start, end in (
+            (0, shard),
+            (shard, 2 * shard),
+            (2 * shard, 3 * shard),
+            (3 * shard, left[0].shape[2]),
+        )
+    )
+    d_proj_1, grad_1, gain_attn_1 = on_core(
+        global_finish_body,
+        [((rows, 3 * width), BF), ((rows, width), BF), ((1, width), F32)],
+        (got, d_mid_1, in_1, gain_attn, first, global_tables),
+    )
 
     up_0 = to_other_section(grad_1, -1)
+    d_mlp = jnp.where(lower, up_0, up_1)
+    across, beside = partner(d_mlp, 2, count), partner(d_mlp, 1, count)
+    d_mlp = [d_mlp, beside, across, partner(across, 1, count)]
+    out_blocks = plane_product([(mixed, d_mlp)])
     d_gu_0, gain_mlp_0, d_mid_0, d_attn_0, d_att_0 = on_core(
         local_back_middle_body,
         [
@@ -822,21 +870,9 @@
         ],
         (up_0, middle_0, gate_up_0, gain_mlp, second, w_out),
     )
-    d_gu, d_mlp, d_attn = (
-        jnp.where(lower, a, b)
-        for a, b in ((d_gu_0, d_gu_1), (up_0, up_1), (d_attn_0, d_attn_1))
-    )
-    right = plane_tokens(jnp.concatenate([d_gu, d_mlp, d_attn], 1), count)
-    early = jnp.concatenate(
-        [
-            stacked_columns(
-                plane_product(left[:, :, 2 * shard : 3 * shard], right[:, :inner]), width
-            ),
-            plane_product(left[:, :, 3 * shard :], right[:, inner : inner + width]),
-            plane_product(left[:, :, shard : 2 * shard], right[:, inner + width :]),
-        ],
-        2,
-    )
+    own = [jnp.where(lower, d_gu_0, d_gu_1), jnp.where(lower, d_attn_0, d_attn_1)]
+    beside = [partner(item, 1, count) for item in own]
+    across = [partner(item, 2, count) for item in own]
     dq_0, d_own, d_before, d_after = on_core(
         local_backward_body,
         [
@@ -849,17 +885,23 @@
     )
     from_after = lax.ppermute(d_before, "dp", down_pairs)
     from_before = lax.ppermute(d_after, "dp", up_pairs)
+    from_after, out_blocks = lax.optimization_barrier((from_after, out_blocks))
+    mlp_out_share = sum_planes(out_blocks, count)
     (d_proj_0,) = on_core(
         local_join_body,
         [((rows, 3 * width), BF)],
         (dq_0, d_own, from_after, from_before, local_tables),
     )
     d_proj = jnp.where(lower, d_proj_0, d_proj_1)
-    d_proj, early = lax.optimization_barrier((d_proj, early))
-    early = sum_planes(early, count)
-    late = stacked_columns(
-        plane_product(left[:, :, :shard], plane_tokens(d_proj, count)), width
-    )
+    d_proj, across = lax.optimization_barrier((d_proj, across))
+    far = [partner(item, 1, count) for item in across]
+    d_gu, d_attn = zip(own, beside, across, far)
+    in_blocks = plane_product([(n2, d_gu), (att, d_attn)])
+    in_share = sum_planes(in_blocks, count)
+    across = partner(d_proj, 2, count)
+    across, in_blocks = lax.optimization_barrier((across, in_blocks))
+    d_proj = [d_proj, partner(d_proj, 1, count), across, partner(across, 1, count)]
+    qkv_share = sum_planes(plane_product([(n1, d_proj)]), count)
     grad_0, gain_attn_0 = on_core(
         input_backward_body,
         [((rows, width), BF), ((1, width), F32)],
@@ -871,28 +913,21 @@
         jnp.concatenate([gain_attn_0, gain_mlp_0]),
         jnp.concatenate([gain_attn_1, gain_mlp_1]),
     )
-    gains = gains + partner(gains, 1, count)
-    gains = gains + partner(gains, 2, count)
-    gains = gains.reshape(2, count // GROUP, 4, 4, shard)
-    gains = lax.dynamic_index_in_dim(gains, group_pos % 4, 3, keepdims=False)
-    gains = jnp.pad(
-        gains.transpose(2, 1, 0, 3), ((0, 0), (0, 0), (0, 14), (0, width - shard))
-    )
-    late = sum_planes(jnp.concatenate([late, gains], 2), count)
-
-    def columns(rows, parts):
-        return jnp.concatenate([rows[p * shard : (p + 1) * shard] for p in range(parts)], 1)[None]
-
-    parts = inner // width
+    apart = 1
+    while apart < count:
+        gains = gains + partner(gains, apart, count)
+        apart *= 2
+    gains = lax.dynamic_slice_in_dim(gains, replica * shard, shard, 1)
+
     return (
         jnp.where(lower, out_0, out_1).reshape(1, micro_count, row_count, width),
         jnp.where(lower, grad_0, grad_1).reshape(1, micro_count, row_count, width),
-        columns(late, 3),
-        early[early.shape[0] - shard :][None],
-        columns(early, parts),
-        early[parts * shard : early.shape[0] - shard][None],
-        late[3 * shard, :shard][None],
-        late[3 * shard + 1, :shard][None],
+        qkv_share[None],
+        in_share[None, :, inner:],
+        in_share[None, :, :inner],
+        mlp_out_share[None],
+        gains[:1],
+        gains[1:],
     )
 
 

time: 369 us -> 367 us (level)
  starting transfers between devices: 48.2 us -> 73 us
  waiting for transfers between devices: 130 us -> 115 us
  blocking collectives: 46 us -> 53.8 us
  matrix products: 6.26 us -> 0 us
  other arithmetic: 25.1 us -> 19.1 us
  local copies, waits for them, and re-layouts: 43.6 us -> 39.4 us
  Pallas kernels: 53.1 us -> 49.1 us
    ppermute x28 -> x51, waiting for transfers between devices: 51.8 us -> 84.3 us  [partner(): return lax.ppermute(rows, 'dp', [(i, i ^ apart) for i in range(count)])]
    all_gather x1, waiting for transfers between devices: 23 us -> 0.01 us  [on_device(): lax.all_gather(jnp.concatenate([attn_out_weight[0], mlp_in_weight[0]], 1)...]
    ppermute x28 -> x51, starting transfers between devices: 24.3 us -> 41.9 us  [partner(): return lax.ppermute(rows, 'dp', [(i, i ^ apart) for i in range(count)])]
    all_to_all x2 -> x3, waiting for transfers between devices: 31.3 us -> 16.8 us  [sum_planes(): got = lax.all_to_all(blocks, 'dp', 0, 0, axis_index_groups=groups)]
    unnamed x139 -> x147, local copies, waits for them, and re-layouts: 13.5 us -> 23.6 us
    dynamic_update_slice x15 -> x16, local copies, waits for them, and re-layouts: 10.7 us -> 1.15 us  [in_order(): whole = lax.dynamic_update_slice(whole, item[None], start)]
    all_to_all x3, blocking collectives: 46 us -> 53.8 us  [exchange(): return lax.all_to_all(blocks, 'dp', 0, 0, axis_index_groups=groups)]
    all_to_all x1, waiting for transfers between devices: 12.2 us -> 5.55 us  [exchange(): return lax.all_to_all(blocks, 'dp', 0, 0, axis_index_groups=groups)]
  transfers between devices with their start and end apart: 38 -> 62, of which waited for: 17 -> 26; matrix products, arithmetic and copies ran while one was open for 10% -> 8% of each run, Pallas kernels for 4% -> 7%
where the time goes in v1:
time: 367 us; the launch traced here: 365 us
  waiting for transfers between devices  115 us (31%)
  starting transfers between devices  73 us (20%)
  blocking collectives  53.8 us (15%)
  Pallas kernels  49.1 us (13%)
  local copies, waits for them, and re-layouts  39.4 us (11%)
  other arithmetic  19.1 us (5%)
  between operations  15.5 us (4%)
    ppermute x51, waiting for transfers between devices, partner(): return lax.ppermute(rows, 'dp', [(i, i ^ apart) for i in range(count)])  84.3 us
    all_to_all x3, blocking collectives, exchange(): return lax.all_to_all(blocks, 'dp', 0, 0, axis_index_groups=groups)  53.8 us
    pallas_call x15, Pallas kernels, on_core(): pl.pallas_call(body, out_shape=[jax.ShapeDtypeStruct(shape, dtype) for sh...  49.1 us
    ppermute x51, starting transfers between devices, partner(): return lax.ppermute(rows, 'dp', [(i, i ^ apart) for i in range(count)])  41.9 us
    unnamed x147, local copies, waits for them, and re-layouts  23.6 us
    all_to_all x3, waiting for transfers between devices, sum_planes(): got = lax.all_to_all(blocks, 'dp', 0, 0, axis_index_groups=groups)  16.8 us
    all_to_all x3, starting transfers between devices, sum_planes(): got = lax.all_to_all(blocks, 'dp', 0, 0, axis_index_groups=groups)  14 us
    ppermute x2, waiting for transfers between devices, to_other_section(): return lax.ppermute(rows, 'section', [(0, 1)] if step > 0 else [(1, 0)])  8.5 us
  transfers between devices with their start and end apart: 62, of which 26 were waited for; matrix products, arithmetic and copies ran while one was open for 8% of the time, Pallas kernels for 7%

profile of v1, /device:TPU:0, one launch (start us, length us, event | category | flops | bytes accessed | tf_op | source)
XLA Modules:
  0.0 365.2 jit_solution(17223841129839970386)
XLA Ops:
  12.4 5.1 %collective-permute-start.5 = (bf16[48,2432]{1,0:T(8,128)(2,1)S(1)}, bf16[48,2432]{1,0:T(8,128)(2,1)S(1)}, u32[]{:S(2)}, u32[]{:S(2)}) collective-permute-start(bf16[48,2432]{1,0:T(8,128)(2,1)S(1)} %pad_maximum_fusion.3.refs_0_), channel_id=1, source_target_pairs={{0,12},{1,13},{2,14},{3,15},{4,8},{5,9},{6,10},{7,11},{8,4},{9,5},... | collective-permute-start | bytes 700424 | tf_op jit(solution)/shard_map/ppermute | solution.py:580
  21.7 3.3 collective-permute-done.5.refs_12_
  25.0 21.9 %collective-permute-done.4.refs_8_ = bf16[48,2432]{1,0:T(8,128)(2,1)S(1)} collective-permute-done((bf16[48,2432]{1,0:T(8,128)(2,1)S(1)}, bf16[48,2432]{1,0:T(8,128)(2,1)S(1)}, u32[]{:S(2)}, u32[]{:S(2)}) %collective-permute-start.4) | collective-permute-done | bytes 233504 | tf_op jit(solution)/shard_map/ppermute | solution.py:580
  49.5 2.4 collective-permute-done.20
  53.2 2.4 collective-permute-start.22
  57.1 9.9 %collective-permute-done.24 = bf16[72,768]{1,0:T(8,128)(2,1)S(1)} collective-permute-done((bf16[72,768]{1,0:T(8,128)(2,1)}, bf16[72,768]{1,0:T(8,128)(2,1)S(1)}, u32[]{:S(2)}, u32[]{:S(2)}) %collective-permute-start.24) | collective-permute-done | bytes 110624 | tf_op jit(solution)/shard_map/ppermute | solution.py:580
  71.6 4.3 %collective-permute-done.28 = bf16[72,768]{1,0:T(8,128)(2,1)S(1)} collective-permute-done((bf16[72,768]{1,0:T(8,128)(2,1)}, bf16[72,768]{1,0:T(8,128)(2,1)S(1)}, u32[]{:S(2)}, u32[]{:S(2)}) %collective-permute-start.28) | collective-permute-done | bytes 110624 | tf_op jit(solution)/shard_map/ppermute | solution.py:580
  81.2 2.4 collective-permute-done.30
  85.6 3.0 collective-permute-done.10.refs_10_
  89.1 4.0 %collective-permute-done.13.refs_14_ = bf16[48,2432]{1,0:T(8,128)(2,1)S(1)} collective-permute-done((bf16[48,2432]{1,0:T(8,128)(2,1)S(1)}, bf16[48,2432]{1,0:T(8,128)(2,1)S(1)}, u32[]{:S(2)}, u32[]{:S(2)}) %collective-permute-start.13) | collective-permute-done | bytes 233504 | tf_op jit(solution)/shard_map/ppermute | solution.py:580
  95.9 5.7 %shard_map.152 = (bf16[768,2432]{1,0:T(8,128)(2,1)S(1)}, f32[8,768]{1,0:T(8,128)S(1)}, bf16[128,768]{1,0:T(8,128)(2,1)S(1)}, bf16[128,768]{1,0:T(8,128)(2,1)S(1)}, bf16[128,1536]{1,0:T(8,128)(2,1)S(1)}) custom-call(s32[1]{0:T(128)} %bitcast.1.place_ref, bf16[128,768]{1,0:T(8,128)(2,1)S(1)} %bitcast.126, f32[3,128,128]{2,1,0:T(8,128)S(1)} %tile.13.table_ref, ...), custom_call_target="tpu_custom_call" | custom-call | tf_op jit(solution)/shard_map/pallas_call | solution.py:63
  101.7 1.9 copy-done.2
  106.2 3.1 collective-permute-start.15
  113.0 3.6 shard_map.153
  117.3 2.3 copy-done
  120.6 2.2 shard_map.154
  124.6 3.3 collective-permute-start.32
  128.4 3.0 collective-permute-done.32.x_ref
  131.4 2.1 copy-done.3
  134.6 30.4 %all_to_all.35.got_ref = bf16[16,144,128]{2,1,0:T(8,128)(2,1)S(1)} all-to-all(bf16[16,144,128]{2,1,0:T(8,128)(2,1)S(1)} %get-tuple-element.71), channel_id=1, replica_groups={{0,1,2,3,4,5,6,7,8,9,10,11,12,13,14,15},{16,17,18,19,20,21,22,23,24,25,..., dimensions={0} | all-to-all | bytes 1179648 | tf_op jit(solution)/shard_map/all_to_all | solution.py:572
  167.7 7.0 %shard_map.156 = (bf16[16,48,128]{2,1,0:T(8,128)(2,1)S(1)}, f32[6,1,256]{2,1,0:T(1,128)S(1)}) custom-call(bf16[16,144,128]{2,1,0:T(8,128)(2,1)S(1)} %all_to_all.35.got_ref, bf16[16,64,128]{2,1,0:T(8,128)(2,1)} %collective-permute-done.33.other_ref, s32[1024,1]{1,0:T(8,128)S(1)} %copy.94.own_seg_ref, s32[1024,1]{1,0:T(8,128)S(1)} %copy.95.shared_seg_ref), custom_call_target="tpu_custom_call" | custom-call | tf_op jit(solution)/shard_map/pallas_call | solution.py:63
  174.7 11.8 %all_to_all.36.got_ref = bf16[16,48,128]{2,1,0:T(8,128)(2,1)S(1)} all-to-all(bf16[16,48,128]{2,1,0:T(8,128)(2,1)S(1)} %get-tuple-element.72), channel_id=1, replica_groups={{0,1,2,3,4,5,6,7,8,9,10,11,12,13,14,15},{16,17,18,19,20,21,22,23,24,25,..., dimensions={0} | all-to-all | bytes 393216 | tf_op jit(solution)/shard_map/all_to_all | solution.py:572
  186.4 2.3 copy-done.1
  188.8 4.2 %shard_map.157 = (bf16[128,768]{1,0:T(8,128)(2,1)S(1)}, bf16[128,768]{1,0:T(8,128)(2,1)S(1)}, bf16[128,768]{1,0:T(8,128)(2,1)S(1)}, bf16[128,1152]{1,0:T(8,128)(...) custom-call(bf16[16,48,128]{2,1,0:T(8,128)(2,1)S(1)} %all_to_all.36., ...), custom_call_target="tpu_custom_call" | custom-call | tf_op jit(solution)/shard_map/pallas_call | solution.py:63
  193.0 11.6 %all_to_all.37.d_ref = bf16[16,48,128]{2,1,0:T(8,128)(2,1)S(1)} all-to-all(bf16[16,48,128]{2,1,0:T(8,128)(2,1)S(1)} %get-tuple-element.82), channel_id=1, replica_groups={{0,1,2,3,4,5,6,7,8,9,10,11,12,13,14,15},{16,17,18,19,20,21,22,23,24,25,..., dimensions={0} | all-to-all | bytes 393216 | tf_op jit(solution)/shard_map/all_to_all | solution.py:572
  204.6 9.0 %shard_map.158 = (bf16[16,144,128]{2,1,0:T(8,128)(2,1)S(1)}, bf16[16,64,128]{2,1,0:T(8,128)(2,1)}) custom-call(bf16[16,144,128]{2,1,0:T(8,128)(2,1)S(1)} %all_to_all.35.got_ref, bf16[16,64,128]{2,1,0:T(8,128)(2,1)} %collective-permute-done.33.other_ref, s32[1024,1]{1,0:T(8,128)S(1)} %copy.94.own_seg_ref, s32[1024,1]{1,0:T(8,128)S(1)} %copy.95.shared_seg_ref, ...), custom_call_target="tpu_custom_call" | custom-call | tf_op jit(solution)/shard_map/pallas_call | solution.py:63
  216.3 2.2 add_convert_fusion
  218.5 3.6 all-to-all-start.3
  229.8 2.2 pad_maximum_fusion
  232.0 5.6 %all-to-all-done.3.got_ref = bf16[16,144,128]{2,1,0:T(8,128)(2,1)S(1)} async-done(((bf16[16,144,128]{2,1,0:T(8,128)(2,1)}), bf16[16,144,128]{2,1,0:T(8,128)(2,1)S(1)}, u32[]{:S(2)}, u32[]{:S(2)}) %all-to-all-start.3) | async-done | bytes 589856 | tf_op jit(solution)/shard_map/all_to_all | solution.py:572
  239.1 2.2 copy-done.4
  247.1 5.5 %collective-permute-done.35.up_ref = bf16[128,768]{1,0:T(8,128)(2,1)S(1)} collective-permute-done((bf16[128,768]{1,0:T(8,128)(2,1)S(1)}, bf16[128,768]{1,0:T(8,128)(2,1)S(1)}, u32[]{:S(2)}, u32[]{:S(2)}) %collective-permute-start.35) | collective-permute-done | bytes 196640 | tf_op jit(solution)/shard_map/ppermute | solution.py:576
  254.1 2.9 shard_map.160
  257.1 4.2 %shard_map.161 = (bf16[128,768]{1,0:T(8,128)(2,1)S(1)}, f32[128,1536]{1,0:T(8,128)S(1)}, bf16[128,1536]{1,0:T(8,128)(2,1)S(1)}, bf16[128,1536]{1,0:T(8,128)(2,1)}) custom-call(bf16[128,768]{1,0:T(8,128)(2,1)S(1)} %copy-done.32, bf16[128,1536]{1,0:T(8,128)(2,1)S(1)} %copy-done.22, bf16[128,1536]{1,0:T(8,128)(2,1)S(1)} %copy-done.18, ...), custom_call_target="tpu_custom_call" | custom-call | tf_op jit(solution)/shard_map/pallas_call | solution.py:63
  262.7 3.1 collective-permute-start.43
  271.9 6.0 %all-to-all-start.6 = ((bf16[4,1,72,768]{3,2,1,0:T(8,128)(2,1)}), bf16[4,1,72,768]{3,2,1,0:T(8,128)(2,1)}, u32[]{:S(2)}, u32[]{:S(2)}) async-start(bf16[4,1,72,768]{3,2,1,0:T(8,128)(2,1)} %bitcast.80), calls=%async_computation.6 | async-start | bytes 884736 | tf_op jit(solution)/shard_map/all_to_all | solution.py:648
  280.1 8.1 %collective-permute-done.44.refs_6_ = bf16[128,2304]{1,0:T(8,128)(2,1)} collective-permute-done((bf16[128,2304]{1,0:T(8,128)(2,1)S(1)}, bf16[128,2304]{1,0:T(8,128)(2,1)}, u32[]{:S(2)}, u32[]{:S(2)}) %collective-permute-start.44) | collective-permute-done | bytes 589856 | tf_op jit(solution)/shard_map/ppermute | solution.py:580
  288.2 2.6 collective-permute-start.49
  291.0 1.9 collective-permute-done.51.refs_15_
  293.0 3.1 shard_map.165
  296.1 4.5 %all-to-all-start.5 = ((bf16[4,1,48,3072]{3,2,1,0:T(8,128)(2,1)}), bf16[4,1,48,3072]{3,2,1,0:T(8,128)(2,1)}, u32[]{:S(2)}, u32[]{:S(2)}) async-start(bf16[4,1,48,3072]{3,2,1,0:T(8,128)(2,1)} %bitcast.77), calls=%async_computation.5 | async-start | bytes 2359296 | tf_op jit(solution)/shard_map/all_to_all | solution.py:648
  300.6 2.3 collective-permute-start.47
  302.9 2.1 copy-done.5
  307.8 9.1 %collective-permute-done.54 = f32[2,768]{1,0:T(2,128)S(1)} collective-permute-done((f32[2,768]{1,0:T(2,128)S(1)}, f32[2,768]{1,0:T(2,128)S(1)}, u32[]{:S(2)}, u32[]{:S(2)}) %collective-permute-start.54) | collective-permute-done | bytes 6176 | tf_op jit(solution)/shard_map/ppermute | solution.py:580
  320.8 4.4 %collective-permute-start.56 = (f32[2,768]{1,0:T(2,128)S(1)}, f32[2,768]{1,0:T(2,128)S(1)}, u32[]{:S(2)}, u32[]{:S(2)}) collective-permute-start(f32[2,768]{1,0:T(2,128)S(1)} %add.181), channel_id=1, source_target_pairs={{0,8},{1,9},{2,10},{3,11},{4,12},{5,13},{6,14},{7,15},{8,0},{9,1},... | collective-permute-start | bytes 18440 | tf_op jit(solution)/shard_map/ppermute | solution.py:580
  325.9 4.2 %collective-permute-done.56 = f32[2,768]{1,0:T(2,128)S(1)} collective-permute-done((f32[2,768]{1,0:T(2,128)S(1)}, f32[2,768]{1,0:T(2,128)S(1)}, u32[]{:S(2)}, u32[]{:S(2)}) %collective-permute-start.56) | collective-permute-done | bytes 6176 | tf_op jit(solution)/shard_map/ppermute | solution.py:580
  331.8 3.5 all-to-all-start.4
  340.6 16.8 %all-to-all-done.4 = bf16[4,1,48,2304]{3,2,1,0:T(8,128)(2,1)S(1)} async-done(((bf16[4,1,48,2304]{3,2,1,0:T(8,128)(2,1)}), bf16[4,1,48,2304]{3,2,1,0:T(8,128)(2,1)S(1)}, u32[]{:S(2)}, u32[]{:S(2)}) %all-to-all-start.4) | async-done | bytes 884768 | tf_op jit(solution)/shard_map/all_to_all | solution.py:648
  (350 shorter events, 87.3 us)
Async XLA Ops:
  7.2 110.2 %all-gather.2.cloned.1.call-start = ((), (), s32[]{:S(2)}) async-start(), calls=%async_computation.7 | async-start | bytes 5013504 | tf_op jit(solution)/shard_map/all_gather | solution.py:680
  12.4 12.6 %collective-permute-start.5 = (bf16[48,2432]{1,0:T(8,128)(2,1)S(1)}, bf16[48,2432]{1,0:T(8,128)(2,1)S(1)}, u32[]{:S(2)}, u32[]{:S(2)}) collective-permute-start(bf16[48,2432]{1,0:T(8,128)(2,1)S(1)} %pad_maximum_fusion.3.refs_0_), channel_id=1, source_target_pairs={{0,12},{1,13},{2,14},{3,15},{4,8},{5,9},{6,10},{7,11},{8,4},{9,5},... | collective-permute-start | bytes 700424 | tf_op jit(solution)/shard_map/ppermute | solution.py:580
  17.6 29.3 %collective-permute-start.4 = (bf16[48,2432]{1,0:T(8,128)(2,1)S(1)}, bf16[48,2432]{1,0:T(8,128)(2,1)S(1)}, u32[]{:S(2)}, u32[]{:S(2)}) collective-permute-start(bf16[48,2432]{1,0:T(8,128)(2,1)S(1)} %pad_maximum_fusion.3.refs_0_), channel_id=1, source_target_pairs={{0,8},{1,9},{2,10},{3,11},{4,12},{5,13},{6,14},{7,15},{8,0},{9,1},... | collective-permute-start | bytes 700424 | tf_op jit(solution)/shard_map/ppermute | solution.py:580
  17.6 29.3 %collective-permute-start.3 = (bf16[48,2432]{1,0:T(8,128)(2,1)S(1)}, bf16[48,2432]{1,0:T(8,128)(2,1)S(1)}, u32[]{:S(2)}, u32[]{:S(2)}) collective-permute-start(bf16[48,2432]{1,0:T(8,128)(2,1)S(1)} %pad_maximum_fusion.3.refs_0_), channel_id=1, source_target_pairs={{0,4},{1,5},{2,6},{3,7},{4,0},{5,1},{6,2},{7,3},{8,12},{9,13},{10,... | collective-permute-start | bytes 700424 | tf_op jit(solution)/shard_map/ppermute | solution.py:580
  18.2 61.2 %collective-permute-start.1 = (bf16[48,2432]{1,0:T(8,128)(2,1)S(1)}, bf16[48,2432]{1,0:T(8,128)(2,1)}, u32[]{:S(2)}, u32[]{:S(2)}) collective-permute-start(bf16[48,2432]{1,0:T(8,128)(2,1)S(1)} %pad_maximum_fusion.3.refs_0_), channel_id=1, source_target_pairs={{0,2},{1,3},{2,0},{3,1},{4,6},{5,7},{6,4},{7,5},{8,10},{9,11},{10,... | collective-permute-start | bytes 700424 | tf_op jit(solution)/shard_map/ppermute | solution.py:580
  19.8 60.0 %collective-permute-start = (bf16[48,2432]{1,0:T(8,128)(2,1)S(1)}, bf16[48,2432]{1,0:T(8,128)(2,1)}, u32[]{:S(2)}, u32[]{:S(2)}) collective-permute-start(bf16[48,2432]{1,0:T(8,128)(2,1)S(1)} %pad_maximum_fusion.3.refs_0_), channel_id=1, source_target_pairs={{0,1},{1,0},{2,3},{3,2},{4,5},{5,4},{6,7},{7,6},{8,9},{9,8},{10,11... | collective-permute-start | bytes 700424 | tf_op jit(solution)/shard_map/ppermute | solution.py:580
  46.9 5.1 %collective-permute-start.20 = (bf16[72,768]{1,0:T(8,128)(2,1)}, bf16[72,768]{1,0:T(8,128)(2,1)S(1)}, u32[]{:S(2)}, u32[]{:S(2)}) collective-permute-start(bf16[72,768]{1,0:T(8,128)(2,1)} %bitcast.8), channel_id=1, source_target_pairs={{0,4},{1,5},{2,6},{3,7},{4,0},{5,1},{6,2},{7,3},{8,12},{9,13},{10,... | collective-permute-start | bytes 331784 | tf_op jit(solution)/shard_map/ppermute | solution.py:580
  46.9 6.3 %collective-permute-start.18 = (bf16[72,768]{1,0:T(8,128)(2,1)}, bf16[72,768]{1,0:T(8,128)(2,1)S(1)}, u32[]{:S(2)}, u32[]{:S(2)}) collective-permute-start(bf16[72,768]{1,0:T(8,128)(2,1)} %bitcast.8), channel_id=1, source_target_pairs={{0,2},{1,3},{2,0},{3,1},{4,6},{5,7},{6,4},{7,5},{8,10},{9,11},{10,... | collective-permute-start | bytes 331784 | tf_op jit(solution)/shard_map/ppermute | solution.py:580
  48.5 7.2 %collective-permute-start.17 = (bf16[72,768]{1,0:T(8,128)(2,1)}, bf16[72,768]{1,0:T(8,128)(2,1)S(1)}, u32[]{:S(2)}, u32[]{:S(2)}) collective-permute-start(bf16[72,768]{1,0:T(8,128)(2,1)} %bitcast.8), channel_id=1, source_target_pairs={{0,1},{1,0},{2,3},{3,2},{4,5},{5,4},{6,7},{7,6},{8,9},{9,8},{10,11... | collective-permute-start | bytes 331784 | tf_op jit(solution)/shard_map/ppermute | solution.py:580
  52.0 15.1 %collective-permute-start.24 = (bf16[72,768]{1,0:T(8,128)(2,1)}, bf16[72,768]{1,0:T(8,128)(2,1)S(1)}, u32[]{:S(2)}, u32[]{:S(2)}) collective-permute-start(bf16[72,768]{1,0:T(8,128)(2,1)} %bitcast.8), channel_id=1, source_target_pairs={{0,8},{1,9},{2,10},{3,11},{4,12},{5,13},{6,14},{7,15},{8,0},{9,1},... | collective-permute-start | bytes 331784 | tf_op jit(solution)/shard_map/ppermute | solution.py:580
  53.2 15.4 %collective-permute-start.22 = (bf16[72,768]{1,0:T(8,128)(2,1)S(1)}, bf16[72,768]{1,0:T(8,128)(2,1)S(1)}, u32[]{:S(2)}, u32[]{:S(2)}) collective-permute-start(bf16[72,768]{1,0:T(8,128)(2,1)S(1)} %collective-permute-done.20), channel_id=1, source_target_pairs={{0,2},{1,3},{2,0},{3,1},{4,6},{5,7},{6,4},{7,5},{8,10},{9,11},{10,... | collective-permute-start | bytes 331784 | tf_op jit(solution)/shard_map/ppermute | solution.py:580
  56.9 13.1 %collective-permute-start.21 = (bf16[72,768]{1,0:T(8,128)(2,1)S(1)}, bf16[72,768]{1,0:T(8,128)(2,1)S(1)}, u32[]{:S(2)}, u32[]{:S(2)}) collective-permute-start(bf16[72,768]{1,0:T(8,128)(2,1)S(1)} %collective-permute-done.20), channel_id=1, source_target_pairs={{0,1},{1,0},{2,3},{3,2},{4,5},{5,4},{6,7},{7,6},{8,9},{9,8},{10,11... | collective-permute-start | bytes 331784 | tf_op jit(solution)/shard_map/ppermute | solution.py:580
  67.0 8.8 %collective-permute-start.28 = (bf16[72,768]{1,0:T(8,128)(2,1)}, bf16[72,768]{1,0:T(8,128)(2,1)S(1)}, u32[]{:S(2)}, u32[]{:S(2)}) collective-permute-start(bf16[72,768]{1,0:T(8,128)(2,1)} %bitcast.8), channel_id=1, source_target_pairs={{0,12},{1,13},{2,14},{3,15},{4,8},{5,9},{6,10},{7,11},{8,4},{9,5},... | collective-permute-start | bytes 331784 | tf_op jit(solution)/shard_map/ppermute | solution.py:580
  68.7 8.5 %collective-permute-start.26 = (bf16[72,768]{1,0:T(8,128)(2,1)S(1)}, bf16[72,768]{1,0:T(8,128)(2,1)S(1)}, u32[]{:S(2)}, u32[]{:S(2)}) collective-permute-start(bf16[72,768]{1,0:T(8,128)(2,1)S(1)} %collective-permute-done.24), channel_id=1, source_target_pairs={{0,2},{1,3},{2,0},{3,1},{4,6},{5,7},{6,4},{7,5},{8,10},{9,11},{10,... | collective-permute-start | bytes 331784 | tf_op jit(solution)/shard_map/ppermute | solution.py:580
  71.4 6.5 %collective-permute-start.25 = (bf16[72,768]{1,0:T(8,128)(2,1)S(1)}, bf16[72,768]{1,0:T(8,128)(2,1)S(1)}, u32[]{:S(2)}, u32[]{:S(2)}) collective-permute-start(bf16[72,768]{1,0:T(8,128)(2,1)S(1)} %collective-permute-done.24), channel_id=1, source_target_pairs={{0,1},{1,0},{2,3},{3,2},{4,5},{5,4},{6,7},{7,6},{8,9},{9,8},{10,11... | collective-permute-start | bytes 331784 | tf_op jit(solution)/shard_map/ppermute | solution.py:580
  75.9 9.1 %collective-permute-start.7 = (bf16[48,2432]{1,0:T(8,128)(2,1)S(1)}, bf16[48,2432]{1,0:T(8,128)(2,1)S(1)}, u32[]{:S(2)}, u32[]{:S(2)}) collective-permute-start(bf16[48,2432]{1,0:T(8,128)(2,1)S(1)} %collective-permute-done.3.refs_4_), channel_id=1, source_target_pairs={{0,2},{1,3},{2,0},{3,1},{4,6},{5,7},{6,4},{7,5},{8,10},{9,11},{10,... | collective-permute-start | bytes 700424 | tf_op jit(solution)/shard_map/ppermute | solution.py:580
  77.2 6.4 %collective-permute-start.30 = (bf16[72,768]{1,0:T(8,128)(2,1)S(1)}, bf16[72,768]{1,0:T(8,128)(2,1)S(1)}, u32[]{:S(2)}, u32[]{:S(2)}) collective-permute-start(bf16[72,768]{1,0:T(8,128)(2,1)S(1)} %collective-permute-done.28), channel_id=1, source_target_pairs={{0,2},{1,3},{2,0},{3,1},{4,6},{5,7},{6,4},{7,5},{8,10},{9,11},{10,... | collective-permute-start | bytes 331784 | tf_op jit(solution)/shard_map/ppermute | solution.py:580
  79.4 5.9 %collective-permute-start.6 = (bf16[48,2432]{1,0:T(8,128)(2,1)S(1)}, bf16[48,2432]{1,0:T(8,128)(2,1)S(1)}, u32[]{:S(2)}, u32[]{:S(2)}) collective-permute-start(bf16[48,2432]{1,0:T(8,128)(2,1)S(1)} %collective-permute-done.3.refs_4_), channel_id=1, source_target_pairs={{0,1},{1,0},{2,3},{3,2},{4,5},{5,4},{6,7},{7,6},{8,9},{9,8},{10,11... | collective-permute-start | bytes 700424 | tf_op jit(solution)/shard_map/ppermute | solution.py:580
  79.8 8.8 %collective-permute-start.10 = (bf16[48,2432]{1,0:T(8,128)(2,1)S(1)}, bf16[48,2432]{1,0:T(8,128)(2,1)S(1)}, u32[]{:S(2)}, u32[]{:S(2)}) collective-permute-start(bf16[48,2432]{1,0:T(8,128)(2,1)S(1)} %collective-permute-done.4.refs_8_), channel_id=1, source_target_pairs={{0,2},{1,3},{2,0},{3,1},{4,6},{5,7},{6,4},{7,5},{8,10},{9,11},{10,... | collective-permute-start | bytes 700424 | tf_op jit(solution)/shard_map/ppermute | solution.py:580
  83.6 5.0 %collective-permute-start.9 = (bf16[48,2432]{1,0:T(8,128)(2,1)S(1)}, bf16[48,2432]{1,0:T(8,128)(2,1)S(1)}, u32[]{:S(2)}, u32[]{:S(2)}) collective-permute-start(bf16[48,2432]{1,0:T(8,128)(2,1)S(1)} %collective-permute-done.4.refs_8_), channel_id=1, source_target_pairs={{0,1},{1,0},{2,3},{3,2},{4,5},{5,4},{6,7},{7,6},{8,9},{9,8},{10,11... | collective-permute-start | bytes 700424 | tf_op jit(solution)/shard_map/ppermute | solution.py:580
  83.6 9.5 %collective-permute-start.13 = (bf16[48,2432]{1,0:T(8,128)(2,1)S(1)}, bf16[48,2432]{1,0:T(8,128)(2,1)S(1)}, u32[]{:S(2)}, u32[]{:S(2)}) collective-permute-start(bf16[48,2432]{1,0:T(8,128)(2,1)S(1)} %collective-permute-done.5.refs_12_), channel_id=1, source_target_pairs={{0,2},{1,3},{2,0},{3,1},{4,6},{5,7},{6,4},{7,5},{8,10},{9,11},{10,... | collective-permute-start | bytes 700424 | tf_op jit(solution)/shard_map/ppermute | solution.py:580
  85.0 8.2 %collective-permute-start.31 = (bf16[72,768]{1,0:T(8,128)(2,1)S(1)}, bf16[72,768]{1,0:T(8,128)(2,1)S(1)}, u32[]{:S(2)}, u32[]{:S(2)}) collective-permute-start(bf16[72,768]{1,0:T(8,128)(2,1)S(1)} %collective-permute-done.30), channel_id=1, source_target_pairs={{0,1},{1,0},{2,3},{3,2},{4,5},{5,4},{6,7},{7,6},{8,9},{9,8},{10,11... | collective-permute-start | bytes 331784 | tf_op jit(solution)/shard_map/ppermute | solution.py:580
  85.3 8.4 %collective-permute-start.12 = (bf16[48,2432]{1,0:T(8,128)(2,1)S(1)}, bf16[48,2432]{1,0:T(8,128)(2,1)S(1)}, u32[]{:S(2)}, u32[]{:S(2)}) collective-permute-start(bf16[48,2432]{1,0:T(8,128)(2,1)S(1)} %collective-permute-done.5.refs_12_), channel_id=1, source_target_pairs={{0,1},{1,0},{2,3},{3,2},{4,5},{5,4},{6,7},{7,6},{8,9},{9,8},{10,11... | collective-permute-start | bytes 700424 | tf_op jit(solution)/shard_map/ppermute | solution.py:580
  88.6 5.1 %collective-permute-start.2 = (bf16[48,2432]{1,0:T(8,128)(2,1)}, bf16[48,2432]{1,0:T(8,128)(2,1)S(1)}, u32[]{:S(2)}, u32[]{:S(2)}) collective-permute-start(bf16[48,2432]{1,0:T(8,128)(2,1)} %collective-permute-done.1.refs_2_), channel_id=1, source_target_pairs={{0,1},{1,0},{2,3},{3,2},{4,5},{5,4},{6,7},{7,6},{8,9},{9,8},{10,11... | collective-permute-start | bytes 700424 | tf_op jit(solution)/shard_map/ppermute | solution.py:580
  88.6 5.1 %collective-permute-start.8 = (bf16[48,2432]{1,0:T(8,128)(2,1)S(1)}, bf16[48,2432]{1,0:T(8,128)(2,1)S(1)}, u32[]{:S(2)}, u32[]{:S(2)}) collective-permute-start(bf16[48,2432]{1,0:T(8,128)(2,1)S(1)} %collective-permute-done.7.refs_6_), channel_id=1, source_target_pairs={{0,1},{1,0},{2,3},{3,2},{4,5},{5,4},{6,7},{7,6},{8,9},{9,8},{10,11... | collective-permute-start | bytes 700424 | tf_op jit(solution)/shard_map/ppermute | solution.py:580
  104.9 6.9 %collective-permute-start.16 = (bf16[128,1536]{1,0:T(8,128)(2,1)S(1)}, bf16[128,1536]{1,0:T(8,128)(2,1)S(1)}, u32[]{:S(2)}, u32[]{:S(2)}) collective-permute-start(bf16[128,1536]{1,0:T(8,128)(2,1)S(1)} %get-tuple-element.65.own_ref), channel_id=1, source_target_pairs={{1,0},{2,1},{3,2},{4,3},{5,4},{6,5},{7,6},{8,7},{9,8},{10,9},{11,1... | collective-permute-start | bytes 1179656 | tf_op jit(solution)/shard_map/ppermute | solution.py:739
  106.2 5.6 %collective-permute-start.15 = (bf16[128,1536]{1,0:T(8,128)(2,1)S(1)}, bf16[128,1536]{1,0:T(8,128)(2,1)S(1)}, u32[]{:S(2)}, u32[]{:S(2)}) collective-permute-start(bf16[128,1536]{1,0:T(8,128)(2,1)S(1)} %get-tuple-element.65.own_ref), channel_id=1, source_target_pairs={{0,1},{1,2},{2,3},{3,4},{4,5},{5,6},{6,7},{7,8},{8,9},{9,10},{10,1... | collective-permute-start | bytes 1179656 | tf_op jit(solution)/shard_map/ppermute | solution.py:737
  124.6 6.8 %collective-permute-start.32 = (bf16[128,768]{1,0:T(8,128)(2,1)}, bf16[128,768]{1,0:T(8,128)(2,1)S(1)}, u32[]{:S(2)}, u32[]{:S(2)}) collective-permute-start(bf16[128,768]{1,0:T(8,128)(2,1)} %get-tuple-element.69), channel_id=1, source_target_pairs={{0,16},{1,17},{2,18},{3,19},{4,20},{5,21},{6,22},{7,23},{8,24},{9,... | collective-permute-start | bytes 589832 | tf_op jit(solution)/shard_map/ppermute | solution.py:576
  218.5 19.1 %all-to-all-start.3 = ((bf16[16,144,128]{2,1,0:T(8,128)(2,1)}), bf16[16,144,128]{2,1,0:T(8,128)(2,1)S(1)}, u32[]{:S(2)}, u32[]{:S(2)}) async-start(bf16[16,144,128]{2,1,0:T(8,128)(2,1)} %add_convert_fusion), calls=%async_computation.3 | async-start | bytes 1179648 | tf_op jit(solution)/shard_map/all_to_all | solution.py:572
  243.9 8.7 %collective-permute-start.35 = (bf16[128,768]{1,0:T(8,128)(2,1)S(1)}, bf16[128,768]{1,0:T(8,128)(2,1)S(1)}, u32[]{:S(2)}, u32[]{:S(2)}) collective-permute-start(bf16[128,768]{1,0:T(8,128)(2,1)S(1)} %get-tuple-element.87), channel_id=1, source_target_pairs={{16,0},{17,1},{18,2},{19,3},{20,4},{21,5},{22,6},{23,7},{24,8},{25... | collective-permute-start | bytes 589832 | tf_op jit(solution)/shard_map/ppermute | solution.py:576
  245.4 20.4 %collective-permute-start.39 = (bf16[1,4,216,128]{3,2,1,0:T(8,128)(2,1)S(1)}, bf16[1,4,216,128]{3,2,1,0:T(8,128)(2,1)S(1)}, u32[]{:S(2)}, u32[]{:S(2)}) collective-permute-start(bf16[1,4,216,128]{3,2,1,0:T(8,128)(2,1)S(1)} %get-tuple-element.116), channel_id=1, source_target_pairs={{0,3},{1,2},{2,1},{3,0},{4,7},{5,6},{6,5},{7,4},{8,11},{9,10},{10,... | collective-permute-start | bytes 663560 | tf_op jit(solution)/shard_map/ppermute | solution.py:580
  246.4 20.4 %collective-permute-start.38 = (bf16[1,4,216,128]{3,2,1,0:T(8,128)(2,1)S(1)}, bf16[1,4,216,128]{3,2,1,0:T(8,128)(2,1)S(1)}, u32[]{:S(2)}, u32[]{:S(2)}) collective-permute-start(bf16[1,4,216,128]{3,2,1,0:T(8,128)(2,1)S(1)} %get-tuple-element.117), channel_id=1, source_target_pairs={{0,2},{1,3},{2,0},{3,1},{4,6},{5,7},{6,4},{7,5},{8,10},{9,11},{10,... | collective-permute-start | bytes 663560 | tf_op jit(solution)/shard_map/ppermute | solution.py:580
  252.7 14.2 %collective-permute-start.41 = (bf16[128,768]{1,0:T(8,128)(2,1)S(1)}, bf16[128,768]{1,0:T(8,128)(2,1)S(1)}, u32[]{:S(2)}, u32[]{:S(2)}) collective-permute-start(bf16[128,768]{1,0:T(8,128)(2,1)S(1)} %broadcast_select_fusion.4.refs_4_), channel_id=1, source_target_pairs={{0,2},{1,3},{2,0},{3,1},{4,6},{5,7},{6,4},{7,5},{8,10},{9,11},{10,... | collective-permute-start | bytes 589832 | tf_op jit(solution)/shard_map/ppermute | solution.py:580
  261.4 10.0 %collective-permute-start.36 = (bf16[128,1536]{1,0:T(8,128)(2,1)S(1)}, bf16[128,1536]{1,0:T(8,128)(2,1)S(1)}, u32[]{:S(2)}, u32[]{:S(2)}) collective-permute-start(bf16[128,1536]{1,0:T(8,128)(2,1)S(1)} %get-tuple-element.95), channel_id=1, source_target_pairs={{1,0},{2,1},{3,2},{4,3},{5,4},{6,5},{7,6},{8,7},{9,8},{10,9},{11,1... | collective-permute-start | bytes 1179656 | tf_op jit(solution)/shard_map/ppermute | solution.py:886
  262.7 15.2 %collective-permute-start.43 = (bf16[128,1536]{1,0:T(8,128)(2,1)}, bf16[128,1536]{1,0:T(8,128)(2,1)S(1)}, u32[]{:S(2)}, u32[]{:S(2)}) collective-permute-start(bf16[128,1536]{1,0:T(8,128)(2,1)} %get-tuple-element.98), channel_id=1, source_target_pairs={{0,1},{1,2},{2,3},{3,4},{4,5},{5,6},{6,7},{7,8},{8,9},{9,10},{10,1... | collective-permute-start | bytes 1179656 | tf_op jit(solution)/shard_map/ppermute | solution.py:887
  267.9 23.1 %collective-permute-start.50 = (bf16[128,768]{1,0:T(8,128)(2,1)S(1)}, bf16[128,768]{1,0:T(8,128)(2,1)S(1)}, u32[]{:S(2)}, u32[]{:S(2)}) collective-permute-start(bf16[128,768]{1,0:T(8,128)(2,1)S(1)} %broadcast_select_fusion.2.refs_12_), channel_id=1, source_target_pairs={{0,1},{1,0},{2,3},{3,2},{4,5},{5,4},{6,7},{7,6},{8,9},{9,8},{10,11... | collective-permute-start | bytes 589832 | tf_op jit(solution)/shard_map/ppermute | solution.py:580
  268.3 11.8 %collective-permute-start.45 = (bf16[128,768]{1,0:T(8,128)(2,1)S(1)}, bf16[128,768]{1,0:T(8,128)(2,1)}, u32[]{:S(2)}, u32[]{:S(2)}) collective-permute-start(bf16[128,768]{1,0:T(8,128)(2,1)S(1)} %broadcast_select_fusion.2.refs_12_), channel_id=1, source_target_pairs={{0,2},{1,3},{2,0},{3,1},{4,6},{5,7},{6,4},{7,5},{8,10},{9,11},{10,... | collective-permute-start | bytes 589832 | tf_op jit(solution)/shard_map/ppermute | solution.py:580
  270.2 20.8 %collective-permute-start.48 = (bf16[128,2304]{1,0:T(8,128)(2,1)S(1)}, bf16[128,2304]{1,0:T(8,128)(2,1)}, u32[]{:S(2)}, u32[]{:S(2)}) collective-permute-start(bf16[128,2304]{1,0:T(8,128)(2,1)S(1)} %broadcast_select_fusion.refs_4_), channel_id=1, source_target_pairs={{0,1},{1,0},{2,3},{3,2},{4,5},{5,4},{6,7},{7,6},{8,9},{9,8},{10,11... | collective-permute-start | bytes 1769480 | tf_op jit(solution)/shard_map/ppermute | solution.py:580
  271.4 16.8 %collective-permute-start.44 = (bf16[128,2304]{1,0:T(8,128)(2,1)S(1)}, bf16[128,2304]{1,0:T(8,128)(2,1)}, u32[]{:S(2)}, u32[]{:S(2)}) collective-permute-start(bf16[128,2304]{1,0:T(8,128)(2,1)S(1)} %broadcast_select_fusion.refs_4_), channel_id=1, source_target_pairs={{0,2},{1,3},{2,0},{3,1},{4,6},{5,7},{6,4},{7,5},{8,10},{9,11},{10,... | collective-permute-start | bytes 1769480 | tf_op jit(solution)/shard_map/ppermute | solution.py:580
  271.9 24.2 %all-to-all-start.6 = ((bf16[4,1,72,768]{3,2,1,0:T(8,128)(2,1)}), bf16[4,1,72,768]{3,2,1,0:T(8,128)(2,1)}, u32[]{:S(2)}, u32[]{:S(2)}) async-start(bf16[4,1,72,768]{3,2,1,0:T(8,128)(2,1)} %bitcast.80), calls=%async_computation.6 | async-start | bytes 884736 | tf_op jit(solution)/shard_map/all_to_all | solution.py:648
  288.2 4.8 %collective-permute-start.49 = (bf16[128,2304]{1,0:T(8,128)(2,1)}, bf16[128,2304]{1,0:T(8,128)(2,1)S(1)}, u32[]{:S(2)}, u32[]{:S(2)}) collective-permute-start(bf16[128,2304]{1,0:T(8,128)(2,1)} %collective-permute-done.44.refs_6_), channel_id=1, source_target_pairs={{0,1},{1,0},{2,3},{3,2},{4,5},{5,4},{6,7},{7,6},{8,9},{9,8},{10,11... | collective-permute-start | bytes 1769480 | tf_op jit(solution)/shard_map/ppermute | solution.py:580
  296.1 35.7 %all-to-all-start.5 = ((bf16[4,1,48,3072]{3,2,1,0:T(8,128)(2,1)}), bf16[4,1,48,3072]{3,2,1,0:T(8,128)(2,1)}, u32[]{:S(2)}, u32[]{:S(2)}) async-start(bf16[4,1,48,3072]{3,2,1,0:T(8,128)(2,1)} %bitcast.77), calls=%async_computation.5 | async-start | bytes 2359296 | tf_op jit(solution)/shard_map/all_to_all | solution.py:648
  300.6 18.1 %collective-permute-start.47 = (bf16[128,2304]{1,0:T(8,128)(2,1)S(1)}, bf16[128,2304]{1,0:T(8,128)(2,1)S(1)}, u32[]{:S(2)}, u32[]{:S(2)}) collective-permute-start(bf16[128,2304]{1,0:T(8,128)(2,1)S(1)} %broadcast_select_fusion.1.refs_4_), channel_id=1, source_target_pairs={{0,2},{1,3},{2,0},{3,1},{4,6},{5,7},{6,4},{7,5},{8,10},{9,11},{10,... | collective-permute-start | bytes 1769480 | tf_op jit(solution)/shard_map/ppermute | solution.py:580
  307.7 9.2 %collective-permute-start.54 = (f32[2,768]{1,0:T(2,128)S(1)}, f32[2,768]{1,0:T(2,128)S(1)}, u32[]{:S(2)}, u32[]{:S(2)}) collective-permute-start(f32[2,768]{1,0:T(2,128)S(1)} %fusion.19), channel_id=1, source_target_pairs={{0,2},{1,3},{2,0},{3,1},{4,6},{5,7},{6,4},{7,5},{8,10},{9,11},{10,... | collective-permute-start | bytes 18440 | tf_op jit(solution)/shard_map/ppermute | solution.py:580
  318.6 11.5 %collective-permute-start.46 = (bf16[128,2304]{1,0:T(8,128)(2,1)S(1)}, bf16[128,2304]{1,0:T(8,128)(2,1)S(1)}, u32[]{:S(2)}, u32[]{:S(2)}) collective-permute-start(bf16[128,2304]{1,0:T(8,128)(2,1)S(1)} %broadcast_select_fusion.1.refs_4_), channel_id=1, source_target_pairs={{0,1},{1,0},{2,3},{3,2},{4,5},{5,4},{6,7},{7,6},{8,9},{9,8},{10,11... | collective-permute-start | bytes 1769480 | tf_op jit(solution)/shard_map/ppermute | solution.py:580
  318.7 11.5 %collective-permute-start.52 = (bf16[128,2304]{1,0:T(8,128)(2,1)S(1)}, bf16[128,2304]{1,0:T(8,128)(2,1)S(1)}, u32[]{:S(2)}, u32[]{:S(2)}) collective-permute-start(bf16[128,2304]{1,0:T(8,128)(2,1)S(1)} %collective-permute-done.47.refs_6_), channel_id=1, source_target_pairs={{0,1},{1,0},{2,3},{3,2},{4,5},{5,4},{6,7},{7,6},{8,9},{9,8},{10,11... | collective-permute-start | bytes 1769480 | tf_op jit(solution)/shard_map/ppermute | solution.py:580
  320.8 9.3 %collective-permute-start.56 = (f32[2,768]{1,0:T(2,128)S(1)}, f32[2,768]{1,0:T(2,128)S(1)}, u32[]{:S(2)}, u32[]{:S(2)}) collective-permute-start(f32[2,768]{1,0:T(2,128)S(1)} %add.181), channel_id=1, source_target_pairs={{0,8},{1,9},{2,10},{3,11},{4,12},{5,13},{6,14},{7,15},{8,0},{9,1},... | collective-permute-start | bytes 18440 | tf_op jit(solution)/shard_map/ppermute | solution.py:580
  331.8 25.6 %all-to-all-start.4 = ((bf16[4,1,48,2304]{3,2,1,0:T(8,128)(2,1)}), bf16[4,1,48,2304]{3,2,1,0:T(8,128)(2,1)S(1)}, u32[]{:S(2)}, u32[]{:S(2)}) async-start(bf16[4,1,48,2304]{3,2,1,0:T(8,128)(2,1)} %bitcast.75), calls=%async_computation.4 | async-start | bytes 1769472 | tf_op jit(solution)/shard_map/all_to_all | solution.py:648
  (87 other events, 806.7 us)
Sparse Core Ops, SparseCore 0:
  10.9 71.9 all-gather.1

commit v2 on v1

--- a/solution.py
+++ b/solution.py
@@ -59,7 +59,7 @@
     return jnp.tile(jnp.stack([cosine, to_first, to_second]), (1, 2, 2))
 
 
-def on_core(body, outs, args, scratch=(), spaces=None):
+def on_core(body, micros, outs, args, scratch=(), spaces=None):
     return pl.pallas_call(
         body,
         out_shape=[jax.ShapeDtypeStruct(shape, dtype) for shape, dtype in outs],
@@ -68,6 +68,9 @@
         ],
         out_specs=[pl.BlockSpec(memory_space=pltpu.VMEM)] * len(outs),
         scratch_shapes=scratch,
+        cost_estimate=pl.CostEstimate(
+            flops=int(micros * 1.15e9), bytes_accessed=2**16, transcendentals=0
+        ),
         compiler_params=pltpu.CompilerParams(vmem_limit_bytes=24 * 2**20),
     )(*args)
 
@@ -250,6 +253,26 @@
     grad_ref[...] = (d_middle + norm_back(d_normed, gain_ref[...], xhat, scale)).astype(BF)
 
 
+def message_body(w_ref, attn_ref, mlp_ref, ids_ref, out_ref, rows_scr, ids_scr):
+    shard, columns = w_ref.shape
+    micro_count, row_count = ids_ref.shape
+    out_ref[:, :columns] = w_ref[...]
+    rows_scr[...] = jnp.zeros_like(rows_scr)
+    ids_scr[...] = jnp.zeros_like(ids_scr)
+    rows_scr[0:1, :shard] = attn_ref[...].astype(F32)
+    rows_scr[1:2, :shard] = mlp_ref[...].astype(F32)
+    ids_scr[:micro_count, :row_count] = ids_ref[...].astype(F32)
+    runs = -(-row_count // shard)
+    for run in range(runs):
+        turned = ids_scr[...]
+        if run:
+            turned = pltpu.roll(turned, LANES - run * shard, 1)
+        for micro in range(micro_count):
+            row = 2 + micro * runs + run
+            rows_scr[row : row + 1] = turned[micro : micro + 1]
+    out_ref[:, columns:] = rows_scr[...].T[:shard].astype(BF)
+
+
 def local_project_body(place_ref, x_ref, table_ref, *refs):
     pieces, (first_ref, extra_ref, normed_ref, q_ref, kv_ref, sem) = refs[:-6], refs[-6:]
     rows = pieces[0].shape[0]
@@ -580,20 +603,15 @@
     return lax.ppermute(rows, "dp", [(i, i ^ apart) for i in range(count)])
 
 
-def group_pieces(piece, count, hold=None):
+def group_pieces(piece, count):
     pieces = {0: piece}
     for apart in (4, 8, 12):
         pieces[apart] = partner(piece, apart, count)
-    held = [pieces[apart] for apart in (4, 8, 12)]
-    if hold is not None:
-        held, hold = lax.optimization_barrier((held, hold))
-        for apart, item in zip((4, 8, 12), held):
-            pieces[apart] = item
     for apart in (0, 4, 8, 12):
         pieces[apart + 2] = partner(pieces[apart], 2, count)
     for apart in range(0, GROUP, 2):
         pieces[apart + 1] = partner(pieces[apart], 1, count)
-    return [pieces[apart] for apart in range(GROUP)], hold
+    return [pieces[apart] for apart in range(GROUP)]
 
 
 def in_order(pieces, group_pos, count):
@@ -637,7 +655,7 @@
         for part in [item.reshape(-1, tokens) for item in lefts] + list(rights)
     ]
     columns = sum(rights[0].shape[1] for _, rights in terms)
-    (product,) = on_core(product_body, [((planes * groups * rows, columns), BF)], args)
+    (product,) = on_core(product_body, 2.0, [((planes * groups * rows, columns), BF)], args)
     return product.reshape(planes, groups, rows, columns)
 
 
@@ -670,22 +688,22 @@
     group_pos = replica % GROUP
     micro_count, row_count, width = tokens_in.shape
     shard = qkv_weight.shape[1]
-    own_ids = segment_ids.reshape(-1)
-    id_columns = -(-own_ids.size // shard)
-    ids = jnp.pad(own_ids.astype(BF), (0, id_columns * shard - own_ids.size))
-    extra = jnp.concatenate(
-        [attn_gain[0][:, None], mlp_gain[0][:, None], ids.reshape(shard, id_columns)], 1
-    )
-    extra = jnp.pad(extra, ((0, 0), (0, LANES - extra.shape[1])))
+    runs = -(-row_count // shard)
+    (message,) = on_core(
+        message_body,
+        1.0,
+        [((shard, 3 * width + LANES), BF)],
+        (qkv_weight[0], attn_gain, mlp_gain, segment_ids),
+        [pltpu.VMEM((LANES, LANES), F32), pltpu.VMEM((8, LANES), F32)],
+    )
     second = lax.all_gather(
         jnp.concatenate([attn_out_weight[0], mlp_in_weight[0]], 1), "dp", axis=0, tiled=True
     )
-    pieces, late_weight = group_pieces(
-        jnp.concatenate([qkv_weight[0], extra], 1), count, mlp_out_weight[0]
-    )
+    pieces = group_pieces(message, count)
+    late_weight, pieces = lax.optimization_barrier((mlp_out_weight[0], pieces))
     if count > GROUP:
         pieces = [in_order(pieces, group_pos, count)]
-    w_out = in_order(group_pieces(late_weight, count)[0], group_pos, count)
+    w_out = in_order(group_pieces(late_weight, count), group_pos, count)
 
     positions = group_pos * row_count + jnp.arange(row_count)
     local_tables = angles(positions, local_log_base)
@@ -696,9 +714,10 @@
     hidden = w_out.shape[0]
     pairs = rows * width // (row_count * LANES)
     in_0 = tokens_in.reshape(rows, width)
-    extra_rows = -(-(2 + id_columns) // 8) * 8
+    extra_rows = -(-(2 + micro_count * runs) // 8) * 8
     first, extra, normed_0, q_0, kv_0 = on_core(
         local_project_body,
+        5,
         [
             ((width, 3 * width + LANES), BF),
             ((extra_rows, width), F32),
@@ -711,11 +730,10 @@
         [pltpu.SMEM, pltpu.VMEM, pltpu.VMEM] + [pl.ANY] * len(pieces),
     )
     gain_attn, gain_mlp = extra[:1], extra[1:2]
-    all_ids = extra[2 : 2 + id_columns].reshape(id_columns, count, shard)
-    all_ids = lax.dynamic_slice_in_dim(all_ids, replica - group_pos, GROUP, 1)
-    all_ids = all_ids.transpose(1, 2, 0).reshape(GROUP, -1)
-    all_ids = all_ids[:, : own_ids.size].reshape(GROUP, micro_count, row_count)
-    segments = all_ids.swapaxes(0, 1).reshape(micro_count, GROUP * row_count).astype(jnp.int32)
+    all_ids = extra[2 : 2 + micro_count * runs].reshape(micro_count, runs, count, shard)
+    all_ids = lax.dynamic_slice_in_dim(all_ids, replica - group_pos, GROUP, 2)
+    all_ids = all_ids.swapaxes(1, 2).reshape(micro_count, GROUP, runs * shard)[..., :row_count]
+    segments = all_ids.reshape(micro_count, GROUP * row_count).astype(jnp.int32)
 
     key_pos = positions[0] - row_count + jnp.arange(3 * row_count)
     around = jnp.pad(segments, ((0, 0), (row_count, row_count)), constant_values=-1)
@@ -740,11 +758,13 @@
     )
     att_0, total_0 = on_core(
         local_forward_body,
+        3.6,
         [((rows, width), BF), ((pairs, 1, LANES), F32)],
         (q_0, *around_0, bias),
     )
     out_0, n2_0, mixed_0, middle_0, gate_up_0 = on_core(
         local_middle_body,
+        2.2,
         [
             ((rows, width), BF),
             ((rows, width), BF),
@@ -760,6 +780,7 @@
     half = row_count // 2
     normed_1, sent = on_core(
         global_project_body,
+        1.2,
         [((rows, width), BF), ((GROUP, 3 * fold, LANES), BF)],
         (in_1, gain_attn, first, global_tables),
     )
@@ -778,6 +799,7 @@
     ]
     folded, total_1 = on_core(
         global_forward_body,
+        7,
         [((GROUP, fold, LANES), BF), ((tiles, 1, TILE), F32)],
         (got, beside, own_seg, shared_seg),
         head_scratch + [pltpu.VMEM((keys * 3 // 2, LANES), F32)],
@@ -787,6 +809,7 @@
     up_1 = out_grad.reshape(rows, width)
     out_1, att_1, n2_1, mixed_1, d_gu_1, gain_mlp_1, d_mid_1, d_attn_1, sent = on_core(
         global_middle_body,
+        4.2,
         [
             ((rows, width), BF),
             ((rows, width), BF),
@@ -803,6 +826,7 @@
     d_folded = exchange(sent, count)
     sent, to_beside = on_core(
         global_backward_body,
+        9,
         [((GROUP, 3 * fold, LANES), BF), ((GROUP, 2 * half, LANES), BF)],
         (got, beside, own_seg, shared_seg, total_1, d_folded),
         head_scratch
@@ -850,6 +874,7 @@
     )
     d_proj_1, grad_1, gain_attn_1 = on_core(
         global_finish_body,
+        1.6,
         [((rows, 3 * width), BF), ((rows, width), BF), ((1, width), F32)],
         (got, d_mid_1, in_1, gain_attn, first, global_tables),
     )
@@ -861,6 +886,7 @@
     out_blocks = plane_product([(mixed, d_mlp)])
     d_gu_0, gain_mlp_0, d_mid_0, d_attn_0, d_att_0 = on_core(
         local_back_middle_body,
+        2.9,
         [
             ((rows, inner), BF),
             ((1, width), F32),
@@ -875,6 +901,7 @@
     across = [partner(item, 2, count) for item in own]
     dq_0, d_own, d_before, d_after = on_core(
         local_backward_body,
+        4.2,
         [
             ((rows, width), BF),
             ((rows, 2 * width), F32),
@@ -889,11 +916,11 @@
     mlp_out_share = sum_planes(out_blocks, count)
     (d_proj_0,) = on_core(
         local_join_body,
+        0.5,
         [((rows, 3 * width), BF)],
         (dq_0, d_own, from_after, from_before, local_tables),
     )
     d_proj = jnp.where(lower, d_proj_0, d_proj_1)
-    d_proj, across = lax.optimization_barrier((d_proj, across))
     far = [partner(item, 1, count) for item in across]
     d_gu, d_attn = zip(own, beside, across, far)
     in_blocks = plane_product([(n2, d_gu), (att, d_attn)])
@@ -901,9 +928,11 @@
     across = partner(d_proj, 2, count)
     across, in_blocks = lax.optimization_barrier((across, in_blocks))
     d_proj = [d_proj, partner(d_proj, 1, count), across, partner(across, 1, count)]
-    qkv_share = sum_planes(plane_product([(n1, d_proj)]), count)
+    qkv_blocks = plane_product([(n1, d_proj)])
+    qkv_share = sum_planes(qkv_blocks, count)
     grad_0, gain_attn_0 = on_core(
         input_backward_body,
+        1.5,
         [((rows, width), BF), ((1, width), F32)],
         (d_mid_0, d_proj_0, in_0, gain_attn, first),
     )
@@ -913,6 +942,7 @@
         jnp.concatenate([gain_attn_0, gain_mlp_0]),
         jnp.concatenate([gain_attn_1, gain_mlp_1]),
     )
+    gains, _ = lax.optimization_barrier((gains, qkv_blocks))
     apart = 1
     while apart < count:
         gains = gains + partner(gains, apart, count)

time: 367 us -> 376 us (1.025)
  local copies, waits for them, and re-layouts: 39.4 us -> 50.4 us
  blocking collectives: 53.8 us -> 45.5 us
  starting transfers between devices: 73 us -> 78.3 us
    all_to_all x3, blocking collectives: 53.8 us -> 45.5 us  [exchange(): return lax.all_to_all(blocks, 'dp', 0, 0, axis_index_groups=groups)]
    ppermute x51, starting transfers between devices: 41.9 us -> 50.1 us  [partner(): return lax.ppermute(rows, 'dp', [(i, i ^ apart) for i in range(count)])]
    unnamed x147 -> x152, local copies, waits for them, and re-layouts: 23.6 us -> 31.7 us
    pallas_call x15 -> x16, Pallas kernels: 49.1 us -> 49.3 us  [on_core(): pl.pallas_call(body, out_shape=[jax.ShapeDtypeStruct(shape, dtype) for sh...]
  transfers between devices with their start and end apart: 62 -> 62, of which waited for: 26 -> 23; matrix products, arithmetic and copies ran while one was open for 8% -> 8% of each run, Pallas kernels for 7% -> 7%
where the time goes in v2:
time: 376 us; the launch traced here: 374 us
  waiting for transfers between devices  118 us (31%)
  starting transfers between devices  78.3 us (21%)
  local copies, waits for them, and re-layouts  50.4 us (13%)
  Pallas kernels  49.3 us (13%)
  blocking collectives  45.5 us (12%)
  other arithmetic  17.1 us (5%)
  between operations  15.5 us (4%)
    ppermute x51, waiting for transfers between devices, partner(): return lax.ppermute(rows, 'dp', [(i, i ^ apart) for i in range(count)])  87.6 us
    ppermute x51, starting transfers between devices, partner(): return lax.ppermute(rows, 'dp', [(i, i ^ apart) for i in range(count)])  50.1 us
    pallas_call x16, Pallas kernels, on_core(): pl.pallas_call(body, out_shape=[jax.ShapeDtypeStruct(shape, dtype) for sh...  49.3 us
    all_to_all x3, blocking collectives, exchange(): return lax.all_to_all(blocks, 'dp', 0, 0, axis_index_groups=groups)  45.5 us
    unnamed x152, local copies, waits for them, and re-layouts  31.7 us
    all_to_all x3, waiting for transfers between devices, sum_planes(): got = lax.all_to_all(blocks, 'dp', 0, 0, axis_index_groups=groups)  18.4 us
    all_to_all x3, starting transfers between devices, sum_planes(): got = lax.all_to_all(blocks, 'dp', 0, 0, axis_index_groups=groups)  11.9 us
    ppermute x2, waiting for transfers between devices, to_other_section(): return lax.ppermute(rows, 'section', [(0, 1)] if step > 0 else [(1, 0)])  7.87 us
  transfers between devices with their start and end apart: 62, of which 23 were waited for; matrix products, arithmetic and copies ran while one was open for 8% of the time, Pallas kernels for 7%

profile of v2, /device:TPU:0, one launch (start us, length us, event | category | flops | bytes accessed | tf_op | source)
XLA Modules:
  0.0 374.5 jit_solution(7869863956473112393)
XLA Ops:
  12.1 5.1 %collective-permute-start.11 = (bf16[48,2432]{1,0:T(8,128)(2,1)S(1)}, bf16[48,2432]{1,0:T(8,128)(2,1)S(1)}, u32[]{:S(2)}, u32[]{:S(2)}) collective-permute-start(bf16[48,2432]{1,0:T(8,128)(2,1)S(1)} %shard_map.152.refs_0_), channel_id=1, source_target_pairs={{0,12},{1,13},{2,14},{3,15},{4,8},{5,9},{6,10},{7,11},{8,4},{9,5},... | collective-permute-start | bytes 700424 | tf_op jit(solution)/shard_map/ppermute | solution.py:603
  21.1 3.1 collective-permute-done.11.refs_12_
  25.5 21.0 %collective-permute-done.7.refs_8_ = bf16[48,2432]{1,0:T(8,128)(2,1)S(1)} collective-permute-done((bf16[48,2432]{1,0:T(8,128)(2,1)S(1)}, bf16[48,2432]{1,0:T(8,128)(2,1)S(1)}, u32[]{:S(2)}, u32[]{:S(2)}) %collective-permute-start.7) | collective-permute-done | bytes 233504 | tf_op jit(solution)/shard_map/ppermute | solution.py:603
  49.5 9.4 %collective-permute-done.9.refs_10_ = bf16[48,2432]{1,0:T(8,128)(2,1)S(1)} collective-permute-done((bf16[48,2432]{1,0:T(8,128)(2,1)S(1)}, bf16[48,2432]{1,0:T(8,128)(2,1)S(1)}, u32[]{:S(2)}, u32[]{:S(2)}) %collective-permute-start.9) | collective-permute-done | bytes 233504 | tf_op jit(solution)/shard_map/ppermute | solution.py:603
  59.4 9.1 %collective-permute-done.5.refs_6_ = bf16[48,2432]{1,0:T(8,128)(2,1)S(1)} collective-permute-done((bf16[48,2432]{1,0:T(8,128)(2,1)S(1)}, bf16[48,2432]{1,0:T(8,128)(2,1)S(1)}, u32[]{:S(2)}, u32[]{:S(2)}) %collective-permute-start.5) | collective-permute-done | bytes 233504 | tf_op jit(solution)/shard_map/ppermute | solution.py:603
  73.5 3.2 collective-permute-start.20
  76.7 2.5 collective-permute-start.18
  82.0 6.2 %shard_map.153 = (bf16[768,2432]{1,0:T(8,128)(2,1)S(1)}, f32[8,768]{1,0:T(8,128)S(1)}, bf16[128,768]{1,0:T(8,128)(2,1)S(1)}, bf16[128,768]{1,0:T(8,128)(2,1)S(1)}, bf16[128,1536]{1,0:T(8,128)(2,1)S(1)}) custom-call(s32[1]{0:T(128)} %bitcast.1.place_ref, bf16[128,768]{1,0:T(8,128)(2,1)S(1)} %bitcast.139, f32[3,128,128]{2,1,0:T(8,128)S(1)} %tile.13.table_ref, ...), custom_call_target="tpu_custom_call" | custom-call | flops 5750000128 | bytes 65536 | tf_op jit(solution)/shard_map/pallas_call | solution.py:63
  94.1 2.8 collective-permute-start.22
  102.3 2.4 collective-permute-done.22
  109.0 3.0 collective-permute-done.30
  114.1 3.7 shard_map.154
  119.1 2.4 copy-done.29
  126.3 3.2 collective-permute-start.32
  130.0 4.0 %collective-permute-done.32.x_ref = bf16[128,768]{1,0:T(8,128)(2,1)S(1)} collective-permute-done((bf16[128,768]{1,0:T(8,128)(2,1)S(1)}, bf16[128,768]{1,0:T(8,128)(2,1)S(1)}, u32[]{:S(2)}, u32[]{:S(2)}) %collective-permute-start.32) | collective-permute-done | bytes 196640 | tf_op jit(solution)/shard_map/ppermute | solution.py:599
  134.0 2.1 copy-done.54
  137.3 22.2 %all_to_all.35.got_ref = bf16[16,144,128]{2,1,0:T(8,128)(2,1)S(1)} all-to-all(bf16[16,144,128]{2,1,0:T(8,128)(2,1)S(1)} %get-tuple-element.95), channel_id=1, replica_groups={{0,1,2,3,4,5,6,7,8,9,10,11,12,13,14,15},{16,17,18,19,20,21,22,23,24,25,..., dimensions={0} | all-to-all | bytes 1179648 | tf_op jit(solution)/shard_map/all_to_all | solution.py:595
  163.1 7.1 %shard_map.157 = (bf16[16,48,128]{2,1,0:T(8,128)(2,1)S(1)}, f32[6,1,256]{2,1,0:T(1,128)S(1)}) custom-call(bf16[16,144,128]{2,1,0:T(8,128)(2,1)S(1)} %all_to_all.35.got_ref, bf16[16,64,128]{2,1,0:T(8,128)(2,1)} %collective-permute-done.33.other_ref, s32[1024,1]{1,0:T(8,128)S(1)} %copy-done.4, s32[1024,1]{1,0:T(8,128)S(1)} %copy.35.shared_seg_ref), custom_call_target="tpu_custom_call" | custom-call | flops 8049999872 | bytes 65536 | tf_op jit(solution)/shard_map/pallas_call | solution.py:63
  170.3 11.8 %all_to_all.36.got_ref = bf16[16,48,128]{2,1,0:T(8,128)(2,1)S(1)} all-to-all(bf16[16,48,128]{2,1,0:T(8,128)(2,1)S(1)} %get-tuple-element.96), channel_id=1, replica_groups={{0,1,2,3,4,5,6,7,8,9,10,11,12,13,14,15},{16,17,18,19,20,21,22,23,24,25,..., dimensions={0} | all-to-all | bytes 393216 | tf_op jit(solution)/shard_map/all_to_all | solution.py:595
  182.1 4.1 %shard_map.158 = (bf16[128,768]{1,0:T(8,128)(2,1)S(1)}, bf16[128,768]{1,0:T(8,128)(2,1)S(1)}, bf16[128,768]{1,0:T(8,128)(2,1)S(1)}, bf16[128,1152]{1,0:T(8,128)(...) custom-call(bf16[16,48,128]{2,1,0:T(8,128)(2,1)S(1)} %all_to_all.36., ...), custom_call_target="tpu_custom_call" | custom-call | flops 4830000128 | bytes 65536 | tf_op jit(solution)/shard_map/pallas_call | solution.py:63
  186.3 11.6 %all_to_all.37.d_ref = bf16[16,48,128]{2,1,0:T(8,128)(2,1)S(1)} all-to-all(bf16[16,48,128]{2,1,0:T(8,128)(2,1)S(1)} %get-tuple-element.106), channel_id=1, replica_groups={{0,1,2,3,4,5,6,7,8,9,10,11,12,13,14,15},{16,17,18,19,20,21,22,23,24,25,..., dimensions={0} | all-to-all | bytes 393216 | tf_op jit(solution)/shard_map/all_to_all | solution.py:595
  197.9 9.0 %shard_map.159 = (bf16[16,144,128]{2,1,0:T(8,128)(2,1)S(1)}, bf16[16,64,128]{2,1,0:T(8,128)(2,1)}) custom-call(bf16[16,144,128]{2,1,0:T(8,128)(2,1)S(1)} %all_to_all.35.got_ref, bf16[16,64,128]{2,1,0:T(8,128)(2,1)} %collective-permute-done.33.other_ref, s32[1024,1]{1,0:T(8,128)S(1)} %copy-done.5, s32[1024,1]{1,0:T(8,128)S(1)} %copy-done.3, ...), custom_call_target="tpu_custom_call" | custom-call | flops 10350000128 | bytes 65536 | tf_op jit(solution)/shard_map/pallas_call | solution.py:63
  209.8 3.7 all-to-all-start.3
  224.5 4.6 %all-to-all-done.3.got_ref = bf16[16,144,128]{2,1,0:T(8,128)(2,1)S(1)} async-done(((bf16[16,144,128]{2,1,0:T(8,128)(2,1)}), bf16[16,144,128]{2,1,0:T(8,128)(2,1)S(1)}, u32[]{:S(2)}, u32[]{:S(2)}) %all-to-all-start.3) | async-done | bytes 589856 | tf_op jit(solution)/shard_map/all_to_all | solution.py:595
  230.0 2.1 copy-done.55
  239.7 3.9 %collective-permute-done.35.up_ref = bf16[128,768]{1,0:T(8,128)(2,1)S(1)} collective-permute-done((bf16[128,768]{1,0:T(8,128)(2,1)S(1)}, bf16[128,768]{1,0:T(8,128)(2,1)S(1)}, u32[]{:S(2)}, u32[]{:S(2)}) %collective-permute-start.35) | collective-permute-done | bytes 196640 | tf_op jit(solution)/shard_map/ppermute | solution.py:599
  245.0 2.3 copy-done.31
  248.3 2.8 shard_map.161
  251.2 3.5 shard_map.162
  256.1 3.1 collective-permute-start.43
  263.7 7.2 %collective-permute-start.45 = (bf16[128,2304]{1,0:T(8,128)(2,1)S(1)}, bf16[128,2304]{1,0:T(8,128)(2,1)S(1)}, u32[]{:S(2)}, u32[]{:S(2)}) collective-permute-start(bf16[128,2304]{1,0:T(8,128)(2,1)S(1)} %broadcast_select_fusion.1.refs_4_), channel_id=1, source_target_pairs={{0,2},{1,3},{2,0},{3,1},{4,6},{5,7},{6,4},{7,5},{8,10},{9,11},{10,... | collective-permute-start | bytes 1769480 | tf_op jit(solution)/shard_map/ppermute | solution.py:603
  271.6 13.5 %collective-permute-done.45.refs_6_ = bf16[128,2304]{1,0:T(8,128)(2,1)S(1)} collective-permute-done((bf16[128,2304]{1,0:T(8,128)(2,1)S(1)}, bf16[128,2304]{1,0:T(8,128)(2,1)S(1)}, u32[]{:S(2)}, u32[]{:S(2)}) %collective-permute-start.45) | collective-permute-done | bytes 589856 | tf_op jit(solution)/shard_map/ppermute | solution.py:603
  285.1 4.1 %all-to-all-start.6 = ((bf16[4,1,72,768]{3,2,1,0:T(8,128)(2,1)}), bf16[4,1,72,768]{3,2,1,0:T(8,128)(2,1)}, u32[]{:S(2)}, u32[]{:S(2)}) async-start(bf16[4,1,72,768]{3,2,1,0:T(8,128)(2,1)} %bitcast.77), calls=%async_computation.6 | async-start | bytes 884736 | tf_op jit(solution)/shard_map/all_to_all | solution.py:666
  292.1 2.8 shard_map.167
  294.9 8.1 %all-to-all-done.6 = bf16[4,1,72,768]{3,2,1,0:T(8,128)(2,1)} async-done(((bf16[4,1,72,768]{3,2,1,0:T(8,128)(2,1)}), bf16[4,1,72,768]{3,2,1,0:T(8,128)(2,1)}, u32[]{:S(2)}, u32[]{:S(2)}) %all-to-all-start.6) | async-done | bytes 442400 | tf_op jit(solution)/shard_map/all_to_all | solution.py:666
  303.0 4.2 %all-to-all-start.4 = ((bf16[4,1,48,2304]{3,2,1,0:T(8,128)(2,1)}), bf16[4,1,48,2304]{3,2,1,0:T(8,128)(2,1)}, u32[]{:S(2)}, u32[]{:S(2)}) async-start(bf16[4,1,48,2304]{3,2,1,0:T(8,128)(2,1)} %bitcast.72), calls=%async_computation.4 | async-start | bytes 1769472 | tf_op jit(solution)/shard_map/all_to_all | solution.py:666
  307.8 2.1 collective-permute-start.50
  310.0 5.1 %collective-permute-done.50.refs_14_ = bf16[128,768]{1,0:T(8,128)(2,1)S(1)} collective-permute-done((bf16[128,768]{1,0:T(8,128)(2,1)S(1)}, bf16[128,768]{1,0:T(8,128)(2,1)S(1)}, u32[]{:S(2)}, u32[]{:S(2)}) %collective-permute-start.50) | collective-permute-done | bytes 196640 | tf_op jit(solution)/shard_map/ppermute | solution.py:603
  316.6 2.9 shard_map.166
  319.4 10.2 %all-to-all-done.4 = bf16[4,1,48,2304]{3,2,1,0:T(8,128)(2,1)} async-done(((bf16[4,1,48,2304]{3,2,1,0:T(8,128)(2,1)}), bf16[4,1,48,2304]{3,2,1,0:T(8,128)(2,1)}, u32[]{:S(2)}, u32[]{:S(2)}) %all-to-all-start.4) | async-done | bytes 884768 | tf_op jit(solution)/shard_map/all_to_all | solution.py:666
  329.7 3.5 all-to-all-start.5
  333.2 2.0 copy-done.56
  338.0 2.0 collective-permute-start.54
  341.7 2.0 collective-permute-start.55
  344.3 7.7 %collective-permute-done.55 = f32[2,768]{1,0:T(2,128)S(1)} collective-permute-done((f32[2,768]{1,0:T(2,128)S(1)}, f32[2,768]{1,0:T(2,128)S(1)}, u32[]{:S(2)}, u32[]{:S(2)}) %collective-permute-start.55) | collective-permute-done | bytes 6176 | tf_op jit(solution)/shard_map/ppermute | solution.py:603
  352.1 4.6 %collective-permute-start.56 = (f32[2,768]{1,0:T(2,128)S(1)}, f32[2,768]{1,0:T(2,128)S(1)}, u32[]{:S(2)}, u32[]{:S(2)}) collective-permute-start(f32[2,768]{1,0:T(2,128)S(1)} %add.177), channel_id=1, source_target_pairs={{0,8},{1,9},{2,10},{3,11},{4,12},{5,13},{6,14},{7,15},{8,0},{9,1},... | collective-permute-start | bytes 18440 | tf_op jit(solution)/shard_map/ppermute | solution.py:603
  357.4 4.1 %collective-permute-done.56 = f32[2,768]{1,0:T(2,128)S(1)} collective-permute-done((f32[2,768]{1,0:T(2,128)S(1)}, f32[2,768]{1,0:T(2,128)S(1)}, u32[]{:S(2)}, u32[]{:S(2)}) %collective-permute-start.56) | collective-permute-done | bytes 6176 | tf_op jit(solution)/shard_map/ppermute | solution.py:603
  363.9 2.1 convert_reduce_fusion.1
  (344 shorter events, 95.5 us)
Async XLA Ops:
  7.2 111.9 %all-gather.2.cloned.1.call-start = ((), (), s32[]{:S(2)}) async-start(), calls=%async_computation.7 | async-start | bytes 5013504 | tf_op jit(solution)/shard_map/all_gather | solution.py:699
  12.1 12.2 %collective-permute-start.11 = (bf16[48,2432]{1,0:T(8,128)(2,1)S(1)}, bf16[48,2432]{1,0:T(8,128)(2,1)S(1)}, u32[]{:S(2)}, u32[]{:S(2)}) collective-permute-start(bf16[48,2432]{1,0:T(8,128)(2,1)S(1)} %shard_map.152.refs_0_), channel_id=1, source_target_pairs={{0,12},{1,13},{2,14},{3,15},{4,8},{5,9},{6,10},{7,11},{8,4},{9,5},... | collective-permute-start | bytes 700424 | tf_op jit(solution)/shard_map/ppermute | solution.py:603
  17.2 29.3 %collective-permute-start.7 = (bf16[48,2432]{1,0:T(8,128)(2,1)S(1)}, bf16[48,2432]{1,0:T(8,128)(2,1)S(1)}, u32[]{:S(2)}, u32[]{:S(2)}) collective-permute-start(bf16[48,2432]{1,0:T(8,128)(2,1)S(1)} %shard_map.152.refs_0_), channel_id=1, source_target_pairs={{0,8},{1,9},{2,10},{3,11},{4,12},{5,13},{6,14},{7,15},{8,0},{9,1},... | collective-permute-start | bytes 700424 | tf_op jit(solution)/shard_map/ppermute | solution.py:603
  17.2 29.3 %collective-permute-start.3 = (bf16[48,2432]{1,0:T(8,128)(2,1)S(1)}, bf16[48,2432]{1,0:T(8,128)(2,1)S(1)}, u32[]{:S(2)}, u32[]{:S(2)}) collective-permute-start(bf16[48,2432]{1,0:T(8,128)(2,1)S(1)} %shard_map.152.refs_0_), channel_id=1, source_target_pairs={{0,4},{1,5},{2,6},{3,7},{4,0},{5,1},{6,2},{7,3},{8,12},{9,13},{10,... | collective-permute-start | bytes 700424 | tf_op jit(solution)/shard_map/ppermute | solution.py:603
  17.8 30.2 %collective-permute-start.1 = (bf16[48,2432]{1,0:T(8,128)(2,1)S(1)}, bf16[48,2432]{1,0:T(8,128)(2,1)S(1)}, u32[]{:S(2)}, u32[]{:S(2)}) collective-permute-start(bf16[48,2432]{1,0:T(8,128)(2,1)S(1)} %shard_map.152.refs_0_), channel_id=1, source_target_pairs={{0,2},{1,3},{2,0},{3,1},{4,6},{5,7},{6,4},{7,5},{8,10},{9,11},{10,... | collective-permute-start | bytes 700424 | tf_op jit(solution)/shard_map/ppermute | solution.py:603
  19.4 28.8 %collective-permute-start = (bf16[48,2432]{1,0:T(8,128)(2,1)S(1)}, bf16[48,2432]{1,0:T(8,128)(2,1)S(1)}, u32[]{:S(2)}, u32[]{:S(2)}) collective-permute-start(bf16[48,2432]{1,0:T(8,128)(2,1)S(1)} %shard_map.152.refs_0_), channel_id=1, source_target_pairs={{0,1},{1,0},{2,3},{3,2},{4,5},{5,4},{6,7},{7,6},{8,9},{9,8},{10,11... | collective-permute-start | bytes 700424 | tf_op jit(solution)/shard_map/ppermute | solution.py:603
  24.2 24.7 %collective-permute-start.13 = (bf16[48,2432]{1,0:T(8,128)(2,1)S(1)}, bf16[48,2432]{1,0:T(8,128)(2,1)S(1)}, u32[]{:S(2)}, u32[]{:S(2)}) collective-permute-start(bf16[48,2432]{1,0:T(8,128)(2,1)S(1)} %collective-permute-done.11.refs_12_), channel_id=1, source_target_pairs={{0,2},{1,3},{2,0},{3,1},{4,6},{5,7},{6,4},{7,5},{8,10},{9,11},{10,... | collective-permute-start | bytes 700424 | tf_op jit(solution)/shard_map/ppermute | solution.py:603
  46.5 12.4 %collective-permute-start.9 = (bf16[48,2432]{1,0:T(8,128)(2,1)S(1)}, bf16[48,2432]{1,0:T(8,128)(2,1)S(1)}, u32[]{:S(2)}, u32[]{:S(2)}) collective-permute-start(bf16[48,2432]{1,0:T(8,128)(2,1)S(1)} %collective-permute-done.7.refs_8_), channel_id=1, source_target_pairs={{0,2},{1,3},{2,0},{3,1},{4,6},{5,7},{6,4},{7,5},{8,10},{9,11},{10,... | collective-permute-start | bytes 700424 | tf_op jit(solution)/shard_map/ppermute | solution.py:603
  48.0 10.9 %collective-permute-start.8 = (bf16[48,2432]{1,0:T(8,128)(2,1)S(1)}, bf16[48,2432]{1,0:T(8,128)(2,1)S(1)}, u32[]{:S(2)}, u32[]{:S(2)}) collective-permute-start(bf16[48,2432]{1,0:T(8,128)(2,1)S(1)} %collective-permute-done.7.refs_8_), channel_id=1, source_target_pairs={{0,1},{1,0},{2,3},{3,2},{4,5},{5,4},{6,7},{7,6},{8,9},{9,8},{10,11... | collective-permute-start | bytes 700424 | tf_op jit(solution)/shard_map/ppermute | solution.py:603
  48.2 20.3 %collective-permute-start.5 = (bf16[48,2432]{1,0:T(8,128)(2,1)S(1)}, bf16[48,2432]{1,0:T(8,128)(2,1)S(1)}, u32[]{:S(2)}, u32[]{:S(2)}) collective-permute-start(bf16[48,2432]{1,0:T(8,128)(2,1)S(1)} %collective-permute-done.3.refs_4_), channel_id=1, source_target_pairs={{0,2},{1,3},{2,0},{3,1},{4,6},{5,7},{6,4},{7,5},{8,10},{9,11},{10,... | collective-permute-start | bytes 700424 | tf_op jit(solution)/shard_map/ppermute | solution.py:603
  48.9 21.9 %collective-permute-start.4 = (bf16[48,2432]{1,0:T(8,128)(2,1)S(1)}, bf16[48,2432]{1,0:T(8,128)(2,1)S(1)}, u32[]{:S(2)}, u32[]{:S(2)}) collective-permute-start(bf16[48,2432]{1,0:T(8,128)(2,1)S(1)} %collective-permute-done.3.refs_4_), channel_id=1, source_target_pairs={{0,1},{1,0},{2,3},{3,2},{4,5},{5,4},{6,7},{7,6},{8,9},{9,8},{10,11... | collective-permute-start | bytes 700424 | tf_op jit(solution)/shard_map/ppermute | solution.py:603
  49.0 22.5 %collective-permute-start.2 = (bf16[48,2432]{1,0:T(8,128)(2,1)S(1)}, bf16[48,2432]{1,0:T(8,128)(2,1)S(1)}, u32[]{:S(2)}, u32[]{:S(2)}) collective-permute-start(bf16[48,2432]{1,0:T(8,128)(2,1)S(1)} %collective-permute-done.1.refs_2_), channel_id=1, source_target_pairs={{0,1},{1,0},{2,3},{3,2},{4,5},{5,4},{6,7},{7,6},{8,9},{9,8},{10,11... | collective-permute-start | bytes 700424 | tf_op jit(solution)/shard_map/ppermute | solution.py:603
  58.9 13.3 %collective-permute-start.14 = (bf16[48,2432]{1,0:T(8,128)(2,1)S(1)}, bf16[48,2432]{1,0:T(8,128)(2,1)}, u32[]{:S(2)}, u32[]{:S(2)}) collective-permute-start(bf16[48,2432]{1,0:T(8,128)(2,1)S(1)} %collective-permute-done.13.refs_14_), channel_id=1, source_target_pairs={{0,1},{1,0},{2,3},{3,2},{4,5},{5,4},{6,7},{7,6},{8,9},{9,8},{10,11... | collective-permute-start | bytes 700424 | tf_op jit(solution)/shard_map/ppermute | solution.py:603
  58.9 13.3 %collective-permute-start.10 = (bf16[48,2432]{1,0:T(8,128)(2,1)S(1)}, bf16[48,2432]{1,0:T(8,128)(2,1)}, u32[]{:S(2)}, u32[]{:S(2)}) collective-permute-start(bf16[48,2432]{1,0:T(8,128)(2,1)S(1)} %collective-permute-done.9.refs_10_), channel_id=1, source_target_pairs={{0,1},{1,0},{2,3},{3,2},{4,5},{5,4},{6,7},{7,6},{8,9},{9,8},{10,11... | collective-permute-start | bytes 700424 | tf_op jit(solution)/shard_map/ppermute | solution.py:603
  72.2 32.8 %collective-permute-start.28 = (bf16[72,768]{1,0:T(8,128)(2,1)}, bf16[72,768]{1,0:T(8,128)(2,1)S(1)}, u32[]{:S(2)}, u32[]{:S(2)}) collective-permute-start(bf16[72,768]{1,0:T(8,128)(2,1)} %bitcast.160), channel_id=1, source_target_pairs={{0,12},{1,13},{2,14},{3,15},{4,8},{5,9},{6,10},{7,11},{8,4},{9,5},... | collective-permute-start | bytes 331784 | tf_op jit(solution)/shard_map/ppermute | solution.py:603
  73.5 26.8 %collective-permute-start.24 = (bf16[72,768]{1,0:T(8,128)(2,1)}, bf16[72,768]{1,0:T(8,128)(2,1)}, u32[]{:S(2)}, u32[]{:S(2)}) collective-permute-start(bf16[72,768]{1,0:T(8,128)(2,1)} %bitcast.161), channel_id=1, source_target_pairs={{0,8},{1,9},{2,10},{3,11},{4,12},{5,13},{6,14},{7,15},{8,0},{9,1},... | collective-permute-start | bytes 331784 | tf_op jit(solution)/shard_map/ppermute | solution.py:603
  73.5 19.2 %collective-permute-start.20 = (bf16[72,768]{1,0:T(8,128)(2,1)}, bf16[72,768]{1,0:T(8,128)(2,1)}, u32[]{:S(2)}, u32[]{:S(2)}) collective-permute-start(bf16[72,768]{1,0:T(8,128)(2,1)} %bitcast.162), channel_id=1, source_target_pairs={{0,4},{1,5},{2,6},{3,7},{4,0},{5,1},{6,2},{7,3},{8,12},{9,13},{10,... | collective-permute-start | bytes 331784 | tf_op jit(solution)/shard_map/ppermute | solution.py:603
  76.7 17.4 %collective-permute-start.18 = (bf16[72,768]{1,0:T(8,128)(2,1)}, bf16[72,768]{1,0:T(8,128)(2,1)}, u32[]{:S(2)}, u32[]{:S(2)}) collective-permute-start(bf16[72,768]{1,0:T(8,128)(2,1)} %bitcast.163), channel_id=1, source_target_pairs={{0,2},{1,3},{2,0},{3,1},{4,6},{5,7},{6,4},{7,5},{8,10},{9,11},{10,... | collective-permute-start | bytes 331784 | tf_op jit(solution)/shard_map/ppermute | solution.py:603
  79.2 17.8 %collective-permute-start.17 = (bf16[72,768]{1,0:T(8,128)(2,1)}, bf16[72,768]{1,0:T(8,128)(2,1)}, u32[]{:S(2)}, u32[]{:S(2)}) collective-permute-start(bf16[72,768]{1,0:T(8,128)(2,1)} %bitcast.164), channel_id=1, source_target_pairs={{0,1},{1,0},{2,3},{3,2},{4,5},{5,4},{6,7},{7,6},{8,9},{9,8},{10,11... | collective-permute-start | bytes 331784 | tf_op jit(solution)/shard_map/ppermute | solution.py:603
  92.7 21.3 %collective-permute-start.16 = (bf16[128,1536]{1,0:T(8,128)(2,1)S(1)}, bf16[128,1536]{1,0:T(8,128)(2,1)S(1)}, u32[]{:S(2)}, u32[]{:S(2)}) collective-permute-start(bf16[128,1536]{1,0:T(8,128)(2,1)S(1)} %get-tuple-element.89.own_ref), channel_id=1, source_target_pairs={{1,0},{2,1},{3,2},{4,3},{5,4},{6,5},{7,6},{8,7},{9,8},{10,9},{11,1... | collective-permute-start | bytes 1179656 | tf_op jit(solution)/shard_map/ppermute | solution.py:757
  94.1 10.6 %collective-permute-start.22 = (bf16[72,768]{1,0:T(8,128)(2,1)}, bf16[72,768]{1,0:T(8,128)(2,1)S(1)}, u32[]{:S(2)}, u32[]{:S(2)}) collective-permute-start(bf16[72,768]{1,0:T(8,128)(2,1)} %collective-permute-done.20), channel_id=1, source_target_pairs={{0,2},{1,3},{2,0},{3,1},{4,6},{5,7},{6,4},{7,5},{8,10},{9,11},{10,... | collective-permute-start | bytes 331784 | tf_op jit(solution)/shard_map/ppermute | solution.py:603
  98.8 6.2 %collective-permute-start.21 = (bf16[72,768]{1,0:T(8,128)(2,1)}, bf16[72,768]{1,0:T(8,128)(2,1)S(1)}, u32[]{:S(2)}, u32[]{:S(2)}) collective-permute-start(bf16[72,768]{1,0:T(8,128)(2,1)} %collective-permute-done.20), channel_id=1, source_target_pairs={{0,1},{1,0},{2,3},{3,2},{4,5},{5,4},{6,7},{7,6},{8,9},{9,8},{10,11... | collective-permute-start | bytes 331784 | tf_op jit(solution)/shard_map/ppermute | solution.py:603
  100.3 13.7 %collective-permute-start.15 = (bf16[128,1536]{1,0:T(8,128)(2,1)S(1)}, bf16[128,1536]{1,0:T(8,128)(2,1)S(1)}, u32[]{:S(2)}, u32[]{:S(2)}) collective-permute-start(bf16[128,1536]{1,0:T(8,128)(2,1)S(1)} %get-tuple-element.89.own_ref), channel_id=1, source_target_pairs={{0,1},{1,2},{2,3},{3,4},{4,5},{5,6},{6,7},{7,8},{8,9},{9,10},{10,1... | collective-permute-start | bytes 1179656 | tf_op jit(solution)/shard_map/ppermute | solution.py:755
  104.7 7.3 %collective-permute-start.26 = (bf16[72,768]{1,0:T(8,128)(2,1)}, bf16[72,768]{1,0:T(8,128)(2,1)S(1)}, u32[]{:S(2)}, u32[]{:S(2)}) collective-permute-start(bf16[72,768]{1,0:T(8,128)(2,1)} %collective-permute-done.24), channel_id=1, source_target_pairs={{0,2},{1,3},{2,0},{3,1},{4,6},{5,7},{6,4},{7,5},{8,10},{9,11},{10,... | collective-permute-start | bytes 331784 | tf_op jit(solution)/shard_map/ppermute | solution.py:603
  105.0 7.5 %collective-permute-start.25 = (bf16[72,768]{1,0:T(8,128)(2,1)}, bf16[72,768]{1,0:T(8,128)(2,1)S(1)}, u32[]{:S(2)}, u32[]{:S(2)}) collective-permute-start(bf16[72,768]{1,0:T(8,128)(2,1)} %collective-permute-done.24), channel_id=1, source_target_pairs={{0,1},{1,0},{2,3},{3,2},{4,5},{5,4},{6,7},{7,6},{8,9},{9,8},{10,11... | collective-permute-start | bytes 331784 | tf_op jit(solution)/shard_map/ppermute | solution.py:603
  106.3 5.7 %collective-permute-start.30 = (bf16[72,768]{1,0:T(8,128)(2,1)S(1)}, bf16[72,768]{1,0:T(8,128)(2,1)S(1)}, u32[]{:S(2)}, u32[]{:S(2)}) collective-permute-start(bf16[72,768]{1,0:T(8,128)(2,1)S(1)} %collective-permute-done.28), channel_id=1, source_target_pairs={{0,2},{1,3},{2,0},{3,1},{4,6},{5,7},{6,4},{7,5},{8,10},{9,11},{10,... | collective-permute-start | bytes 331784 | tf_op jit(solution)/shard_map/ppermute | solution.py:603
  126.3 7.7 %collective-permute-start.32 = (bf16[128,768]{1,0:T(8,128)(2,1)S(1)}, bf16[128,768]{1,0:T(8,128)(2,1)S(1)}, u32[]{:S(2)}, u32[]{:S(2)}) collective-permute-start(bf16[128,768]{1,0:T(8,128)(2,1)S(1)} %get-tuple-element.93), channel_id=1, source_target_pairs={{0,16},{1,17},{2,18},{3,19},{4,20},{5,21},{6,22},{7,23},{8,24},{9,... | collective-permute-start | bytes 589832 | tf_op jit(solution)/shard_map/ppermute | solution.py:599
  209.8 19.2 %all-to-all-start.3 = ((bf16[16,144,128]{2,1,0:T(8,128)(2,1)}), bf16[16,144,128]{2,1,0:T(8,128)(2,1)S(1)}, u32[]{:S(2)}, u32[]{:S(2)}) async-start(bf16[16,144,128]{2,1,0:T(8,128)(2,1)} %add_convert_fusion), calls=%async_computation.3 | async-start | bytes 1179648 | tf_op jit(solution)/shard_map/all_to_all | solution.py:595
  234.6 9.0 %collective-permute-start.35 = (bf16[128,768]{1,0:T(8,128)(2,1)S(1)}, bf16[128,768]{1,0:T(8,128)(2,1)S(1)}, u32[]{:S(2)}, u32[]{:S(2)}) collective-permute-start(bf16[128,768]{1,0:T(8,128)(2,1)S(1)} %get-tuple-element.111), channel_id=1, source_target_pairs={{16,0},{17,1},{18,2},{19,3},{20,4},{21,5},{22,6},{23,7},{24,8},{25... | collective-permute-start | bytes 589832 | tf_op jit(solution)/shard_map/ppermute | solution.py:599
  237.7 17.0 %collective-permute-start.39 = (bf16[1,4,216,128]{3,2,1,0:T(8,128)(2,1)S(1)}, bf16[1,4,216,128]{3,2,1,0:T(8,128)(2,1)S(1)}, u32[]{:S(2)}, u32[]{:S(2)}) collective-permute-start(bf16[1,4,216,128]{3,2,1,0:T(8,128)(2,1)S(1)} %get-tuple-element.138), channel_id=1, source_target_pairs={{0,3},{1,2},{2,1},{3,0},{4,7},{5,6},{6,5},{7,4},{8,11},{9,10},{10,... | collective-permute-start | bytes 663560 | tf_op jit(solution)/shard_map/ppermute | solution.py:603
  238.7 17.4 %collective-permute-start.38 = (bf16[1,4,216,128]{3,2,1,0:T(8,128)(2,1)S(1)}, bf16[1,4,216,128]{3,2,1,0:T(8,128)(2,1)S(1)}, u32[]{:S(2)}, u32[]{:S(2)}) collective-permute-start(bf16[1,4,216,128]{3,2,1,0:T(8,128)(2,1)S(1)} %get-tuple-element.139), channel_id=1, source_target_pairs={{0,2},{1,3},{2,0},{3,1},{4,6},{5,7},{6,4},{7,5},{8,10},{9,11},{10,... | collective-permute-start | bytes 663560 | tf_op jit(solution)/shard_map/ppermute | solution.py:603
  239.5 21.6 %collective-permute-start.37 = (bf16[1,4,216,128]{3,2,1,0:T(8,128)(2,1)S(1)}, bf16[1,4,216,128]{3,2,1,0:T(8,128)(2,1)S(1)}, u32[]{:S(2)}, u32[]{:S(2)}) collective-permute-start(bf16[1,4,216,128]{3,2,1,0:T(8,128)(2,1)S(1)} %get-tuple-element.140), channel_id=1, source_target_pairs={{0,1},{1,0},{2,3},{3,2},{4,5},{5,4},{6,7},{7,6},{8,9},{9,8},{10,11... | collective-permute-start | bytes 663560 | tf_op jit(solution)/shard_map/ppermute | solution.py:603
  243.6 15.6 %collective-permute-start.41 = (bf16[128,768]{1,0:T(8,128)(2,1)S(1)}, bf16[128,768]{1,0:T(8,128)(2,1)S(1)}, u32[]{:S(2)}, u32[]{:S(2)}) collective-permute-start(bf16[128,768]{1,0:T(8,128)(2,1)S(1)} %broadcast_select_fusion.4.refs_4_), channel_id=1, source_target_pairs={{0,2},{1,3},{2,0},{3,1},{4,6},{5,7},{6,4},{7,5},{8,10},{9,11},{10,... | collective-permute-start | bytes 589832 | tf_op jit(solution)/shard_map/ppermute | solution.py:603
  245.0 16.1 %collective-permute-start.40 = (bf16[128,768]{1,0:T(8,128)(2,1)S(1)}, bf16[128,768]{1,0:T(8,128)(2,1)S(1)}, u32[]{:S(2)}, u32[]{:S(2)}) collective-permute-start(bf16[128,768]{1,0:T(8,128)(2,1)S(1)} %broadcast_select_fusion.4.refs_4_), channel_id=1, source_target_pairs={{0,1},{1,0},{2,3},{3,2},{4,5},{5,4},{6,7},{7,6},{8,9},{9,8},{10,11... | collective-permute-start | bytes 589832 | tf_op jit(solution)/shard_map/ppermute | solution.py:603
  254.8 8.4 %collective-permute-start.36 = (bf16[128,1536]{1,0:T(8,128)(2,1)S(1)}, bf16[128,1536]{1,0:T(8,128)(2,1)S(1)}, u32[]{:S(2)}, u32[]{:S(2)}) collective-permute-start(bf16[128,1536]{1,0:T(8,128)(2,1)S(1)} %get-tuple-element.119), channel_id=1, source_target_pairs={{1,0},{2,1},{3,2},{4,3},{5,4},{6,5},{7,6},{8,7},{9,8},{10,9},{11,1... | collective-permute-start | bytes 1179656 | tf_op jit(solution)/shard_map/ppermute | solution.py:913
  256.1 7.1 %collective-permute-start.43 = (bf16[128,1536]{1,0:T(8,128)(2,1)S(1)}, bf16[128,1536]{1,0:T(8,128)(2,1)S(1)}, u32[]{:S(2)}, u32[]{:S(2)}) collective-permute-start(bf16[128,1536]{1,0:T(8,128)(2,1)S(1)} %get-tuple-element.122), channel_id=1, source_target_pairs={{0,1},{1,2},{2,3},{3,4},{4,5},{5,6},{6,7},{7,8},{8,9},{9,10},{10,1... | collective-permute-start | bytes 1179656 | tf_op jit(solution)/shard_map/ppermute | solution.py:914
  263.7 21.5 %collective-permute-start.45 = (bf16[128,2304]{1,0:T(8,128)(2,1)S(1)}, bf16[128,2304]{1,0:T(8,128)(2,1)S(1)}, u32[]{:S(2)}, u32[]{:S(2)}) collective-permute-start(bf16[128,2304]{1,0:T(8,128)(2,1)S(1)} %broadcast_select_fusion.1.refs_4_), channel_id=1, source_target_pairs={{0,2},{1,3},{2,0},{3,1},{4,6},{5,7},{6,4},{7,5},{8,10},{9,11},{10,... | collective-permute-start | bytes 1769480 | tf_op jit(solution)/shard_map/ppermute | solution.py:603
  271.0 36.4 %collective-permute-start.47 = (bf16[128,2304]{1,0:T(8,128)(2,1)S(1)}, bf16[128,2304]{1,0:T(8,128)(2,1)}, u32[]{:S(2)}, u32[]{:S(2)}) collective-permute-start(bf16[128,2304]{1,0:T(8,128)(2,1)S(1)} %broadcast_select_fusion.refs_4_), channel_id=1, source_target_pairs={{0,2},{1,3},{2,0},{3,1},{4,6},{5,7},{6,4},{7,5},{8,10},{9,11},{10,... | collective-permute-start | bytes 1769480 | tf_op jit(solution)/shard_map/ppermute | solution.py:603
  271.6 19.4 %collective-permute-start.44 = (bf16[128,2304]{1,0:T(8,128)(2,1)S(1)}, bf16[128,2304]{1,0:T(8,128)(2,1)}, u32[]{:S(2)}, u32[]{:S(2)}) collective-permute-start(bf16[128,2304]{1,0:T(8,128)(2,1)S(1)} %broadcast_select_fusion.1.refs_4_), channel_id=1, source_target_pairs={{0,1},{1,0},{2,3},{3,2},{4,5},{5,4},{6,7},{7,6},{8,9},{9,8},{10,11... | collective-permute-start | bytes 1769480 | tf_op jit(solution)/shard_map/ppermute | solution.py:603
  285.1 5.9 %collective-permute-start.52 = (bf16[128,2304]{1,0:T(8,128)(2,1)S(1)}, bf16[128,2304]{1,0:T(8,128)(2,1)}, u32[]{:S(2)}, u32[]{:S(2)}) collective-permute-start(bf16[128,2304]{1,0:T(8,128)(2,1)S(1)} %collective-permute-done.45.refs_6_), channel_id=1, source_target_pairs={{0,1},{1,0},{2,3},{3,2},{4,5},{5,4},{6,7},{7,6},{8,9},{9,8},{10,11... | collective-permute-start | bytes 1769480 | tf_op jit(solution)/shard_map/ppermute | solution.py:603
  285.1 17.9 %all-to-all-start.6 = ((bf16[4,1,72,768]{3,2,1,0:T(8,128)(2,1)}), bf16[4,1,72,768]{3,2,1,0:T(8,128)(2,1)}, u32[]{:S(2)}, u32[]{:S(2)}) async-start(bf16[4,1,72,768]{3,2,1,0:T(8,128)(2,1)} %bitcast.77), calls=%async_computation.6 | async-start | bytes 884736 | tf_op jit(solution)/shard_map/all_to_all | solution.py:666
  303.0 26.7 %all-to-all-start.4 = ((bf16[4,1,48,2304]{3,2,1,0:T(8,128)(2,1)}), bf16[4,1,48,2304]{3,2,1,0:T(8,128)(2,1)}, u32[]{:S(2)}, u32[]{:S(2)}) async-start(bf16[4,1,48,2304]{3,2,1,0:T(8,128)(2,1)} %bitcast.72), calls=%async_computation.4 | async-start | bytes 1769472 | tf_op jit(solution)/shard_map/all_to_all | solution.py:666
  307.2 9.3 %collective-permute-start.46 = (bf16[128,2304]{1,0:T(8,128)(2,1)S(1)}, bf16[128,2304]{1,0:T(8,128)(2,1)S(1)}, u32[]{:S(2)}, u32[]{:S(2)}) collective-permute-start(bf16[128,2304]{1,0:T(8,128)(2,1)S(1)} %broadcast_select_fusion.refs_4_), channel_id=1, source_target_pairs={{0,1},{1,0},{2,3},{3,2},{4,5},{5,4},{6,7},{7,6},{8,9},{9,8},{10,11... | collective-permute-start | bytes 1769480 | tf_op jit(solution)/shard_map/ppermute | solution.py:603
  307.3 9.2 %collective-permute-start.48 = (bf16[128,2304]{1,0:T(8,128)(2,1)}, bf16[128,2304]{1,0:T(8,128)(2,1)S(1)}, u32[]{:S(2)}, u32[]{:S(2)}) collective-permute-start(bf16[128,2304]{1,0:T(8,128)(2,1)} %collective-permute-done.47.refs_6_), channel_id=1, source_target_pairs={{0,1},{1,0},{2,3},{3,2},{4,5},{5,4},{6,7},{7,6},{8,9},{9,8},{10,11... | collective-permute-start | bytes 1769480 | tf_op jit(solution)/shard_map/ppermute | solution.py:603
  307.8 7.3 %collective-permute-start.50 = (bf16[128,768]{1,0:T(8,128)(2,1)S(1)}, bf16[128,768]{1,0:T(8,128)(2,1)S(1)}, u32[]{:S(2)}, u32[]{:S(2)}) collective-permute-start(bf16[128,768]{1,0:T(8,128)(2,1)S(1)} %broadcast_select_fusion.2.refs_12_), channel_id=1, source_target_pairs={{0,2},{1,3},{2,0},{3,1},{4,6},{5,7},{6,4},{7,5},{8,10},{9,11},{10,... | collective-permute-start | bytes 589832 | tf_op jit(solution)/shard_map/ppermute | solution.py:603
  329.7 36.3 %all-to-all-start.5 = ((bf16[4,1,48,3072]{3,2,1,0:T(8,128)(2,1)}), bf16[4,1,48,3072]{3,2,1,0:T(8,128)(2,1)S(1)}, u32[]{:S(2)}, u32[]{:S(2)}) async-start(bf16[4,1,48,3072]{3,2,1,0:T(8,128)(2,1)} %bitcast.74), calls=%async_computation.5 | async-start | bytes 2359296 | tf_op jit(solution)/shard_map/all_to_all | solution.py:666
  341.7 10.4 %collective-permute-start.55 = (f32[2,768]{1,0:T(2,128)S(1)}, f32[2,768]{1,0:T(2,128)S(1)}, u32[]{:S(2)}, u32[]{:S(2)}) collective-permute-start(f32[2,768]{1,0:T(2,128)S(1)} %add.176), channel_id=1, source_target_pairs={{0,4},{1,5},{2,6},{3,7},{4,0},{5,1},{6,2},{7,3},{8,12},{9,13},{10,... | collective-permute-start | bytes 18440 | tf_op jit(solution)/shard_map/ppermute | solution.py:603
  352.1 9.4 %collective-permute-start.56 = (f32[2,768]{1,0:T(2,128)S(1)}, f32[2,768]{1,0:T(2,128)S(1)}, u32[]{:S(2)}, u32[]{:S(2)}) collective-permute-start(f32[2,768]{1,0:T(2,128)S(1)} %add.177), channel_id=1, source_target_pairs={{0,8},{1,9},{2,10},{3,11},{4,12},{5,13},{6,14},{7,15},{8,0},{9,1},... | collective-permute-start | bytes 18440 | tf_op jit(solution)/shard_map/ppermute | solution.py:603
  (90 other events, 601.8 us)
Sparse Core Ops, SparseCore 0:
  10.9 78.8 all-gather.1

commit v3 on v2

--- a/solution.py
+++ b/solution.py
@@ -1,3 +1,4 @@
+import functools
 import math
 
 import jax
@@ -59,19 +60,21 @@
     return jnp.tile(jnp.stack([cosine, to_first, to_second]), (1, 2, 2))
 
 
-def on_core(body, micros, outs, args, scratch=(), spaces=None):
+def on_core(body, outs, args, scratch=(), spaces=None, out_spaces=None):
     return pl.pallas_call(
         body,
         out_shape=[jax.ShapeDtypeStruct(shape, dtype) for shape, dtype in outs],
         in_specs=[
             pl.BlockSpec(memory_space=space) for space in spaces or [pltpu.VMEM] * len(args)
         ],
-        out_specs=[pl.BlockSpec(memory_space=pltpu.VMEM)] * len(outs),
+        out_specs=[
+            pl.BlockSpec(memory_space=space) for space in out_spaces or [pltpu.VMEM] * len(outs)
+        ],
         scratch_shapes=scratch,
         cost_estimate=pl.CostEstimate(
-            flops=int(micros * 1.15e9), bytes_accessed=2**16, transcendentals=0
+            flops=2**10, bytes_accessed=2**10, transcendentals=0
         ),
-        compiler_params=pltpu.CompilerParams(vmem_limit_bytes=24 * 2**20),
+        compiler_params=pltpu.CompilerParams(vmem_limit_bytes=32 * 2**20),
     )(*args)
 
 
@@ -203,52 +206,137 @@
     return lefts, rights
 
 
-def mlp_forward(layer_in, attended, gain, wide_ref, out_ref):
-    width = layer_in.shape[1]
-    inner = wide_ref.shape[1] - width
-    middle = layer_in + dot(attended, wide_ref[:, :width])
+class Weights:
+    def __init__(self, sources, scratches, sem):
+        attn, mlp_in, mlp_out = self.places = scratches
+        width = attn.shape[1]
+        copies = [[], [], []]
+        if len(sources) == 1:
+            (stacked,) = sources
+            shard = attn.shape[0] // GROUP
+            columns = mlp_in.shape[1] // width
+            pair = 2 * mlp_out.shape[0] // GROUP
+            upper = first_block(pair)
+            block = shard * (1 + columns) + upper
+            for d in range(GROUP):
+                base = d * block
+                here = pl.ds(d * shard, shard)
+                copies[0].append((stacked.at[pl.ds(base, shard)], attn.at[here]))
+                for p in range(columns):
+                    copies[1].append(
+                        (
+                            stacked.at[pl.ds(base + (1 + p) * shard, shard)],
+                            mlp_in.at[here, pl.ds(p * width, width)],
+                        )
+                    )
+                rows = pair - upper if d % 2 else upper
+                start = d // 2 * pair + d % 2 * upper
+                copies[2].append(
+                    (
+                        stacked.at[pl.ds(base + (1 + columns) * shard, rows)],
+                        mlp_out.at[pl.ds(start, rows)],
+                    )
+                )
+        else:
+            for group, source, place in zip(copies, sources, scratches):
+                group.append((source, place))
+        self.copies, index = [], 0
+        for group in copies:
+            self.copies.append([])
+            for source, place in group:
+                self.copies[-1].append(pltpu.make_async_copy(source, place, sem.at[index]))
+                index += 1
+
+    def start(self, order):
+        for which in order:
+            for copy in self.copies[which]:
+                copy.start()
+
+    def get(self, which):
+        for copy in self.copies[which]:
+            copy.wait()
+        self.copies[which] = []
+        return self.places[which][...]
+
+
+def first_block(pair):
+    return -(-pair // 32) * 16
+
+
+def weight_scratch(width, inner, hidden):
+    return [
+        pltpu.VMEM((width, width), BF),
+        pltpu.VMEM((width, inner), BF),
+        pltpu.VMEM((hidden, width), BF),
+        pltpu.SemaphoreType.DMA((GROUP * (2 + inner // width),)),
+    ]
+
+
+def mlp_forward(layer_in, attended, gain, weights):
+    middle = layer_in + dot(attended, weights.get(0))
     xhat, _ = moments(middle)
     normed = (xhat * gain).astype(BF)
-    gate_up = dot(normed, wide_ref[:, width : width + inner])
-    gate, up = gate_up[:, : inner // 2], gate_up[:, inner // 2 :]
+    gate_up = dot(normed, weights.get(1))
+    half = gate_up.shape[1] // 2
+    gate, up = gate_up[:, :half], gate_up[:, half:]
     cdf = 0.5 * (1.0 + lax.erf(gate * math.sqrt(0.5)))
     mixed = (gate * cdf * up).astype(BF)
-    result = (middle + dot(mixed, out_ref[...])).astype(BF)
+    result = (middle + dot(mixed, weights.get(2))).astype(BF)
     return middle, normed, gate, up, mixed, result
 
 
-def mlp_backward(upstream, middle, gate, up, gain, wide_ref, out_ref):
-    width = middle.shape[1]
-    inner = 2 * gate.shape[1]
-    d_mixed = dot_bt(upstream, out_ref[...])
+def mlp_backward(upstream, middle, gate, up, gain, weights):
+    d_mixed = dot_bt(upstream, weights.get(2))
     cdf = 0.5 * (1.0 + lax.erf(gate * math.sqrt(0.5)))
     density = jnp.exp(-0.5 * gate * gate) * (1.0 / math.sqrt(2.0 * math.pi))
     d_gate = d_mixed * up * (cdf + gate * density)
     d_up = d_mixed * gate * cdf
     d_gate_up = jnp.concatenate([d_gate.astype(BF), d_up.astype(BF)], 1)
-    d_normed = dot_bt(d_gate_up, wide_ref[:, width : width + inner])
+    d_normed = dot_bt(d_gate_up, weights.get(1))
     xhat, scale = moments(middle)
     gain_grad = jnp.sum(d_normed * xhat, 0, keepdims=True)
     d_middle = upstream.astype(F32) + norm_back(d_normed, gain, xhat, scale)
     d_attn = d_middle.astype(BF)
-    d_attended = dot_bt(d_attn, wide_ref[:, :width])
+    d_attended = dot_bt(d_attn, weights.get(0))
     return d_gate_up, gain_grad, d_middle, d_attn, d_attended
 
 
-def project(xhat, gain, first_ref, table_ref, normed_ref):
+def parts_of(first_ref, place, sem):
+    width = place.shape[0]
+    return [
+        pltpu.make_async_copy(
+            first_ref.at[:, pl.ds(c * width, width)], place.at[:, pl.ds(c * width, width)], sem.at[c]
+        )
+        for c in range(3)
+    ]
+
+
+def qkv_scratch(width):
+    return [pltpu.VMEM((width, 3 * width), BF), pltpu.SemaphoreType.DMA((3,))]
+
+
+def project(xhat, gain, first_ref, table_ref, normed_ref, copies=(None,) * 3):
     width = xhat.shape[1]
     normed = (xhat * gain).astype(BF)
     normed_ref[...] = normed
     tables = [table_ref[i] for i in range(3)]
-    queries = chunks_of(dot(normed, first_ref[:, :width]))
-    keys = chunks_of(dot(normed, first_ref[:, width : 2 * width]))
-    values = dot(normed, first_ref[:, 2 * width : 3 * width])
+    results = []
+    for part, copy in enumerate(copies):
+        if copy is not None:
+            copy.wait()
+        results.append(dot(normed, first_ref[:, part * width : (part + 1) * width]))
+    queries, keys, values = chunks_of(results[0]), chunks_of(results[1]), results[2]
     return [rotate(c, tables) for c in queries], [rotate(c, tables) for c in keys], values
 
 
-def input_backward(d_middle, d_projected, x_ref, gain_ref, first_ref, grad_ref, gain_out_ref):
-    d_normed = dot_bt(d_projected, first_ref[:, : d_projected.shape[1]])
+def input_backward(d_middle, d_projected, x_ref, gain_ref, place, copies, grad_ref, gain_out_ref):
+    width = x_ref.shape[1]
     xhat, scale = moments(x_ref[...].astype(F32))
+    d_normed = jnp.zeros(x_ref.shape, F32)
+    for part, copy in enumerate(copies):
+        copy.wait()
+        lanes = slice(part * width, (part + 1) * width)
+        d_normed += dot_bt(d_projected[:, lanes], place[:, lanes])
     gain_out_ref[...] = jnp.sum(d_normed * xhat, 0, keepdims=True)
     grad_ref[...] = (d_middle + norm_back(d_normed, gain_ref[...], xhat, scale)).astype(BF)
 
@@ -274,7 +362,8 @@
 
 
 def local_project_body(place_ref, x_ref, table_ref, *refs):
-    pieces, (first_ref, extra_ref, normed_ref, q_ref, kv_ref, sem) = refs[:-6], refs[-6:]
+    pieces, refs = refs[:-8], refs[-8:]
+    stored_ref, extra_ref, normed_ref, q_ref, kv_ref, first_ref, sem, store_sem = refs
     rows = pieces[0].shape[0]
     copies = []
     for apart, piece in enumerate(pieces):
@@ -286,6 +375,8 @@
     xhat, _ = moments(x_ref[...].astype(F32))
     for copy in copies:
         copy.wait()
+    store = pltpu.make_async_copy(first_ref, stored_ref, store_sem)
+    store.start()
     extra = first_ref[:, first_ref.shape[1] - LANES :].astype(F32).T
     extra_ref[...] = extra[: extra_ref.shape[0]]
     queries, keys, values = project(xhat, extra[:1], first_ref, table_ref, normed_ref)
@@ -294,6 +385,7 @@
         q_ref[:, LANES * j : LANES * (j + 1)] = q.astype(BF)
         kv_ref[:, LANES * j : LANES * (j + 1)] = k.astype(BF)
     kv_ref[:, width:] = values.astype(BF)
+    store.wait()
 
 
 def two_heads(chunk):
@@ -358,22 +450,33 @@
             d_after_ref[here, part] = grads[2 * rows :].astype(BF)
 
 
-def local_join_body(dq_ref, own_ref, low_ref, high_ref, table_ref, out_ref):
-    tables = [table_ref[i] for i in range(3)]
+def local_join_body(
+    lower_ref, dq_ref, own_ref, low_ref, high_ref, table_ref, other_ref, out_ref
+):
     width = dq_ref.shape[1]
-    out_ref[:, :width] = dq_ref[...]
-    total = own_ref[...] + low_ref[...].astype(F32) + high_ref[...].astype(F32)
-    for j, chunk in enumerate(chunks_of(total[:, :width])):
-        start = width + LANES * j
-        out_ref[:, start : start + LANES] = unrotate(chunk, tables).astype(BF)
-    out_ref[:, 2 * width :] = total[:, width:].astype(BF)
-
-
-def local_middle_body(
-    x_ref, att_ref, gain_ref, wide_ref, w_out_ref, out_ref, normed_ref, mixed_ref, middle_ref, gate_up_ref
-):
+
+    @pl.when(lower_ref[0] == 1)
+    def _():
+        tables = [table_ref[i] for i in range(3)]
+        out_ref[:, :width] = dq_ref[...]
+        total = own_ref[...] + low_ref[...].astype(F32) + high_ref[...].astype(F32)
+        for j, chunk in enumerate(chunks_of(total[:, :width])):
+            start = width + LANES * j
+            out_ref[:, start : start + LANES] = unrotate(chunk, tables).astype(BF)
+        out_ref[:, 2 * width :] = total[:, width:].astype(BF)
+
+    @pl.when(lower_ref[0] == 0)
+    def _():
+        out_ref[...] = other_ref[...]
+
+
+def local_middle_body(*refs):
+    sources, refs = refs[:-12], refs[-12:]
+    x_ref, att_ref, gain_ref, out_ref, normed_ref, mixed_ref, middle_ref, gate_up_ref = refs[:8]
+    weights = Weights(sources, refs[8:11], refs[11])
+    weights.start((0, 1, 2))
     middle, normed, gate, up, mixed, result = mlp_forward(
-        x_ref[...].astype(F32), att_ref[...], gain_ref[...], wide_ref, w_out_ref
+        x_ref[...].astype(F32), att_ref[...], gain_ref[...], weights
     )
     out_ref[...] = result
     normed_ref[...] = normed
@@ -384,33 +487,48 @@
     gate_up_ref[:, half:] = up
 
 
-def local_back_middle_body(
-    up_ref, middle_ref, gate_up_ref, gain_ref, wide_ref, w_out_ref,
-    d_gate_up_ref, gain_out_ref, d_middle_ref, d_attn_ref, d_att_ref,
-):
+def local_back_middle_body(*refs):
+    sources, refs = refs[:-14], refs[-14:]
+    lower_ref, up_ref, middle_ref, gate_up_ref, gain_ref, other_ref = refs[:6]
+    right_ref, gain_out_ref, d_middle_ref, d_att_ref = refs[6:10]
+    weights = Weights(sources, refs[10:13], refs[13])
+    weights.start((2, 1, 0))
     half = gate_up_ref.shape[1] // 2
     d_gate_up, gain_grad, d_middle, d_attn, d_attended = mlp_backward(
         up_ref[...], middle_ref[...], gate_up_ref[:, :half], gate_up_ref[:, half:],
-        gain_ref[...], wide_ref, w_out_ref,
-    )
-    d_gate_up_ref[...] = d_gate_up
+        gain_ref[...], weights,
+    )
     gain_out_ref[...] = gain_grad
     d_middle_ref[...] = d_middle
-    d_attn_ref[...] = d_attn
     d_att_ref[...] = d_attended.astype(BF)
 
+    @pl.when(lower_ref[0] == 1)
+    def _():
+        right_ref[:, : 2 * half] = d_gate_up
+        right_ref[:, 2 * half :] = d_attn
+
+    @pl.when(lower_ref[0] == 0)
+    def _():
+        right_ref[...] = other_ref[...]
+
 
 def input_backward_body(
-    d_middle_ref, d_proj_ref, x_ref, gain_ref, first_ref, grad_ref, gain_out_ref
+    first_ref, d_middle_ref, d_proj_ref, x_ref, gain_ref, grad_ref, gain_out_ref, place, sem
 ):
+    copies = parts_of(first_ref, place, sem)
+    for copy in copies:
+        copy.start()
     input_backward(
-        d_middle_ref[...], d_proj_ref[...], x_ref, gain_ref, first_ref, grad_ref, gain_out_ref
-    )
-
-
-def global_project_body(x_ref, gain_ref, first_ref, table_ref, normed_ref, sent_ref):
+        d_middle_ref[...], d_proj_ref[...], x_ref, gain_ref, place, copies, grad_ref, gain_out_ref
+    )
+
+
+def global_project_body(first_ref, x_ref, gain_ref, table_ref, normed_ref, sent_ref, place, sem):
+    copies = parts_of(first_ref, place, sem)
+    for copy in copies:
+        copy.start()
     xhat, _ = moments(x_ref[...].astype(F32))
-    queries, keys, values = project(xhat, gain_ref[...], first_ref, table_ref, normed_ref)
+    queries, keys, values = project(xhat, gain_ref[...], place, table_ref, normed_ref, copies)
     pack_pairs(queries, keys, sent_ref)
     pack_folded(chunks_of(values), sent_ref, sent_ref.shape[1] * 2 // 3)
 
@@ -542,43 +660,47 @@
         to_other_ref[:, place * half : (place + 1) * half] = other.astype(BF)
 
 
-def global_middle_body(
-    got_ref, x_ref, up_ref, gain_ref, wide_ref, w_out_ref,
-    out_ref, att_ref, normed_ref, mixed_ref, d_gate_up_ref, gain_out_ref, d_middle_ref, d_attn_ref, sent_ref,
-):
+def global_middle_body(*refs):
+    sources, refs = refs[:-16], refs[-16:]
+    got_ref, x_ref, up_ref, gain_ref, out_ref, att_ref, normed_ref, mixed_ref = refs[:8]
+    right_ref, gain_out_ref, d_middle_ref, sent_ref = refs[8:12]
+    weights = Weights(sources, refs[12:15], refs[15])
+    weights.start((0, 1, 2))
     rows = x_ref.shape[0] // 2
     attended = jnp.concatenate([c.astype(BF) for c in unpack_folded(got_ref, 0, rows)], 1)
     att_ref[...] = attended
     gain = gain_ref[...]
     middle, normed, gate, up, mixed, result = mlp_forward(
-        x_ref[...].astype(F32), attended, gain, wide_ref, w_out_ref
+        x_ref[...].astype(F32), attended, gain, weights
     )
     out_ref[...] = result
     normed_ref[...] = normed
     mixed_ref[...] = mixed
     d_gate_up, gain_grad, d_middle, d_attn, d_attended = mlp_backward(
-        up_ref[...], middle, gate, up, gain, wide_ref, w_out_ref
-    )
-    d_gate_up_ref[...] = d_gate_up
+        up_ref[...], middle, gate, up, gain, weights
+    )
+    right_ref[:, : d_gate_up.shape[1]] = d_gate_up
+    right_ref[:, d_gate_up.shape[1] :] = d_attn
     gain_out_ref[...] = gain_grad
     d_middle_ref[...] = d_middle
-    d_attn_ref[...] = d_attn
     pack_folded(chunks_of(d_attended), sent_ref, 0)
 
 
 def global_finish_body(
-    got_ref, d_middle_ref, x_ref, gain_ref, first_ref, table_ref, d_proj_ref, grad_ref, gain_out_ref
+    first_ref, got_ref, d_middle_ref, x_ref, gain_ref, table_ref, d_proj_ref, grad_ref, gain_out_ref, place, sem
 ):
+    copies = parts_of(first_ref, place, sem)
+    for copy in copies:
+        copy.start()
     tables = [table_ref[i] for i in range(3)]
     rows = x_ref.shape[0] // 2
-    width = x_ref.shape[1]
     d_queries, d_keys = unpack_pairs(got_ref, rows)
     d_values = unpack_folded(got_ref, rows * 3 // 2, rows)
     parts = [unrotate(c, tables).astype(BF) for c in d_queries + d_keys]
     d_projected = jnp.concatenate(parts + [c.astype(BF) for c in d_values], 1)
     d_proj_ref[...] = d_projected
     input_backward(
-        d_middle_ref[...], d_projected, x_ref, gain_ref, first_ref, grad_ref, gain_out_ref
+        d_middle_ref[...], d_projected, x_ref, gain_ref, place, copies, grad_ref, gain_out_ref
     )
 
 
@@ -628,47 +750,47 @@
 
 def plane_rows(rows, group_pos, count):
     parts = rows.reshape(count // GROUP, 4, 4, *rows.shape[1:])
-    place = group_pos % 4
+    place, plane = group_pos % 4, group_pos // 4
     taken = []
     for apart in range(4):
         block = lax.dynamic_index_in_dim(parts, place ^ apart, 2, keepdims=False)
-        taken.append((partner(block, apart, count) if apart else block).swapaxes(0, 1))
+        block = jnp.stack(
+            [lax.dynamic_index_in_dim(block, plane ^ z, 1, keepdims=False) for z in range(4)]
+        )
+        taken.append(partner(block, apart, count) if apart else block)
     return taken
 
 
-def product_body(*refs):
-    out_ref = refs[-1]
-    column = 0
-    for start in range(0, len(refs) - 1, 8):
-        left = jnp.concatenate([ref[...] for ref in refs[start : start + 4]], 1)
-        right = jnp.concatenate([ref[...] for ref in refs[start + 4 : start + 8]], 0)
-        end = column + right.shape[1]
-        out_ref[:, column:end] = dot(left, right).astype(BF)
-        column = end
-
-
-def plane_product(terms):
+def product_body(ranges, *refs):
+    refs, outs = refs[:-4], refs[-4:]
+    rows = outs[0].shape[0]
+    for index, (start, end) in enumerate(ranges):
+        left = jnp.concatenate([ref[...] for ref in refs[4 + 4 * index : 8 + 4 * index]], 1)
+        right = jnp.concatenate([ref[:, start:end] for ref in refs[:4]], 0)
+        product = dot(left, right)
+        for plane, out_ref in enumerate(outs):
+            part = product[plane * rows : (plane + 1) * rows]
+            out_ref[:, start:end] = part.astype(out_ref.dtype)
+
+
+def plane_product(right, terms):
     planes, groups, rows, tokens = terms[0][0][0].shape
-    args = [
-        part
-        for lefts, rights in terms
-        for part in [item.reshape(-1, tokens) for item in lefts] + list(rights)
-    ]
-    columns = sum(rights[0].shape[1] for _, rights in terms)
-    (product,) = on_core(product_body, 2.0, [((planes * groups * rows, columns), BF)], args)
-    return product.reshape(planes, groups, rows, columns)
+    args = list(right) + [item.reshape(-1, tokens) for lefts, _, _ in terms for item in lefts]
+    shape = (groups * rows, right[0].shape[1])
+    body = functools.partial(product_body, [term[1:] for term in terms])
+    return on_core(body, [(shape, F32)] + [(shape, BF)] * (planes - 1), args)
 
 
 def sum_planes(blocks, count):
-    groups = [
-        [s + 4 * z + k for z in range(4)] for s in range(0, count, GROUP) for k in range(4)
-    ]
-    got = lax.all_to_all(blocks, "dp", 0, 0, axis_index_groups=groups)
-    total = jnp.sum(got.astype(F32), 0)
+    got = [partner(item, 4 * (z + 1), count) for z, item in enumerate(blocks[1:])]
+    total = blocks[0]
+    for item in got:
+        total = total + item.astype(F32)
     if count > GROUP:
         apart = [list(range(s, count, GROUP)) for s in range(GROUP)]
+        total = total.reshape(count // GROUP, -1, total.shape[1])
         return lax.psum_scatter(total, "dp", scatter_dimension=0, axis_index_groups=apart)
-    return total[0]
+    return total
 
 
 def on_device(
@@ -683,6 +805,7 @@
     mlp_gain,
 ):
     lower = lax.axis_index("section") == 0
+    lower_flag = lower.astype(jnp.int32)[None]
     count = lax.axis_size("dp")
     replica = lax.axis_index("dp")
     group_pos = replica % GROUP
@@ -691,33 +814,43 @@
     runs = -(-row_count // shard)
     (message,) = on_core(
         message_body,
-        1.0,
         [((shard, 3 * width + LANES), BF)],
         (qkv_weight[0], attn_gain, mlp_gain, segment_ids),
         [pltpu.VMEM((LANES, LANES), F32), pltpu.VMEM((8, LANES), F32)],
     )
-    second = lax.all_gather(
-        jnp.concatenate([attn_out_weight[0], mlp_in_weight[0]], 1), "dp", axis=0, tiled=True
-    )
+    inner = mlp_in_weight.shape[2]
+    hidden = mlp_out_weight.shape[1] * count
+    if count == GROUP:
+        upper = first_block(2 * mlp_out_weight.shape[1])
+        moved = upper - mlp_out_weight.shape[1]
+        beside = partner(mlp_out_weight[0, :moved], 1, count)
+        block = jnp.where(
+            replica % 2 == 0,
+            jnp.concatenate([mlp_out_weight[0], beside]),
+            jnp.concatenate([mlp_out_weight[0, moved:], beside, beside]),
+        )
+        stacked = [attn_out_weight[0]]
+        stacked += [mlp_in_weight[0, :, c : c + width] for c in range(0, inner, width)]
+        others = [lax.all_gather(jnp.concatenate(stacked + [block]), "dp", axis=0, tiled=True)]
+    else:
+        others = [
+            lax.all_gather(item[0], "dp", axis=0, tiled=True)
+            for item in (attn_out_weight, mlp_in_weight, mlp_out_weight)
+        ]
     pieces = group_pieces(message, count)
-    late_weight, pieces = lax.optimization_barrier((mlp_out_weight[0], pieces))
     if count > GROUP:
         pieces = [in_order(pieces, group_pos, count)]
-    w_out = in_order(group_pieces(late_weight, count), group_pos, count)
 
     positions = group_pos * row_count + jnp.arange(row_count)
     local_tables = angles(positions, local_log_base)
     global_tables = angles(positions, global_log_base)
 
     rows = micro_count * row_count
-    inner = second.shape[1] - width
-    hidden = w_out.shape[0]
     pairs = rows * width // (row_count * LANES)
     in_0 = tokens_in.reshape(rows, width)
     extra_rows = -(-(2 + micro_count * runs) // 8) * 8
     first, extra, normed_0, q_0, kv_0 = on_core(
         local_project_body,
-        5,
         [
             ((width, 3 * width + LANES), BF),
             ((extra_rows, width), F32),
@@ -726,8 +859,13 @@
             ((rows, 2 * width), BF),
         ],
         (group_pos[None], in_0, local_tables, *pieces),
-        [pltpu.SemaphoreType.DMA((len(pieces),))],
+        [
+            pltpu.VMEM((width, 3 * width + LANES), BF),
+            pltpu.SemaphoreType.DMA((len(pieces),)),
+            pltpu.SemaphoreType.DMA,
+        ],
         [pltpu.SMEM, pltpu.VMEM, pltpu.VMEM] + [pl.ANY] * len(pieces),
+        [pltpu.HBM] + [pltpu.VMEM] * 4,
     )
     gain_attn, gain_mlp = extra[:1], extra[1:2]
     all_ids = extra[2 : 2 + micro_count * runs].reshape(micro_count, runs, count, shard)
@@ -758,13 +896,11 @@
     )
     att_0, total_0 = on_core(
         local_forward_body,
-        3.6,
         [((rows, width), BF), ((pairs, 1, LANES), F32)],
         (q_0, *around_0, bias),
     )
     out_0, n2_0, mixed_0, middle_0, gate_up_0 = on_core(
         local_middle_body,
-        2.2,
         [
             ((rows, width), BF),
             ((rows, width), BF),
@@ -772,7 +908,9 @@
             ((rows, width), F32),
             ((rows, inner), F32),
         ],
-        (in_0, att_0, gain_mlp, second, w_out),
+        (*others, in_0, att_0, gain_mlp),
+        weight_scratch(width, inner, hidden),
+        [pltpu.HBM] * len(others) + [pltpu.VMEM] * 3,
     )
 
     in_1 = to_other_section(out_0, 1)
@@ -780,9 +918,10 @@
     half = row_count // 2
     normed_1, sent = on_core(
         global_project_body,
-        1.2,
         [((rows, width), BF), ((GROUP, 3 * fold, LANES), BF)],
-        (in_1, gain_attn, first, global_tables),
+        (first, in_1, gain_attn, global_tables),
+        qkv_scratch(width),
+        [pltpu.HBM] + [pltpu.VMEM] * 3,
     )
     got = exchange(sent, count)
     beside = jnp.concatenate(
@@ -799,7 +938,6 @@
     ]
     folded, total_1 = on_core(
         global_forward_body,
-        7,
         [((GROUP, fold, LANES), BF), ((tiles, 1, TILE), F32)],
         (got, beside, own_seg, shared_seg),
         head_scratch + [pltpu.VMEM((keys * 3 // 2, LANES), F32)],
@@ -807,26 +945,25 @@
     folded = exchange(folded, count)
 
     up_1 = out_grad.reshape(rows, width)
-    out_1, att_1, n2_1, mixed_1, d_gu_1, gain_mlp_1, d_mid_1, d_attn_1, sent = on_core(
+    out_1, att_1, n2_1, mixed_1, right_1, gain_mlp_1, d_mid_1, sent = on_core(
         global_middle_body,
-        4.2,
         [
             ((rows, width), BF),
             ((rows, width), BF),
             ((rows, width), BF),
             ((rows, hidden), BF),
-            ((rows, inner), BF),
+            ((rows, inner + width), BF),
             ((1, width), F32),
             ((rows, width), F32),
-            ((rows, width), BF),
             ((GROUP, fold, LANES), BF),
         ],
-        (folded, in_1, up_1, gain_mlp, second, w_out),
+        (*others, folded, in_1, up_1, gain_mlp),
+        weight_scratch(width, inner, hidden),
+        [pltpu.HBM] * len(others) + [pltpu.VMEM] * 4,
     )
     d_folded = exchange(sent, count)
     sent, to_beside = on_core(
         global_backward_body,
-        9,
         [((GROUP, 3 * fold, LANES), BF), ((GROUP, 2 * half, LANES), BF)],
         (got, beside, own_seg, shared_seg, total_1, d_folded),
         head_scratch
@@ -874,34 +1011,32 @@
     )
     d_proj_1, grad_1, gain_attn_1 = on_core(
         global_finish_body,
-        1.6,
         [((rows, 3 * width), BF), ((rows, width), BF), ((1, width), F32)],
-        (got, d_mid_1, in_1, gain_attn, first, global_tables),
+        (first, got, d_mid_1, in_1, gain_attn, global_tables),
+        qkv_scratch(width),
+        [pltpu.HBM] + [pltpu.VMEM] * 5,
     )
 
     up_0 = to_other_section(grad_1, -1)
     d_mlp = jnp.where(lower, up_0, up_1)
     across, beside = partner(d_mlp, 2, count), partner(d_mlp, 1, count)
     d_mlp = [d_mlp, beside, across, partner(across, 1, count)]
-    out_blocks = plane_product([(mixed, d_mlp)])
-    d_gu_0, gain_mlp_0, d_mid_0, d_attn_0, d_att_0 = on_core(
+    out_blocks = plane_product(d_mlp, [(mixed, 0, width)])
+    right, gain_mlp_0, d_mid_0, d_att_0 = on_core(
         local_back_middle_body,
-        2.9,
         [
-            ((rows, inner), BF),
+            ((rows, inner + width), BF),
             ((1, width), F32),
             ((rows, width), F32),
             ((rows, width), BF),
-            ((rows, width), BF),
         ],
-        (up_0, middle_0, gate_up_0, gain_mlp, second, w_out),
-    )
-    own = [jnp.where(lower, d_gu_0, d_gu_1), jnp.where(lower, d_attn_0, d_attn_1)]
-    beside = [partner(item, 1, count) for item in own]
-    across = [partner(item, 2, count) for item in own]
+        (*others, lower_flag, up_0, middle_0, gate_up_0, gain_mlp, right_1),
+        weight_scratch(width, inner, hidden),
+        [pltpu.HBM] * len(others) + [pltpu.SMEM] + [pltpu.VMEM] * 5,
+    )
+    beside, across = partner(right, 1, count), partner(right, 2, count)
     dq_0, d_own, d_before, d_after = on_core(
         local_backward_body,
-        4.2,
         [
             ((rows, width), BF),
             ((rows, 2 * width), F32),
@@ -914,36 +1049,37 @@
     from_before = lax.ppermute(d_after, "dp", up_pairs)
     from_after, out_blocks = lax.optimization_barrier((from_after, out_blocks))
     mlp_out_share = sum_planes(out_blocks, count)
-    (d_proj_0,) = on_core(
+    (d_proj,) = on_core(
         local_join_body,
-        0.5,
         [((rows, 3 * width), BF)],
-        (dq_0, d_own, from_after, from_before, local_tables),
-    )
-    d_proj = jnp.where(lower, d_proj_0, d_proj_1)
-    far = [partner(item, 1, count) for item in across]
-    d_gu, d_attn = zip(own, beside, across, far)
-    in_blocks = plane_product([(n2, d_gu), (att, d_attn)])
+        (lower_flag, dq_0, d_own, from_after, from_before, local_tables, d_proj_1),
+        (),
+        [pltpu.SMEM] + [pltpu.VMEM] * 6,
+    )
+    right = [right, beside, across, partner(across, 1, count)]
+    in_blocks = plane_product(right, [(n2, 0, inner), (att, inner, inner + width)])
     in_share = sum_planes(in_blocks, count)
-    across = partner(d_proj, 2, count)
-    across, in_blocks = lax.optimization_barrier((across, in_blocks))
-    d_proj = [d_proj, partner(d_proj, 1, count), across, partner(across, 1, count)]
-    qkv_blocks = plane_product([(n1, d_proj)])
-    qkv_share = sum_planes(qkv_blocks, count)
     grad_0, gain_attn_0 = on_core(
         input_backward_body,
-        1.5,
         [((rows, width), BF), ((1, width), F32)],
-        (d_mid_0, d_proj_0, in_0, gain_attn, first),
-    )
-
+        (first, d_mid_0, d_proj, in_0, gain_attn),
+        qkv_scratch(width),
+        [pltpu.HBM] + [pltpu.VMEM] * 4,
+    )
     gains = jnp.where(
         lower,
         jnp.concatenate([gain_attn_0, gain_mlp_0]),
         jnp.concatenate([gain_attn_1, gain_mlp_1]),
     )
+    gains = gains + partner(gains, 1, count)
+    gains = gains + partner(gains, 2, count)
+    across = partner(d_proj, 2, count)
+    across, in_blocks, gains = lax.optimization_barrier((across, in_blocks, gains))
+    d_proj = [d_proj, partner(d_proj, 1, count), across, partner(across, 1, count)]
+    qkv_blocks = plane_product(d_proj, [(n1, 0, 3 * width)])
+    qkv_share = sum_planes(qkv_blocks, count)
     gains, _ = lax.optimization_barrier((gains, qkv_blocks))
-    apart = 1
+    apart = 4
     while apart < count:
         gains = gains + partner(gains, apart, count)
         apart *= 2

time: 376 us -> 364 us (0.968)
  starting transfers between devices: 78.3 us -> 59.8 us
  Pallas kernels: 49.3 us -> 62.4 us
  local copies, waits for them, and re-layouts: 50.4 us -> 40.1 us
  blocking collectives: 45.5 us -> 53.2 us
    ppermute x51 -> x43, waiting for transfers between devices: 87.6 us -> 106 us  [partner(): return lax.ppermute(rows, 'dp', [(i, i ^ apart) for i in range(count)])]
    all_to_all x3 -> x0, waiting for transfers between devices: 18.4 us -> none  [sum_planes(): got = lax.all_to_all(blocks, 'dp', 0, 0, axis_index_groups=groups)]
    pallas_call x16, Pallas kernels: 49.3 us -> 62.4 us  [on_core(): pl.pallas_call(body, out_shape=[jax.ShapeDtypeStruct(shape, dtype) for sh...]
    all_to_all x3 -> x0, starting transfers between devices: 11.9 us -> none  [sum_planes(): got = lax.all_to_all(blocks, 'dp', 0, 0, axis_index_groups=groups)]
    ppermute x51 -> x43, starting transfers between devices: 50.1 us -> 42.3 us  [partner(): return lax.ppermute(rows, 'dp', [(i, i ^ apart) for i in range(count)])]
    all_to_all x3, blocking collectives: 45.5 us -> 53.2 us  [exchange(): return lax.all_to_all(blocks, 'dp', 0, 0, axis_index_groups=groups)]
    unnamed x152 -> x114, local copies, waits for them, and re-layouts: 31.7 us -> 25 us
    reduce_sum x3 -> x0, other arithmetic: 4.05 us -> none  [sum_planes(): total = jnp.sum(got.astype(F32), 0)]
  transfers between devices with their start and end apart: 62 -> 51, of which waited for: 23 -> 19; matrix products, arithmetic and copies ran while one was open for 8% -> 8% of each run, Pallas kernels for 7% -> 7%
where the time goes in v3:
time: 364 us; the launch traced here: 363 us
  waiting for transfers between devices  117 us (32%)
  Pallas kernels  62.4 us (17%)
  starting transfers between devices  59.8 us (16%)
  blocking collectives  53.2 us (15%)
  local copies, waits for them, and re-layouts  40.1 us (11%)
  between operations  15.2 us (4%)
  other arithmetic  14.9 us (4%)
    ppermute x43, waiting for transfers between devices, partner(): return lax.ppermute(rows, 'dp', [(i, i ^ apart) for i in range(count)])  106 us
    pallas_call x16, Pallas kernels, on_core(): pl.pallas_call(body, out_shape=[jax.ShapeDtypeStruct(shape, dtype) for sh...  62.4 us
    all_to_all x3, blocking collectives, exchange(): return lax.all_to_all(blocks, 'dp', 0, 0, axis_index_groups=groups)  53.2 us
    ppermute x43, starting transfers between devices, partner(): return lax.ppermute(rows, 'dp', [(i, i ^ apart) for i in range(count)])  42.3 us
    unnamed x114, local copies, waits for them, and re-layouts  25 us
    ppermute x2, waiting for transfers between devices, to_other_section(): return lax.ppermute(rows, 'section', [(0, 1)] if step > 0 else [(1, 0)])  8.07 us
  transfers between devices with their start and end apart: 51, of which 19 were waited for; matrix products, arithmetic and copies ran while one was open for 8% of the time, Pallas kernels for 7%

profile of v3, /device:TPU:0, one launch (start us, length us, event | category | flops | bytes accessed | tf_op | source)
XLA Modules:
  0.0 362.6 jit_solution(9509334678057965253)
XLA Ops:
  14.9 4.7 %collective-permute-start.12 = (bf16[48,2432]{1,0:T(8,128)(2,1)S(1)}, bf16[48,2432]{1,0:T(8,128)(2,1)S(1)}, u32[]{:S(2)}, u32[]{:S(2)}) collective-permute-start(bf16[48,2432]{1,0:T(8,128)(2,1)S(1)} %shard_map.152.refs_0_), channel_id=1, source_target_pairs={{0,12},{1,13},{2,14},{3,15},{4,8},{5,9},{6,10},{7,11},{8,4},{9,5},... | collective-permute-start | bytes 700424 | tf_op jit(solution)/shard_map/ppermute | solution.py:725
  22.9 3.3 collective-permute-done.12.refs_12_
  27.8 25.6 %collective-permute-done.8.refs_8_ = bf16[48,2432]{1,0:T(8,128)(2,1)S(1)} collective-permute-done((bf16[48,2432]{1,0:T(8,128)(2,1)S(1)}, bf16[48,2432]{1,0:T(8,128)(2,1)S(1)}, u32[]{:S(2)}, u32[]{:S(2)}) %collective-permute-start.8) | collective-permute-done | bytes 233504 | tf_op jit(solution)/shard_map/ppermute | solution.py:725
  56.5 7.2 %collective-permute-done.10.refs_10_ = bf16[48,2432]{1,0:T(8,128)(2,1)S(1)} collective-permute-done((bf16[48,2432]{1,0:T(8,128)(2,1)S(1)}, bf16[48,2432]{1,0:T(8,128)(2,1)S(1)}, u32[]{:S(2)}, u32[]{:S(2)}) %collective-permute-start.10) | collective-permute-done | bytes 233504 | tf_op jit(solution)/shard_map/ppermute | solution.py:725
  64.2 9.1 %collective-permute-done.6.refs_6_ = bf16[48,2432]{1,0:T(8,128)(2,1)S(1)} collective-permute-done((bf16[48,2432]{1,0:T(8,128)(2,1)S(1)}, bf16[48,2432]{1,0:T(8,128)(2,1)S(1)}, u32[]{:S(2)}, u32[]{:S(2)}) %collective-permute-start.6) | collective-permute-done | bytes 233504 | tf_op jit(solution)/shard_map/ppermute | solution.py:725
  78.1 6.1 %shard_map.153 = (bf16[768,2432]{1,0:T(8,128)(2,1)S(1)}, f32[8,768]{1,0:T(8,128)S(1)}, bf16[128,768]{1,0:T(8,128)(2,1)S(1)}, bf16[128,768]{1,0:T(8,128)(2,1)S(1)}, bf16[128,1536]{1,0:T(8,128)(2,1)S(1)}) custom-call(s32[1]{0:T(128)} %bitcast.8.place_ref, bf16[128,768]{1,0:T(8,128)(2,1)S(1)} %bitcast.113, f32[3,128,128]{2,1,0:T(8,128)S(1)} %tile.13.table_ref, ...), custom_call_target="tpu_custom_call" | custom-call | flops 1024 | bytes 1024 | tf_op jit(solution)/shard_map/pallas_call | solution.py:64
  84.3 1.8 copy-done.2
  88.1 3.1 collective-permute-start.16
  92.4 3.6 %shard_map.154 = (bf16[128,768]{1,0:T(8,128)(2,1)S(1)}, f32[12,1,128]{2,1,0:T(1,128)S(1)}) custom-call(bf16[128,768]{1,0:T(8,128)(2,1)S(1)} %get-tuple-element.69.q_ref, bf16[128,1536]{1,0:T(8,128)(2,1)S(1)} %collective-permute-done.16.before_ref, bf16[128,1536]{1,0:T(8,128)(2,1)S(1)} %get-tuple-element.70.own_ref, ...), custom_call_target="tpu_custom_call" | custom-call | flops 1024 | bytes 1024 | tf_op jit(solution)/shard_map/pallas_call | solution.py:64
  96.4 2.9 copy-done
  99.3 7.2 %shard_map.155 = (bf16[128,768]{1,0:T(8,128)(2,1)S(1)}, bf16[128,768]{1,0:T(8,128)(2,1)S(1)}, bf16[128,1152]{1,0:T(8,128)(2,1)S(1)}, f32[128,768]{1,0:T(8,128)S(1)}, f32[128,2304]{1,0:T(8,128)S(1)}) custom-call(bf16[4352,768]{1,0:T(8,128)(2,1)S(1)} %copy-done, bf16[128,768]{1,0:T(8,128)(2,1)S(1)} %bitcast.114, ...), custom_call_target="tpu_custom_call" | custom-call | flops 1024 | bytes 1024 | tf_op jit(solution)/shard_map/pallas_call | solution.py:64
  108.1 3.5 collective-permute-start.18
  112.1 2.7 collective-permute-done.18.x_ref.refs_2_
  114.8 2.1 copy-done.3
  116.9 1.9 shard_map.156
  118.9 29.8 %all_to_all.20.got_ref = bf16[16,144,128]{2,1,0:T(8,128)(2,1)S(1)} all-to-all(bf16[16,144,128]{2,1,0:T(8,128)(2,1)S(1)} %get-tuple-element.75), channel_id=1, replica_groups={{0,1,2,3,4,5,6,7,8,9,10,11,12,13,14,15},{16,17,18,19,20,21,22,23,24,25,..., dimensions={0} | all-to-all | bytes 1179648 | tf_op jit(solution)/shard_map/all_to_all | solution.py:717
  151.2 6.0 %shard_map.157 = (bf16[16,48,128]{2,1,0:T(8,128)(2,1)S(1)}, f32[6,1,256]{2,1,0:T(1,128)S(1)}) custom-call(bf16[16,144,128]{2,1,0:T(8,128)(2,1)S(1)} %all_to_all.20.got_ref, bf16[16,64,128]{2,1,0:T(8,128)(2,1)S(1)} %collective-permute-done.19.other_ref, s32[1024,1]{1,0:T(8,128)S(1)} %copy.35.own_seg_ref, s32[1024,1]{1,0:T(8,128)S(1)} %copy.36.shared_seg_ref), custom_call_target="tpu_custom_call" | custom-call | flops 1024 | bytes 1024 | tf_op jit(solution)/shard_map/pallas_call | solution.py:64
  157.3 11.8 %all_to_all.21.refs_1_ = bf16[16,48,128]{2,1,0:T(8,128)(2,1)S(1)} all-to-all(bf16[16,48,128]{2,1,0:T(8,128)(2,1)S(1)} %get-tuple-element.76), channel_id=1, replica_groups={{0,1,2,3,4,5,6,7,8,9,10,11,12,13,14,15},{16,17,18,19,20,21,22,23,24,25,..., dimensions={0} | all-to-all | bytes 393216 | tf_op jit(solution)/shard_map/all_to_all | solution.py:717
  169.1 2.9 copy-done.1
  172.0 9.9 %shard_map.158 = (bf16[128,768]{1,0:T(8,128)(2,1)S(1)}, bf16[128,768]{1,0:T(8,128)(2,1)S(1)}, bf16[128,768]{1,0:T(8,128)(2,1)S(1)}, bf16[128,1152]{1,0:T(8,128)(...) custom-call(bf16[4352,768]{1,0:T(8,128)(2,1)S(1)} %copy-done.1, ...), custom_call_target="tpu_custom_call" | custom-call | flops 1024 | bytes 1024 | tf_op jit(solution)/shard_map/pallas_call | solution.py:64
  181.9 11.6 %all_to_all.22.d_ref = bf16[16,48,128]{2,1,0:T(8,128)(2,1)S(1)} all-to-all(bf16[16,48,128]{2,1,0:T(8,128)(2,1)S(1)} %get-tuple-element.86), channel_id=1, replica_groups={{0,1,2,3,4,5,6,7,8,9,10,11,12,13,14,15},{16,17,18,19,20,21,22,23,24,25,..., dimensions={0} | all-to-all | bytes 393216 | tf_op jit(solution)/shard_map/all_to_all | solution.py:717
  193.5 8.0 %shard_map.159 = (bf16[16,144,128]{2,1,0:T(8,128)(2,1)S(1)}, bf16[16,64,128]{2,1,0:T(8,128)(2,1)}) custom-call(bf16[16,144,128]{2,1,0:T(8,128)(2,1)S(1)} %all_to_all.20.got_ref, bf16[16,64,128]{2,1,0:T(8,128)(2,1)S(1)} %collective-permute-done.19.other_ref, s32[1024,1]{1,0:T(8,128)S(1)} %copy.35.own_seg_ref, s32[1024,1]{1,0:T(8,128)S(1)} %copy.36.shared_seg_ref, ...), custom_call_target="tpu_custom_call" | custom-call | flops 1024 | bytes 1024 | tf_op jit(solution)/shard_map/pallas_call | solution.py:64
  204.5 3.8 %all-to-all-start.3 = ((bf16[16,144,128]{2,1,0:T(8,128)(2,1)}), bf16[16,144,128]{2,1,0:T(8,128)(2,1)S(1)}, u32[]{:S(2)}, u32[]{:S(2)}) async-start(bf16[16,144,128]{2,1,0:T(8,128)(2,1)} %add_convert_fusion), calls=%async_computation.3 | async-start | bytes 1179648 | tf_op jit(solution)/shard_map/all_to_all | solution.py:717
  208.4 1.9 select_bitcast_fusion
  210.2 1.8 copy.40
  217.0 1.7 copy.38
  218.8 2.3 pad_maximum_fusion
  221.8 1.8 all-to-all-done.3.got_ref
  225.1 2.2 copy-done.4
  230.2 2.5 shard_map.160
  236.3 5.4 %collective-permute-done.21.refs_2_ = bf16[128,768]{1,0:T(8,128)(2,1)S(1)} collective-permute-done((bf16[128,768]{1,0:T(8,128)(2,1)S(1)}, bf16[128,768]{1,0:T(8,128)(2,1)S(1)}, u32[]{:S(2)}, u32[]{:S(2)}) %collective-permute-start.21) | collective-permute-done | bytes 196640 | tf_op jit(solution)/shard_map/ppermute | solution.py:721
  241.8 8.8 %shard_map.161 = (bf16[128,3072]{1,0:T(8,128)(2,1)S(1)}, f32[1,768]{1,0:T(1,128)S(1)}, f32[128,768]{1,0:T(8,128)S(1)}, bf16[128,768]{1,0:T(8,128)(2,1)S(1)}) custom-call(bf16[4352,768]{1,0:T(8,128)(2,1)S(1)} %bitcast.112, s32[1]{0:T(128)} %bitcast.23.refs_1_.lower_ref, bf16[128,768]{1,0:T(8,128)(2,1)S(1)} %collective-permute-done.21.refs_2_, ...), custom_call_target="tpu_custom_call" | custom-call | flops 1024 | bytes 1024 | tf_op jit(solution)/shard_map/pallas_call | solution.py:64
  252.8 3.5 shard_map.162
  257.8 3.1 collective-permute-start.29
  260.9 17.4 %collective-permute-done.24.refs_2_ = bf16[128,768]{1,0:T(8,128)(2,1)S(1)} collective-permute-done((bf16[128,768]{1,0:T(8,128)(2,1)S(1)}, bf16[128,768]{1,0:T(8,128)(2,1)S(1)}, u32[]{:S(2)}, u32[]{:S(2)}) %collective-permute-start.24) | collective-permute-done | bytes 196640 | tf_op jit(solution)/shard_map/ppermute | solution.py:725
  278.8 2.0 collective-permute-done.25.refs_3_
  282.9 2.0 shard_map.165
  285.6 2.5 collective-permute-start.31
  288.2 1.7 collective-permute-start.44
  291.7 3.0 collective-permute-start.46
  295.5 6.4 %collective-permute-done.36 = f32[2,768]{1,0:T(2,128)S(1)} collective-permute-done((f32[2,768]{1,0:T(2,128)S(1)}, f32[2,768]{1,0:T(2,128)S(1)}, u32[]{:S(2)}, u32[]{:S(2)}) %collective-permute-start.36) | collective-permute-done | bytes 6176 | tf_op jit(solution)/shard_map/ppermute | solution.py:725
  303.9 2.5 collective-permute-start.43
  307.7 7.3 %collective-permute-done.41 = bf16[48,3072]{1,0:T(8,128)(2,1)S(1)} collective-permute-done((bf16[48,3072]{1,0:T(8,128)(2,1)S(1)}, bf16[48,3072]{1,0:T(8,128)(2,1)S(1)}, u32[]{:S(2)}, u32[]{:S(2)}) %collective-permute-start.41) | collective-permute-done | bytes 294944 | tf_op jit(solution)/shard_map/ppermute | solution.py:725
  315.0 12.1 %collective-permute-done.42 = bf16[48,3072]{1,0:T(8,128)(2,1)S(1)} collective-permute-done((bf16[48,3072]{1,0:T(8,128)(2,1)S(1)}, bf16[48,3072]{1,0:T(8,128)(2,1)S(1)}, u32[]{:S(2)}, u32[]{:S(2)}) %collective-permute-start.42) | collective-permute-done | bytes 294944 | tf_op jit(solution)/shard_map/ppermute | solution.py:725
  328.0 5.3 %collective-permute-start.47 = (f32[2,768]{1,0:T(2,128)S(1)}, f32[2,768]{1,0:T(2,128)S(1)}, u32[]{:S(2)}, u32[]{:S(2)}) collective-permute-start(f32[2,768]{1,0:T(2,128)S(1)} %fusion.16), channel_id=1, source_target_pairs={{0,4},{1,5},{2,6},{3,7},{4,0},{5,1},{6,2},{7,3},{8,12},{9,13},{10,... | collective-permute-start | bytes 18440 | tf_op jit(solution)/shard_map/ppermute | solution.py:725
  337.6 2.9 collective-permute-start.39
  342.0 3.2 collective-permute-done.38
  345.2 9.7 %collective-permute-done.39 = bf16[48,2304]{1,0:T(8,128)(2,1)S(1)} collective-permute-done((bf16[48,2304]{1,0:T(8,128)(2,1)S(1)}, bf16[48,2304]{1,0:T(8,128)(2,1)S(1)}, u32[]{:S(2)}, u32[]{:S(2)}) %collective-permute-start.39) | collective-permute-done | bytes 221216 | tf_op jit(solution)/shard_map/ppermute | solution.py:725
  (271 shorter events, 65.1 us)
Async XLA Ops:
  7.2 89.2 %all-gather.2.cloned.1.call-start = ((), (), s32[]{:S(2)}) async-start(), calls=%async_computation.4 | async-start | bytes 7102464 | tf_op jit(solution)/shard_map/all_gather | solution.py:834
  8.0 4.9 %collective-permute-start = (bf16[8,768]{1,0:T(8,128)(2,1)S(1)}, bf16[8,768]{1,0:T(8,128)(2,1)S(1)}, u32[]{:S(2)}, u32[]{:S(2)}) collective-permute-start(bf16[8,768]{1,0:T(8,128)(2,1)S(1)} %slice_bitcast_fusion.3), channel_id=1, source_target_pairs={{0,1},{1,0},{2,3},{3,2},{4,5},{5,4},{6,7},{7,6},{8,9},{9,8},{10,11... | collective-permute-start | bytes 36872 | tf_op jit(solution)/shard_map/ppermute | solution.py:725
  14.9 11.4 %collective-permute-start.12 = (bf16[48,2432]{1,0:T(8,128)(2,1)S(1)}, bf16[48,2432]{1,0:T(8,128)(2,1)S(1)}, u32[]{:S(2)}, u32[]{:S(2)}) collective-permute-start(bf16[48,2432]{1,0:T(8,128)(2,1)S(1)} %shard_map.152.refs_0_), channel_id=1, source_target_pairs={{0,12},{1,13},{2,14},{3,15},{4,8},{5,9},{6,10},{7,11},{8,4},{9,5},... | collective-permute-start | bytes 700424 | tf_op jit(solution)/shard_map/ppermute | solution.py:725
  19.5 34.0 %collective-permute-start.8 = (bf16[48,2432]{1,0:T(8,128)(2,1)S(1)}, bf16[48,2432]{1,0:T(8,128)(2,1)S(1)}, u32[]{:S(2)}, u32[]{:S(2)}) collective-permute-start(bf16[48,2432]{1,0:T(8,128)(2,1)S(1)} %shard_map.152.refs_0_), channel_id=1, source_target_pairs={{0,8},{1,9},{2,10},{3,11},{4,12},{5,13},{6,14},{7,15},{8,0},{9,1},... | collective-permute-start | bytes 700424 | tf_op jit(solution)/shard_map/ppermute | solution.py:725
  19.5 34.0 %collective-permute-start.4 = (bf16[48,2432]{1,0:T(8,128)(2,1)S(1)}, bf16[48,2432]{1,0:T(8,128)(2,1)S(1)}, u32[]{:S(2)}, u32[]{:S(2)}) collective-permute-start(bf16[48,2432]{1,0:T(8,128)(2,1)S(1)} %shard_map.152.refs_0_), channel_id=1, source_target_pairs={{0,4},{1,5},{2,6},{3,7},{4,0},{5,1},{6,2},{7,3},{8,12},{9,13},{10,... | collective-permute-start | bytes 700424 | tf_op jit(solution)/shard_map/ppermute | solution.py:725
  20.2 34.8 %collective-permute-start.2 = (bf16[48,2432]{1,0:T(8,128)(2,1)S(1)}, bf16[48,2432]{1,0:T(8,128)(2,1)S(1)}, u32[]{:S(2)}, u32[]{:S(2)}) collective-permute-start(bf16[48,2432]{1,0:T(8,128)(2,1)S(1)} %shard_map.152.refs_0_), channel_id=1, source_target_pairs={{0,2},{1,3},{2,0},{3,1},{4,6},{5,7},{6,4},{7,5},{8,10},{9,11},{10,... | collective-permute-start | bytes 700424 | tf_op jit(solution)/shard_map/ppermute | solution.py:725
  21.8 33.4 %collective-permute-start.1 = (bf16[48,2432]{1,0:T(8,128)(2,1)S(1)}, bf16[48,2432]{1,0:T(8,128)(2,1)S(1)}, u32[]{:S(2)}, u32[]{:S(2)}) collective-permute-start(bf16[48,2432]{1,0:T(8,128)(2,1)S(1)} %shard_map.152.refs_0_), channel_id=1, source_target_pairs={{0,1},{1,0},{2,3},{3,2},{4,5},{5,4},{6,7},{7,6},{8,9},{9,8},{10,11... | collective-permute-start | bytes 700424 | tf_op jit(solution)/shard_map/ppermute | solution.py:725
  26.2 29.7 %collective-permute-start.14 = (bf16[48,2432]{1,0:T(8,128)(2,1)S(1)}, bf16[48,2432]{1,0:T(8,128)(2,1)S(1)}, u32[]{:S(2)}, u32[]{:S(2)}) collective-permute-start(bf16[48,2432]{1,0:T(8,128)(2,1)S(1)} %collective-permute-done.12.refs_12_), channel_id=1, source_target_pairs={{0,2},{1,3},{2,0},{3,1},{4,6},{5,7},{6,4},{7,5},{8,10},{9,11},{10,... | collective-permute-start | bytes 700424 | tf_op jit(solution)/shard_map/ppermute | solution.py:725
  53.5 10.2 %collective-permute-start.10 = (bf16[48,2432]{1,0:T(8,128)(2,1)S(1)}, bf16[48,2432]{1,0:T(8,128)(2,1)S(1)}, u32[]{:S(2)}, u32[]{:S(2)}) collective-permute-start(bf16[48,2432]{1,0:T(8,128)(2,1)S(1)} %collective-permute-done.8.refs_8_), channel_id=1, source_target_pairs={{0,2},{1,3},{2,0},{3,1},{4,6},{5,7},{6,4},{7,5},{8,10},{9,11},{10,... | collective-permute-start | bytes 700424 | tf_op jit(solution)/shard_map/ppermute | solution.py:725
  55.0 8.7 %collective-permute-start.9 = (bf16[48,2432]{1,0:T(8,128)(2,1)S(1)}, bf16[48,2432]{1,0:T(8,128)(2,1)S(1)}, u32[]{:S(2)}, u32[]{:S(2)}) collective-permute-start(bf16[48,2432]{1,0:T(8,128)(2,1)S(1)} %collective-permute-done.8.refs_8_), channel_id=1, source_target_pairs={{0,1},{1,0},{2,3},{3,2},{4,5},{5,4},{6,7},{7,6},{8,9},{9,8},{10,11... | collective-permute-start | bytes 700424 | tf_op jit(solution)/shard_map/ppermute | solution.py:725
  55.2 18.1 %collective-permute-start.6 = (bf16[48,2432]{1,0:T(8,128)(2,1)S(1)}, bf16[48,2432]{1,0:T(8,128)(2,1)S(1)}, u32[]{:S(2)}, u32[]{:S(2)}) collective-permute-start(bf16[48,2432]{1,0:T(8,128)(2,1)S(1)} %collective-permute-done.4.refs_4_), channel_id=1, source_target_pairs={{0,2},{1,3},{2,0},{3,1},{4,6},{5,7},{6,4},{7,5},{8,10},{9,11},{10,... | collective-permute-start | bytes 700424 | tf_op jit(solution)/shard_map/ppermute | solution.py:725
  55.9 19.6 %collective-permute-start.5 = (bf16[48,2432]{1,0:T(8,128)(2,1)S(1)}, bf16[48,2432]{1,0:T(8,128)(2,1)S(1)}, u32[]{:S(2)}, u32[]{:S(2)}) collective-permute-start(bf16[48,2432]{1,0:T(8,128)(2,1)S(1)} %collective-permute-done.4.refs_4_), channel_id=1, source_target_pairs={{0,1},{1,0},{2,3},{3,2},{4,5},{5,4},{6,7},{7,6},{8,9},{9,8},{10,11... | collective-permute-start | bytes 700424 | tf_op jit(solution)/shard_map/ppermute | solution.py:725
  56.0 20.2 %collective-permute-start.3 = (bf16[48,2432]{1,0:T(8,128)(2,1)S(1)}, bf16[48,2432]{1,0:T(8,128)(2,1)}, u32[]{:S(2)}, u32[]{:S(2)}) collective-permute-start(bf16[48,2432]{1,0:T(8,128)(2,1)S(1)} %collective-permute-done.2.refs_2_), channel_id=1, source_target_pairs={{0,1},{1,0},{2,3},{3,2},{4,5},{5,4},{6,7},{7,6},{8,9},{9,8},{10,11... | collective-permute-start | bytes 700424 | tf_op jit(solution)/shard_map/ppermute | solution.py:725
  63.7 12.5 %collective-permute-start.15 = (bf16[48,2432]{1,0:T(8,128)(2,1)S(1)}, bf16[48,2432]{1,0:T(8,128)(2,1)}, u32[]{:S(2)}, u32[]{:S(2)}) collective-permute-start(bf16[48,2432]{1,0:T(8,128)(2,1)S(1)} %collective-permute-done.14.refs_14_), channel_id=1, source_target_pairs={{0,1},{1,0},{2,3},{3,2},{4,5},{5,4},{6,7},{7,6},{8,9},{9,8},{10,11... | collective-permute-start | bytes 700424 | tf_op jit(solution)/shard_map/ppermute | solution.py:725
  63.7 12.5 %collective-permute-start.11 = (bf16[48,2432]{1,0:T(8,128)(2,1)S(1)}, bf16[48,2432]{1,0:T(8,128)(2,1)}, u32[]{:S(2)}, u32[]{:S(2)}) collective-permute-start(bf16[48,2432]{1,0:T(8,128)(2,1)S(1)} %collective-permute-done.10.refs_10_), channel_id=1, source_target_pairs={{0,1},{1,0},{2,3},{3,2},{4,5},{5,4},{6,7},{7,6},{8,9},{9,8},{10,11... | collective-permute-start | bytes 700424 | tf_op jit(solution)/shard_map/ppermute | solution.py:725
  73.3 2.9 collective-permute-start.7
  86.8 5.0 %collective-permute-start.17 = (bf16[128,1536]{1,0:T(8,128)(2,1)S(1)}, bf16[128,1536]{1,0:T(8,128)(2,1)S(1)}, u32[]{:S(2)}, u32[]{:S(2)}) collective-permute-start(bf16[128,1536]{1,0:T(8,128)(2,1)S(1)} %get-tuple-element.70.own_ref), channel_id=1, source_target_pairs={{1,0},{2,1},{3,2},{4,3},{5,4},{6,5},{7,6},{8,7},{9,8},{10,9},{11,1... | collective-permute-start | bytes 1179656 | tf_op jit(solution)/shard_map/ppermute | solution.py:895
  88.1 4.4 %collective-permute-start.16 = (bf16[128,1536]{1,0:T(8,128)(2,1)S(1)}, bf16[128,1536]{1,0:T(8,128)(2,1)S(1)}, u32[]{:S(2)}, u32[]{:S(2)}) collective-permute-start(bf16[128,1536]{1,0:T(8,128)(2,1)S(1)} %get-tuple-element.70.own_ref), channel_id=1, source_target_pairs={{0,1},{1,2},{2,3},{3,4},{4,5},{5,6},{6,7},{7,8},{8,9},{9,10},{10,1... | collective-permute-start | bytes 1179656 | tf_op jit(solution)/shard_map/ppermute | solution.py:893
  108.1 6.7 %collective-permute-start.18 = (bf16[128,768]{1,0:T(8,128)(2,1)S(1)}, bf16[128,768]{1,0:T(8,128)(2,1)S(1)}, u32[]{:S(2)}, u32[]{:S(2)}) collective-permute-start(bf16[128,768]{1,0:T(8,128)(2,1)S(1)} %get-tuple-element.73), channel_id=1, source_target_pairs={{0,16},{1,17},{2,18},{3,19},{4,20},{5,21},{6,22},{7,23},{8,24},{9,... | collective-permute-start | bytes 589832 | tf_op jit(solution)/shard_map/ppermute | solution.py:721
  204.5 19.1 %all-to-all-start.3 = ((bf16[16,144,128]{2,1,0:T(8,128)(2,1)}), bf16[16,144,128]{2,1,0:T(8,128)(2,1)S(1)}, u32[]{:S(2)}, u32[]{:S(2)}) async-start(bf16[16,144,128]{2,1,0:T(8,128)(2,1)} %add_convert_fusion), calls=%async_computation.3 | async-start | bytes 1179648 | tf_op jit(solution)/shard_map/all_to_all | solution.py:717
  232.7 9.0 %collective-permute-start.21 = (bf16[128,768]{1,0:T(8,128)(2,1)S(1)}, bf16[128,768]{1,0:T(8,128)(2,1)S(1)}, u32[]{:S(2)}, u32[]{:S(2)}) collective-permute-start(bf16[128,768]{1,0:T(8,128)(2,1)S(1)} %get-tuple-element.91), channel_id=1, source_target_pairs={{16,0},{17,1},{18,2},{19,3},{20,4},{21,5},{22,6},{23,7},{24,8},{25... | collective-permute-start | bytes 589832 | tf_op jit(solution)/shard_map/ppermute | solution.py:721
  234.2 22.2 %collective-permute-start.26 = (bf16[4,1,216,128]{3,2,0,1:T(8,128)(2,1)S(1)}, bf16[4,1,216,128]{3,2,0,1:T(8,128)(2,1)S(1)}, u32[]{:S(2)}, u32[]{:S(2)}) collective-permute-start(bf16[4,1,216,128]{3,2,0,1:T(8,128)(2,1)S(1)} %pad_maximum_fusion.3), channel_id=1, source_target_pairs={{0,1},{1,0},{2,3},{3,2},{4,5},{5,4},{6,7},{7,6},{8,9},{9,8},{10,11... | collective-permute-start | bytes 663560 | tf_op jit(solution)/shard_map/ppermute | solution.py:725
  234.3 22.1 %collective-permute-start.27 = (bf16[4,1,216,128]{3,2,0,1:T(8,128)(2,1)S(1)}, bf16[4,1,216,128]{3,2,0,1:T(8,128)(2,1)S(1)}, u32[]{:S(2)}, u32[]{:S(2)}) collective-permute-start(bf16[4,1,216,128]{3,2,0,1:T(8,128)(2,1)S(1)} %pad_maximum_fusion.4), channel_id=1, source_target_pairs={{0,2},{1,3},{2,0},{3,1},{4,6},{5,7},{6,4},{7,5},{8,10},{9,11},{10,... | collective-permute-start | bytes 663560 | tf_op jit(solution)/shard_map/ppermute | solution.py:725
  235.7 22.1 %collective-permute-start.28 = (bf16[4,1,216,128]{3,2,0,1:T(8,128)(2,1)S(1)}, bf16[4,1,216,128]{3,2,0,1:T(8,128)(2,1)S(1)}, u32[]{:S(2)}, u32[]{:S(2)}) collective-permute-start(bf16[4,1,216,128]{3,2,0,1:T(8,128)(2,1)S(1)} %pad_maximum_fusion.5), channel_id=1, source_target_pairs={{0,3},{1,2},{2,1},{3,0},{4,7},{5,6},{6,5},{7,4},{8,11},{9,10},{10,... | collective-permute-start | bytes 663560 | tf_op jit(solution)/shard_map/ppermute | solution.py:725
  250.6 34.4 %collective-permute-start.33 = (bf16[128,3072]{1,0:T(8,128)(2,1)S(1)}, bf16[128,3072]{1,0:T(8,128)(2,1)S(1)}, u32[]{:S(2)}, u32[]{:S(2)}) collective-permute-start(bf16[128,3072]{1,0:T(8,128)(2,1)S(1)} %get-tuple-element.110.refs_0_), channel_id=1, source_target_pairs={{0,2},{1,3},{2,0},{3,1},{4,6},{5,7},{6,4},{7,5},{8,10},{9,11},{10,... | collective-permute-start | bytes 2359304 | tf_op jit(solution)/shard_map/ppermute | solution.py:725
  252.0 26.3 %collective-permute-start.24 = (bf16[128,768]{1,0:T(8,128)(2,1)S(1)}, bf16[128,768]{1,0:T(8,128)(2,1)S(1)}, u32[]{:S(2)}, u32[]{:S(2)}) collective-permute-start(bf16[128,768]{1,0:T(8,128)(2,1)S(1)} %broadcast_select_fusion.1.refs_0_), channel_id=1, source_target_pairs={{0,2},{1,3},{2,0},{3,1},{4,6},{5,7},{6,4},{7,5},{8,10},{9,11},{10,... | collective-permute-start | bytes 589832 | tf_op jit(solution)/shard_map/ppermute | solution.py:725
  256.4 21.9 %collective-permute-start.23 = (bf16[128,768]{1,0:T(8,128)(2,1)S(1)}, bf16[128,768]{1,0:T(8,128)(2,1)S(1)}, u32[]{:S(2)}, u32[]{:S(2)}) collective-permute-start(bf16[128,768]{1,0:T(8,128)(2,1)S(1)} %broadcast_select_fusion.1.refs_0_), channel_id=1, source_target_pairs={{0,1},{1,0},{2,3},{3,2},{4,5},{5,4},{6,7},{7,6},{8,9},{9,8},{10,11... | collective-permute-start | bytes 589832 | tf_op jit(solution)/shard_map/ppermute | solution.py:725
  256.5 24.8 %collective-permute-start.22 = (bf16[128,1536]{1,0:T(8,128)(2,1)S(1)}, bf16[128,1536]{1,0:T(8,128)(2,1)S(1)}, u32[]{:S(2)}, u32[]{:S(2)}) collective-permute-start(bf16[128,1536]{1,0:T(8,128)(2,1)S(1)} %get-tuple-element.100), channel_id=1, source_target_pairs={{1,0},{2,1},{3,2},{4,3},{5,4},{6,5},{7,6},{8,7},{9,8},{10,9},{11,1... | collective-permute-start | bytes 1179656 | tf_op jit(solution)/shard_map/ppermute | solution.py:1048
  257.8 23.5 %collective-permute-start.29 = (bf16[128,1536]{1,0:T(8,128)(2,1)S(1)}, bf16[128,1536]{1,0:T(8,128)(2,1)S(1)}, u32[]{:S(2)}, u32[]{:S(2)}) collective-permute-start(bf16[128,1536]{1,0:T(8,128)(2,1)S(1)} %get-tuple-element.107), channel_id=1, source_target_pairs={{0,1},{1,2},{2,3},{3,4},{4,5},{5,6},{6,7},{7,8},{8,9},{9,10},{10,1... | collective-permute-start | bytes 1179656 | tf_op jit(solution)/shard_map/ppermute | solution.py:1049
  278.3 11.7 %collective-permute-start.32 = (bf16[128,3072]{1,0:T(8,128)(2,1)S(1)}, bf16[128,3072]{1,0:T(8,128)(2,1)S(1)}, u32[]{:S(2)}, u32[]{:S(2)}) collective-permute-start(bf16[128,3072]{1,0:T(8,128)(2,1)S(1)} %get-tuple-element.110.refs_0_), channel_id=1, source_target_pairs={{0,1},{1,0},{2,3},{3,2},{4,5},{5,4},{6,7},{7,6},{8,9},{9,8},{10,11... | collective-permute-start | bytes 2359304 | tf_op jit(solution)/shard_map/ppermute | solution.py:725
  278.3 2.6 collective-permute-start.25
  285.0 6.7 %collective-permute-start.34 = (bf16[128,3072]{1,0:T(8,128)(2,1)S(1)}, bf16[128,3072]{1,0:T(8,128)(2,1)S(1)}, u32[]{:S(2)}, u32[]{:S(2)}) collective-permute-start(bf16[128,3072]{1,0:T(8,128)(2,1)S(1)} %collective-permute-done.33.refs_2_), channel_id=1, source_target_pairs={{0,1},{1,0},{2,3},{3,2},{4,5},{5,4},{6,7},{7,6},{8,9},{9,8},{10,11... | collective-permute-start | bytes 2359304 | tf_op jit(solution)/shard_map/ppermute | solution.py:725
  285.2 4.7 %collective-permute-start.35 = (f32[2,768]{1,0:T(2,128)S(1)}, f32[2,768]{1,0:T(2,128)S(1)}, u32[]{:S(2)}, u32[]{:S(2)}) collective-permute-start(f32[2,768]{1,0:T(2,128)S(1)} %maximum_select_fusion), channel_id=1, source_target_pairs={{0,1},{1,0},{2,3},{3,2},{4,5},{5,4},{6,7},{7,6},{8,9},{9,8},{10,11... | collective-permute-start | bytes 18440 | tf_op jit(solution)/shard_map/ppermute | solution.py:725
  285.6 21.6 %collective-permute-start.31 = (bf16[128,2304]{1,0:T(8,128)(2,1)S(1)}, bf16[128,2304]{1,0:T(8,128)(2,1)S(1)}, u32[]{:S(2)}, u32[]{:S(2)}) collective-permute-start(bf16[128,2304]{1,0:T(8,128)(2,1)S(1)} %shard_map.164.d_proj_ref.refs_0_), channel_id=1, source_target_pairs={{0,2},{1,3},{2,0},{3,1},{4,6},{5,7},{6,4},{7,5},{8,10},{9,11},{10,... | collective-permute-start | bytes 1769480 | tf_op jit(solution)/shard_map/ppermute | solution.py:725
  288.2 15.5 %collective-permute-start.44 = (bf16[72,768]{1,0:T(8,128)(2,1)S(1)}, bf16[72,768]{1,0:T(8,128)(2,1)S(1)}, u32[]{:S(2)}, u32[]{:S(2)}) collective-permute-start(bf16[72,768]{1,0:T(8,128)(2,1)S(1)} %get-tuple-element.125), channel_id=1, source_target_pairs={{0,4},{1,5},{2,6},{3,7},{4,0},{5,1},{6,2},{7,3},{8,12},{9,13},{10,... | collective-permute-start | bytes 331784 | tf_op jit(solution)/shard_map/ppermute | solution.py:725
  289.9 13.9 %collective-permute-start.45 = (bf16[72,768]{1,0:T(8,128)(2,1)S(1)}, bf16[72,768]{1,0:T(8,128)(2,1)S(1)}, u32[]{:S(2)}, u32[]{:S(2)}) collective-permute-start(bf16[72,768]{1,0:T(8,128)(2,1)S(1)} %get-tuple-element.126), channel_id=1, source_target_pairs={{0,8},{1,9},{2,10},{3,11},{4,12},{5,13},{6,14},{7,15},{8,0},{9,1},... | collective-permute-start | bytes 331784 | tf_op jit(solution)/shard_map/ppermute | solution.py:725
  290.0 12.0 %collective-permute-start.36 = (f32[2,768]{1,0:T(2,128)S(1)}, f32[2,768]{1,0:T(2,128)S(1)}, u32[]{:S(2)}, u32[]{:S(2)}) collective-permute-start(f32[2,768]{1,0:T(2,128)S(1)} %fusion.15), channel_id=1, source_target_pairs={{0,2},{1,3},{2,0},{3,1},{4,6},{5,7},{6,4},{7,5},{8,10},{9,11},{10,... | collective-permute-start | bytes 18440 | tf_op jit(solution)/shard_map/ppermute | solution.py:725
  291.7 14.7 %collective-permute-start.46 = (bf16[72,768]{1,0:T(8,128)(2,1)S(1)}, bf16[72,768]{1,0:T(8,128)(2,1)S(1)}, u32[]{:S(2)}, u32[]{:S(2)}) collective-permute-start(bf16[72,768]{1,0:T(8,128)(2,1)S(1)} %get-tuple-element.127), channel_id=1, source_target_pairs={{0,12},{1,13},{2,14},{3,15},{4,8},{5,9},{6,10},{7,11},{8,4},{9,5},... | collective-permute-start | bytes 331784 | tf_op jit(solution)/shard_map/ppermute | solution.py:725
  302.0 13.1 %collective-permute-start.41 = (bf16[48,3072]{1,0:T(8,128)(2,1)S(1)}, bf16[48,3072]{1,0:T(8,128)(2,1)S(1)}, u32[]{:S(2)}, u32[]{:S(2)}) collective-permute-start(bf16[48,3072]{1,0:T(8,128)(2,1)S(1)} %get-tuple-element.112), channel_id=1, source_target_pairs={{0,4},{1,5},{2,6},{3,7},{4,0},{5,1},{6,2},{7,3},{8,12},{9,13},{10,... | collective-permute-start | bytes 884744 | tf_op jit(solution)/shard_map/ppermute | solution.py:725
  303.7 23.5 %collective-permute-start.42 = (bf16[48,3072]{1,0:T(8,128)(2,1)S(1)}, bf16[48,3072]{1,0:T(8,128)(2,1)S(1)}, u32[]{:S(2)}, u32[]{:S(2)}) collective-permute-start(bf16[48,3072]{1,0:T(8,128)(2,1)S(1)} %get-tuple-element.113), channel_id=1, source_target_pairs={{0,8},{1,9},{2,10},{3,11},{4,12},{5,13},{6,14},{7,15},{8,0},{9,1},... | collective-permute-start | bytes 884744 | tf_op jit(solution)/shard_map/ppermute | solution.py:725
  303.9 23.3 %collective-permute-start.43 = (bf16[48,3072]{1,0:T(8,128)(2,1)S(1)}, bf16[48,3072]{1,0:T(8,128)(2,1)S(1)}, u32[]{:S(2)}, u32[]{:S(2)}) collective-permute-start(bf16[48,3072]{1,0:T(8,128)(2,1)S(1)} %get-tuple-element.114), channel_id=1, source_target_pairs={{0,12},{1,13},{2,14},{3,15},{4,8},{5,9},{6,10},{7,11},{8,4},{9,5},... | collective-permute-start | bytes 884744 | tf_op jit(solution)/shard_map/ppermute | solution.py:725
  306.4 20.9 %collective-permute-start.30 = (bf16[128,2304]{1,0:T(8,128)(2,1)S(1)}, bf16[128,2304]{1,0:T(8,128)(2,1)S(1)}, u32[]{:S(2)}, u32[]{:S(2)}) collective-permute-start(bf16[128,2304]{1,0:T(8,128)(2,1)S(1)} %shard_map.164.d_proj_ref.refs_0_), channel_id=1, source_target_pairs={{0,1},{1,0},{2,3},{3,2},{4,5},{5,4},{6,7},{7,6},{8,9},{9,8},{10,11... | collective-permute-start | bytes 1769480 | tf_op jit(solution)/shard_map/ppermute | solution.py:725
  307.2 20.1 %collective-permute-start.37 = (bf16[128,2304]{1,0:T(8,128)(2,1)S(1)}, bf16[128,2304]{1,0:T(8,128)(2,1)S(1)}, u32[]{:S(2)}, u32[]{:S(2)}) collective-permute-start(bf16[128,2304]{1,0:T(8,128)(2,1)S(1)} %collective-permute-done.31.refs_2_), channel_id=1, source_target_pairs={{0,1},{1,0},{2,3},{3,2},{4,5},{5,4},{6,7},{7,6},{8,9},{9,8},{10,11... | collective-permute-start | bytes 1769480 | tf_op jit(solution)/shard_map/ppermute | solution.py:725
  328.0 6.9 %collective-permute-start.47 = (f32[2,768]{1,0:T(2,128)S(1)}, f32[2,768]{1,0:T(2,128)S(1)}, u32[]{:S(2)}, u32[]{:S(2)}) collective-permute-start(f32[2,768]{1,0:T(2,128)S(1)} %fusion.16), channel_id=1, source_target_pairs={{0,4},{1,5},{2,6},{3,7},{4,0},{5,1},{6,2},{7,3},{8,12},{9,13},{10,... | collective-permute-start | bytes 18440 | tf_op jit(solution)/shard_map/ppermute | solution.py:725
  334.9 6.4 %collective-permute-start.48 = (f32[2,768]{1,0:T(2,128)S(1)}, f32[2,768]{1,0:T(2,128)S(1)}, u32[]{:S(2)}, u32[]{:S(2)}) collective-permute-start(f32[2,768]{1,0:T(2,128)S(1)} %add.263), channel_id=1, source_target_pairs={{0,8},{1,9},{2,10},{3,11},{4,12},{5,13},{6,14},{7,15},{8,0},{9,1},... | collective-permute-start | bytes 18440 | tf_op jit(solution)/shard_map/ppermute | solution.py:725
  337.0 8.2 %collective-permute-start.38 = (bf16[48,2304]{1,0:T(8,128)(2,1)S(1)}, bf16[48,2304]{1,0:T(8,128)(2,1)S(1)}, u32[]{:S(2)}, u32[]{:S(2)}) collective-permute-start(bf16[48,2304]{1,0:T(8,128)(2,1)S(1)} %get-tuple-element.121), channel_id=1, source_target_pairs={{0,4},{1,5},{2,6},{3,7},{4,0},{5,1},{6,2},{7,3},{8,12},{9,13},{10,... | collective-permute-start | bytes 663560 | tf_op jit(solution)/shard_map/ppermute | solution.py:725
  337.6 17.3 %collective-permute-start.39 = (bf16[48,2304]{1,0:T(8,128)(2,1)S(1)}, bf16[48,2304]{1,0:T(8,128)(2,1)S(1)}, u32[]{:S(2)}, u32[]{:S(2)}) collective-permute-start(bf16[48,2304]{1,0:T(8,128)(2,1)S(1)} %get-tuple-element.122), channel_id=1, source_target_pairs={{0,8},{1,9},{2,10},{3,11},{4,12},{5,13},{6,14},{7,15},{8,0},{9,1},... | collective-permute-start | bytes 663560 | tf_op jit(solution)/shard_map/ppermute | solution.py:725
  340.5 14.3 %collective-permute-start.40 = (bf16[48,2304]{1,0:T(8,128)(2,1)S(1)}, bf16[48,2304]{1,0:T(8,128)(2,1)S(1)}, u32[]{:S(2)}, u32[]{:S(2)}) collective-permute-start(bf16[48,2304]{1,0:T(8,128)(2,1)S(1)} %get-tuple-element.123), channel_id=1, source_target_pairs={{0,12},{1,13},{2,14},{3,15},{4,8},{5,9},{6,10},{7,11},{8,4},{9,5},... | collective-permute-start | bytes 663560 | tf_op jit(solution)/shard_map/ppermute | solution.py:725
  (58 other events, 575.6 us)
Sparse Core Ops, SparseCore 0:
  14.8 81.6 all-gather.1

commit v4 on v3

--- a/solution.py
+++ b/solution.py
@@ -11,6 +11,7 @@
 HEAD_DIM = 64
 GROUP = 16
 HALF_WIN = 64
+CHUNKS = 4
 LANES = 128
 TILE = 256
 
@@ -74,7 +75,7 @@
         cost_estimate=pl.CostEstimate(
             flops=2**10, bytes_accessed=2**10, transcendentals=0
         ),
-        compiler_params=pltpu.CompilerParams(vmem_limit_bytes=32 * 2**20),
+        compiler_params=pltpu.CompilerParams(vmem_limit_bytes=48 * 2**20),
     )(*args)
 
 
@@ -207,69 +208,71 @@
 
 
 class Weights:
-    def __init__(self, sources, scratches, sem):
-        attn, mlp_in, mlp_out = self.places = scratches
-        width = attn.shape[1]
-        copies = [[], [], []]
+    def __init__(self, sources, mlp_out):
+        self.sources = sources
+        self.mlp_out = sources[-1]
         if len(sources) == 1:
-            (stacked,) = sources
-            shard = attn.shape[0] // GROUP
-            columns = mlp_in.shape[1] // width
-            pair = 2 * mlp_out.shape[0] // GROUP
-            upper = first_block(pair)
-            block = shard * (1 + columns) + upper
-            for d in range(GROUP):
-                base = d * block
-                here = pl.ds(d * shard, shard)
-                copies[0].append((stacked.at[pl.ds(base, shard)], attn.at[here]))
-                for p in range(columns):
-                    copies[1].append(
-                        (
-                            stacked.at[pl.ds(base + (1 + p) * shard, shard)],
-                            mlp_in.at[here, pl.ds(p * width, width)],
-                        )
-                    )
-                rows = pair - upper if d % 2 else upper
-                start = d // 2 * pair + d % 2 * upper
-                copies[2].append(
-                    (
-                        stacked.at[pl.ds(base + (1 + columns) * shard, rows)],
-                        mlp_out.at[pl.ds(start, rows)],
-                    )
-                )
-        else:
-            for group, source, place in zip(copies, sources, scratches):
-                group.append((source, place))
-        self.copies, index = [], 0
-        for group in copies:
-            self.copies.append([])
-            for source, place in group:
-                self.copies[-1].append(pltpu.make_async_copy(source, place, sem.at[index]))
-                index += 1
-
-    def start(self, order):
-        for which in order:
-            for copy in self.copies[which]:
-                copy.start()
+            self.mlp_out = mlp_out
+            unpack_rows(sources[0], mlp_out)
 
     def get(self, which):
-        for copy in self.copies[which]:
-            copy.wait()
-        self.copies[which] = []
-        return self.places[which][...]
+        if which == 2:
+            return self.mlp_out[...]
+        if len(self.sources) > 1:
+            return self.sources[which][...]
+        (wide,) = self.sources
+        width = wide.shape[0]
+        inner = 2 * self.mlp_out.shape[0]
+        return wide[:, width : width + inner] if which else wide[:, :width]
 
 
 def first_block(pair):
     return -(-pair // 32) * 16
 
 
-def weight_scratch(width, inner, hidden):
-    return [
-        pltpu.VMEM((width, width), BF),
-        pltpu.VMEM((width, inner), BF),
-        pltpu.VMEM((hidden, width), BF),
-        pltpu.SemaphoreType.DMA((GROUP * (2 + inner // width),)),
-    ]
+def packed_pieces(shard, rows, width):
+    yield 0, shard, 0, width, 0, 0
+    rest = rows - shard
+    side = width // 3
+    yield 0, rest, width, 2 * side, shard, 0
+    yield rest, 16, width, side, shard, 2 * side
+    yield rest, 16, width + side, side, shard + 16, 2 * side
+
+
+def unpack_rows(wide, mlp_out):
+    hidden, width = mlp_out.shape
+    shard = wide.shape[0] // GROUP
+    start = wide.shape[1] - width - 2 * (width // 3)
+    pair = 2 * hidden // GROUP
+    upper = first_block(pair)
+    for d in range(GROUP):
+        low = d // 2 * pair + d % 2 * upper
+        have = pair - upper if d % 2 else upper
+        for row, rows, column, columns, to_row, to_column in packed_pieces(shard, upper, width):
+            rows = min(rows, have - to_row)
+            if rows > 0:
+                mlp_out[low + to_row : low + to_row + rows, to_column : to_column + columns] = wide[
+                    d * shard + row : d * shard + row + rows, start + column : start + column + columns
+                ]
+
+
+def stack_body(odd_ref, attn_ref, mlp_in_ref, own_ref, beside_ref, out_ref):
+    shard, width = attn_ref.shape
+    inner = mlp_in_ref.shape[1]
+    out_ref[:, :width] = attn_ref[...]
+    out_ref[:, width : width + inner] = mlp_in_ref[...]
+    own, beside = own_ref[...].astype(F32), beside_ref[...].astype(F32)
+    moved = beside.shape[0]
+    even = jnp.concatenate([own, beside], 0)
+    odd = jnp.concatenate([own[moved:], beside, beside], 0)
+    block = jnp.where(odd_ref[0] == 1, odd, even).astype(BF)
+    start = width + inner
+    for row, rows, column, columns, from_row, from_column in packed_pieces(
+        shard, block.shape[0], width
+    ):
+        out_ref[row : row + rows, start + column : start + column + columns] = block[
+            from_row : from_row + rows, from_column : from_column + columns
+        ]
 
 
 def mlp_forward(layer_in, attended, gain, weights):
@@ -301,44 +304,31 @@
     return d_gate_up, gain_grad, d_middle, d_attn, d_attended
 
 
-def parts_of(first_ref, place, sem):
-    width = place.shape[0]
-    return [
-        pltpu.make_async_copy(
-            first_ref.at[:, pl.ds(c * width, width)], place.at[:, pl.ds(c * width, width)], sem.at[c]
-        )
-        for c in range(3)
-    ]
-
-
-def qkv_scratch(width):
-    return [pltpu.VMEM((width, 3 * width), BF), pltpu.SemaphoreType.DMA((3,))]
-
-
-def project(xhat, gain, first_ref, table_ref, normed_ref, copies=(None,) * 3):
+def project(xhat, gain, first_ref, table_ref, normed_ref):
     width = xhat.shape[1]
     normed = (xhat * gain).astype(BF)
     normed_ref[...] = normed
     tables = [table_ref[i] for i in range(3)]
-    results = []
-    for part, copy in enumerate(copies):
-        if copy is not None:
-            copy.wait()
-        results.append(dot(normed, first_ref[:, part * width : (part + 1) * width]))
+    results = [dot(normed, first_ref[:, c * width : (c + 1) * width]) for c in range(3)]
     queries, keys, values = chunks_of(results[0]), chunks_of(results[1]), results[2]
     return [rotate(c, tables) for c in queries], [rotate(c, tables) for c in keys], values
 
 
-def input_backward(d_middle, d_projected, x_ref, gain_ref, place, copies, grad_ref, gain_out_ref):
-    width = x_ref.shape[1]
-    xhat, scale = moments(x_ref[...].astype(F32))
-    d_normed = jnp.zeros(x_ref.shape, F32)
-    for part, copy in enumerate(copies):
-        copy.wait()
-        lanes = slice(part * width, (part + 1) * width)
-        d_normed += dot_bt(d_projected[:, lanes], place[:, lanes])
+def input_backward(d_middle, d_projected, x, gain_ref, first_ref, gain_out_ref):
+    d_normed = dot_bt(d_projected, first_ref[:, : d_projected.shape[1]])
+    xhat, scale = moments(x)
     gain_out_ref[...] = jnp.sum(d_normed * xhat, 0, keepdims=True)
-    grad_ref[...] = (d_middle + norm_back(d_normed, gain_ref[...], xhat, scale)).astype(BF)
+    return (d_middle + norm_back(d_normed, gain_ref[...], xhat, scale)).astype(BF)
+
+
+def joined(refs):
+    return jnp.concatenate([ref[...] for ref in refs], 0)
+
+
+def store_chunks(refs, rows):
+    size = rows.shape[0] // len(refs)
+    for i, ref in enumerate(refs):
+        ref[...] = rows[i * size : (i + 1) * size]
 
 
 def message_body(w_ref, attn_ref, mlp_ref, ids_ref, out_ref, rows_scr, ids_scr):
@@ -362,8 +352,7 @@
 
 
 def local_project_body(place_ref, x_ref, table_ref, *refs):
-    pieces, refs = refs[:-8], refs[-8:]
-    stored_ref, extra_ref, normed_ref, q_ref, kv_ref, first_ref, sem, store_sem = refs
+    pieces, (first_ref, extra_ref, normed_ref, q_ref, kv_ref, sem) = refs[:-6], refs[-6:]
     rows = pieces[0].shape[0]
     copies = []
     for apart, piece in enumerate(pieces):
@@ -375,8 +364,6 @@
     xhat, _ = moments(x_ref[...].astype(F32))
     for copy in copies:
         copy.wait()
-    store = pltpu.make_async_copy(first_ref, stored_ref, store_sem)
-    store.start()
     extra = first_ref[:, first_ref.shape[1] - LANES :].astype(F32).T
     extra_ref[...] = extra[: extra_ref.shape[0]]
     queries, keys, values = project(xhat, extra[:1], first_ref, table_ref, normed_ref)
@@ -385,7 +372,6 @@
         q_ref[:, LANES * j : LANES * (j + 1)] = q.astype(BF)
         kv_ref[:, LANES * j : LANES * (j + 1)] = k.astype(BF)
     kv_ref[:, width:] = values.astype(BF)
-    store.wait()
 
 
 def two_heads(chunk):
@@ -450,35 +436,30 @@
             d_after_ref[here, part] = grads[2 * rows :].astype(BF)
 
 
-def local_join_body(
-    lower_ref, dq_ref, own_ref, low_ref, high_ref, table_ref, other_ref, out_ref
-):
-    width = dq_ref.shape[1]
-
+def local_join_body(lower_ref, dq_ref, own_ref, low_ref, high_ref, table_ref, other_ref, *out_refs):
     @pl.when(lower_ref[0] == 1)
     def _():
         tables = [table_ref[i] for i in range(3)]
-        out_ref[:, :width] = dq_ref[...]
+        width = dq_ref.shape[1]
         total = own_ref[...] + low_ref[...].astype(F32) + high_ref[...].astype(F32)
-        for j, chunk in enumerate(chunks_of(total[:, :width])):
-            start = width + LANES * j
-            out_ref[:, start : start + LANES] = unrotate(chunk, tables).astype(BF)
-        out_ref[:, 2 * width :] = total[:, width:].astype(BF)
+        keys = [unrotate(chunk, tables).astype(BF) for chunk in chunks_of(total[:, :width])]
+        store_chunks(
+            out_refs, jnp.concatenate([dq_ref[...]] + keys + [total[:, width:].astype(BF)], 1)
+        )
 
     @pl.when(lower_ref[0] == 0)
     def _():
-        out_ref[...] = other_ref[...]
+        store_chunks(out_refs, other_ref[...])
 
 
 def local_middle_body(*refs):
-    sources, refs = refs[:-12], refs[-12:]
-    x_ref, att_ref, gain_ref, out_ref, normed_ref, mixed_ref, middle_ref, gate_up_ref = refs[:8]
-    weights = Weights(sources, refs[8:11], refs[11])
-    weights.start((0, 1, 2))
+    sources, refs = refs[:-10], refs[-10:]
+    x_ref, att_ref, gain_ref, normed_ref, mixed_ref, middle_ref, gate_up_ref = refs[:7]
+    weights = Weights(sources, refs[9])
     middle, normed, gate, up, mixed, result = mlp_forward(
         x_ref[...].astype(F32), att_ref[...], gain_ref[...], weights
     )
-    out_ref[...] = result
+    store_chunks(refs[7:9], result)
     normed_ref[...] = normed
     mixed_ref[...] = mixed
     middle_ref[...] = middle
@@ -488,14 +469,15 @@
 
 
 def local_back_middle_body(*refs):
-    sources, refs = refs[:-14], refs[-14:]
-    lower_ref, up_ref, middle_ref, gate_up_ref, gain_ref, other_ref = refs[:6]
-    right_ref, gain_out_ref, d_middle_ref, d_att_ref = refs[6:10]
-    weights = Weights(sources, refs[10:13], refs[13])
-    weights.start((2, 1, 0))
+    count = 11 + CHUNKS
+    sources, refs = refs[:-count], refs[-count:]
+    lower_ref, low_ref, high_ref, middle_ref, gate_up_ref, gain_ref, other_ref = refs[:7]
+    gain_out_ref, d_middle_ref, d_att_ref = refs[7:10]
+    chunk_refs = refs[10 : 10 + CHUNKS]
+    weights = Weights(sources, refs[10 + CHUNKS])
     half = gate_up_ref.shape[1] // 2
     d_gate_up, gain_grad, d_middle, d_attn, d_attended = mlp_backward(
-        up_ref[...], middle_ref[...], gate_up_ref[:, :half], gate_up_ref[:, half:],
+        joined([low_ref, high_ref]), middle_ref[...], gate_up_ref[:, :half], gate_up_ref[:, half:],
         gain_ref[...], weights,
     )
     gain_out_ref[...] = gain_grad
@@ -504,31 +486,24 @@
 
     @pl.when(lower_ref[0] == 1)
     def _():
-        right_ref[:, : 2 * half] = d_gate_up
-        right_ref[:, 2 * half :] = d_attn
+        store_chunks(chunk_refs, jnp.concatenate([d_gate_up, d_attn], 1))
 
     @pl.when(lower_ref[0] == 0)
     def _():
-        right_ref[...] = other_ref[...]
-
-
-def input_backward_body(
-    first_ref, d_middle_ref, d_proj_ref, x_ref, gain_ref, grad_ref, gain_out_ref, place, sem
-):
-    copies = parts_of(first_ref, place, sem)
-    for copy in copies:
-        copy.start()
-    input_backward(
-        d_middle_ref[...], d_proj_ref[...], x_ref, gain_ref, place, copies, grad_ref, gain_out_ref
-    )
-
-
-def global_project_body(first_ref, x_ref, gain_ref, table_ref, normed_ref, sent_ref, place, sem):
-    copies = parts_of(first_ref, place, sem)
-    for copy in copies:
-        copy.start()
-    xhat, _ = moments(x_ref[...].astype(F32))
-    queries, keys, values = project(xhat, gain_ref[...], place, table_ref, normed_ref, copies)
+        store_chunks(chunk_refs, other_ref[...])
+
+
+def input_backward_body(first_ref, d_middle_ref, x_ref, gain_ref, *refs):
+    d_proj_refs, (grad_ref, gain_out_ref) = refs[:-2], refs[-2:]
+    x = x_ref[...].astype(F32)
+    grad_ref[...] = input_backward(
+        d_middle_ref[...], joined(d_proj_refs), x, gain_ref, first_ref, gain_out_ref
+    )
+
+
+def global_project_body(first_ref, low_ref, high_ref, gain_ref, table_ref, normed_ref, sent_ref):
+    xhat, _ = moments(joined([low_ref, high_ref]).astype(F32))
+    queries, keys, values = project(xhat, gain_ref[...], first_ref, table_ref, normed_ref)
     pack_pairs(queries, keys, sent_ref)
     pack_folded(chunks_of(values), sent_ref, sent_ref.shape[1] * 2 // 3)
 
@@ -661,17 +636,16 @@
 
 
 def global_middle_body(*refs):
-    sources, refs = refs[:-16], refs[-16:]
-    got_ref, x_ref, up_ref, gain_ref, out_ref, att_ref, normed_ref, mixed_ref = refs[:8]
-    right_ref, gain_out_ref, d_middle_ref, sent_ref = refs[8:12]
-    weights = Weights(sources, refs[12:15], refs[15])
-    weights.start((0, 1, 2))
-    rows = x_ref.shape[0] // 2
+    sources, refs = refs[:-14], refs[-14:]
+    got_ref, low_ref, high_ref, up_ref, gain_ref, out_ref, att_ref, normed_ref, mixed_ref = refs[:9]
+    right_ref, gain_out_ref, d_middle_ref, sent_ref = refs[9:13]
+    weights = Weights(sources, refs[13])
+    rows = low_ref.shape[0]
     attended = jnp.concatenate([c.astype(BF) for c in unpack_folded(got_ref, 0, rows)], 1)
     att_ref[...] = attended
     gain = gain_ref[...]
     middle, normed, gate, up, mixed, result = mlp_forward(
-        x_ref[...].astype(F32), attended, gain, weights
+        joined([low_ref, high_ref]).astype(F32), attended, gain, weights
     )
     out_ref[...] = result
     normed_ref[...] = normed
@@ -687,20 +661,20 @@
 
 
 def global_finish_body(
-    first_ref, got_ref, d_middle_ref, x_ref, gain_ref, table_ref, d_proj_ref, grad_ref, gain_out_ref, place, sem
+    first_ref, got_ref, d_middle_ref, low_ref, high_ref, gain_ref, table_ref,
+    d_proj_ref, gain_out_ref, *grad_refs,
 ):
-    copies = parts_of(first_ref, place, sem)
-    for copy in copies:
-        copy.start()
     tables = [table_ref[i] for i in range(3)]
-    rows = x_ref.shape[0] // 2
+    x = joined([low_ref, high_ref]).astype(F32)
+    rows = low_ref.shape[0]
     d_queries, d_keys = unpack_pairs(got_ref, rows)
     d_values = unpack_folded(got_ref, rows * 3 // 2, rows)
     parts = [unrotate(c, tables).astype(BF) for c in d_queries + d_keys]
     d_projected = jnp.concatenate(parts + [c.astype(BF) for c in d_values], 1)
     d_proj_ref[...] = d_projected
-    input_backward(
-        d_middle_ref[...], d_projected, x_ref, gain_ref, place, copies, grad_ref, gain_out_ref
+    store_chunks(
+        grad_refs,
+        input_backward(d_middle_ref[...], d_projected, x, gain_ref, first_ref, gain_out_ref),
     )
 
 
@@ -717,8 +691,9 @@
     return lax.all_to_all(blocks, "dp", 0, 0, axis_index_groups=groups)
 
 
-def to_other_section(rows, step):
-    return lax.ppermute(rows, "section", [(0, 1)] if step > 0 else [(1, 0)])
+def to_other_section(chunks, step):
+    pairs = [(0, 1)] if step > 0 else [(1, 0)]
+    return [lax.ppermute(rows, "section", pairs) for rows in chunks]
 
 
 def partner(rows, apart, count):
@@ -726,14 +701,11 @@
 
 
 def group_pieces(piece, count):
-    pieces = {0: piece}
-    for apart in (4, 8, 12):
-        pieces[apart] = partner(piece, apart, count)
-    for apart in (0, 4, 8, 12):
-        pieces[apart + 2] = partner(pieces[apart], 2, count)
-    for apart in range(0, GROUP, 2):
-        pieces[apart + 1] = partner(pieces[apart], 1, count)
-    return [pieces[apart] for apart in range(GROUP)]
+    pieces = [piece]
+    pieces += lax.optimization_barrier([partner(piece, apart, count) for apart in (4, 8, 12)])
+    pieces += lax.optimization_barrier([partner(item, 2, count) for item in pieces])
+    pieces += [partner(item, 1, count) for item in pieces]
+    return [pieces[apart % 2 * 8 + apart // 2 % 2 * 4 + apart // 4] for apart in range(GROUP)]
 
 
 def in_order(pieces, group_pos, count):
@@ -763,10 +735,11 @@
 
 def product_body(ranges, *refs):
     refs, outs = refs[:-4], refs[-4:]
+    rights = refs[: len(refs) - 4 * len(ranges)]
     rows = outs[0].shape[0]
     for index, (start, end) in enumerate(ranges):
-        left = jnp.concatenate([ref[...] for ref in refs[4 + 4 * index : 8 + 4 * index]], 1)
-        right = jnp.concatenate([ref[:, start:end] for ref in refs[:4]], 0)
+        left = jnp.concatenate([ref[...] for ref in refs[len(rights) + 4 * index :][:4]], 1)
+        right = jnp.concatenate([ref[:, start:end] for ref in rights], 0)
         product = dot(left, right)
         for plane, out_ref in enumerate(outs):
             part = product[plane * rows : (plane + 1) * rows]
@@ -821,17 +794,22 @@
     inner = mlp_in_weight.shape[2]
     hidden = mlp_out_weight.shape[1] * count
     if count == GROUP:
-        upper = first_block(2 * mlp_out_weight.shape[1])
-        moved = upper - mlp_out_weight.shape[1]
+        moved = first_block(2 * mlp_out_weight.shape[1]) - mlp_out_weight.shape[1]
         beside = partner(mlp_out_weight[0, :moved], 1, count)
-        block = jnp.where(
-            replica % 2 == 0,
-            jnp.concatenate([mlp_out_weight[0], beside]),
-            jnp.concatenate([mlp_out_weight[0, moved:], beside, beside]),
+        (stacked,) = on_core(
+            stack_body,
+            [((shard, width + inner + width + 2 * (width // 3)), BF)],
+            (
+                (replica % 2)[None],
+                attn_out_weight[0],
+                mlp_in_weight[0],
+                mlp_out_weight[0],
+                beside,
+            ),
+            (),
+            [pltpu.SMEM] + [pltpu.VMEM] * 4,
         )
-        stacked = [attn_out_weight[0]]
-        stacked += [mlp_in_weight[0, :, c : c + width] for c in range(0, inner, width)]
-        others = [lax.all_gather(jnp.concatenate(stacked + [block]), "dp", axis=0, tiled=True)]
+        others = [lax.all_gather(stacked, "dp", axis=0, tiled=True)]
     else:
         others = [
             lax.all_gather(item[0], "dp", axis=0, tiled=True)
@@ -859,13 +837,8 @@
             ((rows, 2 * width), BF),
         ],
         (group_pos[None], in_0, local_tables, *pieces),
-        [
-            pltpu.VMEM((width, 3 * width + LANES), BF),
-            pltpu.SemaphoreType.DMA((len(pieces),)),
-            pltpu.SemaphoreType.DMA,
-        ],
+        [pltpu.SemaphoreType.DMA((len(pieces),))],
         [pltpu.SMEM, pltpu.VMEM, pltpu.VMEM] + [pl.ANY] * len(pieces),
-        [pltpu.HBM] + [pltpu.VMEM] * 4,
     )
     gain_attn, gain_mlp = extra[:1], extra[1:2]
     all_ids = extra[2 : 2 + micro_count * runs].reshape(micro_count, runs, count, shard)
@@ -899,18 +872,17 @@
         [((rows, width), BF), ((pairs, 1, LANES), F32)],
         (q_0, *around_0, bias),
     )
-    out_0, n2_0, mixed_0, middle_0, gate_up_0 = on_core(
+    n2_0, mixed_0, middle_0, gate_up_0, *out_0 = on_core(
         local_middle_body,
         [
-            ((rows, width), BF),
             ((rows, width), BF),
             ((rows, hidden), BF),
             ((rows, width), F32),
             ((rows, inner), F32),
-        ],
+        ]
+        + [((row_count, width), BF)] * micro_count,
         (*others, in_0, att_0, gain_mlp),
-        weight_scratch(width, inner, hidden),
-        [pltpu.HBM] * len(others) + [pltpu.VMEM] * 3,
+        [pltpu.VMEM((hidden, width), BF)],
     )
 
     in_1 = to_other_section(out_0, 1)
@@ -919,9 +891,7 @@
     normed_1, sent = on_core(
         global_project_body,
         [((rows, width), BF), ((GROUP, 3 * fold, LANES), BF)],
-        (first, in_1, gain_attn, global_tables),
-        qkv_scratch(width),
-        [pltpu.HBM] + [pltpu.VMEM] * 3,
+        (first, *in_1, gain_attn, global_tables),
     )
     got = exchange(sent, count)
     beside = jnp.concatenate(
@@ -957,9 +927,8 @@
             ((rows, width), F32),
             ((GROUP, fold, LANES), BF),
         ],
-        (*others, folded, in_1, up_1, gain_mlp),
-        weight_scratch(width, inner, hidden),
-        [pltpu.HBM] * len(others) + [pltpu.VMEM] * 4,
+        (*others, folded, *in_1, up_1, gain_mlp),
+        [pltpu.VMEM((hidden, width), BF)],
     )
     d_folded = exchange(sent, count)
     sent, to_beside = on_core(
@@ -1009,32 +978,29 @@
             (3 * shard, left[0].shape[2]),
         )
     )
-    d_proj_1, grad_1, gain_attn_1 = on_core(
+    d_proj_1, gain_attn_1, *grad_1 = on_core(
         global_finish_body,
-        [((rows, 3 * width), BF), ((rows, width), BF), ((1, width), F32)],
-        (first, got, d_mid_1, in_1, gain_attn, global_tables),
-        qkv_scratch(width),
-        [pltpu.HBM] + [pltpu.VMEM] * 5,
+        [((rows, 3 * width), BF), ((1, width), F32)] + [((row_count, width), BF)] * micro_count,
+        (first, got, d_mid_1, *in_1, gain_attn, global_tables),
     )
 
     up_0 = to_other_section(grad_1, -1)
-    d_mlp = jnp.where(lower, up_0, up_1)
-    across, beside = partner(d_mlp, 2, count), partner(d_mlp, 1, count)
-    d_mlp = [d_mlp, beside, across, partner(across, 1, count)]
-    out_blocks = plane_product(d_mlp, [(mixed, 0, width)])
-    right, gain_mlp_0, d_mid_0, d_att_0 = on_core(
+    d_mlp = [
+        jnp.where(lower, a, up_1[i * row_count : (i + 1) * row_count]) for i, a in enumerate(up_0)
+    ]
+    across_mlp = [partner(item, 2, count) for item in d_mlp]
+    beside_mlp = [partner(item, 1, count) for item in d_mlp]
+    chunk = rows // CHUNKS
+    gain_mlp_0, d_mid_0, d_att_0, *right = on_core(
         local_back_middle_body,
-        [
-            ((rows, inner + width), BF),
-            ((1, width), F32),
-            ((rows, width), F32),
-            ((rows, width), BF),
-        ],
-        (*others, lower_flag, up_0, middle_0, gate_up_0, gain_mlp, right_1),
-        weight_scratch(width, inner, hidden),
-        [pltpu.HBM] * len(others) + [pltpu.SMEM] + [pltpu.VMEM] * 5,
-    )
-    beside, across = partner(right, 1, count), partner(right, 2, count)
+        [((1, width), F32), ((rows, width), F32), ((rows, width), BF)]
+        + [((chunk, inner + width), BF)] * CHUNKS,
+        (*others, lower_flag, *up_0, middle_0, gate_up_0, gain_mlp, right_1),
+        [pltpu.VMEM((hidden, width), BF)],
+        [pltpu.VMEM] * len(others) + [pltpu.SMEM] + [pltpu.VMEM] * 6,
+    )
+    across = [partner(item, 2, count) for item in right]
+    beside = [partner(item, 1, count) for item in right]
     dq_0, d_own, d_before, d_after = on_core(
         local_backward_body,
         [
@@ -1047,24 +1013,24 @@
     )
     from_after = lax.ppermute(d_before, "dp", down_pairs)
     from_before = lax.ppermute(d_after, "dp", up_pairs)
-    from_after, out_blocks = lax.optimization_barrier((from_after, out_blocks))
-    mlp_out_share = sum_planes(out_blocks, count)
-    (d_proj,) = on_core(
+    from_after, across_mlp = lax.optimization_barrier((from_after, across_mlp))
+    d_proj = on_core(
         local_join_body,
-        [((rows, 3 * width), BF)],
+        [((chunk, 3 * width), BF)] * CHUNKS,
         (lower_flag, dq_0, d_own, from_after, from_before, local_tables, d_proj_1),
         (),
         [pltpu.SMEM] + [pltpu.VMEM] * 6,
     )
-    right = [right, beside, across, partner(across, 1, count)]
+    d_mlp += beside_mlp + across_mlp + [partner(item, 1, count) for item in across_mlp]
+    mlp_out_share = sum_planes(plane_product(d_mlp, [(mixed, 0, width)]), count)
+    d_proj, across = lax.optimization_barrier((list(d_proj), across))
+    right = right + beside + across + [partner(item, 1, count) for item in across]
     in_blocks = plane_product(right, [(n2, 0, inner), (att, inner, inner + width)])
     in_share = sum_planes(in_blocks, count)
     grad_0, gain_attn_0 = on_core(
         input_backward_body,
         [((rows, width), BF), ((1, width), F32)],
-        (first, d_mid_0, d_proj, in_0, gain_attn),
-        qkv_scratch(width),
-        [pltpu.HBM] + [pltpu.VMEM] * 4,
+        (first, d_mid_0, in_0, gain_attn, *d_proj),
     )
     gains = jnp.where(
         lower,
@@ -1073,9 +1039,10 @@
     )
     gains = gains + partner(gains, 1, count)
     gains = gains + partner(gains, 2, count)
-    across = partner(d_proj, 2, count)
+    across = [partner(item, 2, count) for item in d_proj]
     across, in_blocks, gains = lax.optimization_barrier((across, in_blocks, gains))
-    d_proj = [d_proj, partner(d_proj, 1, count), across, partner(across, 1, count)]
+    beside = [partner(item, 1, count) for item in d_proj]
+    d_proj = d_proj + beside + across + [partner(item, 1, count) for item in across]
     qkv_blocks = plane_product(d_proj, [(n1, 0, 3 * width)])
     qkv_share = sum_planes(qkv_blocks, count)
     gains, _ = lax.optimization_barrier((gains, qkv_blocks))
@@ -1086,8 +1053,8 @@
     gains = lax.dynamic_slice_in_dim(gains, replica * shard, shard, 1)
 
     return (
-        jnp.where(lower, out_0, out_1).reshape(1, micro_count, row_count, width),
-        jnp.where(lower, grad_0, grad_1).reshape(1, micro_count, row_count, width),
+        jnp.where(lower, jnp.concatenate(out_0), out_1).reshape(1, micro_count, row_count, width),
+        jnp.where(lower, grad_0, jnp.concatenate(grad_1)).reshape(1, micro_count, row_count, width),
         qkv_share[None],
         in_share[None, :, inner:],
         in_share[None, :, :inner],

time: 364 us -> 376 us (1.033)
  starting transfers between devices: 59.8 us -> 88.9 us
  local copies, waits for them, and re-layouts: 40.1 us -> 28 us
  Pallas kernels: 62.4 us -> 53 us
  waiting for transfers between devices: 117 us -> 125 us
  other arithmetic: 14.9 us -> 9.69 us
    ppermute x43 -> x64, starting transfers between devices: 42.3 us -> 69.2 us  [partner(): return lax.ppermute(rows, 'dp', [(i, i ^ apart) for i in range(count)])]
    pallas_call x16 -> x17, Pallas kernels: 62.4 us -> 53 us  [on_core(): pl.pallas_call(body, out_shape=[jax.ShapeDtypeStruct(shape, dtype) for sh...]
    unnamed x114 -> x124, local copies, waits for them, and re-layouts: 25 us -> 16.7 us
    all_to_all x1, waiting for transfers between devices: 1.83 us -> 8.15 us  [exchange(): return lax.all_to_all(blocks, 'dp', 0, 0, axis_index_groups=groups)]
    ppermute x43 -> x64, waiting for transfers between devices: 106 us -> 108 us  [partner(): return lax.ppermute(rows, 'dp', [(i, i ^ apart) for i in range(count)])]
    ppermute x2 -> x4, waiting for transfers between devices: 8.07 us -> 7.87 us  [to_other_section(): return [lax.ppermute(rows, 'section', pairs) for rows in chunks]]
  transfers between devices with their start and end apart: 51 -> 74, of which waited for: 19 -> 22; matrix products, arithmetic and copies ran while one was open for 8% -> 4% of each run, Pallas kernels for 7% -> 4%
where the time goes in v4:
time: 376 us; the launch traced here: 373 us
  waiting for transfers between devices  125 us (33%)
  starting transfers between devices  88.9 us (24%)
  blocking collectives  53.2 us (14%)
  Pallas kernels  53 us (14%)
  local copies, waits for them, and re-layouts  28 us (7%)
  between operations  15.2 us (4%)
  other arithmetic  9.69 us (3%)
    ppermute x64, waiting for transfers between devices, partner(): return lax.ppermute(rows, 'dp', [(i, i ^ apart) for i in range(count)])  108 us
    ppermute x64, starting transfers between devices, partner(): return lax.ppermute(rows, 'dp', [(i, i ^ apart) for i in range(count)])  69.2 us
    all_to_all x3, blocking collectives, exchange(): return lax.all_to_all(blocks, 'dp', 0, 0, axis_index_groups=groups)  53.2 us
    pallas_call x17, Pallas kernels, on_core(): pl.pallas_call(body, out_shape=[jax.ShapeDtypeStruct(shape, dtype) for sh...  53 us
    unnamed x124, local copies, waits for them, and re-layouts  16.7 us
    all_to_all x1, waiting for transfers between devices, exchange(): return lax.all_to_all(blocks, 'dp', 0, 0, axis_index_groups=groups)  8.15 us
    ppermute x4, waiting for transfers between devices, to_other_section(): return [lax.ppermute(rows, 'section', pairs) for rows in chunks]  7.87 us
  transfers between devices with their start and end apart: 74, of which 22 were waited for; matrix products, arithmetic and copies ran while one was open for 4% of the time, Pallas kernels for 4%

profile of v4, /device:TPU:0, one launch (start us, length us, event | category | flops | bytes accessed | tf_op | source)
XLA Modules:
  0.0 372.7 jit_solution(7013457554626610072)
XLA Ops:
  13.2 5.0 %collective-permute-start.5 = (bf16[48,2432]{1,0:T(8,128)(2,1)S(1)}, bf16[48,2432]{1,0:T(8,128)(2,1)S(1)}, u32[]{:S(2)}, u32[]{:S(2)}) collective-permute-start(bf16[48,2432]{1,0:T(8,128)(2,1)S(1)} %shard_map.153.refs_0_), channel_id=1, source_target_pairs={{0,12},{1,13},{2,14},{3,15},{4,8},{5,9},{6,10},{7,11},{8,4},{9,5},... | collective-permute-start | bytes 700424 | tf_op jit(solution)/shard_map/ppermute | solution.py:700
  20.5 4.3 %collective-permute-done.5.refs_12_ = bf16[48,2432]{1,0:T(8,128)(2,1)S(1)} collective-permute-done((bf16[48,2432]{1,0:T(8,128)(2,1)S(1)}, bf16[48,2432]{1,0:T(8,128)(2,1)S(1)}, u32[]{:S(2)}, u32[]{:S(2)}) %collective-permute-start.5) | collective-permute-done | bytes 233504 | tf_op jit(solution)/shard_map/ppermute | solution.py:700
  24.8 27.0 %collective-permute-done.4.refs_8_ = bf16[48,2432]{1,0:T(8,128)(2,1)S(1)} collective-permute-done((bf16[48,2432]{1,0:T(8,128)(2,1)S(1)}, bf16[48,2432]{1,0:T(8,128)(2,1)S(1)}, u32[]{:S(2)}, u32[]{:S(2)}) %collective-permute-start.4) | collective-permute-done | bytes 233504 | tf_op jit(solution)/shard_map/ppermute | solution.py:700
  54.8 7.4 %collective-permute-done.6.refs_6_ = bf16[48,2432]{1,0:T(8,128)(2,1)S(1)} collective-permute-done((bf16[48,2432]{1,0:T(8,128)(2,1)S(1)}, bf16[48,2432]{1,0:T(8,128)(2,1)S(1)}, u32[]{:S(2)}, u32[]{:S(2)}) %collective-permute-start.6) | collective-permute-done | bytes 233504 | tf_op jit(solution)/shard_map/ppermute | solution.py:700
  62.3 2.5 collective-permute-start.8
  64.9 7.4 %collective-permute-done.7.refs_10_ = bf16[48,2432]{1,0:T(8,128)(2,1)S(1)} collective-permute-done((bf16[48,2432]{1,0:T(8,128)(2,1)S(1)}, bf16[48,2432]{1,0:T(8,128)(2,1)S(1)}, u32[]{:S(2)}, u32[]{:S(2)}) %collective-permute-start.7) | collective-permute-done | bytes 233504 | tf_op jit(solution)/shard_map/ppermute | solution.py:700
  72.3 8.3 %collective-permute-done.8.refs_14_ = bf16[48,2432]{1,0:T(8,128)(2,1)S(1)} collective-permute-done((bf16[48,2432]{1,0:T(8,128)(2,1)S(1)}, bf16[48,2432]{1,0:T(8,128)(2,1)S(1)}, u32[]{:S(2)}, u32[]{:S(2)}) %collective-permute-start.8) | collective-permute-done | bytes 233504 | tf_op jit(solution)/shard_map/ppermute | solution.py:700
  87.4 6.9 %shard_map.154 = (bf16[768,2432]{1,0:T(8,128)(2,1)}, f32[8,768]{1,0:T(8,128)S(1)}, bf16[128,768]{1,0:T(8,128)(2,1)S(1)}, bf16[128,768]{1,0:T(8,128)(2,1)S(1)}, bf16[128,1536]{1,0:T(8,128)(2,1)S(1)}) custom-call(s32[1]{0:T(128)} %bitcast.6.place_ref, bf16[128,768]{1,0:T(8,128)(2,1)S(1)} %bitcast.107, f32[3,128,128]{2,1,0:T(8,128)S(1)} %tile.13.table_ref, ...), custom_call_target="tpu_custom_call" | custom-call | flops 1024 | bytes 1024 | tf_op jit(solution)/shard_map/pallas_call | solution.py:65
  96.2 3.1 collective-permute-start.16
  100.6 3.6 shard_map.155
  104.3 4.4 %shard_map.156 = (bf16[128,768]{1,0:T(8,128)(2,1)S(1)}, bf16[128,1152]{1,0:T(8,128)(2,1)S(1)}, f32[128,768]{1,0:T(8,128)S(1)}, f32[128,2304]{1,0:T(8,128)S(1)}, ...) custom-call(bf16[768,4352]{1,0:T(8,128)(2,1)} %all-gather.2.cloned.1.call-done.refs_0_, ...), custom_call_target="tpu_custom_call" | custom-call | flops 1024 | bytes 1024 | tf_op jit(solution)/shard_map/pallas_call | solution.py:65
  111.3 3.3 collective-permute-start.18
  118.1 2.1 copy-done
  121.3 29.8 %all_to_all.20.got_ref = bf16[16,144,128]{2,1,0:T(8,128)(2,1)S(1)} all-to-all(bf16[16,144,128]{2,1,0:T(8,128)(2,1)S(1)} %get-tuple-element.108), channel_id=1, replica_groups={{0,1,2,3,4,5,6,7,8,9,10,11,12,13,14,15},{16,17,18,19,20,21,22,23,24,25,..., dimensions={0} | all-to-all | bytes 1179648 | tf_op jit(solution)/shard_map/all_to_all | solution.py:691
  153.6 6.0 %shard_map.158 = (bf16[16,48,128]{2,1,0:T(8,128)(2,1)S(1)}, f32[6,1,256]{2,1,0:T(1,128)S(1)}) custom-call(bf16[16,144,128]{2,1,0:T(8,128)(2,1)S(1)} %all_to_all.20.got_ref, bf16[16,64,128]{2,1,0:T(8,128)(2,1)S(1)} %collective-permute-done.20.other_ref, s32[1024,1]{1,0:T(8,128)S(1)} %copy.35.own_seg_ref, s32[1024,1]{1,0:T(8,128)S(1)} %copy.36.shared_seg_ref), custom_call_target="tpu_custom_call" | custom-call | flops 1024 | bytes 1024 | tf_op jit(solution)/shard_map/pallas_call | solution.py:65
  159.7 11.8 %all_to_all.21.refs_1_ = bf16[16,48,128]{2,1,0:T(8,128)(2,1)S(1)} all-to-all(bf16[16,48,128]{2,1,0:T(8,128)(2,1)S(1)} %get-tuple-element.109), channel_id=1, replica_groups={{0,1,2,3,4,5,6,7,8,9,10,11,12,13,14,15},{16,17,18,19,20,21,22,23,24,25,..., dimensions={0} | all-to-all | bytes 393216 | tf_op jit(solution)/shard_map/all_to_all | solution.py:691
  171.5 7.0 %shard_map.159 = (bf16[128,768]{1,0:T(8,128)(2,1)S(1)}, bf16[128,768]{1,0:T(8,128)(2,1)S(1)}, bf16[128,768]{1,0:T(8,128)(2,1)S(1)}, bf16[128,1152]{1,0:T(8,128)(...) custom-call(bf16[768,4352]{1,0:T(8,128)(2,1)} %all-gather.2.cloned.1, ...), custom_call_target="tpu_custom_call" | custom-call | flops 1024 | bytes 1024 | tf_op jit(solution)/shard_map/pallas_call | solution.py:65
  179.5 11.6 %all_to_all.22.d_ref = bf16[16,48,128]{2,1,0:T(8,128)(2,1)S(1)} all-to-all(bf16[16,48,128]{2,1,0:T(8,128)(2,1)S(1)} %get-tuple-element.119), channel_id=1, replica_groups={{0,1,2,3,4,5,6,7,8,9,10,11,12,13,14,15},{16,17,18,19,20,21,22,23,24,25,..., dimensions={0} | all-to-all | bytes 393216 | tf_op jit(solution)/shard_map/all_to_all | solution.py:691
  191.0 8.0 %shard_map.160 = (bf16[16,144,128]{2,1,0:T(8,128)(2,1)S(1)}, bf16[16,64,128]{2,1,0:T(8,128)(2,1)}) custom-call(bf16[16,144,128]{2,1,0:T(8,128)(2,1)S(1)} %all_to_all.20.got_ref, bf16[16,64,128]{2,1,0:T(8,128)(2,1)S(1)} %collective-permute-done.20.other_ref, s32[1024,1]{1,0:T(8,128)S(1)} %copy.35.own_seg_ref, s32[1024,1]{1,0:T(8,128)S(1)} %copy.36.shared_seg_ref, ...), custom_call_target="tpu_custom_call" | custom-call | flops 1024 | bytes 1024 | tf_op jit(solution)/shard_map/pallas_call | solution.py:65
  200.0 1.6 collective-permute-done.21
  201.7 2.2 add_convert_fusion
  203.8 3.7 all-to-all-start.3
  208.3 1.7 copy.37
  210.8 1.9 copy.40
  214.9 8.1 %all-to-all-done.3.got_ref = bf16[16,144,128]{2,1,0:T(8,128)(2,1)S(1)} async-done(((bf16[16,144,128]{2,1,0:T(8,128)(2,1)}), bf16[16,144,128]{2,1,0:T(8,128)(2,1)S(1)}, u32[]{:S(2)}, u32[]{:S(2)}) %all-to-all-start.3) | async-done | bytes 589856 | tf_op jit(solution)/shard_map/all_to_all | solution.py:691
  223.1 2.1 copy-done.1
  230.6 4.8 %collective-permute-done.22.refs_2_ = bf16[64,768]{1,0:T(8,128)(2,1)S(1)} collective-permute-done((bf16[64,768]{1,0:T(8,128)(2,1)S(1)}, bf16[64,768]{1,0:T(8,128)(2,1)S(1)}, u32[]{:S(2)}, u32[]{:S(2)}) %collective-permute-start.22) | collective-permute-done | bytes 98336 | tf_op jit(solution)/shard_map/ppermute | solution.py:696
  236.7 6.1 %shard_map.162 = (f32[1,768]{1,0:T(1,128)S(1)}, f32[128,768]{1,0:T(8,128)S(1)}, bf16[128,768]{1,0:T(8,128)(2,1)S(1)}, bf16[32,3072]{1,0:T(8,128)(2,1)S(1)}, bf16...) custom-call(bf16[768,4352]{1,0:T(8,128)(2,1)} %all-gather.2.cloned.1.call-done.refs_0_, ...), custom_call_target="tpu_custom_call" | custom-call | flops 1024 | bytes 1024 | tf_op jit(solution)/shard_map/pallas_call | solution.py:65
  242.8 3.5 shard_map.163
  247.7 3.1 collective-permute-start.27
  254.3 3.3 collective-permute-done.26.refs_5_
  257.6 2.4 collective-permute-start.29
  260.0 2.1 collective-permute-start.30
  262.2 8.1 %collective-permute-start.48 = (bf16[4,1,216,128]{3,2,0,1:T(8,128)(2,1)S(1)}, bf16[4,1,216,128]{3,2,0,1:T(8,128)(2,1)S(1)}, u32[]{:S(2)}, u32[]{:S(2)}) collective-permute-start(bf16[4,1,216,128]{3,2,0,1:T(8,128)(2,1)S(1)} %pad_maximum_fusion.2), channel_id=1, source_target_pairs={{0,1},{1,0},{2,3},{3,2},{4,5},{5,4},{6,7},{7,6},{8,9},{9,8},{10,11... | collective-permute-start | bytes 663560 | tf_op jit(solution)/shard_map/ppermute | solution.py:700
  270.8 1.8 collective-permute-start.49
  272.5 6.0 %collective-permute-start.50 = (bf16[4,1,216,128]{3,2,0,1:T(8,128)(2,1)S(1)}, bf16[4,1,216,128]{3,2,0,1:T(8,128)(2,1)S(1)}, u32[]{:S(2)}, u32[]{:S(2)}) collective-permute-start(bf16[4,1,216,128]{3,2,0,1:T(8,128)(2,1)S(1)} %pad_maximum_fusion.4), channel_id=1, source_target_pairs={{0,3},{1,2},{2,1},{3,0},{4,7},{5,6},{6,5},{7,4},{8,11},{9,10},{10,... | collective-permute-start | bytes 663560 | tf_op jit(solution)/shard_map/ppermute | solution.py:700
  278.5 2.1 collective-permute-start.64
  280.6 4.2 %collective-permute-start.63 = (bf16[64,768]{1,0:T(8,128)(2,1)S(1)}, bf16[64,768]{1,0:T(8,128)(2,1)S(1)}, u32[]{:S(2)}, u32[]{:S(2)}) collective-permute-start(bf16[64,768]{1,0:T(8,128)(2,1)S(1)} %get-tuple-element.215.refs_0_), channel_id=1, source_target_pairs={{0,1},{1,0},{2,3},{3,2},{4,5},{5,4},{6,7},{7,6},{8,9},{9,8},{10,11... | collective-permute-start | bytes 294920 | tf_op jit(solution)/shard_map/ppermute | solution.py:700
  288.2 4.4 %collective-permute-start.36 = (bf16[32,2304]{1,0:T(8,128)(2,1)S(1)}, bf16[32,2304]{1,0:T(8,128)(2,1)S(1)}, u32[]{:S(2)}, u32[]{:S(2)}) collective-permute-start(bf16[32,2304]{1,0:T(8,128)(2,1)S(1)} %get-tuple-element.146.refs_0_), channel_id=1, source_target_pairs={{0,2},{1,3},{2,0},{3,1},{4,6},{5,7},{6,4},{7,5},{8,10},{9,11},{10,... | collective-permute-start | bytes 442376 | tf_op jit(solution)/shard_map/ppermute | solution.py:700
  292.6 2.0 collective-permute-start.38
  294.7 2.0 collective-permute-start.39
  296.7 7.0 %collective-permute-done.52 = f32[2,768]{1,0:T(2,128)S(1)} collective-permute-done((f32[2,768]{1,0:T(2,128)S(1)}, f32[2,768]{1,0:T(2,128)S(1)}, u32[]{:S(2)}, u32[]{:S(2)}) %collective-permute-start.52) | collective-permute-done | bytes 6176 | tf_op jit(solution)/shard_map/ppermute | solution.py:700
  310.3 2.0 collective-permute-start.67
  312.5 2.3 collective-permute-start.69
  318.3 4.2 %collective-permute-done.70 = f32[2,768]{1,0:T(2,128)S(1)} collective-permute-done((f32[2,768]{1,0:T(2,128)S(1)}, f32[2,768]{1,0:T(2,128)S(1)}, u32[]{:S(2)}, u32[]{:S(2)}) %collective-permute-start.70) | collective-permute-done | bytes 6176 | tf_op jit(solution)/shard_map/ppermute | solution.py:700
  322.5 3.1 collective-permute-start.62
  327.7 22.9 %collective-permute-done.71 = f32[2,768]{1,0:T(2,128)S(1)} collective-permute-done((f32[2,768]{1,0:T(2,128)S(1)}, f32[2,768]{1,0:T(2,128)S(1)}, u32[]{:S(2)}, u32[]{:S(2)}) %collective-permute-start.71) | collective-permute-done | bytes 6176 | tf_op jit(solution)/shard_map/ppermute | solution.py:700
  353.6 11.4 %collective-permute-done.58 = bf16[48,2304]{1,0:T(8,128)(2,1)S(1)} collective-permute-done((bf16[48,2304]{1,0:T(8,128)(2,1)S(1)}, bf16[48,2304]{1,0:T(8,128)(2,1)S(1)}, u32[]{:S(2)}, u32[]{:S(2)}) %collective-permute-start.58) | collective-permute-done | bytes 221216 | tf_op jit(solution)/shard_map/ppermute | solution.py:700
  (324 shorter events, 68.0 us)
Async XLA Ops:
  7.2 97.1 %all-gather.2.cloned.1.call-start = ((), (), s32[]{:S(2)}) async-start(), calls=%async_computation.4 | async-start | bytes 7102464 | tf_op jit(solution)/shard_map/all_gather | solution.py:812
  13.2 11.6 %collective-permute-start.5 = (bf16[48,2432]{1,0:T(8,128)(2,1)S(1)}, bf16[48,2432]{1,0:T(8,128)(2,1)S(1)}, u32[]{:S(2)}, u32[]{:S(2)}) collective-permute-start(bf16[48,2432]{1,0:T(8,128)(2,1)S(1)} %shard_map.153.refs_0_), channel_id=1, source_target_pairs={{0,12},{1,13},{2,14},{3,15},{4,8},{5,9},{6,10},{7,11},{8,4},{9,5},... | collective-permute-start | bytes 700424 | tf_op jit(solution)/shard_map/ppermute | solution.py:700
  18.2 33.6 %collective-permute-start.4 = (bf16[48,2432]{1,0:T(8,128)(2,1)S(1)}, bf16[48,2432]{1,0:T(8,128)(2,1)S(1)}, u32[]{:S(2)}, u32[]{:S(2)}) collective-permute-start(bf16[48,2432]{1,0:T(8,128)(2,1)S(1)} %shard_map.153.refs_0_), channel_id=1, source_target_pairs={{0,8},{1,9},{2,10},{3,11},{4,12},{5,13},{6,14},{7,15},{8,0},{9,1},... | collective-permute-start | bytes 700424 | tf_op jit(solution)/shard_map/ppermute | solution.py:700
  18.2 33.6 %collective-permute-start.3 = (bf16[48,2432]{1,0:T(8,128)(2,1)S(1)}, bf16[48,2432]{1,0:T(8,128)(2,1)S(1)}, u32[]{:S(2)}, u32[]{:S(2)}) collective-permute-start(bf16[48,2432]{1,0:T(8,128)(2,1)S(1)} %shard_map.153.refs_0_), channel_id=1, source_target_pairs={{0,4},{1,5},{2,6},{3,7},{4,0},{5,1},{6,2},{7,3},{8,12},{9,13},{10,... | collective-permute-start | bytes 700424 | tf_op jit(solution)/shard_map/ppermute | solution.py:700
  18.8 35.5 %collective-permute-start.2 = (bf16[48,2432]{1,0:T(8,128)(2,1)S(1)}, bf16[48,2432]{1,0:T(8,128)(2,1)S(1)}, u32[]{:S(2)}, u32[]{:S(2)}) collective-permute-start(bf16[48,2432]{1,0:T(8,128)(2,1)S(1)} %shard_map.153.refs_0_), channel_id=1, source_target_pairs={{0,2},{1,3},{2,0},{3,1},{4,6},{5,7},{6,4},{7,5},{8,10},{9,11},{10,... | collective-permute-start | bytes 700424 | tf_op jit(solution)/shard_map/ppermute | solution.py:700
  20.5 60.1 %collective-permute-start.1 = (bf16[48,2432]{1,0:T(8,128)(2,1)S(1)}, bf16[48,2432]{1,0:T(8,128)(2,1)S(1)}, u32[]{:S(2)}, u32[]{:S(2)}) collective-permute-start(bf16[48,2432]{1,0:T(8,128)(2,1)S(1)} %shard_map.153.refs_0_), channel_id=1, source_target_pairs={{0,1},{1,0},{2,3},{3,2},{4,5},{5,4},{6,7},{7,6},{8,9},{9,8},{10,11... | collective-permute-start | bytes 700424 | tf_op jit(solution)/shard_map/ppermute | solution.py:700
  51.8 10.5 %collective-permute-start.6 = (bf16[48,2432]{1,0:T(8,128)(2,1)S(1)}, bf16[48,2432]{1,0:T(8,128)(2,1)S(1)}, u32[]{:S(2)}, u32[]{:S(2)}) collective-permute-start(bf16[48,2432]{1,0:T(8,128)(2,1)S(1)} %collective-permute-done.3.refs_4_), channel_id=1, source_target_pairs={{0,2},{1,3},{2,0},{3,1},{4,6},{5,7},{6,4},{7,5},{8,10},{9,11},{10,... | collective-permute-start | bytes 700424 | tf_op jit(solution)/shard_map/ppermute | solution.py:700
  53.8 27.3 %collective-permute-start.10 = (bf16[48,2432]{1,0:T(8,128)(2,1)S(1)}, bf16[48,2432]{1,0:T(8,128)(2,1)S(1)}, u32[]{:S(2)}, u32[]{:S(2)}) collective-permute-start(bf16[48,2432]{1,0:T(8,128)(2,1)S(1)} %collective-permute-done.3.refs_4_), channel_id=1, source_target_pairs={{0,1},{1,0},{2,3},{3,2},{4,5},{5,4},{6,7},{7,6},{8,9},{9,8},{10,11... | collective-permute-start | bytes 700424 | tf_op jit(solution)/shard_map/ppermute | solution.py:700
  53.8 27.4 %collective-permute-start.12 = (bf16[48,2432]{1,0:T(8,128)(2,1)S(1)}, bf16[48,2432]{1,0:T(8,128)(2,1)S(1)}, u32[]{:S(2)}, u32[]{:S(2)}) collective-permute-start(bf16[48,2432]{1,0:T(8,128)(2,1)S(1)} %collective-permute-done.4.refs_8_), channel_id=1, source_target_pairs={{0,1},{1,0},{2,3},{3,2},{4,5},{5,4},{6,7},{7,6},{8,9},{9,8},{10,11... | collective-permute-start | bytes 700424 | tf_op jit(solution)/shard_map/ppermute | solution.py:700
  54.3 18.0 %collective-permute-start.7 = (bf16[48,2432]{1,0:T(8,128)(2,1)S(1)}, bf16[48,2432]{1,0:T(8,128)(2,1)S(1)}, u32[]{:S(2)}, u32[]{:S(2)}) collective-permute-start(bf16[48,2432]{1,0:T(8,128)(2,1)S(1)} %collective-permute-done.4.refs_8_), channel_id=1, source_target_pairs={{0,2},{1,3},{2,0},{3,1},{4,6},{5,7},{6,4},{7,5},{8,10},{9,11},{10,... | collective-permute-start | bytes 700424 | tf_op jit(solution)/shard_map/ppermute | solution.py:700
  62.3 18.3 %collective-permute-start.8 = (bf16[48,2432]{1,0:T(8,128)(2,1)S(1)}, bf16[48,2432]{1,0:T(8,128)(2,1)S(1)}, u32[]{:S(2)}, u32[]{:S(2)}) collective-permute-start(bf16[48,2432]{1,0:T(8,128)(2,1)S(1)} %collective-permute-done.5.refs_12_), channel_id=1, source_target_pairs={{0,2},{1,3},{2,0},{3,1},{4,6},{5,7},{6,4},{7,5},{8,10},{9,11},{10,... | collective-permute-start | bytes 700424 | tf_op jit(solution)/shard_map/ppermute | solution.py:700
  72.3 11.5 %collective-permute-start.14 = (bf16[48,2432]{1,0:T(8,128)(2,1)S(1)}, bf16[48,2432]{1,0:T(8,128)(2,1)S(1)}, u32[]{:S(2)}, u32[]{:S(2)}) collective-permute-start(bf16[48,2432]{1,0:T(8,128)(2,1)S(1)} %collective-permute-done.5.refs_12_), channel_id=1, source_target_pairs={{0,1},{1,0},{2,3},{3,2},{4,5},{5,4},{6,7},{7,6},{8,9},{9,8},{10,11... | collective-permute-start | bytes 700424 | tf_op jit(solution)/shard_map/ppermute | solution.py:700
  203.8 19.2 %all-to-all-start.3 = ((bf16[16,144,128]{2,1,0:T(8,128)(2,1)}), bf16[16,144,128]{2,1,0:T(8,128)(2,1)S(1)}, u32[]{:S(2)}, u32[]{:S(2)}) async-start(bf16[16,144,128]{2,1,0:T(8,128)(2,1)} %add_convert_fusion), calls=%async_computation.3 | async-start | bytes 1179648 | tf_op jit(solution)/shard_map/all_to_all | solution.py:691
  227.8 7.6 %collective-permute-start.22 = (bf16[64,768]{1,0:T(8,128)(2,1)S(1)}, bf16[64,768]{1,0:T(8,128)(2,1)S(1)}, u32[]{:S(2)}, u32[]{:S(2)}) collective-permute-start(bf16[64,768]{1,0:T(8,128)(2,1)S(1)} %get-tuple-element.124), channel_id=1, source_target_pairs={{16,0},{17,1},{18,2},{19,3},{20,4},{21,5},{22,6},{23,7},{24,8},{25... | collective-permute-start | bytes 294920 | tf_op jit(solution)/shard_map/ppermute | solution.py:696
  229.2 7.5 %collective-permute-start.23 = (bf16[64,768]{1,0:T(8,128)(2,1)S(1)}, bf16[64,768]{1,0:T(8,128)(2,1)S(1)}, u32[]{:S(2)}, u32[]{:S(2)}) collective-permute-start(bf16[64,768]{1,0:T(8,128)(2,1)S(1)} %get-tuple-element.125), channel_id=1, source_target_pairs={{16,0},{17,1},{18,2},{19,3},{20,4},{21,5},{22,6},{23,7},{24,8},{25... | collective-permute-start | bytes 294920 | tf_op jit(solution)/shard_map/ppermute | solution.py:696
  246.4 15.8 %collective-permute-start.24 = (bf16[128,1536]{1,0:T(8,128)(2,1)S(1)}, bf16[128,1536]{1,0:T(8,128)(2,1)S(1)}, u32[]{:S(2)}, u32[]{:S(2)}) collective-permute-start(bf16[128,1536]{1,0:T(8,128)(2,1)S(1)} %get-tuple-element.134), channel_id=1, source_target_pairs={{1,0},{2,1},{3,2},{4,3},{5,4},{6,5},{7,6},{8,7},{9,8},{10,9},{11,1... | collective-permute-start | bytes 1179656 | tf_op jit(solution)/shard_map/ppermute | solution.py:1014
  247.7 14.5 %collective-permute-start.27 = (bf16[128,1536]{1,0:T(8,128)(2,1)S(1)}, bf16[128,1536]{1,0:T(8,128)(2,1)S(1)}, u32[]{:S(2)}, u32[]{:S(2)}) collective-permute-start(bf16[128,1536]{1,0:T(8,128)(2,1)S(1)} %get-tuple-element.136), channel_id=1, source_target_pairs={{0,1},{1,2},{2,3},{3,4},{4,5},{5,6},{6,7},{7,8},{8,9},{9,10},{10,1... | collective-permute-start | bytes 1179656 | tf_op jit(solution)/shard_map/ppermute | solution.py:1015
  250.8 6.8 %collective-permute-start.26 = (bf16[64,768]{1,0:T(8,128)(2,1)S(1)}, bf16[64,768]{1,0:T(8,128)(2,1)S(1)}, u32[]{:S(2)}, u32[]{:S(2)}) collective-permute-start(bf16[64,768]{1,0:T(8,128)(2,1)S(1)} %get-tuple-element.214.refs_1_), channel_id=1, source_target_pairs={{0,2},{1,3},{2,0},{3,1},{4,6},{5,7},{6,4},{7,5},{8,10},{9,11},{10,... | collective-permute-start | bytes 294920 | tf_op jit(solution)/shard_map/ppermute | solution.py:700
  252.2 7.9 %collective-permute-start.25 = (bf16[64,768]{1,0:T(8,128)(2,1)S(1)}, bf16[64,768]{1,0:T(8,128)(2,1)S(1)}, u32[]{:S(2)}, u32[]{:S(2)}) collective-permute-start(bf16[64,768]{1,0:T(8,128)(2,1)S(1)} %get-tuple-element.215.refs_0_), channel_id=1, source_target_pairs={{0,2},{1,3},{2,0},{3,1},{4,6},{5,7},{6,4},{7,5},{8,10},{9,11},{10,... | collective-permute-start | bytes 294920 | tf_op jit(solution)/shard_map/ppermute | solution.py:700
  252.9 17.8 %collective-permute-start.28 = (bf16[32,3072]{1,0:T(8,128)(2,1)S(1)}, bf16[32,3072]{1,0:T(8,128)(2,1)S(1)}, u32[]{:S(2)}, u32[]{:S(2)}) collective-permute-start(bf16[32,3072]{1,0:T(8,128)(2,1)S(1)} %get-tuple-element.142.refs_0_), channel_id=1, source_target_pairs={{0,2},{1,3},{2,0},{3,1},{4,6},{5,7},{6,4},{7,5},{8,10},{9,11},{10,... | collective-permute-start | bytes 589832 | tf_op jit(solution)/shard_map/ppermute | solution.py:700
  257.6 15.0 %collective-permute-start.29 = (bf16[32,3072]{1,0:T(8,128)(2,1)S(1)}, bf16[32,3072]{1,0:T(8,128)(2,1)S(1)}, u32[]{:S(2)}, u32[]{:S(2)}) collective-permute-start(bf16[32,3072]{1,0:T(8,128)(2,1)S(1)} %get-tuple-element.143.refs_1_), channel_id=1, source_target_pairs={{0,2},{1,3},{2,0},{3,1},{4,6},{5,7},{6,4},{7,5},{8,10},{9,11},{10,... | collective-permute-start | bytes 589832 | tf_op jit(solution)/shard_map/ppermute | solution.py:700
  260.0 18.5 %collective-permute-start.30 = (bf16[32,3072]{1,0:T(8,128)(2,1)S(1)}, bf16[32,3072]{1,0:T(8,128)(2,1)S(1)}, u32[]{:S(2)}, u32[]{:S(2)}) collective-permute-start(bf16[32,3072]{1,0:T(8,128)(2,1)S(1)} %get-tuple-element.144.refs_2_), channel_id=1, source_target_pairs={{0,2},{1,3},{2,0},{3,1},{4,6},{5,7},{6,4},{7,5},{8,10},{9,11},{10,... | collective-permute-start | bytes 589832 | tf_op jit(solution)/shard_map/ppermute | solution.py:700
  262.1 18.5 %collective-permute-start.31 = (bf16[32,3072]{1,0:T(8,128)(2,1)S(1)}, bf16[32,3072]{1,0:T(8,128)(2,1)S(1)}, u32[]{:S(2)}, u32[]{:S(2)}) collective-permute-start(bf16[32,3072]{1,0:T(8,128)(2,1)S(1)} %get-tuple-element.145.refs_3_), channel_id=1, source_target_pairs={{0,2},{1,3},{2,0},{3,1},{4,6},{5,7},{6,4},{7,5},{8,10},{9,11},{10,... | collective-permute-start | bytes 589832 | tf_op jit(solution)/shard_map/ppermute | solution.py:700
  262.2 24.1 %collective-permute-start.48 = (bf16[4,1,216,128]{3,2,0,1:T(8,128)(2,1)S(1)}, bf16[4,1,216,128]{3,2,0,1:T(8,128)(2,1)S(1)}, u32[]{:S(2)}, u32[]{:S(2)}) collective-permute-start(bf16[4,1,216,128]{3,2,0,1:T(8,128)(2,1)S(1)} %pad_maximum_fusion.2), channel_id=1, source_target_pairs={{0,1},{1,0},{2,3},{3,2},{4,5},{5,4},{6,7},{7,6},{8,9},{9,8},{10,11... | collective-permute-start | bytes 663560 | tf_op jit(solution)/shard_map/ppermute | solution.py:700
  270.8 17.0 %collective-permute-start.49 = (bf16[4,1,216,128]{3,2,0,1:T(8,128)(2,1)S(1)}, bf16[4,1,216,128]{3,2,0,1:T(8,128)(2,1)S(1)}, u32[]{:S(2)}, u32[]{:S(2)}) collective-permute-start(bf16[4,1,216,128]{3,2,0,1:T(8,128)(2,1)S(1)} %pad_maximum_fusion.3), channel_id=1, source_target_pairs={{0,2},{1,3},{2,0},{3,1},{4,6},{5,7},{6,4},{7,5},{8,10},{9,11},{10,... | collective-permute-start | bytes 663560 | tf_op jit(solution)/shard_map/ppermute | solution.py:700
  272.5 15.7 %collective-permute-start.50 = (bf16[4,1,216,128]{3,2,0,1:T(8,128)(2,1)S(1)}, bf16[4,1,216,128]{3,2,0,1:T(8,128)(2,1)S(1)}, u32[]{:S(2)}, u32[]{:S(2)}) collective-permute-start(bf16[4,1,216,128]{3,2,0,1:T(8,128)(2,1)S(1)} %pad_maximum_fusion.4), channel_id=1, source_target_pairs={{0,3},{1,2},{2,1},{3,0},{4,7},{5,6},{6,5},{7,4},{8,11},{9,10},{10,... | collective-permute-start | bytes 663560 | tf_op jit(solution)/shard_map/ppermute | solution.py:700
  278.5 8.0 %collective-permute-start.64 = (bf16[64,768]{1,0:T(8,128)(2,1)S(1)}, bf16[64,768]{1,0:T(8,128)(2,1)S(1)}, u32[]{:S(2)}, u32[]{:S(2)}) collective-permute-start(bf16[64,768]{1,0:T(8,128)(2,1)S(1)} %get-tuple-element.214.refs_1_), channel_id=1, source_target_pairs={{0,1},{1,0},{2,3},{3,2},{4,5},{5,4},{6,7},{7,6},{8,9},{9,8},{10,11... | collective-permute-start | bytes 294920 | tf_op jit(solution)/shard_map/ppermute | solution.py:700
  280.6 6.4 %collective-permute-start.63 = (bf16[64,768]{1,0:T(8,128)(2,1)S(1)}, bf16[64,768]{1,0:T(8,128)(2,1)S(1)}, u32[]{:S(2)}, u32[]{:S(2)}) collective-permute-start(bf16[64,768]{1,0:T(8,128)(2,1)S(1)} %get-tuple-element.215.refs_0_), channel_id=1, source_target_pairs={{0,1},{1,0},{2,3},{3,2},{4,5},{5,4},{6,7},{7,6},{8,9},{9,8},{10,11... | collective-permute-start | bytes 294920 | tf_op jit(solution)/shard_map/ppermute | solution.py:700
  286.5 6.1 %collective-permute-start.40 = (bf16[32,3072]{1,0:T(8,128)(2,1)S(1)}, bf16[32,3072]{1,0:T(8,128)(2,1)S(1)}, u32[]{:S(2)}, u32[]{:S(2)}) collective-permute-start(bf16[32,3072]{1,0:T(8,128)(2,1)S(1)} %get-tuple-element.142.refs_0_), channel_id=1, source_target_pairs={{0,1},{1,0},{2,3},{3,2},{4,5},{5,4},{6,7},{7,6},{8,9},{9,8},{10,11... | collective-permute-start | bytes 589832 | tf_op jit(solution)/shard_map/ppermute | solution.py:700
  287.6 7.0 %collective-permute-start.42 = (bf16[32,3072]{1,0:T(8,128)(2,1)S(1)}, bf16[32,3072]{1,0:T(8,128)(2,1)S(1)}, u32[]{:S(2)}, u32[]{:S(2)}) collective-permute-start(bf16[32,3072]{1,0:T(8,128)(2,1)S(1)} %get-tuple-element.144.refs_2_), channel_id=1, source_target_pairs={{0,1},{1,0},{2,3},{3,2},{4,5},{5,4},{6,7},{7,6},{8,9},{9,8},{10,11... | collective-permute-start | bytes 589832 | tf_op jit(solution)/shard_map/ppermute | solution.py:700
  287.8 6.9 %collective-permute-start.43 = (bf16[32,3072]{1,0:T(8,128)(2,1)S(1)}, bf16[32,3072]{1,0:T(8,128)(2,1)S(1)}, u32[]{:S(2)}, u32[]{:S(2)}) collective-permute-start(bf16[32,3072]{1,0:T(8,128)(2,1)S(1)} %get-tuple-element.145.refs_3_), channel_id=1, source_target_pairs={{0,1},{1,0},{2,3},{3,2},{4,5},{5,4},{6,7},{7,6},{8,9},{9,8},{10,11... | collective-permute-start | bytes 589832 | tf_op jit(solution)/shard_map/ppermute | solution.py:700
  288.2 15.6 %collective-permute-start.36 = (bf16[32,2304]{1,0:T(8,128)(2,1)S(1)}, bf16[32,2304]{1,0:T(8,128)(2,1)S(1)}, u32[]{:S(2)}, u32[]{:S(2)}) collective-permute-start(bf16[32,2304]{1,0:T(8,128)(2,1)S(1)} %get-tuple-element.146.refs_0_), channel_id=1, source_target_pairs={{0,2},{1,3},{2,0},{3,1},{4,6},{5,7},{6,4},{7,5},{8,10},{9,11},{10,... | collective-permute-start | bytes 442376 | tf_op jit(solution)/shard_map/ppermute | solution.py:700
  292.6 11.7 %collective-permute-start.37 = (bf16[32,2304]{1,0:T(8,128)(2,1)S(1)}, bf16[32,2304]{1,0:T(8,128)(2,1)S(1)}, u32[]{:S(2)}, u32[]{:S(2)}) collective-permute-start(bf16[32,2304]{1,0:T(8,128)(2,1)S(1)} %get-tuple-element.147.refs_1_), channel_id=1, source_target_pairs={{0,2},{1,3},{2,0},{3,1},{4,6},{5,7},{6,4},{7,5},{8,10},{9,11},{10,... | collective-permute-start | bytes 442376 | tf_op jit(solution)/shard_map/ppermute | solution.py:700
  292.6 11.7 %collective-permute-start.38 = (bf16[32,2304]{1,0:T(8,128)(2,1)S(1)}, bf16[32,2304]{1,0:T(8,128)(2,1)S(1)}, u32[]{:S(2)}, u32[]{:S(2)}) collective-permute-start(bf16[32,2304]{1,0:T(8,128)(2,1)S(1)} %get-tuple-element.148.refs_2_), channel_id=1, source_target_pairs={{0,2},{1,3},{2,0},{3,1},{4,6},{5,7},{6,4},{7,5},{8,10},{9,11},{10,... | collective-permute-start | bytes 442376 | tf_op jit(solution)/shard_map/ppermute | solution.py:700
  294.6 9.2 %collective-permute-start.52 = (f32[2,768]{1,0:T(2,128)S(1)}, f32[2,768]{1,0:T(2,128)S(1)}, u32[]{:S(2)}, u32[]{:S(2)}) collective-permute-start(f32[2,768]{1,0:T(2,128)S(1)} %fusion.13), channel_id=1, source_target_pairs={{0,2},{1,3},{2,0},{3,1},{4,6},{5,7},{6,4},{7,5},{8,10},{9,11},{10,... | collective-permute-start | bytes 18440 | tf_op jit(solution)/shard_map/ppermute | solution.py:700
  294.7 10.9 %collective-permute-start.39 = (bf16[32,2304]{1,0:T(8,128)(2,1)S(1)}, bf16[32,2304]{1,0:T(8,128)(2,1)S(1)}, u32[]{:S(2)}, u32[]{:S(2)}) collective-permute-start(bf16[32,2304]{1,0:T(8,128)(2,1)S(1)} %get-tuple-element.149.refs_3_), channel_id=1, source_target_pairs={{0,2},{1,3},{2,0},{3,1},{4,6},{5,7},{6,4},{7,5},{8,10},{9,11},{10,... | collective-permute-start | bytes 442376 | tf_op jit(solution)/shard_map/ppermute | solution.py:700
  308.6 6.2 %collective-permute-start.55 = (bf16[32,2304]{1,0:T(8,128)(2,1)S(1)}, bf16[32,2304]{1,0:T(8,128)(2,1)S(1)}, u32[]{:S(2)}, u32[]{:S(2)}) collective-permute-start(bf16[32,2304]{1,0:T(8,128)(2,1)S(1)} %collective-permute-done.38.refs_10_), channel_id=1, source_target_pairs={{0,1},{1,0},{2,3},{3,2},{4,5},{5,4},{6,7},{7,6},{8,9},{9,8},{10,11... | collective-permute-start | bytes 442376 | tf_op jit(solution)/shard_map/ppermute | solution.py:700
  310.3 12.2 %collective-permute-start.67 = (bf16[72,768]{1,0:T(8,128)(2,1)S(1)}, bf16[72,768]{1,0:T(8,128)(2,1)S(1)}, u32[]{:S(2)}, u32[]{:S(2)}) collective-permute-start(bf16[72,768]{1,0:T(8,128)(2,1)S(1)} %get-tuple-element.175), channel_id=1, source_target_pairs={{0,4},{1,5},{2,6},{3,7},{4,0},{5,1},{6,2},{7,3},{8,12},{9,13},{10,... | collective-permute-start | bytes 331784 | tf_op jit(solution)/shard_map/ppermute | solution.py:700
  312.3 13.3 %collective-permute-start.68 = (bf16[72,768]{1,0:T(8,128)(2,1)S(1)}, bf16[72,768]{1,0:T(8,128)(2,1)S(1)}, u32[]{:S(2)}, u32[]{:S(2)}) collective-permute-start(bf16[72,768]{1,0:T(8,128)(2,1)S(1)} %get-tuple-element.176), channel_id=1, source_target_pairs={{0,8},{1,9},{2,10},{3,11},{4,12},{5,13},{6,14},{7,15},{8,0},{9,1},... | collective-permute-start | bytes 331784 | tf_op jit(solution)/shard_map/ppermute | solution.py:700
  312.5 13.1 %collective-permute-start.69 = (bf16[72,768]{1,0:T(8,128)(2,1)S(1)}, bf16[72,768]{1,0:T(8,128)(2,1)S(1)}, u32[]{:S(2)}, u32[]{:S(2)}) collective-permute-start(bf16[72,768]{1,0:T(8,128)(2,1)S(1)} %get-tuple-element.177), channel_id=1, source_target_pairs={{0,12},{1,13},{2,14},{3,15},{4,8},{5,9},{6,10},{7,11},{8,4},{9,5},... | collective-permute-start | bytes 331784 | tf_op jit(solution)/shard_map/ppermute | solution.py:700
  315.4 7.0 %collective-permute-start.70 = (f32[2,768]{1,0:T(2,128)S(1)}, f32[2,768]{1,0:T(2,128)S(1)}, u32[]{:S(2)}, u32[]{:S(2)}) collective-permute-start(f32[2,768]{1,0:T(2,128)S(1)} %fusion.14), channel_id=1, source_target_pairs={{0,4},{1,5},{2,6},{3,7},{4,0},{5,1},{6,2},{7,3},{8,12},{9,13},{10,... | collective-permute-start | bytes 18440 | tf_op jit(solution)/shard_map/ppermute | solution.py:700
  317.2 34.0 %collective-permute-start.60 = (bf16[48,3072]{1,0:T(8,128)(2,1)S(1)}, bf16[48,3072]{1,0:T(8,128)(2,1)S(1)}, u32[]{:S(2)}, u32[]{:S(2)}) collective-permute-start(bf16[48,3072]{1,0:T(8,128)(2,1)S(1)} %get-tuple-element.157), channel_id=1, source_target_pairs={{0,4},{1,5},{2,6},{3,7},{4,0},{5,1},{6,2},{7,3},{8,12},{9,13},{10,... | collective-permute-start | bytes 884744 | tf_op jit(solution)/shard_map/ppermute | solution.py:700
  322.5 29.5 %collective-permute-start.61 = (bf16[48,3072]{1,0:T(8,128)(2,1)S(1)}, bf16[48,3072]{1,0:T(8,128)(2,1)S(1)}, u32[]{:S(2)}, u32[]{:S(2)}) collective-permute-start(bf16[48,3072]{1,0:T(8,128)(2,1)S(1)} %get-tuple-element.158), channel_id=1, source_target_pairs={{0,8},{1,9},{2,10},{3,11},{4,12},{5,13},{6,14},{7,15},{8,0},{9,1},... | collective-permute-start | bytes 884744 | tf_op jit(solution)/shard_map/ppermute | solution.py:700
  322.5 29.5 %collective-permute-start.62 = (bf16[48,3072]{1,0:T(8,128)(2,1)S(1)}, bf16[48,3072]{1,0:T(8,128)(2,1)S(1)}, u32[]{:S(2)}, u32[]{:S(2)}) collective-permute-start(bf16[48,3072]{1,0:T(8,128)(2,1)S(1)} %get-tuple-element.159), channel_id=1, source_target_pairs={{0,12},{1,13},{2,14},{3,15},{4,8},{5,9},{6,10},{7,11},{8,4},{9,5},... | collective-permute-start | bytes 884744 | tf_op jit(solution)/shard_map/ppermute | solution.py:700
  325.5 25.1 %collective-permute-start.71 = (f32[2,768]{1,0:T(2,128)S(1)}, f32[2,768]{1,0:T(2,128)S(1)}, u32[]{:S(2)}, u32[]{:S(2)}) collective-permute-start(f32[2,768]{1,0:T(2,128)S(1)} %add.263), channel_id=1, source_target_pairs={{0,8},{1,9},{2,10},{3,11},{4,12},{5,13},{6,14},{7,15},{8,0},{9,1},... | collective-permute-start | bytes 18440 | tf_op jit(solution)/shard_map/ppermute | solution.py:700
  326.3 27.3 %collective-permute-start.57 = (bf16[48,2304]{1,0:T(8,128)(2,1)S(1)}, bf16[48,2304]{1,0:T(8,128)(2,1)S(1)}, u32[]{:S(2)}, u32[]{:S(2)}) collective-permute-start(bf16[48,2304]{1,0:T(8,128)(2,1)S(1)} %get-tuple-element.169), channel_id=1, source_target_pairs={{0,4},{1,5},{2,6},{3,7},{4,0},{5,1},{6,2},{7,3},{8,12},{9,13},{10,... | collective-permute-start | bytes 663560 | tf_op jit(solution)/shard_map/ppermute | solution.py:700
  350.6 14.3 %collective-permute-start.58 = (bf16[48,2304]{1,0:T(8,128)(2,1)S(1)}, bf16[48,2304]{1,0:T(8,128)(2,1)S(1)}, u32[]{:S(2)}, u32[]{:S(2)}) collective-permute-start(bf16[48,2304]{1,0:T(8,128)(2,1)S(1)} %get-tuple-element.170), channel_id=1, source_target_pairs={{0,8},{1,9},{2,10},{3,11},{4,12},{5,13},{6,14},{7,15},{8,0},{9,1},... | collective-permute-start | bytes 663560 | tf_op jit(solution)/shard_map/ppermute | solution.py:700
  351.2 13.7 %collective-permute-start.59 = (bf16[48,2304]{1,0:T(8,128)(2,1)S(1)}, bf16[48,2304]{1,0:T(8,128)(2,1)S(1)}, u32[]{:S(2)}, u32[]{:S(2)}) collective-permute-start(bf16[48,2304]{1,0:T(8,128)(2,1)S(1)} %get-tuple-element.171), channel_id=1, source_target_pairs={{0,12},{1,13},{2,14},{3,15},{4,8},{5,9},{6,10},{7,11},{8,4},{9,5},... | collective-permute-start | bytes 663560 | tf_op jit(solution)/shard_map/ppermute | solution.py:700
  (88 other events, 592.0 us)
Sparse Core Ops, SparseCore 0:
  12.9 85.5 all-gather.1

commit v5 on v4

--- a/solution.py
+++ b/solution.py
@@ -11,7 +11,7 @@
 HEAD_DIM = 64
 GROUP = 16
 HALF_WIN = 64
-CHUNKS = 4
+EXTRA = 16
 LANES = 128
 TILE = 256
 
@@ -325,6 +325,13 @@
     return jnp.concatenate([ref[...] for ref in refs], 0)
 
 
+def store_right(right_ref, d_gate_up, d_attn, d_mlp):
+    inner, width = d_gate_up.shape[1], d_attn.shape[1]
+    right_ref[:, :inner] = d_gate_up
+    right_ref[:, inner : inner + width] = d_attn
+    right_ref[:, inner + width :] = d_mlp
+
+
 def store_chunks(refs, rows):
     size = rows.shape[0] // len(refs)
     for i, ref in enumerate(refs):
@@ -351,19 +358,8 @@
     out_ref[:, columns:] = rows_scr[...].T[:shard].astype(BF)
 
 
-def local_project_body(place_ref, x_ref, table_ref, *refs):
-    pieces, (first_ref, extra_ref, normed_ref, q_ref, kv_ref, sem) = refs[:-6], refs[-6:]
-    rows = pieces[0].shape[0]
-    copies = []
-    for apart, piece in enumerate(pieces):
-        start = pl.multiple_of((place_ref[0] ^ apart) * rows, rows) if len(pieces) > 1 else 0
-        copies.append(
-            pltpu.make_async_copy(piece, first_ref.at[pl.ds(start, rows)], sem.at[apart])
-        )
-        copies[-1].start()
+def local_project_body(first_ref, x_ref, table_ref, extra_ref, normed_ref, q_ref, kv_ref):
     xhat, _ = moments(x_ref[...].astype(F32))
-    for copy in copies:
-        copy.wait()
     extra = first_ref[:, first_ref.shape[1] - LANES :].astype(F32).T
     extra_ref[...] = extra[: extra_ref.shape[0]]
     queries, keys, values = project(xhat, extra[:1], first_ref, table_ref, normed_ref)
@@ -436,20 +432,41 @@
             d_after_ref[here, part] = grads[2 * rows :].astype(BF)
 
 
-def local_join_body(lower_ref, dq_ref, own_ref, low_ref, high_ref, table_ref, other_ref, *out_refs):
+def local_finish_body(
+    lower_ref, first_ref, dq_ref, own_ref, low_ref, high_ref, table_ref, d_middle_ref, x_ref, gain_ref,
+    gain_mlp_ref, other_ref, other_attn_ref, other_mlp_ref, out_ref, grad_ref, gain_attn_ref, gain_scr,
+):
+    rows, width = dq_ref.shape
+
     @pl.when(lower_ref[0] == 1)
     def _():
         tables = [table_ref[i] for i in range(3)]
-        width = dq_ref.shape[1]
         total = own_ref[...] + low_ref[...].astype(F32) + high_ref[...].astype(F32)
-        keys = [unrotate(chunk, tables).astype(BF) for chunk in chunks_of(total[:, :width])]
-        store_chunks(
-            out_refs, jnp.concatenate([dq_ref[...]] + keys + [total[:, width:].astype(BF)], 1)
+        out_ref[:rows, :width] = dq_ref[...]
+        for j, chunk in enumerate(chunks_of(total[:, :width])):
+            start = width + LANES * j
+            out_ref[:rows, start : start + LANES] = unrotate(chunk, tables).astype(BF)
+        out_ref[:rows, 2 * width :] = total[:, width:].astype(BF)
+        grad_ref[...] = input_backward(
+            d_middle_ref[...], out_ref[:rows], x_ref[...].astype(F32), gain_ref, first_ref, gain_scr
         )
 
     @pl.when(lower_ref[0] == 0)
     def _():
-        store_chunks(out_refs, other_ref[...])
+        out_ref[:rows] = other_ref[...]
+        grad_ref[...] = jnp.zeros_like(grad_ref)
+        gain_scr[...] = other_attn_ref[...]
+
+    gain_attn_ref[...] = gain_scr[...]
+    gain_mlp = jnp.where(lower_ref[0] == 1, gain_mlp_ref[...], other_mlp_ref[...])
+    index = lax.broadcasted_iota(jnp.int32, (EXTRA, width), 0)
+    tail = jnp.zeros((EXTRA, width), F32)
+    for row, gain in ((0, gain_scr[...]), (2, gain_mlp)):
+        high = gain.astype(BF).astype(F32)
+        tail = jnp.where(index == row, high, tail)
+        tail = jnp.where(index == row + 1, gain - high, tail)
+    out_ref[rows:] = jnp.zeros((EXTRA, out_ref.shape[1]), BF)
+    out_ref[rows:, :width] = tail.astype(BF)
 
 
 def local_middle_body(*refs):
@@ -469,15 +486,14 @@
 
 
 def local_back_middle_body(*refs):
-    count = 11 + CHUNKS
-    sources, refs = refs[:-count], refs[-count:]
+    sources, refs = refs[:-12], refs[-12:]
     lower_ref, low_ref, high_ref, middle_ref, gate_up_ref, gain_ref, other_ref = refs[:7]
-    gain_out_ref, d_middle_ref, d_att_ref = refs[7:10]
-    chunk_refs = refs[10 : 10 + CHUNKS]
-    weights = Weights(sources, refs[10 + CHUNKS])
+    gain_out_ref, d_middle_ref, d_att_ref, right_ref = refs[7:11]
+    weights = Weights(sources, refs[11])
     half = gate_up_ref.shape[1] // 2
+    upstream = joined([low_ref, high_ref])
     d_gate_up, gain_grad, d_middle, d_attn, d_attended = mlp_backward(
-        joined([low_ref, high_ref]), middle_ref[...], gate_up_ref[:, :half], gate_up_ref[:, half:],
+        upstream, middle_ref[...], gate_up_ref[:, :half], gate_up_ref[:, half:],
         gain_ref[...], weights,
     )
     gain_out_ref[...] = gain_grad
@@ -486,19 +502,11 @@
 
     @pl.when(lower_ref[0] == 1)
     def _():
-        store_chunks(chunk_refs, jnp.concatenate([d_gate_up, d_attn], 1))
+        store_right(right_ref, d_gate_up, d_attn, upstream)
 
     @pl.when(lower_ref[0] == 0)
     def _():
-        store_chunks(chunk_refs, other_ref[...])
-
-
-def input_backward_body(first_ref, d_middle_ref, x_ref, gain_ref, *refs):
-    d_proj_refs, (grad_ref, gain_out_ref) = refs[:-2], refs[-2:]
-    x = x_ref[...].astype(F32)
-    grad_ref[...] = input_backward(
-        d_middle_ref[...], joined(d_proj_refs), x, gain_ref, first_ref, gain_out_ref
-    )
+        right_ref[...] = other_ref[...]
 
 
 def global_project_body(first_ref, low_ref, high_ref, gain_ref, table_ref, normed_ref, sent_ref):
@@ -653,8 +661,7 @@
     d_gate_up, gain_grad, d_middle, d_attn, d_attended = mlp_backward(
         up_ref[...], middle, gate, up, gain, weights
     )
-    right_ref[:, : d_gate_up.shape[1]] = d_gate_up
-    right_ref[:, d_gate_up.shape[1] :] = d_attn
+    store_right(right_ref, d_gate_up, d_attn, up_ref[...])
     gain_out_ref[...] = gain_grad
     d_middle_ref[...] = d_middle
     pack_folded(chunks_of(d_attended), sent_ref, 0)
@@ -700,24 +707,22 @@
     return lax.ppermute(rows, "dp", [(i, i ^ apart) for i in range(count)])
 
 
-def group_pieces(piece, count):
-    pieces = [piece]
-    pieces += lax.optimization_barrier([partner(piece, apart, count) for apart in (4, 8, 12)])
-    pieces += lax.optimization_barrier([partner(item, 2, count) for item in pieces])
-    pieces += [partner(item, 1, count) for item in pieces]
-    return [pieces[apart % 2 * 8 + apart // 2 % 2 * 4 + apart // 4] for apart in range(GROUP)]
-
-
-def in_order(pieces, group_pos, count):
-    shape = pieces[0].shape
-    whole = jnp.zeros((GROUP,) + shape, pieces[0].dtype)
-    for apart, item in enumerate(pieces):
-        start = (group_pos ^ apart,) + (0,) * len(shape)
+def gather_rows(piece, group_pos, count):
+    pieces = {0: piece}
+    for apart in (4, 8, 12):
+        pieces[apart] = partner(piece, apart, count)
+    for apart in (0, 4, 8, 12):
+        pieces[apart + 2] = partner(pieces[apart], 2, count)
+    for apart in range(0, GROUP, 2):
+        pieces[apart + 1] = partner(pieces[apart], 1, count)
+    whole = jnp.zeros((GROUP,) + piece.shape, piece.dtype)
+    for apart, item in pieces.items():
+        start = (group_pos ^ apart,) + (0,) * piece.ndim
         whole = lax.dynamic_update_slice(whole, item[None], start)
     if count > GROUP:
         groups = [list(range(s, count, GROUP)) for s in range(GROUP)]
         whole = lax.all_gather(whole, "dp", axis=0, tiled=True, axis_index_groups=groups)
-    return whole.reshape(-1, shape[-1])
+    return whole.reshape(-1, piece.shape[-1]), pieces[2]
 
 
 def plane_rows(rows, group_pos, count):
@@ -733,25 +738,67 @@
     return taken
 
 
-def product_body(ranges, *refs):
+def early_body(shard, *refs):
     refs, outs = refs[:-4], refs[-4:]
-    rights = refs[: len(refs) - 4 * len(ranges)]
+    rights, n2, mixed, att = (refs[4 * i : 4 * i + 4] for i in range(4))
+    width = outs[0].shape[1]
+    inner = rights[0].shape[1] - 2 * width
+
+    def product(lefts, start, end):
+        left = jnp.concatenate([ref[...] for ref in lefts], 1)
+        return dot(left, jnp.concatenate([ref[:, start:end] for ref in rights], 0))
+
+    base = 0
+    for lefts, start, end in (
+        (n2, 0, inner),
+        (mixed, inner + width, inner + 2 * width),
+        (att, inner, inner + width),
+    ):
+        result = product(lefts, start, end)
+        rows = result.shape[0] // 4
+        for column in range(0, end - start, width):
+            for plane, out_ref in enumerate(outs):
+                part = result[plane * rows : (plane + 1) * rows, column : column + width]
+                out_ref[base : base + rows] = part.astype(out_ref.dtype)
+            base += rows
+
+
+def late_body(place_ref, *refs):
+    refs, (outs, scr) = refs[:-5], (refs[-5:-1], refs[-1])
+    rights, lefts = refs[:4], refs[4:]
+    tokens = lefts[0].shape[1]
+    columns = rights[0].shape[1]
+    width = columns // 3
     rows = outs[0].shape[0]
-    for index, (start, end) in enumerate(ranges):
-        left = jnp.concatenate([ref[...] for ref in refs[len(rights) + 4 * index :][:4]], 1)
-        right = jnp.concatenate([ref[:, start:end] for ref in rights], 0)
-        product = dot(left, right)
-        for plane, out_ref in enumerate(outs):
-            part = product[plane * rows : (plane + 1) * rows]
-            out_ref[:, start:end] = part.astype(out_ref.dtype)
-
-
-def plane_product(right, terms):
-    planes, groups, rows, tokens = terms[0][0][0].shape
-    args = list(right) + [item.reshape(-1, tokens) for lefts, _, _ in terms for item in lefts]
-    shape = (groups * rows, right[0].shape[1])
-    body = functools.partial(product_body, [term[1:] for term in terms])
-    return on_core(body, [(shape, F32)] + [(shape, BF)] * (planes - 1), args)
+    left = jnp.concatenate([ref[...] for ref in lefts], 1)
+    product = dot(left, jnp.concatenate([ref[:tokens] for ref in rights], 0))
+    tail = sum(ref[tokens:, :width].astype(F32) for ref in rights)
+    both = jnp.concatenate([tail, jnp.zeros((LANES - EXTRA, width), F32)], 0).T
+    lane = lax.broadcasted_iota(jnp.int32, (1, LANES), 1)
+    lows = pltpu.roll(both, LANES - 1, 1)
+    scr[...] = jnp.where(lane % 2 == 0, both + lows, 0.0)
+    for plane, out_ref in enumerate(outs):
+        part = product[plane * rows : (plane + 1) * rows]
+        out_ref[:, :columns] = part.astype(out_ref.dtype)
+        d = (place_ref[0] // 4 ^ plane) * 4 + place_ref[0] % 4
+        start = pl.multiple_of(d * rows, 16)
+        out_ref[:, columns:] = scr[pl.ds(start, rows)].astype(out_ref.dtype)
+
+
+def flat_rows(parts):
+    return [part.reshape(-1, part.shape[-1]) for part in parts]
+
+
+def four_planes(shape):
+    return [(shape, F32)] + [(shape, BF)] * 3
+
+
+def plane_parts(rows, count, after=None):
+    across = partner(rows, 2, count)
+    beside = partner(rows, 1, count)
+    if after is not None:
+        across, _ = lax.optimization_barrier((across, after))
+    return [rows, beside, across, partner(across, 1, count)]
 
 
 def sum_planes(blocks, count):
@@ -759,11 +806,15 @@
     total = blocks[0]
     for item in got:
         total = total + item.astype(F32)
-    if count > GROUP:
-        apart = [list(range(s, count, GROUP)) for s in range(GROUP)]
-        total = total.reshape(count // GROUP, -1, total.shape[1])
-        return lax.psum_scatter(total, "dp", scatter_dimension=0, axis_index_groups=apart)
     return total
+
+
+def over_groups(rows, count):
+    if count == GROUP:
+        return rows
+    apart = [list(range(s, count, GROUP)) for s in range(GROUP)]
+    rows = rows.reshape(count // GROUP, -1, rows.shape[1])
+    return lax.psum_scatter(rows, "dp", scatter_dimension=0, axis_index_groups=apart)
 
 
 def on_device(
@@ -779,6 +830,8 @@
 ):
     lower = lax.axis_index("section") == 0
     lower_flag = lower.astype(jnp.int32)[None]
+    shard_total = qkv_weight.shape[1] * (lax.axis_size("dp") // GROUP)
+    hidden_total = mlp_out_weight.shape[1] * (lax.axis_size("dp") // GROUP)
     count = lax.axis_size("dp")
     replica = lax.axis_index("dp")
     group_pos = replica % GROUP
@@ -791,6 +844,7 @@
         (qkv_weight[0], attn_gain, mlp_gain, segment_ids),
         [pltpu.VMEM((LANES, LANES), F32), pltpu.VMEM((8, LANES), F32)],
     )
+    first, early_piece = gather_rows(message, group_pos, count)
     inner = mlp_in_weight.shape[2]
     hidden = mlp_out_weight.shape[1] * count
     if count == GROUP:
@@ -809,16 +863,13 @@
             (),
             [pltpu.SMEM] + [pltpu.VMEM] * 4,
         )
+        stacked, _ = lax.optimization_barrier((stacked, early_piece))
         others = [lax.all_gather(stacked, "dp", axis=0, tiled=True)]
     else:
         others = [
             lax.all_gather(item[0], "dp", axis=0, tiled=True)
             for item in (attn_out_weight, mlp_in_weight, mlp_out_weight)
         ]
-    pieces = group_pieces(message, count)
-    if count > GROUP:
-        pieces = [in_order(pieces, group_pos, count)]
-
     positions = group_pos * row_count + jnp.arange(row_count)
     local_tables = angles(positions, local_log_base)
     global_tables = angles(positions, global_log_base)
@@ -827,18 +878,15 @@
     pairs = rows * width // (row_count * LANES)
     in_0 = tokens_in.reshape(rows, width)
     extra_rows = -(-(2 + micro_count * runs) // 8) * 8
-    first, extra, normed_0, q_0, kv_0 = on_core(
+    extra, normed_0, q_0, kv_0 = on_core(
         local_project_body,
         [
-            ((width, 3 * width + LANES), BF),
             ((extra_rows, width), F32),
             ((rows, width), BF),
             ((rows, width), BF),
             ((rows, 2 * width), BF),
         ],
-        (group_pos[None], in_0, local_tables, *pieces),
-        [pltpu.SemaphoreType.DMA((len(pieces),))],
-        [pltpu.SMEM, pltpu.VMEM, pltpu.VMEM] + [pl.ANY] * len(pieces),
+        (first, in_0, local_tables),
     )
     gain_attn, gain_mlp = extra[:1], extra[1:2]
     all_ids = extra[2 : 2 + micro_count * runs].reshape(micro_count, runs, count, shard)
@@ -922,7 +970,7 @@
             ((rows, width), BF),
             ((rows, width), BF),
             ((rows, hidden), BF),
-            ((rows, inner + width), BF),
+            ((rows, inner + 2 * width), BF),
             ((1, width), F32),
             ((rows, width), F32),
             ((GROUP, fold, LANES), BF),
@@ -967,8 +1015,8 @@
         )
     )
     left = jnp.concatenate([n1, att, n2, mixed], 1)
+    left = plane_rows(left, group_pos, count)
     left, got = lax.optimization_barrier((left, got))
-    left = plane_rows(left, group_pos, count)
     n1, att, n2, mixed = (
         [part[:, :, start:end] for part in left]
         for start, end in (
@@ -985,22 +1033,19 @@
     )
 
     up_0 = to_other_section(grad_1, -1)
-    d_mlp = [
-        jnp.where(lower, a, up_1[i * row_count : (i + 1) * row_count]) for i, a in enumerate(up_0)
-    ]
-    across_mlp = [partner(item, 2, count) for item in d_mlp]
-    beside_mlp = [partner(item, 1, count) for item in d_mlp]
-    chunk = rows // CHUNKS
-    gain_mlp_0, d_mid_0, d_att_0, *right = on_core(
+    gain_mlp_0, d_mid_0, d_att_0, right = on_core(
         local_back_middle_body,
-        [((1, width), F32), ((rows, width), F32), ((rows, width), BF)]
-        + [((chunk, inner + width), BF)] * CHUNKS,
+        [
+            ((1, width), F32),
+            ((rows, width), F32),
+            ((rows, width), BF),
+            ((rows, inner + 2 * width), BF),
+        ],
         (*others, lower_flag, *up_0, middle_0, gate_up_0, gain_mlp, right_1),
         [pltpu.VMEM((hidden, width), BF)],
         [pltpu.VMEM] * len(others) + [pltpu.SMEM] + [pltpu.VMEM] * 6,
     )
-    across = [partner(item, 2, count) for item in right]
-    beside = [partner(item, 1, count) for item in right]
+    right = plane_parts(right, count)
     dq_0, d_own, d_before, d_after = on_core(
         local_backward_body,
         [
@@ -1013,51 +1058,56 @@
     )
     from_after = lax.ppermute(d_before, "dp", down_pairs)
     from_before = lax.ppermute(d_after, "dp", up_pairs)
-    from_after, across_mlp = lax.optimization_barrier((from_after, across_mlp))
-    d_proj = on_core(
-        local_join_body,
-        [((chunk, 3 * width), BF)] * CHUNKS,
-        (lower_flag, dq_0, d_own, from_after, from_before, local_tables, d_proj_1),
-        (),
-        [pltpu.SMEM] + [pltpu.VMEM] * 6,
-    )
-    d_mlp += beside_mlp + across_mlp + [partner(item, 1, count) for item in across_mlp]
-    mlp_out_share = sum_planes(plane_product(d_mlp, [(mixed, 0, width)]), count)
-    d_proj, across = lax.optimization_barrier((list(d_proj), across))
-    right = right + beside + across + [partner(item, 1, count) for item in across]
-    in_blocks = plane_product(right, [(n2, 0, inner), (att, inner, inner + width)])
-    in_share = sum_planes(in_blocks, count)
-    grad_0, gain_attn_0 = on_core(
-        input_backward_body,
-        [((rows, width), BF), ((1, width), F32)],
-        (first, d_mid_0, in_0, gain_attn, *d_proj),
-    )
-    gains = jnp.where(
-        lower,
-        jnp.concatenate([gain_attn_0, gain_mlp_0]),
-        jnp.concatenate([gain_attn_1, gain_mlp_1]),
-    )
-    gains = gains + partner(gains, 1, count)
-    gains = gains + partner(gains, 2, count)
-    across = [partner(item, 2, count) for item in d_proj]
-    across, in_blocks, gains = lax.optimization_barrier((across, in_blocks, gains))
-    beside = [partner(item, 1, count) for item in d_proj]
-    d_proj = d_proj + beside + across + [partner(item, 1, count) for item in across]
-    qkv_blocks = plane_product(d_proj, [(n1, 0, 3 * width)])
-    qkv_share = sum_planes(qkv_blocks, count)
-    gains, _ = lax.optimization_barrier((gains, qkv_blocks))
-    apart = 4
-    while apart < count:
-        gains = gains + partner(gains, apart, count)
-        apart *= 2
-    gains = lax.dynamic_slice_in_dim(gains, replica * shard, shard, 1)
+    d_proj, grad_0, gain_attn_sum = on_core(
+        local_finish_body,
+        [((rows + EXTRA, 3 * width), BF), ((rows, width), BF), ((1, width), F32)],
+        (
+            lower_flag, first, dq_0, d_own, from_after, from_before, local_tables, d_mid_0, in_0, gain_attn,
+            gain_mlp_0, d_proj_1, gain_attn_1, gain_mlp_1,
+        ),
+        [pltpu.VMEM((1, width), F32)],
+        [pltpu.SMEM] + [pltpu.VMEM] * 13,
+    )
+    early_rows = shard_total * (inner // width + 1) + hidden_total
+    early = on_core(
+        functools.partial(early_body, shard),
+        four_planes((early_rows, width)),
+        (*right, *flat_rows(n2), *flat_rows(mixed), *flat_rows(att)),
+    )
+    d_proj = plane_parts(d_proj, count, early)
+    early = sum_planes(early, count)
+    late_in = (group_pos[None], *d_proj, *flat_rows(n1))
+    late = on_core(
+        late_body,
+        four_planes((shard_total, 3 * width + LANES)),
+        late_in,
+        [pltpu.VMEM((width, LANES), F32)],
+        [pltpu.SMEM] + [pltpu.VMEM] * (len(late_in) - 1),
+    )
+    late = sum_planes(late, count)
+    parts = [early[p * shard_total : (p + 1) * shard_total] for p in range(inner // width)]
+    start = shard_total * (inner // width)
+    in_share = jnp.concatenate(parts, 1)
+    mlp_out_share = early[start : start + hidden_total]
+    attn_share = early[start + hidden_total :]
+    gain_columns = late[:, 3 * width :]
+    qkv_share, in_share, mlp_out_share, attn_share, gain_columns = (
+        over_groups(item, count)
+        for item in (late[:, : 3 * width], in_share, mlp_out_share, attn_share, gain_columns)
+    )
+    if count == GROUP:
+        gains = jnp.stack([gain_columns[:, 0], gain_columns[:, 2]])
+    else:
+        gain_mlp_sum = jnp.where(lower, gain_mlp_0, gain_mlp_1)
+        gains = lax.psum(jnp.concatenate([gain_attn_sum, gain_mlp_sum]), "dp")
+        gains = lax.dynamic_slice_in_dim(gains, replica * shard, shard, 1)
 
     return (
         jnp.where(lower, jnp.concatenate(out_0), out_1).reshape(1, micro_count, row_count, width),
         jnp.where(lower, grad_0, jnp.concatenate(grad_1)).reshape(1, micro_count, row_count, width),
         qkv_share[None],
-        in_share[None, :, inner:],
-        in_share[None, :, :inner],
+        attn_share[None],
+        in_share[None],
         mlp_out_share[None],
         gains[:1],
         gains[1:],

time: 376 us -> 362 us (0.963)
  starting transfers between devices: 88.9 us -> 64.4 us
  blocking collectives: 53.2 us -> 32.1 us
  local copies, waits for them, and re-layouts: 28 us -> 49 us
  waiting for transfers between devices: 125 us -> 131 us
    ppermute x64 -> x33, starting transfers between devices: 69.2 us -> 40.7 us  [partner(): return lax.ppermute(rows, 'dp', [(i, i ^ apart) for i in range(count)])]
    all_to_all x3 -> x2, blocking collectives: 53.2 us -> 32.1 us  [exchange(): return lax.all_to_all(blocks, 'dp', 0, 0, axis_index_groups=groups)]
    all_gather x1, waiting for transfers between devices: 0.02 us -> 21 us  [on_device(): others = [lax.all_gather(stacked, 'dp', axis=0, tiled=True)]]
    ppermute x64 -> x33, waiting for transfers between devices: 108 us -> 93.5 us  [partner(): return lax.ppermute(rows, 'dp', [(i, i ^ apart) for i in range(count)])]
    dynamic_update_slice x0 -> x16, local copies, waits for them, and re-layouts: none -> 11.4 us  [gather_rows(): whole = lax.dynamic_update_slice(whole, item[None], start)]
    unnamed x124 -> x118, local copies, waits for them, and re-layouts: 16.7 us -> 23.1 us
    all_to_all x1 -> x2, starting transfers between devices: 3.71 us -> 7.76 us  [exchange(): return lax.all_to_all(blocks, 'dp', 0, 0, axis_index_groups=groups)]
    pallas_call x17 -> x15, Pallas kernels: 53 us -> 56.5 us  [on_core(): pl.pallas_call(body, out_shape=[jax.ShapeDtypeStruct(shape, dtype) for sh...]
  transfers between devices with their start and end apart: 74 -> 44, of which waited for: 22 -> 23; matrix products, arithmetic and copies ran while one was open for 4% -> 9% of each run, Pallas kernels for 4% -> 5%
where the time goes in v5:
time: 362 us; the launch traced here: 359 us
  waiting for transfers between devices  131 us (36%)
  starting transfers between devices  64.4 us (18%)
  Pallas kernels  56.5 us (16%)
  local copies, waits for them, and re-layouts  49 us (14%)
  blocking collectives  32.1 us (9%)
  between operations  15.2 us (4%)
  other arithmetic  10.6 us (3%)
    ppermute x33, waiting for transfers between devices, partner(): return lax.ppermute(rows, 'dp', [(i, i ^ apart) for i in range(count)])  93.5 us
    pallas_call x15, Pallas kernels, on_core(): pl.pallas_call(body, out_shape=[jax.ShapeDtypeStruct(shape, dtype) for sh...  56.5 us
    ppermute x33, starting transfers between devices, partner(): return lax.ppermute(rows, 'dp', [(i, i ^ apart) for i in range(count)])  40.7 us
    all_to_all x2, blocking collectives, exchange(): return lax.all_to_all(blocks, 'dp', 0, 0, axis_index_groups=groups)  32.1 us
    unnamed x118, local copies, waits for them, and re-layouts  23.1 us
    all_gather x1, waiting for transfers between devices, on_device(): others = [lax.all_gather(stacked, 'dp', axis=0, tiled=True)]  21 us
    dynamic_update_slice x16, local copies, waits for them, and re-layouts, gather_rows(): whole = lax.dynamic_update_slice(whole, item[None], start)  11.4 us
    ppermute x4, waiting for transfers between devices, to_other_section(): return [lax.ppermute(rows, 'section', pairs) for rows in chunks]  9.23 us
  transfers between devices with their start and end apart: 44, of which 23 were waited for; matrix products, arithmetic and copies ran while one was open for 9% of the time, Pallas kernels for 5%

profile of v5, /device:TPU:0, one launch (start us, length us, event | category | flops | bytes accessed | tf_op | source)
XLA Modules:
  0.0 358.9 jit_solution(6884245785674333146)
XLA Ops:
  10.8 4.7 %collective-permute-start.4 = (bf16[48,2432]{1,0:T(8,128)(2,1)S(1)}, bf16[48,2432]{1,0:T(8,128)(2,1)S(1)}, u32[]{:S(2)}, u32[]{:S(2)}) collective-permute-start(bf16[48,2432]{1,0:T(8,128)(2,1)S(1)} %shard_map.153), channel_id=1, source_target_pairs={{0,12},{1,13},{2,14},{3,15},{4,8},{5,9},{6,10},{7,11},{8,4},{9,5},... | collective-permute-start | bytes 700424 | tf_op jit(solution)/shard_map/ppermute | solution.py:707
  15.5 1.5 collective-permute-start.1
  23.5 2.1 broadcast_in_dim.104
  26.9 1.5 collective-permute-start.7
  28.5 7.7 %collective-permute-done.3 = bf16[48,2432]{1,0:T(8,128)(2,1)S(1)} collective-permute-done((bf16[48,2432]{1,0:T(8,128)(2,1)S(1)}, bf16[48,2432]{1,0:T(8,128)(2,1)S(1)}, u32[]{:S(2)}, u32[]{:S(2)}) %collective-permute-start.3) | collective-permute-done | bytes 233504 | tf_op jit(solution)/shard_map/ppermute | solution.py:707
  36.2 1.7 collective-permute-start.5
  40.7 3.8 %collective-permute-done.5 = bf16[48,2432]{1,0:T(8,128)(2,1)S(1)} collective-permute-done((bf16[48,2432]{1,0:T(8,128)(2,1)S(1)}, bf16[48,2432]{1,0:T(8,128)(2,1)S(1)}, u32[]{:S(2)}, u32[]{:S(2)}) %collective-permute-start.5) | collective-permute-done | bytes 233504 | tf_op jit(solution)/shard_map/ppermute | solution.py:707
  46.7 5.3 %collective-permute-done.6 = bf16[48,2432]{1,0:T(8,128)(2,1)S(1)} collective-permute-done((bf16[48,2432]{1,0:T(8,128)(2,1)S(1)}, bf16[48,2432]{1,0:T(8,128)(2,1)S(1)}, u32[]{:S(2)}, u32[]{:S(2)}) %collective-permute-start.6) | collective-permute-done | bytes 233504 | tf_op jit(solution)/shard_map/ppermute | solution.py:707
  61.3 3.1 shard_map.154
  66.4 3.1 collective-permute-start.16
  70.7 3.6 %shard_map.155 = (bf16[128,768]{1,0:T(8,128)(2,1)S(1)}, f32[12,1,128]{2,1,0:T(1,128)S(1)}) custom-call(bf16[128,768]{1,0:T(8,128)(2,1)S(1)} %get-tuple-element.64.q_ref, bf16[128,1536]{1,0:T(8,128)(2,1)S(1)} %collective-permute-done.16.before_ref, bf16[128,1536]{1,0:T(8,128)(2,1)S(1)} %get-tuple-element.65.own_ref, ...), custom_call_target="tpu_custom_call" | custom-call | flops 1024 | bytes 1024 | tf_op jit(solution)/shard_map/pallas_call | solution.py:65
  74.4 21.0 %all-gather.2.cloned.1.call-done.refs_0_ = bf16[768,4352]{1,0:T(8,128)(2,1)} async-done(((bf16[48,4352]{1,0:T(8,128)(2,1)}), bf16[768,4352]{1,0:T(8,128)(2,1)}) %all-gather.2.cloned.1.call-update) | async-done | bytes 6684688 | tf_op jit(solution)/shard_map/all_gather | solution.py:867
  95.4 4.4 %shard_map.156 = (bf16[128,768]{1,0:T(8,128)(2,1)S(1)}, bf16[128,1152]{1,0:T(8,128)(2,1)S(1)}, f32[128,768]{1,0:T(8,128)S(1)}, f32[128,2304]{1,0:T(8,128)S(1)}, ...) custom-call(bf16[768,4352]{1,0:T(8,128)(2,1)} %all-gather.2.cloned.1.call-done.refs_0_, ...), custom_call_target="tpu_custom_call" | custom-call | flops 1024 | bytes 1024 | tf_op jit(solution)/shard_map/pallas_call | solution.py:65
  102.3 3.4 collective-permute-start.18
  110.3 3.2 shard_map.157
  113.5 20.3 %all_to_all.20.got_ref = bf16[16,144,128]{2,1,0:T(8,128)(2,1)S(1)} all-to-all(bf16[16,144,128]{2,1,0:T(8,128)(2,1)S(1)} %get-tuple-element.70), channel_id=1, replica_groups={{0,1,2,3,4,5,6,7,8,9,10,11,12,13,14,15},{16,17,18,19,20,21,22,23,24,25,..., dimensions={0} | all-to-all | bytes 1179648 | tf_op jit(solution)/shard_map/all_to_all | solution.py:698
  136.3 6.0 %shard_map.158 = (bf16[16,48,128]{2,1,0:T(8,128)(2,1)S(1)}, f32[6,1,256]{2,1,0:T(1,128)S(1)}) custom-call(bf16[16,144,128]{2,1,0:T(8,128)(2,1)S(1)} %all_to_all.20.got_ref, bf16[16,64,128]{2,1,0:T(8,128)(2,1)S(1)} %collective-permute-done.20.other_ref, s32[1024,1]{1,0:T(8,128)S(1)} %copy.35.own_seg_ref, s32[1024,1]{1,0:T(8,128)S(1)} %copy.36.shared_seg_ref), custom_call_target="tpu_custom_call" | custom-call | flops 1024 | bytes 1024 | tf_op jit(solution)/shard_map/pallas_call | solution.py:65
  142.3 11.8 %all_to_all.21.refs_1_ = bf16[16,48,128]{2,1,0:T(8,128)(2,1)S(1)} all-to-all(bf16[16,48,128]{2,1,0:T(8,128)(2,1)S(1)} %get-tuple-element.71), channel_id=1, replica_groups={{0,1,2,3,4,5,6,7,8,9,10,11,12,13,14,15},{16,17,18,19,20,21,22,23,24,25,..., dimensions={0} | all-to-all | bytes 393216 | tf_op jit(solution)/shard_map/all_to_all | solution.py:698
  156.8 7.0 %shard_map.159 = (bf16[128,768]{1,0:T(8,128)(2,1)S(1)}, bf16[128,768]{1,0:T(8,128)(2,1)S(1)}, bf16[128,768]{1,0:T(8,128)(2,1)S(1)}, bf16[128,1152]{1,0:T(8,128)(...) custom-call(bf16[768,4352]{1,0:T(8,128)(2,1)} %all-gather.2.cloned.1, ...), custom_call_target="tpu_custom_call" | custom-call | flops 1024 | bytes 1024 | tf_op jit(solution)/shard_map/pallas_call | solution.py:65
  169.0 4.2 %all-to-all-start.2 = ((bf16[16,48,128]{2,1,0:T(8,128)(2,1)}), bf16[16,48,128]{2,1,0:T(8,128)(2,1)}, u32[]{:S(2)}, u32[]{:S(2)}) async-start(bf16[16,48,128]{2,1,0:T(8,128)(2,1)} %copy-done.27), calls=%async_computation.2 | async-start | bytes 393216 | tf_op jit(solution)/shard_map/all_to_all | solution.py:698
  173.4 1.6 select_bitcast_fusion.3
  175.0 1.7 copy.37
  176.7 5.5 %all-to-all-done.2.d_ref = bf16[16,48,128]{2,1,0:T(8,128)(2,1)} async-done(((bf16[16,48,128]{2,1,0:T(8,128)(2,1)}), bf16[16,48,128]{2,1,0:T(8,128)(2,1)}, u32[]{:S(2)}, u32[]{:S(2)}) %all-to-all-start.2) | async-done | bytes 196640 | tf_op jit(solution)/shard_map/all_to_all | solution.py:698
  182.2 8.2 %shard_map.160 = (bf16[16,144,128]{2,1,0:T(8,128)(2,1)S(1)}, bf16[16,64,128]{2,1,0:T(8,128)(2,1)S(1)}) custom-call(bf16[16,144,128]{2,1,0:T(8,128)(2,1)S(1)} %all_to_all.20.got_ref, bf16[16,64,128]{2,1,0:T(8,128)(2,1)S(1)} %collective-permute-done.20.other_ref, s32[1024,1]{1,0:T(8,128)S(1)} %copy.35.own_seg_ref, s32[1024,1]{1,0:T(8,128)S(1)} %copy.36.shared_seg_ref, ...), custom_call_target="tpu_custom_call" | custom-call | flops 1024 | bytes 1024 | tf_op jit(solution)/shard_map/pallas_call | solution.py:65
  190.6 1.9 select_bitcast_fusion
  193.6 3.6 all-to-all-start.3
  197.3 1.9 copy.40
  201.9 1.8 collective-permute-start.22
  204.5 8.0 %collective-permute-done.22 = bf16[4,1,216,128]{3,2,0,1:T(8,128)(2,1)S(1)} collective-permute-done((bf16[4,1,216,128]{3,2,0,1:T(8,128)(2,1)S(1)}, bf16[4,1,216,128]{3,2,0,1:T(8,128)(2,1)S(1)}, u32[]{:S(2)}, u32[]{:S(2)}) %collective-permute-start.22) | collective-permute-done | bytes 221216 | tf_op jit(solution)/shard_map/ppermute | solution.py:707
  213.2 3.8 %collective-permute-done.23 = bf16[4,1,216,128]{3,2,0,1:T(8,128)(2,1)} collective-permute-done((bf16[4,1,216,128]{3,2,0,1:T(8,128)(2,1)S(1)}, bf16[4,1,216,128]{3,2,0,1:T(8,128)(2,1)}, u32[]{:S(2)}, u32[]{:S(2)}) %collective-permute-start.23) | collective-permute-done | bytes 221216 | tf_op jit(solution)/shard_map/ppermute | solution.py:707
  218.0 3.6 %shard_map.161 = (bf16[128,2304]{1,0:T(8,128)(2,1)S(1)}, f32[1,768]{1,0:T(1,128)S(1)}, bf16[64,768]{1,0:T(8,128)(2,1)S(1)}, bf16[64,768]{1,0:T(8,128)(2,1)S(1)}) custom-call(bf16[768,2432]{1,0:T(8,128)(2,1)} %bitcast.23.first_ref, bf16[16,144,128]{2,1,0:T(8,128)(2,1)S(1)} %all-to-all-done.3.got_ref, f32[128,768]{1,0:T(8,128)S(1)} %copy-done.22, ...), custom_call_target="tpu_custom_call" | custom-call | flops 1024 | bytes 1024 | tf_op jit(solution)/shard_map/pallas_call | solution.py:65
  225.6 4.9 %collective-permute-done.25.refs_2_ = bf16[64,768]{1,0:T(8,128)(2,1)S(1)} collective-permute-done((bf16[64,768]{1,0:T(8,128)(2,1)S(1)}, bf16[64,768]{1,0:T(8,128)(2,1)S(1)}, u32[]{:S(2)}, u32[]{:S(2)}) %collective-permute-start.25) | collective-permute-done | bytes 98336 | tf_op jit(solution)/shard_map/ppermute | solution.py:703
  234.3 6.1 %shard_map.162 = (f32[1,768]{1,0:T(1,128)S(1)}, f32[128,768]{1,0:T(8,128)S(1)}, bf16[128,768]{1,0:T(8,128)(2,1)S(1)}, bf16[128,3840]{1,0:T(8,128)(2,1)S(1)}) custom-call(bf16[768,4352]{1,0:T(8,128)(2,1)} %all-gather.2.cloned.1.call-done.refs_0_, s32[1]{0:T(128)} %bitcast.37.refs_1_.lower_ref, bf16[64,768]{1,0:T(8,128)(2,1)S(1)} %collective-permute-done.25.refs_2_, ...), custom_call_target="tpu_custom_call" | custom-call | flops 1024 | bytes 1024 | tf_op jit(solution)/shard_map/pallas_call | solution.py:65
  240.4 1.5 collective-permute-start.32
  241.9 21.6 %collective-permute-done.32.refs_2_ = bf16[128,3840]{1,0:T(8,128)(2,1)S(1)} collective-permute-done((bf16[128,3840]{1,0:T(8,128)(2,1)S(1)}, bf16[128,3840]{1,0:T(8,128)(2,1)S(1)}, u32[]{:S(2)}, u32[]{:S(2)}) %collective-permute-start.32) | collective-permute-done | bytes 983072 | tf_op jit(solution)/shard_map/ppermute | solution.py:707
  264.6 3.5 shard_map.163
  269.4 3.1 collective-permute-start.28
  273.8 4.0 %shard_map.164 = (bf16[144,2304]{1,0:T(8,128)(2,1)S(1)}, bf16[128,768]{1,0:T(8,128)(2,1)S(1)}, f32[1,768]{1,0:T(1,128)}) custom-call(s32[1]{0:T(128)} %bitcast.37.refs_1_.lower_ref, bf16[768,2432]{1,0:T(8,128)(2,1)} %bitcast.23.first_ref, bf16[128,768]{1,0:T(8,128)(2,1)S(1)} %get-tuple-element.93.dq_ref, f32[128,1536]{1,0:T(8,128)S(1)} %get-tuple-element.94.own_ref, ...), custom_call_target="tpu_custom_call" | custom-call | flops 1024 | bytes 1024 | tf_op jit(solution)/shard_map/pallas_call | solution.py:65
  277.8 10.7 %collective-permute-start.30 = (bf16[144,2304]{1,0:T(8,128)(2,1)S(1)}, bf16[144,2304]{1,0:T(8,128)(2,1)S(1)}, u32[]{:S(2)}, u32[]{:S(2)}) collective-permute-start(bf16[144,2304]{1,0:T(8,128)(2,1)S(1)} %get-tuple-element.103.refs_0_), channel_id=1, source_target_pairs={{0,2},{1,3},{2,0},{3,1},{4,6},{5,7},{6,4},{7,5},{8,10},{9,11},{10,... | collective-permute-start | bytes 1990664 | tf_op jit(solution)/shard_map/ppermute | solution.py:707
  290.3 2.2 shard_map.165
  292.5 1.7 collective-permute-start.38
  295.1 1.9 collective-permute-start.40
  298.5 4.4 %collective-permute-done.30.refs_2_ = bf16[144,2304]{1,0:T(8,128)(2,1)S(1)} collective-permute-done((bf16[144,2304]{1,0:T(8,128)(2,1)S(1)}, bf16[144,2304]{1,0:T(8,128)(2,1)S(1)}, u32[]{:S(2)}, u32[]{:S(2)}) %collective-permute-start.30) | collective-permute-done | bytes 663584 | tf_op jit(solution)/shard_map/ppermute | solution.py:707
  302.9 5.6 %collective-permute-done.38 = bf16[264,768]{1,0:T(8,128)(2,1)S(1)} collective-permute-done((bf16[264,768]{1,0:T(8,128)(2,1)S(1)}, bf16[264,768]{1,0:T(8,128)(2,1)S(1)}, u32[]{:S(2)}, u32[]{:S(2)}) %collective-permute-start.38) | collective-permute-done | bytes 405536 | tf_op jit(solution)/shard_map/ppermute | solution.py:707
  308.5 16.4 %collective-permute-done.39 = bf16[264,768]{1,0:T(8,128)(2,1)S(1)} collective-permute-done((bf16[264,768]{1,0:T(8,128)(2,1)S(1)}, bf16[264,768]{1,0:T(8,128)(2,1)S(1)}, u32[]{:S(2)}, u32[]{:S(2)}) %collective-permute-start.39) | collective-permute-done | bytes 405536 | tf_op jit(solution)/shard_map/ppermute | solution.py:707
  327.3 5.8 %collective-permute-start.35 = (bf16[48,2432]{1,0:T(8,128)(2,1)S(1)}, bf16[48,2432]{1,0:T(8,128)(2,1)S(1)}, u32[]{:S(2)}, u32[]{:S(2)}) collective-permute-start(bf16[48,2432]{1,0:T(8,128)(2,1)S(1)} %get-tuple-element.115), channel_id=1, source_target_pairs={{0,4},{1,5},{2,6},{3,7},{4,0},{5,1},{6,2},{7,3},{8,12},{9,13},{10,... | collective-permute-start | bytes 700424 | tf_op jit(solution)/shard_map/ppermute | solution.py:707
  336.3 3.0 collective-permute-done.35
  339.3 11.2 %collective-permute-done.36 = bf16[48,2432]{1,0:T(8,128)(2,1)S(1)} collective-permute-done((bf16[48,2432]{1,0:T(8,128)(2,1)S(1)}, bf16[48,2432]{1,0:T(8,128)(2,1)S(1)}, u32[]{:S(2)}, u32[]{:S(2)}) %collective-permute-start.36) | collective-permute-done | bytes 233504 | tf_op jit(solution)/shard_map/ppermute | solution.py:707
  (269 shorter events, 75.2 us)
Async XLA Ops:
  7.2 88.2 %all-gather.2.cloned.1.call-start = ((), (), s32[]{:S(2)}) async-start(), calls=%async_computation.4 | async-start | bytes 7102464 | tf_op jit(solution)/shard_map/all_gather | solution.py:867
  10.3 43.7 %collective-permute-start.8 = (bf16[48,2432]{1,0:T(8,128)(2,1)S(1)}, bf16[48,2432]{1,0:T(8,128)(2,1)S(1)}, u32[]{:S(2)}, u32[]{:S(2)}) collective-permute-start(bf16[48,2432]{1,0:T(8,128)(2,1)S(1)} %shard_map.153), channel_id=1, source_target_pairs={{0,1},{1,0},{2,3},{3,2},{4,5},{5,4},{6,7},{7,6},{8,9},{9,8},{10,11... | collective-permute-start | bytes 700424 | tf_op jit(solution)/shard_map/ppermute | solution.py:707
  10.8 16.0 %collective-permute-start.4 = (bf16[48,2432]{1,0:T(8,128)(2,1)S(1)}, bf16[48,2432]{1,0:T(8,128)(2,1)S(1)}, u32[]{:S(2)}, u32[]{:S(2)}) collective-permute-start(bf16[48,2432]{1,0:T(8,128)(2,1)S(1)} %shard_map.153), channel_id=1, source_target_pairs={{0,12},{1,13},{2,14},{3,15},{4,8},{5,9},{6,10},{7,11},{8,4},{9,5},... | collective-permute-start | bytes 700424 | tf_op jit(solution)/shard_map/ppermute | solution.py:707
  15.5 20.7 %collective-permute-start.3 = (bf16[48,2432]{1,0:T(8,128)(2,1)S(1)}, bf16[48,2432]{1,0:T(8,128)(2,1)S(1)}, u32[]{:S(2)}, u32[]{:S(2)}) collective-permute-start(bf16[48,2432]{1,0:T(8,128)(2,1)S(1)} %shard_map.153), channel_id=1, source_target_pairs={{0,8},{1,9},{2,10},{3,11},{4,12},{5,13},{6,14},{7,15},{8,0},{9,1},... | collective-permute-start | bytes 700424 | tf_op jit(solution)/shard_map/ppermute | solution.py:707
  15.5 7.8 %collective-permute-start.1 = (bf16[48,2432]{1,0:T(8,128)(2,1)S(1)}, bf16[48,2432]{1,0:T(8,128)(2,1)S(1)}, u32[]{:S(2)}, u32[]{:S(2)}) collective-permute-start(bf16[48,2432]{1,0:T(8,128)(2,1)S(1)} %shard_map.153), channel_id=1, source_target_pairs={{0,2},{1,3},{2,0},{3,1},{4,6},{5,7},{6,4},{7,5},{8,10},{9,11},{10,... | collective-permute-start | bytes 700424 | tf_op jit(solution)/shard_map/ppermute | solution.py:707
  17.7 1.2 collective-permute-start
  18.9 17.3 %collective-permute-start.2 = (bf16[48,2432]{1,0:T(8,128)(2,1)S(1)}, bf16[48,2432]{1,0:T(8,128)(2,1)S(1)}, u32[]{:S(2)}, u32[]{:S(2)}) collective-permute-start(bf16[48,2432]{1,0:T(8,128)(2,1)S(1)} %shard_map.153), channel_id=1, source_target_pairs={{0,4},{1,5},{2,6},{3,7},{4,0},{5,1},{6,2},{7,3},{8,12},{9,13},{10,... | collective-permute-start | bytes 700424 | tf_op jit(solution)/shard_map/ppermute | solution.py:707
  26.4 34.9 %copy-start = (bf16[2,64,768]{2,1,0:T(8,128)(2,1)S(1)}, bf16[2,64,768]{2,1,0:T(8,128)(2,1)}, u32[]{:S(2)}) copy-start(bf16[2,64,768]{2,1,0:T(8,128)(2,1)} %param.9) | copy-start | bytes 589828
  26.9 33.0 %collective-permute-start.14 = (bf16[48,2432]{1,0:T(8,128)(2,1)S(1)}, bf16[48,2432]{1,0:T(8,128)(2,1)S(1)}, u32[]{:S(2)}, u32[]{:S(2)}) collective-permute-start(bf16[48,2432]{1,0:T(8,128)(2,1)S(1)} %collective-permute-done.4), channel_id=1, source_target_pairs={{0,1},{1,0},{2,3},{3,2},{4,5},{5,4},{6,7},{7,6},{8,9},{9,8},{10,11... | collective-permute-start | bytes 700424 | tf_op jit(solution)/shard_map/ppermute | solution.py:707
  26.9 25.8 %collective-permute-start.7 = (bf16[48,2432]{1,0:T(8,128)(2,1)S(1)}, bf16[48,2432]{1,0:T(8,128)(2,1)S(1)}, u32[]{:S(2)}, u32[]{:S(2)}) collective-permute-start(bf16[48,2432]{1,0:T(8,128)(2,1)S(1)} %collective-permute-done.4), channel_id=1, source_target_pairs={{0,2},{1,3},{2,0},{3,1},{4,6},{5,7},{6,4},{7,5},{8,10},{9,11},{10,... | collective-permute-start | bytes 700424 | tf_op jit(solution)/shard_map/ppermute | solution.py:707
  36.2 22.3 %collective-permute-start.12 = (bf16[48,2432]{1,0:T(8,128)(2,1)S(1)}, bf16[48,2432]{1,0:T(8,128)(2,1)S(1)}, u32[]{:S(2)}, u32[]{:S(2)}) collective-permute-start(bf16[48,2432]{1,0:T(8,128)(2,1)S(1)} %collective-permute-done.3), channel_id=1, source_target_pairs={{0,1},{1,0},{2,3},{3,2},{4,5},{5,4},{6,7},{7,6},{8,9},{9,8},{10,11... | collective-permute-start | bytes 700424 | tf_op jit(solution)/shard_map/ppermute | solution.py:707
  36.2 8.3 %collective-permute-start.5 = (bf16[48,2432]{1,0:T(8,128)(2,1)S(1)}, bf16[48,2432]{1,0:T(8,128)(2,1)S(1)}, u32[]{:S(2)}, u32[]{:S(2)}) collective-permute-start(bf16[48,2432]{1,0:T(8,128)(2,1)S(1)} %collective-permute-done.2), channel_id=1, source_target_pairs={{0,2},{1,3},{2,0},{3,1},{4,6},{5,7},{6,4},{7,5},{8,10},{9,11},{10,... | collective-permute-start | bytes 700424 | tf_op jit(solution)/shard_map/ppermute | solution.py:707
  44.5 7.5 %collective-permute-start.6 = (bf16[48,2432]{1,0:T(8,128)(2,1)S(1)}, bf16[48,2432]{1,0:T(8,128)(2,1)S(1)}, u32[]{:S(2)}, u32[]{:S(2)}) collective-permute-start(bf16[48,2432]{1,0:T(8,128)(2,1)S(1)} %collective-permute-done.3), channel_id=1, source_target_pairs={{0,2},{1,3},{2,0},{3,1},{4,6},{5,7},{6,4},{7,5},{8,10},{9,11},{10,... | collective-permute-start | bytes 700424 | tf_op jit(solution)/shard_map/ppermute | solution.py:707
  52.0 3.9 %collective-permute-start.10 = (bf16[48,2432]{1,0:T(8,128)(2,1)S(1)}, bf16[48,2432]{1,0:T(8,128)(2,1)S(1)}, u32[]{:S(2)}, u32[]{:S(2)}) collective-permute-start(bf16[48,2432]{1,0:T(8,128)(2,1)S(1)} %collective-permute-done.2), channel_id=1, source_target_pairs={{0,1},{1,0},{2,3},{3,2},{4,5},{5,4},{6,7},{7,6},{8,9},{9,8},{10,11... | collective-permute-start | bytes 700424 | tf_op jit(solution)/shard_map/ppermute | solution.py:707
  52.7 2.0 collective-permute-start.9
  54.0 6.6 %collective-permute-start.15 = (bf16[48,2432]{1,0:T(8,128)(2,1)S(1)}, bf16[48,2432]{1,0:T(8,128)(2,1)S(1)}, u32[]{:S(2)}, u32[]{:S(2)}) collective-permute-start(bf16[48,2432]{1,0:T(8,128)(2,1)S(1)} %collective-permute-done.7), channel_id=1, source_target_pairs={{0,1},{1,0},{2,3},{3,2},{4,5},{5,4},{6,7},{7,6},{8,9},{9,8},{10,11... | collective-permute-start | bytes 700424 | tf_op jit(solution)/shard_map/ppermute | solution.py:707
  54.7 4.5 %collective-permute-start.13 = (bf16[48,2432]{1,0:T(8,128)(2,1)S(1)}, bf16[48,2432]{1,0:T(8,128)(2,1)S(1)}, u32[]{:S(2)}, u32[]{:S(2)}) collective-permute-start(bf16[48,2432]{1,0:T(8,128)(2,1)S(1)} %collective-permute-done.6), channel_id=1, source_target_pairs={{0,1},{1,0},{2,3},{3,2},{4,5},{5,4},{6,7},{7,6},{8,9},{9,8},{10,11... | collective-permute-start | bytes 700424 | tf_op jit(solution)/shard_map/ppermute | solution.py:707
  55.9 1.8 collective-permute-start.11
  65.1 34.7 %copy-start.15 = (bf16[128,768]{1,0:T(8,128)(2,1)}, bf16[128,768]{1,0:T(8,128)(2,1)S(1)}, u32[]{:S(2)}) copy-start(bf16[128,768]{1,0:T(8,128)(2,1)S(1)} %get-tuple-element.64.q_ref) | copy-start | bytes 589828
  65.1 5.0 %collective-permute-start.17 = (bf16[128,1536]{1,0:T(8,128)(2,1)S(1)}, bf16[128,1536]{1,0:T(8,128)(2,1)S(1)}, u32[]{:S(2)}, u32[]{:S(2)}) collective-permute-start(bf16[128,1536]{1,0:T(8,128)(2,1)S(1)} %get-tuple-element.65.own_ref), channel_id=1, source_target_pairs={{1,0},{2,1},{3,2},{4,3},{5,4},{6,5},{7,6},{8,7},{9,8},{10,9},{11,1... | collective-permute-start | bytes 1179656 | tf_op jit(solution)/shard_map/ppermute | solution.py:916
  66.4 4.4 %collective-permute-start.16 = (bf16[128,1536]{1,0:T(8,128)(2,1)S(1)}, bf16[128,1536]{1,0:T(8,128)(2,1)S(1)}, u32[]{:S(2)}, u32[]{:S(2)}) collective-permute-start(bf16[128,1536]{1,0:T(8,128)(2,1)S(1)} %get-tuple-element.65.own_ref), channel_id=1, source_target_pairs={{0,1},{1,2},{2,3},{3,4},{4,5},{5,6},{6,7},{7,8},{8,9},{9,10},{10,1... | collective-permute-start | bytes 1179656 | tf_op jit(solution)/shard_map/ppermute | solution.py:914
  102.3 6.5 %collective-permute-start.18 = (bf16[64,768]{1,0:T(8,128)(2,1)S(1)}, bf16[64,768]{1,0:T(8,128)(2,1)S(1)}, u32[]{:S(2)}, u32[]{:S(2)}) collective-permute-start(bf16[64,768]{1,0:T(8,128)(2,1)S(1)} %get-tuple-element.68), channel_id=1, source_target_pairs={{0,16},{1,17},{2,18},{3,19},{4,20},{5,21},{6,22},{7,23},{8,24},{9,... | collective-permute-start | bytes 294920 | tf_op jit(solution)/shard_map/ppermute | solution.py:703
  105.7 4.6 %collective-permute-start.19 = (bf16[64,768]{1,0:T(8,128)(2,1)S(1)}, bf16[64,768]{1,0:T(8,128)(2,1)S(1)}, u32[]{:S(2)}, u32[]{:S(2)}) collective-permute-start(bf16[64,768]{1,0:T(8,128)(2,1)S(1)} %get-tuple-element.69), channel_id=1, source_target_pairs={{0,16},{1,17},{2,18},{3,19},{4,20},{5,21},{6,22},{7,23},{8,24},{9,... | collective-permute-start | bytes 294920 | tf_op jit(solution)/shard_map/ppermute | solution.py:703
  134.6 1.7 collective-permute-start.20
  169.0 13.2 %all-to-all-start.2 = ((bf16[16,48,128]{2,1,0:T(8,128)(2,1)}), bf16[16,48,128]{2,1,0:T(8,128)(2,1)}, u32[]{:S(2)}, u32[]{:S(2)}) async-start(bf16[16,48,128]{2,1,0:T(8,128)(2,1)} %copy-done.27), calls=%async_computation.2 | async-start | bytes 393216 | tf_op jit(solution)/shard_map/all_to_all | solution.py:698
  190.5 2.0 collective-permute-start.24
  193.6 23.4 %all-to-all-start.3 = ((bf16[16,144,128]{2,1,0:T(8,128)(2,1)}), bf16[16,144,128]{2,1,0:T(8,128)(2,1)S(1)}, u32[]{:S(2)}, u32[]{:S(2)}) async-start(bf16[16,144,128]{2,1,0:T(8,128)(2,1)} %add_convert_fusion), calls=%async_computation.3 | async-start | bytes 1179648 | tf_op jit(solution)/shard_map/all_to_all | solution.py:698
  201.5 3.0 collective-permute-start.21
  201.9 10.6 %collective-permute-start.22 = (bf16[4,1,216,128]{3,2,0,1:T(8,128)(2,1)S(1)}, bf16[4,1,216,128]{3,2,0,1:T(8,128)(2,1)S(1)}, u32[]{:S(2)}, u32[]{:S(2)}) collective-permute-start(bf16[4,1,216,128]{3,2,0,1:T(8,128)(2,1)S(1)} %pad_maximum_fusion.4), channel_id=1, source_target_pairs={{0,2},{1,3},{2,0},{3,1},{4,6},{5,7},{6,4},{7,5},{8,10},{9,11},{10,... | collective-permute-start | bytes 663560 | tf_op jit(solution)/shard_map/ppermute | solution.py:707
  203.7 13.3 %collective-permute-start.23 = (bf16[4,1,216,128]{3,2,0,1:T(8,128)(2,1)S(1)}, bf16[4,1,216,128]{3,2,0,1:T(8,128)(2,1)}, u32[]{:S(2)}, u32[]{:S(2)}) collective-permute-start(bf16[4,1,216,128]{3,2,0,1:T(8,128)(2,1)S(1)} %pad_maximum_fusion.5), channel_id=1, source_target_pairs={{0,3},{1,2},{2,1},{3,0},{4,7},{5,6},{6,5},{7,4},{8,11},{9,10},{10,... | collective-permute-start | bytes 663560 | tf_op jit(solution)/shard_map/ppermute | solution.py:707
  223.0 7.5 %collective-permute-start.25 = (bf16[64,768]{1,0:T(8,128)(2,1)S(1)}, bf16[64,768]{1,0:T(8,128)(2,1)S(1)}, u32[]{:S(2)}, u32[]{:S(2)}) collective-permute-start(bf16[64,768]{1,0:T(8,128)(2,1)S(1)} %get-tuple-element.87), channel_id=1, source_target_pairs={{16,0},{17,1},{18,2},{19,3},{20,4},{21,5},{22,6},{23,7},{24,8},{25... | collective-permute-start | bytes 294920 | tf_op jit(solution)/shard_map/ppermute | solution.py:703
  224.3 7.7 %collective-permute-start.26 = (bf16[64,768]{1,0:T(8,128)(2,1)S(1)}, bf16[64,768]{1,0:T(8,128)(2,1)S(1)}, u32[]{:S(2)}, u32[]{:S(2)}) collective-permute-start(bf16[64,768]{1,0:T(8,128)(2,1)S(1)} %get-tuple-element.88), channel_id=1, source_target_pairs={{16,0},{17,1},{18,2},{19,3},{20,4},{21,5},{22,6},{23,7},{24,8},{25... | collective-permute-start | bytes 294920 | tf_op jit(solution)/shard_map/ppermute | solution.py:703
  234.3 39.5 %copy-start.48 = (f32[1,768]{1,0:T(1,128)S(1)}, f32[1,768]{1,0:T(1,128)}, u32[]{:S(2)}) copy-start(f32[1,768]{1,0:T(1,128)} %copy-done.47) | copy-start | bytes 9220
  234.3 39.5 %copy-start.50 = (f32[1,768]{1,0:T(1,128)S(1)}, f32[1,768]{1,0:T(1,128)}, u32[]{:S(2)}) copy-start(f32[1,768]{1,0:T(1,128)} %copy-done.49) | copy-start | bytes 9220
  240.4 23.2 %collective-permute-start.32 = (bf16[128,3840]{1,0:T(8,128)(2,1)S(1)}, bf16[128,3840]{1,0:T(8,128)(2,1)S(1)}, u32[]{:S(2)}, u32[]{:S(2)}) collective-permute-start(bf16[128,3840]{1,0:T(8,128)(2,1)S(1)} %get-tuple-element.104.refs_0_), channel_id=1, source_target_pairs={{0,2},{1,3},{2,0},{3,1},{4,6},{5,7},{6,4},{7,5},{8,10},{9,11},{10,... | collective-permute-start | bytes 2949128 | tf_op jit(solution)/shard_map/ppermute | solution.py:707
  241.9 47.4 %collective-permute-start.31 = (bf16[128,3840]{1,0:T(8,128)(2,1)S(1)}, bf16[128,3840]{1,0:T(8,128)(2,1)S(1)}, u32[]{:S(2)}, u32[]{:S(2)}) collective-permute-start(bf16[128,3840]{1,0:T(8,128)(2,1)S(1)} %get-tuple-element.104.refs_0_), channel_id=1, source_target_pairs={{0,1},{1,0},{2,3},{3,2},{4,5},{5,4},{6,7},{7,6},{8,9},{9,8},{10,11... | collective-permute-start | bytes 2949128 | tf_op jit(solution)/shard_map/ppermute | solution.py:707
  263.6 25.8 %collective-permute-start.33 = (bf16[128,3840]{1,0:T(8,128)(2,1)S(1)}, bf16[128,3840]{1,0:T(8,128)(2,1)S(1)}, u32[]{:S(2)}, u32[]{:S(2)}) collective-permute-start(bf16[128,3840]{1,0:T(8,128)(2,1)S(1)} %collective-permute-done.32.refs_2_), channel_id=1, source_target_pairs={{0,1},{1,0},{2,3},{3,2},{4,5},{5,4},{6,7},{7,6},{8,9},{9,8},{10,11... | collective-permute-start | bytes 2949128 | tf_op jit(solution)/shard_map/ppermute | solution.py:707
  268.1 4.4 %collective-permute-start.27 = (bf16[128,1536]{1,0:T(8,128)(2,1)S(1)}, bf16[128,1536]{1,0:T(8,128)(2,1)S(1)}, u32[]{:S(2)}, u32[]{:S(2)}) collective-permute-start(bf16[128,1536]{1,0:T(8,128)(2,1)S(1)} %get-tuple-element.95), channel_id=1, source_target_pairs={{1,0},{2,1},{3,2},{4,3},{5,4},{6,5},{7,6},{8,7},{9,8},{10,9},{11,1... | collective-permute-start | bytes 1179656 | tf_op jit(solution)/shard_map/ppermute | solution.py:1059
  269.4 4.4 %collective-permute-start.28 = (bf16[128,1536]{1,0:T(8,128)(2,1)S(1)}, bf16[128,1536]{1,0:T(8,128)(2,1)S(1)}, u32[]{:S(2)}, u32[]{:S(2)}) collective-permute-start(bf16[128,1536]{1,0:T(8,128)(2,1)S(1)} %get-tuple-element.96), channel_id=1, source_target_pairs={{0,1},{1,2},{2,3},{3,4},{4,5},{5,6},{6,7},{7,8},{8,9},{9,10},{10,1... | collective-permute-start | bytes 1179656 | tf_op jit(solution)/shard_map/ppermute | solution.py:1060
  277.8 25.1 %collective-permute-start.30 = (bf16[144,2304]{1,0:T(8,128)(2,1)S(1)}, bf16[144,2304]{1,0:T(8,128)(2,1)S(1)}, u32[]{:S(2)}, u32[]{:S(2)}) collective-permute-start(bf16[144,2304]{1,0:T(8,128)(2,1)S(1)} %get-tuple-element.103.refs_0_), channel_id=1, source_target_pairs={{0,2},{1,3},{2,0},{3,1},{4,6},{5,7},{6,4},{7,5},{8,10},{9,11},{10,... | collective-permute-start | bytes 1990664 | tf_op jit(solution)/shard_map/ppermute | solution.py:707
  292.5 16.0 %collective-permute-start.38 = (bf16[264,768]{1,0:T(8,128)(2,1)S(1)}, bf16[264,768]{1,0:T(8,128)(2,1)S(1)}, u32[]{:S(2)}, u32[]{:S(2)}) collective-permute-start(bf16[264,768]{1,0:T(8,128)(2,1)S(1)} %get-tuple-element.110), channel_id=1, source_target_pairs={{0,4},{1,5},{2,6},{3,7},{4,0},{5,1},{6,2},{7,3},{8,12},{9,13},{10,... | collective-permute-start | bytes 1216520 | tf_op jit(solution)/shard_map/ppermute | solution.py:707
  294.3 30.6 %collective-permute-start.39 = (bf16[264,768]{1,0:T(8,128)(2,1)S(1)}, bf16[264,768]{1,0:T(8,128)(2,1)S(1)}, u32[]{:S(2)}, u32[]{:S(2)}) collective-permute-start(bf16[264,768]{1,0:T(8,128)(2,1)S(1)} %get-tuple-element.111), channel_id=1, source_target_pairs={{0,8},{1,9},{2,10},{3,11},{4,12},{5,13},{6,14},{7,15},{8,0},{9,1},... | collective-permute-start | bytes 1216520 | tf_op jit(solution)/shard_map/ppermute | solution.py:707
  295.1 29.8 %collective-permute-start.40 = (bf16[264,768]{1,0:T(8,128)(2,1)S(1)}, bf16[264,768]{1,0:T(8,128)(2,1)S(1)}, u32[]{:S(2)}, u32[]{:S(2)}) collective-permute-start(bf16[264,768]{1,0:T(8,128)(2,1)S(1)} %get-tuple-element.112), channel_id=1, source_target_pairs={{0,12},{1,13},{2,14},{3,15},{4,8},{5,9},{6,10},{7,11},{8,4},{9,5},... | collective-permute-start | bytes 1216520 | tf_op jit(solution)/shard_map/ppermute | solution.py:707
  297.7 28.9 %collective-permute-start.29 = (bf16[144,2304]{1,0:T(8,128)(2,1)S(1)}, bf16[144,2304]{1,0:T(8,128)(2,1)S(1)}, u32[]{:S(2)}, u32[]{:S(2)}) collective-permute-start(bf16[144,2304]{1,0:T(8,128)(2,1)S(1)} %get-tuple-element.103.refs_0_), channel_id=1, source_target_pairs={{0,1},{1,0},{2,3},{3,2},{4,5},{5,4},{6,7},{7,6},{8,9},{9,8},{10,11... | collective-permute-start | bytes 1990664 | tf_op jit(solution)/shard_map/ppermute | solution.py:707
  302.9 23.7 %collective-permute-start.34 = (bf16[144,2304]{1,0:T(8,128)(2,1)S(1)}, bf16[144,2304]{1,0:T(8,128)(2,1)S(1)}, u32[]{:S(2)}, u32[]{:S(2)}) collective-permute-start(bf16[144,2304]{1,0:T(8,128)(2,1)S(1)} %collective-permute-done.30.refs_2_), channel_id=1, source_target_pairs={{0,1},{1,0},{2,3},{3,2},{4,5},{5,4},{6,7},{7,6},{8,9},{9,8},{10,11... | collective-permute-start | bytes 1990664 | tf_op jit(solution)/shard_map/ppermute | solution.py:707
  327.3 12.0 %collective-permute-start.35 = (bf16[48,2432]{1,0:T(8,128)(2,1)S(1)}, bf16[48,2432]{1,0:T(8,128)(2,1)S(1)}, u32[]{:S(2)}, u32[]{:S(2)}) collective-permute-start(bf16[48,2432]{1,0:T(8,128)(2,1)S(1)} %get-tuple-element.115), channel_id=1, source_target_pairs={{0,4},{1,5},{2,6},{3,7},{4,0},{5,1},{6,2},{7,3},{8,12},{9,13},{10,... | collective-permute-start | bytes 700424 | tf_op jit(solution)/shard_map/ppermute | solution.py:707
  333.1 17.4 %collective-permute-start.36 = (bf16[48,2432]{1,0:T(8,128)(2,1)S(1)}, bf16[48,2432]{1,0:T(8,128)(2,1)S(1)}, u32[]{:S(2)}, u32[]{:S(2)}) collective-permute-start(bf16[48,2432]{1,0:T(8,128)(2,1)S(1)} %get-tuple-element.116), channel_id=1, source_target_pairs={{0,8},{1,9},{2,10},{3,11},{4,12},{5,13},{6,14},{7,15},{8,0},{9,1},... | collective-permute-start | bytes 700424 | tf_op jit(solution)/shard_map/ppermute | solution.py:707
  334.2 16.3 %collective-permute-start.37 = (bf16[48,2432]{1,0:T(8,128)(2,1)S(1)}, bf16[48,2432]{1,0:T(8,128)(2,1)S(1)}, u32[]{:S(2)}, u32[]{:S(2)}) collective-permute-start(bf16[48,2432]{1,0:T(8,128)(2,1)S(1)} %get-tuple-element.117), channel_id=1, source_target_pairs={{0,12},{1,13},{2,14},{3,15},{4,8},{5,9},{6,10},{7,11},{8,4},{9,5},... | collective-permute-start | bytes 700424 | tf_op jit(solution)/shard_map/ppermute | solution.py:707
  (55 other events, 569.0 us)
Sparse Core Ops, SparseCore 0:
  23.4 71.9 all-gather.1

commit v6 on v5

--- a/solution.py
+++ b/solution.py
@@ -75,7 +75,7 @@
         cost_estimate=pl.CostEstimate(
             flops=2**10, bytes_accessed=2**10, transcendentals=0
         ),
-        compiler_params=pltpu.CompilerParams(vmem_limit_bytes=48 * 2**20),
+        compiler_params=pltpu.CompilerParams(vmem_limit_bytes=60 * 2**20),
     )(*args)
 
 
@@ -738,6 +738,20 @@
     return taken
 
 
+def left_body(lower_ref, place_ref, *refs):
+    refs, out_ref = refs[:-1], refs[-1]
+    base = 0
+    for first_ref, second_ref in zip(refs[0::2], refs[1::2]):
+        rows = jnp.where(lower_ref[0] == 1, first_ref[...].astype(F32), second_ref[...].astype(F32))
+        turned = rows.T
+        size = turned.shape[0] // GROUP
+        for d in range(GROUP):
+            side = d % 4 ^ place_ref[0] % 4
+            plane = d // 4 ^ place_ref[0] // 4
+            out_ref[side, plane, base : base + size] = turned[d * size : (d + 1) * size].astype(BF)
+        base += size
+
+
 def early_body(shard, *refs):
     refs, outs = refs[:-4], refs[-4:]
     rights, n2, mixed, att = (refs[4 * i : 4 * i + 4] for i in range(4))
@@ -801,10 +815,13 @@
     return [rows, beside, across, partner(across, 1, count)]
 
 
-def sum_planes(blocks, count):
-    got = [partner(item, 4 * (z + 1), count) for z, item in enumerate(blocks[1:])]
+def sent_planes(blocks, count):
+    return [blocks[0]] + [partner(item, 4 * (z + 1), count) for z, item in enumerate(blocks[1:])]
+
+
+def sum_planes(blocks):
     total = blocks[0]
-    for item in got:
+    for item in blocks[1:]:
         total = total + item.astype(F32)
     return total
 
@@ -991,6 +1008,22 @@
             pltpu.VMEM((2, keys, LANES), F32),
         ],
     )
+    pairs = ((normed_0, normed_1), (att_0, att_1), (n2_0, n2_1), (mixed_0, mixed_1))
+    left_rows = 3 * shard + mlp_out_weight.shape[1]
+    if count == GROUP:
+        (left,) = on_core(
+            left_body,
+            [((4, 4, left_rows, rows), BF)],
+            (lower_flag, group_pos[None], *(item for pair in pairs for item in pair)),
+            (),
+            [pltpu.SMEM] * 2 + [pltpu.VMEM] * 8,
+        )
+        left, sent = lax.optimization_barrier((left, sent))
+        left = [left[0]] + [partner(left[apart], apart, count) for apart in range(1, 4)]
+        left = [item[:, None] for item in left]
+    else:
+        left = [jnp.where(lower, a, b).T.reshape(count, -1, rows) for a, b in pairs]
+        left = plane_rows(jnp.concatenate(left, 1), group_pos, count)
     back = partner(to_beside, 1, count)
     gap = 3 * fold - half - row_count - half
     back = jnp.concatenate(
@@ -1005,17 +1038,6 @@
     sent = (sent.astype(F32) + back.astype(F32)).astype(BF)
     got = exchange(sent, count)
 
-    n1, att, n2, mixed = (
-        jnp.where(lower, a, b).T.reshape(count, -1, micro_count * row_count)
-        for a, b in (
-            (normed_0, normed_1),
-            (att_0, att_1),
-            (n2_0, n2_1),
-            (mixed_0, mixed_1),
-        )
-    )
-    left = jnp.concatenate([n1, att, n2, mixed], 1)
-    left = plane_rows(left, group_pos, count)
     left, got = lax.optimization_barrier((left, got))
     n1, att, n2, mixed = (
         [part[:, :, start:end] for part in left]
@@ -1023,7 +1045,7 @@
             (0, shard),
             (shard, 2 * shard),
             (2 * shard, 3 * shard),
-            (3 * shard, left[0].shape[2]),
+            (3 * shard, left_rows),
         )
     )
     d_proj_1, gain_attn_1, *grad_1 = on_core(
@@ -1045,7 +1067,7 @@
         [pltpu.VMEM((hidden, width), BF)],
         [pltpu.VMEM] * len(others) + [pltpu.SMEM] + [pltpu.VMEM] * 6,
     )
-    right = plane_parts(right, count)
+    across, beside = partner(right, 2, count), partner(right, 1, count)
     dq_0, d_own, d_before, d_after = on_core(
         local_backward_body,
         [
@@ -1068,6 +1090,8 @@
         [pltpu.VMEM((1, width), F32)],
         [pltpu.SMEM] + [pltpu.VMEM] * 13,
     )
+    across, d_proj = lax.optimization_barrier((across, d_proj))
+    right = [right, beside, across, partner(across, 1, count)]
     early_rows = shard_total * (inner // width + 1) + hidden_total
     early = on_core(
         functools.partial(early_body, shard),
@@ -1075,7 +1099,7 @@
         (*right, *flat_rows(n2), *flat_rows(mixed), *flat_rows(att)),
     )
     d_proj = plane_parts(d_proj, count, early)
-    early = sum_planes(early, count)
+    early = sent_planes(early, count)
     late_in = (group_pos[None], *d_proj, *flat_rows(n1))
     late = on_core(
         late_body,
@@ -1084,7 +1108,8 @@
         [pltpu.VMEM((width, LANES), F32)],
         [pltpu.SMEM] + [pltpu.VMEM] * (len(late_in) - 1),
     )
-    late = sum_planes(late, count)
+    early, late = lax.optimization_barrier((early, list(late)))
+    early, late = sum_planes(early), sum_planes(sent_planes(late, count))
     parts = [early[p * shard_total : (p + 1) * shard_total] for p in range(inner // width)]
     start = shard_total * (inner // width)
     in_share = jnp.concatenate(parts, 1)

time: 362 us -> 373 us (1.030)
  Pallas kernels: 56.5 us -> 83.4 us
  waiting for transfers between devices: 131 us -> 112 us
  blocking collectives: 32.1 us -> 49.7 us
  local copies, waits for them, and re-layouts: 49 us -> 39.2 us
    pallas_call x15 -> x16, Pallas kernels: 56.5 us -> 83.4 us  [on_core(): pl.pallas_call(body, out_shape=[jax.ShapeDtypeStruct(shape, dtype) for sh...]
    all_to_all x2 -> x3, blocking collectives: 32.1 us -> 49.7 us  [exchange(): return lax.all_to_all(blocks, 'dp', 0, 0, axis_index_groups=groups)]
    unnamed x118 -> x46, local copies, waits for them, and re-layouts: 23.1 us -> 7.02 us
    ppermute x33, waiting for transfers between devices: 93.5 us -> 81.8 us  [partner(): return lax.ppermute(rows, 'dp', [(i, i ^ apart) for i in range(count)])]
    ppermute x33, starting transfers between devices: 40.7 us -> 46.2 us  [partner(): return lax.ppermute(rows, 'dp', [(i, i ^ apart) for i in range(count)])]
    all_to_all x2 -> x1, waiting for transfers between devices: 5.47 us -> 0.01 us  [exchange(): return lax.all_to_all(blocks, 'dp', 0, 0, axis_index_groups=groups)]
    slice x8, local copies, waits for them, and re-layouts: 1.81 us -> 6.94 us  [on_device(): part[:, :, start:end]]
    transpose x4 -> x0, local copies, waits for them, and re-layouts: 4.59 us -> none  [on_device(): jnp.where(lower, a, b).T.reshape(count, -1, micro_count * row_count)]
  transfers between devices with their start and end apart: 44 -> 43, of which waited for: 23 -> 17; matrix products, arithmetic and copies ran while one was open for 9% -> 10% of each run, Pallas kernels for 5% -> 9%
where the time goes in v6:
time: 373 us; the launch traced here: 371 us
  waiting for transfers between devices  112 us (30%)
  Pallas kernels  83.4 us (22%)
  starting transfers between devices  64.9 us (17%)
  blocking collectives  49.7 us (13%)
  local copies, waits for them, and re-layouts  39.2 us (11%)
  between operations  14.4 us (4%)
  other arithmetic  7.38 us (2%)
    pallas_call x16, Pallas kernels, on_core(): pl.pallas_call(body, out_shape=[jax.ShapeDtypeStruct(shape, dtype) for sh...  83.4 us
    ppermute x33, waiting for transfers between devices, partner(): return lax.ppermute(rows, 'dp', [(i, i ^ apart) for i in range(count)])  81.8 us
    all_to_all x3, blocking collectives, exchange(): return lax.all_to_all(blocks, 'dp', 0, 0, axis_index_groups=groups)  49.7 us
    ppermute x33, starting transfers between devices, partner(): return lax.ppermute(rows, 'dp', [(i, i ^ apart) for i in range(count)])  46.2 us
    all_gather x1, waiting for transfers between devices, on_device(): others = [lax.all_gather(stacked, 'dp', axis=0, tiled=True)]  21.3 us
    dynamic_update_slice x16, local copies, waits for them, and re-layouts, gather_rows(): whole = lax.dynamic_update_slice(whole, item[None], start)  11.3 us
    ppermute x4, waiting for transfers between devices, to_other_section(): return [lax.ppermute(rows, 'section', pairs) for rows in chunks]  9.12 us
  transfers between devices with their start and end apart: 43, of which 17 were waited for; matrix products, arithmetic and copies ran while one was open for 10% of the time, Pallas kernels for 9%

profile of v6, /device:TPU:0, one launch (start us, length us, event | category | flops | bytes accessed | tf_op | source)
XLA Modules:
  0.0 371.5 jit_solution(3630356220435180882)
XLA Ops:
  7.2 1.8 shard_map.153
  9.0 2.9 collective-permute-start.1
  12.0 1.6 collective-permute-start.2
  13.5 2.6 collective-permute-start.3
  18.8 1.8 shard_map.152
  20.9 2.1 broadcast_in_dim.114
  25.4 7.9 %collective-permute-done.3 = bf16[48,2432]{1,0:T(8,128)(2,1)S(1)} collective-permute-done((bf16[48,2432]{1,0:T(8,128)(2,1)}, bf16[48,2432]{1,0:T(8,128)(2,1)S(1)}, u32[]{:S(2)}, u32[]{:S(2)}) %collective-permute-start.3) | collective-permute-done | bytes 233504 | tf_op jit(solution)/shard_map/ppermute | solution.py:707
  38.9 4.8 %collective-permute-done.6 = bf16[48,2432]{1,0:T(8,128)(2,1)S(1)} collective-permute-done((bf16[48,2432]{1,0:T(8,128)(2,1)S(1)}, bf16[48,2432]{1,0:T(8,128)(2,1)S(1)}, u32[]{:S(2)}, u32[]{:S(2)}) %collective-permute-start.6) | collective-permute-done | bytes 233504 | tf_op jit(solution)/shard_map/ppermute | solution.py:707
  44.3 3.2 collective-permute-done.7
  54.9 4.0 %shard_map.154 = (f32[8,768]{1,0:T(8,128)}, bf16[128,768]{1,0:T(8,128)(2,1)}, bf16[128,768]{1,0:T(8,128)(2,1)}, bf16[128,1536]{1,0:T(8,128)(2,1)}) custom-call(bf16[768,2432]{1,0:T(8,128)(2,1)} %bitcast.23.first_ref, bf16[128,768]{1,0:T(8,128)(2,1)} %bitcast.104, f32[3,128,128]{2,1,0:T(8,128)} %tile.13.table_ref), custom_call_target="tpu_custom_call" | custom-call | flops 1024 | bytes 1024 | tf_op jit(solution)/shard_map/pallas_call | solution.py:65
  58.9 2.1 collective-permute-start.16
  66.8 5.7 %shard_map.155 = (bf16[128,768]{1,0:T(8,128)(2,1)}, f32[12,1,128]{2,1,0:T(1,128)}) custom-call(bf16[128,768]{1,0:T(8,128)(2,1)} %get-tuple-element.76.q_ref, bf16[128,1536]{1,0:T(8,128)(2,1)} %copy-done.3, bf16[128,1536]{1,0:T(8,128)(2,1)} %get-tuple-element.77.own_ref, bf16[128,1536]{1,0:T(8,128)(2,1)} %copy-done.4, f32[2,192,128]{2,1,0:T(8,128)} %copy.18.bias_ref), custom_call_target="tpu_custom_call" | custom-call | flops 1024 | bytes 1024 | tf_op jit(solution)/shard_map/pallas_call | solution.py:65
  72.5 21.3 %all-gather.2.cloned.1.call-done.refs_0_ = bf16[768,4352]{1,0:T(8,128)(2,1)} async-done(((bf16[48,4352]{1,0:T(8,128)(2,1)}), bf16[768,4352]{1,0:T(8,128)(2,1)}) %all-gather.2.cloned.1.call-update) | async-done | bytes 6684688 | tf_op jit(solution)/shard_map/all_gather | solution.py:884
  93.8 5.5 %shard_map.156 = (bf16[128,768]{1,0:T(8,128)(2,1)}, bf16[128,1152]{1,0:T(8,128)(2,1)}, f32[128,768]{1,0:T(8,128)}, f32[128,2304]{1,0:T(8,128)}, bf16[64,768]{1,0:T(8,128)(2,1)}, /*index=5*/bf16[64,768]{1,0:T(8,128)(2,1)}) custom-call(bf16[768,4352]{1,0:T(8,128)(2,1)} %all-gather.2.cloned.1.call-done.refs_0_, bf16[128,768]{1,0:T(8,128)(2,1)} %bitcast.105, ...), custom_call_target="tpu_custom_call" | custom-call | flops 1024 | bytes 1024 | tf_op jit(solution)/shard_map/pallas_call | solution.py:65
  99.3 3.4 collective-permute-start.18
  108.2 4.0 %shard_map.157 = (bf16[128,768]{1,0:T(8,128)(2,1)}, bf16[16,144,128]{2,1,0:T(8,128)(2,1)}) custom-call(bf16[768,2432]{1,0:T(8,128)(2,1)} %bitcast.23.first_ref, bf16[64,768]{1,0:T(8,128)(2,1)} %copy-done.10, bf16[64,768]{1,0:T(8,128)(2,1)} %copy-done.11, f32[1,768]{1,0:T(1,128)} %get-tuple-element.170.gain_ref, f32[3,128,128]{2,1,0:T(8,128)} %tile.32.table_ref), custom_call_target="tpu_custom_call" | custom-call | flops 1024 | bytes 1024 | tf_op jit(solution)/shard_map/pallas_call | solution.py:65
  112.2 23.3 %all_to_all.20.got_ref = bf16[16,144,128]{2,1,0:T(8,128)(2,1)S(1)} all-to-all(bf16[16,144,128]{2,1,0:T(8,128)(2,1)} %get-tuple-element.82), channel_id=1, replica_groups={{0,1,2,3,4,5,6,7,8,9,10,11,12,13,14,15},{16,17,18,19,20,21,22,23,24,25,..., dimensions={0} | all-to-all | bytes 1179648 | tf_op jit(solution)/shard_map/all_to_all | solution.py:698
  138.9 8.2 %shard_map.158 = (bf16[16,48,128]{2,1,0:T(8,128)(2,1)}, f32[6,1,256]{2,1,0:T(1,128)}) custom-call(bf16[16,144,128]{2,1,0:T(8,128)(2,1)} %copy-done, bf16[16,64,128]{2,1,0:T(8,128)(2,1)} %copy-done.5, s32[1024,1]{1,0:T(8,128)} %copy.19.own_seg_ref, s32[1024,1]{1,0:T(8,128)} %copy.20.shared_seg_ref), custom_call_target="tpu_custom_call" | custom-call | flops 1024 | bytes 1024 | tf_op jit(solution)/shard_map/pallas_call | solution.py:65
  147.1 13.2 %all_to_all.21.refs_1_ = bf16[16,48,128]{2,1,0:T(8,128)(2,1)} all-to-all(bf16[16,48,128]{2,1,0:T(8,128)(2,1)} %get-tuple-element.83), channel_id=1, replica_groups={{0,1,2,3,4,5,6,7,8,9,10,11,12,13,14,15},{16,17,18,19,20,21,22,23,24,25,..., dimensions={0} | all-to-all | bytes 393216 | tf_op jit(solution)/shard_map/all_to_all | solution.py:698
  160.3 7.9 %shard_map.159 = (bf16[128,768]{1,0:T(8,128)(2,1)}, bf16[128,768]{1,0:T(8,128)(2,1)}, bf16[128,768]{1,0:T(8,128)(2,1)}, bf16[128,1152]{1,0:T(8,128)(2,1)}, bf16[...) custom-call(bf16[768,4352]{1,0:T(8,128)(2,1)} %all-gather.2.cloned.1.call-done.refs_, ...), custom_call_target="tpu_custom_call" | custom-call | flops 1024 | bytes 1024 | tf_op jit(solution)/shard_map/pallas_call | solution.py:65
  168.2 13.2 %all_to_all.22.d_ref = bf16[16,48,128]{2,1,0:T(8,128)(2,1)} all-to-all(bf16[16,48,128]{2,1,0:T(8,128)(2,1)} %get-tuple-element.94), channel_id=1, replica_groups={{0,1,2,3,4,5,6,7,8,9,10,11,12,13,14,15},{16,17,18,19,20,21,22,23,24,25,..., dimensions={0} | all-to-all | bytes 393216 | tf_op jit(solution)/shard_map/all_to_all | solution.py:698
  181.4 9.7 %shard_map.161 = (bf16[16,144,128]{2,1,0:T(8,128)(2,1)}, bf16[16,64,128]{2,1,0:T(8,128)(2,1)}) custom-call(bf16[16,144,128]{2,1,0:T(8,128)(2,1)} %copy-done, bf16[16,64,128]{2,1,0:T(8,128)(2,1)} %copy-done.5, s32[1024,1]{1,0:T(8,128)} %copy.19.own_seg_ref, s32[1024,1]{1,0:T(8,128)} %copy.20.shared_seg_ref, f32[6,1,256]{2,1,0:T(1,128)} %get-tuple-element.93.total_ref, ...), custom_call_target="tpu_custom_call" | custom-call | flops 1024 | bytes 1024 | tf_op jit(solution)/shard_map/pallas_call | solution.py:65
  191.1 2.8 shard_map.160
  194.0 2.2 add_convert_fusion
  196.2 3.6 all-to-all-start.3
  201.9 10.9 %collective-permute-done.22 = bf16[4,216,128]{2,1,0:T(8,128)(2,1)S(1)} collective-permute-done((bf16[4,216,128]{2,1,0:T(8,128)(2,1)S(1)}, bf16[4,216,128]{2,1,0:T(8,128)(2,1)S(1)}, u32[]{:S(2)}, u32[]{:S(2)}) %collective-permute-start.22) | collective-permute-done | bytes 221216 | tf_op jit(solution)/shard_map/ppermute | solution.py:707
  212.8 5.3 %collective-permute-done.23 = bf16[4,216,128]{2,1,0:T(8,128)(2,1)S(1)} collective-permute-done((bf16[4,216,128]{2,1,0:T(8,128)(2,1)S(1)}, bf16[4,216,128]{2,1,0:T(8,128)(2,1)S(1)}, u32[]{:S(2)}, u32[]{:S(2)}) %collective-permute-start.23) | collective-permute-done | bytes 221216 | tf_op jit(solution)/shard_map/ppermute | solution.py:707
  218.9 4.8 %shard_map.162 = (bf16[128,2304]{1,0:T(8,128)(2,1)}, f32[1,768]{1,0:T(1,128)}, bf16[64,768]{1,0:T(8,128)(2,1)}, bf16[64,768]{1,0:T(8,128)(2,1)}) custom-call(bf16[768,2432]{1,0:T(8,128)(2,1)} %bitcast.23.first_ref, bf16[16,144,128]{2,1,0:T(8,128)(2,1)} %copy-done.2, f32[128,768]{1,0:T(8,128)} %get-tuple-element.100.d_middle_ref, bf16[64,768]{1,0:T(8,128)(2,1)} %copy-done.10, ...), custom_call_target="tpu_custom_call" | custom-call | flops 1024 | bytes 1024 | tf_op jit(solution)/shard_map/pallas_call | solution.py:65
  226.3 5.1 %collective-permute-done.25.refs_2_ = bf16[64,768]{1,0:T(8,128)(2,1)S(1)} collective-permute-done((bf16[64,768]{1,0:T(8,128)(2,1)}, bf16[64,768]{1,0:T(8,128)(2,1)S(1)}, u32[]{:S(2)}, u32[]{:S(2)}) %collective-permute-start.25) | collective-permute-done | bytes 98336 | tf_op jit(solution)/shard_map/ppermute | solution.py:703
  233.6 7.9 %shard_map.163 = (f32[1,768]{1,0:T(1,128)}, f32[128,768]{1,0:T(8,128)}, bf16[128,768]{1,0:T(8,128)(2,1)}, bf16[128,3840]{1,0:T(8,128)(2,1)}) custom-call(bf16[768,4352]{1,0:T(8,128)(2,1)} %all-gather.2.cloned.1.call-done.refs_0_, s32[1]{0:T(128)} %bitcast.37.lower_ref.refs_1_, bf16[64,768]{1,0:T(8,128)(2,1)} %copy-done.19, bf16[64,768]{1,0:T(8,128)(2,1)} %copy-done.20, ...), custom_call_target="tpu_custom_call" | custom-call | flops 1024 | bytes 1024 | tf_op jit(solution)/shard_map/pallas_call | solution.py:65
  241.8 6.1 %shard_map.164 = (bf16[128,768]{1,0:T(8,128)(2,1)}, f32[128,1536]{1,0:T(8,128)}, bf16[128,1536]{1,0:T(8,128)(2,1)}, bf16[128,1536]{1,0:T(8,128)(2,1)}) custom-call(bf16[128,768]{1,0:T(8,128)(2,1)} %get-tuple-element.76.q_ref, bf16[128,1536]{1,0:T(8,128)(2,1)} %copy-done.3, bf16[128,1536]{1,0:T(8,128)(2,1)} %get-tuple-element.77.own_ref, ...), custom_call_target="tpu_custom_call" | custom-call | flops 1024 | bytes 1024 | tf_op jit(solution)/shard_map/pallas_call | solution.py:65
  249.3 3.1 collective-permute-start.28
  254.6 5.3 %shard_map.165 = (bf16[144,2304]{1,0:T(8,128)(2,1)}, bf16[128,768]{1,0:T(8,128)(2,1)}, f32[1,768]{1,0:T(1,128)}) custom-call(s32[1]{0:T(128)} %bitcast.37.lower_ref.refs_1_, bf16[768,2432]{1,0:T(8,128)(2,1)} %bitcast.23.first_ref, bf16[128,768]{1,0:T(8,128)(2,1)} %get-tuple-element.107.dq_ref, f32[128,1536]{1,0:T(8,128)} %get-tuple-element.108.own_ref, ...), custom_call_target="tpu_custom_call" | custom-call | flops 1024 | bytes 1024 | tf_op jit(solution)/shard_map/pallas_call | solution.py:65
  259.9 8.7 %collective-permute-done.30.refs_2_ = bf16[128,3840]{1,0:T(8,128)(2,1)S(1)} collective-permute-done((bf16[128,3840]{1,0:T(8,128)(2,1)}, bf16[128,3840]{1,0:T(8,128)(2,1)S(1)}, u32[]{:S(2)}, u32[]{:S(2)}) %collective-permute-start.30) | collective-permute-done | bytes 983072 | tf_op jit(solution)/shard_map/ppermute | solution.py:707
  268.6 8.8 %collective-permute-start.31 = (bf16[128,3840]{1,0:T(8,128)(2,1)S(1)}, bf16[128,3840]{1,0:T(8,128)(2,1)S(1)}, u32[]{:S(2)}, u32[]{:S(2)}) collective-permute-start(bf16[128,3840]{1,0:T(8,128)(2,1)S(1)} %collective-permute-done.30.refs_2_), channel_id=1, source_target_pairs={{0,1},{1,0},{2,3},{3,2},{4,5},{5,4},{6,7},{7,6},{8,9},{9,8},{10,11... | collective-permute-start | bytes 2949128 | tf_op jit(solution)/shard_map/ppermute | solution.py:707
  281.5 2.4 collective-permute-start.36
  288.1 4.6 %shard_map.166 = (f32[264,768]{1,0:T(8,128)}, bf16[264,768]{1,0:T(8,128)(2,1)}, bf16[264,768]{1,0:T(8,128)(2,1)}, bf16[264,768]{1,0:T(8,128)(2,1)}) custom-call(bf16[128,3840]{1,0:T(8,128)(2,1)} %get-tuple-element.117.refs_0_, bf16[128,3840]{1,0:T(8,128)(2,1)} %copy-done.7, bf16[128,3840]{1,0:T(8,128)(2,1)} %copy-done.6, bf16[128,3840]{1,0:T(8,128)(2,1)} %copy-done.8, ...), custom_call_target="tpu_custom_call" | custom-call | flops 1024 | bytes 1024 | tf_op jit(solution)/shard_map/pallas_call | solution.py:65
  292.6 6.9 %collective-permute-done.36.refs_2_ = bf16[144,2304]{1,0:T(8,128)(2,1)S(1)} collective-permute-done((bf16[144,2304]{1,0:T(8,128)(2,1)}, bf16[144,2304]{1,0:T(8,128)(2,1)S(1)}, u32[]{:S(2)}, u32[]{:S(2)}) %collective-permute-start.36) | collective-permute-done | bytes 663584 | tf_op jit(solution)/shard_map/ppermute | solution.py:707
  299.5 2.5 collective-permute-start.32
  302.0 2.3 collective-permute-start.33
  304.5 1.7 maximum_select_fusion
  306.1 1.7 maximum_select_fusion.1
  308.7 3.3 shard_map.167
  312.0 8.5 %collective-permute-done.32 = bf16[264,768]{1,0:T(8,128)(2,1)S(1)} collective-permute-done((bf16[264,768]{1,0:T(8,128)(2,1)}, bf16[264,768]{1,0:T(8,128)(2,1)S(1)}, u32[]{:S(2)}, u32[]{:S(2)}) %collective-permute-start.32) | collective-permute-done | bytes 405536 | tf_op jit(solution)/shard_map/ppermute | solution.py:707
  320.5 12.3 %collective-permute-done.33 = bf16[264,768]{1,0:T(8,128)(2,1)S(1)} collective-permute-done((bf16[264,768]{1,0:T(8,128)(2,1)}, bf16[264,768]{1,0:T(8,128)(2,1)S(1)}, u32[]{:S(2)}, u32[]{:S(2)}) %collective-permute-start.33) | collective-permute-done | bytes 405536 | tf_op jit(solution)/shard_map/ppermute | solution.py:707
  332.8 2.3 collective-permute-start.40
  335.1 12.7 %collective-permute-start.39 = (bf16[48,2432]{1,0:T(8,128)(2,1)}, bf16[48,2432]{1,0:T(8,128)(2,1)S(1)}, u32[]{:S(2)}, u32[]{:S(2)}) collective-permute-start(bf16[48,2432]{1,0:T(8,128)(2,1)} %get-tuple-element.136), channel_id=1, source_target_pairs={{0,8},{1,9},{2,10},{3,11},{4,12},{5,13},{6,14},{7,15},{8,0},{9,1},... | collective-permute-start | bytes 700424 | tf_op jit(solution)/shard_map/ppermute | solution.py:707
  350.2 12.8 %collective-permute-done.39 = bf16[48,2432]{1,0:T(8,128)(2,1)S(1)} collective-permute-done((bf16[48,2432]{1,0:T(8,128)(2,1)}, bf16[48,2432]{1,0:T(8,128)(2,1)S(1)}, u32[]{:S(2)}, u32[]{:S(2)}) %collective-permute-start.39) | collective-permute-done | bytes 233504 | tf_op jit(solution)/shard_map/ppermute | solution.py:707
  (184 shorter events, 58.4 us)
Async XLA Ops:
  7.2 86.6 %all-gather.2.cloned.1.call-start = ((), (), s32[]{:S(2)}) async-start(), calls=%async_computation.4 | async-start | bytes 7102464 | tf_op jit(solution)/shard_map/all_gather | solution.py:884
  9.0 11.7 %collective-permute-start.1 = (bf16[48,2432]{1,0:T(8,128)(2,1)}, bf16[48,2432]{1,0:T(8,128)(2,1)S(1)}, u32[]{:S(2)}, u32[]{:S(2)}) collective-permute-start(bf16[48,2432]{1,0:T(8,128)(2,1)} %shard_map.153), channel_id=1, source_target_pairs={{0,2},{1,3},{2,0},{3,1},{4,6},{5,7},{6,4},{7,5},{8,10},{9,11},{10,... | collective-permute-start | bytes 700424 | tf_op jit(solution)/shard_map/ppermute | solution.py:707
  12.0 13.1 %collective-permute-start.2 = (bf16[48,2432]{1,0:T(8,128)(2,1)}, bf16[48,2432]{1,0:T(8,128)(2,1)S(1)}, u32[]{:S(2)}, u32[]{:S(2)}) collective-permute-start(bf16[48,2432]{1,0:T(8,128)(2,1)} %shard_map.153), channel_id=1, source_target_pairs={{0,4},{1,5},{2,6},{3,7},{4,0},{5,1},{6,2},{7,3},{8,12},{9,13},{10,... | collective-permute-start | bytes 700424 | tf_op jit(solution)/shard_map/ppermute | solution.py:707
  13.5 19.7 %collective-permute-start.3 = (bf16[48,2432]{1,0:T(8,128)(2,1)}, bf16[48,2432]{1,0:T(8,128)(2,1)S(1)}, u32[]{:S(2)}, u32[]{:S(2)}) collective-permute-start(bf16[48,2432]{1,0:T(8,128)(2,1)} %shard_map.153), channel_id=1, source_target_pairs={{0,8},{1,9},{2,10},{3,11},{4,12},{5,13},{6,14},{7,15},{8,0},{9,1},... | collective-permute-start | bytes 700424 | tf_op jit(solution)/shard_map/ppermute | solution.py:707
  16.1 17.7 %collective-permute-start.4 = (bf16[48,2432]{1,0:T(8,128)(2,1)}, bf16[48,2432]{1,0:T(8,128)(2,1)S(1)}, u32[]{:S(2)}, u32[]{:S(2)}) collective-permute-start(bf16[48,2432]{1,0:T(8,128)(2,1)} %shard_map.153), channel_id=1, source_target_pairs={{0,12},{1,13},{2,14},{3,15},{4,8},{5,9},{6,10},{7,11},{8,4},{9,5},... | collective-permute-start | bytes 700424 | tf_op jit(solution)/shard_map/ppermute | solution.py:707
  17.1 1.2 collective-permute-start
  18.2 30.0 %collective-permute-start.8 = (bf16[48,2432]{1,0:T(8,128)(2,1)}, bf16[48,2432]{1,0:T(8,128)(2,1)S(1)}, u32[]{:S(2)}, u32[]{:S(2)}) collective-permute-start(bf16[48,2432]{1,0:T(8,128)(2,1)} %shard_map.153), channel_id=1, source_target_pairs={{0,1},{1,0},{2,3},{3,2},{4,5},{5,4},{6,7},{7,6},{8,9},{9,8},{10,11... | collective-permute-start | bytes 700424 | tf_op jit(solution)/shard_map/ppermute | solution.py:707
  24.8 24.6 %collective-permute-start.9 = (bf16[48,2432]{1,0:T(8,128)(2,1)S(1)}, bf16[48,2432]{1,0:T(8,128)(2,1)S(1)}, u32[]{:S(2)}, u32[]{:S(2)}) collective-permute-start(bf16[48,2432]{1,0:T(8,128)(2,1)S(1)} %collective-permute-done.1), channel_id=1, source_target_pairs={{0,1},{1,0},{2,3},{3,2},{4,5},{5,4},{6,7},{7,6},{8,9},{9,8},{10,11... | collective-permute-start | bytes 700424 | tf_op jit(solution)/shard_map/ppermute | solution.py:707
  25.1 13.1 %collective-permute-start.5 = (bf16[48,2432]{1,0:T(8,128)(2,1)S(1)}, bf16[48,2432]{1,0:T(8,128)(2,1)S(1)}, u32[]{:S(2)}, u32[]{:S(2)}) collective-permute-start(bf16[48,2432]{1,0:T(8,128)(2,1)S(1)} %collective-permute-done.2), channel_id=1, source_target_pairs={{0,2},{1,3},{2,0},{3,1},{4,6},{5,7},{6,4},{7,5},{8,10},{9,11},{10,... | collective-permute-start | bytes 700424 | tf_op jit(solution)/shard_map/ppermute | solution.py:707
  33.3 10.3 %collective-permute-start.6 = (bf16[48,2432]{1,0:T(8,128)(2,1)S(1)}, bf16[48,2432]{1,0:T(8,128)(2,1)S(1)}, u32[]{:S(2)}, u32[]{:S(2)}) collective-permute-start(bf16[48,2432]{1,0:T(8,128)(2,1)S(1)} %collective-permute-done.3), channel_id=1, source_target_pairs={{0,2},{1,3},{2,0},{3,1},{4,6},{5,7},{6,4},{7,5},{8,10},{9,11},{10,... | collective-permute-start | bytes 700424 | tf_op jit(solution)/shard_map/ppermute | solution.py:707
  33.8 13.7 %collective-permute-start.7 = (bf16[48,2432]{1,0:T(8,128)(2,1)S(1)}, bf16[48,2432]{1,0:T(8,128)(2,1)S(1)}, u32[]{:S(2)}, u32[]{:S(2)}) collective-permute-start(bf16[48,2432]{1,0:T(8,128)(2,1)S(1)} %collective-permute-done.4), channel_id=1, source_target_pairs={{0,2},{1,3},{2,0},{3,1},{4,6},{5,7},{6,4},{7,5},{8,10},{9,11},{10,... | collective-permute-start | bytes 700424 | tf_op jit(solution)/shard_map/ppermute | solution.py:707
  38.2 12.0 %collective-permute-start.10 = (bf16[48,2432]{1,0:T(8,128)(2,1)S(1)}, bf16[48,2432]{1,0:T(8,128)(2,1)S(1)}, u32[]{:S(2)}, u32[]{:S(2)}) collective-permute-start(bf16[48,2432]{1,0:T(8,128)(2,1)S(1)} %collective-permute-done.2), channel_id=1, source_target_pairs={{0,1},{1,0},{2,3},{3,2},{4,5},{5,4},{6,7},{7,6},{8,9},{9,8},{10,11... | collective-permute-start | bytes 700424 | tf_op jit(solution)/shard_map/ppermute | solution.py:707
  43.6 8.5 %collective-permute-start.12 = (bf16[48,2432]{1,0:T(8,128)(2,1)S(1)}, bf16[48,2432]{1,0:T(8,128)(2,1)S(1)}, u32[]{:S(2)}, u32[]{:S(2)}) collective-permute-start(bf16[48,2432]{1,0:T(8,128)(2,1)S(1)} %collective-permute-done.3), channel_id=1, source_target_pairs={{0,1},{1,0},{2,3},{3,2},{4,5},{5,4},{6,7},{7,6},{8,9},{9,8},{10,11... | collective-permute-start | bytes 700424 | tf_op jit(solution)/shard_map/ppermute | solution.py:707
  47.5 6.0 %collective-permute-start.14 = (bf16[48,2432]{1,0:T(8,128)(2,1)S(1)}, bf16[48,2432]{1,0:T(8,128)(2,1)S(1)}, u32[]{:S(2)}, u32[]{:S(2)}) collective-permute-start(bf16[48,2432]{1,0:T(8,128)(2,1)S(1)} %collective-permute-done.4), channel_id=1, source_target_pairs={{0,1},{1,0},{2,3},{3,2},{4,5},{5,4},{6,7},{7,6},{8,9},{9,8},{10,11... | collective-permute-start | bytes 700424 | tf_op jit(solution)/shard_map/ppermute | solution.py:707
  48.2 3.2 collective-permute-start.11
  49.4 14.1 %copy-start.22 = (s32[2,64]{1,0:T(2,128)S(1)}, s32[2,64]{1,0:T(2,128)}, u32[]{:S(2)}) copy-start(s32[2,64]{1,0:T(2,128)} %ids_ref.1) | copy-start | bytes 1540
  49.4 3.4 collective-permute-start.13
  50.2 4.0 %collective-permute-start.15 = (bf16[48,2432]{1,0:T(8,128)(2,1)S(1)}, bf16[48,2432]{1,0:T(8,128)(2,1)S(1)}, u32[]{:S(2)}, u32[]{:S(2)}) collective-permute-start(bf16[48,2432]{1,0:T(8,128)(2,1)S(1)} %collective-permute-done.7), channel_id=1, source_target_pairs={{0,1},{1,0},{2,3},{3,2},{4,5},{5,4},{6,7},{7,6},{8,9},{9,8},{10,11... | collective-permute-start | bytes 700424 | tf_op jit(solution)/shard_map/ppermute | solution.py:707
  58.9 6.9 %collective-permute-start.16 = (bf16[128,1536]{1,0:T(8,128)(2,1)}, bf16[128,1536]{1,0:T(8,128)(2,1)S(1)}, u32[]{:S(2)}, u32[]{:S(2)}) collective-permute-start(bf16[128,1536]{1,0:T(8,128)(2,1)} %get-tuple-element.77.own_ref), channel_id=1, source_target_pairs={{0,1},{1,2},{2,3},{3,4},{4,5},{5,6},{6,7},{7,8},{8,9},{9,10},{10,1... | collective-permute-start | bytes 1179656 | tf_op jit(solution)/shard_map/ppermute | solution.py:931
  61.1 4.8 %collective-permute-start.17 = (bf16[128,1536]{1,0:T(8,128)(2,1)}, bf16[128,1536]{1,0:T(8,128)(2,1)S(1)}, u32[]{:S(2)}, u32[]{:S(2)}) collective-permute-start(bf16[128,1536]{1,0:T(8,128)(2,1)} %get-tuple-element.77.own_ref), channel_id=1, source_target_pairs={{1,0},{2,1},{3,2},{4,3},{5,4},{6,5},{7,6},{8,7},{9,8},{10,9},{11,1... | collective-permute-start | bytes 1179656 | tf_op jit(solution)/shard_map/ppermute | solution.py:933
  99.3 6.9 %collective-permute-start.18 = (bf16[64,768]{1,0:T(8,128)(2,1)}, bf16[64,768]{1,0:T(8,128)(2,1)S(1)}, u32[]{:S(2)}, u32[]{:S(2)}) collective-permute-start(bf16[64,768]{1,0:T(8,128)(2,1)} %get-tuple-element.80), channel_id=1, source_target_pairs={{0,16},{1,17},{2,18},{3,19},{4,20},{5,21},{6,22},{7,23},{8,24},{9,... | collective-permute-start | bytes 294920 | tf_op jit(solution)/shard_map/ppermute | solution.py:703
  102.7 4.9 %collective-permute-start.19 = (bf16[64,768]{1,0:T(8,128)(2,1)}, bf16[64,768]{1,0:T(8,128)(2,1)S(1)}, u32[]{:S(2)}, u32[]{:S(2)}) collective-permute-start(bf16[64,768]{1,0:T(8,128)(2,1)} %get-tuple-element.81), channel_id=1, source_target_pairs={{0,16},{1,17},{2,18},{3,19},{4,20},{5,21},{6,22},{7,23},{8,24},{9,... | collective-permute-start | bytes 294920 | tf_op jit(solution)/shard_map/ppermute | solution.py:703
  135.6 2.6 collective-permute-start.20
  191.0 2.9 collective-permute-start.24
  196.2 21.9 %all-to-all-start.3 = ((bf16[16,144,128]{2,1,0:T(8,128)(2,1)}), bf16[16,144,128]{2,1,0:T(8,128)(2,1)S(1)}, u32[]{:S(2)}, u32[]{:S(2)}) async-start(bf16[16,144,128]{2,1,0:T(8,128)(2,1)} %add_convert_fusion), calls=%async_computation.3 | async-start | bytes 1179648 | tf_op jit(solution)/shard_map/all_to_all | solution.py:698
  199.8 2.0 collective-permute-start.21
  200.3 12.5 %collective-permute-start.22 = (bf16[4,216,128]{2,1,0:T(8,128)(2,1)S(1)}, bf16[4,216,128]{2,1,0:T(8,128)(2,1)S(1)}, u32[]{:S(2)}, u32[]{:S(2)}) collective-permute-start(bf16[4,216,128]{2,1,0:T(8,128)(2,1)S(1)} %get-tuple-element.147), channel_id=1, source_target_pairs={{0,2},{1,3},{2,0},{3,1},{4,6},{5,7},{6,4},{7,5},{8,10},{9,11},{10,... | collective-permute-start | bytes 663560 | tf_op jit(solution)/shard_map/ppermute | solution.py:707
  201.9 16.2 %collective-permute-start.23 = (bf16[4,216,128]{2,1,0:T(8,128)(2,1)S(1)}, bf16[4,216,128]{2,1,0:T(8,128)(2,1)S(1)}, u32[]{:S(2)}, u32[]{:S(2)}) collective-permute-start(bf16[4,216,128]{2,1,0:T(8,128)(2,1)S(1)} %get-tuple-element.146), channel_id=1, source_target_pairs={{0,3},{1,2},{2,1},{3,0},{4,7},{5,6},{6,5},{7,4},{8,11},{9,10},{10,... | collective-permute-start | bytes 663560 | tf_op jit(solution)/shard_map/ppermute | solution.py:707
  223.7 7.7 %collective-permute-start.25 = (bf16[64,768]{1,0:T(8,128)(2,1)}, bf16[64,768]{1,0:T(8,128)(2,1)S(1)}, u32[]{:S(2)}, u32[]{:S(2)}) collective-permute-start(bf16[64,768]{1,0:T(8,128)(2,1)} %get-tuple-element.101), channel_id=1, source_target_pairs={{16,0},{17,1},{18,2},{19,3},{20,4},{21,5},{22,6},{23,7},{24,8},{25... | collective-permute-start | bytes 294920 | tf_op jit(solution)/shard_map/ppermute | solution.py:703
  225.0 7.9 %collective-permute-start.26 = (bf16[64,768]{1,0:T(8,128)(2,1)}, bf16[64,768]{1,0:T(8,128)(2,1)S(1)}, u32[]{:S(2)}, u32[]{:S(2)}) collective-permute-start(bf16[64,768]{1,0:T(8,128)(2,1)} %get-tuple-element.102), channel_id=1, source_target_pairs={{16,0},{17,1},{18,2},{19,3},{20,4},{21,5},{22,6},{23,7},{24,8},{25... | collective-permute-start | bytes 294920 | tf_op jit(solution)/shard_map/ppermute | solution.py:703
  241.4 27.1 %collective-permute-start.30 = (bf16[128,3840]{1,0:T(8,128)(2,1)}, bf16[128,3840]{1,0:T(8,128)(2,1)S(1)}, u32[]{:S(2)}, u32[]{:S(2)}) collective-permute-start(bf16[128,3840]{1,0:T(8,128)(2,1)} %get-tuple-element.117.refs_0_), channel_id=1, source_target_pairs={{0,2},{1,3},{2,0},{3,1},{4,6},{5,7},{6,4},{7,5},{8,10},{9,11},{10,... | collective-permute-start | bytes 2949128 | tf_op jit(solution)/shard_map/ppermute | solution.py:707
  248.0 5.6 %collective-permute-start.27 = (bf16[128,1536]{1,0:T(8,128)(2,1)}, bf16[128,1536]{1,0:T(8,128)(2,1)S(1)}, u32[]{:S(2)}, u32[]{:S(2)}) collective-permute-start(bf16[128,1536]{1,0:T(8,128)(2,1)} %get-tuple-element.109), channel_id=1, source_target_pairs={{1,0},{2,1},{3,2},{4,3},{5,4},{6,5},{7,6},{8,7},{9,8},{10,9},{11,1... | collective-permute-start | bytes 1179656 | tf_op jit(solution)/shard_map/ppermute | solution.py:1081
  249.3 4.6 %collective-permute-start.28 = (bf16[128,1536]{1,0:T(8,128)(2,1)}, bf16[128,1536]{1,0:T(8,128)(2,1)S(1)}, u32[]{:S(2)}, u32[]{:S(2)}) collective-permute-start(bf16[128,1536]{1,0:T(8,128)(2,1)} %get-tuple-element.110), channel_id=1, source_target_pairs={{0,1},{1,2},{2,3},{3,4},{4,5},{5,6},{6,7},{7,8},{8,9},{9,10},{10,1... | collective-permute-start | bytes 1179656 | tf_op jit(solution)/shard_map/ppermute | solution.py:1082
  252.3 34.4 %collective-permute-start.29 = (bf16[128,3840]{1,0:T(8,128)(2,1)}, bf16[128,3840]{1,0:T(8,128)(2,1)S(1)}, u32[]{:S(2)}, u32[]{:S(2)}) collective-permute-start(bf16[128,3840]{1,0:T(8,128)(2,1)} %get-tuple-element.117.refs_0_), channel_id=1, source_target_pairs={{0,1},{1,0},{2,3},{3,2},{4,5},{5,4},{6,7},{7,6},{8,9},{9,8},{10,11... | collective-permute-start | bytes 2949128 | tf_op jit(solution)/shard_map/ppermute | solution.py:707
  268.6 18.2 %copy-start.6 = (bf16[128,3840]{1,0:T(8,128)(2,1)}, bf16[128,3840]{1,0:T(8,128)(2,1)S(1)}, u32[]{:S(2)}) copy-start(bf16[128,3840]{1,0:T(8,128)(2,1)S(1)} %collective-permute-done.30.refs_2_) | copy-start | bytes 2949124
  268.6 18.2 %collective-permute-start.31 = (bf16[128,3840]{1,0:T(8,128)(2,1)S(1)}, bf16[128,3840]{1,0:T(8,128)(2,1)S(1)}, u32[]{:S(2)}, u32[]{:S(2)}) collective-permute-start(bf16[128,3840]{1,0:T(8,128)(2,1)S(1)} %collective-permute-done.30.refs_2_), channel_id=1, source_target_pairs={{0,1},{1,0},{2,3},{3,2},{4,5},{5,4},{6,7},{7,6},{8,9},{9,8},{10,11... | collective-permute-start | bytes 2949128 | tf_op jit(solution)/shard_map/ppermute | solution.py:707
  281.5 18.0 %collective-permute-start.36 = (bf16[144,2304]{1,0:T(8,128)(2,1)}, bf16[144,2304]{1,0:T(8,128)(2,1)S(1)}, u32[]{:S(2)}, u32[]{:S(2)}) collective-permute-start(bf16[144,2304]{1,0:T(8,128)(2,1)} %get-tuple-element.128.refs_0_), channel_id=1, source_target_pairs={{0,2},{1,3},{2,0},{3,1},{4,6},{5,7},{6,4},{7,5},{8,10},{9,11},{10,... | collective-permute-start | bytes 1990664 | tf_op jit(solution)/shard_map/ppermute | solution.py:707
  286.0 20.1 %copy-start.18 = (bf16[128,768]{1,0:T(8,128)(2,1)S(1)}, bf16[128,768]{1,0:T(8,128)(2,1)}, u32[]{:S(2)}) copy-start(bf16[128,768]{1,0:T(8,128)(2,1)} %get-tuple-element.116) | copy-start | bytes 589828
  286.7 21.1 %collective-permute-start.35 = (bf16[144,2304]{1,0:T(8,128)(2,1)}, bf16[144,2304]{1,0:T(8,128)(2,1)}, u32[]{:S(2)}, u32[]{:S(2)}) collective-permute-start(bf16[144,2304]{1,0:T(8,128)(2,1)} %get-tuple-element.128.refs_0_), channel_id=1, source_target_pairs={{0,1},{1,0},{2,3},{3,2},{4,5},{5,4},{6,7},{7,6},{8,9},{9,8},{10,11... | collective-permute-start | bytes 1990664 | tf_op jit(solution)/shard_map/ppermute | solution.py:707
  292.6 55.2 %copy-start.12 = (f32[264,768]{1,0:T(8,128)S(1)}, f32[264,768]{1,0:T(8,128)}, u32[]{:S(2)}) copy-start(f32[264,768]{1,0:T(8,128)} %get-tuple-element.138) | copy-start | bytes 2433028
  299.5 8.3 %collective-permute-start.37 = (bf16[144,2304]{1,0:T(8,128)(2,1)S(1)}, bf16[144,2304]{1,0:T(8,128)(2,1)S(1)}, u32[]{:S(2)}, u32[]{:S(2)}) collective-permute-start(bf16[144,2304]{1,0:T(8,128)(2,1)S(1)} %collective-permute-done.36.refs_2_), channel_id=1, source_target_pairs={{0,1},{1,0},{2,3},{3,2},{4,5},{5,4},{6,7},{7,6},{8,9},{9,8},{10,11... | collective-permute-start | bytes 1990664 | tf_op jit(solution)/shard_map/ppermute | solution.py:707
  299.5 21.0 %collective-permute-start.32 = (bf16[264,768]{1,0:T(8,128)(2,1)}, bf16[264,768]{1,0:T(8,128)(2,1)S(1)}, u32[]{:S(2)}, u32[]{:S(2)}) collective-permute-start(bf16[264,768]{1,0:T(8,128)(2,1)} %get-tuple-element.125), channel_id=1, source_target_pairs={{0,4},{1,5},{2,6},{3,7},{4,0},{5,1},{6,2},{7,3},{8,12},{9,13},{10,... | collective-permute-start | bytes 1216520 | tf_op jit(solution)/shard_map/ppermute | solution.py:707
  302.0 30.7 %collective-permute-start.33 = (bf16[264,768]{1,0:T(8,128)(2,1)}, bf16[264,768]{1,0:T(8,128)(2,1)S(1)}, u32[]{:S(2)}, u32[]{:S(2)}) collective-permute-start(bf16[264,768]{1,0:T(8,128)(2,1)} %get-tuple-element.126), channel_id=1, source_target_pairs={{0,8},{1,9},{2,10},{3,11},{4,12},{5,13},{6,14},{7,15},{8,0},{9,1},... | collective-permute-start | bytes 1216520 | tf_op jit(solution)/shard_map/ppermute | solution.py:707
  304.4 28.4 %collective-permute-start.34 = (bf16[264,768]{1,0:T(8,128)(2,1)}, bf16[264,768]{1,0:T(8,128)(2,1)S(1)}, u32[]{:S(2)}, u32[]{:S(2)}) collective-permute-start(bf16[264,768]{1,0:T(8,128)(2,1)} %get-tuple-element.127), channel_id=1, source_target_pairs={{0,12},{1,13},{2,14},{3,15},{4,8},{5,9},{6,10},{7,11},{8,4},{9,5},... | collective-permute-start | bytes 1216520 | tf_op jit(solution)/shard_map/ppermute | solution.py:707
  312.0 51.0 %copy-start.15 = (f32[48,2432]{1,0:T(8,128)S(1)}, f32[48,2432]{1,0:T(8,128)}, u32[]{:S(2)}) copy-start(f32[48,2432]{1,0:T(8,128)} %get-tuple-element.134) | copy-start | bytes 1400836
  332.8 17.4 %collective-permute-start.40 = (bf16[48,2432]{1,0:T(8,128)(2,1)}, bf16[48,2432]{1,0:T(8,128)(2,1)S(1)}, u32[]{:S(2)}, u32[]{:S(2)}) collective-permute-start(bf16[48,2432]{1,0:T(8,128)(2,1)} %get-tuple-element.137), channel_id=1, source_target_pairs={{0,12},{1,13},{2,14},{3,15},{4,8},{5,9},{6,10},{7,11},{8,4},{9,5},... | collective-permute-start | bytes 700424 | tf_op jit(solution)/shard_map/ppermute | solution.py:707
  335.1 27.9 %collective-permute-start.39 = (bf16[48,2432]{1,0:T(8,128)(2,1)}, bf16[48,2432]{1,0:T(8,128)(2,1)S(1)}, u32[]{:S(2)}, u32[]{:S(2)}) collective-permute-start(bf16[48,2432]{1,0:T(8,128)(2,1)} %get-tuple-element.136), channel_id=1, source_target_pairs={{0,8},{1,9},{2,10},{3,11},{4,12},{5,13},{6,14},{7,15},{8,0},{9,1},... | collective-permute-start | bytes 700424 | tf_op jit(solution)/shard_map/ppermute | solution.py:707
  347.8 15.2 %collective-permute-start.38 = (bf16[48,2432]{1,0:T(8,128)(2,1)}, bf16[48,2432]{1,0:T(8,128)(2,1)S(1)}, u32[]{:S(2)}, u32[]{:S(2)}) collective-permute-start(bf16[48,2432]{1,0:T(8,128)(2,1)} %get-tuple-element.135), channel_id=1, source_target_pairs={{0,4},{1,5},{2,6},{3,7},{4,0},{5,1},{6,2},{7,3},{8,12},{9,13},{10,... | collective-permute-start | bytes 700424 | tf_op jit(solution)/shard_map/ppermute | solution.py:707
  (18 other events, 43.4 us)
Sparse Core Ops, SparseCore 0:
  20.8 72.8 all-gather.1

commit v7 on v6

--- a/solution.py
+++ b/solution.py
@@ -75,7 +75,7 @@
         cost_estimate=pl.CostEstimate(
             flops=2**10, bytes_accessed=2**10, transcendentals=0
         ),
-        compiler_params=pltpu.CompilerParams(vmem_limit_bytes=60 * 2**20),
+        compiler_params=pltpu.CompilerParams(vmem_limit_bytes=48 * 2**20),
     )(*args)
 
 
@@ -325,13 +325,6 @@
     return jnp.concatenate([ref[...] for ref in refs], 0)
 
 
-def store_right(right_ref, d_gate_up, d_attn, d_mlp):
-    inner, width = d_gate_up.shape[1], d_attn.shape[1]
-    right_ref[:, :inner] = d_gate_up
-    right_ref[:, inner : inner + width] = d_attn
-    right_ref[:, inner + width :] = d_mlp
-
-
 def store_chunks(refs, rows):
     size = rows.shape[0] // len(refs)
     for i, ref in enumerate(refs):
@@ -502,7 +495,8 @@
 
     @pl.when(lower_ref[0] == 1)
     def _():
-        store_right(right_ref, d_gate_up, d_attn, upstream)
+        right_ref[:, : 2 * half] = d_gate_up
+        right_ref[:, 2 * half :] = d_attn
 
     @pl.when(lower_ref[0] == 0)
     def _():
@@ -661,7 +655,8 @@
     d_gate_up, gain_grad, d_middle, d_attn, d_attended = mlp_backward(
         up_ref[...], middle, gate, up, gain, weights
     )
-    store_right(right_ref, d_gate_up, d_attn, up_ref[...])
+    right_ref[:, : d_gate_up.shape[1]] = d_gate_up
+    right_ref[:, d_gate_up.shape[1] :] = d_attn
     gain_out_ref[...] = gain_grad
     d_middle_ref[...] = d_middle
     pack_folded(chunks_of(d_attended), sent_ref, 0)
@@ -752,78 +747,72 @@
         base += size
 
 
-def early_body(shard, *refs):
-    refs, outs = refs[:-4], refs[-4:]
-    rights, n2, mixed, att = (refs[4 * i : 4 * i + 4] for i in range(4))
+def left_rows_of(refs, rows):
+    start, end = rows
+    parts = [
+        jnp.concatenate([ref[p, start:end].astype(F32) for p in range(4)], 0).astype(BF) for ref in refs
+    ]
+    return jnp.concatenate(parts, 1)
+
+
+def by_plane(result, base, outs, columns=slice(None)):
+    keep, keep_far, send = outs
+    rows = result.shape[0] // 4
+    half = send.shape[0] // 2
+    here = slice(base, base + rows)
+    keep[here, columns] = result[:rows]
+    keep_far[here, columns] = result[2 * rows : 3 * rows]
+    send[here, columns] = result[rows : 2 * rows].astype(BF)
+    send[half + base : half + base + rows, columns] = result[3 * rows :].astype(BF)
+
+
+def early_body(terms, *refs):
+    refs, outs = refs[:-3], refs[-3:]
+    rights, lefts = refs[:4], refs[4:]
     width = outs[0].shape[1]
-    inner = rights[0].shape[1] - 2 * width
-
-    def product(lefts, start, end):
-        left = jnp.concatenate([ref[...] for ref in lefts], 1)
-        return dot(left, jnp.concatenate([ref[:, start:end] for ref in rights], 0))
-
     base = 0
-    for lefts, start, end in (
-        (n2, 0, inner),
-        (mixed, inner + width, inner + 2 * width),
-        (att, inner, inner + width),
-    ):
-        result = product(lefts, start, end)
-        rows = result.shape[0] // 4
+    for rows, (start, end) in terms:
+        right = jnp.concatenate([ref[:, start:end] for ref in rights], 0)
+        result = dot(left_rows_of(lefts, rows), right)
         for column in range(0, end - start, width):
-            for plane, out_ref in enumerate(outs):
-                part = result[plane * rows : (plane + 1) * rows, column : column + width]
-                out_ref[base : base + rows] = part.astype(out_ref.dtype)
-            base += rows
-
-
-def late_body(place_ref, *refs):
-    refs, (outs, scr) = refs[:-5], (refs[-5:-1], refs[-1])
+            by_plane(result[:, column : column + width], base, outs)
+            base += result.shape[0] // 4
+
+
+def late_body(rows, place_ref, *refs):
+    refs, outs, scr = refs[:-4], refs[-4:-1], refs[-1]
     rights, lefts = refs[:4], refs[4:]
-    tokens = lefts[0].shape[1]
+    tokens = lefts[0].shape[2]
     columns = rights[0].shape[1]
     width = columns // 3
-    rows = outs[0].shape[0]
-    left = jnp.concatenate([ref[...] for ref in lefts], 1)
-    product = dot(left, jnp.concatenate([ref[:tokens] for ref in rights], 0))
+    size = outs[0].shape[0]
+    right = jnp.concatenate([ref[:tokens] for ref in rights], 0)
+    by_plane(dot(left_rows_of(lefts, rows), right), 0, outs, slice(0, columns))
     tail = sum(ref[tokens:, :width].astype(F32) for ref in rights)
     both = jnp.concatenate([tail, jnp.zeros((LANES - EXTRA, width), F32)], 0).T
     lane = lax.broadcasted_iota(jnp.int32, (1, LANES), 1)
     lows = pltpu.roll(both, LANES - 1, 1)
     scr[...] = jnp.where(lane % 2 == 0, both + lows, 0.0)
-    for plane, out_ref in enumerate(outs):
-        part = product[plane * rows : (plane + 1) * rows]
-        out_ref[:, :columns] = part.astype(out_ref.dtype)
+    gains = []
+    for plane in range(4):
         d = (place_ref[0] // 4 ^ plane) * 4 + place_ref[0] % 4
-        start = pl.multiple_of(d * rows, 16)
-        out_ref[:, columns:] = scr[pl.ds(start, rows)].astype(out_ref.dtype)
-
-
-def flat_rows(parts):
-    return [part.reshape(-1, part.shape[-1]) for part in parts]
-
-
-def four_planes(shape):
-    return [(shape, F32)] + [(shape, BF)] * 3
-
-
-def plane_parts(rows, count, after=None):
-    across = partner(rows, 2, count)
-    beside = partner(rows, 1, count)
-    if after is not None:
-        across, _ = lax.optimization_barrier((across, after))
-    return [rows, beside, across, partner(across, 1, count)]
-
-
-def sent_planes(blocks, count):
-    return [blocks[0]] + [partner(item, 4 * (z + 1), count) for z, item in enumerate(blocks[1:])]
-
-
-def sum_planes(blocks):
-    total = blocks[0]
-    for item in blocks[1:]:
-        total = total + item.astype(F32)
-    return total
+        gains.append(scr[pl.ds(pl.multiple_of(d * size, 16), size)])
+    by_plane(jnp.concatenate(gains, 0), 0, outs, slice(columns, columns + LANES))
+
+
+def three_parts(shape):
+    return [(shape, F32), (shape, F32), ((2 * shape[0], shape[1]), BF)]
+
+
+def first_hop(blocks, count):
+    keep, keep_far, send = blocks
+    got = partner(send, 4, count)
+    half = keep.shape[0]
+    return keep + got[:half].astype(F32), (keep_far + got[half:].astype(F32)).astype(BF)
+
+
+def second_hop(near, far, count):
+    return near + partner(far, 8, count).astype(F32)
 
 
 def over_groups(rows, count):
@@ -987,7 +976,7 @@
             ((rows, width), BF),
             ((rows, width), BF),
             ((rows, hidden), BF),
-            ((rows, inner + 2 * width), BF),
+            ((rows, inner + width), BF),
             ((1, width), F32),
             ((rows, width), F32),
             ((GROUP, fold, LANES), BF),
@@ -996,6 +985,24 @@
         [pltpu.VMEM((hidden, width), BF)],
     )
     d_folded = exchange(sent, count)
+    pairs = ((normed_0, normed_1), (att_0, att_1), (n2_0, n2_1), (mixed_0, mixed_1))
+    left_total = 3 * shard_total + hidden_total
+    if count == GROUP:
+        (left,) = on_core(
+            left_body,
+            [((4, 4, left_total, rows), BF)],
+            (lower_flag, group_pos[None], *(item for pair in pairs for item in pair)),
+            (),
+            [pltpu.SMEM] * 2 + [pltpu.VMEM] * 8,
+        )
+        left, d_folded = lax.optimization_barrier((left, d_folded))
+        left = [left[0]] + [partner(left[apart], apart, count) for apart in range(1, 4)]
+    else:
+        left = [
+            plane_rows(jnp.where(lower, a, b).T.reshape(count, -1, rows), group_pos, count)
+            for a, b in pairs
+        ]
+        left = [jnp.concatenate([i.reshape(4, -1, rows) for i in items], 1) for items in zip(*left)]
     sent, to_beside = on_core(
         global_backward_body,
         [((GROUP, 3 * fold, LANES), BF), ((GROUP, 2 * half, LANES), BF)],
@@ -1008,22 +1015,6 @@
             pltpu.VMEM((2, keys, LANES), F32),
         ],
     )
-    pairs = ((normed_0, normed_1), (att_0, att_1), (n2_0, n2_1), (mixed_0, mixed_1))
-    left_rows = 3 * shard + mlp_out_weight.shape[1]
-    if count == GROUP:
-        (left,) = on_core(
-            left_body,
-            [((4, 4, left_rows, rows), BF)],
-            (lower_flag, group_pos[None], *(item for pair in pairs for item in pair)),
-            (),
-            [pltpu.SMEM] * 2 + [pltpu.VMEM] * 8,
-        )
-        left, sent = lax.optimization_barrier((left, sent))
-        left = [left[0]] + [partner(left[apart], apart, count) for apart in range(1, 4)]
-        left = [item[:, None] for item in left]
-    else:
-        left = [jnp.where(lower, a, b).T.reshape(count, -1, rows) for a, b in pairs]
-        left = plane_rows(jnp.concatenate(left, 1), group_pos, count)
     back = partner(to_beside, 1, count)
     gap = 3 * fold - half - row_count - half
     back = jnp.concatenate(
@@ -1036,18 +1027,9 @@
         1,
     )
     sent = (sent.astype(F32) + back.astype(F32)).astype(BF)
+    left, sent = lax.optimization_barrier((left, sent))
     got = exchange(sent, count)
 
-    left, got = lax.optimization_barrier((left, got))
-    n1, att, n2, mixed = (
-        [part[:, :, start:end] for part in left]
-        for start, end in (
-            (0, shard),
-            (shard, 2 * shard),
-            (2 * shard, 3 * shard),
-            (3 * shard, left_rows),
-        )
-    )
     d_proj_1, gain_attn_1, *grad_1 = on_core(
         global_finish_body,
         [((rows, 3 * width), BF), ((1, width), F32)] + [((row_count, width), BF)] * micro_count,
@@ -1055,19 +1037,33 @@
     )
 
     up_0 = to_other_section(grad_1, -1)
+    d_mlp = jnp.concatenate(
+        [jnp.where(lower, a, up_1[i * row_count :][:row_count]) for i, a in enumerate(up_0)]
+    )
+    across_mlp, beside_mlp = partner(d_mlp, 2, count), partner(d_mlp, 1, count)
     gain_mlp_0, d_mid_0, d_att_0, right = on_core(
         local_back_middle_body,
         [
             ((1, width), F32),
             ((rows, width), F32),
             ((rows, width), BF),
-            ((rows, inner + 2 * width), BF),
+            ((rows, inner + width), BF),
         ],
         (*others, lower_flag, *up_0, middle_0, gate_up_0, gain_mlp, right_1),
         [pltpu.VMEM((hidden, width), BF)],
         [pltpu.VMEM] * len(others) + [pltpu.SMEM] + [pltpu.VMEM] * 6,
     )
+    d_att_0, right, across_mlp = lax.optimization_barrier((d_att_0, right, across_mlp))
     across, beside = partner(right, 2, count), partner(right, 1, count)
+    d_mlp = [d_mlp, beside_mlp, across_mlp, partner(across_mlp, 1, count)]
+    out_near, out_far = first_hop(
+        on_core(
+            functools.partial(early_body, [((3 * shard_total, left_total), (0, width))]),
+            three_parts((hidden_total, width)),
+            (*d_mlp, *left),
+        ),
+        count,
+    )
     dq_0, d_own, d_before, d_after = on_core(
         local_backward_body,
         [
@@ -1090,31 +1086,39 @@
         [pltpu.VMEM((1, width), F32)],
         [pltpu.SMEM] + [pltpu.VMEM] * 13,
     )
-    across, d_proj = lax.optimization_barrier((across, d_proj))
+    across, d_proj, out_far = lax.optimization_barrier((across, d_proj, out_far))
+    mlp_out_share = second_hop(out_near, out_far, count)
     right = [right, beside, across, partner(across, 1, count)]
-    early_rows = shard_total * (inner // width + 1) + hidden_total
-    early = on_core(
-        functools.partial(early_body, shard),
-        four_planes((early_rows, width)),
-        (*right, *flat_rows(n2), *flat_rows(mixed), *flat_rows(att)),
-    )
-    d_proj = plane_parts(d_proj, count, early)
-    early = sent_planes(early, count)
-    late_in = (group_pos[None], *d_proj, *flat_rows(n1))
+    early_rows = shard_total * (inner // width + 1)
+    near, far = first_hop(
+        on_core(
+            functools.partial(
+                early_body,
+                [
+                    ((2 * shard_total, 3 * shard_total), (0, inner)),
+                    ((shard_total, 2 * shard_total), (inner, inner + width)),
+                ],
+            ),
+            three_parts((early_rows, width)),
+            (*right, *left),
+        ),
+        count,
+    )
+    across, beside = partner(d_proj, 2, count), partner(d_proj, 1, count)
+    across, far = lax.optimization_barrier((across, far))
+    early = second_hop(near, far, count)
+    late_in = (group_pos[None], d_proj, beside, across, partner(across, 1, count), *left)
     late = on_core(
-        late_body,
-        four_planes((shard_total, 3 * width + LANES)),
+        functools.partial(late_body, (0, shard_total)),
+        three_parts((shard_total, 3 * width + LANES)),
         late_in,
         [pltpu.VMEM((width, LANES), F32)],
         [pltpu.SMEM] + [pltpu.VMEM] * (len(late_in) - 1),
     )
-    early, late = lax.optimization_barrier((early, list(late)))
-    early, late = sum_planes(early), sum_planes(sent_planes(late, count))
+    late = second_hop(*first_hop(late, count), count)
     parts = [early[p * shard_total : (p + 1) * shard_total] for p in range(inner // width)]
-    start = shard_total * (inner // width)
     in_share = jnp.concatenate(parts, 1)
-    mlp_out_share = early[start : start + hidden_total]
-    attn_share = early[start + hidden_total :]
+    attn_share = early[early_rows - shard_total :]
     gain_columns = late[:, 3 * width :]
     qkv_share, in_share, mlp_out_share, attn_share, gain_columns = (
         over_groups(item, count)

time: 373 us -> 351 us (0.941)
  Pallas kernels: 83.4 us -> 56.8 us
  waiting for transfers between devices: 112 us -> 128 us
  starting transfers between devices: 64.9 us -> 50.2 us
  blocking collectives: 49.7 us -> 55.1 us
    pallas_call x16 -> x17, Pallas kernels: 83.4 us -> 56.8 us  [on_core(): pl.pallas_call(body, out_shape=[jax.ShapeDtypeStruct(shape, dtype) for sh...]
    ppermute x33 -> x36, starting transfers between devices: 46.2 us -> 31 us  [partner(): return lax.ppermute(rows, 'dp', [(i, i ^ apart) for i in range(count)])]
    unnamed x46 -> x102, local copies, waits for them, and re-layouts: 7.02 us -> 21.8 us
    all_gather x1, waiting for transfers between devices: 21.3 us -> 28.3 us  [on_device(): others = [lax.all_gather(stacked, 'dp', axis=0, tiled=True)]]
    slice x8 -> x0, local copies, waits for them, and re-layouts: 6.94 us -> none  [on_device(): part[:, :, start:end]]
    ppermute x33 -> x36, waiting for transfers between devices: 81.8 us -> 88 us  [partner(): return lax.ppermute(rows, 'dp', [(i, i ^ apart) for i in range(count)])]
    all_to_all x3, blocking collectives: 49.7 us -> 55.1 us  [exchange(): return lax.all_to_all(blocks, 'dp', 0, 0, axis_index_groups=groups)]
  transfers between devices with their start and end apart: 43 -> 46, of which waited for: 17 -> 23; matrix products, arithmetic and copies ran while one was open for 10% -> 6% of each run, Pallas kernels for 9% -> 6%
where the time goes in v7:
time: 351 us; the launch traced here: 350 us
  waiting for transfers between devices  128 us (36%)
  Pallas kernels  56.8 us (16%)
  blocking collectives  55.1 us (16%)
  starting transfers between devices  50.2 us (14%)
  local copies, waits for them, and re-layouts  40.4 us (12%)
  between operations  14.9 us (4%)
  other arithmetic  4.31 us (1%)
    ppermute x36, waiting for transfers between devices, partner(): return lax.ppermute(rows, 'dp', [(i, i ^ apart) for i in range(count)])  88 us
    pallas_call x17, Pallas kernels, on_core(): pl.pallas_call(body, out_shape=[jax.ShapeDtypeStruct(shape, dtype) for sh...  56.8 us
    all_to_all x3, blocking collectives, exchange(): return lax.all_to_all(blocks, 'dp', 0, 0, axis_index_groups=groups)  55.1 us
    ppermute x36, starting transfers between devices, partner(): return lax.ppermute(rows, 'dp', [(i, i ^ apart) for i in range(count)])  31 us
    all_gather x1, waiting for transfers between devices, on_device(): others = [lax.all_gather(stacked, 'dp', axis=0, tiled=True)]  28.3 us
    unnamed x102, local copies, waits for them, and re-layouts  21.8 us
    dynamic_update_slice x16, local copies, waits for them, and re-layouts, gather_rows(): whole = lax.dynamic_update_slice(whole, item[None], start)  11.4 us
    ppermute x4, waiting for transfers between devices, to_other_section(): return [lax.ppermute(rows, 'section', pairs) for rows in chunks]  9.19 us
  transfers between devices with their start and end apart: 46, of which 23 were waited for; matrix products, arithmetic and copies ran while one was open for 6% of the time, Pallas kernels for 6%

profile of v7, /device:TPU:0, one launch (start us, length us, event | category | flops | bytes accessed | tf_op | source)
XLA Modules:
  0.0 350.1 jit_solution(5089997787910642364)
XLA Ops:
  10.3 3.0 collective-permute-start.1
  13.3 1.6 collective-permute-start.2
  14.9 2.6 collective-permute-start.3
  23.5 2.1 broadcast_in_dim.105
  27.5 6.9 %collective-permute-done.3 = bf16[48,2432]{1,0:T(8,128)(2,1)S(1)} collective-permute-done((bf16[48,2432]{1,0:T(8,128)(2,1)S(1)}, bf16[48,2432]{1,0:T(8,128)(2,1)S(1)}, u32[]{:S(2)}, u32[]{:S(2)}) %collective-permute-start.3) | collective-permute-done | bytes 233504 | tf_op jit(solution)/shard_map/ppermute | solution.py:702
  34.9 1.5 collective-permute-start.7
  40.0 5.6 %collective-permute-done.6 = bf16[48,2432]{1,0:T(8,128)(2,1)S(1)} collective-permute-done((bf16[48,2432]{1,0:T(8,128)(2,1)S(1)}, bf16[48,2432]{1,0:T(8,128)(2,1)S(1)}, u32[]{:S(2)}, u32[]{:S(2)}) %collective-permute-start.6) | collective-permute-done | bytes 233504 | tf_op jit(solution)/shard_map/ppermute | solution.py:702
  46.3 3.2 collective-permute-done.7
  56.9 3.1 shard_map.154
  60.7 2.1 collective-permute-start.16
  64.8 1.7 collective-permute-done.17.after_ref
  66.6 3.6 %shard_map.155 = (bf16[128,768]{1,0:T(8,128)(2,1)S(1)}, f32[12,1,128]{2,1,0:T(1,128)S(1)}) custom-call(bf16[128,768]{1,0:T(8,128)(2,1)S(1)} %get-tuple-element.74.q_ref, bf16[128,1536]{1,0:T(8,128)(2,1)S(1)} %collective-permute-done.16.before_ref, bf16[128,1536]{1,0:T(8,128)(2,1)S(1)} %get-tuple-element.75.own_ref, ...), custom_call_target="tpu_custom_call" | custom-call | flops 1024 | bytes 1024 | tf_op jit(solution)/shard_map/pallas_call | solution.py:65
  70.2 28.3 %all-gather.2.cloned.1.call-done.refs_0_ = bf16[768,4352]{1,0:T(8,128)(2,1)} async-done(((bf16[48,4352]{1,0:T(8,128)(2,1)}), bf16[768,4352]{1,0:T(8,128)(2,1)}) %all-gather.2.cloned.1.call-update) | async-done | bytes 6684688 | tf_op jit(solution)/shard_map/all_gather | solution.py:873
  98.6 4.4 %shard_map.156 = (bf16[128,768]{1,0:T(8,128)(2,1)S(1)}, bf16[128,1152]{1,0:T(8,128)(2,1)S(1)}, f32[128,768]{1,0:T(8,128)S(1)}, f32[128,2304]{1,0:T(8,128)S(1)}, ...) custom-call(bf16[768,4352]{1,0:T(8,128)(2,1)} %all-gather.2.cloned.1.call-done.refs_0_, ...), custom_call_target="tpu_custom_call" | custom-call | flops 1024 | bytes 1024 | tf_op jit(solution)/shard_map/pallas_call | solution.py:65
  105.6 3.4 collective-permute-start.18
  110.6 1.4 collective-permute-done.18.low_ref.refs_2_
  112.0 1.4 collective-permute-done.19.high_ref.refs_3_
  113.5 3.1 shard_map.157
  116.6 21.2 %all_to_all.20.got_ref = bf16[16,144,128]{2,1,0:T(8,128)(2,1)S(1)} all-to-all(bf16[16,144,128]{2,1,0:T(8,128)(2,1)S(1)} %get-tuple-element.80), channel_id=1, replica_groups={{0,1,2,3,4,5,6,7,8,9,10,11,12,13,14,15},{16,17,18,19,20,21,22,23,24,25,..., dimensions={0} | all-to-all | bytes 1179648 | tf_op jit(solution)/shard_map/all_to_all | solution.py:693
  139.5 6.0 %shard_map.158 = (bf16[16,48,128]{2,1,0:T(8,128)(2,1)S(1)}, f32[6,1,256]{2,1,0:T(1,128)S(1)}) custom-call(bf16[16,144,128]{2,1,0:T(8,128)(2,1)S(1)} %all_to_all.20.got_ref, bf16[16,64,128]{2,1,0:T(8,128)(2,1)S(1)} %collective-permute-done.20.other_ref, s32[1024,1]{1,0:T(8,128)S(1)} %copy.19.own_seg_ref, s32[1024,1]{1,0:T(8,128)S(1)} %copy.20.shared_seg_ref), custom_call_target="tpu_custom_call" | custom-call | flops 1024 | bytes 1024 | tf_op jit(solution)/shard_map/pallas_call | solution.py:65
  145.5 11.8 %all_to_all.21.refs_1_ = bf16[16,48,128]{2,1,0:T(8,128)(2,1)S(1)} all-to-all(bf16[16,48,128]{2,1,0:T(8,128)(2,1)S(1)} %get-tuple-element.81), channel_id=1, replica_groups={{0,1,2,3,4,5,6,7,8,9,10,11,12,13,14,15},{16,17,18,19,20,21,22,23,24,25,..., dimensions={0} | all-to-all | bytes 393216 | tf_op jit(solution)/shard_map/all_to_all | solution.py:693
  157.3 7.7 %shard_map.159 = (bf16[128,768]{1,0:T(8,128)(2,1)S(1)}, bf16[128,768]{1,0:T(8,128)(2,1)S(1)}, bf16[128,768]{1,0:T(8,128)(2,1)S(1)}, bf16[128,1152]{1,0:T(8,128)(...) custom-call(bf16[768,4352]{1,0:T(8,128)(2,1)} %all-gather.2.cloned.1, ...), custom_call_target="tpu_custom_call" | custom-call | flops 1024 | bytes 1024 | tf_op jit(solution)/shard_map/pallas_call | solution.py:65
  169.4 4.2 %all-to-all-start.2 = ((bf16[16,48,128]{2,1,0:T(8,128)(2,1)}), bf16[16,48,128]{2,1,0:T(8,128)(2,1)}, u32[]{:S(2)}, u32[]{:S(2)}) async-start(bf16[16,48,128]{2,1,0:T(8,128)(2,1)} %get-tuple-element.91), calls=%async_computation.2 | async-start | bytes 393216 | tf_op jit(solution)/shard_map/all_to_all | solution.py:693
  183.5 8.3 %shard_map.161 = (bf16[16,144,128]{2,1,0:T(8,128)(2,1)S(1)}, bf16[16,64,128]{2,1,0:T(8,128)(2,1)S(1)}) custom-call(bf16[16,144,128]{2,1,0:T(8,128)(2,1)S(1)} %all_to_all.20.got_ref, bf16[16,64,128]{2,1,0:T(8,128)(2,1)S(1)} %copy-done.10, s32[1024,1]{1,0:T(8,128)S(1)} %copy.19.own_seg_ref, s32[1024,1]{1,0:T(8,128)S(1)} %copy.20.shared_seg_ref, ...), custom_call_target="tpu_custom_call" | custom-call | flops 1024 | bytes 1024 | tf_op jit(solution)/shard_map/pallas_call | solution.py:65
  194.4 6.5 %collective-permute-done.22.refs_6_ = bf16[4,216,128]{2,1,0:T(8,128)(2,1)S(1)} collective-permute-done((bf16[4,216,128]{2,1,0:T(8,128)(2,1)S(1)}, bf16[4,216,128]{2,1,0:T(8,128)(2,1)S(1)}, u32[]{:S(2)}, u32[]{:S(2)}) %collective-permute-start.22) | collective-permute-done | bytes 221216 | tf_op jit(solution)/shard_map/ppermute | solution.py:702
  200.9 3.0 collective-permute-done.23.refs_7_
  203.9 22.2 %all_to_all.22.got_ref = bf16[16,144,128]{2,1,0:T(8,128)(2,1)S(1)} all-to-all(bf16[16,144,128]{2,1,0:T(8,128)(2,1)S(1)} %add_convert_fusion), channel_id=1, replica_groups={{0,1,2,3,4,5,6,7,8,9,10,11,12,13,14,15},{16,17,18,19,20,21,22,23,24,25,..., dimensions={0} | all-to-all | bytes 1179648 | tf_op jit(solution)/shard_map/all_to_all | solution.py:693
  226.1 3.6 %shard_map.162 = (bf16[128,2304]{1,0:T(8,128)(2,1)S(1)}, f32[1,768]{1,0:T(1,128)S(1)}, bf16[64,768]{1,0:T(8,128)(2,1)S(1)}, bf16[64,768]{1,0:T(8,128)(2,1)S(1)}) custom-call(bf16[768,2432]{1,0:T(8,128)(2,1)} %bitcast.23.first_ref, bf16[16,144,128]{2,1,0:T(8,128)(2,1)S(1)} %all_to_all.22.got_ref, f32[128,768]{1,0:T(8,128)S(1)} %copy-done.22, ...), custom_call_target="tpu_custom_call" | custom-call | flops 1024 | bytes 1024 | tf_op jit(solution)/shard_map/pallas_call | solution.py:65
  232.4 4.9 %collective-permute-done.25.refs_2_ = bf16[64,768]{1,0:T(8,128)(2,1)S(1)} collective-permute-done((bf16[64,768]{1,0:T(8,128)(2,1)S(1)}, bf16[64,768]{1,0:T(8,128)(2,1)S(1)}, u32[]{:S(2)}, u32[]{:S(2)}) %collective-permute-start.25) | collective-permute-done | bytes 98336 | tf_op jit(solution)/shard_map/ppermute | solution.py:698
  239.5 6.1 %shard_map.163 = (f32[1,768]{1,0:T(1,128)S(1)}, f32[128,768]{1,0:T(8,128)S(1)}, bf16[128,768]{1,0:T(8,128)(2,1)S(1)}, bf16[128,3072]{1,0:T(8,128)(2,1)S(1)}) custom-call(bf16[768,4352]{1,0:T(8,128)(2,1)} %all-gather.2.cloned.1.call-done.refs_0_, s32[1]{0:T(128)} %bitcast.37.lower_ref.refs_1_, bf16[64,768]{1,0:T(8,128)(2,1)S(1)} %collective-permute-done.25.refs_2_, ...), custom_call_target="tpu_custom_call" | custom-call | flops 1024 | bytes 1024 | tf_op jit(solution)/shard_map/pallas_call | solution.py:65
  245.6 1.5 collective-permute-start.30
  247.6 3.5 %shard_map.164 = (bf16[128,768]{1,0:T(8,128)(2,1)S(1)}, f32[128,1536]{1,0:T(8,128)S(1)}, bf16[128,1536]{1,0:T(8,128)(2,1)S(1)}, bf16[128,1536]{1,0:T(8,128)(2,1)S(1)}) custom-call(bf16[128,768]{1,0:T(8,128)(2,1)S(1)} %copy-done.14, bf16[128,1536]{1,0:T(8,128)(2,1)S(1)} %copy-done.4, bf16[128,1536]{1,0:T(8,128)(2,1)S(1)} %copy-done.2, ...), custom_call_target="tpu_custom_call" | custom-call | flops 1024 | bytes 1024 | tf_op jit(solution)/shard_map/pallas_call | solution.py:65
  252.4 3.1 collective-permute-start.29
  257.6 4.0 %shard_map.165 = (bf16[144,2304]{1,0:T(8,128)(2,1)S(1)}, bf16[128,768]{1,0:T(8,128)(2,1)S(1)}, f32[1,768]{1,0:T(1,128)}) custom-call(s32[1]{0:T(128)} %bitcast.37.lower_ref.refs_1_, bf16[768,2432]{1,0:T(8,128)(2,1)} %bitcast.23.first_ref, bf16[128,768]{1,0:T(8,128)(2,1)S(1)} %get-tuple-element.107.dq_ref, f32[128,1536]{1,0:T(8,128)S(1)} %get-tuple-element.108.own_ref, ...), custom_call_target="tpu_custom_call" | custom-call | flops 1024 | bytes 1024 | tf_op jit(solution)/shard_map/pallas_call | solution.py:65
  261.6 3.6 %collective-permute-done.33 = bf16[144,768]{1,0:T(8,128)(2,1)S(1)} collective-permute-done((bf16[144,768]{1,0:T(8,128)(2,1)S(1)}, bf16[144,768]{1,0:T(8,128)(2,1)S(1)}, u32[]{:S(2)}, u32[]{:S(2)}) %collective-permute-start.33) | collective-permute-done | bytes 221216 | tf_op jit(solution)/shard_map/ppermute | solution.py:702
  265.3 4.0 %collective-permute-done.30.refs_2_ = bf16[128,3072]{1,0:T(8,128)(2,1)S(1)} collective-permute-done((bf16[128,3072]{1,0:T(8,128)(2,1)S(1)}, bf16[128,3072]{1,0:T(8,128)(2,1)S(1)}, u32[]{:S(2)}, u32[]{:S(2)}) %collective-permute-start.30) | collective-permute-done | bytes 786464 | tf_op jit(solution)/shard_map/ppermute | solution.py:702
  269.3 6.5 %collective-permute-start.37 = (bf16[128,3072]{1,0:T(8,128)(2,1)S(1)}, bf16[128,3072]{1,0:T(8,128)(2,1)S(1)}, u32[]{:S(2)}, u32[]{:S(2)}) collective-permute-start(bf16[128,3072]{1,0:T(8,128)(2,1)S(1)} %collective-permute-done.30.refs_2_), channel_id=1, source_target_pairs={{0,1},{1,0},{2,3},{3,2},{4,5},{5,4},{6,7},{7,6},{8,9},{9,8},{10,11... | collective-permute-start | bytes 2359304 | tf_op jit(solution)/shard_map/ppermute | solution.py:702
  275.8 1.9 collective-permute-done.37.refs_3_
  278.6 1.5 collective-permute-start.38
  280.1 2.0 collective-permute-start.35
  282.0 12.2 %collective-permute-done.38 = bf16[384,768]{1,0:T(8,128)(2,1)S(1)} collective-permute-done((bf16[384,768]{1,0:T(8,128)(2,1)S(1)}, bf16[384,768]{1,0:T(8,128)(2,1)S(1)}, u32[]{:S(2)}, u32[]{:S(2)}) %collective-permute-start.38) | collective-permute-done | bytes 589856 | tf_op jit(solution)/shard_map/ppermute | solution.py:702
  294.3 2.7 collective-permute-done.35.refs_2_
  297.7 1.5 collective-permute-start.43
  299.2 1.4 collective-permute-start.42
  301.4 11.8 %collective-permute-done.43 = bf16[72,768]{1,0:T(8,128)(2,1)S(1)} collective-permute-done((bf16[72,768]{1,0:T(8,128)(2,1)S(1)}, bf16[72,768]{1,0:T(8,128)(2,1)S(1)}, u32[]{:S(2)}, u32[]{:S(2)}) %collective-permute-start.43) | collective-permute-done | bytes 110624 | tf_op jit(solution)/shard_map/ppermute | solution.py:702
  314.6 4.6 %collective-permute-done.42 = bf16[192,768]{1,0:T(8,128)(2,1)S(1)} collective-permute-done((bf16[192,768]{1,0:T(8,128)(2,1)S(1)}, bf16[192,768]{1,0:T(8,128)(2,1)S(1)}, u32[]{:S(2)}, u32[]{:S(2)}) %collective-permute-start.42) | collective-permute-done | bytes 294944 | tf_op jit(solution)/shard_map/ppermute | solution.py:702
  320.0 9.1 %collective-permute-done.40 = bf16[96,2432]{1,0:T(8,128)(2,1)S(1)} collective-permute-done((bf16[96,2432]{1,0:T(8,128)(2,1)S(1)}, bf16[96,2432]{1,0:T(8,128)(2,1)S(1)}, u32[]{:S(2)}, u32[]{:S(2)}) %collective-permute-start.40) | collective-permute-done | bytes 466976 | tf_op jit(solution)/shard_map/ppermute | solution.py:702
  330.0 11.7 %collective-permute-done.41 = bf16[48,2432]{1,0:T(8,128)(2,1)S(1)} collective-permute-done((bf16[48,2432]{1,0:T(8,128)(2,1)S(1)}, bf16[48,2432]{1,0:T(8,128)(2,1)S(1)}, u32[]{:S(2)}, u32[]{:S(2)}) %collective-permute-start.41) | collective-permute-done | bytes 233504 | tf_op jit(solution)/shard_map/ppermute | solution.py:702
  (244 shorter events, 64.1 us)
Async XLA Ops:
  7.2 91.4 %all-gather.2.cloned.1.call-start = ((), (), s32[]{:S(2)}) async-start(), calls=%async_computation.4 | async-start | bytes 7102464 | tf_op jit(solution)/shard_map/all_gather | solution.py:873
  10.3 13.0 %collective-permute-start.1 = (bf16[48,2432]{1,0:T(8,128)(2,1)S(1)}, bf16[48,2432]{1,0:T(8,128)(2,1)S(1)}, u32[]{:S(2)}, u32[]{:S(2)}) collective-permute-start(bf16[48,2432]{1,0:T(8,128)(2,1)S(1)} %shard_map.153), channel_id=1, source_target_pairs={{0,2},{1,3},{2,0},{3,1},{4,6},{5,7},{6,4},{7,5},{8,10},{9,11},{10,... | collective-permute-start | bytes 700424 | tf_op jit(solution)/shard_map/ppermute | solution.py:702
  13.3 13.9 %collective-permute-start.2 = (bf16[48,2432]{1,0:T(8,128)(2,1)S(1)}, bf16[48,2432]{1,0:T(8,128)(2,1)S(1)}, u32[]{:S(2)}, u32[]{:S(2)}) collective-permute-start(bf16[48,2432]{1,0:T(8,128)(2,1)S(1)} %shard_map.153), channel_id=1, source_target_pairs={{0,4},{1,5},{2,6},{3,7},{4,0},{5,1},{6,2},{7,3},{8,12},{9,13},{10,... | collective-permute-start | bytes 700424 | tf_op jit(solution)/shard_map/ppermute | solution.py:702
  14.9 19.5 %collective-permute-start.3 = (bf16[48,2432]{1,0:T(8,128)(2,1)S(1)}, bf16[48,2432]{1,0:T(8,128)(2,1)S(1)}, u32[]{:S(2)}, u32[]{:S(2)}) collective-permute-start(bf16[48,2432]{1,0:T(8,128)(2,1)S(1)} %shard_map.153), channel_id=1, source_target_pairs={{0,8},{1,9},{2,10},{3,11},{4,12},{5,13},{6,14},{7,15},{8,0},{9,1},... | collective-permute-start | bytes 700424 | tf_op jit(solution)/shard_map/ppermute | solution.py:702
  17.5 17.5 %collective-permute-start.4 = (bf16[48,2432]{1,0:T(8,128)(2,1)S(1)}, bf16[48,2432]{1,0:T(8,128)(2,1)S(1)}, u32[]{:S(2)}, u32[]{:S(2)}) collective-permute-start(bf16[48,2432]{1,0:T(8,128)(2,1)S(1)} %shard_map.153), channel_id=1, source_target_pairs={{0,12},{1,13},{2,14},{3,15},{4,8},{5,9},{6,10},{7,11},{8,4},{9,5},... | collective-permute-start | bytes 700424 | tf_op jit(solution)/shard_map/ppermute | solution.py:702
  18.4 1.2 collective-permute-start
  19.6 30.6 %collective-permute-start.8 = (bf16[48,2432]{1,0:T(8,128)(2,1)S(1)}, bf16[48,2432]{1,0:T(8,128)(2,1)S(1)}, u32[]{:S(2)}, u32[]{:S(2)}) collective-permute-start(bf16[48,2432]{1,0:T(8,128)(2,1)S(1)} %shard_map.153), channel_id=1, source_target_pairs={{0,1},{1,0},{2,3},{3,2},{4,5},{5,4},{6,7},{7,6},{8,9},{9,8},{10,11... | collective-permute-start | bytes 700424 | tf_op jit(solution)/shard_map/ppermute | solution.py:702
  26.8 24.6 %collective-permute-start.9 = (bf16[48,2432]{1,0:T(8,128)(2,1)S(1)}, bf16[48,2432]{1,0:T(8,128)(2,1)S(1)}, u32[]{:S(2)}, u32[]{:S(2)}) collective-permute-start(bf16[48,2432]{1,0:T(8,128)(2,1)S(1)} %collective-permute-done.1), channel_id=1, source_target_pairs={{0,1},{1,0},{2,3},{3,2},{4,5},{5,4},{6,7},{7,6},{8,9},{9,8},{10,11... | collective-permute-start | bytes 700424 | tf_op jit(solution)/shard_map/ppermute | solution.py:702
  27.2 12.1 %collective-permute-start.5 = (bf16[48,2432]{1,0:T(8,128)(2,1)S(1)}, bf16[48,2432]{1,0:T(8,128)(2,1)S(1)}, u32[]{:S(2)}, u32[]{:S(2)}) collective-permute-start(bf16[48,2432]{1,0:T(8,128)(2,1)S(1)} %collective-permute-done.2), channel_id=1, source_target_pairs={{0,2},{1,3},{2,0},{3,1},{4,6},{5,7},{6,4},{7,5},{8,10},{9,11},{10,... | collective-permute-start | bytes 700424 | tf_op jit(solution)/shard_map/ppermute | solution.py:702
  34.4 11.2 %collective-permute-start.6 = (bf16[48,2432]{1,0:T(8,128)(2,1)S(1)}, bf16[48,2432]{1,0:T(8,128)(2,1)S(1)}, u32[]{:S(2)}, u32[]{:S(2)}) collective-permute-start(bf16[48,2432]{1,0:T(8,128)(2,1)S(1)} %collective-permute-done.3), channel_id=1, source_target_pairs={{0,2},{1,3},{2,0},{3,1},{4,6},{5,7},{6,4},{7,5},{8,10},{9,11},{10,... | collective-permute-start | bytes 700424 | tf_op jit(solution)/shard_map/ppermute | solution.py:702
  34.9 14.5 %collective-permute-start.7 = (bf16[48,2432]{1,0:T(8,128)(2,1)S(1)}, bf16[48,2432]{1,0:T(8,128)(2,1)S(1)}, u32[]{:S(2)}, u32[]{:S(2)}) collective-permute-start(bf16[48,2432]{1,0:T(8,128)(2,1)S(1)} %collective-permute-done.4), channel_id=1, source_target_pairs={{0,2},{1,3},{2,0},{3,1},{4,6},{5,7},{6,4},{7,5},{8,10},{9,11},{10,... | collective-permute-start | bytes 700424 | tf_op jit(solution)/shard_map/ppermute | solution.py:702
  39.3 12.9 %collective-permute-start.10 = (bf16[48,2432]{1,0:T(8,128)(2,1)S(1)}, bf16[48,2432]{1,0:T(8,128)(2,1)S(1)}, u32[]{:S(2)}, u32[]{:S(2)}) collective-permute-start(bf16[48,2432]{1,0:T(8,128)(2,1)S(1)} %collective-permute-done.2), channel_id=1, source_target_pairs={{0,1},{1,0},{2,3},{3,2},{4,5},{5,4},{6,7},{7,6},{8,9},{9,8},{10,11... | collective-permute-start | bytes 700424 | tf_op jit(solution)/shard_map/ppermute | solution.py:702
  45.6 8.5 %collective-permute-start.12 = (bf16[48,2432]{1,0:T(8,128)(2,1)S(1)}, bf16[48,2432]{1,0:T(8,128)(2,1)S(1)}, u32[]{:S(2)}, u32[]{:S(2)}) collective-permute-start(bf16[48,2432]{1,0:T(8,128)(2,1)S(1)} %collective-permute-done.3), channel_id=1, source_target_pairs={{0,1},{1,0},{2,3},{3,2},{4,5},{5,4},{6,7},{7,6},{8,9},{9,8},{10,11... | collective-permute-start | bytes 700424 | tf_op jit(solution)/shard_map/ppermute | solution.py:702
  49.5 6.0 %collective-permute-start.14 = (bf16[48,2432]{1,0:T(8,128)(2,1)S(1)}, bf16[48,2432]{1,0:T(8,128)(2,1)S(1)}, u32[]{:S(2)}, u32[]{:S(2)}) collective-permute-start(bf16[48,2432]{1,0:T(8,128)(2,1)S(1)} %collective-permute-done.4), channel_id=1, source_target_pairs={{0,1},{1,0},{2,3},{3,2},{4,5},{5,4},{6,7},{7,6},{8,9},{9,8},{10,11... | collective-permute-start | bytes 700424 | tf_op jit(solution)/shard_map/ppermute | solution.py:702
  50.2 3.2 collective-permute-start.11
  51.4 3.4 collective-permute-start.13
  52.2 4.1 %collective-permute-start.15 = (bf16[48,2432]{1,0:T(8,128)(2,1)S(1)}, bf16[48,2432]{1,0:T(8,128)(2,1)S(1)}, u32[]{:S(2)}, u32[]{:S(2)}) collective-permute-start(bf16[48,2432]{1,0:T(8,128)(2,1)S(1)} %collective-permute-done.7), channel_id=1, source_target_pairs={{0,1},{1,0},{2,3},{3,2},{4,5},{5,4},{6,7},{7,6},{8,9},{9,8},{10,11... | collective-permute-start | bytes 700424 | tf_op jit(solution)/shard_map/ppermute | solution.py:702
  60.7 4.1 %collective-permute-start.16 = (bf16[128,1536]{1,0:T(8,128)(2,1)S(1)}, bf16[128,1536]{1,0:T(8,128)(2,1)S(1)}, u32[]{:S(2)}, u32[]{:S(2)}) collective-permute-start(bf16[128,1536]{1,0:T(8,128)(2,1)S(1)} %get-tuple-element.75.own_ref), channel_id=1, source_target_pairs={{0,1},{1,2},{2,3},{3,4},{4,5},{5,6},{6,7},{7,8},{8,9},{9,10},{10,1... | collective-permute-start | bytes 1179656 | tf_op jit(solution)/shard_map/ppermute | solution.py:920
  62.9 3.7 %collective-permute-start.17 = (bf16[128,1536]{1,0:T(8,128)(2,1)S(1)}, bf16[128,1536]{1,0:T(8,128)(2,1)S(1)}, u32[]{:S(2)}, u32[]{:S(2)}) collective-permute-start(bf16[128,1536]{1,0:T(8,128)(2,1)S(1)} %get-tuple-element.75.own_ref), channel_id=1, source_target_pairs={{1,0},{2,1},{3,2},{4,3},{5,4},{6,5},{7,6},{8,7},{9,8},{10,9},{11,1... | collective-permute-start | bytes 1179656 | tf_op jit(solution)/shard_map/ppermute | solution.py:922
  105.6 6.5 %collective-permute-start.18 = (bf16[64,768]{1,0:T(8,128)(2,1)S(1)}, bf16[64,768]{1,0:T(8,128)(2,1)S(1)}, u32[]{:S(2)}, u32[]{:S(2)}) collective-permute-start(bf16[64,768]{1,0:T(8,128)(2,1)S(1)} %get-tuple-element.78), channel_id=1, source_target_pairs={{0,16},{1,17},{2,18},{3,19},{4,20},{5,21},{6,22},{7,23},{8,24},{9,... | collective-permute-start | bytes 294920 | tf_op jit(solution)/shard_map/ppermute | solution.py:698
  108.9 4.6 %collective-permute-start.19 = (bf16[64,768]{1,0:T(8,128)(2,1)S(1)}, bf16[64,768]{1,0:T(8,128)(2,1)S(1)}, u32[]{:S(2)}, u32[]{:S(2)}) collective-permute-start(bf16[64,768]{1,0:T(8,128)(2,1)S(1)} %get-tuple-element.79), channel_id=1, source_target_pairs={{0,16},{1,17},{2,18},{3,19},{4,20},{5,21},{6,22},{7,23},{8,24},{9,... | collective-permute-start | bytes 294920 | tf_op jit(solution)/shard_map/ppermute | solution.py:698
  137.9 1.6 collective-permute-start.20
  169.4 13.2 %all-to-all-start.2 = ((bf16[16,48,128]{2,1,0:T(8,128)(2,1)}), bf16[16,48,128]{2,1,0:T(8,128)(2,1)}, u32[]{:S(2)}, u32[]{:S(2)}) async-start(bf16[16,48,128]{2,1,0:T(8,128)(2,1)} %get-tuple-element.91), calls=%async_computation.2 | async-start | bytes 393216 | tf_op jit(solution)/shard_map/all_to_all | solution.py:693
  191.8 2.2 collective-permute-start.24
  192.1 2.3 collective-permute-start.21
  192.6 8.3 %collective-permute-start.22 = (bf16[4,216,128]{2,1,0:T(8,128)(2,1)S(1)}, bf16[4,216,128]{2,1,0:T(8,128)(2,1)S(1)}, u32[]{:S(2)}, u32[]{:S(2)}) collective-permute-start(bf16[4,216,128]{2,1,0:T(8,128)(2,1)S(1)} %get-tuple-element.143), channel_id=1, source_target_pairs={{0,2},{1,3},{2,0},{3,1},{4,6},{5,7},{6,4},{7,5},{8,10},{9,11},{10,... | collective-permute-start | bytes 663560 | tf_op jit(solution)/shard_map/ppermute | solution.py:702
  193.2 10.7 %collective-permute-start.23 = (bf16[4,216,128]{2,1,0:T(8,128)(2,1)S(1)}, bf16[4,216,128]{2,1,0:T(8,128)(2,1)S(1)}, u32[]{:S(2)}, u32[]{:S(2)}) collective-permute-start(bf16[4,216,128]{2,1,0:T(8,128)(2,1)S(1)} %get-tuple-element.142), channel_id=1, source_target_pairs={{0,3},{1,2},{2,1},{3,0},{4,7},{5,6},{6,5},{7,4},{8,11},{9,10},{10,... | collective-permute-start | bytes 663560 | tf_op jit(solution)/shard_map/ppermute | solution.py:702
  194.4 45.0 %copy-start.8 = (f32[128,2304]{1,0:T(8,128)S(1)}, f32[128,2304]{1,0:T(8,128)}, u32[]{:S(2)}) copy-start(f32[128,2304]{1,0:T(8,128)} %copy-done.7) | copy-start | bytes 3538948
  194.4 45.0 %copy-start.18 = (bf16[128,3072]{1,0:T(8,128)(2,1)S(1)}, bf16[128,3072]{1,0:T(8,128)(2,1)}, u32[]{:S(2)}) copy-start(bf16[128,3072]{1,0:T(8,128)(2,1)} %copy-done.17) | copy-start | bytes 2359300
  229.8 7.5 %collective-permute-start.25 = (bf16[64,768]{1,0:T(8,128)(2,1)S(1)}, bf16[64,768]{1,0:T(8,128)(2,1)S(1)}, u32[]{:S(2)}, u32[]{:S(2)}) collective-permute-start(bf16[64,768]{1,0:T(8,128)(2,1)S(1)} %get-tuple-element.99), channel_id=1, source_target_pairs={{16,0},{17,1},{18,2},{19,3},{20,4},{21,5},{22,6},{23,7},{24,8},{25... | collective-permute-start | bytes 294920 | tf_op jit(solution)/shard_map/ppermute | solution.py:698
  231.1 7.6 %collective-permute-start.26 = (bf16[64,768]{1,0:T(8,128)(2,1)S(1)}, bf16[64,768]{1,0:T(8,128)(2,1)S(1)}, u32[]{:S(2)}, u32[]{:S(2)}) collective-permute-start(bf16[64,768]{1,0:T(8,128)(2,1)S(1)} %get-tuple-element.100), channel_id=1, source_target_pairs={{16,0},{17,1},{18,2},{19,3},{20,4},{21,5},{22,6},{23,7},{24,8},{25... | collective-permute-start | bytes 294920 | tf_op jit(solution)/shard_map/ppermute | solution.py:698
  238.7 6.9 %collective-permute-start.27 = (bf16[128,768]{1,0:T(8,128)(2,1)S(1)}, bf16[128,768]{1,0:T(8,128)(2,1)S(1)}, u32[]{:S(2)}, u32[]{:S(2)}) collective-permute-start(bf16[128,768]{1,0:T(8,128)(2,1)S(1)} %pad_maximum_fusion.1.refs_0_), channel_id=1, source_target_pairs={{0,2},{1,3},{2,0},{3,1},{4,6},{5,7},{6,4},{7,5},{8,10},{9,11},{10,... | collective-permute-start | bytes 589832 | tf_op jit(solution)/shard_map/ppermute | solution.py:702
  245.6 23.7 %collective-permute-start.30 = (bf16[128,3072]{1,0:T(8,128)(2,1)S(1)}, bf16[128,3072]{1,0:T(8,128)(2,1)S(1)}, u32[]{:S(2)}, u32[]{:S(2)}) collective-permute-start(bf16[128,3072]{1,0:T(8,128)(2,1)S(1)} %get-tuple-element.117.refs_0_), channel_id=1, source_target_pairs={{0,2},{1,3},{2,0},{3,1},{4,6},{5,7},{6,4},{7,5},{8,10},{9,11},{10,... | collective-permute-start | bytes 2359304 | tf_op jit(solution)/shard_map/ppermute | solution.py:702
  247.1 8.4 %collective-permute-start.31 = (bf16[128,768]{1,0:T(8,128)(2,1)S(1)}, bf16[128,768]{1,0:T(8,128)(2,1)S(1)}, u32[]{:S(2)}, u32[]{:S(2)}) collective-permute-start(bf16[128,768]{1,0:T(8,128)(2,1)S(1)} %pad_maximum_fusion.1.refs_0_), channel_id=1, source_target_pairs={{0,1},{1,0},{2,3},{3,2},{4,5},{5,4},{6,7},{7,6},{8,9},{9,8},{10,11... | collective-permute-start | bytes 589832 | tf_op jit(solution)/shard_map/ppermute | solution.py:702
  247.1 8.4 %collective-permute-start.32 = (bf16[128,768]{1,0:T(8,128)(2,1)S(1)}, bf16[128,768]{1,0:T(8,128)(2,1)S(1)}, u32[]{:S(2)}, u32[]{:S(2)}) collective-permute-start(bf16[128,768]{1,0:T(8,128)(2,1)S(1)} %collective-permute-done.27.refs_2_), channel_id=1, source_target_pairs={{0,1},{1,0},{2,3},{3,2},{4,5},{5,4},{6,7},{7,6},{8,9},{9,8},{10,11... | collective-permute-start | bytes 589832 | tf_op jit(solution)/shard_map/ppermute | solution.py:702
  251.1 6.5 %collective-permute-start.28 = (bf16[128,1536]{1,0:T(8,128)(2,1)S(1)}, bf16[128,1536]{1,0:T(8,128)(2,1)S(1)}, u32[]{:S(2)}, u32[]{:S(2)}) collective-permute-start(bf16[128,1536]{1,0:T(8,128)(2,1)S(1)} %get-tuple-element.109), channel_id=1, source_target_pairs={{1,0},{2,1},{3,2},{4,3},{5,4},{6,5},{7,6},{8,7},{9,8},{10,9},{11,1... | collective-permute-start | bytes 1179656 | tf_op jit(solution)/shard_map/ppermute | solution.py:1077
  252.4 5.2 %collective-permute-start.29 = (bf16[128,1536]{1,0:T(8,128)(2,1)S(1)}, bf16[128,1536]{1,0:T(8,128)(2,1)S(1)}, u32[]{:S(2)}, u32[]{:S(2)}) collective-permute-start(bf16[128,1536]{1,0:T(8,128)(2,1)S(1)} %get-tuple-element.110), channel_id=1, source_target_pairs={{0,1},{1,2},{2,3},{3,4},{4,5},{5,6},{6,7},{7,8},{8,9},{9,10},{10,1... | collective-permute-start | bytes 1179656 | tf_op jit(solution)/shard_map/ppermute | solution.py:1078
  255.9 9.3 %collective-permute-start.33 = (bf16[144,768]{1,0:T(8,128)(2,1)S(1)}, bf16[144,768]{1,0:T(8,128)(2,1)S(1)}, u32[]{:S(2)}, u32[]{:S(2)}) collective-permute-start(bf16[144,768]{1,0:T(8,128)(2,1)S(1)} %get-tuple-element.125), channel_id=1, source_target_pairs={{0,4},{1,5},{2,6},{3,7},{4,0},{5,1},{6,2},{7,3},{8,12},{9,13},{10,... | collective-permute-start | bytes 663560 | tf_op jit(solution)/shard_map/ppermute | solution.py:702
  257.2 18.7 %collective-permute-start.36 = (bf16[128,3072]{1,0:T(8,128)(2,1)S(1)}, bf16[128,3072]{1,0:T(8,128)(2,1)S(1)}, u32[]{:S(2)}, u32[]{:S(2)}) collective-permute-start(bf16[128,3072]{1,0:T(8,128)(2,1)S(1)} %get-tuple-element.117.refs_0_), channel_id=1, source_target_pairs={{0,1},{1,0},{2,3},{3,2},{4,5},{5,4},{6,7},{7,6},{8,9},{9,8},{10,11... | collective-permute-start | bytes 2359304 | tf_op jit(solution)/shard_map/ppermute | solution.py:702
  269.3 8.5 %collective-permute-start.37 = (bf16[128,3072]{1,0:T(8,128)(2,1)S(1)}, bf16[128,3072]{1,0:T(8,128)(2,1)S(1)}, u32[]{:S(2)}, u32[]{:S(2)}) collective-permute-start(bf16[128,3072]{1,0:T(8,128)(2,1)S(1)} %collective-permute-done.30.refs_2_), channel_id=1, source_target_pairs={{0,1},{1,0},{2,3},{3,2},{4,5},{5,4},{6,7},{7,6},{8,9},{9,8},{10,11... | collective-permute-start | bytes 2359304 | tf_op jit(solution)/shard_map/ppermute | solution.py:702
  278.6 15.7 %collective-permute-start.38 = (bf16[384,768]{1,0:T(8,128)(2,1)S(1)}, bf16[384,768]{1,0:T(8,128)(2,1)S(1)}, u32[]{:S(2)}, u32[]{:S(2)}) collective-permute-start(bf16[384,768]{1,0:T(8,128)(2,1)S(1)} %get-tuple-element.129), channel_id=1, source_target_pairs={{0,4},{1,5},{2,6},{3,7},{4,0},{5,1},{6,2},{7,3},{8,12},{9,13},{10,... | collective-permute-start | bytes 1769480 | tf_op jit(solution)/shard_map/ppermute | solution.py:702
  280.1 16.9 %collective-permute-start.35 = (bf16[144,2304]{1,0:T(8,128)(2,1)S(1)}, bf16[144,2304]{1,0:T(8,128)(2,1)S(1)}, u32[]{:S(2)}, u32[]{:S(2)}) collective-permute-start(bf16[144,2304]{1,0:T(8,128)(2,1)S(1)} %get-tuple-element.126.refs_0_), channel_id=1, source_target_pairs={{0,2},{1,3},{2,0},{3,1},{4,6},{5,7},{6,4},{7,5},{8,10},{9,11},{10,... | collective-permute-start | bytes 1990664 | tf_op jit(solution)/shard_map/ppermute | solution.py:702
  282.0 31.9 %collective-permute-start.34 = (bf16[144,2304]{1,0:T(8,128)(2,1)S(1)}, bf16[144,2304]{1,0:T(8,128)(2,1)S(1)}, u32[]{:S(2)}, u32[]{:S(2)}) collective-permute-start(bf16[144,2304]{1,0:T(8,128)(2,1)S(1)} %get-tuple-element.126.refs_0_), channel_id=1, source_target_pairs={{0,1},{1,0},{2,3},{3,2},{4,5},{5,4},{6,7},{7,6},{8,9},{9,8},{10,11... | collective-permute-start | bytes 1990664 | tf_op jit(solution)/shard_map/ppermute | solution.py:702
  297.0 16.9 %collective-permute-start.39 = (bf16[144,2304]{1,0:T(8,128)(2,1)S(1)}, bf16[144,2304]{1,0:T(8,128)(2,1)S(1)}, u32[]{:S(2)}, u32[]{:S(2)}) collective-permute-start(bf16[144,2304]{1,0:T(8,128)(2,1)S(1)} %collective-permute-done.35.refs_2_), channel_id=1, source_target_pairs={{0,1},{1,0},{2,3},{3,2},{4,5},{5,4},{6,7},{7,6},{8,9},{9,8},{10,11... | collective-permute-start | bytes 1990664 | tf_op jit(solution)/shard_map/ppermute | solution.py:702
  297.7 15.4 %collective-permute-start.43 = (bf16[72,768]{1,0:T(8,128)(2,1)S(1)}, bf16[72,768]{1,0:T(8,128)(2,1)S(1)}, u32[]{:S(2)}, u32[]{:S(2)}) collective-permute-start(bf16[72,768]{1,0:T(8,128)(2,1)S(1)} %add_convert_fusion.3), channel_id=1, source_target_pairs={{0,8},{1,9},{2,10},{3,11},{4,12},{5,13},{6,14},{7,15},{8,0},{9,1},... | collective-permute-start | bytes 331784 | tf_op jit(solution)/shard_map/ppermute | solution.py:702
  299.2 20.0 %collective-permute-start.42 = (bf16[192,768]{1,0:T(8,128)(2,1)S(1)}, bf16[192,768]{1,0:T(8,128)(2,1)S(1)}, u32[]{:S(2)}, u32[]{:S(2)}) collective-permute-start(bf16[192,768]{1,0:T(8,128)(2,1)S(1)} %add_convert_fusion.1), channel_id=1, source_target_pairs={{0,8},{1,9},{2,10},{3,11},{4,12},{5,13},{6,14},{7,15},{8,0},{9,1},... | collective-permute-start | bytes 884744 | tf_op jit(solution)/shard_map/ppermute | solution.py:702
  314.6 14.5 %collective-permute-start.40 = (bf16[96,2432]{1,0:T(8,128)(2,1)S(1)}, bf16[96,2432]{1,0:T(8,128)(2,1)S(1)}, u32[]{:S(2)}, u32[]{:S(2)}) collective-permute-start(bf16[96,2432]{1,0:T(8,128)(2,1)S(1)} %get-tuple-element.132), channel_id=1, source_target_pairs={{0,4},{1,5},{2,6},{3,7},{4,0},{5,1},{6,2},{7,3},{8,12},{9,13},{10,... | collective-permute-start | bytes 1400840 | tf_op jit(solution)/shard_map/ppermute | solution.py:702
  329.2 12.6 %collective-permute-start.41 = (bf16[48,2432]{1,0:T(8,128)(2,1)S(1)}, bf16[48,2432]{1,0:T(8,128)(2,1)S(1)}, u32[]{:S(2)}, u32[]{:S(2)}) collective-permute-start(bf16[48,2432]{1,0:T(8,128)(2,1)S(1)} %add_convert_fusion.2), channel_id=1, source_target_pairs={{0,8},{1,9},{2,10},{3,11},{4,12},{5,13},{6,14},{7,15},{8,0},{9,1},... | collective-permute-start | bytes 700424 | tf_op jit(solution)/shard_map/ppermute | solution.py:702
  (49 other events, 692.1 us)
Sparse Core Ops, SparseCore 0:
  23.4 75.1 all-gather.1

commit v8 on v7

--- a/solution.py
+++ b/solution.py
@@ -427,7 +427,8 @@
 
 def local_finish_body(
     lower_ref, first_ref, dq_ref, own_ref, low_ref, high_ref, table_ref, d_middle_ref, x_ref, gain_ref,
-    gain_mlp_ref, other_ref, other_attn_ref, other_mlp_ref, out_ref, grad_ref, gain_attn_ref, gain_scr,
+    gain_mlp_ref, other_ref, other_attn_ref, other_mlp_ref, low_out_ref, high_out_ref, grad_ref, gain_attn_ref,
+    gain_scr, out_ref,
 ):
     rows, width = dq_ref.shape
 
@@ -435,18 +436,18 @@
     def _():
         tables = [table_ref[i] for i in range(3)]
         total = own_ref[...] + low_ref[...].astype(F32) + high_ref[...].astype(F32)
-        out_ref[:rows, :width] = dq_ref[...]
+        out_ref[:, :width] = dq_ref[...]
         for j, chunk in enumerate(chunks_of(total[:, :width])):
             start = width + LANES * j
-            out_ref[:rows, start : start + LANES] = unrotate(chunk, tables).astype(BF)
-        out_ref[:rows, 2 * width :] = total[:, width:].astype(BF)
+            out_ref[:, start : start + LANES] = unrotate(chunk, tables).astype(BF)
+        out_ref[:, 2 * width :] = total[:, width:].astype(BF)
         grad_ref[...] = input_backward(
-            d_middle_ref[...], out_ref[:rows], x_ref[...].astype(F32), gain_ref, first_ref, gain_scr
+            d_middle_ref[...], out_ref[...], x_ref[...].astype(F32), gain_ref, first_ref, gain_scr
         )
 
     @pl.when(lower_ref[0] == 0)
     def _():
-        out_ref[:rows] = other_ref[...]
+        out_ref[...] = other_ref[...]
         grad_ref[...] = jnp.zeros_like(grad_ref)
         gain_scr[...] = other_attn_ref[...]
 
@@ -458,8 +459,11 @@
         high = gain.astype(BF).astype(F32)
         tail = jnp.where(index == row, high, tail)
         tail = jnp.where(index == row + 1, gain - high, tail)
-    out_ref[rows:] = jnp.zeros((EXTRA, out_ref.shape[1]), BF)
-    out_ref[rows:, :width] = tail.astype(BF)
+    half = rows // 2
+    low_out_ref[...] = out_ref[:half]
+    high_out_ref[:half] = out_ref[half:]
+    high_out_ref[half:] = jnp.zeros((EXTRA, out_ref.shape[1]), BF)
+    high_out_ref[half:, :width] = tail.astype(BF)
 
 
 def local_middle_body(*refs):
@@ -479,10 +483,10 @@
 
 
 def local_back_middle_body(*refs):
-    sources, refs = refs[:-12], refs[-12:]
+    sources, refs = refs[:-13], refs[-13:]
     lower_ref, low_ref, high_ref, middle_ref, gate_up_ref, gain_ref, other_ref = refs[:7]
-    gain_out_ref, d_middle_ref, d_att_ref, right_ref = refs[7:11]
-    weights = Weights(sources, refs[11])
+    gain_out_ref, d_middle_ref, d_att_ref, right_low_ref, right_high_ref = refs[7:12]
+    weights = Weights(sources, refs[12])
     half = gate_up_ref.shape[1] // 2
     upstream = joined([low_ref, high_ref])
     d_gate_up, gain_grad, d_middle, d_attn, d_attended = mlp_backward(
@@ -495,12 +499,13 @@
 
     @pl.when(lower_ref[0] == 1)
     def _():
-        right_ref[:, : 2 * half] = d_gate_up
-        right_ref[:, 2 * half :] = d_attn
+        store_chunks(
+            (right_low_ref, right_high_ref), jnp.concatenate([d_gate_up, d_attn], 1)
+        )
 
     @pl.when(lower_ref[0] == 0)
     def _():
-        right_ref[...] = other_ref[...]
+        store_chunks((right_low_ref, right_high_ref), other_ref[...])
 
 
 def global_project_body(first_ref, low_ref, high_ref, gain_ref, table_ref, normed_ref, sent_ref):
@@ -768,7 +773,7 @@
 
 def early_body(terms, *refs):
     refs, outs = refs[:-3], refs[-3:]
-    rights, lefts = refs[:4], refs[4:]
+    rights, lefts = refs[:-4], refs[-4:]
     width = outs[0].shape[1]
     base = 0
     for rows, (start, end) in terms:
@@ -781,14 +786,15 @@
 
 def late_body(rows, place_ref, *refs):
     refs, outs, scr = refs[:-4], refs[-4:-1], refs[-1]
-    rights, lefts = refs[:4], refs[4:]
-    tokens = lefts[0].shape[2]
+    rights, lefts = refs[:-4], refs[-4:]
     columns = rights[0].shape[1]
     width = columns // 3
     size = outs[0].shape[0]
-    right = jnp.concatenate([ref[:tokens] for ref in rights], 0)
+    low, high = rights[0::2], rights[1::2]
+    half = low[0].shape[0]
+    right = jnp.concatenate([part for a, b in zip(low, high) for part in (a[...], b[:half])], 0)
     by_plane(dot(left_rows_of(lefts, rows), right), 0, outs, slice(0, columns))
-    tail = sum(ref[tokens:, :width].astype(F32) for ref in rights)
+    tail = sum(ref[half:, :width].astype(F32) for ref in high)
     both = jnp.concatenate([tail, jnp.zeros((LANES - EXTRA, width), F32)], 0).T
     lane = lax.broadcasted_iota(jnp.int32, (1, LANES), 1)
     lows = pltpu.roll(both, LANES - 1, 1)
@@ -996,7 +1002,6 @@
             [pltpu.SMEM] * 2 + [pltpu.VMEM] * 8,
         )
         left, d_folded = lax.optimization_barrier((left, d_folded))
-        left = [left[0]] + [partner(left[apart], apart, count) for apart in range(1, 4)]
     else:
         left = [
             plane_rows(jnp.where(lower, a, b).T.reshape(count, -1, rows), group_pos, count)
@@ -1027,7 +1032,6 @@
         1,
     )
     sent = (sent.astype(F32) + back.astype(F32)).astype(BF)
-    left, sent = lax.optimization_barrier((left, sent))
     got = exchange(sent, count)
 
     d_proj_1, gain_attn_1, *grad_1 = on_core(
@@ -1036,25 +1040,29 @@
         (first, got, d_mid_1, *in_1, gain_attn, global_tables),
     )
 
+    if count == GROUP:
+        left, grad_1 = lax.optimization_barrier((left, grad_1))
+        left = [left[0]] + [partner(left[apart], apart, count) for apart in range(1, 4)]
     up_0 = to_other_section(grad_1, -1)
     d_mlp = jnp.concatenate(
         [jnp.where(lower, a, up_1[i * row_count :][:row_count]) for i, a in enumerate(up_0)]
     )
     across_mlp, beside_mlp = partner(d_mlp, 2, count), partner(d_mlp, 1, count)
-    gain_mlp_0, d_mid_0, d_att_0, right = on_core(
+    gain_mlp_0, d_mid_0, d_att_0, *right = on_core(
         local_back_middle_body,
         [
             ((1, width), F32),
             ((rows, width), F32),
             ((rows, width), BF),
-            ((rows, inner + width), BF),
-        ],
+        ]
+        + [((row_count, inner + width), BF)] * micro_count,
         (*others, lower_flag, *up_0, middle_0, gate_up_0, gain_mlp, right_1),
         [pltpu.VMEM((hidden, width), BF)],
         [pltpu.VMEM] * len(others) + [pltpu.SMEM] + [pltpu.VMEM] * 6,
     )
     d_att_0, right, across_mlp = lax.optimization_barrier((d_att_0, right, across_mlp))
-    across, beside = partner(right, 2, count), partner(right, 1, count)
+    across = [partner(item, 2, count) for item in right]
+    beside = [partner(item, 1, count) for item in right]
     d_mlp = [d_mlp, beside_mlp, across_mlp, partner(across_mlp, 1, count)]
     out_near, out_far = first_hop(
         on_core(
@@ -1076,19 +1084,23 @@
     )
     from_after = lax.ppermute(d_before, "dp", down_pairs)
     from_before = lax.ppermute(d_after, "dp", up_pairs)
-    d_proj, grad_0, gain_attn_sum = on_core(
+    *d_proj, grad_0, gain_attn_sum = on_core(
         local_finish_body,
-        [((rows + EXTRA, 3 * width), BF), ((rows, width), BF), ((1, width), F32)],
+        [
+            ((row_count, 3 * width), BF),
+            ((row_count + EXTRA, 3 * width), BF),
+            ((rows, width), BF),
+            ((1, width), F32),
+        ],
         (
             lower_flag, first, dq_0, d_own, from_after, from_before, local_tables, d_mid_0, in_0, gain_attn,
             gain_mlp_0, d_proj_1, gain_attn_1, gain_mlp_1,
         ),
-        [pltpu.VMEM((1, width), F32)],
+        [pltpu.VMEM((1, width), F32), pltpu.VMEM((rows, 3 * width), BF)],
         [pltpu.SMEM] + [pltpu.VMEM] * 13,
     )
-    across, d_proj, out_far = lax.optimization_barrier((across, d_proj, out_far))
-    mlp_out_share = second_hop(out_near, out_far, count)
-    right = [right, beside, across, partner(across, 1, count)]
+    across, out_far, _ = lax.optimization_barrier((across, out_far, d_proj[0]))
+    right = right + beside + across + [partner(item, 1, count) for item in across]
     early_rows = shard_total * (inner // width + 1)
     near, far = first_hop(
         on_core(
@@ -1104,10 +1116,16 @@
         ),
         count,
     )
-    across, beside = partner(d_proj, 2, count), partner(d_proj, 1, count)
+    across = [partner(item, 2, count) for item in d_proj]
+    beside = [partner(item, 1, count) for item in d_proj]
+    far = jnp.concatenate([far, out_far])
     across, far = lax.optimization_barrier((across, far))
-    early = second_hop(near, far, count)
-    late_in = (group_pos[None], d_proj, beside, across, partner(across, 1, count), *left)
+    far = partner(far, 8, count)
+    right = []
+    for low, high in zip(d_proj[:1] + beside[:1] + across[:1], d_proj[1:] + beside[1:] + across[1:]):
+        right += [low, high]
+    right += [partner(item, 1, count) for item in across]
+    late_in = (group_pos[None], *right, *left)
     late = on_core(
         functools.partial(late_body, (0, shard_total)),
         three_parts((shard_total, 3 * width + LANES)),
@@ -1115,6 +1133,9 @@
         [pltpu.VMEM((width, LANES), F32)],
         [pltpu.SMEM] + [pltpu.VMEM] * (len(late_in) - 1),
     )
+    far, late = lax.optimization_barrier((far, list(late)))
+    early = near + far[:early_rows].astype(F32)
+    mlp_out_share = out_near + far[early_rows:].astype(F32)
     late = second_hop(*first_hop(late, count), count)
     parts = [early[p * shard_total : (p + 1) * shard_total] for p in range(inner // width)]
     in_share = jnp.concatenate(parts, 1)

time: 351 us -> 345 us (0.983)
  waiting for transfers between devices: 128 us -> 116 us
  starting transfers between devices: 50.2 us -> 55.8 us
    ppermute x36 -> x41, waiting for transfers between devices: 88 us -> 76.7 us  [partner(): return lax.ppermute(rows, 'dp', [(i, i ^ apart) for i in range(count)])]
    ppermute x36 -> x41, starting transfers between devices: 31 us -> 36.6 us  [partner(): return lax.ppermute(rows, 'dp', [(i, i ^ apart) for i in range(count)])]
  transfers between devices with their start and end apart: 46 -> 51, of which waited for: 23 -> 22; matrix products, arithmetic and copies ran while one was open for 6% -> 6% of each run, Pallas kernels for 6% -> 7%
where the time goes in v8:
time: 345 us; the launch traced here: 344 us
  waiting for transfers between devices  116 us (34%)
  Pallas kernels  56.9 us (16%)
  starting transfers between devices  55.8 us (16%)
  blocking collectives  54.8 us (16%)
  local copies, waits for them, and re-layouts  40.5 us (12%)
  between operations  15 us (4%)
  other arithmetic  4.35 us (1%)
    ppermute x41, waiting for transfers between devices, partner(): return lax.ppermute(rows, 'dp', [(i, i ^ apart) for i in range(count)])  76.7 us
    pallas_call x17, Pallas kernels, on_core(): pl.pallas_call(body, out_shape=[jax.ShapeDtypeStruct(shape, dtype) for sh...  56.9 us
    all_to_all x3, blocking collectives, exchange(): return lax.all_to_all(blocks, 'dp', 0, 0, axis_index_groups=groups)  54.8 us
    ppermute x41, starting transfers between devices, partner(): return lax.ppermute(rows, 'dp', [(i, i ^ apart) for i in range(count)])  36.6 us
    all_gather x1, waiting for transfers between devices, on_device(): others = [lax.all_gather(stacked, 'dp', axis=0, tiled=True)]  28.2 us
    unnamed x102, local copies, waits for them, and re-layouts  21.8 us
    dynamic_update_slice x16, local copies, waits for them, and re-layouts, gather_rows(): whole = lax.dynamic_update_slice(whole, item[None], start)  11.5 us
    ppermute x4, waiting for transfers between devices, to_other_section(): return [lax.ppermute(rows, 'section', pairs) for rows in chunks]  8.35 us
  transfers between devices with their start and end apart: 51, of which 22 were waited for; matrix products, arithmetic and copies ran while one was open for 6% of the time, Pallas kernels for 7%

profile of v8, /device:TPU:0, one launch (start us, length us, event | category | flops | bytes accessed | tf_op | source)
XLA Modules:
  0.0 343.6 jit_solution(18283961860735377132)
XLA Ops:
  10.3 3.0 collective-permute-start.1
  13.3 1.6 collective-permute-start.2
  14.9 2.6 collective-permute-start.3
  23.5 2.1 broadcast_in_dim.105
  27.5 6.9 %collective-permute-done.3 = bf16[48,2432]{1,0:T(8,128)(2,1)S(1)} collective-permute-done((bf16[48,2432]{1,0:T(8,128)(2,1)S(1)}, bf16[48,2432]{1,0:T(8,128)(2,1)S(1)}, u32[]{:S(2)}, u32[]{:S(2)}) %collective-permute-start.3) | collective-permute-done | bytes 233504 | tf_op jit(solution)/shard_map/ppermute | solution.py:707
  34.9 1.5 collective-permute-start.7
  40.0 5.6 %collective-permute-done.6 = bf16[48,2432]{1,0:T(8,128)(2,1)S(1)} collective-permute-done((bf16[48,2432]{1,0:T(8,128)(2,1)S(1)}, bf16[48,2432]{1,0:T(8,128)(2,1)S(1)}, u32[]{:S(2)}, u32[]{:S(2)}) %collective-permute-start.6) | collective-permute-done | bytes 233504 | tf_op jit(solution)/shard_map/ppermute | solution.py:707
  46.3 3.2 collective-permute-done.7
  57.0 3.1 shard_map.154
  60.8 2.1 collective-permute-start.16
  64.8 1.8 collective-permute-done.17.after_ref
  66.7 3.6 %shard_map.155 = (bf16[128,768]{1,0:T(8,128)(2,1)S(1)}, f32[12,1,128]{2,1,0:T(1,128)S(1)}) custom-call(bf16[128,768]{1,0:T(8,128)(2,1)S(1)} %get-tuple-element.80.q_ref, bf16[128,1536]{1,0:T(8,128)(2,1)S(1)} %collective-permute-done.16.before_ref, bf16[128,1536]{1,0:T(8,128)(2,1)S(1)} %get-tuple-element.81.own_ref, ...), custom_call_target="tpu_custom_call" | custom-call | flops 1024 | bytes 1024 | tf_op jit(solution)/shard_map/pallas_call | solution.py:65
  70.3 28.2 %all-gather.2.cloned.1.call-done.refs_0_ = bf16[768,4352]{1,0:T(8,128)(2,1)} async-done(((bf16[48,4352]{1,0:T(8,128)(2,1)}), bf16[768,4352]{1,0:T(8,128)(2,1)}) %all-gather.2.cloned.1.call-update) | async-done | bytes 6684688 | tf_op jit(solution)/shard_map/all_gather | solution.py:879
  98.5 4.4 %shard_map.156 = (bf16[128,768]{1,0:T(8,128)(2,1)S(1)}, bf16[128,1152]{1,0:T(8,128)(2,1)S(1)}, f32[128,768]{1,0:T(8,128)S(1)}, f32[128,2304]{1,0:T(8,128)S(1)}, ...) custom-call(bf16[768,4352]{1,0:T(8,128)(2,1)} %all-gather.2.cloned.1.call-done.refs_0_, ...), custom_call_target="tpu_custom_call" | custom-call | flops 1024 | bytes 1024 | tf_op jit(solution)/shard_map/pallas_call | solution.py:65
  105.5 3.4 collective-permute-start.18
  108.9 1.3 collective-permute-start.19
  110.6 1.4 collective-permute-done.18.low_ref.refs_2_
  112.0 1.4 collective-permute-done.19.high_ref.refs_3_
  113.5 3.1 shard_map.157
  116.6 21.2 %all_to_all.20.got_ref = bf16[16,144,128]{2,1,0:T(8,128)(2,1)S(1)} all-to-all(bf16[16,144,128]{2,1,0:T(8,128)(2,1)S(1)} %get-tuple-element.86), channel_id=1, replica_groups={{0,1,2,3,4,5,6,7,8,9,10,11,12,13,14,15},{16,17,18,19,20,21,22,23,24,25,..., dimensions={0} | all-to-all | bytes 1179648 | tf_op jit(solution)/shard_map/all_to_all | solution.py:698
  139.5 6.0 %shard_map.158 = (bf16[16,48,128]{2,1,0:T(8,128)(2,1)S(1)}, f32[6,1,256]{2,1,0:T(1,128)S(1)}) custom-call(bf16[16,144,128]{2,1,0:T(8,128)(2,1)S(1)} %all_to_all.20.got_ref, bf16[16,64,128]{2,1,0:T(8,128)(2,1)S(1)} %collective-permute-done.20.other_ref, s32[1024,1]{1,0:T(8,128)S(1)} %copy.19.own_seg_ref, s32[1024,1]{1,0:T(8,128)S(1)} %copy.20.shared_seg_ref), custom_call_target="tpu_custom_call" | custom-call | flops 1024 | bytes 1024 | tf_op jit(solution)/shard_map/pallas_call | solution.py:65
  145.5 11.8 %all_to_all.21.refs_1_ = bf16[16,48,128]{2,1,0:T(8,128)(2,1)S(1)} all-to-all(bf16[16,48,128]{2,1,0:T(8,128)(2,1)S(1)} %get-tuple-element.87), channel_id=1, replica_groups={{0,1,2,3,4,5,6,7,8,9,10,11,12,13,14,15},{16,17,18,19,20,21,22,23,24,25,..., dimensions={0} | all-to-all | bytes 393216 | tf_op jit(solution)/shard_map/all_to_all | solution.py:698
  157.3 7.7 %shard_map.159 = (bf16[128,768]{1,0:T(8,128)(2,1)S(1)}, bf16[128,768]{1,0:T(8,128)(2,1)S(1)}, bf16[128,768]{1,0:T(8,128)(2,1)S(1)}, bf16[128,1152]{1,0:T(8,128)(...) custom-call(bf16[768,4352]{1,0:T(8,128)(2,1)} %all-gather.2.cloned.1, ...), custom_call_target="tpu_custom_call" | custom-call | flops 1024 | bytes 1024 | tf_op jit(solution)/shard_map/pallas_call | solution.py:65
  169.4 4.2 %all-to-all-start.2 = ((bf16[16,48,128]{2,1,0:T(8,128)(2,1)}), bf16[16,48,128]{2,1,0:T(8,128)(2,1)}, u32[]{:S(2)}, u32[]{:S(2)}) async-start(bf16[16,48,128]{2,1,0:T(8,128)(2,1)} %get-tuple-element.97), calls=%async_computation.2 | async-start | bytes 393216 | tf_op jit(solution)/shard_map/all_to_all | solution.py:698
  183.6 8.3 %shard_map.161 = (bf16[16,144,128]{2,1,0:T(8,128)(2,1)S(1)}, bf16[16,64,128]{2,1,0:T(8,128)(2,1)S(1)}) custom-call(bf16[16,144,128]{2,1,0:T(8,128)(2,1)S(1)} %all_to_all.20.got_ref, bf16[16,64,128]{2,1,0:T(8,128)(2,1)S(1)} %copy-done.10, s32[1024,1]{1,0:T(8,128)S(1)} %copy.19.own_seg_ref, s32[1024,1]{1,0:T(8,128)S(1)} %copy.20.shared_seg_ref, ...), custom_call_target="tpu_custom_call" | custom-call | flops 1024 | bytes 1024 | tf_op jit(solution)/shard_map/pallas_call | solution.py:65
  192.1 1.4 collective-permute-done.21
  193.8 21.8 %all_to_all.22.got_ref = bf16[16,144,128]{2,1,0:T(8,128)(2,1)S(1)} all-to-all(bf16[16,144,128]{2,1,0:T(8,128)(2,1)S(1)} %add_convert_fusion), channel_id=1, replica_groups={{0,1,2,3,4,5,6,7,8,9,10,11,12,13,14,15},{16,17,18,19,20,21,22,23,24,25,..., dimensions={0} | all-to-all | bytes 1179648 | tf_op jit(solution)/shard_map/all_to_all | solution.py:698
  215.6 3.8 %shard_map.162 = (bf16[128,2304]{1,0:T(8,128)(2,1)S(1)}, f32[1,768]{1,0:T(1,128)S(1)}, bf16[64,768]{1,0:T(8,128)(2,1)S(1)}, bf16[64,768]{1,0:T(8,128)(2,1)S(1)}) custom-call(bf16[768,2432]{1,0:T(8,128)(2,1)} %bitcast.23.first_ref, bf16[16,144,128]{2,1,0:T(8,128)(2,1)S(1)} %all_to_all.22.got_ref, f32[128,768]{1,0:T(8,128)S(1)} %copy-done.22, ...), custom_call_target="tpu_custom_call" | custom-call | flops 1024 | bytes 1024 | tf_op jit(solution)/shard_map/pallas_call | solution.py:65
  222.9 4.1 %collective-permute-done.22.refs_2_ = bf16[64,768]{1,0:T(8,128)(2,1)S(1)} collective-permute-done((bf16[64,768]{1,0:T(8,128)(2,1)S(1)}, bf16[64,768]{1,0:T(8,128)(2,1)S(1)}, u32[]{:S(2)}, u32[]{:S(2)}) %collective-permute-start.22) | collective-permute-done | bytes 98336 | tf_op jit(solution)/shard_map/ppermute | solution.py:703
  226.9 1.4 collective-permute-done.23.refs_3_
  229.3 1.4 collective-permute-start.33
  230.7 6.1 %shard_map.163 = (f32[1,768]{1,0:T(1,128)S(1)}, f32[128,768]{1,0:T(8,128)S(1)}, bf16[128,768]{1,0:T(8,128)(2,1)S(1)}, bf16[64,3072]{1,0:T(8,128)(2,1)S(1)}, bf16[64,3072]{1,0:T(8,128)(2,1)S(1)}) custom-call(bf16[768,4352]{1,0:T(8,128)(2,1)} %all-gather.2.cloned.1.call-done.refs_0_, s32[1]{0:T(128)} %bitcast.37.lower_ref.refs_1_, ...), custom_call_target="tpu_custom_call" | custom-call | flops 1024 | bytes 1024 | tf_op jit(solution)/shard_map/pallas_call | solution.py:65
  236.9 3.5 %shard_map.164 = (bf16[128,768]{1,0:T(8,128)(2,1)S(1)}, f32[128,1536]{1,0:T(8,128)S(1)}, bf16[128,1536]{1,0:T(8,128)(2,1)S(1)}, bf16[128,1536]{1,0:T(8,128)(2,1)S(1)}) custom-call(bf16[128,768]{1,0:T(8,128)(2,1)S(1)} %copy-done.14, bf16[128,1536]{1,0:T(8,128)(2,1)S(1)} %copy-done.4, bf16[128,1536]{1,0:T(8,128)(2,1)S(1)} %copy-done.2, ...), custom_call_target="tpu_custom_call" | custom-call | flops 1024 | bytes 1024 | tf_op jit(solution)/shard_map/pallas_call | solution.py:65
  241.8 3.1 collective-permute-start.26
  245.3 1.7 collective-permute-start.38
  247.6 1.4 collective-permute-start.32
  250.1 7.5 %collective-permute-start.30 = (bf16[64,3072]{1,0:T(8,128)(2,1)S(1)}, bf16[64,3072]{1,0:T(8,128)(2,1)S(1)}, u32[]{:S(2)}, u32[]{:S(2)}) collective-permute-start(bf16[64,3072]{1,0:T(8,128)(2,1)S(1)} %get-tuple-element.128.refs_1_), channel_id=1, source_target_pairs={{0,1},{1,0},{2,3},{3,2},{4,5},{5,4},{6,7},{7,6},{8,9},{9,8},{10,11... | collective-permute-start | bytes 1179656 | tf_op jit(solution)/shard_map/ppermute | solution.py:707
  257.7 4.0 %shard_map.165 = (bf16[64,2304]{1,0:T(8,128)(2,1)S(1)}, bf16[80,2304]{1,0:T(8,128)(2,1)S(1)}, bf16[128,768]{1,0:T(8,128)(2,1)S(1)}, f32[1,768]{1,0:T(1,128)}) custom-call(s32[1]{0:T(128)} %bitcast.37.lower_ref.refs_1_, bf16[768,2432]{1,0:T(8,128)(2,1)} %bitcast.23.first_ref, bf16[128,768]{1,0:T(8,128)(2,1)S(1)} %get-tuple-element.115.dq_ref, ...), custom_call_target="tpu_custom_call" | custom-call | flops 1024 | bytes 1024 | tf_op jit(solution)/shard_map/pallas_call | solution.py:65
  261.7 5.3 %collective-permute-done.32.refs_5_ = bf16[64,3072]{1,0:T(8,128)(2,1)S(1)} collective-permute-done((bf16[64,3072]{1,0:T(8,128)(2,1)S(1)}, bf16[64,3072]{1,0:T(8,128)(2,1)S(1)}, u32[]{:S(2)}, u32[]{:S(2)}) %collective-permute-start.32) | collective-permute-done | bytes 393248 | tf_op jit(solution)/shard_map/ppermute | solution.py:707
  267.0 3.4 collective-permute-start.39
  270.4 1.3 collective-permute-done.39.refs_6_
  273.1 2.0 collective-permute-start.41
  277.4 11.5 %collective-permute-done.41 = bf16[384,768]{1,0:T(8,128)(2,1)S(1)} collective-permute-done((bf16[384,768]{1,0:T(8,128)(2,1)S(1)}, bf16[384,768]{1,0:T(8,128)(2,1)S(1)}, u32[]{:S(2)}, u32[]{:S(2)}) %collective-permute-start.41) | collective-permute-done | bytes 589856 | tf_op jit(solution)/shard_map/ppermute | solution.py:707
  288.9 2.8 collective-permute-done.28.refs_5_
  291.8 1.4 collective-permute-start.42
  295.9 15.7 %collective-permute-done.42 = bf16[264,768]{1,0:T(8,128)(2,1)S(1)} collective-permute-done((bf16[264,768]{1,0:T(8,128)(2,1)S(1)}, bf16[264,768]{1,0:T(8,128)(2,1)S(1)}, u32[]{:S(2)}, u32[]{:S(2)}) %collective-permute-start.42) | collective-permute-done | bytes 405536 | tf_op jit(solution)/shard_map/ppermute | solution.py:707
  313.2 10.1 %collective-permute-done.47 = bf16[96,2432]{1,0:T(8,128)(2,1)S(1)} collective-permute-done((bf16[96,2432]{1,0:T(8,128)(2,1)S(1)}, bf16[96,2432]{1,0:T(8,128)(2,1)S(1)}, u32[]{:S(2)}, u32[]{:S(2)}) %collective-permute-start.47) | collective-permute-done | bytes 466976 | tf_op jit(solution)/shard_map/ppermute | solution.py:707
  324.2 10.9 %collective-permute-done.48 = bf16[48,2432]{1,0:T(8,128)(2,1)S(1)} collective-permute-done((bf16[48,2432]{1,0:T(8,128)(2,1)S(1)}, bf16[48,2432]{1,0:T(8,128)(2,1)S(1)}, u32[]{:S(2)}, u32[]{:S(2)}) %collective-permute-start.48) | collective-permute-done | bytes 233504 | tf_op jit(solution)/shard_map/ppermute | solution.py:707
  (255 shorter events, 63.6 us)
Async XLA Ops:
  7.2 91.4 %all-gather.2.cloned.1.call-start = ((), (), s32[]{:S(2)}) async-start(), calls=%async_computation.4 | async-start | bytes 7102464 | tf_op jit(solution)/shard_map/all_gather | solution.py:879
  10.3 13.0 %collective-permute-start.1 = (bf16[48,2432]{1,0:T(8,128)(2,1)S(1)}, bf16[48,2432]{1,0:T(8,128)(2,1)S(1)}, u32[]{:S(2)}, u32[]{:S(2)}) collective-permute-start(bf16[48,2432]{1,0:T(8,128)(2,1)S(1)} %shard_map.153), channel_id=1, source_target_pairs={{0,2},{1,3},{2,0},{3,1},{4,6},{5,7},{6,4},{7,5},{8,10},{9,11},{10,... | collective-permute-start | bytes 700424 | tf_op jit(solution)/shard_map/ppermute | solution.py:707
  13.3 13.9 %collective-permute-start.2 = (bf16[48,2432]{1,0:T(8,128)(2,1)S(1)}, bf16[48,2432]{1,0:T(8,128)(2,1)S(1)}, u32[]{:S(2)}, u32[]{:S(2)}) collective-permute-start(bf16[48,2432]{1,0:T(8,128)(2,1)S(1)} %shard_map.153), channel_id=1, source_target_pairs={{0,4},{1,5},{2,6},{3,7},{4,0},{5,1},{6,2},{7,3},{8,12},{9,13},{10,... | collective-permute-start | bytes 700424 | tf_op jit(solution)/shard_map/ppermute | solution.py:707
  14.9 19.5 %collective-permute-start.3 = (bf16[48,2432]{1,0:T(8,128)(2,1)S(1)}, bf16[48,2432]{1,0:T(8,128)(2,1)S(1)}, u32[]{:S(2)}, u32[]{:S(2)}) collective-permute-start(bf16[48,2432]{1,0:T(8,128)(2,1)S(1)} %shard_map.153), channel_id=1, source_target_pairs={{0,8},{1,9},{2,10},{3,11},{4,12},{5,13},{6,14},{7,15},{8,0},{9,1},... | collective-permute-start | bytes 700424 | tf_op jit(solution)/shard_map/ppermute | solution.py:707
  17.5 17.5 %collective-permute-start.4 = (bf16[48,2432]{1,0:T(8,128)(2,1)S(1)}, bf16[48,2432]{1,0:T(8,128)(2,1)S(1)}, u32[]{:S(2)}, u32[]{:S(2)}) collective-permute-start(bf16[48,2432]{1,0:T(8,128)(2,1)S(1)} %shard_map.153), channel_id=1, source_target_pairs={{0,12},{1,13},{2,14},{3,15},{4,8},{5,9},{6,10},{7,11},{8,4},{9,5},... | collective-permute-start | bytes 700424 | tf_op jit(solution)/shard_map/ppermute | solution.py:707
  19.6 30.6 %collective-permute-start.8 = (bf16[48,2432]{1,0:T(8,128)(2,1)S(1)}, bf16[48,2432]{1,0:T(8,128)(2,1)S(1)}, u32[]{:S(2)}, u32[]{:S(2)}) collective-permute-start(bf16[48,2432]{1,0:T(8,128)(2,1)S(1)} %shard_map.153), channel_id=1, source_target_pairs={{0,1},{1,0},{2,3},{3,2},{4,5},{5,4},{6,7},{7,6},{8,9},{9,8},{10,11... | collective-permute-start | bytes 700424 | tf_op jit(solution)/shard_map/ppermute | solution.py:707
  26.8 24.6 %collective-permute-start.9 = (bf16[48,2432]{1,0:T(8,128)(2,1)S(1)}, bf16[48,2432]{1,0:T(8,128)(2,1)S(1)}, u32[]{:S(2)}, u32[]{:S(2)}) collective-permute-start(bf16[48,2432]{1,0:T(8,128)(2,1)S(1)} %collective-permute-done.1), channel_id=1, source_target_pairs={{0,1},{1,0},{2,3},{3,2},{4,5},{5,4},{6,7},{7,6},{8,9},{9,8},{10,11... | collective-permute-start | bytes 700424 | tf_op jit(solution)/shard_map/ppermute | solution.py:707
  27.2 12.1 %collective-permute-start.5 = (bf16[48,2432]{1,0:T(8,128)(2,1)S(1)}, bf16[48,2432]{1,0:T(8,128)(2,1)S(1)}, u32[]{:S(2)}, u32[]{:S(2)}) collective-permute-start(bf16[48,2432]{1,0:T(8,128)(2,1)S(1)} %collective-permute-done.2), channel_id=1, source_target_pairs={{0,2},{1,3},{2,0},{3,1},{4,6},{5,7},{6,4},{7,5},{8,10},{9,11},{10,... | collective-permute-start | bytes 700424 | tf_op jit(solution)/shard_map/ppermute | solution.py:707
  34.4 11.2 %collective-permute-start.6 = (bf16[48,2432]{1,0:T(8,128)(2,1)S(1)}, bf16[48,2432]{1,0:T(8,128)(2,1)S(1)}, u32[]{:S(2)}, u32[]{:S(2)}) collective-permute-start(bf16[48,2432]{1,0:T(8,128)(2,1)S(1)} %collective-permute-done.3), channel_id=1, source_target_pairs={{0,2},{1,3},{2,0},{3,1},{4,6},{5,7},{6,4},{7,5},{8,10},{9,11},{10,... | collective-permute-start | bytes 700424 | tf_op jit(solution)/shard_map/ppermute | solution.py:707
  34.9 14.5 %collective-permute-start.7 = (bf16[48,2432]{1,0:T(8,128)(2,1)S(1)}, bf16[48,2432]{1,0:T(8,128)(2,1)S(1)}, u32[]{:S(2)}, u32[]{:S(2)}) collective-permute-start(bf16[48,2432]{1,0:T(8,128)(2,1)S(1)} %collective-permute-done.4), channel_id=1, source_target_pairs={{0,2},{1,3},{2,0},{3,1},{4,6},{5,7},{6,4},{7,5},{8,10},{9,11},{10,... | collective-permute-start | bytes 700424 | tf_op jit(solution)/shard_map/ppermute | solution.py:707
  39.3 12.9 %collective-permute-start.10 = (bf16[48,2432]{1,0:T(8,128)(2,1)S(1)}, bf16[48,2432]{1,0:T(8,128)(2,1)S(1)}, u32[]{:S(2)}, u32[]{:S(2)}) collective-permute-start(bf16[48,2432]{1,0:T(8,128)(2,1)S(1)} %collective-permute-done.2), channel_id=1, source_target_pairs={{0,1},{1,0},{2,3},{3,2},{4,5},{5,4},{6,7},{7,6},{8,9},{9,8},{10,11... | collective-permute-start | bytes 700424 | tf_op jit(solution)/shard_map/ppermute | solution.py:707
  45.6 8.5 %collective-permute-start.12 = (bf16[48,2432]{1,0:T(8,128)(2,1)S(1)}, bf16[48,2432]{1,0:T(8,128)(2,1)S(1)}, u32[]{:S(2)}, u32[]{:S(2)}) collective-permute-start(bf16[48,2432]{1,0:T(8,128)(2,1)S(1)} %collective-permute-done.3), channel_id=1, source_target_pairs={{0,1},{1,0},{2,3},{3,2},{4,5},{5,4},{6,7},{7,6},{8,9},{9,8},{10,11... | collective-permute-start | bytes 700424 | tf_op jit(solution)/shard_map/ppermute | solution.py:707
  49.5 6.1 %collective-permute-start.14 = (bf16[48,2432]{1,0:T(8,128)(2,1)S(1)}, bf16[48,2432]{1,0:T(8,128)(2,1)S(1)}, u32[]{:S(2)}, u32[]{:S(2)}) collective-permute-start(bf16[48,2432]{1,0:T(8,128)(2,1)S(1)} %collective-permute-done.4), channel_id=1, source_target_pairs={{0,1},{1,0},{2,3},{3,2},{4,5},{5,4},{6,7},{7,6},{8,9},{9,8},{10,11... | collective-permute-start | bytes 700424 | tf_op jit(solution)/shard_map/ppermute | solution.py:707
  50.2 3.2 collective-permute-start.11
  51.4 3.4 collective-permute-start.13
  52.2 4.1 %collective-permute-start.15 = (bf16[48,2432]{1,0:T(8,128)(2,1)S(1)}, bf16[48,2432]{1,0:T(8,128)(2,1)S(1)}, u32[]{:S(2)}, u32[]{:S(2)}) collective-permute-start(bf16[48,2432]{1,0:T(8,128)(2,1)S(1)} %collective-permute-done.7), channel_id=1, source_target_pairs={{0,1},{1,0},{2,3},{3,2},{4,5},{5,4},{6,7},{7,6},{8,9},{9,8},{10,11... | collective-permute-start | bytes 700424 | tf_op jit(solution)/shard_map/ppermute | solution.py:707
  60.8 4.1 %collective-permute-start.16 = (bf16[128,1536]{1,0:T(8,128)(2,1)S(1)}, bf16[128,1536]{1,0:T(8,128)(2,1)S(1)}, u32[]{:S(2)}, u32[]{:S(2)}) collective-permute-start(bf16[128,1536]{1,0:T(8,128)(2,1)S(1)} %get-tuple-element.81.own_ref), channel_id=1, source_target_pairs={{0,1},{1,2},{2,3},{3,4},{4,5},{5,6},{6,7},{7,8},{8,9},{9,10},{10,1... | collective-permute-start | bytes 1179656 | tf_op jit(solution)/shard_map/ppermute | solution.py:926
  62.9 3.8 %collective-permute-start.17 = (bf16[128,1536]{1,0:T(8,128)(2,1)S(1)}, bf16[128,1536]{1,0:T(8,128)(2,1)S(1)}, u32[]{:S(2)}, u32[]{:S(2)}) collective-permute-start(bf16[128,1536]{1,0:T(8,128)(2,1)S(1)} %get-tuple-element.81.own_ref), channel_id=1, source_target_pairs={{1,0},{2,1},{3,2},{4,3},{5,4},{6,5},{7,6},{8,7},{9,8},{10,9},{11,1... | collective-permute-start | bytes 1179656 | tf_op jit(solution)/shard_map/ppermute | solution.py:928
  105.5 6.5 %collective-permute-start.18 = (bf16[64,768]{1,0:T(8,128)(2,1)S(1)}, bf16[64,768]{1,0:T(8,128)(2,1)S(1)}, u32[]{:S(2)}, u32[]{:S(2)}) collective-permute-start(bf16[64,768]{1,0:T(8,128)(2,1)S(1)} %get-tuple-element.84), channel_id=1, source_target_pairs={{0,16},{1,17},{2,18},{3,19},{4,20},{5,21},{6,22},{7,23},{8,24},{9,... | collective-permute-start | bytes 294920 | tf_op jit(solution)/shard_map/ppermute | solution.py:703
  108.9 4.6 %collective-permute-start.19 = (bf16[64,768]{1,0:T(8,128)(2,1)S(1)}, bf16[64,768]{1,0:T(8,128)(2,1)S(1)}, u32[]{:S(2)}, u32[]{:S(2)}) collective-permute-start(bf16[64,768]{1,0:T(8,128)(2,1)S(1)} %get-tuple-element.85), channel_id=1, source_target_pairs={{0,16},{1,17},{2,18},{3,19},{4,20},{5,21},{6,22},{7,23},{8,24},{9,... | collective-permute-start | bytes 294920 | tf_op jit(solution)/shard_map/ppermute | solution.py:703
  169.4 13.2 %all-to-all-start.2 = ((bf16[16,48,128]{2,1,0:T(8,128)(2,1)}), bf16[16,48,128]{2,1,0:T(8,128)(2,1)}, u32[]{:S(2)}, u32[]{:S(2)}) async-start(bf16[16,48,128]{2,1,0:T(8,128)(2,1)} %get-tuple-element.97), calls=%async_computation.2 | async-start | bytes 393216 | tf_op jit(solution)/shard_map/all_to_all | solution.py:698
  219.4 7.5 %collective-permute-start.22 = (bf16[64,768]{1,0:T(8,128)(2,1)S(1)}, bf16[64,768]{1,0:T(8,128)(2,1)S(1)}, u32[]{:S(2)}, u32[]{:S(2)}) collective-permute-start(bf16[64,768]{1,0:T(8,128)(2,1)S(1)} %get-tuple-element.106), channel_id=1, source_target_pairs={{16,0},{17,1},{18,2},{19,3},{20,4},{21,5},{22,6},{23,7},{24,8},{25... | collective-permute-start | bytes 294920 | tf_op jit(solution)/shard_map/ppermute | solution.py:703
  220.7 7.6 %collective-permute-start.23 = (bf16[64,768]{1,0:T(8,128)(2,1)S(1)}, bf16[64,768]{1,0:T(8,128)(2,1)S(1)}, u32[]{:S(2)}, u32[]{:S(2)}) collective-permute-start(bf16[64,768]{1,0:T(8,128)(2,1)S(1)} %get-tuple-element.107), channel_id=1, source_target_pairs={{16,0},{17,1},{18,2},{19,3},{20,4},{21,5},{22,6},{23,7},{24,8},{25... | collective-permute-start | bytes 294920 | tf_op jit(solution)/shard_map/ppermute | solution.py:703
  222.1 18.3 %collective-permute-start.35 = (bf16[4,216,128]{2,1,0:T(8,128)(2,1)S(1)}, bf16[4,216,128]{2,1,0:T(8,128)(2,1)S(1)}, u32[]{:S(2)}, u32[]{:S(2)}) collective-permute-start(bf16[4,216,128]{2,1,0:T(8,128)(2,1)S(1)} %get-tuple-element.156), channel_id=1, source_target_pairs={{0,1},{1,0},{2,3},{3,2},{4,5},{5,4},{6,7},{7,6},{8,9},{9,8},{10,11... | collective-permute-start | bytes 663560 | tf_op jit(solution)/shard_map/ppermute | solution.py:707
  222.3 19.5 %collective-permute-start.36 = (bf16[4,216,128]{2,1,0:T(8,128)(2,1)S(1)}, bf16[4,216,128]{2,1,0:T(8,128)(2,1)S(1)}, u32[]{:S(2)}, u32[]{:S(2)}) collective-permute-start(bf16[4,216,128]{2,1,0:T(8,128)(2,1)S(1)} %get-tuple-element.155), channel_id=1, source_target_pairs={{0,2},{1,3},{2,0},{3,1},{4,6},{5,7},{6,4},{7,5},{8,10},{9,11},{10,... | collective-permute-start | bytes 663560 | tf_op jit(solution)/shard_map/ppermute | solution.py:707
  228.4 8.3 %collective-permute-start.24 = (bf16[128,768]{1,0:T(8,128)(2,1)S(1)}, bf16[128,768]{1,0:T(8,128)(2,1)S(1)}, u32[]{:S(2)}, u32[]{:S(2)}) collective-permute-start(bf16[128,768]{1,0:T(8,128)(2,1)S(1)} %pad_maximum_fusion.2.refs_0_), channel_id=1, source_target_pairs={{0,2},{1,3},{2,0},{3,1},{4,6},{5,7},{6,4},{7,5},{8,10},{9,11},{10,... | collective-permute-start | bytes 589832 | tf_op jit(solution)/shard_map/ppermute | solution.py:707
  229.1 15.7 %collective-permute-start.37 = (bf16[4,216,128]{2,1,0:T(8,128)(2,1)S(1)}, bf16[4,216,128]{2,1,0:T(8,128)(2,1)S(1)}, u32[]{:S(2)}, u32[]{:S(2)}) collective-permute-start(bf16[4,216,128]{2,1,0:T(8,128)(2,1)S(1)} %get-tuple-element.154), channel_id=1, source_target_pairs={{0,3},{1,2},{2,1},{3,0},{4,7},{5,6},{6,5},{7,4},{8,11},{9,10},{10,... | collective-permute-start | bytes 663560 | tf_op jit(solution)/shard_map/ppermute | solution.py:707
  229.3 15.6 %collective-permute-start.33 = (bf16[128,768]{1,0:T(8,128)(2,1)S(1)}, bf16[128,768]{1,0:T(8,128)(2,1)S(1)}, u32[]{:S(2)}, u32[]{:S(2)}) collective-permute-start(bf16[128,768]{1,0:T(8,128)(2,1)S(1)} %pad_maximum_fusion.2.refs_0_), channel_id=1, source_target_pairs={{0,1},{1,0},{2,3},{3,2},{4,5},{5,4},{6,7},{7,6},{8,9},{9,8},{10,11... | collective-permute-start | bytes 589832 | tf_op jit(solution)/shard_map/ppermute | solution.py:707
  236.8 8.1 %collective-permute-start.34 = (bf16[128,768]{1,0:T(8,128)(2,1)S(1)}, bf16[128,768]{1,0:T(8,128)(2,1)S(1)}, u32[]{:S(2)}, u32[]{:S(2)}) collective-permute-start(bf16[128,768]{1,0:T(8,128)(2,1)S(1)} %collective-permute-done.24.refs_2_), channel_id=1, source_target_pairs={{0,1},{1,0},{2,3},{3,2},{4,5},{5,4},{6,7},{7,6},{8,9},{9,8},{10,11... | collective-permute-start | bytes 589832 | tf_op jit(solution)/shard_map/ppermute | solution.py:707
  240.4 8.5 %collective-permute-start.25 = (bf16[128,1536]{1,0:T(8,128)(2,1)S(1)}, bf16[128,1536]{1,0:T(8,128)(2,1)S(1)}, u32[]{:S(2)}, u32[]{:S(2)}) collective-permute-start(bf16[128,1536]{1,0:T(8,128)(2,1)S(1)} %get-tuple-element.117), channel_id=1, source_target_pairs={{1,0},{2,1},{3,2},{4,3},{5,4},{6,5},{7,6},{8,7},{9,8},{10,9},{11,1... | collective-permute-start | bytes 1179656 | tf_op jit(solution)/shard_map/ppermute | solution.py:1085
  241.8 8.4 %collective-permute-start.26 = (bf16[128,1536]{1,0:T(8,128)(2,1)S(1)}, bf16[128,1536]{1,0:T(8,128)(2,1)S(1)}, u32[]{:S(2)}, u32[]{:S(2)}) collective-permute-start(bf16[128,1536]{1,0:T(8,128)(2,1)S(1)} %get-tuple-element.118), channel_id=1, source_target_pairs={{0,1},{1,2},{2,3},{3,4},{4,5},{5,6},{6,7},{7,8},{8,9},{9,10},{10,1... | collective-permute-start | bytes 1179656 | tf_op jit(solution)/shard_map/ppermute | solution.py:1086
  245.3 16.4 %collective-permute-start.38 = (bf16[144,768]{1,0:T(8,128)(2,1)S(1)}, bf16[144,768]{1,0:T(8,128)(2,1)S(1)}, u32[]{:S(2)}, u32[]{:S(2)}) collective-permute-start(bf16[144,768]{1,0:T(8,128)(2,1)S(1)} %get-tuple-element.132), channel_id=1, source_target_pairs={{0,4},{1,5},{2,6},{3,7},{4,0},{5,1},{6,2},{7,3},{8,12},{9,13},{10,... | collective-permute-start | bytes 663560 | tf_op jit(solution)/shard_map/ppermute | solution.py:707
  246.9 14.8 %collective-permute-start.31 = (bf16[64,3072]{1,0:T(8,128)(2,1)S(1)}, bf16[64,3072]{1,0:T(8,128)(2,1)S(1)}, u32[]{:S(2)}, u32[]{:S(2)}) collective-permute-start(bf16[64,3072]{1,0:T(8,128)(2,1)S(1)} %get-tuple-element.127.refs_0_), channel_id=1, source_target_pairs={{0,2},{1,3},{2,0},{3,1},{4,6},{5,7},{6,4},{7,5},{8,10},{9,11},{10,... | collective-permute-start | bytes 1179656 | tf_op jit(solution)/shard_map/ppermute | solution.py:707
  247.6 19.5 %collective-permute-start.32 = (bf16[64,3072]{1,0:T(8,128)(2,1)S(1)}, bf16[64,3072]{1,0:T(8,128)(2,1)S(1)}, u32[]{:S(2)}, u32[]{:S(2)}) collective-permute-start(bf16[64,3072]{1,0:T(8,128)(2,1)S(1)} %get-tuple-element.128.refs_1_), channel_id=1, source_target_pairs={{0,2},{1,3},{2,0},{3,1},{4,6},{5,7},{6,4},{7,5},{8,10},{9,11},{10,... | collective-permute-start | bytes 1179656 | tf_op jit(solution)/shard_map/ppermute | solution.py:707
  249.0 21.4 %collective-permute-start.29 = (bf16[64,3072]{1,0:T(8,128)(2,1)S(1)}, bf16[64,3072]{1,0:T(8,128)(2,1)S(1)}, u32[]{:S(2)}, u32[]{:S(2)}) collective-permute-start(bf16[64,3072]{1,0:T(8,128)(2,1)S(1)} %get-tuple-element.127.refs_0_), channel_id=1, source_target_pairs={{0,1},{1,0},{2,3},{3,2},{4,5},{5,4},{6,7},{7,6},{8,9},{9,8},{10,11... | collective-permute-start | bytes 1179656 | tf_op jit(solution)/shard_map/ppermute | solution.py:707
  250.1 20.3 %collective-permute-start.30 = (bf16[64,3072]{1,0:T(8,128)(2,1)S(1)}, bf16[64,3072]{1,0:T(8,128)(2,1)S(1)}, u32[]{:S(2)}, u32[]{:S(2)}) collective-permute-start(bf16[64,3072]{1,0:T(8,128)(2,1)S(1)} %get-tuple-element.128.refs_1_), channel_id=1, source_target_pairs={{0,1},{1,0},{2,3},{3,2},{4,5},{5,4},{6,7},{7,6},{8,9},{9,8},{10,11... | collective-permute-start | bytes 1179656 | tf_op jit(solution)/shard_map/ppermute | solution.py:707
  267.0 4.7 %collective-permute-start.39 = (bf16[64,3072]{1,0:T(8,128)(2,1)S(1)}, bf16[64,3072]{1,0:T(8,128)(2,1)S(1)}, u32[]{:S(2)}, u32[]{:S(2)}) collective-permute-start(bf16[64,3072]{1,0:T(8,128)(2,1)S(1)} %collective-permute-done.31.refs_4_), channel_id=1, source_target_pairs={{0,1},{1,0},{2,3},{3,2},{4,5},{5,4},{6,7},{7,6},{8,9},{9,8},{10,11... | collective-permute-start | bytes 1179656 | tf_op jit(solution)/shard_map/ppermute | solution.py:707
  270.4 1.9 collective-permute-start.40
  273.1 15.7 %collective-permute-start.41 = (bf16[384,768]{1,0:T(8,128)(2,1)S(1)}, bf16[384,768]{1,0:T(8,128)(2,1)S(1)}, u32[]{:S(2)}, u32[]{:S(2)}) collective-permute-start(bf16[384,768]{1,0:T(8,128)(2,1)S(1)} %get-tuple-element.136), channel_id=1, source_target_pairs={{0,4},{1,5},{2,6},{3,7},{4,0},{5,1},{6,2},{7,3},{8,12},{9,13},{10,... | collective-permute-start | bytes 1769480 | tf_op jit(solution)/shard_map/ppermute | solution.py:707
  275.1 13.8 %collective-permute-start.27 = (bf16[64,2304]{1,0:T(8,128)(2,1)S(1)}, bf16[64,2304]{1,0:T(8,128)(2,1)S(1)}, u32[]{:S(2)}, u32[]{:S(2)}) collective-permute-start(bf16[64,2304]{1,0:T(8,128)(2,1)S(1)} %get-tuple-element.125.refs_0_), channel_id=1, source_target_pairs={{0,2},{1,3},{2,0},{3,1},{4,6},{5,7},{6,4},{7,5},{8,10},{9,11},{10,... | collective-permute-start | bytes 884744 | tf_op jit(solution)/shard_map/ppermute | solution.py:707
  276.1 19.1 %collective-permute-start.43 = (bf16[64,2304]{1,0:T(8,128)(2,1)S(1)}, bf16[64,2304]{1,0:T(8,128)(2,1)S(1)}, u32[]{:S(2)}, u32[]{:S(2)}) collective-permute-start(bf16[64,2304]{1,0:T(8,128)(2,1)S(1)} %get-tuple-element.125.refs_0_), channel_id=1, source_target_pairs={{0,1},{1,0},{2,3},{3,2},{4,5},{5,4},{6,7},{7,6},{8,9},{9,8},{10,11... | collective-permute-start | bytes 884744 | tf_op jit(solution)/shard_map/ppermute | solution.py:707
  276.1 15.7 %collective-permute-start.28 = (bf16[80,2304]{1,0:T(8,128)(2,1)S(1)}, bf16[80,2304]{1,0:T(8,128)(2,1)S(1)}, u32[]{:S(2)}, u32[]{:S(2)}) collective-permute-start(bf16[80,2304]{1,0:T(8,128)(2,1)S(1)} %get-tuple-element.126.refs_1_), channel_id=1, source_target_pairs={{0,2},{1,3},{2,0},{3,1},{4,6},{5,7},{6,4},{7,5},{8,10},{9,11},{10,... | collective-permute-start | bytes 1105928 | tf_op jit(solution)/shard_map/ppermute | solution.py:707
  277.1 18.0 %collective-permute-start.44 = (bf16[80,2304]{1,0:T(8,128)(2,1)S(1)}, bf16[80,2304]{1,0:T(8,128)(2,1)S(1)}, u32[]{:S(2)}, u32[]{:S(2)}) collective-permute-start(bf16[80,2304]{1,0:T(8,128)(2,1)S(1)} %get-tuple-element.126.refs_1_), channel_id=1, source_target_pairs={{0,1},{1,0},{2,3},{3,2},{4,5},{5,4},{6,7},{7,6},{8,9},{9,8},{10,11... | collective-permute-start | bytes 1105928 | tf_op jit(solution)/shard_map/ppermute | solution.py:707
  291.8 19.9 %collective-permute-start.42 = (bf16[264,768]{1,0:T(8,128)(2,1)S(1)}, bf16[264,768]{1,0:T(8,128)(2,1)S(1)}, u32[]{:S(2)}, u32[]{:S(2)}) collective-permute-start(bf16[264,768]{1,0:T(8,128)(2,1)S(1)} %pad_maximum_fusion), channel_id=1, source_target_pairs={{0,8},{1,9},{2,10},{3,11},{4,12},{5,13},{6,14},{7,15},{8,0},{9,1},... | collective-permute-start | bytes 1216520 | tf_op jit(solution)/shard_map/ppermute | solution.py:707
  293.2 2.0 collective-permute-start.45
  293.2 2.1 collective-permute-start.46
  311.6 11.7 %collective-permute-start.47 = (bf16[96,2432]{1,0:T(8,128)(2,1)S(1)}, bf16[96,2432]{1,0:T(8,128)(2,1)S(1)}, u32[]{:S(2)}, u32[]{:S(2)}) collective-permute-start(bf16[96,2432]{1,0:T(8,128)(2,1)S(1)} %get-tuple-element.145), channel_id=1, source_target_pairs={{0,4},{1,5},{2,6},{3,7},{4,0},{5,1},{6,2},{7,3},{8,12},{9,13},{10,... | collective-permute-start | bytes 1400840 | tf_op jit(solution)/shard_map/ppermute | solution.py:707
  323.4 11.8 %collective-permute-start.48 = (bf16[48,2432]{1,0:T(8,128)(2,1)S(1)}, bf16[48,2432]{1,0:T(8,128)(2,1)S(1)}, u32[]{:S(2)}, u32[]{:S(2)}) collective-permute-start(bf16[48,2432]{1,0:T(8,128)(2,1)S(1)} %add_convert_fusion.2), channel_id=1, source_target_pairs={{0,8},{1,9},{2,10},{3,11},{4,12},{5,13},{6,14},{7,15},{8,0},{9,1},... | collective-permute-start | bytes 700424 | tf_op jit(solution)/shard_map/ppermute | solution.py:707
  (54 other events, 636.2 us)
Sparse Core Ops, SparseCore 0:
  23.4 75.0 all-gather.1

commit v9 on v8

--- a/solution.py
+++ b/solution.py
@@ -1032,7 +1032,11 @@
         1,
     )
     sent = (sent.astype(F32) + back.astype(F32)).astype(BF)
+    if count == GROUP:
+        left, sent = lax.optimization_barrier((left, sent))
+        left = [left[0]] + [partner(left[apart], apart, count) for apart in range(1, 4)]
     got = exchange(sent, count)
+    left, got = lax.optimization_barrier((left, got))
 
     d_proj_1, gain_attn_1, *grad_1 = on_core(
         global_finish_body,
@@ -1040,9 +1044,6 @@
         (first, got, d_mid_1, *in_1, gain_attn, global_tables),
     )
 
-    if count == GROUP:
-        left, grad_1 = lax.optimization_barrier((left, grad_1))
-        left = [left[0]] + [partner(left[apart], apart, count) for apart in range(1, 4)]
     up_0 = to_other_section(grad_1, -1)
     d_mlp = jnp.concatenate(
         [jnp.where(lower, a, up_1[i * row_count :][:row_count]) for i, a in enumerate(up_0)]
@@ -1119,7 +1120,7 @@
     across = [partner(item, 2, count) for item in d_proj]
     beside = [partner(item, 1, count) for item in d_proj]
     far = jnp.concatenate([far, out_far])
-    across, far = lax.optimization_barrier((across, far))
+    across, _ = lax.optimization_barrier((across, far))
     far = partner(far, 8, count)
     right = []
     for low, high in zip(d_proj[:1] + beside[:1] + across[:1], d_proj[1:] + beside[1:] + across[1:]):
@@ -1133,7 +1134,7 @@
         [pltpu.VMEM((width, LANES), F32)],
         [pltpu.SMEM] + [pltpu.VMEM] * (len(late_in) - 1),
     )
-    far, late = lax.optimization_barrier((far, list(late)))
+    far, _ = lax.optimization_barrier((far, late[0]))
     early = near + far[:early_rows].astype(F32)
     mlp_out_share = out_near + far[early_rows:].astype(F32)
     late = second_hop(*first_hop(late, count), count)

time: 345 us -> 344 us (level)
  blocking collectives: 54.8 us -> 33 us
  waiting for transfers between devices: 116 us -> 125 us
  starting transfers between devices: 55.8 us -> 63.4 us
  local copies, waits for them, and re-layouts: 40.5 us -> 44.9 us
    all_to_all x3 -> x2, blocking collectives: 54.8 us -> 33 us  [exchange(): return lax.all_to_all(blocks, 'dp', 0, 0, axis_index_groups=groups)]
    ppermute x41, waiting for transfers between devices: 76.7 us -> 84.4 us  [partner(): return lax.ppermute(rows, 'dp', [(i, i ^ apart) for i in range(count)])]
    all_to_all x1 -> x2, starting transfers between devices: 4.18 us -> 8.92 us  [exchange(): return lax.all_to_all(blocks, 'dp', 0, 0, axis_index_groups=groups)]
    unnamed x102, local copies, waits for them, and re-layouts: 21.8 us -> 26.2 us
  transfers between devices with their start and end apart: 51 -> 52, of which waited for: 22 -> 24; matrix products, arithmetic and copies ran while one was open for 6% -> 6% of each run, Pallas kernels for 7% -> 7%
where the time goes in v9:
time: 344 us; the launch traced here: 343 us
  waiting for transfers between devices  125 us (36%)
  starting transfers between devices  63.4 us (18%)
  Pallas kernels  56.7 us (16%)
  local copies, waits for them, and re-layouts  44.9 us (13%)
  blocking collectives  33 us (10%)
  between operations  14.9 us (4%)
  other arithmetic  5.16 us (2%)
    ppermute x41, waiting for transfers between devices, partner(): return lax.ppermute(rows, 'dp', [(i, i ^ apart) for i in range(count)])  84.4 us
    pallas_call x17, Pallas kernels, on_core(): pl.pallas_call(body, out_shape=[jax.ShapeDtypeStruct(shape, dtype) for sh...  56.7 us
    ppermute x41, starting transfers between devices, partner(): return lax.ppermute(rows, 'dp', [(i, i ^ apart) for i in range(count)])  39.5 us
    all_to_all x2, blocking collectives, exchange(): return lax.all_to_all(blocks, 'dp', 0, 0, axis_index_groups=groups)  33 us
    all_gather x1, waiting for transfers between devices, on_device(): others = [lax.all_gather(stacked, 'dp', axis=0, tiled=True)]  28.2 us
    unnamed x102, local copies, waits for them, and re-layouts  26.2 us
    dynamic_update_slice x16, local copies, waits for them, and re-layouts, gather_rows(): whole = lax.dynamic_update_slice(whole, item[None], start)  11.4 us
    ppermute x4, waiting for transfers between devices, to_other_section(): return [lax.ppermute(rows, 'section', pairs) for rows in chunks]  9.39 us
  transfers between devices with their start and end apart: 52, of which 24 were waited for; matrix products, arithmetic and copies ran while one was open for 6% of the time, Pallas kernels for 7%

profile of v9, /device:TPU:0, one launch (start us, length us, event | category | flops | bytes accessed | tf_op | source)
XLA Modules:
  0.0 343.0 jit_solution(11818930344416517134)
XLA Ops:
  10.3 3.0 collective-permute-start.1
  13.3 1.6 collective-permute-start.2
  14.9 2.6 collective-permute-start.3
  23.5 2.1 broadcast_in_dim.105
  27.5 6.9 %collective-permute-done.3 = bf16[48,2432]{1,0:T(8,128)(2,1)S(1)} collective-permute-done((bf16[48,2432]{1,0:T(8,128)(2,1)S(1)}, bf16[48,2432]{1,0:T(8,128)(2,1)S(1)}, u32[]{:S(2)}, u32[]{:S(2)}) %collective-permute-start.3) | collective-permute-done | bytes 233504 | tf_op jit(solution)/shard_map/ppermute | solution.py:707
  34.9 1.5 collective-permute-start.7
  40.0 5.6 %collective-permute-done.6 = bf16[48,2432]{1,0:T(8,128)(2,1)S(1)} collective-permute-done((bf16[48,2432]{1,0:T(8,128)(2,1)S(1)}, bf16[48,2432]{1,0:T(8,128)(2,1)S(1)}, u32[]{:S(2)}, u32[]{:S(2)}) %collective-permute-start.6) | collective-permute-done | bytes 233504 | tf_op jit(solution)/shard_map/ppermute | solution.py:707
  46.3 3.2 collective-permute-done.7
  57.0 3.1 shard_map.154
  60.8 2.1 collective-permute-start.16
  64.8 1.9 collective-permute-done.17.after_ref
  66.7 3.6 %shard_map.155 = (bf16[128,768]{1,0:T(8,128)(2,1)S(1)}, f32[12,1,128]{2,1,0:T(1,128)S(1)}) custom-call(bf16[128,768]{1,0:T(8,128)(2,1)S(1)} %get-tuple-element.80.q_ref, bf16[128,1536]{1,0:T(8,128)(2,1)S(1)} %collective-permute-done.16.before_ref, bf16[128,1536]{1,0:T(8,128)(2,1)S(1)} %get-tuple-element.81.own_ref, ...), custom_call_target="tpu_custom_call" | custom-call | flops 1024 | bytes 1024 | tf_op jit(solution)/shard_map/pallas_call | solution.py:65
  70.4 28.2 %all-gather.2.cloned.1.call-done.refs_0_ = bf16[768,4352]{1,0:T(8,128)(2,1)} async-done(((bf16[48,4352]{1,0:T(8,128)(2,1)}), bf16[768,4352]{1,0:T(8,128)(2,1)}) %all-gather.2.cloned.1.call-update) | async-done | bytes 6684688 | tf_op jit(solution)/shard_map/all_gather | solution.py:879
  98.6 4.4 %shard_map.156 = (bf16[128,768]{1,0:T(8,128)(2,1)S(1)}, bf16[128,1152]{1,0:T(8,128)(2,1)S(1)}, f32[128,768]{1,0:T(8,128)S(1)}, f32[128,2304]{1,0:T(8,128)S(1)}, ...) custom-call(bf16[768,4352]{1,0:T(8,128)(2,1)} %all-gather.2.cloned.1.call-done.refs_0_, ...), custom_call_target="tpu_custom_call" | custom-call | flops 1024 | bytes 1024 | tf_op jit(solution)/shard_map/pallas_call | solution.py:65
  105.5 3.4 collective-permute-start.18
  110.6 1.4 collective-permute-done.18.low_ref.refs_2_
  112.0 1.4 collective-permute-done.19.high_ref.refs_3_
  113.5 3.1 shard_map.157
  116.6 21.2 %all_to_all.20.got_ref = bf16[16,144,128]{2,1,0:T(8,128)(2,1)S(1)} all-to-all(bf16[16,144,128]{2,1,0:T(8,128)(2,1)S(1)} %get-tuple-element.86), channel_id=1, replica_groups={{0,1,2,3,4,5,6,7,8,9,10,11,12,13,14,15},{16,17,18,19,20,21,22,23,24,25,..., dimensions={0} | all-to-all | bytes 1179648 | tf_op jit(solution)/shard_map/all_to_all | solution.py:698
  139.5 6.0 %shard_map.158 = (bf16[16,48,128]{2,1,0:T(8,128)(2,1)S(1)}, f32[6,1,256]{2,1,0:T(1,128)S(1)}) custom-call(bf16[16,144,128]{2,1,0:T(8,128)(2,1)S(1)} %all_to_all.20.got_ref, bf16[16,64,128]{2,1,0:T(8,128)(2,1)S(1)} %collective-permute-done.20.other_ref, s32[1024,1]{1,0:T(8,128)S(1)} %copy.19.own_seg_ref, s32[1024,1]{1,0:T(8,128)S(1)} %copy.20.shared_seg_ref), custom_call_target="tpu_custom_call" | custom-call | flops 1024 | bytes 1024 | tf_op jit(solution)/shard_map/pallas_call | solution.py:65
  145.5 11.8 %all_to_all.21.refs_1_ = bf16[16,48,128]{2,1,0:T(8,128)(2,1)S(1)} all-to-all(bf16[16,48,128]{2,1,0:T(8,128)(2,1)S(1)} %get-tuple-element.87), channel_id=1, replica_groups={{0,1,2,3,4,5,6,7,8,9,10,11,12,13,14,15},{16,17,18,19,20,21,22,23,24,25,..., dimensions={0} | all-to-all | bytes 393216 | tf_op jit(solution)/shard_map/all_to_all | solution.py:698
  157.3 7.7 %shard_map.159 = (bf16[128,768]{1,0:T(8,128)(2,1)S(1)}, bf16[128,768]{1,0:T(8,128)(2,1)S(1)}, bf16[128,768]{1,0:T(8,128)(2,1)S(1)}, bf16[128,1152]{1,0:T(8,128)(...) custom-call(bf16[768,4352]{1,0:T(8,128)(2,1)} %all-gather.2.cloned.1, ...), custom_call_target="tpu_custom_call" | custom-call | flops 1024 | bytes 1024 | tf_op jit(solution)/shard_map/pallas_call | solution.py:65
  169.4 4.2 %all-to-all-start.2 = ((bf16[16,48,128]{2,1,0:T(8,128)(2,1)}), bf16[16,48,128]{2,1,0:T(8,128)(2,1)}, u32[]{:S(2)}, u32[]{:S(2)}) async-start(bf16[16,48,128]{2,1,0:T(8,128)(2,1)} %get-tuple-element.97), calls=%async_computation.2 | async-start | bytes 393216 | tf_op jit(solution)/shard_map/all_to_all | solution.py:698
  183.6 8.2 %shard_map.161 = (bf16[16,144,128]{2,1,0:T(8,128)(2,1)S(1)}, bf16[16,64,128]{2,1,0:T(8,128)(2,1)S(1)}) custom-call(bf16[16,144,128]{2,1,0:T(8,128)(2,1)S(1)} %all_to_all.20.got_ref, bf16[16,64,128]{2,1,0:T(8,128)(2,1)S(1)} %copy-done.10, s32[1024,1]{1,0:T(8,128)S(1)} %copy.19.own_seg_ref, s32[1024,1]{1,0:T(8,128)S(1)} %copy.20.shared_seg_ref, ...), custom_call_target="tpu_custom_call" | custom-call | flops 1024 | bytes 1024 | tf_op jit(solution)/shard_map/pallas_call | solution.py:65
  192.0 1.4 collective-permute-done.21
  194.5 4.8 %all-to-all-start.3 = ((bf16[16,144,128]{2,1,0:T(8,128)(2,1)}), bf16[16,144,128]{2,1,0:T(8,128)(2,1)S(1)}, u32[]{:S(2)}, u32[]{:S(2)}) async-start(bf16[16,144,128]{2,1,0:T(8,128)(2,1)} %add_convert_fusion), calls=%async_computation.3 | async-start | bytes 1179648 | tf_op jit(solution)/shard_map/all_to_all | solution.py:698
  199.8 1.7 collective-permute-start.23
  201.5 10.9 %collective-permute-done.23.refs_6_.refs_10_ = bf16[4,216,128]{2,1,0:T(8,128)(2,1)S(1)} collective-permute-done((bf16[4,216,128]{2,1,0:T(8,128)(2,1)S(1)}, bf16[4,216,128]{2,1,0:T(8,128)(2,1)S(1)}, u32[]{:S(2)}, u32[]{:S(2)}) %collective-permute-start.23) | collective-permute-done | bytes 221216 | tf_op jit(solution)/shard_map/ppermute | solution.py:707
  212.4 5.3 %collective-permute-done.24.refs_7_.refs_11_ = bf16[4,216,128]{2,1,0:T(8,128)(2,1)S(1)} collective-permute-done((bf16[4,216,128]{2,1,0:T(8,128)(2,1)S(1)}, bf16[4,216,128]{2,1,0:T(8,128)(2,1)S(1)}, u32[]{:S(2)}, u32[]{:S(2)}) %collective-permute-start.24) | collective-permute-done | bytes 221216 | tf_op jit(solution)/shard_map/ppermute | solution.py:707
  218.7 3.6 %shard_map.162 = (bf16[128,2304]{1,0:T(8,128)(2,1)S(1)}, f32[1,768]{1,0:T(1,128)S(1)}, bf16[64,768]{1,0:T(8,128)(2,1)S(1)}, bf16[64,768]{1,0:T(8,128)(2,1)S(1)}) custom-call(bf16[768,2432]{1,0:T(8,128)(2,1)} %bitcast.23.first_ref, bf16[16,144,128]{2,1,0:T(8,128)(2,1)S(1)} %all-to-all-done.3.got_ref, f32[128,768]{1,0:T(8,128)S(1)} %copy-done.22, ...), custom_call_target="tpu_custom_call" | custom-call | flops 1024 | bytes 1024 | tf_op jit(solution)/shard_map/pallas_call | solution.py:65
  225.0 4.9 %collective-permute-done.25.refs_2_ = bf16[64,768]{1,0:T(8,128)(2,1)S(1)} collective-permute-done((bf16[64,768]{1,0:T(8,128)(2,1)S(1)}, bf16[64,768]{1,0:T(8,128)(2,1)S(1)}, u32[]{:S(2)}, u32[]{:S(2)}) %collective-permute-start.25) | collective-permute-done | bytes 98336 | tf_op jit(solution)/shard_map/ppermute | solution.py:703
  229.8 1.6 collective-permute-done.26.refs_3_
  235.4 6.1 %shard_map.163 = (f32[1,768]{1,0:T(1,128)S(1)}, f32[128,768]{1,0:T(8,128)S(1)}, bf16[128,768]{1,0:T(8,128)(2,1)S(1)}, bf16[64,3072]{1,0:T(8,128)(2,1)S(1)}, bf16[64,3072]{1,0:T(8,128)(2,1)S(1)}) custom-call(bf16[768,4352]{1,0:T(8,128)(2,1)} %all-gather.2.cloned.1.call-done.refs_0_, s32[1]{0:T(128)} %bitcast.37.lower_ref.refs_1_, ...), custom_call_target="tpu_custom_call" | custom-call | flops 1024 | bytes 1024 | tf_op jit(solution)/shard_map/pallas_call | solution.py:65
  242.1 3.5 %shard_map.164 = (bf16[128,768]{1,0:T(8,128)(2,1)S(1)}, f32[128,1536]{1,0:T(8,128)S(1)}, bf16[128,1536]{1,0:T(8,128)(2,1)S(1)}, bf16[128,1536]{1,0:T(8,128)(2,1)S(1)}) custom-call(bf16[128,768]{1,0:T(8,128)(2,1)S(1)} %copy-done.14, bf16[128,1536]{1,0:T(8,128)(2,1)S(1)} %copy-done.4, bf16[128,1536]{1,0:T(8,128)(2,1)S(1)} %copy-done.2, ...), custom_call_target="tpu_custom_call" | custom-call | flops 1024 | bytes 1024 | tf_op jit(solution)/shard_map/pallas_call | solution.py:65
  246.9 3.1 collective-permute-start.29
  250.4 2.3 collective-permute-start.40
  255.3 7.6 %collective-permute-start.35 = (bf16[64,3072]{1,0:T(8,128)(2,1)S(1)}, bf16[64,3072]{1,0:T(8,128)(2,1)S(1)}, u32[]{:S(2)}, u32[]{:S(2)}) collective-permute-start(bf16[64,3072]{1,0:T(8,128)(2,1)S(1)} %get-tuple-element.129.refs_1_), channel_id=1, source_target_pairs={{0,1},{1,0},{2,3},{3,2},{4,5},{5,4},{6,7},{7,6},{8,9},{9,8},{10,11... | collective-permute-start | bytes 1179656 | tf_op jit(solution)/shard_map/ppermute | solution.py:707
  262.8 4.0 %shard_map.165 = (bf16[64,2304]{1,0:T(8,128)(2,1)S(1)}, bf16[80,2304]{1,0:T(8,128)(2,1)S(1)}, bf16[128,768]{1,0:T(8,128)(2,1)S(1)}, f32[1,768]{1,0:T(1,128)}) custom-call(s32[1]{0:T(128)} %bitcast.37.lower_ref.refs_1_, bf16[768,2432]{1,0:T(8,128)(2,1)} %bitcast.23.first_ref, bf16[128,768]{1,0:T(8,128)(2,1)S(1)} %get-tuple-element.116.dq_ref, ...), custom_call_target="tpu_custom_call" | custom-call | flops 1024 | bytes 1024 | tf_op jit(solution)/shard_map/pallas_call | solution.py:65
  266.9 6.3 %collective-permute-done.37.refs_5_ = bf16[64,3072]{1,0:T(8,128)(2,1)S(1)} collective-permute-done((bf16[64,3072]{1,0:T(8,128)(2,1)S(1)}, bf16[64,3072]{1,0:T(8,128)(2,1)S(1)}, u32[]{:S(2)}, u32[]{:S(2)}) %collective-permute-start.37) | collective-permute-done | bytes 393248 | tf_op jit(solution)/shard_map/ppermute | solution.py:707
  273.2 3.0 collective-permute-start.41
  276.2 1.3 collective-permute-done.41.refs_6_
  279.0 1.9 collective-permute-start.43
  280.9 1.9 collective-permute-start.32
  283.2 11.4 %collective-permute-done.43 = bf16[384,768]{1,0:T(8,128)(2,1)S(1)} collective-permute-done((bf16[384,768]{1,0:T(8,128)(2,1)S(1)}, bf16[384,768]{1,0:T(8,128)(2,1)S(1)}, u32[]{:S(2)}, u32[]{:S(2)}) %collective-permute-start.43) | collective-permute-done | bytes 589856 | tf_op jit(solution)/shard_map/ppermute | solution.py:707
  294.7 2.6 collective-permute-start.48
  301.7 13.7 %collective-permute-done.48 = bf16[264,768]{1,0:T(8,128)(2,1)S(1)} collective-permute-done((bf16[264,768]{1,0:T(8,128)(2,1)S(1)}, bf16[264,768]{1,0:T(8,128)(2,1)S(1)}, u32[]{:S(2)}, u32[]{:S(2)}) %collective-permute-start.48) | collective-permute-done | bytes 405536 | tf_op jit(solution)/shard_map/ppermute | solution.py:707
  316.9 4.7 %collective-permute-done.46 = bf16[96,2432]{1,0:T(8,128)(2,1)S(1)} collective-permute-done((bf16[96,2432]{1,0:T(8,128)(2,1)S(1)}, bf16[96,2432]{1,0:T(8,128)(2,1)S(1)}, u32[]{:S(2)}, u32[]{:S(2)}) %collective-permute-start.46) | collective-permute-done | bytes 466976 | tf_op jit(solution)/shard_map/ppermute | solution.py:707
  323.8 10.8 %collective-permute-done.47 = bf16[48,2432]{1,0:T(8,128)(2,1)S(1)} collective-permute-done((bf16[48,2432]{1,0:T(8,128)(2,1)S(1)}, bf16[48,2432]{1,0:T(8,128)(2,1)S(1)}, u32[]{:S(2)}, u32[]{:S(2)}) %collective-permute-start.47) | collective-permute-done | bytes 233504 | tf_op jit(solution)/shard_map/ppermute | solution.py:707
  (256 shorter events, 71.6 us)
Async XLA Ops:
  7.2 91.4 %all-gather.2.cloned.1.call-start = ((), (), s32[]{:S(2)}) async-start(), calls=%async_computation.4 | async-start | bytes 7102464 | tf_op jit(solution)/shard_map/all_gather | solution.py:879
  10.3 13.0 %collective-permute-start.1 = (bf16[48,2432]{1,0:T(8,128)(2,1)S(1)}, bf16[48,2432]{1,0:T(8,128)(2,1)S(1)}, u32[]{:S(2)}, u32[]{:S(2)}) collective-permute-start(bf16[48,2432]{1,0:T(8,128)(2,1)S(1)} %shard_map.153), channel_id=1, source_target_pairs={{0,2},{1,3},{2,0},{3,1},{4,6},{5,7},{6,4},{7,5},{8,10},{9,11},{10,... | collective-permute-start | bytes 700424 | tf_op jit(solution)/shard_map/ppermute | solution.py:707
  13.3 13.9 %collective-permute-start.2 = (bf16[48,2432]{1,0:T(8,128)(2,1)S(1)}, bf16[48,2432]{1,0:T(8,128)(2,1)S(1)}, u32[]{:S(2)}, u32[]{:S(2)}) collective-permute-start(bf16[48,2432]{1,0:T(8,128)(2,1)S(1)} %shard_map.153), channel_id=1, source_target_pairs={{0,4},{1,5},{2,6},{3,7},{4,0},{5,1},{6,2},{7,3},{8,12},{9,13},{10,... | collective-permute-start | bytes 700424 | tf_op jit(solution)/shard_map/ppermute | solution.py:707
  14.9 19.5 %collective-permute-start.3 = (bf16[48,2432]{1,0:T(8,128)(2,1)S(1)}, bf16[48,2432]{1,0:T(8,128)(2,1)S(1)}, u32[]{:S(2)}, u32[]{:S(2)}) collective-permute-start(bf16[48,2432]{1,0:T(8,128)(2,1)S(1)} %shard_map.153), channel_id=1, source_target_pairs={{0,8},{1,9},{2,10},{3,11},{4,12},{5,13},{6,14},{7,15},{8,0},{9,1},... | collective-permute-start | bytes 700424 | tf_op jit(solution)/shard_map/ppermute | solution.py:707
  17.5 17.5 %collective-permute-start.4 = (bf16[48,2432]{1,0:T(8,128)(2,1)S(1)}, bf16[48,2432]{1,0:T(8,128)(2,1)S(1)}, u32[]{:S(2)}, u32[]{:S(2)}) collective-permute-start(bf16[48,2432]{1,0:T(8,128)(2,1)S(1)} %shard_map.153), channel_id=1, source_target_pairs={{0,12},{1,13},{2,14},{3,15},{4,8},{5,9},{6,10},{7,11},{8,4},{9,5},... | collective-permute-start | bytes 700424 | tf_op jit(solution)/shard_map/ppermute | solution.py:707
  19.6 30.6 %collective-permute-start.8 = (bf16[48,2432]{1,0:T(8,128)(2,1)S(1)}, bf16[48,2432]{1,0:T(8,128)(2,1)S(1)}, u32[]{:S(2)}, u32[]{:S(2)}) collective-permute-start(bf16[48,2432]{1,0:T(8,128)(2,1)S(1)} %shard_map.153), channel_id=1, source_target_pairs={{0,1},{1,0},{2,3},{3,2},{4,5},{5,4},{6,7},{7,6},{8,9},{9,8},{10,11... | collective-permute-start | bytes 700424 | tf_op jit(solution)/shard_map/ppermute | solution.py:707
  26.8 24.6 %collective-permute-start.9 = (bf16[48,2432]{1,0:T(8,128)(2,1)S(1)}, bf16[48,2432]{1,0:T(8,128)(2,1)S(1)}, u32[]{:S(2)}, u32[]{:S(2)}) collective-permute-start(bf16[48,2432]{1,0:T(8,128)(2,1)S(1)} %collective-permute-done.1), channel_id=1, source_target_pairs={{0,1},{1,0},{2,3},{3,2},{4,5},{5,4},{6,7},{7,6},{8,9},{9,8},{10,11... | collective-permute-start | bytes 700424 | tf_op jit(solution)/shard_map/ppermute | solution.py:707
  27.2 12.1 %collective-permute-start.5 = (bf16[48,2432]{1,0:T(8,128)(2,1)S(1)}, bf16[48,2432]{1,0:T(8,128)(2,1)S(1)}, u32[]{:S(2)}, u32[]{:S(2)}) collective-permute-start(bf16[48,2432]{1,0:T(8,128)(2,1)S(1)} %collective-permute-done.2), channel_id=1, source_target_pairs={{0,2},{1,3},{2,0},{3,1},{4,6},{5,7},{6,4},{7,5},{8,10},{9,11},{10,... | collective-permute-start | bytes 700424 | tf_op jit(solution)/shard_map/ppermute | solution.py:707
  34.4 11.2 %collective-permute-start.6 = (bf16[48,2432]{1,0:T(8,128)(2,1)S(1)}, bf16[48,2432]{1,0:T(8,128)(2,1)S(1)}, u32[]{:S(2)}, u32[]{:S(2)}) collective-permute-start(bf16[48,2432]{1,0:T(8,128)(2,1)S(1)} %collective-permute-done.3), channel_id=1, source_target_pairs={{0,2},{1,3},{2,0},{3,1},{4,6},{5,7},{6,4},{7,5},{8,10},{9,11},{10,... | collective-permute-start | bytes 700424 | tf_op jit(solution)/shard_map/ppermute | solution.py:707
  34.9 14.5 %collective-permute-start.7 = (bf16[48,2432]{1,0:T(8,128)(2,1)S(1)}, bf16[48,2432]{1,0:T(8,128)(2,1)S(1)}, u32[]{:S(2)}, u32[]{:S(2)}) collective-permute-start(bf16[48,2432]{1,0:T(8,128)(2,1)S(1)} %collective-permute-done.4), channel_id=1, source_target_pairs={{0,2},{1,3},{2,0},{3,1},{4,6},{5,7},{6,4},{7,5},{8,10},{9,11},{10,... | collective-permute-start | bytes 700424 | tf_op jit(solution)/shard_map/ppermute | solution.py:707
  39.3 12.9 %collective-permute-start.10 = (bf16[48,2432]{1,0:T(8,128)(2,1)S(1)}, bf16[48,2432]{1,0:T(8,128)(2,1)S(1)}, u32[]{:S(2)}, u32[]{:S(2)}) collective-permute-start(bf16[48,2432]{1,0:T(8,128)(2,1)S(1)} %collective-permute-done.2), channel_id=1, source_target_pairs={{0,1},{1,0},{2,3},{3,2},{4,5},{5,4},{6,7},{7,6},{8,9},{9,8},{10,11... | collective-permute-start | bytes 700424 | tf_op jit(solution)/shard_map/ppermute | solution.py:707
  45.6 8.5 %collective-permute-start.12 = (bf16[48,2432]{1,0:T(8,128)(2,1)S(1)}, bf16[48,2432]{1,0:T(8,128)(2,1)S(1)}, u32[]{:S(2)}, u32[]{:S(2)}) collective-permute-start(bf16[48,2432]{1,0:T(8,128)(2,1)S(1)} %collective-permute-done.3), channel_id=1, source_target_pairs={{0,1},{1,0},{2,3},{3,2},{4,5},{5,4},{6,7},{7,6},{8,9},{9,8},{10,11... | collective-permute-start | bytes 700424 | tf_op jit(solution)/shard_map/ppermute | solution.py:707
  49.5 6.1 %collective-permute-start.14 = (bf16[48,2432]{1,0:T(8,128)(2,1)S(1)}, bf16[48,2432]{1,0:T(8,128)(2,1)S(1)}, u32[]{:S(2)}, u32[]{:S(2)}) collective-permute-start(bf16[48,2432]{1,0:T(8,128)(2,1)S(1)} %collective-permute-done.4), channel_id=1, source_target_pairs={{0,1},{1,0},{2,3},{3,2},{4,5},{5,4},{6,7},{7,6},{8,9},{9,8},{10,11... | collective-permute-start | bytes 700424 | tf_op jit(solution)/shard_map/ppermute | solution.py:707
  50.2 3.2 collective-permute-start.11
  51.4 3.4 collective-permute-start.13
  52.2 4.1 %collective-permute-start.15 = (bf16[48,2432]{1,0:T(8,128)(2,1)S(1)}, bf16[48,2432]{1,0:T(8,128)(2,1)S(1)}, u32[]{:S(2)}, u32[]{:S(2)}) collective-permute-start(bf16[48,2432]{1,0:T(8,128)(2,1)S(1)} %collective-permute-done.7), channel_id=1, source_target_pairs={{0,1},{1,0},{2,3},{3,2},{4,5},{5,4},{6,7},{7,6},{8,9},{9,8},{10,11... | collective-permute-start | bytes 700424 | tf_op jit(solution)/shard_map/ppermute | solution.py:707
  60.8 4.0 %collective-permute-start.16 = (bf16[128,1536]{1,0:T(8,128)(2,1)S(1)}, bf16[128,1536]{1,0:T(8,128)(2,1)S(1)}, u32[]{:S(2)}, u32[]{:S(2)}) collective-permute-start(bf16[128,1536]{1,0:T(8,128)(2,1)S(1)} %get-tuple-element.81.own_ref), channel_id=1, source_target_pairs={{0,1},{1,2},{2,3},{3,4},{4,5},{5,6},{6,7},{7,8},{8,9},{9,10},{10,1... | collective-permute-start | bytes 1179656 | tf_op jit(solution)/shard_map/ppermute | solution.py:926
  62.9 3.8 %collective-permute-start.17 = (bf16[128,1536]{1,0:T(8,128)(2,1)S(1)}, bf16[128,1536]{1,0:T(8,128)(2,1)S(1)}, u32[]{:S(2)}, u32[]{:S(2)}) collective-permute-start(bf16[128,1536]{1,0:T(8,128)(2,1)S(1)} %get-tuple-element.81.own_ref), channel_id=1, source_target_pairs={{1,0},{2,1},{3,2},{4,3},{5,4},{6,5},{7,6},{8,7},{9,8},{10,9},{11,1... | collective-permute-start | bytes 1179656 | tf_op jit(solution)/shard_map/ppermute | solution.py:928
  105.5 6.5 %collective-permute-start.18 = (bf16[64,768]{1,0:T(8,128)(2,1)S(1)}, bf16[64,768]{1,0:T(8,128)(2,1)S(1)}, u32[]{:S(2)}, u32[]{:S(2)}) collective-permute-start(bf16[64,768]{1,0:T(8,128)(2,1)S(1)} %get-tuple-element.84), channel_id=1, source_target_pairs={{0,16},{1,17},{2,18},{3,19},{4,20},{5,21},{6,22},{7,23},{8,24},{9,... | collective-permute-start | bytes 294920 | tf_op jit(solution)/shard_map/ppermute | solution.py:703
  108.9 4.6 %collective-permute-start.19 = (bf16[64,768]{1,0:T(8,128)(2,1)S(1)}, bf16[64,768]{1,0:T(8,128)(2,1)S(1)}, u32[]{:S(2)}, u32[]{:S(2)}) collective-permute-start(bf16[64,768]{1,0:T(8,128)(2,1)S(1)} %get-tuple-element.85), channel_id=1, source_target_pairs={{0,16},{1,17},{2,18},{3,19},{4,20},{5,21},{6,22},{7,23},{8,24},{9,... | collective-permute-start | bytes 294920 | tf_op jit(solution)/shard_map/ppermute | solution.py:703
  169.4 13.2 %all-to-all-start.2 = ((bf16[16,48,128]{2,1,0:T(8,128)(2,1)}), bf16[16,48,128]{2,1,0:T(8,128)(2,1)}, u32[]{:S(2)}, u32[]{:S(2)}) async-start(bf16[16,48,128]{2,1,0:T(8,128)(2,1)} %get-tuple-element.97), calls=%async_computation.2 | async-start | bytes 393216 | tf_op jit(solution)/shard_map/all_to_all | solution.py:698
  194.5 23.2 %all-to-all-start.3 = ((bf16[16,144,128]{2,1,0:T(8,128)(2,1)}), bf16[16,144,128]{2,1,0:T(8,128)(2,1)S(1)}, u32[]{:S(2)}, u32[]{:S(2)}) async-start(bf16[16,144,128]{2,1,0:T(8,128)(2,1)} %add_convert_fusion), calls=%async_computation.3 | async-start | bytes 1179648 | tf_op jit(solution)/shard_map/all_to_all | solution.py:698
  199.4 2.2 collective-permute-start.22
  199.8 12.6 %collective-permute-start.23 = (bf16[4,216,128]{2,1,0:T(8,128)(2,1)S(1)}, bf16[4,216,128]{2,1,0:T(8,128)(2,1)S(1)}, u32[]{:S(2)}, u32[]{:S(2)}) collective-permute-start(bf16[4,216,128]{2,1,0:T(8,128)(2,1)S(1)} %get-tuple-element.155), channel_id=1, source_target_pairs={{0,2},{1,3},{2,0},{3,1},{4,6},{5,7},{6,4},{7,5},{8,10},{9,11},{10,... | collective-permute-start | bytes 663560 | tf_op jit(solution)/shard_map/ppermute | solution.py:707
  201.5 16.2 %collective-permute-start.24 = (bf16[4,216,128]{2,1,0:T(8,128)(2,1)S(1)}, bf16[4,216,128]{2,1,0:T(8,128)(2,1)S(1)}, u32[]{:S(2)}, u32[]{:S(2)}) collective-permute-start(bf16[4,216,128]{2,1,0:T(8,128)(2,1)S(1)} %get-tuple-element.154), channel_id=1, source_target_pairs={{0,3},{1,2},{2,1},{3,0},{4,7},{5,6},{6,5},{7,4},{8,11},{9,10},{10,... | collective-permute-start | bytes 663560 | tf_op jit(solution)/shard_map/ppermute | solution.py:707
  222.4 7.5 %collective-permute-start.25 = (bf16[64,768]{1,0:T(8,128)(2,1)S(1)}, bf16[64,768]{1,0:T(8,128)(2,1)S(1)}, u32[]{:S(2)}, u32[]{:S(2)}) collective-permute-start(bf16[64,768]{1,0:T(8,128)(2,1)S(1)} %get-tuple-element.107), channel_id=1, source_target_pairs={{16,0},{17,1},{18,2},{19,3},{20,4},{21,5},{22,6},{23,7},{24,8},{25... | collective-permute-start | bytes 294920 | tf_op jit(solution)/shard_map/ppermute | solution.py:703
  223.7 7.8 %collective-permute-start.26 = (bf16[64,768]{1,0:T(8,128)(2,1)S(1)}, bf16[64,768]{1,0:T(8,128)(2,1)S(1)}, u32[]{:S(2)}, u32[]{:S(2)}) collective-permute-start(bf16[64,768]{1,0:T(8,128)(2,1)S(1)} %get-tuple-element.108), channel_id=1, source_target_pairs={{16,0},{17,1},{18,2},{19,3},{20,4},{21,5},{22,6},{23,7},{24,8},{25... | collective-permute-start | bytes 294920 | tf_op jit(solution)/shard_map/ppermute | solution.py:703
  231.5 10.0 %collective-permute-start.27 = (bf16[128,768]{1,0:T(8,128)(2,1)S(1)}, bf16[128,768]{1,0:T(8,128)(2,1)S(1)}, u32[]{:S(2)}, u32[]{:S(2)}) collective-permute-start(bf16[128,768]{1,0:T(8,128)(2,1)S(1)} %pad_maximum_fusion.2.refs_0_), channel_id=1, source_target_pairs={{0,2},{1,3},{2,0},{3,1},{4,6},{5,7},{6,4},{7,5},{8,10},{9,11},{10,... | collective-permute-start | bytes 589832 | tf_op jit(solution)/shard_map/ppermute | solution.py:707
  232.0 18.0 %collective-permute-start.38 = (bf16[128,768]{1,0:T(8,128)(2,1)S(1)}, bf16[128,768]{1,0:T(8,128)(2,1)S(1)}, u32[]{:S(2)}, u32[]{:S(2)}) collective-permute-start(bf16[128,768]{1,0:T(8,128)(2,1)S(1)} %pad_maximum_fusion.2.refs_0_), channel_id=1, source_target_pairs={{0,1},{1,0},{2,3},{3,2},{4,5},{5,4},{6,7},{7,6},{8,9},{9,8},{10,11... | collective-permute-start | bytes 589832 | tf_op jit(solution)/shard_map/ppermute | solution.py:707
  241.5 8.5 %collective-permute-start.39 = (bf16[128,768]{1,0:T(8,128)(2,1)S(1)}, bf16[128,768]{1,0:T(8,128)(2,1)S(1)}, u32[]{:S(2)}, u32[]{:S(2)}) collective-permute-start(bf16[128,768]{1,0:T(8,128)(2,1)S(1)} %collective-permute-done.27.refs_2_), channel_id=1, source_target_pairs={{0,1},{1,0},{2,3},{3,2},{4,5},{5,4},{6,7},{7,6},{8,9},{9,8},{10,11... | collective-permute-start | bytes 589832 | tf_op jit(solution)/shard_map/ppermute | solution.py:707
  245.6 9.2 %collective-permute-start.28 = (bf16[128,1536]{1,0:T(8,128)(2,1)S(1)}, bf16[128,1536]{1,0:T(8,128)(2,1)S(1)}, u32[]{:S(2)}, u32[]{:S(2)}) collective-permute-start(bf16[128,1536]{1,0:T(8,128)(2,1)S(1)} %get-tuple-element.118), channel_id=1, source_target_pairs={{1,0},{2,1},{3,2},{4,3},{5,4},{6,5},{7,6},{8,7},{9,8},{10,9},{11,1... | collective-permute-start | bytes 1179656 | tf_op jit(solution)/shard_map/ppermute | solution.py:1086
  246.9 8.3 %collective-permute-start.29 = (bf16[128,1536]{1,0:T(8,128)(2,1)S(1)}, bf16[128,1536]{1,0:T(8,128)(2,1)S(1)}, u32[]{:S(2)}, u32[]{:S(2)}) collective-permute-start(bf16[128,1536]{1,0:T(8,128)(2,1)S(1)} %get-tuple-element.119), channel_id=1, source_target_pairs={{0,1},{1,2},{2,3},{3,4},{4,5},{5,6},{6,7},{7,8},{8,9},{9,10},{10,1... | collective-permute-start | bytes 1179656 | tf_op jit(solution)/shard_map/ppermute | solution.py:1087
  250.4 16.4 %collective-permute-start.40 = (bf16[144,768]{1,0:T(8,128)(2,1)S(1)}, bf16[144,768]{1,0:T(8,128)(2,1)S(1)}, u32[]{:S(2)}, u32[]{:S(2)}) collective-permute-start(bf16[144,768]{1,0:T(8,128)(2,1)S(1)} %get-tuple-element.136), channel_id=1, source_target_pairs={{0,4},{1,5},{2,6},{3,7},{4,0},{5,1},{6,2},{7,3},{8,12},{9,13},{10,... | collective-permute-start | bytes 663560 | tf_op jit(solution)/shard_map/ppermute | solution.py:707
  252.8 14.1 %collective-permute-start.36 = (bf16[64,3072]{1,0:T(8,128)(2,1)S(1)}, bf16[64,3072]{1,0:T(8,128)(2,1)S(1)}, u32[]{:S(2)}, u32[]{:S(2)}) collective-permute-start(bf16[64,3072]{1,0:T(8,128)(2,1)S(1)} %get-tuple-element.128.refs_0_), channel_id=1, source_target_pairs={{0,2},{1,3},{2,0},{3,1},{4,6},{5,7},{6,4},{7,5},{8,10},{9,11},{10,... | collective-permute-start | bytes 1179656 | tf_op jit(solution)/shard_map/ppermute | solution.py:707
  253.6 19.6 %collective-permute-start.37 = (bf16[64,3072]{1,0:T(8,128)(2,1)S(1)}, bf16[64,3072]{1,0:T(8,128)(2,1)S(1)}, u32[]{:S(2)}, u32[]{:S(2)}) collective-permute-start(bf16[64,3072]{1,0:T(8,128)(2,1)S(1)} %get-tuple-element.129.refs_1_), channel_id=1, source_target_pairs={{0,2},{1,3},{2,0},{3,1},{4,6},{5,7},{6,4},{7,5},{8,10},{9,11},{10,... | collective-permute-start | bytes 1179656 | tf_op jit(solution)/shard_map/ppermute | solution.py:707
  254.8 21.4 %collective-permute-start.34 = (bf16[64,3072]{1,0:T(8,128)(2,1)S(1)}, bf16[64,3072]{1,0:T(8,128)(2,1)S(1)}, u32[]{:S(2)}, u32[]{:S(2)}) collective-permute-start(bf16[64,3072]{1,0:T(8,128)(2,1)S(1)} %get-tuple-element.128.refs_0_), channel_id=1, source_target_pairs={{0,1},{1,0},{2,3},{3,2},{4,5},{5,4},{6,7},{7,6},{8,9},{9,8},{10,11... | collective-permute-start | bytes 1179656 | tf_op jit(solution)/shard_map/ppermute | solution.py:707
  255.3 21.0 %collective-permute-start.35 = (bf16[64,3072]{1,0:T(8,128)(2,1)S(1)}, bf16[64,3072]{1,0:T(8,128)(2,1)S(1)}, u32[]{:S(2)}, u32[]{:S(2)}) collective-permute-start(bf16[64,3072]{1,0:T(8,128)(2,1)S(1)} %get-tuple-element.129.refs_1_), channel_id=1, source_target_pairs={{0,1},{1,0},{2,3},{3,2},{4,5},{5,4},{6,7},{7,6},{8,9},{9,8},{10,11... | collective-permute-start | bytes 1179656 | tf_op jit(solution)/shard_map/ppermute | solution.py:707
  273.2 4.4 %collective-permute-start.41 = (bf16[64,3072]{1,0:T(8,128)(2,1)S(1)}, bf16[64,3072]{1,0:T(8,128)(2,1)S(1)}, u32[]{:S(2)}, u32[]{:S(2)}) collective-permute-start(bf16[64,3072]{1,0:T(8,128)(2,1)S(1)} %collective-permute-done.36.refs_4_), channel_id=1, source_target_pairs={{0,1},{1,0},{2,3},{3,2},{4,5},{5,4},{6,7},{7,6},{8,9},{9,8},{10,11... | collective-permute-start | bytes 1179656 | tf_op jit(solution)/shard_map/ppermute | solution.py:707
  279.0 15.7 %collective-permute-start.43 = (bf16[384,768]{1,0:T(8,128)(2,1)S(1)}, bf16[384,768]{1,0:T(8,128)(2,1)S(1)}, u32[]{:S(2)}, u32[]{:S(2)}) collective-permute-start(bf16[384,768]{1,0:T(8,128)(2,1)S(1)} %get-tuple-element.140), channel_id=1, source_target_pairs={{0,4},{1,5},{2,6},{3,7},{4,0},{5,1},{6,2},{7,3},{8,12},{9,13},{10,... | collective-permute-start | bytes 1769480 | tf_op jit(solution)/shard_map/ppermute | solution.py:707
  280.9 19.4 %collective-permute-start.30 = (bf16[64,2304]{1,0:T(8,128)(2,1)S(1)}, bf16[64,2304]{1,0:T(8,128)(2,1)S(1)}, u32[]{:S(2)}, u32[]{:S(2)}) collective-permute-start(bf16[64,2304]{1,0:T(8,128)(2,1)S(1)} %get-tuple-element.126.refs_0_), channel_id=1, source_target_pairs={{0,1},{1,0},{2,3},{3,2},{4,5},{5,4},{6,7},{7,6},{8,9},{9,8},{10,11... | collective-permute-start | bytes 884744 | tf_op jit(solution)/shard_map/ppermute | solution.py:707
  280.9 16.4 %collective-permute-start.32 = (bf16[64,2304]{1,0:T(8,128)(2,1)S(1)}, bf16[64,2304]{1,0:T(8,128)(2,1)S(1)}, u32[]{:S(2)}, u32[]{:S(2)}) collective-permute-start(bf16[64,2304]{1,0:T(8,128)(2,1)S(1)} %get-tuple-element.126.refs_0_), channel_id=1, source_target_pairs={{0,2},{1,3},{2,0},{3,1},{4,6},{5,7},{6,4},{7,5},{8,10},{9,11},{10,... | collective-permute-start | bytes 884744 | tf_op jit(solution)/shard_map/ppermute | solution.py:707
  282.8 17.5 %collective-permute-start.31 = (bf16[80,2304]{1,0:T(8,128)(2,1)S(1)}, bf16[80,2304]{1,0:T(8,128)(2,1)S(1)}, u32[]{:S(2)}, u32[]{:S(2)}) collective-permute-start(bf16[80,2304]{1,0:T(8,128)(2,1)S(1)} %get-tuple-element.127.refs_1_), channel_id=1, source_target_pairs={{0,1},{1,0},{2,3},{3,2},{4,5},{5,4},{6,7},{7,6},{8,9},{9,8},{10,11... | collective-permute-start | bytes 1105928 | tf_op jit(solution)/shard_map/ppermute | solution.py:707
  282.9 15.3 %collective-permute-start.33 = (bf16[80,2304]{1,0:T(8,128)(2,1)S(1)}, bf16[80,2304]{1,0:T(8,128)(2,1)S(1)}, u32[]{:S(2)}, u32[]{:S(2)}) collective-permute-start(bf16[80,2304]{1,0:T(8,128)(2,1)S(1)} %get-tuple-element.127.refs_1_), channel_id=1, source_target_pairs={{0,2},{1,3},{2,0},{3,1},{4,6},{5,7},{6,4},{7,5},{8,10},{9,11},{10,... | collective-permute-start | bytes 1105928 | tf_op jit(solution)/shard_map/ppermute | solution.py:707
  294.7 20.6 %collective-permute-start.48 = (bf16[264,768]{1,0:T(8,128)(2,1)S(1)}, bf16[264,768]{1,0:T(8,128)(2,1)S(1)}, u32[]{:S(2)}, u32[]{:S(2)}) collective-permute-start(bf16[264,768]{1,0:T(8,128)(2,1)S(1)} %pad_maximum_fusion), channel_id=1, source_target_pairs={{0,8},{1,9},{2,10},{3,11},{4,12},{5,13},{6,14},{7,15},{8,0},{9,1},... | collective-permute-start | bytes 1216520 | tf_op jit(solution)/shard_map/ppermute | solution.py:707
  298.3 2.0 collective-permute-start.44
  298.3 2.1 collective-permute-start.45
  301.1 20.6 %collective-permute-start.46 = (bf16[96,2432]{1,0:T(8,128)(2,1)S(1)}, bf16[96,2432]{1,0:T(8,128)(2,1)S(1)}, u32[]{:S(2)}, u32[]{:S(2)}) collective-permute-start(bf16[96,2432]{1,0:T(8,128)(2,1)S(1)} %get-tuple-element.145), channel_id=1, source_target_pairs={{0,4},{1,5},{2,6},{3,7},{4,0},{5,1},{6,2},{7,3},{8,12},{9,13},{10,... | collective-permute-start | bytes 1400840 | tf_op jit(solution)/shard_map/ppermute | solution.py:707
  321.7 12.9 %collective-permute-start.47 = (bf16[48,2432]{1,0:T(8,128)(2,1)S(1)}, bf16[48,2432]{1,0:T(8,128)(2,1)S(1)}, u32[]{:S(2)}, u32[]{:S(2)}) collective-permute-start(bf16[48,2432]{1,0:T(8,128)(2,1)S(1)} %add_convert_fusion.2), channel_id=1, source_target_pairs={{0,8},{1,9},{2,10},{3,11},{4,12},{5,13},{6,14},{7,15},{8,0},{9,1},... | collective-permute-start | bytes 700424 | tf_op jit(solution)/shard_map/ppermute | solution.py:707
  (55 other events, 586.5 us)
Sparse Core Ops, SparseCore 0:
  23.4 75.1 all-gather.1

commit v10 on v7

--- a/solution.py
+++ b/solution.py
@@ -427,7 +427,8 @@
 
 def local_finish_body(
     lower_ref, first_ref, dq_ref, own_ref, low_ref, high_ref, table_ref, d_middle_ref, x_ref, gain_ref,
-    gain_mlp_ref, other_ref, other_attn_ref, other_mlp_ref, out_ref, grad_ref, gain_attn_ref, gain_scr,
+    gain_mlp_ref, other_ref, other_attn_ref, other_mlp_ref, out_ref, grad_ref, gain_attn_ref,
+    gain_scr,
 ):
     rows, width = dq_ref.shape
 
@@ -766,13 +767,13 @@
     send[half + base : half + base + rows, columns] = result[3 * rows :].astype(BF)
 
 
-def early_body(terms, *refs):
+def early_body(terms, split, *refs):
     refs, outs = refs[:-3], refs[-3:]
-    rights, lefts = refs[:4], refs[4:]
+    operands, lefts = (refs[:split], refs[split:-4]), refs[-4:]
     width = outs[0].shape[1]
     base = 0
-    for rows, (start, end) in terms:
-        right = jnp.concatenate([ref[:, start:end] for ref in rights], 0)
+    for which, rows, (start, end) in terms:
+        right = jnp.concatenate([ref[:, start:end] for ref in operands[which]], 0)
         result = dot(left_rows_of(lefts, rows), right)
         for column in range(0, end - start, width):
             by_plane(result[:, column : column + width], base, outs)
@@ -781,11 +782,11 @@
 
 def late_body(rows, place_ref, *refs):
     refs, outs, scr = refs[:-4], refs[-4:-1], refs[-1]
-    rights, lefts = refs[:4], refs[4:]
-    tokens = lefts[0].shape[2]
+    rights, lefts = refs[:-4], refs[-4:]
     columns = rights[0].shape[1]
     width = columns // 3
     size = outs[0].shape[0]
+    tokens = lefts[0].shape[2]
     right = jnp.concatenate([ref[:tokens] for ref in rights], 0)
     by_plane(dot(left_rows_of(lefts, rows), right), 0, outs, slice(0, columns))
     tail = sum(ref[tokens:, :width].astype(F32) for ref in rights)
@@ -996,7 +997,6 @@
             [pltpu.SMEM] * 2 + [pltpu.VMEM] * 8,
         )
         left, d_folded = lax.optimization_barrier((left, d_folded))
-        left = [left[0]] + [partner(left[apart], apart, count) for apart in range(1, 4)]
     else:
         left = [
             plane_rows(jnp.where(lower, a, b).T.reshape(count, -1, rows), group_pos, count)
@@ -1027,8 +1027,11 @@
         1,
     )
     sent = (sent.astype(F32) + back.astype(F32)).astype(BF)
-    left, sent = lax.optimization_barrier((left, sent))
+    if count == GROUP:
+        left, sent = lax.optimization_barrier((left, sent))
+        left = [left[0]] + [partner(left[apart], apart, count) for apart in range(1, 4)]
     got = exchange(sent, count)
+    left, got = lax.optimization_barrier((left, got))
 
     d_proj_1, gain_attn_1, *grad_1 = on_core(
         global_finish_body,
@@ -1040,7 +1043,7 @@
     d_mlp = jnp.concatenate(
         [jnp.where(lower, a, up_1[i * row_count :][:row_count]) for i, a in enumerate(up_0)]
     )
-    across_mlp, beside_mlp = partner(d_mlp, 2, count), partner(d_mlp, 1, count)
+    across_mlp = partner(d_mlp, 2, count)
     gain_mlp_0, d_mid_0, d_att_0, right = on_core(
         local_back_middle_body,
         [
@@ -1054,11 +1057,11 @@
         [pltpu.VMEM] * len(others) + [pltpu.SMEM] + [pltpu.VMEM] * 6,
     )
     d_att_0, right, across_mlp = lax.optimization_barrier((d_att_0, right, across_mlp))
-    across, beside = partner(right, 2, count), partner(right, 1, count)
-    d_mlp = [d_mlp, beside_mlp, across_mlp, partner(across_mlp, 1, count)]
+    across = [partner(right, 2, count)]
+    d_mlp = [d_mlp, partner(d_mlp, 1, count), across_mlp, partner(across_mlp, 1, count)]
     out_near, out_far = first_hop(
         on_core(
-            functools.partial(early_body, [((3 * shard_total, left_total), (0, width))]),
+            functools.partial(early_body, [(0, (3 * shard_total, left_total), (0, width))], 4),
             three_parts((hidden_total, width)),
             (*d_mlp, *left),
         ),
@@ -1076,9 +1079,14 @@
     )
     from_after = lax.ppermute(d_before, "dp", down_pairs)
     from_before = lax.ppermute(d_after, "dp", up_pairs)
+    from_after, out_far = lax.optimization_barrier((from_after, out_far))
     d_proj, grad_0, gain_attn_sum = on_core(
         local_finish_body,
-        [((rows + EXTRA, 3 * width), BF), ((rows, width), BF), ((1, width), F32)],
+        [
+            ((rows + EXTRA, 3 * width), BF),
+            ((rows, width), BF),
+            ((1, width), F32),
+        ],
         (
             lower_flag, first, dq_0, d_own, from_after, from_before, local_tables, d_mid_0, in_0, gain_attn,
             gain_mlp_0, d_proj_1, gain_attn_1, gain_mlp_1,
@@ -1086,28 +1094,30 @@
         [pltpu.VMEM((1, width), F32)],
         [pltpu.SMEM] + [pltpu.VMEM] * 13,
     )
-    across, d_proj, out_far = lax.optimization_barrier((across, d_proj, out_far))
-    mlp_out_share = second_hop(out_near, out_far, count)
-    right = [right, beside, across, partner(across, 1, count)]
-    early_rows = shard_total * (inner // width + 1)
+    across_chunks = [partner(d_proj, 2, count)]
+    across, right, _ = lax.optimization_barrier((across, right, d_proj))
+    right = [right, partner(right, 1, count)] + across
+    right += [partner(item, 1, count) for item in across]
+    in_rows, attn_rows = shard_total * (inner // width), shard_total
+    early_rows = in_rows + attn_rows
+    terms = [
+        (0, (2 * shard_total, 3 * shard_total), (0, inner)),
+        (0, (shard_total, 2 * shard_total), (inner, inner + width)),
+    ]
     near, far = first_hop(
         on_core(
-            functools.partial(
-                early_body,
-                [
-                    ((2 * shard_total, 3 * shard_total), (0, inner)),
-                    ((shard_total, 2 * shard_total), (inner, inner + width)),
-                ],
-            ),
+            functools.partial(early_body, terms, len(right)),
             three_parts((early_rows, width)),
             (*right, *left),
         ),
         count,
     )
-    across, beside = partner(d_proj, 2, count), partner(d_proj, 1, count)
-    across, far = lax.optimization_barrier((across, far))
-    early = second_hop(near, far, count)
-    late_in = (group_pos[None], d_proj, beside, across, partner(across, 1, count), *left)
+    far = jnp.concatenate([far, out_far])
+    across_chunks, d_proj, _ = lax.optimization_barrier((across_chunks, d_proj, far))
+    far = partner(far, 8, count)
+    right = [d_proj, partner(d_proj, 1, count)] + across_chunks
+    right += [partner(item, 1, count) for item in across_chunks]
+    late_in = (group_pos[None], *right, *left)
     late = on_core(
         functools.partial(late_body, (0, shard_total)),
         three_parts((shard_total, 3 * width + LANES)),
@@ -1115,10 +1125,13 @@
         [pltpu.VMEM((width, LANES), F32)],
         [pltpu.SMEM] + [pltpu.VMEM] * (len(late_in) - 1),
     )
+    far, _ = lax.optimization_barrier((far, late[0]))
+    early = near + far[:early_rows].astype(F32)
+    mlp_out_share = out_near + far[early_rows:].astype(F32)
     late = second_hop(*first_hop(late, count), count)
     parts = [early[p * shard_total : (p + 1) * shard_total] for p in range(inner // width)]
     in_share = jnp.concatenate(parts, 1)
-    attn_share = early[early_rows - shard_total :]
+    attn_share = early[in_rows : in_rows + attn_rows]
     gain_columns = late[:, 3 * width :]
     qkv_share, in_share, mlp_out_share, attn_share, gain_columns = (
         over_groups(item, count)

time: 351 us -> 342 us (0.974)
  blocking collectives: 55.1 us -> 32.9 us
  starting transfers between devices: 50.2 us -> 56.5 us
  local copies, waits for them, and re-layouts: 40.4 us -> 44.8 us
    all_to_all x3 -> x2, blocking collectives: 55.1 us -> 32.9 us  [exchange(): return lax.all_to_all(blocks, 'dp', 0, 0, axis_index_groups=groups)]
    all_to_all x1 -> x2, starting transfers between devices: 4.17 us -> 8.92 us  [exchange(): return lax.all_to_all(blocks, 'dp', 0, 0, axis_index_groups=groups)]
    unnamed x102, local copies, waits for them, and re-layouts: 21.8 us -> 26.1 us
    ppermute x36 -> x35, starting transfers between devices: 31 us -> 32.5 us  [partner(): return lax.ppermute(rows, 'dp', [(i, i ^ apart) for i in range(count)])]
    ppermute x36 -> x35, waiting for transfers between devices: 88 us -> 88.1 us  [partner(): return lax.ppermute(rows, 'dp', [(i, i ^ apart) for i in range(count)])]
  transfers between devices with their start and end apart: 46 -> 46, of which waited for: 23 -> 26; matrix products, arithmetic and copies ran while one was open for 6% -> 6% of each run, Pallas kernels for 6% -> 7%
where the time goes in v10:
time: 342 us; the launch traced here: 341 us
  waiting for transfers between devices  130 us (38%)
  Pallas kernels  56.6 us (17%)
  starting transfers between devices  56.5 us (17%)
  local copies, waits for them, and re-layouts  44.8 us (13%)
  blocking collectives  32.9 us (10%)
  between operations  14.9 us (4%)
  other arithmetic  5.13 us (2%)
    ppermute x35, waiting for transfers between devices, partner(): return lax.ppermute(rows, 'dp', [(i, i ^ apart) for i in range(count)])  88.1 us
    pallas_call x17, Pallas kernels, on_core(): pl.pallas_call(body, out_shape=[jax.ShapeDtypeStruct(shape, dtype) for sh...  56.6 us
    all_to_all x2, blocking collectives, exchange(): return lax.all_to_all(blocks, 'dp', 0, 0, axis_index_groups=groups)  32.9 us
    ppermute x35, starting transfers between devices, partner(): return lax.ppermute(rows, 'dp', [(i, i ^ apart) for i in range(count)])  32.5 us
    all_gather x1, waiting for transfers between devices, on_device(): others = [lax.all_gather(stacked, 'dp', axis=0, tiled=True)]  28.3 us
    unnamed x102, local copies, waits for them, and re-layouts  26.1 us
    dynamic_update_slice x16, local copies, waits for them, and re-layouts, gather_rows(): whole = lax.dynamic_update_slice(whole, item[None], start)  11.4 us
    ppermute x4, waiting for transfers between devices, to_other_section(): return [lax.ppermute(rows, 'section', pairs) for rows in chunks]  9.38 us
  transfers between devices with their start and end apart: 46, of which 26 were waited for; matrix products, arithmetic and copies ran while one was open for 6% of the time, Pallas kernels for 7%

profile of v10, /device:TPU:0, one launch (start us, length us, event | category | flops | bytes accessed | tf_op | source)
XLA Modules:
  0.0 340.9 jit_solution(8682739929130710195)
XLA Ops:
  10.3 3.0 collective-permute-start.1
  13.3 1.6 collective-permute-start.2
  14.9 2.6 collective-permute-start.3
  23.5 2.1 broadcast_in_dim.105
  27.5 6.9 %collective-permute-done.3 = bf16[48,2432]{1,0:T(8,128)(2,1)S(1)} collective-permute-done((bf16[48,2432]{1,0:T(8,128)(2,1)S(1)}, bf16[48,2432]{1,0:T(8,128)(2,1)S(1)}, u32[]{:S(2)}, u32[]{:S(2)}) %collective-permute-start.3) | collective-permute-done | bytes 233504 | tf_op jit(solution)/shard_map/ppermute | solution.py:703
  34.9 1.5 collective-permute-start.7
  40.0 5.6 %collective-permute-done.6 = bf16[48,2432]{1,0:T(8,128)(2,1)S(1)} collective-permute-done((bf16[48,2432]{1,0:T(8,128)(2,1)S(1)}, bf16[48,2432]{1,0:T(8,128)(2,1)S(1)}, u32[]{:S(2)}, u32[]{:S(2)}) %collective-permute-start.6) | collective-permute-done | bytes 233504 | tf_op jit(solution)/shard_map/ppermute | solution.py:703
  46.3 3.2 collective-permute-done.7
  56.9 3.1 shard_map.154
  60.7 2.1 collective-permute-start.16
  64.9 1.7 collective-permute-done.17.after_ref
  66.6 3.6 %shard_map.155 = (bf16[128,768]{1,0:T(8,128)(2,1)S(1)}, f32[12,1,128]{2,1,0:T(1,128)S(1)}) custom-call(bf16[128,768]{1,0:T(8,128)(2,1)S(1)} %get-tuple-element.78.q_ref, bf16[128,1536]{1,0:T(8,128)(2,1)S(1)} %collective-permute-done.16.before_ref, bf16[128,1536]{1,0:T(8,128)(2,1)S(1)} %get-tuple-element.79.own_ref, ...), custom_call_target="tpu_custom_call" | custom-call | flops 1024 | bytes 1024 | tf_op jit(solution)/shard_map/pallas_call | solution.py:65
  70.2 28.3 %all-gather.2.cloned.1.call-done.refs_0_ = bf16[768,4352]{1,0:T(8,128)(2,1)} async-done(((bf16[48,4352]{1,0:T(8,128)(2,1)}), bf16[768,4352]{1,0:T(8,128)(2,1)}) %all-gather.2.cloned.1.call-update) | async-done | bytes 6684688 | tf_op jit(solution)/shard_map/all_gather | solution.py:874
  98.6 4.4 %shard_map.156 = (bf16[128,768]{1,0:T(8,128)(2,1)S(1)}, bf16[128,1152]{1,0:T(8,128)(2,1)S(1)}, f32[128,768]{1,0:T(8,128)S(1)}, f32[128,2304]{1,0:T(8,128)S(1)}, ...) custom-call(bf16[768,4352]{1,0:T(8,128)(2,1)} %all-gather.2.cloned.1.call-done.refs_0_, ...), custom_call_target="tpu_custom_call" | custom-call | flops 1024 | bytes 1024 | tf_op jit(solution)/shard_map/pallas_call | solution.py:65
  105.5 3.3 collective-permute-start.18
  110.6 1.4 collective-permute-done.18.low_ref.refs_2_
  112.0 1.4 collective-permute-done.19.high_ref.refs_3_
  113.5 3.1 shard_map.157
  116.6 21.2 %all_to_all.20.got_ref = bf16[16,144,128]{2,1,0:T(8,128)(2,1)S(1)} all-to-all(bf16[16,144,128]{2,1,0:T(8,128)(2,1)S(1)} %get-tuple-element.84), channel_id=1, replica_groups={{0,1,2,3,4,5,6,7,8,9,10,11,12,13,14,15},{16,17,18,19,20,21,22,23,24,25,..., dimensions={0} | all-to-all | bytes 1179648 | tf_op jit(solution)/shard_map/all_to_all | solution.py:694
  139.5 6.0 %shard_map.158 = (bf16[16,48,128]{2,1,0:T(8,128)(2,1)S(1)}, f32[6,1,256]{2,1,0:T(1,128)S(1)}) custom-call(bf16[16,144,128]{2,1,0:T(8,128)(2,1)S(1)} %all_to_all.20.got_ref, bf16[16,64,128]{2,1,0:T(8,128)(2,1)S(1)} %collective-permute-done.20.other_ref, s32[1024,1]{1,0:T(8,128)S(1)} %copy.19.own_seg_ref, s32[1024,1]{1,0:T(8,128)S(1)} %copy.20.shared_seg_ref), custom_call_target="tpu_custom_call" | custom-call | flops 1024 | bytes 1024 | tf_op jit(solution)/shard_map/pallas_call | solution.py:65
  145.5 11.8 %all_to_all.21.refs_1_ = bf16[16,48,128]{2,1,0:T(8,128)(2,1)S(1)} all-to-all(bf16[16,48,128]{2,1,0:T(8,128)(2,1)S(1)} %get-tuple-element.85), channel_id=1, replica_groups={{0,1,2,3,4,5,6,7,8,9,10,11,12,13,14,15},{16,17,18,19,20,21,22,23,24,25,..., dimensions={0} | all-to-all | bytes 393216 | tf_op jit(solution)/shard_map/all_to_all | solution.py:694
  157.3 7.7 %shard_map.159 = (bf16[128,768]{1,0:T(8,128)(2,1)S(1)}, bf16[128,768]{1,0:T(8,128)(2,1)S(1)}, bf16[128,768]{1,0:T(8,128)(2,1)S(1)}, bf16[128,1152]{1,0:T(8,128)(...) custom-call(bf16[768,4352]{1,0:T(8,128)(2,1)} %all-gather.2.cloned.1, ...), custom_call_target="tpu_custom_call" | custom-call | flops 1024 | bytes 1024 | tf_op jit(solution)/shard_map/pallas_call | solution.py:65
  169.4 4.2 %all-to-all-start.2 = ((bf16[16,48,128]{2,1,0:T(8,128)(2,1)}), bf16[16,48,128]{2,1,0:T(8,128)(2,1)}, u32[]{:S(2)}, u32[]{:S(2)}) async-start(bf16[16,48,128]{2,1,0:T(8,128)(2,1)} %get-tuple-element.95), calls=%async_computation.2 | async-start | bytes 393216 | tf_op jit(solution)/shard_map/all_to_all | solution.py:694
  183.5 8.2 %shard_map.161 = (bf16[16,144,128]{2,1,0:T(8,128)(2,1)S(1)}, bf16[16,64,128]{2,1,0:T(8,128)(2,1)S(1)}) custom-call(bf16[16,144,128]{2,1,0:T(8,128)(2,1)S(1)} %all_to_all.20.got_ref, bf16[16,64,128]{2,1,0:T(8,128)(2,1)S(1)} %copy-done.10, s32[1024,1]{1,0:T(8,128)S(1)} %copy.19.own_seg_ref, s32[1024,1]{1,0:T(8,128)S(1)} %copy.20.shared_seg_ref, ...), custom_call_target="tpu_custom_call" | custom-call | flops 1024 | bytes 1024 | tf_op jit(solution)/shard_map/pallas_call | solution.py:65
  194.5 4.8 %all-to-all-start.3 = ((bf16[16,144,128]{2,1,0:T(8,128)(2,1)}), bf16[16,144,128]{2,1,0:T(8,128)(2,1)S(1)}, u32[]{:S(2)}, u32[]{:S(2)}) async-start(bf16[16,144,128]{2,1,0:T(8,128)(2,1)} %add_convert_fusion), calls=%async_computation.3 | async-start | bytes 1179648 | tf_op jit(solution)/shard_map/all_to_all | solution.py:694
  199.8 1.7 collective-permute-start.23
  201.5 10.9 %collective-permute-done.23.refs_6_ = bf16[4,216,128]{2,1,0:T(8,128)(2,1)S(1)} collective-permute-done((bf16[4,216,128]{2,1,0:T(8,128)(2,1)S(1)}, bf16[4,216,128]{2,1,0:T(8,128)(2,1)S(1)}, u32[]{:S(2)}, u32[]{:S(2)}) %collective-permute-start.23) | collective-permute-done | bytes 221216 | tf_op jit(solution)/shard_map/ppermute | solution.py:703
  212.4 5.3 %collective-permute-done.24.refs_7_ = bf16[4,216,128]{2,1,0:T(8,128)(2,1)S(1)} collective-permute-done((bf16[4,216,128]{2,1,0:T(8,128)(2,1)S(1)}, bf16[4,216,128]{2,1,0:T(8,128)(2,1)S(1)}, u32[]{:S(2)}, u32[]{:S(2)}) %collective-permute-start.24) | collective-permute-done | bytes 221216 | tf_op jit(solution)/shard_map/ppermute | solution.py:703
  218.7 3.6 %shard_map.162 = (bf16[128,2304]{1,0:T(8,128)(2,1)S(1)}, f32[1,768]{1,0:T(1,128)S(1)}, bf16[64,768]{1,0:T(8,128)(2,1)S(1)}, bf16[64,768]{1,0:T(8,128)(2,1)S(1)}) custom-call(bf16[768,2432]{1,0:T(8,128)(2,1)} %bitcast.23.first_ref, bf16[16,144,128]{2,1,0:T(8,128)(2,1)S(1)} %all-to-all-done.3.got_ref, f32[128,768]{1,0:T(8,128)S(1)} %copy-done.22, ...), custom_call_target="tpu_custom_call" | custom-call | flops 1024 | bytes 1024 | tf_op jit(solution)/shard_map/pallas_call | solution.py:65
  224.9 4.9 %collective-permute-done.25.refs_2_ = bf16[64,768]{1,0:T(8,128)(2,1)S(1)} collective-permute-done((bf16[64,768]{1,0:T(8,128)(2,1)S(1)}, bf16[64,768]{1,0:T(8,128)(2,1)S(1)}, u32[]{:S(2)}, u32[]{:S(2)}) %collective-permute-start.25) | collective-permute-done | bytes 98336 | tf_op jit(solution)/shard_map/ppermute | solution.py:699
  229.8 1.6 collective-permute-done.26.refs_3_
  235.3 6.1 %shard_map.163 = (f32[1,768]{1,0:T(1,128)S(1)}, f32[128,768]{1,0:T(8,128)S(1)}, bf16[128,768]{1,0:T(8,128)(2,1)S(1)}, bf16[128,3072]{1,0:T(8,128)(2,1)S(1)}) custom-call(bf16[768,4352]{1,0:T(8,128)(2,1)} %all-gather.2.cloned.1.call-done.refs_0_, s32[1]{0:T(128)} %bitcast.37.lower_ref.refs_1_, bf16[64,768]{1,0:T(8,128)(2,1)S(1)} %collective-permute-done.25.refs_2_, ...), custom_call_target="tpu_custom_call" | custom-call | flops 1024 | bytes 1024 | tf_op jit(solution)/shard_map/pallas_call | solution.py:65
  241.4 1.7 collective-permute-start.34
  245.3 1.5 collective-permute-start.31
  246.9 3.5 %shard_map.164 = (bf16[128,768]{1,0:T(8,128)(2,1)S(1)}, f32[128,1536]{1,0:T(8,128)S(1)}, bf16[128,1536]{1,0:T(8,128)(2,1)S(1)}, bf16[128,1536]{1,0:T(8,128)(2,1)S(1)}) custom-call(bf16[128,768]{1,0:T(8,128)(2,1)S(1)} %copy-done.14, bf16[128,1536]{1,0:T(8,128)(2,1)S(1)} %copy-done.4, bf16[128,1536]{1,0:T(8,128)(2,1)S(1)} %copy-done.2, ...), custom_call_target="tpu_custom_call" | custom-call | flops 1024 | bytes 1024 | tf_op jit(solution)/shard_map/pallas_call | solution.py:65
  251.7 3.1 collective-permute-start.32
  256.1 4.0 %shard_map.166 = (bf16[144,2304]{1,0:T(8,128)(2,1)S(1)}, bf16[128,768]{1,0:T(8,128)(2,1)S(1)}, f32[1,768]{1,0:T(1,128)}) custom-call(s32[1]{0:T(128)} %bitcast.37.lower_ref.refs_1_, bf16[768,2432]{1,0:T(8,128)(2,1)} %bitcast.23.first_ref, bf16[128,768]{1,0:T(8,128)(2,1)S(1)} %get-tuple-element.113.dq_ref, f32[128,1536]{1,0:T(8,128)S(1)} %get-tuple-element.114.own_ref, ...), custom_call_target="tpu_custom_call" | custom-call | flops 1024 | bytes 1024 | tf_op jit(solution)/shard_map/pallas_call | solution.py:65
  260.0 5.3 %collective-permute-done.34.refs_2_ = bf16[128,3072]{1,0:T(8,128)(2,1)S(1)} collective-permute-done((bf16[128,3072]{1,0:T(8,128)(2,1)S(1)}, bf16[128,3072]{1,0:T(8,128)(2,1)S(1)}, u32[]{:S(2)}, u32[]{:S(2)}) %collective-permute-start.34) | collective-permute-done | bytes 786464 | tf_op jit(solution)/shard_map/ppermute | solution.py:703
  265.4 6.7 %collective-permute-start.35 = (bf16[128,3072]{1,0:T(8,128)(2,1)S(1)}, bf16[128,3072]{1,0:T(8,128)(2,1)S(1)}, u32[]{:S(2)}, u32[]{:S(2)}) collective-permute-start(bf16[128,3072]{1,0:T(8,128)(2,1)S(1)} %get-tuple-element.133.refs_0_), channel_id=1, source_target_pairs={{0,1},{1,0},{2,3},{3,2},{4,5},{5,4},{6,7},{7,6},{8,9},{9,8},{10,11... | collective-permute-start | bytes 2359304 | tf_op jit(solution)/shard_map/ppermute | solution.py:703
  272.2 1.8 collective-permute-done.35.refs_1_
  275.9 2.2 collective-permute-start.37
  278.1 2.1 collective-permute-start.33
  280.2 11.8 %collective-permute-done.37 = bf16[384,768]{1,0:T(8,128)(2,1)S(1)} collective-permute-done((bf16[384,768]{1,0:T(8,128)(2,1)S(1)}, bf16[384,768]{1,0:T(8,128)(2,1)S(1)}, u32[]{:S(2)}, u32[]{:S(2)}) %collective-permute-start.37) | collective-permute-done | bytes 589856 | tf_op jit(solution)/shard_map/ppermute | solution.py:703
  292.1 3.1 collective-permute-done.33.refs_2_
  295.7 2.3 collective-permute-start.42
  300.7 15.9 %collective-permute-done.42 = bf16[264,768]{1,0:T(8,128)(2,1)S(1)} collective-permute-done((bf16[264,768]{1,0:T(8,128)(2,1)S(1)}, bf16[264,768]{1,0:T(8,128)(2,1)S(1)}, u32[]{:S(2)}, u32[]{:S(2)}) %collective-permute-start.42) | collective-permute-done | bytes 405536 | tf_op jit(solution)/shard_map/ppermute | solution.py:703
  318.2 2.8 collective-permute-done.40
  321.9 10.6 %collective-permute-done.41 = bf16[48,2432]{1,0:T(8,128)(2,1)S(1)} collective-permute-done((bf16[48,2432]{1,0:T(8,128)(2,1)S(1)}, bf16[48,2432]{1,0:T(8,128)(2,1)S(1)}, u32[]{:S(2)}, u32[]{:S(2)}) %collective-permute-start.41) | collective-permute-done | bytes 233504 | tf_op jit(solution)/shard_map/ppermute | solution.py:703
  (244 shorter events, 70.7 us)
Async XLA Ops:
  7.2 91.4 %all-gather.2.cloned.1.call-start = ((), (), s32[]{:S(2)}) async-start(), calls=%async_computation.4 | async-start | bytes 7102464 | tf_op jit(solution)/shard_map/all_gather | solution.py:874
  10.3 13.0 %collective-permute-start.1 = (bf16[48,2432]{1,0:T(8,128)(2,1)S(1)}, bf16[48,2432]{1,0:T(8,128)(2,1)S(1)}, u32[]{:S(2)}, u32[]{:S(2)}) collective-permute-start(bf16[48,2432]{1,0:T(8,128)(2,1)S(1)} %shard_map.153), channel_id=1, source_target_pairs={{0,2},{1,3},{2,0},{3,1},{4,6},{5,7},{6,4},{7,5},{8,10},{9,11},{10,... | collective-permute-start | bytes 700424 | tf_op jit(solution)/shard_map/ppermute | solution.py:703
  13.3 13.9 %collective-permute-start.2 = (bf16[48,2432]{1,0:T(8,128)(2,1)S(1)}, bf16[48,2432]{1,0:T(8,128)(2,1)S(1)}, u32[]{:S(2)}, u32[]{:S(2)}) collective-permute-start(bf16[48,2432]{1,0:T(8,128)(2,1)S(1)} %shard_map.153), channel_id=1, source_target_pairs={{0,4},{1,5},{2,6},{3,7},{4,0},{5,1},{6,2},{7,3},{8,12},{9,13},{10,... | collective-permute-start | bytes 700424 | tf_op jit(solution)/shard_map/ppermute | solution.py:703
  14.9 19.5 %collective-permute-start.3 = (bf16[48,2432]{1,0:T(8,128)(2,1)S(1)}, bf16[48,2432]{1,0:T(8,128)(2,1)S(1)}, u32[]{:S(2)}, u32[]{:S(2)}) collective-permute-start(bf16[48,2432]{1,0:T(8,128)(2,1)S(1)} %shard_map.153), channel_id=1, source_target_pairs={{0,8},{1,9},{2,10},{3,11},{4,12},{5,13},{6,14},{7,15},{8,0},{9,1},... | collective-permute-start | bytes 700424 | tf_op jit(solution)/shard_map/ppermute | solution.py:703
  17.5 17.5 %collective-permute-start.4 = (bf16[48,2432]{1,0:T(8,128)(2,1)S(1)}, bf16[48,2432]{1,0:T(8,128)(2,1)S(1)}, u32[]{:S(2)}, u32[]{:S(2)}) collective-permute-start(bf16[48,2432]{1,0:T(8,128)(2,1)S(1)} %shard_map.153), channel_id=1, source_target_pairs={{0,12},{1,13},{2,14},{3,15},{4,8},{5,9},{6,10},{7,11},{8,4},{9,5},... | collective-permute-start | bytes 700424 | tf_op jit(solution)/shard_map/ppermute | solution.py:703
  18.4 1.2 collective-permute-start
  19.6 30.6 %collective-permute-start.8 = (bf16[48,2432]{1,0:T(8,128)(2,1)S(1)}, bf16[48,2432]{1,0:T(8,128)(2,1)S(1)}, u32[]{:S(2)}, u32[]{:S(2)}) collective-permute-start(bf16[48,2432]{1,0:T(8,128)(2,1)S(1)} %shard_map.153), channel_id=1, source_target_pairs={{0,1},{1,0},{2,3},{3,2},{4,5},{5,4},{6,7},{7,6},{8,9},{9,8},{10,11... | collective-permute-start | bytes 700424 | tf_op jit(solution)/shard_map/ppermute | solution.py:703
  26.8 24.6 %collective-permute-start.9 = (bf16[48,2432]{1,0:T(8,128)(2,1)S(1)}, bf16[48,2432]{1,0:T(8,128)(2,1)S(1)}, u32[]{:S(2)}, u32[]{:S(2)}) collective-permute-start(bf16[48,2432]{1,0:T(8,128)(2,1)S(1)} %collective-permute-done.1), channel_id=1, source_target_pairs={{0,1},{1,0},{2,3},{3,2},{4,5},{5,4},{6,7},{7,6},{8,9},{9,8},{10,11... | collective-permute-start | bytes 700424 | tf_op jit(solution)/shard_map/ppermute | solution.py:703
  27.2 12.1 %collective-permute-start.5 = (bf16[48,2432]{1,0:T(8,128)(2,1)S(1)}, bf16[48,2432]{1,0:T(8,128)(2,1)S(1)}, u32[]{:S(2)}, u32[]{:S(2)}) collective-permute-start(bf16[48,2432]{1,0:T(8,128)(2,1)S(1)} %collective-permute-done.2), channel_id=1, source_target_pairs={{0,2},{1,3},{2,0},{3,1},{4,6},{5,7},{6,4},{7,5},{8,10},{9,11},{10,... | collective-permute-start | bytes 700424 | tf_op jit(solution)/shard_map/ppermute | solution.py:703
  34.4 11.2 %collective-permute-start.6 = (bf16[48,2432]{1,0:T(8,128)(2,1)S(1)}, bf16[48,2432]{1,0:T(8,128)(2,1)S(1)}, u32[]{:S(2)}, u32[]{:S(2)}) collective-permute-start(bf16[48,2432]{1,0:T(8,128)(2,1)S(1)} %collective-permute-done.3), channel_id=1, source_target_pairs={{0,2},{1,3},{2,0},{3,1},{4,6},{5,7},{6,4},{7,5},{8,10},{9,11},{10,... | collective-permute-start | bytes 700424 | tf_op jit(solution)/shard_map/ppermute | solution.py:703
  34.9 14.5 %collective-permute-start.7 = (bf16[48,2432]{1,0:T(8,128)(2,1)S(1)}, bf16[48,2432]{1,0:T(8,128)(2,1)S(1)}, u32[]{:S(2)}, u32[]{:S(2)}) collective-permute-start(bf16[48,2432]{1,0:T(8,128)(2,1)S(1)} %collective-permute-done.4), channel_id=1, source_target_pairs={{0,2},{1,3},{2,0},{3,1},{4,6},{5,7},{6,4},{7,5},{8,10},{9,11},{10,... | collective-permute-start | bytes 700424 | tf_op jit(solution)/shard_map/ppermute | solution.py:703
  39.3 12.8 %collective-permute-start.10 = (bf16[48,2432]{1,0:T(8,128)(2,1)S(1)}, bf16[48,2432]{1,0:T(8,128)(2,1)S(1)}, u32[]{:S(2)}, u32[]{:S(2)}) collective-permute-start(bf16[48,2432]{1,0:T(8,128)(2,1)S(1)} %collective-permute-done.2), channel_id=1, source_target_pairs={{0,1},{1,0},{2,3},{3,2},{4,5},{5,4},{6,7},{7,6},{8,9},{9,8},{10,11... | collective-permute-start | bytes 700424 | tf_op jit(solution)/shard_map/ppermute | solution.py:703
  45.6 8.5 %collective-permute-start.12 = (bf16[48,2432]{1,0:T(8,128)(2,1)S(1)}, bf16[48,2432]{1,0:T(8,128)(2,1)S(1)}, u32[]{:S(2)}, u32[]{:S(2)}) collective-permute-start(bf16[48,2432]{1,0:T(8,128)(2,1)S(1)} %collective-permute-done.3), channel_id=1, source_target_pairs={{0,1},{1,0},{2,3},{3,2},{4,5},{5,4},{6,7},{7,6},{8,9},{9,8},{10,11... | collective-permute-start | bytes 700424 | tf_op jit(solution)/shard_map/ppermute | solution.py:703
  49.5 6.0 %collective-permute-start.14 = (bf16[48,2432]{1,0:T(8,128)(2,1)S(1)}, bf16[48,2432]{1,0:T(8,128)(2,1)S(1)}, u32[]{:S(2)}, u32[]{:S(2)}) collective-permute-start(bf16[48,2432]{1,0:T(8,128)(2,1)S(1)} %collective-permute-done.4), channel_id=1, source_target_pairs={{0,1},{1,0},{2,3},{3,2},{4,5},{5,4},{6,7},{7,6},{8,9},{9,8},{10,11... | collective-permute-start | bytes 700424 | tf_op jit(solution)/shard_map/ppermute | solution.py:703
  50.2 3.2 collective-permute-start.11
  51.4 3.4 collective-permute-start.13
  52.2 4.0 %collective-permute-start.15 = (bf16[48,2432]{1,0:T(8,128)(2,1)S(1)}, bf16[48,2432]{1,0:T(8,128)(2,1)S(1)}, u32[]{:S(2)}, u32[]{:S(2)}) collective-permute-start(bf16[48,2432]{1,0:T(8,128)(2,1)S(1)} %collective-permute-done.7), channel_id=1, source_target_pairs={{0,1},{1,0},{2,3},{3,2},{4,5},{5,4},{6,7},{7,6},{8,9},{9,8},{10,11... | collective-permute-start | bytes 700424 | tf_op jit(solution)/shard_map/ppermute | solution.py:703
  60.7 42.2 %copy-start.1 = (bf16[128,1536]{1,0:T(8,128)(2,1)}, bf16[128,1536]{1,0:T(8,128)(2,1)S(1)}, u32[]{:S(2)}) copy-start(bf16[128,1536]{1,0:T(8,128)(2,1)S(1)} %get-tuple-element.79.own_ref) | copy-start | bytes 1179652
  60.7 42.2 %copy-start.13 = (bf16[128,768]{1,0:T(8,128)(2,1)}, bf16[128,768]{1,0:T(8,128)(2,1)S(1)}, u32[]{:S(2)}) copy-start(bf16[128,768]{1,0:T(8,128)(2,1)S(1)} %get-tuple-element.78.q_ref) | copy-start | bytes 589828
  60.7 4.1 %collective-permute-start.16 = (bf16[128,1536]{1,0:T(8,128)(2,1)S(1)}, bf16[128,1536]{1,0:T(8,128)(2,1)S(1)}, u32[]{:S(2)}, u32[]{:S(2)}) collective-permute-start(bf16[128,1536]{1,0:T(8,128)(2,1)S(1)} %get-tuple-element.79.own_ref), channel_id=1, source_target_pairs={{0,1},{1,2},{2,3},{3,4},{4,5},{5,6},{6,7},{7,8},{8,9},{9,10},{10,1... | collective-permute-start | bytes 1179656 | tf_op jit(solution)/shard_map/ppermute | solution.py:921
  62.9 3.7 %collective-permute-start.17 = (bf16[128,1536]{1,0:T(8,128)(2,1)S(1)}, bf16[128,1536]{1,0:T(8,128)(2,1)S(1)}, u32[]{:S(2)}, u32[]{:S(2)}) collective-permute-start(bf16[128,1536]{1,0:T(8,128)(2,1)S(1)} %get-tuple-element.79.own_ref), channel_id=1, source_target_pairs={{1,0},{2,1},{3,2},{4,3},{5,4},{6,5},{7,6},{8,7},{9,8},{10,9},{11,1... | collective-permute-start | bytes 1179656 | tf_op jit(solution)/shard_map/ppermute | solution.py:923
  105.5 6.5 %collective-permute-start.18 = (bf16[64,768]{1,0:T(8,128)(2,1)S(1)}, bf16[64,768]{1,0:T(8,128)(2,1)S(1)}, u32[]{:S(2)}, u32[]{:S(2)}) collective-permute-start(bf16[64,768]{1,0:T(8,128)(2,1)S(1)} %get-tuple-element.82), channel_id=1, source_target_pairs={{0,16},{1,17},{2,18},{3,19},{4,20},{5,21},{6,22},{7,23},{8,24},{9,... | collective-permute-start | bytes 294920 | tf_op jit(solution)/shard_map/ppermute | solution.py:699
  108.9 4.6 %collective-permute-start.19 = (bf16[64,768]{1,0:T(8,128)(2,1)S(1)}, bf16[64,768]{1,0:T(8,128)(2,1)S(1)}, u32[]{:S(2)}, u32[]{:S(2)}) collective-permute-start(bf16[64,768]{1,0:T(8,128)(2,1)S(1)} %get-tuple-element.83), channel_id=1, source_target_pairs={{0,16},{1,17},{2,18},{3,19},{4,20},{5,21},{6,22},{7,23},{8,24},{9,... | collective-permute-start | bytes 294920 | tf_op jit(solution)/shard_map/ppermute | solution.py:699
  137.9 1.6 collective-permute-start.20
  169.4 13.2 %all-to-all-start.2 = ((bf16[16,48,128]{2,1,0:T(8,128)(2,1)}), bf16[16,48,128]{2,1,0:T(8,128)(2,1)}, u32[]{:S(2)}, u32[]{:S(2)}) async-start(bf16[16,48,128]{2,1,0:T(8,128)(2,1)} %get-tuple-element.95), calls=%async_computation.2 | async-start | bytes 393216 | tf_op jit(solution)/shard_map/all_to_all | solution.py:694
  191.8 1.6 collective-permute-start.21
  194.5 23.2 %all-to-all-start.3 = ((bf16[16,144,128]{2,1,0:T(8,128)(2,1)}), bf16[16,144,128]{2,1,0:T(8,128)(2,1)S(1)}, u32[]{:S(2)}, u32[]{:S(2)}) async-start(bf16[16,144,128]{2,1,0:T(8,128)(2,1)} %add_convert_fusion), calls=%async_computation.3 | async-start | bytes 1179648 | tf_op jit(solution)/shard_map/all_to_all | solution.py:694
  199.3 2.2 collective-permute-start.22
  199.8 12.6 %collective-permute-start.23 = (bf16[4,216,128]{2,1,0:T(8,128)(2,1)S(1)}, bf16[4,216,128]{2,1,0:T(8,128)(2,1)S(1)}, u32[]{:S(2)}, u32[]{:S(2)}) collective-permute-start(bf16[4,216,128]{2,1,0:T(8,128)(2,1)S(1)} %get-tuple-element.151), channel_id=1, source_target_pairs={{0,2},{1,3},{2,0},{3,1},{4,6},{5,7},{6,4},{7,5},{8,10},{9,11},{10,... | collective-permute-start | bytes 663560 | tf_op jit(solution)/shard_map/ppermute | solution.py:703
  201.5 16.2 %collective-permute-start.24 = (bf16[4,216,128]{2,1,0:T(8,128)(2,1)S(1)}, bf16[4,216,128]{2,1,0:T(8,128)(2,1)S(1)}, u32[]{:S(2)}, u32[]{:S(2)}) collective-permute-start(bf16[4,216,128]{2,1,0:T(8,128)(2,1)S(1)} %get-tuple-element.150), channel_id=1, source_target_pairs={{0,3},{1,2},{2,1},{3,0},{4,7},{5,6},{6,5},{7,4},{8,11},{9,10},{10,... | collective-permute-start | bytes 663560 | tf_op jit(solution)/shard_map/ppermute | solution.py:703
  222.3 7.5 %collective-permute-start.25 = (bf16[64,768]{1,0:T(8,128)(2,1)S(1)}, bf16[64,768]{1,0:T(8,128)(2,1)S(1)}, u32[]{:S(2)}, u32[]{:S(2)}) collective-permute-start(bf16[64,768]{1,0:T(8,128)(2,1)S(1)} %get-tuple-element.105), channel_id=1, source_target_pairs={{16,0},{17,1},{18,2},{19,3},{20,4},{21,5},{22,6},{23,7},{24,8},{25... | collective-permute-start | bytes 294920 | tf_op jit(solution)/shard_map/ppermute | solution.py:699
  223.6 7.8 %collective-permute-start.26 = (bf16[64,768]{1,0:T(8,128)(2,1)S(1)}, bf16[64,768]{1,0:T(8,128)(2,1)S(1)}, u32[]{:S(2)}, u32[]{:S(2)}) collective-permute-start(bf16[64,768]{1,0:T(8,128)(2,1)S(1)} %get-tuple-element.106), channel_id=1, source_target_pairs={{16,0},{17,1},{18,2},{19,3},{20,4},{21,5},{22,6},{23,7},{24,8},{25... | collective-permute-start | bytes 294920 | tf_op jit(solution)/shard_map/ppermute | solution.py:699
  231.5 10.0 %collective-permute-start.27 = (bf16[128,768]{1,0:T(8,128)(2,1)S(1)}, bf16[128,768]{1,0:T(8,128)(2,1)S(1)}, u32[]{:S(2)}, u32[]{:S(2)}) collective-permute-start(bf16[128,768]{1,0:T(8,128)(2,1)S(1)} %pad_maximum_fusion.2.refs_0_), channel_id=1, source_target_pairs={{0,2},{1,3},{2,0},{3,1},{4,6},{5,7},{6,4},{7,5},{8,10},{9,11},{10,... | collective-permute-start | bytes 589832 | tf_op jit(solution)/shard_map/ppermute | solution.py:703
  241.4 23.9 %collective-permute-start.34 = (bf16[128,3072]{1,0:T(8,128)(2,1)S(1)}, bf16[128,3072]{1,0:T(8,128)(2,1)S(1)}, u32[]{:S(2)}, u32[]{:S(2)}) collective-permute-start(bf16[128,3072]{1,0:T(8,128)(2,1)S(1)} %get-tuple-element.133.refs_0_), channel_id=1, source_target_pairs={{0,2},{1,3},{2,0},{3,1},{4,6},{5,7},{6,4},{7,5},{8,10},{9,11},{10,... | collective-permute-start | bytes 2359304 | tf_op jit(solution)/shard_map/ppermute | solution.py:703
  243.2 1.4 collective-permute-start.29
  243.2 1.7 collective-permute-start.30
  245.3 9.5 %collective-permute-start.31 = (bf16[144,768]{1,0:T(8,128)(2,1)S(1)}, bf16[144,768]{1,0:T(8,128)(2,1)S(1)}, u32[]{:S(2)}, u32[]{:S(2)}) collective-permute-start(bf16[144,768]{1,0:T(8,128)(2,1)S(1)} %get-tuple-element.122), channel_id=1, source_target_pairs={{0,4},{1,5},{2,6},{3,7},{4,0},{5,1},{6,2},{7,3},{8,12},{9,13},{10,... | collective-permute-start | bytes 663560 | tf_op jit(solution)/shard_map/ppermute | solution.py:703
  250.4 4.4 %collective-permute-start.28 = (bf16[128,1536]{1,0:T(8,128)(2,1)S(1)}, bf16[128,1536]{1,0:T(8,128)(2,1)S(1)}, u32[]{:S(2)}, u32[]{:S(2)}) collective-permute-start(bf16[128,1536]{1,0:T(8,128)(2,1)S(1)} %get-tuple-element.115), channel_id=1, source_target_pairs={{1,0},{2,1},{3,2},{4,3},{5,4},{6,5},{7,6},{8,7},{9,8},{10,9},{11,1... | collective-permute-start | bytes 1179656 | tf_op jit(solution)/shard_map/ppermute | solution.py:1080
  251.7 4.4 %collective-permute-start.32 = (bf16[128,1536]{1,0:T(8,128)(2,1)S(1)}, bf16[128,1536]{1,0:T(8,128)(2,1)S(1)}, u32[]{:S(2)}, u32[]{:S(2)}) collective-permute-start(bf16[128,1536]{1,0:T(8,128)(2,1)S(1)} %get-tuple-element.124), channel_id=1, source_target_pairs={{0,1},{1,2},{2,3},{3,4},{4,5},{5,6},{6,7},{7,8},{8,9},{9,10},{10,1... | collective-permute-start | bytes 1179656 | tf_op jit(solution)/shard_map/ppermute | solution.py:1081
  265.4 8.6 %collective-permute-start.35 = (bf16[128,3072]{1,0:T(8,128)(2,1)S(1)}, bf16[128,3072]{1,0:T(8,128)(2,1)S(1)}, u32[]{:S(2)}, u32[]{:S(2)}) collective-permute-start(bf16[128,3072]{1,0:T(8,128)(2,1)S(1)} %get-tuple-element.133.refs_0_), channel_id=1, source_target_pairs={{0,1},{1,0},{2,3},{3,2},{4,5},{5,4},{6,7},{7,6},{8,9},{9,8},{10,11... | collective-permute-start | bytes 2359304 | tf_op jit(solution)/shard_map/ppermute | solution.py:703
  272.1 3.0 collective-permute-start.36
  275.9 16.0 %collective-permute-start.37 = (bf16[384,768]{1,0:T(8,128)(2,1)S(1)}, bf16[384,768]{1,0:T(8,128)(2,1)S(1)}, u32[]{:S(2)}, u32[]{:S(2)}) collective-permute-start(bf16[384,768]{1,0:T(8,128)(2,1)S(1)} %get-tuple-element.136), channel_id=1, source_target_pairs={{0,4},{1,5},{2,6},{3,7},{4,0},{5,1},{6,2},{7,3},{8,12},{9,13},{10,... | collective-permute-start | bytes 1769480 | tf_op jit(solution)/shard_map/ppermute | solution.py:703
  278.1 17.0 %collective-permute-start.33 = (bf16[144,2304]{1,0:T(8,128)(2,1)S(1)}, bf16[144,2304]{1,0:T(8,128)(2,1)S(1)}, u32[]{:S(2)}, u32[]{:S(2)}) collective-permute-start(bf16[144,2304]{1,0:T(8,128)(2,1)S(1)} %get-tuple-element.138.refs_0_), channel_id=1, source_target_pairs={{0,2},{1,3},{2,0},{3,1},{4,6},{5,7},{6,4},{7,5},{8,10},{9,11},{10,... | collective-permute-start | bytes 1990664 | tf_op jit(solution)/shard_map/ppermute | solution.py:703
  295.2 4.2 %collective-permute-start.38 = (bf16[144,2304]{1,0:T(8,128)(2,1)S(1)}, bf16[144,2304]{1,0:T(8,128)(2,1)S(1)}, u32[]{:S(2)}, u32[]{:S(2)}) collective-permute-start(bf16[144,2304]{1,0:T(8,128)(2,1)S(1)} %get-tuple-element.138.refs_0_), channel_id=1, source_target_pairs={{0,1},{1,0},{2,3},{3,2},{4,5},{5,4},{6,7},{7,6},{8,9},{9,8},{10,11... | collective-permute-start | bytes 1990664 | tf_op jit(solution)/shard_map/ppermute | solution.py:703
  295.2 4.2 %collective-permute-start.39 = (bf16[144,2304]{1,0:T(8,128)(2,1)S(1)}, bf16[144,2304]{1,0:T(8,128)(2,1)S(1)}, u32[]{:S(2)}, u32[]{:S(2)}) collective-permute-start(bf16[144,2304]{1,0:T(8,128)(2,1)S(1)} %collective-permute-done.33.refs_2_), channel_id=1, source_target_pairs={{0,1},{1,0},{2,3},{3,2},{4,5},{5,4},{6,7},{7,6},{8,9},{9,8},{10,11... | collective-permute-start | bytes 1990664 | tf_op jit(solution)/shard_map/ppermute | solution.py:703
  295.7 21.0 %collective-permute-start.42 = (bf16[264,768]{1,0:T(8,128)(2,1)S(1)}, bf16[264,768]{1,0:T(8,128)(2,1)S(1)}, u32[]{:S(2)}, u32[]{:S(2)}) collective-permute-start(bf16[264,768]{1,0:T(8,128)(2,1)S(1)} %pad_maximum_fusion), channel_id=1, source_target_pairs={{0,8},{1,9},{2,10},{3,11},{4,12},{5,13},{6,14},{7,15},{8,0},{9,1},... | collective-permute-start | bytes 1216520 | tf_op jit(solution)/shard_map/ppermute | solution.py:703
  300.1 21.0 %collective-permute-start.40 = (bf16[96,2432]{1,0:T(8,128)(2,1)S(1)}, bf16[96,2432]{1,0:T(8,128)(2,1)S(1)}, u32[]{:S(2)}, u32[]{:S(2)}) collective-permute-start(bf16[96,2432]{1,0:T(8,128)(2,1)S(1)} %get-tuple-element.141), channel_id=1, source_target_pairs={{0,4},{1,5},{2,6},{3,7},{4,0},{5,1},{6,2},{7,3},{8,12},{9,13},{10,... | collective-permute-start | bytes 1400840 | tf_op jit(solution)/shard_map/ppermute | solution.py:703
  321.1 11.4 %collective-permute-start.41 = (bf16[48,2432]{1,0:T(8,128)(2,1)S(1)}, bf16[48,2432]{1,0:T(8,128)(2,1)S(1)}, u32[]{:S(2)}, u32[]{:S(2)}) collective-permute-start(bf16[48,2432]{1,0:T(8,128)(2,1)S(1)} %add_convert_fusion.2), channel_id=1, source_target_pairs={{0,8},{1,9},{2,10},{3,11},{4,12},{5,13},{6,14},{7,15},{8,0},{9,1},... | collective-permute-start | bytes 700424 | tf_op jit(solution)/shard_map/ppermute | solution.py:703
  (49 other events, 533.2 us)
Sparse Core Ops, SparseCore 0:
  23.4 75.1 all-gather.1

commit v11 on v10

--- a/solution.py
+++ b/solution.py
@@ -480,10 +480,10 @@
 
 
 def local_back_middle_body(*refs):
-    sources, refs = refs[:-12], refs[-12:]
+    sources, refs = refs[:-14], refs[-14:]
     lower_ref, low_ref, high_ref, middle_ref, gate_up_ref, gain_ref, other_ref = refs[:7]
-    gain_out_ref, d_middle_ref, d_att_ref, right_ref = refs[7:11]
-    weights = Weights(sources, refs[11])
+    gain_out_ref, d_middle_ref, d_att_ref, right_ref, right_low_ref, right_high_ref = refs[7:13]
+    weights = Weights(sources, refs[13])
     half = gate_up_ref.shape[1] // 2
     upstream = joined([low_ref, high_ref])
     d_gate_up, gain_grad, d_middle, d_attn, d_attended = mlp_backward(
@@ -502,6 +502,8 @@
     @pl.when(lower_ref[0] == 0)
     def _():
         right_ref[...] = other_ref[...]
+
+    store_chunks((right_low_ref, right_high_ref), right_ref[...])
 
 
 def global_project_body(first_ref, low_ref, high_ref, gain_ref, table_ref, normed_ref, sent_ref):
@@ -767,13 +769,21 @@
     send[half + base : half + base + rows, columns] = result[3 * rows :].astype(BF)
 
 
+def four_parts(refs, columns, tokens):
+    own, other, across = refs[0], refs[1], refs[2:]
+    size = own.shape[0]
+    got = [across[0][:tokens, columns]] if len(across) == 1 else [ref[:, columns] for ref in across]
+    parts = [own[:tokens, columns], other[:tokens, columns], *got]
+    return jnp.concatenate(parts + [other[size : size + tokens, columns]], 0)
+
+
 def early_body(terms, split, *refs):
     refs, outs = refs[:-3], refs[-3:]
     operands, lefts = (refs[:split], refs[split:-4]), refs[-4:]
     width = outs[0].shape[1]
     base = 0
     for which, rows, (start, end) in terms:
-        right = jnp.concatenate([ref[:, start:end] for ref in operands[which]], 0)
+        right = four_parts(operands[which], slice(start, end), lefts[0].shape[2])
         result = dot(left_rows_of(lefts, rows), right)
         for column in range(0, end - start, width):
             by_plane(result[:, column : column + width], base, outs)
@@ -787,9 +797,12 @@
     width = columns // 3
     size = outs[0].shape[0]
     tokens = lefts[0].shape[2]
-    right = jnp.concatenate([ref[:tokens] for ref in rights], 0)
+    right = four_parts(rights, slice(None), tokens)
     by_plane(dot(left_rows_of(lefts, rows), right), 0, outs, slice(0, columns))
-    tail = sum(ref[tokens:, :width].astype(F32) for ref in rights)
+    own, other, across = rights
+    ends = [ref[tokens : tokens + EXTRA, :width] for ref in rights]
+    ends.append(other[own.shape[0] + tokens :, :width])
+    tail = sum(part.astype(F32) for part in ends)
     both = jnp.concatenate([tail, jnp.zeros((LANES - EXTRA, width), F32)], 0).T
     lane = lax.broadcasted_iota(jnp.int32, (1, LANES), 1)
     lows = pltpu.roll(both, LANES - 1, 1)
@@ -803,6 +816,10 @@
 
 def three_parts(shape):
     return [(shape, F32), (shape, F32), ((2 * shape[0], shape[1]), BF)]
+
+
+def with_core(rows, across, count):
+    return [rows, partner(jnp.concatenate([rows, *across]), 1, count), *across]
 
 
 def first_hop(blocks, count):
@@ -1044,24 +1061,27 @@
         [jnp.where(lower, a, up_1[i * row_count :][:row_count]) for i, a in enumerate(up_0)]
     )
     across_mlp = partner(d_mlp, 2, count)
-    gain_mlp_0, d_mid_0, d_att_0, right = on_core(
+    gain_mlp_0, d_mid_0, d_att_0, right, *right_chunks = on_core(
         local_back_middle_body,
         [
             ((1, width), F32),
             ((rows, width), F32),
             ((rows, width), BF),
             ((rows, inner + width), BF),
-        ],
+        ]
+        + [((row_count, inner + width), BF)] * micro_count,
         (*others, lower_flag, *up_0, middle_0, gate_up_0, gain_mlp, right_1),
         [pltpu.VMEM((hidden, width), BF)],
         [pltpu.VMEM] * len(others) + [pltpu.SMEM] + [pltpu.VMEM] * 6,
     )
-    d_att_0, right, across_mlp = lax.optimization_barrier((d_att_0, right, across_mlp))
-    across = [partner(right, 2, count)]
-    d_mlp = [d_mlp, partner(d_mlp, 1, count), across_mlp, partner(across_mlp, 1, count)]
+    d_att_0, right_chunks, across_mlp = lax.optimization_barrier(
+        (d_att_0, right_chunks, across_mlp)
+    )
+    across = [partner(item, 2, count) for item in right_chunks]
+    d_mlp = with_core(d_mlp, [across_mlp], count)
     out_near, out_far = first_hop(
         on_core(
-            functools.partial(early_body, [(0, (3 * shard_total, left_total), (0, width))], 4),
+            functools.partial(early_body, [(0, (3 * shard_total, left_total), (0, width))], 3),
             three_parts((hidden_total, width)),
             (*d_mlp, *left),
         ),
@@ -1079,7 +1099,21 @@
     )
     from_after = lax.ppermute(d_before, "dp", down_pairs)
     from_before = lax.ppermute(d_after, "dp", up_pairs)
-    from_after, out_far = lax.optimization_barrier((from_after, out_far))
+    across, right, _ = lax.optimization_barrier((across, right, d_own))
+    right = with_core(right, across, count)
+    in_rows, attn_rows = shard_total * (inner // width), shard_total
+    early_rows = in_rows + attn_rows
+    terms = [
+        (0, (2 * shard_total, 3 * shard_total), (0, inner)),
+        (0, (shard_total, 2 * shard_total), (inner, inner + width)),
+    ]
+    early = on_core(
+        functools.partial(early_body, terms, len(right)),
+        three_parts((early_rows, width)),
+        (*right, *left),
+    )
+    from_after, _ = lax.optimization_barrier((from_after, early[0]))
+    near, far = first_hop(early, count)
     d_proj, grad_0, gain_attn_sum = on_core(
         local_finish_body,
         [
@@ -1095,28 +1129,10 @@
         [pltpu.SMEM] + [pltpu.VMEM] * 13,
     )
     across_chunks = [partner(d_proj, 2, count)]
-    across, right, _ = lax.optimization_barrier((across, right, d_proj))
-    right = [right, partner(right, 1, count)] + across
-    right += [partner(item, 1, count) for item in across]
-    in_rows, attn_rows = shard_total * (inner // width), shard_total
-    early_rows = in_rows + attn_rows
-    terms = [
-        (0, (2 * shard_total, 3 * shard_total), (0, inner)),
-        (0, (shard_total, 2 * shard_total), (inner, inner + width)),
-    ]
-    near, far = first_hop(
-        on_core(
-            functools.partial(early_body, terms, len(right)),
-            three_parts((early_rows, width)),
-            (*right, *left),
-        ),
-        count,
-    )
     far = jnp.concatenate([far, out_far])
     across_chunks, d_proj, _ = lax.optimization_barrier((across_chunks, d_proj, far))
     far = partner(far, 8, count)
-    right = [d_proj, partner(d_proj, 1, count)] + across_chunks
-    right += [partner(item, 1, count) for item in across_chunks]
+    right = with_core(d_proj, across_chunks, count)
     late_in = (group_pos[None], *right, *left)
     late = on_core(
         functools.partial(late_body, (0, shard_total)),

time: 342 us -> 344 us (level)
  waiting for transfers between devices: 130 us -> 134 us
    ppermute x35 -> x33, waiting for transfers between devices: 88.1 us -> 93.3 us  [partner(): return lax.ppermute(rows, 'dp', [(i, i ^ apart) for i in range(count)])]
    ppermute x35 -> x33, starting transfers between devices: 32.5 us -> 29.9 us  [partner(): return lax.ppermute(rows, 'dp', [(i, i ^ apart) for i in range(count)])]
  transfers between devices with their start and end apart: 46 -> 44, of which waited for: 26 -> 22; matrix products, arithmetic and copies ran while one was open for 6% -> 6% of each run, Pallas kernels for 7% -> 7%
where the time goes in v11:
time: 344 us; the launch traced here: 343 us
  waiting for transfers between devices  134 us (39%)
  Pallas kernels  56.7 us (16%)
  starting transfers between devices  53.9 us (16%)
  local copies, waits for them, and re-layouts  44.8 us (13%)
  blocking collectives  32.9 us (10%)
  between operations  14.9 us (4%)
  other arithmetic  5.33 us (2%)
    ppermute x33, waiting for transfers between devices, partner(): return lax.ppermute(rows, 'dp', [(i, i ^ apart) for i in range(count)])  93.3 us
    pallas_call x17, Pallas kernels, on_core(): pl.pallas_call(body, out_shape=[jax.ShapeDtypeStruct(shape, dtype) for sh...  56.7 us
    all_to_all x2, blocking collectives, exchange(): return lax.all_to_all(blocks, 'dp', 0, 0, axis_index_groups=groups)  32.9 us
    ppermute x33, starting transfers between devices, partner(): return lax.ppermute(rows, 'dp', [(i, i ^ apart) for i in range(count)])  29.9 us
    all_gather x1, waiting for transfers between devices, on_device(): others = [lax.all_gather(stacked, 'dp', axis=0, tiled=True)]  28.3 us
    unnamed x102, local copies, waits for them, and re-layouts  26.1 us
    dynamic_update_slice x16, local copies, waits for them, and re-layouts, gather_rows(): whole = lax.dynamic_update_slice(whole, item[None], start)  11.4 us
    ppermute x4, waiting for transfers between devices, to_other_section(): return [lax.ppermute(rows, 'section', pairs) for rows in chunks]  9.38 us
  transfers between devices with their start and end apart: 44, of which 22 were waited for; matrix products, arithmetic and copies ran while one was open for 6% of the time, Pallas kernels for 7%

profile of v11, /device:TPU:0, one launch (start us, length us, event | category | flops | bytes accessed | tf_op | source)
XLA Modules:
  0.0 342.6 jit_solution(15507057116433438882)
XLA Ops:
  10.3 3.0 collective-permute-start.1
  13.3 1.6 collective-permute-start.2
  14.9 2.6 collective-permute-start.3
  23.5 2.1 broadcast_in_dim.105
  27.6 6.8 %collective-permute-done.3 = bf16[48,2432]{1,0:T(8,128)(2,1)S(1)} collective-permute-done((bf16[48,2432]{1,0:T(8,128)(2,1)S(1)}, bf16[48,2432]{1,0:T(8,128)(2,1)S(1)}, u32[]{:S(2)}, u32[]{:S(2)}) %collective-permute-start.3) | collective-permute-done | bytes 233504 | tf_op jit(solution)/shard_map/ppermute | solution.py:705
  34.9 1.5 collective-permute-start.7
  40.0 5.6 %collective-permute-done.6 = bf16[48,2432]{1,0:T(8,128)(2,1)S(1)} collective-permute-done((bf16[48,2432]{1,0:T(8,128)(2,1)S(1)}, bf16[48,2432]{1,0:T(8,128)(2,1)S(1)}, u32[]{:S(2)}, u32[]{:S(2)}) %collective-permute-start.6) | collective-permute-done | bytes 233504 | tf_op jit(solution)/shard_map/ppermute | solution.py:705
  46.3 3.2 collective-permute-done.7
  57.0 3.1 shard_map.154
  60.8 2.1 collective-permute-start.16
  64.9 1.8 collective-permute-done.17.after_ref
  66.7 3.6 %shard_map.155 = (bf16[128,768]{1,0:T(8,128)(2,1)S(1)}, f32[12,1,128]{2,1,0:T(1,128)S(1)}) custom-call(bf16[128,768]{1,0:T(8,128)(2,1)S(1)} %get-tuple-element.81.q_ref, bf16[128,1536]{1,0:T(8,128)(2,1)S(1)} %collective-permute-done.16.before_ref, bf16[128,1536]{1,0:T(8,128)(2,1)S(1)} %get-tuple-element.82.own_ref, ...), custom_call_target="tpu_custom_call" | custom-call | flops 1024 | bytes 1024 | tf_op jit(solution)/shard_map/pallas_call | solution.py:65
  70.3 28.3 %all-gather.2.cloned.1.call-done.refs_0_ = bf16[768,4352]{1,0:T(8,128)(2,1)} async-done(((bf16[48,4352]{1,0:T(8,128)(2,1)}), bf16[768,4352]{1,0:T(8,128)(2,1)}) %all-gather.2.cloned.1.call-update) | async-done | bytes 6684688 | tf_op jit(solution)/shard_map/all_gather | solution.py:891
  98.6 4.4 %shard_map.156 = (bf16[128,768]{1,0:T(8,128)(2,1)S(1)}, bf16[128,1152]{1,0:T(8,128)(2,1)S(1)}, f32[128,768]{1,0:T(8,128)S(1)}, f32[128,2304]{1,0:T(8,128)S(1)}, ...) custom-call(bf16[768,4352]{1,0:T(8,128)(2,1)} %all-gather.2.cloned.1.call-done.refs_0_, ...), custom_call_target="tpu_custom_call" | custom-call | flops 1024 | bytes 1024 | tf_op jit(solution)/shard_map/pallas_call | solution.py:65
  105.6 3.4 collective-permute-start.18
  108.9 1.3 collective-permute-start.19
  110.6 1.4 collective-permute-done.18.low_ref.refs_2_
  112.0 1.4 collective-permute-done.19.high_ref.refs_3_
  113.5 3.1 shard_map.157
  116.6 21.2 %all_to_all.20.got_ref = bf16[16,144,128]{2,1,0:T(8,128)(2,1)S(1)} all-to-all(bf16[16,144,128]{2,1,0:T(8,128)(2,1)S(1)} %get-tuple-element.87), channel_id=1, replica_groups={{0,1,2,3,4,5,6,7,8,9,10,11,12,13,14,15},{16,17,18,19,20,21,22,23,24,25,..., dimensions={0} | all-to-all | bytes 1179648 | tf_op jit(solution)/shard_map/all_to_all | solution.py:696
  139.5 6.0 %shard_map.158 = (bf16[16,48,128]{2,1,0:T(8,128)(2,1)S(1)}, f32[6,1,256]{2,1,0:T(1,128)S(1)}) custom-call(bf16[16,144,128]{2,1,0:T(8,128)(2,1)S(1)} %all_to_all.20.got_ref, bf16[16,64,128]{2,1,0:T(8,128)(2,1)S(1)} %collective-permute-done.20.other_ref, s32[1024,1]{1,0:T(8,128)S(1)} %copy.19.own_seg_ref, s32[1024,1]{1,0:T(8,128)S(1)} %copy.20.shared_seg_ref), custom_call_target="tpu_custom_call" | custom-call | flops 1024 | bytes 1024 | tf_op jit(solution)/shard_map/pallas_call | solution.py:65
  145.5 11.8 %all_to_all.21.refs_1_ = bf16[16,48,128]{2,1,0:T(8,128)(2,1)S(1)} all-to-all(bf16[16,48,128]{2,1,0:T(8,128)(2,1)S(1)} %get-tuple-element.88), channel_id=1, replica_groups={{0,1,2,3,4,5,6,7,8,9,10,11,12,13,14,15},{16,17,18,19,20,21,22,23,24,25,..., dimensions={0} | all-to-all | bytes 393216 | tf_op jit(solution)/shard_map/all_to_all | solution.py:696
  157.3 7.7 %shard_map.159 = (bf16[128,768]{1,0:T(8,128)(2,1)S(1)}, bf16[128,768]{1,0:T(8,128)(2,1)S(1)}, bf16[128,768]{1,0:T(8,128)(2,1)S(1)}, bf16[128,1152]{1,0:T(8,128)(...) custom-call(bf16[768,4352]{1,0:T(8,128)(2,1)} %all-gather.2.cloned.1, ...), custom_call_target="tpu_custom_call" | custom-call | flops 1024 | bytes 1024 | tf_op jit(solution)/shard_map/pallas_call | solution.py:65
  169.4 4.2 %all-to-all-start.2 = ((bf16[16,48,128]{2,1,0:T(8,128)(2,1)}), bf16[16,48,128]{2,1,0:T(8,128)(2,1)}, u32[]{:S(2)}, u32[]{:S(2)}) async-start(bf16[16,48,128]{2,1,0:T(8,128)(2,1)} %get-tuple-element.98), calls=%async_computation.2 | async-start | bytes 393216 | tf_op jit(solution)/shard_map/all_to_all | solution.py:696
  183.5 8.2 %shard_map.161 = (bf16[16,144,128]{2,1,0:T(8,128)(2,1)S(1)}, bf16[16,64,128]{2,1,0:T(8,128)(2,1)S(1)}) custom-call(bf16[16,144,128]{2,1,0:T(8,128)(2,1)S(1)} %all_to_all.20.got_ref, bf16[16,64,128]{2,1,0:T(8,128)(2,1)S(1)} %copy-done.10, s32[1024,1]{1,0:T(8,128)S(1)} %copy.19.own_seg_ref, s32[1024,1]{1,0:T(8,128)S(1)} %copy.20.shared_seg_ref, ...), custom_call_target="tpu_custom_call" | custom-call | flops 1024 | bytes 1024 | tf_op jit(solution)/shard_map/pallas_call | solution.py:65
  192.0 1.4 collective-permute-done.21
  194.4 4.8 %all-to-all-start.3 = ((bf16[16,144,128]{2,1,0:T(8,128)(2,1)}), bf16[16,144,128]{2,1,0:T(8,128)(2,1)S(1)}, u32[]{:S(2)}, u32[]{:S(2)}) async-start(bf16[16,144,128]{2,1,0:T(8,128)(2,1)} %add_convert_fusion), calls=%async_computation.3 | async-start | bytes 1179648 | tf_op jit(solution)/shard_map/all_to_all | solution.py:696
  199.8 1.7 collective-permute-start.23
  201.5 10.9 %collective-permute-done.23.refs_6_.refs_5_ = bf16[4,216,128]{2,1,0:T(8,128)(2,1)S(1)} collective-permute-done((bf16[4,216,128]{2,1,0:T(8,128)(2,1)S(1)}, bf16[4,216,128]{2,1,0:T(8,128)(2,1)S(1)}, u32[]{:S(2)}, u32[]{:S(2)}) %collective-permute-start.23) | collective-permute-done | bytes 221216 | tf_op jit(solution)/shard_map/ppermute | solution.py:705
  212.4 5.3 %collective-permute-done.24.refs_7_.refs_6_ = bf16[4,216,128]{2,1,0:T(8,128)(2,1)S(1)} collective-permute-done((bf16[4,216,128]{2,1,0:T(8,128)(2,1)S(1)}, bf16[4,216,128]{2,1,0:T(8,128)(2,1)S(1)}, u32[]{:S(2)}, u32[]{:S(2)}) %collective-permute-start.24) | collective-permute-done | bytes 221216 | tf_op jit(solution)/shard_map/ppermute | solution.py:705
  218.7 3.6 %shard_map.162 = (bf16[128,2304]{1,0:T(8,128)(2,1)S(1)}, f32[1,768]{1,0:T(1,128)S(1)}, bf16[64,768]{1,0:T(8,128)(2,1)S(1)}, bf16[64,768]{1,0:T(8,128)(2,1)S(1)}) custom-call(bf16[768,2432]{1,0:T(8,128)(2,1)} %bitcast.23.first_ref, bf16[16,144,128]{2,1,0:T(8,128)(2,1)S(1)} %all-to-all-done.3.got_ref, f32[128,768]{1,0:T(8,128)S(1)} %copy-done.22, ...), custom_call_target="tpu_custom_call" | custom-call | flops 1024 | bytes 1024 | tf_op jit(solution)/shard_map/pallas_call | solution.py:65
  224.9 4.9 %collective-permute-done.25.refs_2_ = bf16[64,768]{1,0:T(8,128)(2,1)S(1)} collective-permute-done((bf16[64,768]{1,0:T(8,128)(2,1)S(1)}, bf16[64,768]{1,0:T(8,128)(2,1)S(1)}, u32[]{:S(2)}, u32[]{:S(2)}) %collective-permute-start.25) | collective-permute-done | bytes 98336 | tf_op jit(solution)/shard_map/ppermute | solution.py:701
  229.8 1.6 collective-permute-done.26.refs_3_
  235.3 6.2 %shard_map.163 = (f32[1,768]{1,0:T(1,128)S(1)}, f32[128,768]{1,0:T(8,128)S(1)}, bf16[128,768]{1,0:T(8,128)(2,1)S(1)}, bf16[128,3072]{1,0:T(8,128)(2,1)S(1)}, bf1...) custom-call(bf16[768,4352]{1,0:T(8,128)(2,1)} %all-gather.2.cloned.1.call-done.refs_0_, ...), custom_call_target="tpu_custom_call" | custom-call | flops 1024 | bytes 1024 | tf_op jit(solution)/shard_map/pallas_call | solution.py:65
  241.5 1.7 collective-permute-start.29
  243.6 3.5 %shard_map.164 = (bf16[128,768]{1,0:T(8,128)(2,1)S(1)}, f32[128,1536]{1,0:T(8,128)S(1)}, bf16[128,1536]{1,0:T(8,128)(2,1)S(1)}, bf16[128,1536]{1,0:T(8,128)(2,1)S(1)}) custom-call(bf16[128,768]{1,0:T(8,128)(2,1)S(1)} %copy-done.14, bf16[128,1536]{1,0:T(8,128)(2,1)S(1)} %copy-done.4, bf16[128,1536]{1,0:T(8,128)(2,1)S(1)} %copy-done.2, ...), custom_call_target="tpu_custom_call" | custom-call | flops 1024 | bytes 1024 | tf_op jit(solution)/shard_map/pallas_call | solution.py:65
  247.1 6.5 %collective-permute-done.29.refs_2_ = bf16[64,3072]{1,0:T(8,128)(2,1)S(1)} collective-permute-done((bf16[64,3072]{1,0:T(8,128)(2,1)S(1)}, bf16[64,3072]{1,0:T(8,128)(2,1)S(1)}, u32[]{:S(2)}, u32[]{:S(2)}) %collective-permute-start.29) | collective-permute-done | bytes 393248 | tf_op jit(solution)/shard_map/ppermute | solution.py:705
  253.6 6.7 %collective-permute-done.30.refs_3_ = bf16[64,3072]{1,0:T(8,128)(2,1)S(1)} collective-permute-done((bf16[64,3072]{1,0:T(8,128)(2,1)S(1)}, bf16[64,3072]{1,0:T(8,128)(2,1)S(1)}, u32[]{:S(2)}, u32[]{:S(2)}) %collective-permute-start.30) | collective-permute-done | bytes 393248 | tf_op jit(solution)/shard_map/ppermute | solution.py:705
  262.3 3.1 collective-permute-start.32
  266.2 2.4 collective-permute-start.34
  269.1 4.0 %shard_map.166 = (bf16[144,2304]{1,0:T(8,128)(2,1)S(1)}, bf16[128,768]{1,0:T(8,128)(2,1)S(1)}, f32[1,768]{1,0:T(1,128)}) custom-call(s32[1]{0:T(128)} %bitcast.37.lower_ref.refs_1_, bf16[768,2432]{1,0:T(8,128)(2,1)} %bitcast.23.first_ref, bf16[128,768]{1,0:T(8,128)(2,1)S(1)} %get-tuple-element.117.dq_ref, f32[128,1536]{1,0:T(8,128)S(1)} %get-tuple-element.118.own_ref, ...), custom_call_target="tpu_custom_call" | custom-call | flops 1024 | bytes 1024 | tf_op jit(solution)/shard_map/pallas_call | solution.py:65
  273.1 8.1 %collective-permute-start.33 = (bf16[144,2304]{1,0:T(8,128)(2,1)S(1)}, bf16[144,2304]{1,0:T(8,128)(2,1)S(1)}, u32[]{:S(2)}, u32[]{:S(2)}) collective-permute-start(bf16[144,2304]{1,0:T(8,128)(2,1)S(1)} %get-tuple-element.145.refs_0_), channel_id=1, source_target_pairs={{0,2},{1,3},{2,0},{3,1},{4,6},{5,7},{6,4},{7,5},{8,10},{9,11},{10,... | collective-permute-start | bytes 1990664 | tf_op jit(solution)/shard_map/ppermute | solution.py:705
  281.2 7.8 %collective-permute-done.36 = bf16[144,768]{1,0:T(8,128)(2,1)S(1)} collective-permute-done((bf16[144,768]{1,0:T(8,128)(2,1)S(1)}, bf16[144,768]{1,0:T(8,128)(2,1)S(1)}, u32[]{:S(2)}, u32[]{:S(2)}) %collective-permute-start.36) | collective-permute-done | bytes 221216 | tf_op jit(solution)/shard_map/ppermute | solution.py:705
  289.1 7.3 %collective-permute-done.33.refs_2_ = bf16[144,2304]{1,0:T(8,128)(2,1)S(1)} collective-permute-done((bf16[144,2304]{1,0:T(8,128)(2,1)S(1)}, bf16[144,2304]{1,0:T(8,128)(2,1)S(1)}, u32[]{:S(2)}, u32[]{:S(2)}) %collective-permute-start.33) | collective-permute-done | bytes 663584 | tf_op jit(solution)/shard_map/ppermute | solution.py:705
  296.5 2.3 collective-permute-start.40
  301.1 16.9 %collective-permute-done.40 = bf16[264,768]{1,0:T(8,128)(2,1)S(1)} collective-permute-done((bf16[264,768]{1,0:T(8,128)(2,1)S(1)}, bf16[264,768]{1,0:T(8,128)(2,1)S(1)}, u32[]{:S(2)}, u32[]{:S(2)}) %collective-permute-start.40) | collective-permute-done | bytes 405536 | tf_op jit(solution)/shard_map/ppermute | solution.py:705
  319.6 2.6 collective-permute-done.38
  323.1 11.1 %collective-permute-done.39 = bf16[48,2432]{1,0:T(8,128)(2,1)S(1)} collective-permute-done((bf16[48,2432]{1,0:T(8,128)(2,1)S(1)}, bf16[48,2432]{1,0:T(8,128)(2,1)S(1)}, u32[]{:S(2)}, u32[]{:S(2)}) %collective-permute-start.39) | collective-permute-done | bytes 233504 | tf_op jit(solution)/shard_map/ppermute | solution.py:705
  (243 shorter events, 64.0 us)
Async XLA Ops:
  7.2 91.4 %all-gather.2.cloned.1.call-start = ((), (), s32[]{:S(2)}) async-start(), calls=%async_computation.4 | async-start | bytes 7102464 | tf_op jit(solution)/shard_map/all_gather | solution.py:891
  10.3 13.0 %collective-permute-start.1 = (bf16[48,2432]{1,0:T(8,128)(2,1)S(1)}, bf16[48,2432]{1,0:T(8,128)(2,1)S(1)}, u32[]{:S(2)}, u32[]{:S(2)}) collective-permute-start(bf16[48,2432]{1,0:T(8,128)(2,1)S(1)} %shard_map.153), channel_id=1, source_target_pairs={{0,2},{1,3},{2,0},{3,1},{4,6},{5,7},{6,4},{7,5},{8,10},{9,11},{10,... | collective-permute-start | bytes 700424 | tf_op jit(solution)/shard_map/ppermute | solution.py:705
  13.3 13.9 %collective-permute-start.2 = (bf16[48,2432]{1,0:T(8,128)(2,1)S(1)}, bf16[48,2432]{1,0:T(8,128)(2,1)S(1)}, u32[]{:S(2)}, u32[]{:S(2)}) collective-permute-start(bf16[48,2432]{1,0:T(8,128)(2,1)S(1)} %shard_map.153), channel_id=1, source_target_pairs={{0,4},{1,5},{2,6},{3,7},{4,0},{5,1},{6,2},{7,3},{8,12},{9,13},{10,... | collective-permute-start | bytes 700424 | tf_op jit(solution)/shard_map/ppermute | solution.py:705
  14.9 19.5 %collective-permute-start.3 = (bf16[48,2432]{1,0:T(8,128)(2,1)S(1)}, bf16[48,2432]{1,0:T(8,128)(2,1)S(1)}, u32[]{:S(2)}, u32[]{:S(2)}) collective-permute-start(bf16[48,2432]{1,0:T(8,128)(2,1)S(1)} %shard_map.153), channel_id=1, source_target_pairs={{0,8},{1,9},{2,10},{3,11},{4,12},{5,13},{6,14},{7,15},{8,0},{9,1},... | collective-permute-start | bytes 700424 | tf_op jit(solution)/shard_map/ppermute | solution.py:705
  17.5 17.5 %collective-permute-start.4 = (bf16[48,2432]{1,0:T(8,128)(2,1)S(1)}, bf16[48,2432]{1,0:T(8,128)(2,1)S(1)}, u32[]{:S(2)}, u32[]{:S(2)}) collective-permute-start(bf16[48,2432]{1,0:T(8,128)(2,1)S(1)} %shard_map.153), channel_id=1, source_target_pairs={{0,12},{1,13},{2,14},{3,15},{4,8},{5,9},{6,10},{7,11},{8,4},{9,5},... | collective-permute-start | bytes 700424 | tf_op jit(solution)/shard_map/ppermute | solution.py:705
  18.4 1.2 collective-permute-start
  19.6 30.6 %collective-permute-start.8 = (bf16[48,2432]{1,0:T(8,128)(2,1)S(1)}, bf16[48,2432]{1,0:T(8,128)(2,1)S(1)}, u32[]{:S(2)}, u32[]{:S(2)}) collective-permute-start(bf16[48,2432]{1,0:T(8,128)(2,1)S(1)} %shard_map.153), channel_id=1, source_target_pairs={{0,1},{1,0},{2,3},{3,2},{4,5},{5,4},{6,7},{7,6},{8,9},{9,8},{10,11... | collective-permute-start | bytes 700424 | tf_op jit(solution)/shard_map/ppermute | solution.py:705
  26.8 24.6 %collective-permute-start.9 = (bf16[48,2432]{1,0:T(8,128)(2,1)S(1)}, bf16[48,2432]{1,0:T(8,128)(2,1)S(1)}, u32[]{:S(2)}, u32[]{:S(2)}) collective-permute-start(bf16[48,2432]{1,0:T(8,128)(2,1)S(1)} %collective-permute-done.1), channel_id=1, source_target_pairs={{0,1},{1,0},{2,3},{3,2},{4,5},{5,4},{6,7},{7,6},{8,9},{9,8},{10,11... | collective-permute-start | bytes 700424 | tf_op jit(solution)/shard_map/ppermute | solution.py:705
  27.2 12.1 %collective-permute-start.5 = (bf16[48,2432]{1,0:T(8,128)(2,1)S(1)}, bf16[48,2432]{1,0:T(8,128)(2,1)S(1)}, u32[]{:S(2)}, u32[]{:S(2)}) collective-permute-start(bf16[48,2432]{1,0:T(8,128)(2,1)S(1)} %collective-permute-done.2), channel_id=1, source_target_pairs={{0,2},{1,3},{2,0},{3,1},{4,6},{5,7},{6,4},{7,5},{8,10},{9,11},{10,... | collective-permute-start | bytes 700424 | tf_op jit(solution)/shard_map/ppermute | solution.py:705
  34.4 11.2 %collective-permute-start.6 = (bf16[48,2432]{1,0:T(8,128)(2,1)S(1)}, bf16[48,2432]{1,0:T(8,128)(2,1)S(1)}, u32[]{:S(2)}, u32[]{:S(2)}) collective-permute-start(bf16[48,2432]{1,0:T(8,128)(2,1)S(1)} %collective-permute-done.3), channel_id=1, source_target_pairs={{0,2},{1,3},{2,0},{3,1},{4,6},{5,7},{6,4},{7,5},{8,10},{9,11},{10,... | collective-permute-start | bytes 700424 | tf_op jit(solution)/shard_map/ppermute | solution.py:705
  34.9 14.6 %collective-permute-start.7 = (bf16[48,2432]{1,0:T(8,128)(2,1)S(1)}, bf16[48,2432]{1,0:T(8,128)(2,1)S(1)}, u32[]{:S(2)}, u32[]{:S(2)}) collective-permute-start(bf16[48,2432]{1,0:T(8,128)(2,1)S(1)} %collective-permute-done.4), channel_id=1, source_target_pairs={{0,2},{1,3},{2,0},{3,1},{4,6},{5,7},{6,4},{7,5},{8,10},{9,11},{10,... | collective-permute-start | bytes 700424 | tf_op jit(solution)/shard_map/ppermute | solution.py:705
  39.3 12.9 %collective-permute-start.10 = (bf16[48,2432]{1,0:T(8,128)(2,1)S(1)}, bf16[48,2432]{1,0:T(8,128)(2,1)S(1)}, u32[]{:S(2)}, u32[]{:S(2)}) collective-permute-start(bf16[48,2432]{1,0:T(8,128)(2,1)S(1)} %collective-permute-done.2), channel_id=1, source_target_pairs={{0,1},{1,0},{2,3},{3,2},{4,5},{5,4},{6,7},{7,6},{8,9},{9,8},{10,11... | collective-permute-start | bytes 700424 | tf_op jit(solution)/shard_map/ppermute | solution.py:705
  45.6 8.5 %collective-permute-start.12 = (bf16[48,2432]{1,0:T(8,128)(2,1)S(1)}, bf16[48,2432]{1,0:T(8,128)(2,1)S(1)}, u32[]{:S(2)}, u32[]{:S(2)}) collective-permute-start(bf16[48,2432]{1,0:T(8,128)(2,1)S(1)} %collective-permute-done.3), channel_id=1, source_target_pairs={{0,1},{1,0},{2,3},{3,2},{4,5},{5,4},{6,7},{7,6},{8,9},{9,8},{10,11... | collective-permute-start | bytes 700424 | tf_op jit(solution)/shard_map/ppermute | solution.py:705
  49.5 6.0 %collective-permute-start.14 = (bf16[48,2432]{1,0:T(8,128)(2,1)S(1)}, bf16[48,2432]{1,0:T(8,128)(2,1)S(1)}, u32[]{:S(2)}, u32[]{:S(2)}) collective-permute-start(bf16[48,2432]{1,0:T(8,128)(2,1)S(1)} %collective-permute-done.4), channel_id=1, source_target_pairs={{0,1},{1,0},{2,3},{3,2},{4,5},{5,4},{6,7},{7,6},{8,9},{9,8},{10,11... | collective-permute-start | bytes 700424 | tf_op jit(solution)/shard_map/ppermute | solution.py:705
  50.2 3.2 collective-permute-start.11
  51.4 3.4 collective-permute-start.13
  52.2 4.0 %collective-permute-start.15 = (bf16[48,2432]{1,0:T(8,128)(2,1)S(1)}, bf16[48,2432]{1,0:T(8,128)(2,1)S(1)}, u32[]{:S(2)}, u32[]{:S(2)}) collective-permute-start(bf16[48,2432]{1,0:T(8,128)(2,1)S(1)} %collective-permute-done.7), channel_id=1, source_target_pairs={{0,1},{1,0},{2,3},{3,2},{4,5},{5,4},{6,7},{7,6},{8,9},{9,8},{10,11... | collective-permute-start | bytes 700424 | tf_op jit(solution)/shard_map/ppermute | solution.py:705
  60.7 42.2 %copy-start.1 = (bf16[128,1536]{1,0:T(8,128)(2,1)}, bf16[128,1536]{1,0:T(8,128)(2,1)S(1)}, u32[]{:S(2)}) copy-start(bf16[128,1536]{1,0:T(8,128)(2,1)S(1)} %get-tuple-element.82.own_ref) | copy-start | bytes 1179652
  60.8 42.2 %copy-start.13 = (bf16[128,768]{1,0:T(8,128)(2,1)}, bf16[128,768]{1,0:T(8,128)(2,1)S(1)}, u32[]{:S(2)}) copy-start(bf16[128,768]{1,0:T(8,128)(2,1)S(1)} %get-tuple-element.81.q_ref) | copy-start | bytes 589828
  60.8 4.1 %collective-permute-start.16 = (bf16[128,1536]{1,0:T(8,128)(2,1)S(1)}, bf16[128,1536]{1,0:T(8,128)(2,1)S(1)}, u32[]{:S(2)}, u32[]{:S(2)}) collective-permute-start(bf16[128,1536]{1,0:T(8,128)(2,1)S(1)} %get-tuple-element.82.own_ref), channel_id=1, source_target_pairs={{0,1},{1,2},{2,3},{3,4},{4,5},{5,6},{6,7},{7,8},{8,9},{9,10},{10,1... | collective-permute-start | bytes 1179656 | tf_op jit(solution)/shard_map/ppermute | solution.py:938
  62.9 3.8 %collective-permute-start.17 = (bf16[128,1536]{1,0:T(8,128)(2,1)S(1)}, bf16[128,1536]{1,0:T(8,128)(2,1)S(1)}, u32[]{:S(2)}, u32[]{:S(2)}) collective-permute-start(bf16[128,1536]{1,0:T(8,128)(2,1)S(1)} %get-tuple-element.82.own_ref), channel_id=1, source_target_pairs={{1,0},{2,1},{3,2},{4,3},{5,4},{6,5},{7,6},{8,7},{9,8},{10,9},{11,1... | collective-permute-start | bytes 1179656 | tf_op jit(solution)/shard_map/ppermute | solution.py:940
  70.3 40.1 %copy-start.11 = (bf16[128,768]{1,0:T(8,128)(2,1)}, bf16[128,768]{1,0:T(8,128)(2,1)S(1)}, u32[]{:S(2)}) copy-start(bf16[128,768]{1,0:T(8,128)(2,1)S(1)} %get-tuple-element.84.refs_2_) | copy-start | bytes 589828
  105.6 6.5 %collective-permute-start.18 = (bf16[64,768]{1,0:T(8,128)(2,1)S(1)}, bf16[64,768]{1,0:T(8,128)(2,1)S(1)}, u32[]{:S(2)}, u32[]{:S(2)}) collective-permute-start(bf16[64,768]{1,0:T(8,128)(2,1)S(1)} %get-tuple-element.85), channel_id=1, source_target_pairs={{0,16},{1,17},{2,18},{3,19},{4,20},{5,21},{6,22},{7,23},{8,24},{9,... | collective-permute-start | bytes 294920 | tf_op jit(solution)/shard_map/ppermute | solution.py:701
  108.9 4.6 %collective-permute-start.19 = (bf16[64,768]{1,0:T(8,128)(2,1)S(1)}, bf16[64,768]{1,0:T(8,128)(2,1)S(1)}, u32[]{:S(2)}, u32[]{:S(2)}) collective-permute-start(bf16[64,768]{1,0:T(8,128)(2,1)S(1)} %get-tuple-element.86), channel_id=1, source_target_pairs={{0,16},{1,17},{2,18},{3,19},{4,20},{5,21},{6,22},{7,23},{8,24},{9,... | collective-permute-start | bytes 294920 | tf_op jit(solution)/shard_map/ppermute | solution.py:701
  116.6 40.7 %copy-start.15 = (bf16[2,64,768]{2,1,0:T(8,128)(2,1)S(1)}, bf16[2,64,768]{2,1,0:T(8,128)(2,1)}, u32[]{:S(2)}) copy-start(bf16[2,64,768]{2,1,0:T(8,128)(2,1)} %param.11) | copy-start | bytes 589828
  137.9 1.6 collective-permute-start.20
  169.4 13.2 %all-to-all-start.2 = ((bf16[16,48,128]{2,1,0:T(8,128)(2,1)}), bf16[16,48,128]{2,1,0:T(8,128)(2,1)}, u32[]{:S(2)}, u32[]{:S(2)}) async-start(bf16[16,48,128]{2,1,0:T(8,128)(2,1)} %get-tuple-element.98), calls=%async_computation.2 | async-start | bytes 393216 | tf_op jit(solution)/shard_map/all_to_all | solution.py:696
  191.8 1.6 collective-permute-start.21
  194.4 23.2 %all-to-all-start.3 = ((bf16[16,144,128]{2,1,0:T(8,128)(2,1)}), bf16[16,144,128]{2,1,0:T(8,128)(2,1)S(1)}, u32[]{:S(2)}, u32[]{:S(2)}) async-start(bf16[16,144,128]{2,1,0:T(8,128)(2,1)} %add_convert_fusion), calls=%async_computation.3 | async-start | bytes 1179648 | tf_op jit(solution)/shard_map/all_to_all | solution.py:696
  199.3 2.2 collective-permute-start.22
  199.8 12.6 %collective-permute-start.23 = (bf16[4,216,128]{2,1,0:T(8,128)(2,1)S(1)}, bf16[4,216,128]{2,1,0:T(8,128)(2,1)S(1)}, u32[]{:S(2)}, u32[]{:S(2)}) collective-permute-start(bf16[4,216,128]{2,1,0:T(8,128)(2,1)S(1)} %get-tuple-element.157), channel_id=1, source_target_pairs={{0,2},{1,3},{2,0},{3,1},{4,6},{5,7},{6,4},{7,5},{8,10},{9,11},{10,... | collective-permute-start | bytes 663560 | tf_op jit(solution)/shard_map/ppermute | solution.py:705
  201.5 16.2 %collective-permute-start.24 = (bf16[4,216,128]{2,1,0:T(8,128)(2,1)S(1)}, bf16[4,216,128]{2,1,0:T(8,128)(2,1)S(1)}, u32[]{:S(2)}, u32[]{:S(2)}) collective-permute-start(bf16[4,216,128]{2,1,0:T(8,128)(2,1)S(1)} %get-tuple-element.156), channel_id=1, source_target_pairs={{0,3},{1,2},{2,1},{3,0},{4,7},{5,6},{6,5},{7,4},{8,11},{9,10},{10,... | collective-permute-start | bytes 663560 | tf_op jit(solution)/shard_map/ppermute | solution.py:705
  222.3 7.5 %collective-permute-start.25 = (bf16[64,768]{1,0:T(8,128)(2,1)S(1)}, bf16[64,768]{1,0:T(8,128)(2,1)S(1)}, u32[]{:S(2)}, u32[]{:S(2)}) collective-permute-start(bf16[64,768]{1,0:T(8,128)(2,1)S(1)} %get-tuple-element.108), channel_id=1, source_target_pairs={{16,0},{17,1},{18,2},{19,3},{20,4},{21,5},{22,6},{23,7},{24,8},{25... | collective-permute-start | bytes 294920 | tf_op jit(solution)/shard_map/ppermute | solution.py:701
  223.6 7.8 %collective-permute-start.26 = (bf16[64,768]{1,0:T(8,128)(2,1)S(1)}, bf16[64,768]{1,0:T(8,128)(2,1)S(1)}, u32[]{:S(2)}, u32[]{:S(2)}) collective-permute-start(bf16[64,768]{1,0:T(8,128)(2,1)S(1)} %get-tuple-element.109), channel_id=1, source_target_pairs={{16,0},{17,1},{18,2},{19,3},{20,4},{21,5},{22,6},{23,7},{24,8},{25... | collective-permute-start | bytes 294920 | tf_op jit(solution)/shard_map/ppermute | solution.py:701
  231.5 10.0 %collective-permute-start.27 = (bf16[128,768]{1,0:T(8,128)(2,1)S(1)}, bf16[128,768]{1,0:T(8,128)(2,1)S(1)}, u32[]{:S(2)}, u32[]{:S(2)}) collective-permute-start(bf16[128,768]{1,0:T(8,128)(2,1)S(1)} %pad_maximum_fusion.5.refs_0_), channel_id=1, source_target_pairs={{0,2},{1,3},{2,0},{3,1},{4,6},{5,7},{6,4},{7,5},{8,10},{9,11},{10,... | collective-permute-start | bytes 589832 | tf_op jit(solution)/shard_map/ppermute | solution.py:705
  241.5 12.1 %collective-permute-start.29 = (bf16[64,3072]{1,0:T(8,128)(2,1)S(1)}, bf16[64,3072]{1,0:T(8,128)(2,1)S(1)}, u32[]{:S(2)}, u32[]{:S(2)}) collective-permute-start(bf16[64,3072]{1,0:T(8,128)(2,1)S(1)} %get-tuple-element.120), channel_id=1, source_target_pairs={{0,2},{1,3},{2,0},{3,1},{4,6},{5,7},{6,4},{7,5},{8,10},{9,11},{10,... | collective-permute-start | bytes 1179656 | tf_op jit(solution)/shard_map/ppermute | solution.py:705
  243.2 17.1 %collective-permute-start.30 = (bf16[64,3072]{1,0:T(8,128)(2,1)S(1)}, bf16[64,3072]{1,0:T(8,128)(2,1)S(1)}, u32[]{:S(2)}, u32[]{:S(2)}) collective-permute-start(bf16[64,3072]{1,0:T(8,128)(2,1)S(1)} %get-tuple-element.121), channel_id=1, source_target_pairs={{0,2},{1,3},{2,0},{3,1},{4,6},{5,7},{6,4},{7,5},{8,10},{9,11},{10,... | collective-permute-start | bytes 1179656 | tf_op jit(solution)/shard_map/ppermute | solution.py:705
  260.4 5.0 %collective-permute-start.31 = (bf16[256,3072]{1,0:T(8,128)(2,1)S(1)}, bf16[256,3072]{1,0:T(8,128)(2,1)S(1)}, u32[]{:S(2)}, u32[]{:S(2)}) collective-permute-start(bf16[256,3072]{1,0:T(8,128)(2,1)S(1)} %pad_maximum_fusion), channel_id=1, source_target_pairs={{0,1},{1,0},{2,3},{3,2},{4,5},{5,4},{6,7},{7,6},{8,9},{9,8},{10,11... | collective-permute-start | bytes 4718600 | tf_op jit(solution)/shard_map/ppermute | solution.py:705
  260.5 8.1 %collective-permute-start.35 = (bf16[256,768]{1,0:T(8,128)(2,1)S(1)}, bf16[256,768]{1,0:T(8,128)(2,1)S(1)}, u32[]{:S(2)}, u32[]{:S(2)}) collective-permute-start(bf16[256,768]{1,0:T(8,128)(2,1)S(1)} %pad_maximum_fusion.3), channel_id=1, source_target_pairs={{0,1},{1,0},{2,3},{3,2},{4,5},{5,4},{6,7},{7,6},{8,9},{9,8},{10,11... | collective-permute-start | bytes 1179656 | tf_op jit(solution)/shard_map/ppermute | solution.py:705
  261.0 8.1 %collective-permute-start.28 = (bf16[128,1536]{1,0:T(8,128)(2,1)S(1)}, bf16[128,1536]{1,0:T(8,128)(2,1)S(1)}, u32[]{:S(2)}, u32[]{:S(2)}) collective-permute-start(bf16[128,1536]{1,0:T(8,128)(2,1)S(1)} %get-tuple-element.119), channel_id=1, source_target_pairs={{1,0},{2,1},{3,2},{4,3},{5,4},{6,5},{7,6},{8,7},{9,8},{10,9},{11,1... | collective-permute-start | bytes 1179656 | tf_op jit(solution)/shard_map/ppermute | solution.py:1100
  262.3 6.8 %collective-permute-start.32 = (bf16[128,1536]{1,0:T(8,128)(2,1)S(1)}, bf16[128,1536]{1,0:T(8,128)(2,1)S(1)}, u32[]{:S(2)}, u32[]{:S(2)}) collective-permute-start(bf16[128,1536]{1,0:T(8,128)(2,1)S(1)} %get-tuple-element.132), channel_id=1, source_target_pairs={{0,1},{1,2},{2,3},{3,4},{4,5},{5,6},{6,7},{7,8},{8,9},{9,10},{10,1... | collective-permute-start | bytes 1179656 | tf_op jit(solution)/shard_map/ppermute | solution.py:1101
  266.2 22.7 %collective-permute-start.34 = (bf16[384,768]{1,0:T(8,128)(2,1)S(1)}, bf16[384,768]{1,0:T(8,128)(2,1)S(1)}, u32[]{:S(2)}, u32[]{:S(2)}) collective-permute-start(bf16[384,768]{1,0:T(8,128)(2,1)S(1)} %get-tuple-element.141), channel_id=1, source_target_pairs={{0,4},{1,5},{2,6},{3,7},{4,0},{5,1},{6,2},{7,3},{8,12},{9,13},{10,... | collective-permute-start | bytes 1769480 | tf_op jit(solution)/shard_map/ppermute | solution.py:705
  269.0 19.9 %collective-permute-start.36 = (bf16[144,768]{1,0:T(8,128)(2,1)S(1)}, bf16[144,768]{1,0:T(8,128)(2,1)S(1)}, u32[]{:S(2)}, u32[]{:S(2)}) collective-permute-start(bf16[144,768]{1,0:T(8,128)(2,1)S(1)} %get-tuple-element.144), channel_id=1, source_target_pairs={{0,4},{1,5},{2,6},{3,7},{4,0},{5,1},{6,2},{7,3},{8,12},{9,13},{10,... | collective-permute-start | bytes 663560 | tf_op jit(solution)/shard_map/ppermute | solution.py:705
  273.1 23.2 %collective-permute-start.33 = (bf16[144,2304]{1,0:T(8,128)(2,1)S(1)}, bf16[144,2304]{1,0:T(8,128)(2,1)S(1)}, u32[]{:S(2)}, u32[]{:S(2)}) collective-permute-start(bf16[144,2304]{1,0:T(8,128)(2,1)S(1)} %get-tuple-element.145.refs_0_), channel_id=1, source_target_pairs={{0,2},{1,3},{2,0},{3,1},{4,6},{5,7},{6,4},{7,5},{8,10},{9,11},{10,... | collective-permute-start | bytes 1990664 | tf_op jit(solution)/shard_map/ppermute | solution.py:705
  296.4 3.9 %collective-permute-start.37 = (bf16[288,2304]{1,0:T(8,128)(2,1)S(1)}, bf16[288,2304]{1,0:T(8,128)(2,1)S(1)}, u32[]{:S(2)}, u32[]{:S(2)}) collective-permute-start(bf16[288,2304]{1,0:T(8,128)(2,1)S(1)} %pad_maximum_fusion.1), channel_id=1, source_target_pairs={{0,1},{1,0},{2,3},{3,2},{4,5},{5,4},{6,7},{7,6},{8,9},{9,8},{10,11... | collective-permute-start | bytes 3981320 | tf_op jit(solution)/shard_map/ppermute | solution.py:705
  296.5 21.5 %collective-permute-start.40 = (bf16[264,768]{1,0:T(8,128)(2,1)S(1)}, bf16[264,768]{1,0:T(8,128)(2,1)S(1)}, u32[]{:S(2)}, u32[]{:S(2)}) collective-permute-start(bf16[264,768]{1,0:T(8,128)(2,1)S(1)} %pad_maximum_fusion.2), channel_id=1, source_target_pairs={{0,8},{1,9},{2,10},{3,11},{4,12},{5,13},{6,14},{7,15},{8,0},{9,1},... | collective-permute-start | bytes 1216520 | tf_op jit(solution)/shard_map/ppermute | solution.py:705
  301.0 21.2 %collective-permute-start.38 = (bf16[96,2432]{1,0:T(8,128)(2,1)S(1)}, bf16[96,2432]{1,0:T(8,128)(2,1)S(1)}, u32[]{:S(2)}, u32[]{:S(2)}) collective-permute-start(bf16[96,2432]{1,0:T(8,128)(2,1)S(1)} %get-tuple-element.148), channel_id=1, source_target_pairs={{0,4},{1,5},{2,6},{3,7},{4,0},{5,1},{6,2},{7,3},{8,12},{9,13},{10,... | collective-permute-start | bytes 1400840 | tf_op jit(solution)/shard_map/ppermute | solution.py:705
  322.3 11.9 %collective-permute-start.39 = (bf16[48,2432]{1,0:T(8,128)(2,1)S(1)}, bf16[48,2432]{1,0:T(8,128)(2,1)S(1)}, u32[]{:S(2)}, u32[]{:S(2)}) collective-permute-start(bf16[48,2432]{1,0:T(8,128)(2,1)S(1)} %add_convert_fusion.2), channel_id=1, source_target_pairs={{0,8},{1,9},{2,10},{3,11},{4,12},{5,13},{6,14},{7,15},{8,0},{9,1},... | collective-permute-start | bytes 700424 | tf_op jit(solution)/shard_map/ppermute | solution.py:705
  (47 other events, 402.8 us)
Sparse Core Ops, SparseCore 0:
  23.4 75.1 all-gather.1

commit v12 on v11

--- a/solution.py
+++ b/solution.py
@@ -759,14 +759,10 @@
 
 
 def by_plane(result, base, outs, columns=slice(None)):
-    keep, keep_far, send = outs
     rows = result.shape[0] // 4
-    half = send.shape[0] // 2
-    here = slice(base, base + rows)
-    keep[here, columns] = result[:rows]
-    keep_far[here, columns] = result[2 * rows : 3 * rows]
-    send[here, columns] = result[rows : 2 * rows].astype(BF)
-    send[half + base : half + base + rows, columns] = result[3 * rows :].astype(BF)
+    for plane, out_ref in enumerate(outs):
+        part = result[plane * rows : (plane + 1) * rows]
+        out_ref[base : base + rows, columns] = part.astype(out_ref.dtype)
 
 
 def four_parts(refs, columns, tokens):
@@ -778,7 +774,7 @@
 
 
 def early_body(terms, split, *refs):
-    refs, outs = refs[:-3], refs[-3:]
+    refs, outs = refs[:-4], refs[-4:]
     operands, lefts = (refs[:split], refs[split:-4]), refs[-4:]
     width = outs[0].shape[1]
     base = 0
@@ -791,7 +787,7 @@
 
 
 def late_body(rows, place_ref, *refs):
-    refs, outs, scr = refs[:-4], refs[-4:-1], refs[-1]
+    refs, outs, scr = refs[:-5], refs[-5:-1], refs[-1]
     rights, lefts = refs[:-4], refs[-4:]
     columns = rights[0].shape[1]
     width = columns // 3
@@ -814,23 +810,22 @@
     by_plane(jnp.concatenate(gains, 0), 0, outs, slice(columns, columns + LANES))
 
 
-def three_parts(shape):
-    return [(shape, F32), (shape, F32), ((2 * shape[0], shape[1]), BF)]
+def four_planes(shape):
+    return [(shape, F32)] + [(shape, BF)] * 3
 
 
 def with_core(rows, across, count):
     return [rows, partner(jnp.concatenate([rows, *across]), 1, count), *across]
 
 
-def first_hop(blocks, count):
-    keep, keep_far, send = blocks
-    got = partner(send, 4, count)
-    half = keep.shape[0]
-    return keep + got[:half].astype(F32), (keep_far + got[half:].astype(F32)).astype(BF)
-
-
-def second_hop(near, far, count):
-    return near + partner(far, 8, count).astype(F32)
+def from_planes(blocks, count):
+    return [partner(item, 4 * (z + 1), count) for z, item in enumerate(blocks[1:])]
+
+
+def sum_planes(own, got):
+    for item in got:
+        own = own + item.astype(F32)
+    return own
 
 
 def over_groups(rows, count):
@@ -1079,14 +1074,6 @@
     )
     across = [partner(item, 2, count) for item in right_chunks]
     d_mlp = with_core(d_mlp, [across_mlp], count)
-    out_near, out_far = first_hop(
-        on_core(
-            functools.partial(early_body, [(0, (3 * shard_total, left_total), (0, width))], 3),
-            three_parts((hidden_total, width)),
-            (*d_mlp, *left),
-        ),
-        count,
-    )
     dq_0, d_own, d_before, d_after = on_core(
         local_backward_body,
         [
@@ -1102,18 +1089,19 @@
     across, right, _ = lax.optimization_barrier((across, right, d_own))
     right = with_core(right, across, count)
     in_rows, attn_rows = shard_total * (inner // width), shard_total
-    early_rows = in_rows + attn_rows
+    early_rows = in_rows + attn_rows + hidden_total
     terms = [
         (0, (2 * shard_total, 3 * shard_total), (0, inner)),
         (0, (shard_total, 2 * shard_total), (inner, inner + width)),
+        (1, (3 * shard_total, left_total), (0, width)),
     ]
     early = on_core(
         functools.partial(early_body, terms, len(right)),
-        three_parts((early_rows, width)),
-        (*right, *left),
+        four_planes((early_rows, width)),
+        (*right, *d_mlp, *left),
     )
     from_after, _ = lax.optimization_barrier((from_after, early[0]))
-    near, far = first_hop(early, count)
+    early_got = from_planes(early, count)
     d_proj, grad_0, gain_attn_sum = on_core(
         local_finish_body,
         [
@@ -1129,24 +1117,21 @@
         [pltpu.SMEM] + [pltpu.VMEM] * 13,
     )
     across_chunks = [partner(d_proj, 2, count)]
-    far = jnp.concatenate([far, out_far])
-    across_chunks, d_proj, _ = lax.optimization_barrier((across_chunks, d_proj, far))
-    far = partner(far, 8, count)
+    early = sum_planes(early[0], early_got)
+    parts = [early[p * shard_total : (p + 1) * shard_total] for p in range(inner // width)]
+    in_share = jnp.concatenate(parts, 1)
+    across_chunks, d_proj, _ = lax.optimization_barrier((across_chunks, d_proj, in_share))
     right = with_core(d_proj, across_chunks, count)
     late_in = (group_pos[None], *right, *left)
     late = on_core(
         functools.partial(late_body, (0, shard_total)),
-        three_parts((shard_total, 3 * width + LANES)),
+        four_planes((shard_total, 3 * width + LANES)),
         late_in,
         [pltpu.VMEM((width, LANES), F32)],
         [pltpu.SMEM] + [pltpu.VMEM] * (len(late_in) - 1),
     )
-    far, _ = lax.optimization_barrier((far, late[0]))
-    early = near + far[:early_rows].astype(F32)
-    mlp_out_share = out_near + far[early_rows:].astype(F32)
-    late = second_hop(*first_hop(late, count), count)
-    parts = [early[p * shard_total : (p + 1) * shard_total] for p in range(inner // width)]
-    in_share = jnp.concatenate(parts, 1)
+    late = sum_planes(late[0], from_planes(late, count))
+    mlp_out_share = early[in_rows + attn_rows :]
     attn_share = early[in_rows : in_rows + attn_rows]
     gain_columns = late[:, 3 * width :]
     qkv_share, in_share, mlp_out_share, attn_share, gain_columns = (

time: 344 us -> 351 us (1.020)
    ppermute x33 -> x34, starting transfers between devices: 29.9 us -> 33.8 us  [partner(): return lax.ppermute(rows, 'dp', [(i, i ^ apart) for i in range(count)])]
    unnamed x102 -> x116, local copies, waits for them, and re-layouts: 26.1 us -> 27.5 us
    pallas_call x17 -> x16, Pallas kernels: 56.7 us -> 58.1 us  [on_core(): pl.pallas_call(body, out_shape=[jax.ShapeDtypeStruct(shape, dtype) for sh...]
    ppermute x33 -> x34, waiting for transfers between devices: 93.3 us -> 92.6 us  [partner(): return lax.ppermute(rows, 'dp', [(i, i ^ apart) for i in range(count)])]
  transfers between devices with their start and end apart: 44 -> 45, of which waited for: 22 -> 21; matrix products, arithmetic and copies ran while one was open for 6% -> 6% of each run, Pallas kernels for 7% -> 6%
where the time goes in v12:
time: 351 us; the launch traced here: 350 us
  waiting for transfers between devices  135 us (38%)
  Pallas kernels  58.1 us (17%)
  starting transfers between devices  56.9 us (16%)
  local copies, waits for them, and re-layouts  46.9 us (13%)
  blocking collectives  32.5 us (9%)
  between operations  15 us (4%)
  other arithmetic  5.31 us (2%)
    ppermute x34, waiting for transfers between devices, partner(): return lax.ppermute(rows, 'dp', [(i, i ^ apart) for i in range(count)])  92.6 us
    pallas_call x16, Pallas kernels, on_core(): pl.pallas_call(body, out_shape=[jax.ShapeDtypeStruct(shape, dtype) for sh...  58.1 us
    ppermute x34, starting transfers between devices, partner(): return lax.ppermute(rows, 'dp', [(i, i ^ apart) for i in range(count)])  33.8 us
    all_to_all x2, blocking collectives, exchange(): return lax.all_to_all(blocks, 'dp', 0, 0, axis_index_groups=groups)  32.5 us
    all_gather x1, waiting for transfers between devices, on_device(): others = [lax.all_gather(stacked, 'dp', axis=0, tiled=True)]  29.4 us
    unnamed x116, local copies, waits for them, and re-layouts  27.5 us
    dynamic_update_slice x16, local copies, waits for them, and re-layouts, gather_rows(): whole = lax.dynamic_update_slice(whole, item[None], start)  11.4 us
    ppermute x4, waiting for transfers between devices, to_other_section(): return [lax.ppermute(rows, 'section', pairs) for rows in chunks]  9.41 us
  transfers between devices with their start and end apart: 45, of which 21 were waited for; matrix products, arithmetic and copies ran while one was open for 6% of the time, Pallas kernels for 6%

profile of v12, /device:TPU:0, one launch (start us, length us, event | category | flops | bytes accessed | tf_op | source)
XLA Modules:
  0.0 349.9 jit_solution(9968736570012616096)
XLA Ops:
  10.3 3.0 collective-permute-start.1
  13.3 1.6 collective-permute-start.2
  14.9 2.6 collective-permute-start.3
  23.5 2.1 broadcast_in_dim.105
  27.5 6.9 %collective-permute-done.3 = bf16[48,2432]{1,0:T(8,128)(2,1)S(1)} collective-permute-done((bf16[48,2432]{1,0:T(8,128)(2,1)S(1)}, bf16[48,2432]{1,0:T(8,128)(2,1)S(1)}, u32[]{:S(2)}, u32[]{:S(2)}) %collective-permute-start.3) | collective-permute-done | bytes 233504 | tf_op jit(solution)/shard_map/ppermute | solution.py:705
  34.9 1.5 collective-permute-start.7
  40.0 5.6 %collective-permute-done.6 = bf16[48,2432]{1,0:T(8,128)(2,1)S(1)} collective-permute-done((bf16[48,2432]{1,0:T(8,128)(2,1)S(1)}, bf16[48,2432]{1,0:T(8,128)(2,1)S(1)}, u32[]{:S(2)}, u32[]{:S(2)}) %collective-permute-start.6) | collective-permute-done | bytes 233504 | tf_op jit(solution)/shard_map/ppermute | solution.py:705
  46.3 3.2 collective-permute-done.7
  56.9 3.1 shard_map.154
  60.1 2.1 collective-permute-start.16
  64.2 1.8 collective-permute-done.17.after_ref
  66.0 3.6 %shard_map.155 = (bf16[128,768]{1,0:T(8,128)(2,1)S(1)}, f32[12,1,128]{2,1,0:T(1,128)S(1)}) custom-call(bf16[128,768]{1,0:T(8,128)(2,1)S(1)} %get-tuple-element.79.q_ref, bf16[128,1536]{1,0:T(8,128)(2,1)S(1)} %collective-permute-done.16.before_ref, bf16[128,1536]{1,0:T(8,128)(2,1)S(1)} %get-tuple-element.80.own_ref, ...), custom_call_target="tpu_custom_call" | custom-call | flops 1024 | bytes 1024 | tf_op jit(solution)/shard_map/pallas_call | solution.py:65
  69.6 29.4 %all-gather.2.cloned.1.call-done.refs_0_ = bf16[768,4352]{1,0:T(8,128)(2,1)} async-done(((bf16[48,4352]{1,0:T(8,128)(2,1)}), bf16[768,4352]{1,0:T(8,128)(2,1)}) %all-gather.2.cloned.1.call-update) | async-done | bytes 6684688 | tf_op jit(solution)/shard_map/all_gather | solution.py:886
  99.0 4.4 %shard_map.156 = (bf16[128,768]{1,0:T(8,128)(2,1)S(1)}, bf16[128,1152]{1,0:T(8,128)(2,1)S(1)}, f32[128,768]{1,0:T(8,128)S(1)}, f32[128,2304]{1,0:T(8,128)S(1)}, ...) custom-call(bf16[768,4352]{1,0:T(8,128)(2,1)} %all-gather.2.cloned.1.call-done.refs_0_, ...), custom_call_target="tpu_custom_call" | custom-call | flops 1024 | bytes 1024 | tf_op jit(solution)/shard_map/pallas_call | solution.py:65
  106.0 3.3 collective-permute-start.18
  112.4 1.4 collective-permute-done.19.high_ref.refs_3_
  113.9 3.2 shard_map.157
  117.1 20.8 %all_to_all.20.got_ref = bf16[16,144,128]{2,1,0:T(8,128)(2,1)S(1)} all-to-all(bf16[16,144,128]{2,1,0:T(8,128)(2,1)S(1)} %get-tuple-element.85), channel_id=1, replica_groups={{0,1,2,3,4,5,6,7,8,9,10,11,12,13,14,15},{16,17,18,19,20,21,22,23,24,25,..., dimensions={0} | all-to-all | bytes 1179648 | tf_op jit(solution)/shard_map/all_to_all | solution.py:696
  140.3 6.0 %shard_map.158 = (bf16[16,48,128]{2,1,0:T(8,128)(2,1)S(1)}, f32[6,1,256]{2,1,0:T(1,128)S(1)}) custom-call(bf16[16,144,128]{2,1,0:T(8,128)(2,1)S(1)} %all_to_all.20.got_ref, bf16[16,64,128]{2,1,0:T(8,128)(2,1)S(1)} %collective-permute-done.20.other_ref, s32[1024,1]{1,0:T(8,128)S(1)} %copy.19.own_seg_ref, s32[1024,1]{1,0:T(8,128)S(1)} %copy.20.shared_seg_ref), custom_call_target="tpu_custom_call" | custom-call | flops 1024 | bytes 1024 | tf_op jit(solution)/shard_map/pallas_call | solution.py:65
  146.4 11.8 %all_to_all.21.refs_1_ = bf16[16,48,128]{2,1,0:T(8,128)(2,1)S(1)} all-to-all(bf16[16,48,128]{2,1,0:T(8,128)(2,1)S(1)} %get-tuple-element.86), channel_id=1, replica_groups={{0,1,2,3,4,5,6,7,8,9,10,11,12,13,14,15},{16,17,18,19,20,21,22,23,24,25,..., dimensions={0} | all-to-all | bytes 393216 | tf_op jit(solution)/shard_map/all_to_all | solution.py:696
  158.2 7.7 %shard_map.159 = (bf16[128,768]{1,0:T(8,128)(2,1)S(1)}, bf16[128,768]{1,0:T(8,128)(2,1)S(1)}, bf16[128,768]{1,0:T(8,128)(2,1)S(1)}, bf16[128,1152]{1,0:T(8,128)(...) custom-call(bf16[768,4352]{1,0:T(8,128)(2,1)} %all-gather.2.cloned.1, ...), custom_call_target="tpu_custom_call" | custom-call | flops 1024 | bytes 1024 | tf_op jit(solution)/shard_map/pallas_call | solution.py:65
  170.3 4.2 %all-to-all-start.2 = ((bf16[16,48,128]{2,1,0:T(8,128)(2,1)}), bf16[16,48,128]{2,1,0:T(8,128)(2,1)}, u32[]{:S(2)}, u32[]{:S(2)}) async-start(bf16[16,48,128]{2,1,0:T(8,128)(2,1)} %get-tuple-element.96), calls=%async_computation.2 | async-start | bytes 393216 | tf_op jit(solution)/shard_map/all_to_all | solution.py:696
  181.4 2.1 all-to-all-done.2.d_ref
  184.4 8.2 %shard_map.161 = (bf16[16,144,128]{2,1,0:T(8,128)(2,1)S(1)}, bf16[16,64,128]{2,1,0:T(8,128)(2,1)S(1)}) custom-call(bf16[16,144,128]{2,1,0:T(8,128)(2,1)S(1)} %all_to_all.20.got_ref, bf16[16,64,128]{2,1,0:T(8,128)(2,1)S(1)} %copy-done.10, s32[1024,1]{1,0:T(8,128)S(1)} %copy.19.own_seg_ref, s32[1024,1]{1,0:T(8,128)S(1)} %copy.20.shared_seg_ref, ...), custom_call_target="tpu_custom_call" | custom-call | flops 1024 | bytes 1024 | tf_op jit(solution)/shard_map/pallas_call | solution.py:65
  195.4 3.8 %all-to-all-start.3 = ((bf16[16,144,128]{2,1,0:T(8,128)(2,1)}), bf16[16,144,128]{2,1,0:T(8,128)(2,1)S(1)}, u32[]{:S(2)}, u32[]{:S(2)}) async-start(bf16[16,144,128]{2,1,0:T(8,128)(2,1)} %add_convert_fusion), calls=%async_computation.3 | async-start | bytes 1179648 | tf_op jit(solution)/shard_map/all_to_all | solution.py:696
  199.8 1.7 collective-permute-start.23
  201.4 10.9 %collective-permute-done.23.refs_9_.refs_5_ = bf16[4,216,128]{2,1,0:T(8,128)(2,1)S(1)} collective-permute-done((bf16[4,216,128]{2,1,0:T(8,128)(2,1)S(1)}, bf16[4,216,128]{2,1,0:T(8,128)(2,1)S(1)}, u32[]{:S(2)}, u32[]{:S(2)}) %collective-permute-start.23) | collective-permute-done | bytes 221216 | tf_op jit(solution)/shard_map/ppermute | solution.py:705
  212.4 5.3 %collective-permute-done.24.refs_10_.refs_6_ = bf16[4,216,128]{2,1,0:T(8,128)(2,1)S(1)} collective-permute-done((bf16[4,216,128]{2,1,0:T(8,128)(2,1)S(1)}, bf16[4,216,128]{2,1,0:T(8,128)(2,1)S(1)}, u32[]{:S(2)}, u32[]{:S(2)}) %collective-permute-start.24) | collective-permute-done | bytes 221216 | tf_op jit(solution)/shard_map/ppermute | solution.py:705
  220.5 3.6 %shard_map.162 = (bf16[128,2304]{1,0:T(8,128)(2,1)S(1)}, f32[1,768]{1,0:T(1,128)S(1)}, bf16[64,768]{1,0:T(8,128)(2,1)S(1)}, bf16[64,768]{1,0:T(8,128)(2,1)S(1)}) custom-call(bf16[768,2432]{1,0:T(8,128)(2,1)} %bitcast.23.first_ref, bf16[16,144,128]{2,1,0:T(8,128)(2,1)S(1)} %all-to-all-done.3.got_ref, f32[128,768]{1,0:T(8,128)S(1)} %copy-done.28, ...), custom_call_target="tpu_custom_call" | custom-call | flops 1024 | bytes 1024 | tf_op jit(solution)/shard_map/pallas_call | solution.py:65
  226.7 4.9 %collective-permute-done.25.refs_2_ = bf16[64,768]{1,0:T(8,128)(2,1)S(1)} collective-permute-done((bf16[64,768]{1,0:T(8,128)(2,1)S(1)}, bf16[64,768]{1,0:T(8,128)(2,1)S(1)}, u32[]{:S(2)}, u32[]{:S(2)}) %collective-permute-start.25) | collective-permute-done | bytes 98336 | tf_op jit(solution)/shard_map/ppermute | solution.py:701
  231.6 1.6 collective-permute-done.26.refs_3_
  237.2 6.2 %shard_map.163 = (f32[1,768]{1,0:T(1,128)S(1)}, f32[128,768]{1,0:T(8,128)S(1)}, bf16[128,768]{1,0:T(8,128)(2,1)S(1)}, bf16[128,3072]{1,0:T(8,128)(2,1)S(1)}, bf1...) custom-call(bf16[768,4352]{1,0:T(8,128)(2,1)} %all-gather.2.cloned.1.call-done.refs_0_, ...), custom_call_target="tpu_custom_call" | custom-call | flops 1024 | bytes 1024 | tf_op jit(solution)/shard_map/pallas_call | solution.py:65
  243.4 1.7 collective-permute-start.29
  245.5 3.5 %shard_map.164 = (bf16[128,768]{1,0:T(8,128)(2,1)S(1)}, f32[128,1536]{1,0:T(8,128)S(1)}, bf16[128,1536]{1,0:T(8,128)(2,1)S(1)}, bf16[128,1536]{1,0:T(8,128)(2,1)S(1)}) custom-call(bf16[128,768]{1,0:T(8,128)(2,1)S(1)} %copy-done.20, bf16[128,1536]{1,0:T(8,128)(2,1)S(1)} %copy-done.4, bf16[128,1536]{1,0:T(8,128)(2,1)S(1)} %copy-done.2, ...), custom_call_target="tpu_custom_call" | custom-call | flops 1024 | bytes 1024 | tf_op jit(solution)/shard_map/pallas_call | solution.py:65
  249.0 6.5 %collective-permute-done.29.refs_2_ = bf16[64,3072]{1,0:T(8,128)(2,1)S(1)} collective-permute-done((bf16[64,3072]{1,0:T(8,128)(2,1)S(1)}, bf16[64,3072]{1,0:T(8,128)(2,1)S(1)}, u32[]{:S(2)}, u32[]{:S(2)}) %collective-permute-start.29) | collective-permute-done | bytes 393248 | tf_op jit(solution)/shard_map/ppermute | solution.py:705
  255.5 6.7 %collective-permute-done.30.refs_3_ = bf16[64,3072]{1,0:T(8,128)(2,1)S(1)} collective-permute-done((bf16[64,3072]{1,0:T(8,128)(2,1)S(1)}, bf16[64,3072]{1,0:T(8,128)(2,1)S(1)}, u32[]{:S(2)}, u32[]{:S(2)}) %collective-permute-start.30) | collective-permute-done | bytes 393248 | tf_op jit(solution)/shard_map/ppermute | solution.py:705
  264.3 3.1 collective-permute-start.33
  268.5 2.5 shard_map.165
  271.0 4.1 %shard_map.166 = (bf16[144,2304]{1,0:T(8,128)(2,1)S(1)}, bf16[128,768]{1,0:T(8,128)(2,1)S(1)}, f32[1,768]{1,0:T(1,128)}) custom-call(s32[1]{0:T(128)} %bitcast.37.lower_ref.refs_1_, bf16[768,2432]{1,0:T(8,128)(2,1)} %bitcast.23.first_ref, bf16[128,768]{1,0:T(8,128)(2,1)S(1)} %get-tuple-element.115.dq_ref, f32[128,1536]{1,0:T(8,128)S(1)} %get-tuple-element.116.own_ref, ...), custom_call_target="tpu_custom_call" | custom-call | flops 1024 | bytes 1024 | tf_op jit(solution)/shard_map/pallas_call | solution.py:65
  275.1 8.1 %collective-permute-start.34 = (bf16[144,2304]{1,0:T(8,128)(2,1)S(1)}, bf16[144,2304]{1,0:T(8,128)(2,1)S(1)}, u32[]{:S(2)}, u32[]{:S(2)}) collective-permute-start(bf16[144,2304]{1,0:T(8,128)(2,1)S(1)} %get-tuple-element.142.refs_0_), channel_id=1, source_target_pairs={{0,2},{1,3},{2,0},{3,1},{4,6},{5,7},{6,4},{7,5},{8,10},{9,11},{10,... | collective-permute-start | bytes 1990664 | tf_op jit(solution)/shard_map/ppermute | solution.py:705
  283.6 2.5 collective-permute-start.36
  286.1 1.5 collective-permute-start.35
  287.6 10.1 %collective-permute-done.34.refs_2_ = bf16[144,2304]{1,0:T(8,128)(2,1)S(1)} collective-permute-done((bf16[144,2304]{1,0:T(8,128)(2,1)S(1)}, bf16[144,2304]{1,0:T(8,128)(2,1)S(1)}, u32[]{:S(2)}, u32[]{:S(2)}) %collective-permute-start.34) | collective-permute-done | bytes 663584 | tf_op jit(solution)/shard_map/ppermute | solution.py:705
  299.3 19.8 %collective-permute-done.36 = bf16[264,768]{1,0:T(8,128)(2,1)S(1)} collective-permute-done((bf16[264,768]{1,0:T(8,128)(2,1)S(1)}, bf16[264,768]{1,0:T(8,128)(2,1)S(1)}, u32[]{:S(2)}, u32[]{:S(2)}) %collective-permute-start.36) | collective-permute-done | bytes 405536 | tf_op jit(solution)/shard_map/ppermute | solution.py:705
  321.4 2.4 collective-permute-start.41
  323.8 2.1 collective-permute-start.39
  326.6 5.4 %collective-permute-done.41 = bf16[48,2432]{1,0:T(8,128)(2,1)S(1)} collective-permute-done((bf16[48,2432]{1,0:T(8,128)(2,1)S(1)}, bf16[48,2432]{1,0:T(8,128)(2,1)S(1)}, u32[]{:S(2)}, u32[]{:S(2)}) %collective-permute-start.41) | collective-permute-done | bytes 233504 | tf_op jit(solution)/shard_map/ppermute | solution.py:705
  332.0 9.5 %collective-permute-done.40 = bf16[48,2432]{1,0:T(8,128)(2,1)S(1)} collective-permute-done((bf16[48,2432]{1,0:T(8,128)(2,1)S(1)}, bf16[48,2432]{1,0:T(8,128)(2,1)S(1)}, u32[]{:S(2)}, u32[]{:S(2)}) %collective-permute-start.40) | collective-permute-done | bytes 233504 | tf_op jit(solution)/shard_map/ppermute | solution.py:705
  (254 shorter events, 68.2 us)
Async XLA Ops:
  7.2 91.8 %all-gather.2.cloned.1.call-start = ((), (), s32[]{:S(2)}) async-start(), calls=%async_computation.4 | async-start | bytes 7102464 | tf_op jit(solution)/shard_map/all_gather | solution.py:886
  10.3 13.0 %collective-permute-start.1 = (bf16[48,2432]{1,0:T(8,128)(2,1)S(1)}, bf16[48,2432]{1,0:T(8,128)(2,1)S(1)}, u32[]{:S(2)}, u32[]{:S(2)}) collective-permute-start(bf16[48,2432]{1,0:T(8,128)(2,1)S(1)} %shard_map.153), channel_id=1, source_target_pairs={{0,2},{1,3},{2,0},{3,1},{4,6},{5,7},{6,4},{7,5},{8,10},{9,11},{10,... | collective-permute-start | bytes 700424 | tf_op jit(solution)/shard_map/ppermute | solution.py:705
  13.3 13.9 %collective-permute-start.2 = (bf16[48,2432]{1,0:T(8,128)(2,1)S(1)}, bf16[48,2432]{1,0:T(8,128)(2,1)S(1)}, u32[]{:S(2)}, u32[]{:S(2)}) collective-permute-start(bf16[48,2432]{1,0:T(8,128)(2,1)S(1)} %shard_map.153), channel_id=1, source_target_pairs={{0,4},{1,5},{2,6},{3,7},{4,0},{5,1},{6,2},{7,3},{8,12},{9,13},{10,... | collective-permute-start | bytes 700424 | tf_op jit(solution)/shard_map/ppermute | solution.py:705
  14.9 19.5 %collective-permute-start.3 = (bf16[48,2432]{1,0:T(8,128)(2,1)S(1)}, bf16[48,2432]{1,0:T(8,128)(2,1)S(1)}, u32[]{:S(2)}, u32[]{:S(2)}) collective-permute-start(bf16[48,2432]{1,0:T(8,128)(2,1)S(1)} %shard_map.153), channel_id=1, source_target_pairs={{0,8},{1,9},{2,10},{3,11},{4,12},{5,13},{6,14},{7,15},{8,0},{9,1},... | collective-permute-start | bytes 700424 | tf_op jit(solution)/shard_map/ppermute | solution.py:705
  17.5 17.5 %collective-permute-start.4 = (bf16[48,2432]{1,0:T(8,128)(2,1)S(1)}, bf16[48,2432]{1,0:T(8,128)(2,1)S(1)}, u32[]{:S(2)}, u32[]{:S(2)}) collective-permute-start(bf16[48,2432]{1,0:T(8,128)(2,1)S(1)} %shard_map.153), channel_id=1, source_target_pairs={{0,12},{1,13},{2,14},{3,15},{4,8},{5,9},{6,10},{7,11},{8,4},{9,5},... | collective-permute-start | bytes 700424 | tf_op jit(solution)/shard_map/ppermute | solution.py:705
  18.4 1.2 collective-permute-start
  19.6 30.6 %collective-permute-start.8 = (bf16[48,2432]{1,0:T(8,128)(2,1)S(1)}, bf16[48,2432]{1,0:T(8,128)(2,1)S(1)}, u32[]{:S(2)}, u32[]{:S(2)}) collective-permute-start(bf16[48,2432]{1,0:T(8,128)(2,1)S(1)} %shard_map.153), channel_id=1, source_target_pairs={{0,1},{1,0},{2,3},{3,2},{4,5},{5,4},{6,7},{7,6},{8,9},{9,8},{10,11... | collective-permute-start | bytes 700424 | tf_op jit(solution)/shard_map/ppermute | solution.py:705
  26.8 24.6 %collective-permute-start.9 = (bf16[48,2432]{1,0:T(8,128)(2,1)S(1)}, bf16[48,2432]{1,0:T(8,128)(2,1)S(1)}, u32[]{:S(2)}, u32[]{:S(2)}) collective-permute-start(bf16[48,2432]{1,0:T(8,128)(2,1)S(1)} %collective-permute-done.1), channel_id=1, source_target_pairs={{0,1},{1,0},{2,3},{3,2},{4,5},{5,4},{6,7},{7,6},{8,9},{9,8},{10,11... | collective-permute-start | bytes 700424 | tf_op jit(solution)/shard_map/ppermute | solution.py:705
  27.2 12.1 %collective-permute-start.5 = (bf16[48,2432]{1,0:T(8,128)(2,1)S(1)}, bf16[48,2432]{1,0:T(8,128)(2,1)S(1)}, u32[]{:S(2)}, u32[]{:S(2)}) collective-permute-start(bf16[48,2432]{1,0:T(8,128)(2,1)S(1)} %collective-permute-done.2), channel_id=1, source_target_pairs={{0,2},{1,3},{2,0},{3,1},{4,6},{5,7},{6,4},{7,5},{8,10},{9,11},{10,... | collective-permute-start | bytes 700424 | tf_op jit(solution)/shard_map/ppermute | solution.py:705
  34.4 11.2 %collective-permute-start.6 = (bf16[48,2432]{1,0:T(8,128)(2,1)S(1)}, bf16[48,2432]{1,0:T(8,128)(2,1)S(1)}, u32[]{:S(2)}, u32[]{:S(2)}) collective-permute-start(bf16[48,2432]{1,0:T(8,128)(2,1)S(1)} %collective-permute-done.3), channel_id=1, source_target_pairs={{0,2},{1,3},{2,0},{3,1},{4,6},{5,7},{6,4},{7,5},{8,10},{9,11},{10,... | collective-permute-start | bytes 700424 | tf_op jit(solution)/shard_map/ppermute | solution.py:705
  34.9 14.5 %collective-permute-start.7 = (bf16[48,2432]{1,0:T(8,128)(2,1)S(1)}, bf16[48,2432]{1,0:T(8,128)(2,1)S(1)}, u32[]{:S(2)}, u32[]{:S(2)}) collective-permute-start(bf16[48,2432]{1,0:T(8,128)(2,1)S(1)} %collective-permute-done.4), channel_id=1, source_target_pairs={{0,2},{1,3},{2,0},{3,1},{4,6},{5,7},{6,4},{7,5},{8,10},{9,11},{10,... | collective-permute-start | bytes 700424 | tf_op jit(solution)/shard_map/ppermute | solution.py:705
  39.3 12.8 %collective-permute-start.10 = (bf16[48,2432]{1,0:T(8,128)(2,1)S(1)}, bf16[48,2432]{1,0:T(8,128)(2,1)S(1)}, u32[]{:S(2)}, u32[]{:S(2)}) collective-permute-start(bf16[48,2432]{1,0:T(8,128)(2,1)S(1)} %collective-permute-done.2), channel_id=1, source_target_pairs={{0,1},{1,0},{2,3},{3,2},{4,5},{5,4},{6,7},{7,6},{8,9},{9,8},{10,11... | collective-permute-start | bytes 700424 | tf_op jit(solution)/shard_map/ppermute | solution.py:705
  45.6 8.5 %collective-permute-start.12 = (bf16[48,2432]{1,0:T(8,128)(2,1)S(1)}, bf16[48,2432]{1,0:T(8,128)(2,1)S(1)}, u32[]{:S(2)}, u32[]{:S(2)}) collective-permute-start(bf16[48,2432]{1,0:T(8,128)(2,1)S(1)} %collective-permute-done.3), channel_id=1, source_target_pairs={{0,1},{1,0},{2,3},{3,2},{4,5},{5,4},{6,7},{7,6},{8,9},{9,8},{10,11... | collective-permute-start | bytes 700424 | tf_op jit(solution)/shard_map/ppermute | solution.py:705
  49.5 6.1 %collective-permute-start.14 = (bf16[48,2432]{1,0:T(8,128)(2,1)S(1)}, bf16[48,2432]{1,0:T(8,128)(2,1)S(1)}, u32[]{:S(2)}, u32[]{:S(2)}) collective-permute-start(bf16[48,2432]{1,0:T(8,128)(2,1)S(1)} %collective-permute-done.4), channel_id=1, source_target_pairs={{0,1},{1,0},{2,3},{3,2},{4,5},{5,4},{6,7},{7,6},{8,9},{9,8},{10,11... | collective-permute-start | bytes 700424 | tf_op jit(solution)/shard_map/ppermute | solution.py:705
  50.2 3.2 collective-permute-start.11
  51.4 3.4 collective-permute-start.13
  52.2 4.1 %collective-permute-start.15 = (bf16[48,2432]{1,0:T(8,128)(2,1)S(1)}, bf16[48,2432]{1,0:T(8,128)(2,1)S(1)}, u32[]{:S(2)}, u32[]{:S(2)}) collective-permute-start(bf16[48,2432]{1,0:T(8,128)(2,1)S(1)} %collective-permute-done.7), channel_id=1, source_target_pairs={{0,1},{1,0},{2,3},{3,2},{4,5},{5,4},{6,7},{7,6},{8,9},{9,8},{10,11... | collective-permute-start | bytes 700424 | tf_op jit(solution)/shard_map/ppermute | solution.py:705
  60.1 43.3 %copy-start.1 = (bf16[128,1536]{1,0:T(8,128)(2,1)}, bf16[128,1536]{1,0:T(8,128)(2,1)S(1)}, u32[]{:S(2)}) copy-start(bf16[128,1536]{1,0:T(8,128)(2,1)S(1)} %get-tuple-element.80.own_ref) | copy-start | bytes 1179652
  60.1 4.1 %collective-permute-start.16 = (bf16[128,1536]{1,0:T(8,128)(2,1)S(1)}, bf16[128,1536]{1,0:T(8,128)(2,1)S(1)}, u32[]{:S(2)}, u32[]{:S(2)}) collective-permute-start(bf16[128,1536]{1,0:T(8,128)(2,1)S(1)} %get-tuple-element.80.own_ref), channel_id=1, source_target_pairs={{0,1},{1,2},{2,3},{3,4},{4,5},{5,6},{6,7},{7,8},{8,9},{9,10},{10,1... | collective-permute-start | bytes 1179656 | tf_op jit(solution)/shard_map/ppermute | solution.py:933
  62.2 3.7 %collective-permute-start.17 = (bf16[128,1536]{1,0:T(8,128)(2,1)S(1)}, bf16[128,1536]{1,0:T(8,128)(2,1)S(1)}, u32[]{:S(2)}, u32[]{:S(2)}) collective-permute-start(bf16[128,1536]{1,0:T(8,128)(2,1)S(1)} %get-tuple-element.80.own_ref), channel_id=1, source_target_pairs={{1,0},{2,1},{3,2},{4,3},{5,4},{6,5},{7,6},{8,7},{9,8},{10,9},{11,1... | collective-permute-start | bytes 1179656 | tf_op jit(solution)/shard_map/ppermute | solution.py:935
  106.0 6.5 %collective-permute-start.18 = (bf16[64,768]{1,0:T(8,128)(2,1)S(1)}, bf16[64,768]{1,0:T(8,128)(2,1)S(1)}, u32[]{:S(2)}, u32[]{:S(2)}) collective-permute-start(bf16[64,768]{1,0:T(8,128)(2,1)S(1)} %get-tuple-element.83), channel_id=1, source_target_pairs={{0,16},{1,17},{2,18},{3,19},{4,20},{5,21},{6,22},{7,23},{8,24},{9,... | collective-permute-start | bytes 294920 | tf_op jit(solution)/shard_map/ppermute | solution.py:701
  109.3 4.6 %collective-permute-start.19 = (bf16[64,768]{1,0:T(8,128)(2,1)S(1)}, bf16[64,768]{1,0:T(8,128)(2,1)S(1)}, u32[]{:S(2)}, u32[]{:S(2)}) collective-permute-start(bf16[64,768]{1,0:T(8,128)(2,1)S(1)} %get-tuple-element.84), channel_id=1, source_target_pairs={{0,16},{1,17},{2,18},{3,19},{4,20},{5,21},{6,22},{7,23},{8,24},{9,... | collective-permute-start | bytes 294920 | tf_op jit(solution)/shard_map/ppermute | solution.py:701
  112.4 45.7 %copy-start.15 = (bf16[64,768]{1,0:T(8,128)(2,1)}, bf16[64,768]{1,0:T(8,128)(2,1)S(1)}, u32[]{:S(2)}) copy-start(bf16[64,768]{1,0:T(8,128)(2,1)S(1)} %collective-permute-done.18.low_ref.refs_2_) | copy-start | bytes 294916
  113.9 44.3 %copy-start.17 = (bf16[64,768]{1,0:T(8,128)(2,1)}, bf16[64,768]{1,0:T(8,128)(2,1)S(1)}, u32[]{:S(2)}) copy-start(bf16[64,768]{1,0:T(8,128)(2,1)S(1)} %collective-permute-done.19.high_ref.refs_3_) | copy-start | bytes 294916
  138.6 1.7 collective-permute-start.20
  170.3 13.2 %all-to-all-start.2 = ((bf16[16,48,128]{2,1,0:T(8,128)(2,1)}), bf16[16,48,128]{2,1,0:T(8,128)(2,1)}, u32[]{:S(2)}, u32[]{:S(2)}) async-start(bf16[16,48,128]{2,1,0:T(8,128)(2,1)} %get-tuple-element.96), calls=%async_computation.2 | async-start | bytes 393216 | tf_op jit(solution)/shard_map/all_to_all | solution.py:696
  192.7 1.6 collective-permute-start.21
  195.4 22.3 %all-to-all-start.3 = ((bf16[16,144,128]{2,1,0:T(8,128)(2,1)}), bf16[16,144,128]{2,1,0:T(8,128)(2,1)S(1)}, u32[]{:S(2)}, u32[]{:S(2)}) async-start(bf16[16,144,128]{2,1,0:T(8,128)(2,1)} %add_convert_fusion), calls=%async_computation.3 | async-start | bytes 1179648 | tf_op jit(solution)/shard_map/all_to_all | solution.py:696
  199.3 2.2 collective-permute-start.22
  199.8 12.6 %collective-permute-start.23 = (bf16[4,216,128]{2,1,0:T(8,128)(2,1)S(1)}, bf16[4,216,128]{2,1,0:T(8,128)(2,1)S(1)}, u32[]{:S(2)}, u32[]{:S(2)}) collective-permute-start(bf16[4,216,128]{2,1,0:T(8,128)(2,1)S(1)} %get-tuple-element.153), channel_id=1, source_target_pairs={{0,2},{1,3},{2,0},{3,1},{4,6},{5,7},{6,4},{7,5},{8,10},{9,11},{10,... | collective-permute-start | bytes 663560 | tf_op jit(solution)/shard_map/ppermute | solution.py:705
  201.4 16.2 %collective-permute-start.24 = (bf16[4,216,128]{2,1,0:T(8,128)(2,1)S(1)}, bf16[4,216,128]{2,1,0:T(8,128)(2,1)S(1)}, u32[]{:S(2)}, u32[]{:S(2)}) collective-permute-start(bf16[4,216,128]{2,1,0:T(8,128)(2,1)S(1)} %get-tuple-element.152), channel_id=1, source_target_pairs={{0,3},{1,2},{2,1},{3,0},{4,7},{5,6},{6,5},{7,4},{8,11},{9,10},{10,... | collective-permute-start | bytes 663560 | tf_op jit(solution)/shard_map/ppermute | solution.py:705
  224.1 7.5 %collective-permute-start.25 = (bf16[64,768]{1,0:T(8,128)(2,1)S(1)}, bf16[64,768]{1,0:T(8,128)(2,1)S(1)}, u32[]{:S(2)}, u32[]{:S(2)}) collective-permute-start(bf16[64,768]{1,0:T(8,128)(2,1)S(1)} %get-tuple-element.106), channel_id=1, source_target_pairs={{16,0},{17,1},{18,2},{19,3},{20,4},{21,5},{22,6},{23,7},{24,8},{25... | collective-permute-start | bytes 294920 | tf_op jit(solution)/shard_map/ppermute | solution.py:701
  225.4 7.8 %collective-permute-start.26 = (bf16[64,768]{1,0:T(8,128)(2,1)S(1)}, bf16[64,768]{1,0:T(8,128)(2,1)S(1)}, u32[]{:S(2)}, u32[]{:S(2)}) collective-permute-start(bf16[64,768]{1,0:T(8,128)(2,1)S(1)} %get-tuple-element.107), channel_id=1, source_target_pairs={{16,0},{17,1},{18,2},{19,3},{20,4},{21,5},{22,6},{23,7},{24,8},{25... | collective-permute-start | bytes 294920 | tf_op jit(solution)/shard_map/ppermute | solution.py:701
  233.3 10.0 %collective-permute-start.27 = (bf16[128,768]{1,0:T(8,128)(2,1)S(1)}, bf16[128,768]{1,0:T(8,128)(2,1)S(1)}, u32[]{:S(2)}, u32[]{:S(2)}) collective-permute-start(bf16[128,768]{1,0:T(8,128)(2,1)S(1)} %pad_maximum_fusion.5.refs_4_), channel_id=1, source_target_pairs={{0,2},{1,3},{2,0},{3,1},{4,6},{5,7},{6,4},{7,5},{8,10},{9,11},{10,... | collective-permute-start | bytes 589832 | tf_op jit(solution)/shard_map/ppermute | solution.py:705
  243.4 12.1 %collective-permute-start.29 = (bf16[64,3072]{1,0:T(8,128)(2,1)S(1)}, bf16[64,3072]{1,0:T(8,128)(2,1)S(1)}, u32[]{:S(2)}, u32[]{:S(2)}) collective-permute-start(bf16[64,3072]{1,0:T(8,128)(2,1)S(1)} %get-tuple-element.118), channel_id=1, source_target_pairs={{0,2},{1,3},{2,0},{3,1},{4,6},{5,7},{6,4},{7,5},{8,10},{9,11},{10,... | collective-permute-start | bytes 1179656 | tf_op jit(solution)/shard_map/ppermute | solution.py:705
  245.1 17.1 %collective-permute-start.30 = (bf16[64,3072]{1,0:T(8,128)(2,1)S(1)}, bf16[64,3072]{1,0:T(8,128)(2,1)S(1)}, u32[]{:S(2)}, u32[]{:S(2)}) collective-permute-start(bf16[64,3072]{1,0:T(8,128)(2,1)S(1)} %get-tuple-element.119), channel_id=1, source_target_pairs={{0,2},{1,3},{2,0},{3,1},{4,6},{5,7},{6,4},{7,5},{8,10},{9,11},{10,... | collective-permute-start | bytes 1179656 | tf_op jit(solution)/shard_map/ppermute | solution.py:705
  262.3 5.0 %collective-permute-start.31 = (bf16[256,3072]{1,0:T(8,128)(2,1)S(1)}, bf16[256,3072]{1,0:T(8,128)(2,1)S(1)}, u32[]{:S(2)}, u32[]{:S(2)}) collective-permute-start(bf16[256,3072]{1,0:T(8,128)(2,1)S(1)} %pad_maximum_fusion), channel_id=1, source_target_pairs={{0,1},{1,0},{2,3},{3,2},{4,5},{5,4},{6,7},{7,6},{8,9},{9,8},{10,11... | collective-permute-start | bytes 4718600 | tf_op jit(solution)/shard_map/ppermute | solution.py:705
  262.4 4.9 %collective-permute-start.32 = (bf16[256,768]{1,0:T(8,128)(2,1)S(1)}, bf16[256,768]{1,0:T(8,128)(2,1)S(1)}, u32[]{:S(2)}, u32[]{:S(2)}) collective-permute-start(bf16[256,768]{1,0:T(8,128)(2,1)S(1)} %pad_maximum_fusion.3), channel_id=1, source_target_pairs={{0,1},{1,0},{2,3},{3,2},{4,5},{5,4},{6,7},{7,6},{8,9},{9,8},{10,11... | collective-permute-start | bytes 1179656 | tf_op jit(solution)/shard_map/ppermute | solution.py:705
  263.0 8.0 %collective-permute-start.28 = (bf16[128,1536]{1,0:T(8,128)(2,1)S(1)}, bf16[128,1536]{1,0:T(8,128)(2,1)S(1)}, u32[]{:S(2)}, u32[]{:S(2)}) collective-permute-start(bf16[128,1536]{1,0:T(8,128)(2,1)S(1)} %get-tuple-element.117), channel_id=1, source_target_pairs={{1,0},{2,1},{3,2},{4,3},{5,4},{6,5},{7,6},{8,7},{9,8},{10,9},{11,1... | collective-permute-start | bytes 1179656 | tf_op jit(solution)/shard_map/ppermute | solution.py:1087
  264.3 6.7 %collective-permute-start.33 = (bf16[128,1536]{1,0:T(8,128)(2,1)S(1)}, bf16[128,1536]{1,0:T(8,128)(2,1)S(1)}, u32[]{:S(2)}, u32[]{:S(2)}) collective-permute-start(bf16[128,1536]{1,0:T(8,128)(2,1)S(1)} %get-tuple-element.131), channel_id=1, source_target_pairs={{0,1},{1,2},{2,3},{3,4},{4,5},{5,6},{6,7},{7,8},{8,9},{9,10},{10,1... | collective-permute-start | bytes 1179656 | tf_op jit(solution)/shard_map/ppermute | solution.py:1088
  275.1 22.5 %collective-permute-start.34 = (bf16[144,2304]{1,0:T(8,128)(2,1)S(1)}, bf16[144,2304]{1,0:T(8,128)(2,1)S(1)}, u32[]{:S(2)}, u32[]{:S(2)}) collective-permute-start(bf16[144,2304]{1,0:T(8,128)(2,1)S(1)} %get-tuple-element.142.refs_0_), channel_id=1, source_target_pairs={{0,2},{1,3},{2,0},{3,1},{4,6},{5,7},{6,4},{7,5},{8,10},{9,11},{10,... | collective-permute-start | bytes 1990664 | tf_op jit(solution)/shard_map/ppermute | solution.py:705
  283.2 16.1 %collective-permute-start.37 = (bf16[264,768]{1,0:T(8,128)(2,1)S(1)}, bf16[264,768]{1,0:T(8,128)(2,1)S(1)}, u32[]{:S(2)}, u32[]{:S(2)}) collective-permute-start(bf16[264,768]{1,0:T(8,128)(2,1)S(1)} %get-tuple-element.141), channel_id=1, source_target_pairs={{0,12},{1,13},{2,14},{3,15},{4,8},{5,9},{6,10},{7,11},{8,4},{9,5},... | collective-permute-start | bytes 1216520 | tf_op jit(solution)/shard_map/ppermute | solution.py:705
  283.6 35.4 %collective-permute-start.36 = (bf16[264,768]{1,0:T(8,128)(2,1)S(1)}, bf16[264,768]{1,0:T(8,128)(2,1)S(1)}, u32[]{:S(2)}, u32[]{:S(2)}) collective-permute-start(bf16[264,768]{1,0:T(8,128)(2,1)S(1)} %get-tuple-element.140), channel_id=1, source_target_pairs={{0,8},{1,9},{2,10},{3,11},{4,12},{5,13},{6,14},{7,15},{8,0},{9,1},... | collective-permute-start | bytes 1216520 | tf_op jit(solution)/shard_map/ppermute | solution.py:705
  286.1 33.0 %collective-permute-start.35 = (bf16[264,768]{1,0:T(8,128)(2,1)S(1)}, bf16[264,768]{1,0:T(8,128)(2,1)S(1)}, u32[]{:S(2)}, u32[]{:S(2)}) collective-permute-start(bf16[264,768]{1,0:T(8,128)(2,1)S(1)} %get-tuple-element.139), channel_id=1, source_target_pairs={{0,4},{1,5},{2,6},{3,7},{4,0},{5,1},{6,2},{7,3},{8,12},{9,13},{10,... | collective-permute-start | bytes 1216520 | tf_op jit(solution)/shard_map/ppermute | solution.py:705
  297.7 23.1 %collective-permute-start.38 = (bf16[288,2304]{1,0:T(8,128)(2,1)S(1)}, bf16[288,2304]{1,0:T(8,128)(2,1)S(1)}, u32[]{:S(2)}, u32[]{:S(2)}) collective-permute-start(bf16[288,2304]{1,0:T(8,128)(2,1)S(1)} %pad_maximum_fusion.1), channel_id=1, source_target_pairs={{0,1},{1,0},{2,3},{3,2},{4,5},{5,4},{6,7},{7,6},{8,9},{9,8},{10,11... | collective-permute-start | bytes 3981320 | tf_op jit(solution)/shard_map/ppermute | solution.py:705
  321.4 10.6 %collective-permute-start.41 = (bf16[48,2432]{1,0:T(8,128)(2,1)S(1)}, bf16[48,2432]{1,0:T(8,128)(2,1)S(1)}, u32[]{:S(2)}, u32[]{:S(2)}) collective-permute-start(bf16[48,2432]{1,0:T(8,128)(2,1)S(1)} %get-tuple-element.147), channel_id=1, source_target_pairs={{0,12},{1,13},{2,14},{3,15},{4,8},{5,9},{6,10},{7,11},{8,4},{9,5},... | collective-permute-start | bytes 700424 | tf_op jit(solution)/shard_map/ppermute | solution.py:705
  323.8 17.7 %collective-permute-start.40 = (bf16[48,2432]{1,0:T(8,128)(2,1)S(1)}, bf16[48,2432]{1,0:T(8,128)(2,1)S(1)}, u32[]{:S(2)}, u32[]{:S(2)}) collective-permute-start(bf16[48,2432]{1,0:T(8,128)(2,1)S(1)} %get-tuple-element.146), channel_id=1, source_target_pairs={{0,8},{1,9},{2,10},{3,11},{4,12},{5,13},{6,14},{7,15},{8,0},{9,1},... | collective-permute-start | bytes 700424 | tf_op jit(solution)/shard_map/ppermute | solution.py:705
  323.8 17.7 %collective-permute-start.39 = (bf16[48,2432]{1,0:T(8,128)(2,1)S(1)}, bf16[48,2432]{1,0:T(8,128)(2,1)S(1)}, u32[]{:S(2)}, u32[]{:S(2)}) collective-permute-start(bf16[48,2432]{1,0:T(8,128)(2,1)S(1)} %get-tuple-element.145), channel_id=1, source_target_pairs={{0,4},{1,5},{2,6},{3,7},{4,0},{5,1},{6,2},{7,3},{8,12},{9,13},{10,... | collective-permute-start | bytes 700424 | tf_op jit(solution)/shard_map/ppermute | solution.py:705
  (55 other events, 557.2 us)
Sparse Core Ops, SparseCore 0:
  23.4 75.5 all-gather.1

commit v13 on v10

--- a/solution.py
+++ b/solution.py
@@ -464,30 +464,31 @@
 
 
 def local_middle_body(*refs):
-    sources, refs = refs[:-10], refs[-10:]
-    x_ref, att_ref, gain_ref, normed_ref, mixed_ref, middle_ref, gate_up_ref = refs[:7]
-    weights = Weights(sources, refs[9])
+    sources, refs = refs[:-8], refs[-8:]
+    x_ref, att_ref, gain_ref, kept_ref, state_ref = refs[:5]
+    weights = Weights(sources, refs[7])
     middle, normed, gate, up, mixed, result = mlp_forward(
         x_ref[...].astype(F32), att_ref[...], gain_ref[...], weights
     )
-    store_chunks(refs[7:9], result)
-    normed_ref[...] = normed
-    mixed_ref[...] = mixed
-    middle_ref[...] = middle
-    half = gate.shape[1]
-    gate_up_ref[:, :half] = gate
-    gate_up_ref[:, half:] = up
+    store_chunks(refs[5:7], result)
+    width, half = middle.shape[1], gate.shape[1]
+    kept_ref[:, :width] = normed
+    kept_ref[:, width:] = mixed
+    state_ref[:, :width] = middle
+    state_ref[:, width : width + half] = gate
+    state_ref[:, width + half :] = up
 
 
 def local_back_middle_body(*refs):
-    sources, refs = refs[:-12], refs[-12:]
-    lower_ref, low_ref, high_ref, middle_ref, gate_up_ref, gain_ref, other_ref = refs[:7]
-    gain_out_ref, d_middle_ref, d_att_ref, right_ref = refs[7:11]
-    weights = Weights(sources, refs[11])
-    half = gate_up_ref.shape[1] // 2
+    sources, refs = refs[:-11], refs[-11:]
+    lower_ref, low_ref, high_ref, state_ref, gain_ref, other_ref = refs[:6]
+    gain_out_ref, d_middle_ref, d_att_ref, right_ref = refs[6:10]
+    weights = Weights(sources, refs[10])
+    width = low_ref.shape[1]
+    half = (state_ref.shape[1] - width) // 2
     upstream = joined([low_ref, high_ref])
     d_gate_up, gain_grad, d_middle, d_attn, d_attended = mlp_backward(
-        upstream, middle_ref[...], gate_up_ref[:, :half], gate_up_ref[:, half:],
+        upstream, state_ref[:, :width], state_ref[:, width : width + half], state_ref[:, width + half :],
         gain_ref[...], weights,
     )
     gain_out_ref[...] = gain_grad
@@ -501,7 +502,7 @@
 
     @pl.when(lower_ref[0] == 0)
     def _():
-        right_ref[...] = other_ref[...]
+        right_ref[...] = other_ref[:, other_ref.shape[1] - right_ref.shape[1] :]
 
 
 def global_project_body(first_ref, low_ref, high_ref, gain_ref, table_ref, normed_ref, sent_ref):
@@ -639,25 +640,22 @@
 
 
 def global_middle_body(*refs):
-    sources, refs = refs[:-14], refs[-14:]
-    got_ref, low_ref, high_ref, up_ref, gain_ref, out_ref, att_ref, normed_ref, mixed_ref = refs[:9]
-    right_ref, gain_out_ref, d_middle_ref, sent_ref = refs[9:13]
-    weights = Weights(sources, refs[13])
-    rows = low_ref.shape[0]
+    sources, refs = refs[:-10], refs[-10:]
+    got_ref, low_ref, high_ref, up_ref, gain_ref, kept_ref, gain_out_ref, d_middle_ref, sent_ref = refs[:9]
+    weights = Weights(sources, refs[9])
+    rows, width = low_ref.shape
     attended = jnp.concatenate([c.astype(BF) for c in unpack_folded(got_ref, 0, rows)], 1)
-    att_ref[...] = attended
     gain = gain_ref[...]
     middle, normed, gate, up, mixed, result = mlp_forward(
         joined([low_ref, high_ref]).astype(F32), attended, gain, weights
     )
-    out_ref[...] = result
-    normed_ref[...] = normed
-    mixed_ref[...] = mixed
     d_gate_up, gain_grad, d_middle, d_attn, d_attended = mlp_backward(
         up_ref[...], middle, gate, up, gain, weights
     )
-    right_ref[:, : d_gate_up.shape[1]] = d_gate_up
-    right_ref[:, d_gate_up.shape[1] :] = d_attn
+    start = 0
+    for part in (result, attended, normed, mixed, d_gate_up, d_attn):
+        kept_ref[:, start : start + part.shape[1]] = part
+        start += part.shape[1]
     gain_out_ref[...] = gain_grad
     d_middle_ref[...] = d_middle
     pack_folded(chunks_of(d_attended), sent_ref, 0)
@@ -734,12 +732,12 @@
     return taken
 
 
-def left_body(lower_ref, place_ref, *refs):
+def left_body(spans, lower_ref, place_ref, *refs):
     refs, out_ref = refs[:-1], refs[-1]
     base = 0
-    for first_ref, second_ref in zip(refs[0::2], refs[1::2]):
-        rows = jnp.where(lower_ref[0] == 1, first_ref[...].astype(F32), second_ref[...].astype(F32))
-        turned = rows.T
+    for span in spans:
+        first, second = (refs[i][:, start:end].astype(F32) for i, start, end in span)
+        turned = jnp.where(lower_ref[0] == 1, first, second).T
         size = turned.shape[0] // GROUP
         for d in range(GROUP):
             side = d % 4 ^ place_ref[0] % 4
@@ -927,14 +925,9 @@
         [((rows, width), BF), ((pairs, 1, LANES), F32)],
         (q_0, *around_0, bias),
     )
-    n2_0, mixed_0, middle_0, gate_up_0, *out_0 = on_core(
+    kept_0, state_0, *out_0 = on_core(
         local_middle_body,
-        [
-            ((rows, width), BF),
-            ((rows, hidden), BF),
-            ((rows, width), F32),
-            ((rows, inner), F32),
-        ]
+        [((rows, width + hidden), BF), ((rows, width + inner), F32)]
         + [((row_count, width), BF)] * micro_count,
         (*others, in_0, att_0, gain_mlp),
         [pltpu.VMEM((hidden, width), BF)],
@@ -970,14 +963,10 @@
     folded = exchange(folded, count)
 
     up_1 = out_grad.reshape(rows, width)
-    out_1, att_1, n2_1, mixed_1, right_1, gain_mlp_1, d_mid_1, sent = on_core(
+    kept_1, gain_mlp_1, d_mid_1, sent = on_core(
         global_middle_body,
         [
-            ((rows, width), BF),
-            ((rows, width), BF),
-            ((rows, width), BF),
-            ((rows, hidden), BF),
-            ((rows, inner + width), BF),
+            ((rows, 4 * width + hidden + inner), BF),
             ((1, width), F32),
             ((rows, width), F32),
             ((GROUP, fold, LANES), BF),
@@ -986,21 +975,33 @@
         [pltpu.VMEM((hidden, width), BF)],
     )
     d_folded = exchange(sent, count)
-    pairs = ((normed_0, normed_1), (att_0, att_1), (n2_0, n2_1), (mixed_0, mixed_1))
+    sources = (normed_0, normed_1, att_0, kept_0, kept_1)
+    cut = 2 * width
+    spans = (
+        ((0, 0, width), (1, 0, width)),
+        ((2, 0, width), (4, width, cut)),
+        ((3, 0, width), (4, cut, cut + width)),
+        ((3, width, width + hidden), (4, cut + width, cut + width + hidden)),
+    )
     left_total = 3 * shard_total + hidden_total
     if count == GROUP:
         (left,) = on_core(
-            left_body,
+            functools.partial(left_body, spans),
             [((4, 4, left_total, rows), BF)],
-            (lower_flag, group_pos[None], *(item for pair in pairs for item in pair)),
+            (lower_flag, group_pos[None], *sources),
             (),
-            [pltpu.SMEM] * 2 + [pltpu.VMEM] * 8,
+            [pltpu.SMEM] * 2 + [pltpu.VMEM] * len(sources),
         )
         left, d_folded = lax.optimization_barrier((left, d_folded))
     else:
         left = [
-            plane_rows(jnp.where(lower, a, b).T.reshape(count, -1, rows), group_pos, count)
-            for a, b in pairs
+            plane_rows(
+                jnp.where(lower, *(sources[i][:, start:end] for i, start, end in span))
+                .T.reshape(count, -1, rows),
+                group_pos,
+                count,
+            )
+            for span in spans
         ]
         left = [jnp.concatenate([i.reshape(4, -1, rows) for i in items], 1) for items in zip(*left)]
     sent, to_beside = on_core(
@@ -1052,9 +1053,9 @@
             ((rows, width), BF),
             ((rows, inner + width), BF),
         ],
-        (*others, lower_flag, *up_0, middle_0, gate_up_0, gain_mlp, right_1),
+        (*others, lower_flag, *up_0, state_0, gain_mlp, kept_1),
         [pltpu.VMEM((hidden, width), BF)],
-        [pltpu.VMEM] * len(others) + [pltpu.SMEM] + [pltpu.VMEM] * 6,
+        [pltpu.VMEM] * len(others) + [pltpu.SMEM] + [pltpu.VMEM] * 5,
     )
     d_att_0, right, across_mlp = lax.optimization_barrier((d_att_0, right, across_mlp))
     across = [partner(right, 2, count)]
@@ -1145,7 +1146,7 @@
         gains = lax.dynamic_slice_in_dim(gains, replica * shard, shard, 1)
 
     return (
-        jnp.where(lower, jnp.concatenate(out_0), out_1).reshape(1, micro_count, row_count, width),
+        jnp.where(lower, jnp.concatenate(out_0), kept_1[:, :width]).reshape(1, micro_count, row_count, width),
         jnp.where(lower, grad_0, jnp.concatenate(grad_1)).reshape(1, micro_count, row_count, width),
         qkv_share[None],
         attn_share[None],

time: 342 us -> 340 us (level)
  local copies, waits for them, and re-layouts: 44.8 us -> 40.6 us
    unnamed x102, local copies, waits for them, and re-layouts: 26.1 us -> 22 us
where the time goes in v13:
time: 340 us; the launch traced here: 338 us
  waiting for transfers between devices  133 us (39%)
  Pallas kernels  56.2 us (17%)
  starting transfers between devices  55.8 us (16%)
  local copies, waits for them, and re-layouts  40.6 us (12%)
  blocking collectives  32.8 us (10%)
  between operations  15 us (4%)
  other arithmetic  5.14 us (2%)
    ppermute x35, waiting for transfers between devices, partner(): return lax.ppermute(rows, 'dp', [(i, i ^ apart) for i in range(count)])  88.1 us
    pallas_call x17, Pallas kernels, on_core(): pl.pallas_call(body, out_shape=[jax.ShapeDtypeStruct(shape, dtype) for sh...  56.2 us
    all_to_all x2, blocking collectives, exchange(): return lax.all_to_all(blocks, 'dp', 0, 0, axis_index_groups=groups)  32.8 us
    ppermute x35, starting transfers between devices, partner(): return lax.ppermute(rows, 'dp', [(i, i ^ apart) for i in range(count)])  32.4 us
    all_gather x1, waiting for transfers between devices, on_device(): others = [lax.all_gather(stacked, 'dp', axis=0, tiled=True)]  28.4 us
    unnamed x102, local copies, waits for them, and re-layouts  22 us
    dynamic_update_slice x16, local copies, waits for them, and re-layouts, gather_rows(): whole = lax.dynamic_update_slice(whole, item[None], start)  11.4 us
    ppermute x4, waiting for transfers between devices, to_other_section(): return [lax.ppermute(rows, 'section', pairs) for rows in chunks]  9.39 us
  transfers between devices with their start and end apart: 46, of which 26 were waited for; matrix products, arithmetic and copies ran while one was open for 6% of the time, Pallas kernels for 7%

profile of v13, /device:TPU:0, one launch (start us, length us, event | category | flops | bytes accessed | tf_op | source)
XLA Modules:
  0.0 338.3 jit_solution(15214947759092336858)
XLA Ops:
  10.3 3.0 collective-permute-start.1
  13.3 1.6 collective-permute-start.2
  14.9 2.6 collective-permute-start.3
  23.5 2.1 broadcast_in_dim.105
  27.5 6.9 %collective-permute-done.3 = bf16[48,2432]{1,0:T(8,128)(2,1)S(1)} collective-permute-done((bf16[48,2432]{1,0:T(8,128)(2,1)S(1)}, bf16[48,2432]{1,0:T(8,128)(2,1)S(1)}, u32[]{:S(2)}, u32[]{:S(2)}) %collective-permute-start.3) | collective-permute-done | bytes 233504 | tf_op jit(solution)/shard_map/ppermute | solution.py:701
  34.9 1.5 collective-permute-start.7
  40.0 5.6 %collective-permute-done.6 = bf16[48,2432]{1,0:T(8,128)(2,1)S(1)} collective-permute-done((bf16[48,2432]{1,0:T(8,128)(2,1)S(1)}, bf16[48,2432]{1,0:T(8,128)(2,1)S(1)}, u32[]{:S(2)}, u32[]{:S(2)}) %collective-permute-start.6) | collective-permute-done | bytes 233504 | tf_op jit(solution)/shard_map/ppermute | solution.py:701
  46.3 3.2 collective-permute-done.7
  56.9 3.1 shard_map.154
  60.7 2.1 collective-permute-start.16
  64.8 1.7 collective-permute-done.17.after_ref
  66.5 3.6 %shard_map.155 = (bf16[128,768]{1,0:T(8,128)(2,1)S(1)}, f32[12,1,128]{2,1,0:T(1,128)S(1)}) custom-call(bf16[128,768]{1,0:T(8,128)(2,1)S(1)} %get-tuple-element.72.q_ref, bf16[128,1536]{1,0:T(8,128)(2,1)S(1)} %collective-permute-done.16.before_ref, bf16[128,1536]{1,0:T(8,128)(2,1)S(1)} %get-tuple-element.73.own_ref, ...), custom_call_target="tpu_custom_call" | custom-call | flops 1024 | bytes 1024 | tf_op jit(solution)/shard_map/pallas_call | solution.py:65
  70.2 28.4 %all-gather.2.cloned.1.call-done.refs_0_ = bf16[768,4352]{1,0:T(8,128)(2,1)} async-done(((bf16[48,4352]{1,0:T(8,128)(2,1)}), bf16[768,4352]{1,0:T(8,128)(2,1)}) %all-gather.2.cloned.1.call-update) | async-done | bytes 6684688 | tf_op jit(solution)/shard_map/all_gather | solution.py:872
  98.6 4.4 %shard_map.156 = (bf16[128,1920]{1,0:T(8,128)(2,1)S(1)}, f32[128,3072]{1,0:T(8,128)S(1)}, bf16[64,768]{1,0:T(8,128)(2,1)S(1)}, bf16[64,768]{1,0:T(8,128)(2,1)S(1)}) custom-call(bf16[768,4352]{1,0:T(8,128)(2,1)} %all-gather.2.cloned.1.call-done.refs_0_, bf16[128,768]{1,0:T(8,128)(2,1)S(1)} %bitcast.90, bf16[128,768]{1,0:T(8,128)(2,1)S(1)} %get-tuple-element.75.refs_2_, ...), custom_call_target="tpu_custom_call" | custom-call | flops 1024 | bytes 1024 | tf_op jit(solution)/shard_map/pallas_call | solution.py:65
  105.1 3.3 collective-permute-start.18
  111.5 1.4 collective-permute-done.19.high_ref.refs_3_
  113.0 3.2 shard_map.157
  116.2 21.0 %all_to_all.20.got_ref = bf16[16,144,128]{2,1,0:T(8,128)(2,1)S(1)} all-to-all(bf16[16,144,128]{2,1,0:T(8,128)(2,1)S(1)} %get-tuple-element.78), channel_id=1, replica_groups={{0,1,2,3,4,5,6,7,8,9,10,11,12,13,14,15},{16,17,18,19,20,21,22,23,24,25,..., dimensions={0} | all-to-all | bytes 1179648 | tf_op jit(solution)/shard_map/all_to_all | solution.py:692
  138.9 6.0 %shard_map.158 = (bf16[16,48,128]{2,1,0:T(8,128)(2,1)S(1)}, f32[6,1,256]{2,1,0:T(1,128)S(1)}) custom-call(bf16[16,144,128]{2,1,0:T(8,128)(2,1)S(1)} %all_to_all.20.got_ref, bf16[16,64,128]{2,1,0:T(8,128)(2,1)S(1)} %collective-permute-done.20.other_ref, s32[1024,1]{1,0:T(8,128)S(1)} %copy.19.own_seg_ref, s32[1024,1]{1,0:T(8,128)S(1)} %copy.20.shared_seg_ref), custom_call_target="tpu_custom_call" | custom-call | flops 1024 | bytes 1024 | tf_op jit(solution)/shard_map/pallas_call | solution.py:65
  144.9 11.8 %all_to_all.21.refs_1_ = bf16[16,48,128]{2,1,0:T(8,128)(2,1)S(1)} all-to-all(bf16[16,48,128]{2,1,0:T(8,128)(2,1)S(1)} %get-tuple-element.79), channel_id=1, replica_groups={{0,1,2,3,4,5,6,7,8,9,10,11,12,13,14,15},{16,17,18,19,20,21,22,23,24,25,..., dimensions={0} | all-to-all | bytes 393216 | tf_op jit(solution)/shard_map/all_to_all | solution.py:692
  159.4 7.0 %shard_map.159 = (bf16[128,6528]{1,0:T(8,128)(2,1)S(1)}, f32[1,768]{1,0:T(1,128)S(1)}, f32[128,768]{1,0:T(8,128)S(1)}, bf16[16,48,128]{2,1,0:T(8,128)(2,1)S(1)}) custom-call(bf16[768,4352]{1,0:T(8,128)(2,1)} %all-gather.2.cloned.1.call-done.refs_0_, bf16[16,48,128]{2,1,0:T(8,128)(2,1)S(1)} %all_to_all.21.refs_1_, bf16[64,768]{1,0:T(8,128)(2,1)S(1)} %copy-done.19, ...), custom_call_target="tpu_custom_call" | custom-call | flops 1024 | bytes 1024 | tf_op jit(solution)/shard_map/pallas_call | solution.py:65
  167.9 4.2 %all-to-all-start.2 = ((bf16[16,48,128]{2,1,0:T(8,128)(2,1)}), bf16[16,48,128]{2,1,0:T(8,128)(2,1)}, u32[]{:S(2)}, u32[]{:S(2)}) async-start(bf16[16,48,128]{2,1,0:T(8,128)(2,1)} %copy-done.36), calls=%async_computation.2 | async-start | bytes 393216 | tf_op jit(solution)/shard_map/all_to_all | solution.py:692
  177.2 3.9 %all-to-all-done.2.d_ref = bf16[16,48,128]{2,1,0:T(8,128)(2,1)} async-done(((bf16[16,48,128]{2,1,0:T(8,128)(2,1)}), bf16[16,48,128]{2,1,0:T(8,128)(2,1)}, u32[]{:S(2)}, u32[]{:S(2)}) %all-to-all-start.2) | async-done | bytes 196640 | tf_op jit(solution)/shard_map/all_to_all | solution.py:692
  182.0 8.2 %shard_map.161 = (bf16[16,144,128]{2,1,0:T(8,128)(2,1)S(1)}, bf16[16,64,128]{2,1,0:T(8,128)(2,1)S(1)}) custom-call(bf16[16,144,128]{2,1,0:T(8,128)(2,1)S(1)} %all_to_all.20.got_ref, bf16[16,64,128]{2,1,0:T(8,128)(2,1)S(1)} %copy-done.17, s32[1024,1]{1,0:T(8,128)S(1)} %copy.19.own_seg_ref, s32[1024,1]{1,0:T(8,128)S(1)} %copy.20.shared_seg_ref, ...), custom_call_target="tpu_custom_call" | custom-call | flops 1024 | bytes 1024 | tf_op jit(solution)/shard_map/pallas_call | solution.py:65
  193.0 4.2 %all-to-all-start.3 = ((bf16[16,144,128]{2,1,0:T(8,128)(2,1)}), bf16[16,144,128]{2,1,0:T(8,128)(2,1)}, u32[]{:S(2)}, u32[]{:S(2)}) async-start(bf16[16,144,128]{2,1,0:T(8,128)(2,1)} %add_convert_fusion), calls=%async_computation.3 | async-start | bytes 1179648 | tf_op jit(solution)/shard_map/all_to_all | solution.py:692
  197.6 1.7 collective-permute-start.23
  199.3 10.9 %collective-permute-done.23.refs_6_ = bf16[4,216,128]{2,1,0:T(8,128)(2,1)S(1)} collective-permute-done((bf16[4,216,128]{2,1,0:T(8,128)(2,1)S(1)}, bf16[4,216,128]{2,1,0:T(8,128)(2,1)S(1)}, u32[]{:S(2)}, u32[]{:S(2)}) %collective-permute-start.23) | collective-permute-done | bytes 221216 | tf_op jit(solution)/shard_map/ppermute | solution.py:701
  210.2 5.3 %collective-permute-done.24.refs_7_ = bf16[4,216,128]{2,1,0:T(8,128)(2,1)S(1)} collective-permute-done((bf16[4,216,128]{2,1,0:T(8,128)(2,1)S(1)}, bf16[4,216,128]{2,1,0:T(8,128)(2,1)S(1)}, u32[]{:S(2)}, u32[]{:S(2)}) %collective-permute-start.24) | collective-permute-done | bytes 221216 | tf_op jit(solution)/shard_map/ppermute | solution.py:701
  219.2 3.9 %shard_map.162 = (bf16[128,2304]{1,0:T(8,128)(2,1)S(1)}, f32[1,768]{1,0:T(1,128)S(1)}, bf16[64,768]{1,0:T(8,128)(2,1)S(1)}, bf16[64,768]{1,0:T(8,128)(2,1)S(1)}) custom-call(bf16[768,2432]{1,0:T(8,128)(2,1)} %bitcast.23.first_ref, bf16[16,144,128]{2,1,0:T(8,128)(2,1)} %all-to-all-done.3.got_ref, f32[128,768]{1,0:T(8,128)S(1)} %copy-done.33, ...), custom_call_target="tpu_custom_call" | custom-call | flops 1024 | bytes 1024 | tf_op jit(solution)/shard_map/pallas_call | solution.py:65
  225.7 4.9 %collective-permute-done.25.refs_2_ = bf16[64,768]{1,0:T(8,128)(2,1)S(1)} collective-permute-done((bf16[64,768]{1,0:T(8,128)(2,1)S(1)}, bf16[64,768]{1,0:T(8,128)(2,1)S(1)}, u32[]{:S(2)}, u32[]{:S(2)}) %collective-permute-start.25) | collective-permute-done | bytes 98336 | tf_op jit(solution)/shard_map/ppermute | solution.py:697
  230.6 1.6 collective-permute-done.26.refs_3_
  232.7 6.1 %shard_map.163 = (f32[1,768]{1,0:T(1,128)S(1)}, f32[128,768]{1,0:T(8,128)S(1)}, bf16[128,768]{1,0:T(8,128)(2,1)S(1)}, bf16[128,3072]{1,0:T(8,128)(2,1)S(1)}) custom-call(bf16[768,4352]{1,0:T(8,128)(2,1)} %all-gather.2.cloned.1.call-done.refs_0_, s32[1]{0:T(128)} %bitcast.37.lower_ref.refs_1_, bf16[64,768]{1,0:T(8,128)(2,1)S(1)} %collective-permute-done.25.refs_2_, ...), custom_call_target="tpu_custom_call" | custom-call | flops 1024 | bytes 1024 | tf_op jit(solution)/shard_map/pallas_call | solution.py:65
  238.8 1.7 collective-permute-start.34
  242.7 1.6 collective-permute-start.31
  244.3 3.5 %shard_map.164 = (bf16[128,768]{1,0:T(8,128)(2,1)S(1)}, f32[128,1536]{1,0:T(8,128)S(1)}, bf16[128,1536]{1,0:T(8,128)(2,1)S(1)}, bf16[128,1536]{1,0:T(8,128)(2,1)S(1)}) custom-call(bf16[128,768]{1,0:T(8,128)(2,1)S(1)} %copy-done.25, bf16[128,1536]{1,0:T(8,128)(2,1)S(1)} %copy-done.11, bf16[128,1536]{1,0:T(8,128)(2,1)S(1)} %copy-done.9, ...), custom_call_target="tpu_custom_call" | custom-call | flops 1024 | bytes 1024 | tf_op jit(solution)/shard_map/pallas_call | solution.py:65
  249.1 3.1 collective-permute-start.32
  253.5 4.0 %shard_map.166 = (bf16[144,2304]{1,0:T(8,128)(2,1)S(1)}, bf16[128,768]{1,0:T(8,128)(2,1)S(1)}, f32[1,768]{1,0:T(1,128)}) custom-call(s32[1]{0:T(128)} %bitcast.37.lower_ref.refs_1_, bf16[768,2432]{1,0:T(8,128)(2,1)} %bitcast.23.first_ref, bf16[128,768]{1,0:T(8,128)(2,1)S(1)} %get-tuple-element.101.dq_ref, f32[128,1536]{1,0:T(8,128)S(1)} %get-tuple-element.102.own_ref, ...), custom_call_target="tpu_custom_call" | custom-call | flops 1024 | bytes 1024 | tf_op jit(solution)/shard_map/pallas_call | solution.py:65
  257.5 5.3 %collective-permute-done.34.refs_2_ = bf16[128,3072]{1,0:T(8,128)(2,1)S(1)} collective-permute-done((bf16[128,3072]{1,0:T(8,128)(2,1)S(1)}, bf16[128,3072]{1,0:T(8,128)(2,1)S(1)}, u32[]{:S(2)}, u32[]{:S(2)}) %collective-permute-start.34) | collective-permute-done | bytes 786464 | tf_op jit(solution)/shard_map/ppermute | solution.py:701
  262.8 6.7 %collective-permute-start.35 = (bf16[128,3072]{1,0:T(8,128)(2,1)S(1)}, bf16[128,3072]{1,0:T(8,128)(2,1)S(1)}, u32[]{:S(2)}, u32[]{:S(2)}) collective-permute-start(bf16[128,3072]{1,0:T(8,128)(2,1)S(1)} %get-tuple-element.121.refs_0_), channel_id=1, source_target_pairs={{0,1},{1,0},{2,3},{3,2},{4,5},{5,4},{6,7},{7,6},{8,9},{9,8},{10,11... | collective-permute-start | bytes 2359304 | tf_op jit(solution)/shard_map/ppermute | solution.py:701
  269.5 1.8 collective-permute-done.35.refs_1_
  273.3 2.1 collective-permute-start.37
  275.5 2.2 collective-permute-start.33
  277.6 11.7 %collective-permute-done.37 = bf16[384,768]{1,0:T(8,128)(2,1)S(1)} collective-permute-done((bf16[384,768]{1,0:T(8,128)(2,1)S(1)}, bf16[384,768]{1,0:T(8,128)(2,1)S(1)}, u32[]{:S(2)}, u32[]{:S(2)}) %collective-permute-start.37) | collective-permute-done | bytes 589856 | tf_op jit(solution)/shard_map/ppermute | solution.py:701
  289.4 3.2 collective-permute-done.33.refs_2_
  293.1 2.3 collective-permute-start.42
  298.1 15.9 %collective-permute-done.42 = bf16[264,768]{1,0:T(8,128)(2,1)S(1)} collective-permute-done((bf16[264,768]{1,0:T(8,128)(2,1)S(1)}, bf16[264,768]{1,0:T(8,128)(2,1)S(1)}, u32[]{:S(2)}, u32[]{:S(2)}) %collective-permute-start.42) | collective-permute-done | bytes 405536 | tf_op jit(solution)/shard_map/ppermute | solution.py:701
  315.6 2.9 collective-permute-done.40
  319.3 10.6 %collective-permute-done.41 = bf16[48,2432]{1,0:T(8,128)(2,1)S(1)} collective-permute-done((bf16[48,2432]{1,0:T(8,128)(2,1)S(1)}, bf16[48,2432]{1,0:T(8,128)(2,1)S(1)}, u32[]{:S(2)}, u32[]{:S(2)}) %collective-permute-start.41) | collective-permute-done | bytes 233504 | tf_op jit(solution)/shard_map/ppermute | solution.py:701
  (244 shorter events, 66.5 us)
Async XLA Ops:
  7.2 91.4 %all-gather.2.cloned.1.call-start = ((), (), s32[]{:S(2)}) async-start(), calls=%async_computation.4 | async-start | bytes 7102464 | tf_op jit(solution)/shard_map/all_gather | solution.py:872
  10.3 13.0 %collective-permute-start.1 = (bf16[48,2432]{1,0:T(8,128)(2,1)S(1)}, bf16[48,2432]{1,0:T(8,128)(2,1)S(1)}, u32[]{:S(2)}, u32[]{:S(2)}) collective-permute-start(bf16[48,2432]{1,0:T(8,128)(2,1)S(1)} %shard_map.153), channel_id=1, source_target_pairs={{0,2},{1,3},{2,0},{3,1},{4,6},{5,7},{6,4},{7,5},{8,10},{9,11},{10,... | collective-permute-start | bytes 700424 | tf_op jit(solution)/shard_map/ppermute | solution.py:701
  13.3 13.9 %collective-permute-start.2 = (bf16[48,2432]{1,0:T(8,128)(2,1)S(1)}, bf16[48,2432]{1,0:T(8,128)(2,1)S(1)}, u32[]{:S(2)}, u32[]{:S(2)}) collective-permute-start(bf16[48,2432]{1,0:T(8,128)(2,1)S(1)} %shard_map.153), channel_id=1, source_target_pairs={{0,4},{1,5},{2,6},{3,7},{4,0},{5,1},{6,2},{7,3},{8,12},{9,13},{10,... | collective-permute-start | bytes 700424 | tf_op jit(solution)/shard_map/ppermute | solution.py:701
  14.9 19.5 %collective-permute-start.3 = (bf16[48,2432]{1,0:T(8,128)(2,1)S(1)}, bf16[48,2432]{1,0:T(8,128)(2,1)S(1)}, u32[]{:S(2)}, u32[]{:S(2)}) collective-permute-start(bf16[48,2432]{1,0:T(8,128)(2,1)S(1)} %shard_map.153), channel_id=1, source_target_pairs={{0,8},{1,9},{2,10},{3,11},{4,12},{5,13},{6,14},{7,15},{8,0},{9,1},... | collective-permute-start | bytes 700424 | tf_op jit(solution)/shard_map/ppermute | solution.py:701
  17.5 17.5 %collective-permute-start.4 = (bf16[48,2432]{1,0:T(8,128)(2,1)S(1)}, bf16[48,2432]{1,0:T(8,128)(2,1)S(1)}, u32[]{:S(2)}, u32[]{:S(2)}) collective-permute-start(bf16[48,2432]{1,0:T(8,128)(2,1)S(1)} %shard_map.153), channel_id=1, source_target_pairs={{0,12},{1,13},{2,14},{3,15},{4,8},{5,9},{6,10},{7,11},{8,4},{9,5},... | collective-permute-start | bytes 700424 | tf_op jit(solution)/shard_map/ppermute | solution.py:701
  18.4 1.2 collective-permute-start
  19.6 30.6 %collective-permute-start.8 = (bf16[48,2432]{1,0:T(8,128)(2,1)S(1)}, bf16[48,2432]{1,0:T(8,128)(2,1)S(1)}, u32[]{:S(2)}, u32[]{:S(2)}) collective-permute-start(bf16[48,2432]{1,0:T(8,128)(2,1)S(1)} %shard_map.153), channel_id=1, source_target_pairs={{0,1},{1,0},{2,3},{3,2},{4,5},{5,4},{6,7},{7,6},{8,9},{9,8},{10,11... | collective-permute-start | bytes 700424 | tf_op jit(solution)/shard_map/ppermute | solution.py:701
  26.8 24.6 %collective-permute-start.9 = (bf16[48,2432]{1,0:T(8,128)(2,1)S(1)}, bf16[48,2432]{1,0:T(8,128)(2,1)S(1)}, u32[]{:S(2)}, u32[]{:S(2)}) collective-permute-start(bf16[48,2432]{1,0:T(8,128)(2,1)S(1)} %collective-permute-done.1), channel_id=1, source_target_pairs={{0,1},{1,0},{2,3},{3,2},{4,5},{5,4},{6,7},{7,6},{8,9},{9,8},{10,11... | collective-permute-start | bytes 700424 | tf_op jit(solution)/shard_map/ppermute | solution.py:701
  27.2 12.1 %collective-permute-start.5 = (bf16[48,2432]{1,0:T(8,128)(2,1)S(1)}, bf16[48,2432]{1,0:T(8,128)(2,1)S(1)}, u32[]{:S(2)}, u32[]{:S(2)}) collective-permute-start(bf16[48,2432]{1,0:T(8,128)(2,1)S(1)} %collective-permute-done.2), channel_id=1, source_target_pairs={{0,2},{1,3},{2,0},{3,1},{4,6},{5,7},{6,4},{7,5},{8,10},{9,11},{10,... | collective-permute-start | bytes 700424 | tf_op jit(solution)/shard_map/ppermute | solution.py:701
  34.4 11.2 %collective-permute-start.6 = (bf16[48,2432]{1,0:T(8,128)(2,1)S(1)}, bf16[48,2432]{1,0:T(8,128)(2,1)S(1)}, u32[]{:S(2)}, u32[]{:S(2)}) collective-permute-start(bf16[48,2432]{1,0:T(8,128)(2,1)S(1)} %collective-permute-done.3), channel_id=1, source_target_pairs={{0,2},{1,3},{2,0},{3,1},{4,6},{5,7},{6,4},{7,5},{8,10},{9,11},{10,... | collective-permute-start | bytes 700424 | tf_op jit(solution)/shard_map/ppermute | solution.py:701
  34.9 14.5 %collective-permute-start.7 = (bf16[48,2432]{1,0:T(8,128)(2,1)S(1)}, bf16[48,2432]{1,0:T(8,128)(2,1)S(1)}, u32[]{:S(2)}, u32[]{:S(2)}) collective-permute-start(bf16[48,2432]{1,0:T(8,128)(2,1)S(1)} %collective-permute-done.4), channel_id=1, source_target_pairs={{0,2},{1,3},{2,0},{3,1},{4,6},{5,7},{6,4},{7,5},{8,10},{9,11},{10,... | collective-permute-start | bytes 700424 | tf_op jit(solution)/shard_map/ppermute | solution.py:701
  39.3 12.8 %collective-permute-start.10 = (bf16[48,2432]{1,0:T(8,128)(2,1)S(1)}, bf16[48,2432]{1,0:T(8,128)(2,1)S(1)}, u32[]{:S(2)}, u32[]{:S(2)}) collective-permute-start(bf16[48,2432]{1,0:T(8,128)(2,1)S(1)} %collective-permute-done.2), channel_id=1, source_target_pairs={{0,1},{1,0},{2,3},{3,2},{4,5},{5,4},{6,7},{7,6},{8,9},{9,8},{10,11... | collective-permute-start | bytes 700424 | tf_op jit(solution)/shard_map/ppermute | solution.py:701
  45.6 8.5 %collective-permute-start.12 = (bf16[48,2432]{1,0:T(8,128)(2,1)S(1)}, bf16[48,2432]{1,0:T(8,128)(2,1)S(1)}, u32[]{:S(2)}, u32[]{:S(2)}) collective-permute-start(bf16[48,2432]{1,0:T(8,128)(2,1)S(1)} %collective-permute-done.3), channel_id=1, source_target_pairs={{0,1},{1,0},{2,3},{3,2},{4,5},{5,4},{6,7},{7,6},{8,9},{9,8},{10,11... | collective-permute-start | bytes 700424 | tf_op jit(solution)/shard_map/ppermute | solution.py:701
  49.5 6.0 %collective-permute-start.14 = (bf16[48,2432]{1,0:T(8,128)(2,1)S(1)}, bf16[48,2432]{1,0:T(8,128)(2,1)S(1)}, u32[]{:S(2)}, u32[]{:S(2)}) collective-permute-start(bf16[48,2432]{1,0:T(8,128)(2,1)S(1)} %collective-permute-done.4), channel_id=1, source_target_pairs={{0,1},{1,0},{2,3},{3,2},{4,5},{5,4},{6,7},{7,6},{8,9},{9,8},{10,11... | collective-permute-start | bytes 700424 | tf_op jit(solution)/shard_map/ppermute | solution.py:701
  50.2 3.2 collective-permute-start.11
  51.4 3.4 collective-permute-start.13
  52.2 4.0 %collective-permute-start.15 = (bf16[48,2432]{1,0:T(8,128)(2,1)S(1)}, bf16[48,2432]{1,0:T(8,128)(2,1)S(1)}, u32[]{:S(2)}, u32[]{:S(2)}) collective-permute-start(bf16[48,2432]{1,0:T(8,128)(2,1)S(1)} %collective-permute-done.7), channel_id=1, source_target_pairs={{0,1},{1,0},{2,3},{3,2},{4,5},{5,4},{6,7},{7,6},{8,9},{9,8},{10,11... | collective-permute-start | bytes 700424 | tf_op jit(solution)/shard_map/ppermute | solution.py:701
  60.7 42.3 %copy-start.8 = (bf16[128,1536]{1,0:T(8,128)(2,1)}, bf16[128,1536]{1,0:T(8,128)(2,1)S(1)}, u32[]{:S(2)}) copy-start(bf16[128,1536]{1,0:T(8,128)(2,1)S(1)} %get-tuple-element.73.own_ref) | copy-start | bytes 1179652
  60.7 42.3 %copy-start.24 = (bf16[128,768]{1,0:T(8,128)(2,1)}, bf16[128,768]{1,0:T(8,128)(2,1)S(1)}, u32[]{:S(2)}) copy-start(bf16[128,768]{1,0:T(8,128)(2,1)S(1)} %get-tuple-element.72.q_ref) | copy-start | bytes 589828
  60.7 4.1 %collective-permute-start.16 = (bf16[128,1536]{1,0:T(8,128)(2,1)S(1)}, bf16[128,1536]{1,0:T(8,128)(2,1)S(1)}, u32[]{:S(2)}, u32[]{:S(2)}) collective-permute-start(bf16[128,1536]{1,0:T(8,128)(2,1)S(1)} %get-tuple-element.73.own_ref), channel_id=1, source_target_pairs={{0,1},{1,2},{2,3},{3,4},{4,5},{5,6},{6,7},{7,8},{8,9},{9,10},{10,1... | collective-permute-start | bytes 1179656 | tf_op jit(solution)/shard_map/ppermute | solution.py:919
  62.9 3.7 %collective-permute-start.17 = (bf16[128,1536]{1,0:T(8,128)(2,1)S(1)}, bf16[128,1536]{1,0:T(8,128)(2,1)S(1)}, u32[]{:S(2)}, u32[]{:S(2)}) collective-permute-start(bf16[128,1536]{1,0:T(8,128)(2,1)S(1)} %get-tuple-element.73.own_ref), channel_id=1, source_target_pairs={{1,0},{2,1},{3,2},{4,3},{5,4},{6,5},{7,6},{8,7},{9,8},{10,9},{11,1... | collective-permute-start | bytes 1179656 | tf_op jit(solution)/shard_map/ppermute | solution.py:921
  105.1 6.5 %collective-permute-start.18 = (bf16[64,768]{1,0:T(8,128)(2,1)S(1)}, bf16[64,768]{1,0:T(8,128)(2,1)S(1)}, u32[]{:S(2)}, u32[]{:S(2)}) collective-permute-start(bf16[64,768]{1,0:T(8,128)(2,1)S(1)} %get-tuple-element.76), channel_id=1, source_target_pairs={{0,16},{1,17},{2,18},{3,19},{4,20},{5,21},{6,22},{7,23},{8,24},{9,... | collective-permute-start | bytes 294920 | tf_op jit(solution)/shard_map/ppermute | solution.py:697
  108.4 4.6 %collective-permute-start.19 = (bf16[64,768]{1,0:T(8,128)(2,1)S(1)}, bf16[64,768]{1,0:T(8,128)(2,1)S(1)}, u32[]{:S(2)}, u32[]{:S(2)}) collective-permute-start(bf16[64,768]{1,0:T(8,128)(2,1)S(1)} %get-tuple-element.77), channel_id=1, source_target_pairs={{0,16},{1,17},{2,18},{3,19},{4,20},{5,21},{6,22},{7,23},{8,24},{9,... | collective-permute-start | bytes 294920 | tf_op jit(solution)/shard_map/ppermute | solution.py:697
  137.3 1.6 collective-permute-start.20
  167.9 13.2 %all-to-all-start.2 = ((bf16[16,48,128]{2,1,0:T(8,128)(2,1)}), bf16[16,48,128]{2,1,0:T(8,128)(2,1)}, u32[]{:S(2)}, u32[]{:S(2)}) async-start(bf16[16,48,128]{2,1,0:T(8,128)(2,1)} %copy-done.36), calls=%async_computation.2 | async-start | bytes 393216 | tf_op jit(solution)/shard_map/all_to_all | solution.py:692
  190.3 1.6 collective-permute-start.21
  193.0 22.5 %all-to-all-start.3 = ((bf16[16,144,128]{2,1,0:T(8,128)(2,1)}), bf16[16,144,128]{2,1,0:T(8,128)(2,1)}, u32[]{:S(2)}, u32[]{:S(2)}) async-start(bf16[16,144,128]{2,1,0:T(8,128)(2,1)} %add_convert_fusion), calls=%async_computation.3 | async-start | bytes 1179648 | tf_op jit(solution)/shard_map/all_to_all | solution.py:692
  197.3 2.0 collective-permute-start.22
  197.6 12.6 %collective-permute-start.23 = (bf16[4,216,128]{2,1,0:T(8,128)(2,1)S(1)}, bf16[4,216,128]{2,1,0:T(8,128)(2,1)S(1)}, u32[]{:S(2)}, u32[]{:S(2)}) collective-permute-start(bf16[4,216,128]{2,1,0:T(8,128)(2,1)S(1)} %get-tuple-element.139), channel_id=1, source_target_pairs={{0,2},{1,3},{2,0},{3,1},{4,6},{5,7},{6,4},{7,5},{8,10},{9,11},{10,... | collective-permute-start | bytes 663560 | tf_op jit(solution)/shard_map/ppermute | solution.py:701
  199.3 16.2 %collective-permute-start.24 = (bf16[4,216,128]{2,1,0:T(8,128)(2,1)S(1)}, bf16[4,216,128]{2,1,0:T(8,128)(2,1)S(1)}, u32[]{:S(2)}, u32[]{:S(2)}) collective-permute-start(bf16[4,216,128]{2,1,0:T(8,128)(2,1)S(1)} %get-tuple-element.138), channel_id=1, source_target_pairs={{0,3},{1,2},{2,1},{3,0},{4,7},{5,6},{6,5},{7,4},{8,11},{9,10},{10,... | collective-permute-start | bytes 663560 | tf_op jit(solution)/shard_map/ppermute | solution.py:701
  223.1 7.5 %collective-permute-start.25 = (bf16[64,768]{1,0:T(8,128)(2,1)S(1)}, bf16[64,768]{1,0:T(8,128)(2,1)S(1)}, u32[]{:S(2)}, u32[]{:S(2)}) collective-permute-start(bf16[64,768]{1,0:T(8,128)(2,1)S(1)} %get-tuple-element.95), channel_id=1, source_target_pairs={{16,0},{17,1},{18,2},{19,3},{20,4},{21,5},{22,6},{23,7},{24,8},{25... | collective-permute-start | bytes 294920 | tf_op jit(solution)/shard_map/ppermute | solution.py:697
  224.4 7.8 %collective-permute-start.26 = (bf16[64,768]{1,0:T(8,128)(2,1)S(1)}, bf16[64,768]{1,0:T(8,128)(2,1)S(1)}, u32[]{:S(2)}, u32[]{:S(2)}) collective-permute-start(bf16[64,768]{1,0:T(8,128)(2,1)S(1)} %get-tuple-element.96), channel_id=1, source_target_pairs={{16,0},{17,1},{18,2},{19,3},{20,4},{21,5},{22,6},{23,7},{24,8},{25... | collective-permute-start | bytes 294920 | tf_op jit(solution)/shard_map/ppermute | solution.py:697
  232.3 6.6 %collective-permute-start.27 = (bf16[128,768]{1,0:T(8,128)(2,1)S(1)}, bf16[128,768]{1,0:T(8,128)(2,1)S(1)}, u32[]{:S(2)}, u32[]{:S(2)}) collective-permute-start(bf16[128,768]{1,0:T(8,128)(2,1)S(1)} %pad_maximum_fusion.2.refs_0_), channel_id=1, source_target_pairs={{0,2},{1,3},{2,0},{3,1},{4,6},{5,7},{6,4},{7,5},{8,10},{9,11},{10,... | collective-permute-start | bytes 589832 | tf_op jit(solution)/shard_map/ppermute | solution.py:701
  238.8 23.9 %collective-permute-start.34 = (bf16[128,3072]{1,0:T(8,128)(2,1)S(1)}, bf16[128,3072]{1,0:T(8,128)(2,1)S(1)}, u32[]{:S(2)}, u32[]{:S(2)}) collective-permute-start(bf16[128,3072]{1,0:T(8,128)(2,1)S(1)} %get-tuple-element.121.refs_0_), channel_id=1, source_target_pairs={{0,2},{1,3},{2,0},{3,1},{4,6},{5,7},{6,4},{7,5},{8,10},{9,11},{10,... | collective-permute-start | bytes 2359304 | tf_op jit(solution)/shard_map/ppermute | solution.py:701
  240.6 1.4 collective-permute-start.29
  240.6 1.7 collective-permute-start.30
  242.7 9.5 %collective-permute-start.31 = (bf16[144,768]{1,0:T(8,128)(2,1)S(1)}, bf16[144,768]{1,0:T(8,128)(2,1)S(1)}, u32[]{:S(2)}, u32[]{:S(2)}) collective-permute-start(bf16[144,768]{1,0:T(8,128)(2,1)S(1)} %get-tuple-element.110), channel_id=1, source_target_pairs={{0,4},{1,5},{2,6},{3,7},{4,0},{5,1},{6,2},{7,3},{8,12},{9,13},{10,... | collective-permute-start | bytes 663560 | tf_op jit(solution)/shard_map/ppermute | solution.py:701
  247.8 4.4 %collective-permute-start.28 = (bf16[128,1536]{1,0:T(8,128)(2,1)S(1)}, bf16[128,1536]{1,0:T(8,128)(2,1)S(1)}, u32[]{:S(2)}, u32[]{:S(2)}) collective-permute-start(bf16[128,1536]{1,0:T(8,128)(2,1)S(1)} %get-tuple-element.103), channel_id=1, source_target_pairs={{1,0},{2,1},{3,2},{4,3},{5,4},{6,5},{7,6},{8,7},{9,8},{10,9},{11,1... | collective-permute-start | bytes 1179656 | tf_op jit(solution)/shard_map/ppermute | solution.py:1081
  249.1 4.4 %collective-permute-start.32 = (bf16[128,1536]{1,0:T(8,128)(2,1)S(1)}, bf16[128,1536]{1,0:T(8,128)(2,1)S(1)}, u32[]{:S(2)}, u32[]{:S(2)}) collective-permute-start(bf16[128,1536]{1,0:T(8,128)(2,1)S(1)} %get-tuple-element.112), channel_id=1, source_target_pairs={{0,1},{1,2},{2,3},{3,4},{4,5},{5,6},{6,7},{7,8},{8,9},{9,10},{10,1... | collective-permute-start | bytes 1179656 | tf_op jit(solution)/shard_map/ppermute | solution.py:1082
  262.8 8.6 %collective-permute-start.35 = (bf16[128,3072]{1,0:T(8,128)(2,1)S(1)}, bf16[128,3072]{1,0:T(8,128)(2,1)S(1)}, u32[]{:S(2)}, u32[]{:S(2)}) collective-permute-start(bf16[128,3072]{1,0:T(8,128)(2,1)S(1)} %get-tuple-element.121.refs_0_), channel_id=1, source_target_pairs={{0,1},{1,0},{2,3},{3,2},{4,5},{5,4},{6,7},{7,6},{8,9},{9,8},{10,11... | collective-permute-start | bytes 2359304 | tf_op jit(solution)/shard_map/ppermute | solution.py:701
  269.5 3.0 collective-permute-start.36
  273.3 16.0 %collective-permute-start.37 = (bf16[384,768]{1,0:T(8,128)(2,1)S(1)}, bf16[384,768]{1,0:T(8,128)(2,1)S(1)}, u32[]{:S(2)}, u32[]{:S(2)}) collective-permute-start(bf16[384,768]{1,0:T(8,128)(2,1)S(1)} %get-tuple-element.124), channel_id=1, source_target_pairs={{0,4},{1,5},{2,6},{3,7},{4,0},{5,1},{6,2},{7,3},{8,12},{9,13},{10,... | collective-permute-start | bytes 1769480 | tf_op jit(solution)/shard_map/ppermute | solution.py:701
  275.5 17.1 %collective-permute-start.33 = (bf16[144,2304]{1,0:T(8,128)(2,1)S(1)}, bf16[144,2304]{1,0:T(8,128)(2,1)S(1)}, u32[]{:S(2)}, u32[]{:S(2)}) collective-permute-start(bf16[144,2304]{1,0:T(8,128)(2,1)S(1)} %get-tuple-element.126.refs_0_), channel_id=1, source_target_pairs={{0,2},{1,3},{2,0},{3,1},{4,6},{5,7},{6,4},{7,5},{8,10},{9,11},{10,... | collective-permute-start | bytes 1990664 | tf_op jit(solution)/shard_map/ppermute | solution.py:701
  292.6 4.3 %collective-permute-start.38 = (bf16[144,2304]{1,0:T(8,128)(2,1)S(1)}, bf16[144,2304]{1,0:T(8,128)(2,1)S(1)}, u32[]{:S(2)}, u32[]{:S(2)}) collective-permute-start(bf16[144,2304]{1,0:T(8,128)(2,1)S(1)} %get-tuple-element.126.refs_0_), channel_id=1, source_target_pairs={{0,1},{1,0},{2,3},{3,2},{4,5},{5,4},{6,7},{7,6},{8,9},{9,8},{10,11... | collective-permute-start | bytes 1990664 | tf_op jit(solution)/shard_map/ppermute | solution.py:701
  292.6 4.3 %collective-permute-start.39 = (bf16[144,2304]{1,0:T(8,128)(2,1)S(1)}, bf16[144,2304]{1,0:T(8,128)(2,1)S(1)}, u32[]{:S(2)}, u32[]{:S(2)}) collective-permute-start(bf16[144,2304]{1,0:T(8,128)(2,1)S(1)} %collective-permute-done.33.refs_2_), channel_id=1, source_target_pairs={{0,1},{1,0},{2,3},{3,2},{4,5},{5,4},{6,7},{7,6},{8,9},{9,8},{10,11... | collective-permute-start | bytes 1990664 | tf_op jit(solution)/shard_map/ppermute | solution.py:701
  293.1 20.9 %collective-permute-start.42 = (bf16[264,768]{1,0:T(8,128)(2,1)S(1)}, bf16[264,768]{1,0:T(8,128)(2,1)S(1)}, u32[]{:S(2)}, u32[]{:S(2)}) collective-permute-start(bf16[264,768]{1,0:T(8,128)(2,1)S(1)} %pad_maximum_fusion), channel_id=1, source_target_pairs={{0,8},{1,9},{2,10},{3,11},{4,12},{5,13},{6,14},{7,15},{8,0},{9,1},... | collective-permute-start | bytes 1216520 | tf_op jit(solution)/shard_map/ppermute | solution.py:701
  297.5 21.0 %collective-permute-start.40 = (bf16[96,2432]{1,0:T(8,128)(2,1)S(1)}, bf16[96,2432]{1,0:T(8,128)(2,1)S(1)}, u32[]{:S(2)}, u32[]{:S(2)}) collective-permute-start(bf16[96,2432]{1,0:T(8,128)(2,1)S(1)} %get-tuple-element.129), channel_id=1, source_target_pairs={{0,4},{1,5},{2,6},{3,7},{4,0},{5,1},{6,2},{7,3},{8,12},{9,13},{10,... | collective-permute-start | bytes 1400840 | tf_op jit(solution)/shard_map/ppermute | solution.py:701
  318.5 11.4 %collective-permute-start.41 = (bf16[48,2432]{1,0:T(8,128)(2,1)S(1)}, bf16[48,2432]{1,0:T(8,128)(2,1)S(1)}, u32[]{:S(2)}, u32[]{:S(2)}) collective-permute-start(bf16[48,2432]{1,0:T(8,128)(2,1)S(1)} %add_convert_fusion.2), channel_id=1, source_target_pairs={{0,8},{1,9},{2,10},{3,11},{4,12},{5,13},{6,14},{7,15},{8,0},{9,1},... | collective-permute-start | bytes 700424 | tf_op jit(solution)/shard_map/ppermute | solution.py:701
  (49 other events, 561.0 us)
Sparse Core Ops, SparseCore 0:
  23.4 75.1 all-gather.1

commit v14 on v13

--- a/solution.py
+++ b/solution.py
@@ -75,7 +75,9 @@
         cost_estimate=pl.CostEstimate(
             flops=2**10, bytes_accessed=2**10, transcendentals=0
         ),
-        compiler_params=pltpu.CompilerParams(vmem_limit_bytes=48 * 2**20),
+        compiler_params=pltpu.CompilerParams(
+            vmem_limit_bytes=(60 if body in LARGE else 48) * 2**20
+        ),
     )(*args)
 
 
@@ -677,6 +679,15 @@
         grad_refs,
         input_backward(d_middle_ref[...], d_projected, x, gain_ref, first_ref, gain_out_ref),
     )
+
+
+LARGE = (
+    message_body,
+    stack_body,
+    local_middle_body,
+    global_middle_body,
+    global_finish_body,
+)
 
 
 def neighbours(count, step):

time: 340 us -> 332 us (0.976)
  local copies, waits for them, and re-layouts: 40.6 us -> 27 us
  Pallas kernels: 56.2 us -> 62.4 us
    unnamed x102 -> x78, local copies, waits for them, and re-layouts: 22 us -> 7.61 us
    pallas_call x17, Pallas kernels: 56.2 us -> 62.4 us  [on_core(): pl.pallas_call(body, out_shape=[jax.ShapeDtypeStruct(shape, dtype) for sh...]
  transfers between devices with their start and end apart: 46 -> 46, of which waited for: 26 -> 26; matrix products, arithmetic and copies ran while one was open for 6% -> 7% of each run, Pallas kernels for 7% -> 7%
where the time goes in v14:
time: 332 us; the launch traced here: 331 us
  waiting for transfers between devices  130 us (39%)
  Pallas kernels  62.4 us (19%)
  starting transfers between devices  55.9 us (17%)
  blocking collectives  35.9 us (11%)
  local copies, waits for them, and re-layouts  27 us (8%)
  between operations  14.8 us (4%)
  other arithmetic  5.12 us (2%)
    ppermute x35, waiting for transfers between devices, partner(): return lax.ppermute(rows, 'dp', [(i, i ^ apart) for i in range(count)])  88.2 us
    pallas_call x17, Pallas kernels, on_core(): pl.pallas_call(body, out_shape=[jax.ShapeDtypeStruct(shape, dtype) for sh...  62.4 us
    all_to_all x2, blocking collectives, exchange(): return lax.all_to_all(blocks, 'dp', 0, 0, axis_index_groups=groups)  35.9 us
    ppermute x35, starting transfers between devices, partner(): return lax.ppermute(rows, 'dp', [(i, i ^ apart) for i in range(count)])  32.1 us
    all_gather x1, waiting for transfers between devices, on_device(): others = [lax.all_gather(stacked, 'dp', axis=0, tiled=True)]  25 us
    dynamic_update_slice x16, local copies, waits for them, and re-layouts, gather_rows(): whole = lax.dynamic_update_slice(whole, item[None], start)  11.4 us
    ppermute x4, waiting for transfers between devices, to_other_section(): return [lax.ppermute(rows, 'section', pairs) for rows in chunks]  9.81 us
    all_to_all x2, starting transfers between devices, exchange(): return lax.all_to_all(blocks, 'dp', 0, 0, axis_index_groups=groups)  8.56 us
  transfers between devices with their start and end apart: 46, of which 26 were waited for; matrix products, arithmetic and copies ran while one was open for 7% of the time, Pallas kernels for 7%

profile of v14, /device:TPU:0, one launch (start us, length us, event | category | flops | bytes accessed | tf_op | source)
XLA Modules:
  0.0 330.9 jit_solution(13978098819544432355)
XLA Ops:
  7.2 1.8 shard_map.153
  9.0 2.9 collective-permute-start.1
  12.0 1.6 collective-permute-start.2
  13.5 2.6 collective-permute-start.3
  18.8 1.8 shard_map.152
  20.9 2.1 broadcast_in_dim.105
  24.9 8.4 %collective-permute-done.3 = bf16[48,2432]{1,0:T(8,128)(2,1)S(1)} collective-permute-done((bf16[48,2432]{1,0:T(8,128)(2,1)}, bf16[48,2432]{1,0:T(8,128)(2,1)S(1)}, u32[]{:S(2)}, u32[]{:S(2)}) %collective-permute-start.3) | collective-permute-done | bytes 233504 | tf_op jit(solution)/shard_map/ppermute | solution.py:712
  38.9 4.6 %collective-permute-done.6 = bf16[48,2432]{1,0:T(8,128)(2,1)S(1)} collective-permute-done((bf16[48,2432]{1,0:T(8,128)(2,1)S(1)}, bf16[48,2432]{1,0:T(8,128)(2,1)S(1)}, u32[]{:S(2)}, u32[]{:S(2)}) %collective-permute-start.6) | collective-permute-done | bytes 233504 | tf_op jit(solution)/shard_map/ppermute | solution.py:712
  44.2 2.8 collective-permute-done.7
  54.4 3.6 %shard_map.154 = (f32[8,768]{1,0:T(8,128)S(1)}, bf16[128,768]{1,0:T(8,128)(2,1)S(1)}, bf16[128,768]{1,0:T(8,128)(2,1)S(1)}, bf16[128,1536]{1,0:T(8,128)(2,1)S(1)}) custom-call(bf16[768,2432]{1,0:T(8,128)(2,1)} %bitcast.23.first_ref, bf16[128,768]{1,0:T(8,128)(2,1)S(1)} %bitcast.90, f32[3,128,128]{2,1,0:T(8,128)S(1)} %tile.13.table_ref), custom_call_target="tpu_custom_call" | custom-call | flops 1024 | bytes 1024 | tf_op jit(solution)/shard_map/pallas_call | solution.py:65
  58.7 2.2 collective-permute-start.16
  64.6 3.6 %shard_map.155 = (bf16[128,768]{1,0:T(8,128)(2,1)S(1)}, f32[12,1,128]{2,1,0:T(1,128)S(1)}) custom-call(bf16[128,768]{1,0:T(8,128)(2,1)S(1)} %get-tuple-element.72.q_ref, bf16[128,1536]{1,0:T(8,128)(2,1)S(1)} %collective-permute-done.16.before_ref, bf16[128,1536]{1,0:T(8,128)(2,1)S(1)} %get-tuple-element.73.own_ref, ...), custom_call_target="tpu_custom_call" | custom-call | flops 1024 | bytes 1024 | tf_op jit(solution)/shard_map/pallas_call | solution.py:65
  68.9 25.0 %all-gather.2.cloned.1.call-done.refs_0_ = bf16[768,4352]{1,0:T(8,128)(2,1)} async-done(((bf16[48,4352]{1,0:T(8,128)(2,1)}), bf16[768,4352]{1,0:T(8,128)(2,1)}) %all-gather.2.cloned.1.call-update) | async-done | bytes 6684688 | tf_op jit(solution)/shard_map/all_gather | solution.py:883
  93.9 5.5 %shard_map.156 = (bf16[128,1920]{1,0:T(8,128)(2,1)}, f32[128,3072]{1,0:T(8,128)}, bf16[64,768]{1,0:T(8,128)(2,1)}, bf16[64,768]{1,0:T(8,128)(2,1)}) custom-call(bf16[768,4352]{1,0:T(8,128)(2,1)} %all-gather.2.cloned.1.call-done.refs_0_, bf16[128,768]{1,0:T(8,128)(2,1)} %bitcast.89, bf16[128,768]{1,0:T(8,128)(2,1)} %copy-done.18, ...), custom_call_target="tpu_custom_call" | custom-call | flops 1024 | bytes 1024 | tf_op jit(solution)/shard_map/pallas_call | solution.py:65
  99.4 3.5 %collective-permute-start.18 = (bf16[64,768]{1,0:T(8,128)(2,1)}, bf16[64,768]{1,0:T(8,128)(2,1)S(1)}, u32[]{:S(2)}, u32[]{:S(2)}) collective-permute-start(bf16[64,768]{1,0:T(8,128)(2,1)} %get-tuple-element.76), channel_id=1, source_target_pairs={{0,16},{1,17},{2,18},{3,19},{4,20},{5,21},{6,22},{7,23},{8,24},{9,... | collective-permute-start | bytes 294920 | tf_op jit(solution)/shard_map/ppermute | solution.py:708
  104.6 1.8 collective-permute-done.18.low_ref.refs_2_
  107.8 3.2 shard_map.157
  111.0 23.6 %all_to_all.20.got_ref = bf16[16,144,128]{2,1,0:T(8,128)(2,1)S(1)} all-to-all(bf16[16,144,128]{2,1,0:T(8,128)(2,1)S(1)} %get-tuple-element.78), channel_id=1, replica_groups={{0,1,2,3,4,5,6,7,8,9,10,11,12,13,14,15},{16,17,18,19,20,21,22,23,24,25,..., dimensions={0} | all-to-all | bytes 1179648 | tf_op jit(solution)/shard_map/all_to_all | solution.py:703
  136.3 6.0 %shard_map.158 = (bf16[16,48,128]{2,1,0:T(8,128)(2,1)S(1)}, f32[6,1,256]{2,1,0:T(1,128)S(1)}) custom-call(bf16[16,144,128]{2,1,0:T(8,128)(2,1)S(1)} %all_to_all.20.got_ref, bf16[16,64,128]{2,1,0:T(8,128)(2,1)S(1)} %collective-permute-done.20.other_ref, s32[1024,1]{1,0:T(8,128)S(1)} %copy.19.own_seg_ref, s32[1024,1]{1,0:T(8,128)S(1)} %copy.20.shared_seg_ref), custom_call_target="tpu_custom_call" | custom-call | flops 1024 | bytes 1024 | tf_op jit(solution)/shard_map/pallas_call | solution.py:65
  142.4 12.3 %all_to_all.21.refs_1_ = bf16[16,48,128]{2,1,0:T(8,128)(2,1)} all-to-all(bf16[16,48,128]{2,1,0:T(8,128)(2,1)S(1)} %get-tuple-element.79), channel_id=1, replica_groups={{0,1,2,3,4,5,6,7,8,9,10,11,12,13,14,15},{16,17,18,19,20,21,22,23,24,25,..., dimensions={0} | all-to-all | bytes 393216 | tf_op jit(solution)/shard_map/all_to_all | solution.py:703
  154.6 7.9 %shard_map.159 = (bf16[128,6528]{1,0:T(8,128)(2,1)}, f32[1,768]{1,0:T(1,128)}, f32[128,768]{1,0:T(8,128)}, bf16[16,48,128]{2,1,0:T(8,128)(2,1)}) custom-call(bf16[768,4352]{1,0:T(8,128)(2,1)} %all-gather.2.cloned.1.call-done.refs_0_, bf16[16,48,128]{2,1,0:T(8,128)(2,1)} %all_to_all.21.refs_1_, bf16[64,768]{1,0:T(8,128)(2,1)} %copy-done.14, ...), custom_call_target="tpu_custom_call" | custom-call | flops 1024 | bytes 1024 | tf_op jit(solution)/shard_map/pallas_call | solution.py:65
  162.6 4.3 %all-to-all-start.2 = ((bf16[16,48,128]{2,1,0:T(8,128)(2,1)}), bf16[16,48,128]{2,1,0:T(8,128)(2,1)}, u32[]{:S(2)}, u32[]{:S(2)}) async-start(bf16[16,48,128]{2,1,0:T(8,128)(2,1)} %get-tuple-element.85), calls=%async_computation.2 | async-start | bytes 393216 | tf_op jit(solution)/shard_map/all_to_all | solution.py:703
  171.6 4.3 %all-to-all-done.2.d_ref = bf16[16,48,128]{2,1,0:T(8,128)(2,1)} async-done(((bf16[16,48,128]{2,1,0:T(8,128)(2,1)}), bf16[16,48,128]{2,1,0:T(8,128)(2,1)}, u32[]{:S(2)}, u32[]{:S(2)}) %all-to-all-start.2) | async-done | bytes 196640 | tf_op jit(solution)/shard_map/all_to_all | solution.py:703
  175.9 8.2 %shard_map.161 = (bf16[16,144,128]{2,1,0:T(8,128)(2,1)S(1)}, bf16[16,64,128]{2,1,0:T(8,128)(2,1)S(1)}) custom-call(bf16[16,144,128]{2,1,0:T(8,128)(2,1)S(1)} %all_to_all.20.got_ref, bf16[16,64,128]{2,1,0:T(8,128)(2,1)S(1)} %copy-done.13, s32[1024,1]{1,0:T(8,128)S(1)} %copy.19.own_seg_ref, s32[1024,1]{1,0:T(8,128)S(1)} %copy.20.shared_seg_ref, ...), custom_call_target="tpu_custom_call" | custom-call | flops 1024 | bytes 1024 | tf_op jit(solution)/shard_map/pallas_call | solution.py:65
  186.9 4.2 %all-to-all-start.3 = ((bf16[16,144,128]{2,1,0:T(8,128)(2,1)}), bf16[16,144,128]{2,1,0:T(8,128)(2,1)}, u32[]{:S(2)}, u32[]{:S(2)}) async-start(bf16[16,144,128]{2,1,0:T(8,128)(2,1)} %add_convert_fusion), calls=%async_computation.3 | async-start | bytes 1179648 | tf_op jit(solution)/shard_map/all_to_all | solution.py:703
  191.5 1.7 collective-permute-start.23
  193.2 10.9 %collective-permute-done.23.refs_6_ = bf16[4,216,128]{2,1,0:T(8,128)(2,1)S(1)} collective-permute-done((bf16[4,216,128]{2,1,0:T(8,128)(2,1)S(1)}, bf16[4,216,128]{2,1,0:T(8,128)(2,1)S(1)}, u32[]{:S(2)}, u32[]{:S(2)}) %collective-permute-start.23) | collective-permute-done | bytes 221216 | tf_op jit(solution)/shard_map/ppermute | solution.py:712
  204.1 5.3 %collective-permute-done.24.refs_7_ = bf16[4,216,128]{2,1,0:T(8,128)(2,1)S(1)} collective-permute-done((bf16[4,216,128]{2,1,0:T(8,128)(2,1)S(1)}, bf16[4,216,128]{2,1,0:T(8,128)(2,1)S(1)}, u32[]{:S(2)}, u32[]{:S(2)}) %collective-permute-start.24) | collective-permute-done | bytes 221216 | tf_op jit(solution)/shard_map/ppermute | solution.py:712
  209.4 4.7 %shard_map.162 = (bf16[128,2304]{1,0:T(8,128)(2,1)}, f32[1,768]{1,0:T(1,128)}, bf16[64,768]{1,0:T(8,128)(2,1)}, bf16[64,768]{1,0:T(8,128)(2,1)}) custom-call(bf16[768,2432]{1,0:T(8,128)(2,1)} %bitcast.23.first_ref, bf16[16,144,128]{2,1,0:T(8,128)(2,1)} %all-to-all-done.3.got_ref, f32[128,768]{1,0:T(8,128)} %get-tuple-element.94.d_middle_ref, ...), custom_call_target="tpu_custom_call" | custom-call | flops 1024 | bytes 1024 | tf_op jit(solution)/shard_map/pallas_call | solution.py:65
  216.7 5.1 %collective-permute-done.25.refs_2_ = bf16[64,768]{1,0:T(8,128)(2,1)S(1)} collective-permute-done((bf16[64,768]{1,0:T(8,128)(2,1)}, bf16[64,768]{1,0:T(8,128)(2,1)S(1)}, u32[]{:S(2)}, u32[]{:S(2)}) %collective-permute-start.25) | collective-permute-done | bytes 98336 | tf_op jit(solution)/shard_map/ppermute | solution.py:708
  221.8 1.5 collective-permute-done.26.refs_3_
  225.2 6.1 %shard_map.163 = (f32[1,768]{1,0:T(1,128)S(1)}, f32[128,768]{1,0:T(8,128)S(1)}, bf16[128,768]{1,0:T(8,128)(2,1)S(1)}, bf16[128,3072]{1,0:T(8,128)(2,1)S(1)}) custom-call(bf16[768,4352]{1,0:T(8,128)(2,1)} %all-gather.2.cloned.1.call-done.refs_0_, s32[1]{0:T(128)} %bitcast.37.lower_ref.refs_1_, bf16[64,768]{1,0:T(8,128)(2,1)S(1)} %collective-permute-done.25.refs_2_, ...), custom_call_target="tpu_custom_call" | custom-call | flops 1024 | bytes 1024 | tf_op jit(solution)/shard_map/pallas_call | solution.py:65
  231.4 1.7 collective-permute-start.34
  235.3 1.6 collective-permute-start.31
  236.9 3.5 %shard_map.164 = (bf16[128,768]{1,0:T(8,128)(2,1)S(1)}, f32[128,1536]{1,0:T(8,128)S(1)}, bf16[128,1536]{1,0:T(8,128)(2,1)S(1)}, bf16[128,1536]{1,0:T(8,128)(2,1)S(1)}) custom-call(bf16[128,768]{1,0:T(8,128)(2,1)S(1)} %copy-done.17, bf16[128,1536]{1,0:T(8,128)(2,1)S(1)} %copy-done.8, bf16[128,1536]{1,0:T(8,128)(2,1)S(1)} %copy-done.6, ...), custom_call_target="tpu_custom_call" | custom-call | flops 1024 | bytes 1024 | tf_op jit(solution)/shard_map/pallas_call | solution.py:65
  241.7 3.1 collective-permute-start.32
  246.1 4.0 %shard_map.166 = (bf16[144,2304]{1,0:T(8,128)(2,1)S(1)}, bf16[128,768]{1,0:T(8,128)(2,1)S(1)}, f32[1,768]{1,0:T(1,128)}) custom-call(s32[1]{0:T(128)} %bitcast.37.lower_ref.refs_1_, bf16[768,2432]{1,0:T(8,128)(2,1)} %bitcast.23.first_ref, bf16[128,768]{1,0:T(8,128)(2,1)S(1)} %get-tuple-element.101.dq_ref, f32[128,1536]{1,0:T(8,128)S(1)} %get-tuple-element.102.own_ref, ...), custom_call_target="tpu_custom_call" | custom-call | flops 1024 | bytes 1024 | tf_op jit(solution)/shard_map/pallas_call | solution.py:65
  250.1 5.2 %collective-permute-done.34.refs_2_ = bf16[128,3072]{1,0:T(8,128)(2,1)S(1)} collective-permute-done((bf16[128,3072]{1,0:T(8,128)(2,1)S(1)}, bf16[128,3072]{1,0:T(8,128)(2,1)S(1)}, u32[]{:S(2)}, u32[]{:S(2)}) %collective-permute-start.34) | collective-permute-done | bytes 786464 | tf_op jit(solution)/shard_map/ppermute | solution.py:712
  255.4 6.7 %collective-permute-start.35 = (bf16[128,3072]{1,0:T(8,128)(2,1)S(1)}, bf16[128,3072]{1,0:T(8,128)(2,1)S(1)}, u32[]{:S(2)}, u32[]{:S(2)}) collective-permute-start(bf16[128,3072]{1,0:T(8,128)(2,1)S(1)} %get-tuple-element.121.refs_0_), channel_id=1, source_target_pairs={{0,1},{1,0},{2,3},{3,2},{4,5},{5,4},{6,7},{7,6},{8,9},{9,8},{10,11... | collective-permute-start | bytes 2359304 | tf_op jit(solution)/shard_map/ppermute | solution.py:712
  262.1 1.8 collective-permute-done.35.refs_1_
  265.9 2.2 collective-permute-start.37
  268.0 2.1 collective-permute-start.33
  270.2 11.7 %collective-permute-done.37 = bf16[384,768]{1,0:T(8,128)(2,1)S(1)} collective-permute-done((bf16[384,768]{1,0:T(8,128)(2,1)S(1)}, bf16[384,768]{1,0:T(8,128)(2,1)S(1)}, u32[]{:S(2)}, u32[]{:S(2)}) %collective-permute-start.37) | collective-permute-done | bytes 589856 | tf_op jit(solution)/shard_map/ppermute | solution.py:712
  282.0 3.1 collective-permute-done.33.refs_2_
  285.6 2.3 collective-permute-start.42
  290.7 15.9 %collective-permute-done.42 = bf16[264,768]{1,0:T(8,128)(2,1)S(1)} collective-permute-done((bf16[264,768]{1,0:T(8,128)(2,1)S(1)}, bf16[264,768]{1,0:T(8,128)(2,1)S(1)}, u32[]{:S(2)}, u32[]{:S(2)}) %collective-permute-start.42) | collective-permute-done | bytes 405536 | tf_op jit(solution)/shard_map/ppermute | solution.py:712
  308.2 2.9 collective-permute-done.40
  311.9 10.6 %collective-permute-done.41 = bf16[48,2432]{1,0:T(8,128)(2,1)S(1)} collective-permute-done((bf16[48,2432]{1,0:T(8,128)(2,1)S(1)}, bf16[48,2432]{1,0:T(8,128)(2,1)S(1)}, u32[]{:S(2)}, u32[]{:S(2)}) %collective-permute-start.41) | collective-permute-done | bytes 233504 | tf_op jit(solution)/shard_map/ppermute | solution.py:712
  (220 shorter events, 54.2 us)
Async XLA Ops:
  7.2 86.7 %all-gather.2.cloned.1.call-start = ((), (), s32[]{:S(2)}) async-start(), calls=%async_computation.4 | async-start | bytes 7102464 | tf_op jit(solution)/shard_map/all_gather | solution.py:883
  9.0 11.7 %collective-permute-start.1 = (bf16[48,2432]{1,0:T(8,128)(2,1)}, bf16[48,2432]{1,0:T(8,128)(2,1)S(1)}, u32[]{:S(2)}, u32[]{:S(2)}) collective-permute-start(bf16[48,2432]{1,0:T(8,128)(2,1)} %shard_map.153), channel_id=1, source_target_pairs={{0,2},{1,3},{2,0},{3,1},{4,6},{5,7},{6,4},{7,5},{8,10},{9,11},{10,... | collective-permute-start | bytes 700424 | tf_op jit(solution)/shard_map/ppermute | solution.py:712
  12.0 12.6 %collective-permute-start.2 = (bf16[48,2432]{1,0:T(8,128)(2,1)}, bf16[48,2432]{1,0:T(8,128)(2,1)S(1)}, u32[]{:S(2)}, u32[]{:S(2)}) collective-permute-start(bf16[48,2432]{1,0:T(8,128)(2,1)} %shard_map.153), channel_id=1, source_target_pairs={{0,4},{1,5},{2,6},{3,7},{4,0},{5,1},{6,2},{7,3},{8,12},{9,13},{10,... | collective-permute-start | bytes 700424 | tf_op jit(solution)/shard_map/ppermute | solution.py:712
  13.5 19.7 %collective-permute-start.3 = (bf16[48,2432]{1,0:T(8,128)(2,1)}, bf16[48,2432]{1,0:T(8,128)(2,1)S(1)}, u32[]{:S(2)}, u32[]{:S(2)}) collective-permute-start(bf16[48,2432]{1,0:T(8,128)(2,1)} %shard_map.153), channel_id=1, source_target_pairs={{0,8},{1,9},{2,10},{3,11},{4,12},{5,13},{6,14},{7,15},{8,0},{9,1},... | collective-permute-start | bytes 700424 | tf_op jit(solution)/shard_map/ppermute | solution.py:712
  16.1 17.7 %collective-permute-start.4 = (bf16[48,2432]{1,0:T(8,128)(2,1)}, bf16[48,2432]{1,0:T(8,128)(2,1)S(1)}, u32[]{:S(2)}, u32[]{:S(2)}) collective-permute-start(bf16[48,2432]{1,0:T(8,128)(2,1)} %shard_map.153), channel_id=1, source_target_pairs={{0,12},{1,13},{2,14},{3,15},{4,8},{5,9},{6,10},{7,11},{8,4},{9,5},... | collective-permute-start | bytes 700424 | tf_op jit(solution)/shard_map/ppermute | solution.py:712
  17.1 1.2 collective-permute-start
  18.2 29.4 %collective-permute-start.8 = (bf16[48,2432]{1,0:T(8,128)(2,1)}, bf16[48,2432]{1,0:T(8,128)(2,1)S(1)}, u32[]{:S(2)}, u32[]{:S(2)}) collective-permute-start(bf16[48,2432]{1,0:T(8,128)(2,1)} %shard_map.153), channel_id=1, source_target_pairs={{0,1},{1,0},{2,3},{3,2},{4,5},{5,4},{6,7},{7,6},{8,9},{9,8},{10,11... | collective-permute-start | bytes 700424 | tf_op jit(solution)/shard_map/ppermute | solution.py:712
  24.3 24.6 %collective-permute-start.9 = (bf16[48,2432]{1,0:T(8,128)(2,1)S(1)}, bf16[48,2432]{1,0:T(8,128)(2,1)S(1)}, u32[]{:S(2)}, u32[]{:S(2)}) collective-permute-start(bf16[48,2432]{1,0:T(8,128)(2,1)S(1)} %collective-permute-done.1), channel_id=1, source_target_pairs={{0,1},{1,0},{2,3},{3,2},{4,5},{5,4},{6,7},{7,6},{8,9},{9,8},{10,11... | collective-permute-start | bytes 700424 | tf_op jit(solution)/shard_map/ppermute | solution.py:712
  24.5 13.6 %collective-permute-start.5 = (bf16[48,2432]{1,0:T(8,128)(2,1)S(1)}, bf16[48,2432]{1,0:T(8,128)(2,1)S(1)}, u32[]{:S(2)}, u32[]{:S(2)}) collective-permute-start(bf16[48,2432]{1,0:T(8,128)(2,1)S(1)} %collective-permute-done.2), channel_id=1, source_target_pairs={{0,2},{1,3},{2,0},{3,1},{4,6},{5,7},{6,4},{7,5},{8,10},{9,11},{10,... | collective-permute-start | bytes 700424 | tf_op jit(solution)/shard_map/ppermute | solution.py:712
  33.3 10.2 %collective-permute-start.6 = (bf16[48,2432]{1,0:T(8,128)(2,1)S(1)}, bf16[48,2432]{1,0:T(8,128)(2,1)S(1)}, u32[]{:S(2)}, u32[]{:S(2)}) collective-permute-start(bf16[48,2432]{1,0:T(8,128)(2,1)S(1)} %collective-permute-done.3), channel_id=1, source_target_pairs={{0,2},{1,3},{2,0},{3,1},{4,6},{5,7},{6,4},{7,5},{8,10},{9,11},{10,... | collective-permute-start | bytes 700424 | tf_op jit(solution)/shard_map/ppermute | solution.py:712
  33.8 13.2 %collective-permute-start.7 = (bf16[48,2432]{1,0:T(8,128)(2,1)S(1)}, bf16[48,2432]{1,0:T(8,128)(2,1)S(1)}, u32[]{:S(2)}, u32[]{:S(2)}) collective-permute-start(bf16[48,2432]{1,0:T(8,128)(2,1)S(1)} %collective-permute-done.4), channel_id=1, source_target_pairs={{0,2},{1,3},{2,0},{3,1},{4,6},{5,7},{6,4},{7,5},{8,10},{9,11},{10,... | collective-permute-start | bytes 700424 | tf_op jit(solution)/shard_map/ppermute | solution.py:712
  38.2 11.5 %collective-permute-start.10 = (bf16[48,2432]{1,0:T(8,128)(2,1)S(1)}, bf16[48,2432]{1,0:T(8,128)(2,1)S(1)}, u32[]{:S(2)}, u32[]{:S(2)}) collective-permute-start(bf16[48,2432]{1,0:T(8,128)(2,1)S(1)} %collective-permute-done.2), channel_id=1, source_target_pairs={{0,1},{1,0},{2,3},{3,2},{4,5},{5,4},{6,7},{7,6},{8,9},{9,8},{10,11... | collective-permute-start | bytes 700424 | tf_op jit(solution)/shard_map/ppermute | solution.py:712
  43.5 8.1 %collective-permute-start.12 = (bf16[48,2432]{1,0:T(8,128)(2,1)S(1)}, bf16[48,2432]{1,0:T(8,128)(2,1)S(1)}, u32[]{:S(2)}, u32[]{:S(2)}) collective-permute-start(bf16[48,2432]{1,0:T(8,128)(2,1)S(1)} %collective-permute-done.3), channel_id=1, source_target_pairs={{0,1},{1,0},{2,3},{3,2},{4,5},{5,4},{6,7},{7,6},{8,9},{9,8},{10,11... | collective-permute-start | bytes 700424 | tf_op jit(solution)/shard_map/ppermute | solution.py:712
  47.0 6.0 %collective-permute-start.14 = (bf16[48,2432]{1,0:T(8,128)(2,1)S(1)}, bf16[48,2432]{1,0:T(8,128)(2,1)S(1)}, u32[]{:S(2)}, u32[]{:S(2)}) collective-permute-start(bf16[48,2432]{1,0:T(8,128)(2,1)S(1)} %collective-permute-done.4), channel_id=1, source_target_pairs={{0,1},{1,0},{2,3},{3,2},{4,5},{5,4},{6,7},{7,6},{8,9},{9,8},{10,11... | collective-permute-start | bytes 700424 | tf_op jit(solution)/shard_map/ppermute | solution.py:712
  47.7 3.2 collective-permute-start.11
  48.9 3.4 %collective-permute-start.13 = (bf16[48,2432]{1,0:T(8,128)(2,1)S(1)}, bf16[48,2432]{1,0:T(8,128)(2,1)S(1)}, u32[]{:S(2)}, u32[]{:S(2)}) collective-permute-start(bf16[48,2432]{1,0:T(8,128)(2,1)S(1)} %collective-permute-done.6), channel_id=1, source_target_pairs={{0,1},{1,0},{2,3},{3,2},{4,5},{5,4},{6,7},{7,6},{8,9},{9,8},{10,11... | collective-permute-start | bytes 700424 | tf_op jit(solution)/shard_map/ppermute | solution.py:712
  49.7 4.1 %collective-permute-start.15 = (bf16[48,2432]{1,0:T(8,128)(2,1)S(1)}, bf16[48,2432]{1,0:T(8,128)(2,1)S(1)}, u32[]{:S(2)}, u32[]{:S(2)}) collective-permute-start(bf16[48,2432]{1,0:T(8,128)(2,1)S(1)} %collective-permute-done.7), channel_id=1, source_target_pairs={{0,1},{1,0},{2,3},{3,2},{4,5},{5,4},{6,7},{7,6},{8,9},{9,8},{10,11... | collective-permute-start | bytes 700424 | tf_op jit(solution)/shard_map/ppermute | solution.py:712
  58.7 40.7 %copy-start.16 = (bf16[128,768]{1,0:T(8,128)(2,1)}, bf16[128,768]{1,0:T(8,128)(2,1)S(1)}, u32[]{:S(2)}) copy-start(bf16[128,768]{1,0:T(8,128)(2,1)S(1)} %get-tuple-element.72.q_ref) | copy-start | bytes 589828
  58.7 4.8 %collective-permute-start.16 = (bf16[128,1536]{1,0:T(8,128)(2,1)S(1)}, bf16[128,1536]{1,0:T(8,128)(2,1)S(1)}, u32[]{:S(2)}, u32[]{:S(2)}) collective-permute-start(bf16[128,1536]{1,0:T(8,128)(2,1)S(1)} %get-tuple-element.73.own_ref), channel_id=1, source_target_pairs={{0,1},{1,2},{2,3},{3,4},{4,5},{5,6},{6,7},{7,8},{8,9},{9,10},{10,1... | collective-permute-start | bytes 1179656 | tf_op jit(solution)/shard_map/ppermute | solution.py:930
  60.9 3.6 %collective-permute-start.17 = (bf16[128,1536]{1,0:T(8,128)(2,1)S(1)}, bf16[128,1536]{1,0:T(8,128)(2,1)S(1)}, u32[]{:S(2)}, u32[]{:S(2)}) collective-permute-start(bf16[128,1536]{1,0:T(8,128)(2,1)S(1)} %get-tuple-element.73.own_ref), channel_id=1, source_target_pairs={{1,0},{2,1},{3,2},{4,3},{5,4},{6,5},{7,6},{8,7},{9,8},{10,9},{11,1... | collective-permute-start | bytes 1179656 | tf_op jit(solution)/shard_map/ppermute | solution.py:932
  63.5 44.3 %copy-start.27 = (f32[1,768]{1,0:T(1,128)}, f32[1,768]{1,0:T(1,128)S(1)}, u32[]{:S(2)}) copy-start(f32[1,768]{1,0:T(1,128)S(1)} %get-tuple-element.152.gain_ref) | copy-start | bytes 9220
  99.4 6.9 %collective-permute-start.18 = (bf16[64,768]{1,0:T(8,128)(2,1)}, bf16[64,768]{1,0:T(8,128)(2,1)S(1)}, u32[]{:S(2)}, u32[]{:S(2)}) collective-permute-start(bf16[64,768]{1,0:T(8,128)(2,1)} %get-tuple-element.76), channel_id=1, source_target_pairs={{0,16},{1,17},{2,18},{3,19},{4,20},{5,21},{6,22},{7,23},{8,24},{9,... | collective-permute-start | bytes 294920 | tf_op jit(solution)/shard_map/ppermute | solution.py:708
  102.9 4.9 %collective-permute-start.19 = (bf16[64,768]{1,0:T(8,128)(2,1)}, bf16[64,768]{1,0:T(8,128)(2,1)S(1)}, u32[]{:S(2)}, u32[]{:S(2)}) collective-permute-start(bf16[64,768]{1,0:T(8,128)(2,1)} %get-tuple-element.77), channel_id=1, source_target_pairs={{0,16},{1,17},{2,18},{3,19},{4,20},{5,21},{6,22},{7,23},{8,24},{9,... | collective-permute-start | bytes 294920 | tf_op jit(solution)/shard_map/ppermute | solution.py:708
  134.7 1.6 collective-permute-start.20
  162.6 13.3 %all-to-all-start.2 = ((bf16[16,48,128]{2,1,0:T(8,128)(2,1)}), bf16[16,48,128]{2,1,0:T(8,128)(2,1)}, u32[]{:S(2)}, u32[]{:S(2)}) async-start(bf16[16,48,128]{2,1,0:T(8,128)(2,1)} %get-tuple-element.85), calls=%async_computation.2 | async-start | bytes 393216 | tf_op jit(solution)/shard_map/all_to_all | solution.py:703
  184.2 1.6 collective-permute-start.21
  186.9 22.5 %all-to-all-start.3 = ((bf16[16,144,128]{2,1,0:T(8,128)(2,1)}), bf16[16,144,128]{2,1,0:T(8,128)(2,1)}, u32[]{:S(2)}, u32[]{:S(2)}) async-start(bf16[16,144,128]{2,1,0:T(8,128)(2,1)} %add_convert_fusion), calls=%async_computation.3 | async-start | bytes 1179648 | tf_op jit(solution)/shard_map/all_to_all | solution.py:703
  191.2 2.0 collective-permute-start.22
  191.5 12.6 %collective-permute-start.23 = (bf16[4,216,128]{2,1,0:T(8,128)(2,1)S(1)}, bf16[4,216,128]{2,1,0:T(8,128)(2,1)S(1)}, u32[]{:S(2)}, u32[]{:S(2)}) collective-permute-start(bf16[4,216,128]{2,1,0:T(8,128)(2,1)S(1)} %get-tuple-element.139), channel_id=1, source_target_pairs={{0,2},{1,3},{2,0},{3,1},{4,6},{5,7},{6,4},{7,5},{8,10},{9,11},{10,... | collective-permute-start | bytes 663560 | tf_op jit(solution)/shard_map/ppermute | solution.py:712
  193.2 16.2 %collective-permute-start.24 = (bf16[4,216,128]{2,1,0:T(8,128)(2,1)S(1)}, bf16[4,216,128]{2,1,0:T(8,128)(2,1)S(1)}, u32[]{:S(2)}, u32[]{:S(2)}) collective-permute-start(bf16[4,216,128]{2,1,0:T(8,128)(2,1)S(1)} %get-tuple-element.138), channel_id=1, source_target_pairs={{0,3},{1,2},{2,1},{3,0},{4,7},{5,6},{6,5},{7,4},{8,11},{9,10},{10,... | collective-permute-start | bytes 663560 | tf_op jit(solution)/shard_map/ppermute | solution.py:712
  214.1 7.7 %collective-permute-start.25 = (bf16[64,768]{1,0:T(8,128)(2,1)}, bf16[64,768]{1,0:T(8,128)(2,1)S(1)}, u32[]{:S(2)}, u32[]{:S(2)}) collective-permute-start(bf16[64,768]{1,0:T(8,128)(2,1)} %get-tuple-element.95), channel_id=1, source_target_pairs={{16,0},{17,1},{18,2},{19,3},{20,4},{21,5},{22,6},{23,7},{24,8},{25... | collective-permute-start | bytes 294920 | tf_op jit(solution)/shard_map/ppermute | solution.py:708
  215.4 7.9 %collective-permute-start.26 = (bf16[64,768]{1,0:T(8,128)(2,1)}, bf16[64,768]{1,0:T(8,128)(2,1)S(1)}, u32[]{:S(2)}, u32[]{:S(2)}) collective-permute-start(bf16[64,768]{1,0:T(8,128)(2,1)} %get-tuple-element.96), channel_id=1, source_target_pairs={{16,0},{17,1},{18,2},{19,3},{20,4},{21,5},{22,6},{23,7},{24,8},{25... | collective-permute-start | bytes 294920 | tf_op jit(solution)/shard_map/ppermute | solution.py:708
  223.4 8.0 %collective-permute-start.27 = (bf16[128,768]{1,0:T(8,128)(2,1)S(1)}, bf16[128,768]{1,0:T(8,128)(2,1)S(1)}, u32[]{:S(2)}, u32[]{:S(2)}) collective-permute-start(bf16[128,768]{1,0:T(8,128)(2,1)S(1)} %pad_maximum_fusion.2.refs_0_), channel_id=1, source_target_pairs={{0,2},{1,3},{2,0},{3,1},{4,6},{5,7},{6,4},{7,5},{8,10},{9,11},{10,... | collective-permute-start | bytes 589832 | tf_op jit(solution)/shard_map/ppermute | solution.py:712
  231.4 23.9 %collective-permute-start.34 = (bf16[128,3072]{1,0:T(8,128)(2,1)S(1)}, bf16[128,3072]{1,0:T(8,128)(2,1)S(1)}, u32[]{:S(2)}, u32[]{:S(2)}) collective-permute-start(bf16[128,3072]{1,0:T(8,128)(2,1)S(1)} %get-tuple-element.121.refs_0_), channel_id=1, source_target_pairs={{0,2},{1,3},{2,0},{3,1},{4,6},{5,7},{6,4},{7,5},{8,10},{9,11},{10,... | collective-permute-start | bytes 2359304 | tf_op jit(solution)/shard_map/ppermute | solution.py:712
  233.2 1.4 collective-permute-start.29
  233.2 1.7 collective-permute-start.30
  235.3 9.5 %collective-permute-start.31 = (bf16[144,768]{1,0:T(8,128)(2,1)S(1)}, bf16[144,768]{1,0:T(8,128)(2,1)S(1)}, u32[]{:S(2)}, u32[]{:S(2)}) collective-permute-start(bf16[144,768]{1,0:T(8,128)(2,1)S(1)} %get-tuple-element.110), channel_id=1, source_target_pairs={{0,4},{1,5},{2,6},{3,7},{4,0},{5,1},{6,2},{7,3},{8,12},{9,13},{10,... | collective-permute-start | bytes 663560 | tf_op jit(solution)/shard_map/ppermute | solution.py:712
  240.4 4.4 %collective-permute-start.28 = (bf16[128,1536]{1,0:T(8,128)(2,1)S(1)}, bf16[128,1536]{1,0:T(8,128)(2,1)S(1)}, u32[]{:S(2)}, u32[]{:S(2)}) collective-permute-start(bf16[128,1536]{1,0:T(8,128)(2,1)S(1)} %get-tuple-element.103), channel_id=1, source_target_pairs={{1,0},{2,1},{3,2},{4,3},{5,4},{6,5},{7,6},{8,7},{9,8},{10,9},{11,1... | collective-permute-start | bytes 1179656 | tf_op jit(solution)/shard_map/ppermute | solution.py:1092
  241.7 4.4 %collective-permute-start.32 = (bf16[128,1536]{1,0:T(8,128)(2,1)S(1)}, bf16[128,1536]{1,0:T(8,128)(2,1)S(1)}, u32[]{:S(2)}, u32[]{:S(2)}) collective-permute-start(bf16[128,1536]{1,0:T(8,128)(2,1)S(1)} %get-tuple-element.112), channel_id=1, source_target_pairs={{0,1},{1,2},{2,3},{3,4},{4,5},{5,6},{6,7},{7,8},{8,9},{9,10},{10,1... | collective-permute-start | bytes 1179656 | tf_op jit(solution)/shard_map/ppermute | solution.py:1093
  255.4 8.6 %collective-permute-start.35 = (bf16[128,3072]{1,0:T(8,128)(2,1)S(1)}, bf16[128,3072]{1,0:T(8,128)(2,1)S(1)}, u32[]{:S(2)}, u32[]{:S(2)}) collective-permute-start(bf16[128,3072]{1,0:T(8,128)(2,1)S(1)} %get-tuple-element.121.refs_0_), channel_id=1, source_target_pairs={{0,1},{1,0},{2,3},{3,2},{4,5},{5,4},{6,7},{7,6},{8,9},{9,8},{10,11... | collective-permute-start | bytes 2359304 | tf_op jit(solution)/shard_map/ppermute | solution.py:712
  262.0 3.0 collective-permute-start.36
  265.9 16.0 %collective-permute-start.37 = (bf16[384,768]{1,0:T(8,128)(2,1)S(1)}, bf16[384,768]{1,0:T(8,128)(2,1)S(1)}, u32[]{:S(2)}, u32[]{:S(2)}) collective-permute-start(bf16[384,768]{1,0:T(8,128)(2,1)S(1)} %get-tuple-element.124), channel_id=1, source_target_pairs={{0,4},{1,5},{2,6},{3,7},{4,0},{5,1},{6,2},{7,3},{8,12},{9,13},{10,... | collective-permute-start | bytes 1769480 | tf_op jit(solution)/shard_map/ppermute | solution.py:712
  268.0 17.1 %collective-permute-start.33 = (bf16[144,2304]{1,0:T(8,128)(2,1)S(1)}, bf16[144,2304]{1,0:T(8,128)(2,1)S(1)}, u32[]{:S(2)}, u32[]{:S(2)}) collective-permute-start(bf16[144,2304]{1,0:T(8,128)(2,1)S(1)} %get-tuple-element.126.refs_0_), channel_id=1, source_target_pairs={{0,2},{1,3},{2,0},{3,1},{4,6},{5,7},{6,4},{7,5},{8,10},{9,11},{10,... | collective-permute-start | bytes 1990664 | tf_op jit(solution)/shard_map/ppermute | solution.py:712
  285.1 4.3 %collective-permute-start.38 = (bf16[144,2304]{1,0:T(8,128)(2,1)S(1)}, bf16[144,2304]{1,0:T(8,128)(2,1)S(1)}, u32[]{:S(2)}, u32[]{:S(2)}) collective-permute-start(bf16[144,2304]{1,0:T(8,128)(2,1)S(1)} %get-tuple-element.126.refs_0_), channel_id=1, source_target_pairs={{0,1},{1,0},{2,3},{3,2},{4,5},{5,4},{6,7},{7,6},{8,9},{9,8},{10,11... | collective-permute-start | bytes 1990664 | tf_op jit(solution)/shard_map/ppermute | solution.py:712
  285.1 4.3 %collective-permute-start.39 = (bf16[144,2304]{1,0:T(8,128)(2,1)S(1)}, bf16[144,2304]{1,0:T(8,128)(2,1)S(1)}, u32[]{:S(2)}, u32[]{:S(2)}) collective-permute-start(bf16[144,2304]{1,0:T(8,128)(2,1)S(1)} %collective-permute-done.33.refs_2_), channel_id=1, source_target_pairs={{0,1},{1,0},{2,3},{3,2},{4,5},{5,4},{6,7},{7,6},{8,9},{9,8},{10,11... | collective-permute-start | bytes 1990664 | tf_op jit(solution)/shard_map/ppermute | solution.py:712
  285.6 21.0 %collective-permute-start.42 = (bf16[264,768]{1,0:T(8,128)(2,1)S(1)}, bf16[264,768]{1,0:T(8,128)(2,1)S(1)}, u32[]{:S(2)}, u32[]{:S(2)}) collective-permute-start(bf16[264,768]{1,0:T(8,128)(2,1)S(1)} %pad_maximum_fusion), channel_id=1, source_target_pairs={{0,8},{1,9},{2,10},{3,11},{4,12},{5,13},{6,14},{7,15},{8,0},{9,1},... | collective-permute-start | bytes 1216520 | tf_op jit(solution)/shard_map/ppermute | solution.py:712
  290.1 21.0 %collective-permute-start.40 = (bf16[96,2432]{1,0:T(8,128)(2,1)S(1)}, bf16[96,2432]{1,0:T(8,128)(2,1)S(1)}, u32[]{:S(2)}, u32[]{:S(2)}) collective-permute-start(bf16[96,2432]{1,0:T(8,128)(2,1)S(1)} %get-tuple-element.129), channel_id=1, source_target_pairs={{0,4},{1,5},{2,6},{3,7},{4,0},{5,1},{6,2},{7,3},{8,12},{9,13},{10,... | collective-permute-start | bytes 1400840 | tf_op jit(solution)/shard_map/ppermute | solution.py:712
  311.1 11.4 %collective-permute-start.41 = (bf16[48,2432]{1,0:T(8,128)(2,1)S(1)}, bf16[48,2432]{1,0:T(8,128)(2,1)S(1)}, u32[]{:S(2)}, u32[]{:S(2)}) collective-permute-start(bf16[48,2432]{1,0:T(8,128)(2,1)S(1)} %add_convert_fusion.2), channel_id=1, source_target_pairs={{0,8},{1,9},{2,10},{3,11},{4,12},{5,13},{6,14},{7,15},{8,0},{9,1},... | collective-permute-start | bytes 700424 | tf_op jit(solution)/shard_map/ppermute | solution.py:712
  (37 other events, 711.8 us)
Sparse Core Ops, SparseCore 0:
  20.8 73.0 all-gather.1

commit v15 on v14

--- a/solution.py
+++ b/solution.py
@@ -776,13 +776,20 @@
     send[half + base : half + base + rows, columns] = result[3 * rows :].astype(BF)
 
 
+def four_parts(refs, columns, tokens):
+    own, other, across = refs
+    size = own.shape[0]
+    parts = [ref[:tokens, columns] for ref in (own, other, across)]
+    return jnp.concatenate(parts + [other[size : size + tokens, columns]], 0)
+
+
 def early_body(terms, split, *refs):
     refs, outs = refs[:-3], refs[-3:]
     operands, lefts = (refs[:split], refs[split:-4]), refs[-4:]
     width = outs[0].shape[1]
     base = 0
     for which, rows, (start, end) in terms:
-        right = jnp.concatenate([ref[:, start:end] for ref in operands[which]], 0)
+        right = four_parts(operands[which], slice(start, end), lefts[0].shape[2])
         result = dot(left_rows_of(lefts, rows), right)
         for column in range(0, end - start, width):
             by_plane(result[:, column : column + width], base, outs)
@@ -796,9 +803,11 @@
     width = columns // 3
     size = outs[0].shape[0]
     tokens = lefts[0].shape[2]
-    right = jnp.concatenate([ref[:tokens] for ref in rights], 0)
+    right = four_parts(rights, slice(None), tokens)
     by_plane(dot(left_rows_of(lefts, rows), right), 0, outs, slice(0, columns))
-    tail = sum(ref[tokens:, :width].astype(F32) for ref in rights)
+    ends = [ref[tokens : tokens + EXTRA, :width] for ref in rights]
+    ends.append(rights[1][rights[0].shape[0] + tokens :, :width])
+    tail = sum(part.astype(F32) for part in ends)
     both = jnp.concatenate([tail, jnp.zeros((LANES - EXTRA, width), F32)], 0).T
     lane = lax.broadcasted_iota(jnp.int32, (1, LANES), 1)
     lows = pltpu.roll(both, LANES - 1, 1)
@@ -812,6 +821,10 @@
 
 def three_parts(shape):
     return [(shape, F32), (shape, F32), ((2 * shape[0], shape[1]), BF)]
+
+
+def with_core(rows, across, count):
+    return [rows, partner(jnp.concatenate([rows, *across]), 1, count), *across]
 
 
 def first_hop(blocks, count):
@@ -1070,10 +1083,10 @@
     )
     d_att_0, right, across_mlp = lax.optimization_barrier((d_att_0, right, across_mlp))
     across = [partner(right, 2, count)]
-    d_mlp = [d_mlp, partner(d_mlp, 1, count), across_mlp, partner(across_mlp, 1, count)]
+    d_mlp = with_core(d_mlp, [across_mlp], count)
     out_near, out_far = first_hop(
         on_core(
-            functools.partial(early_body, [(0, (3 * shard_total, left_total), (0, width))], 4),
+            functools.partial(early_body, [(0, (3 * shard_total, left_total), (0, width))], 3),
             three_parts((hidden_total, width)),
             (*d_mlp, *left),
         ),
@@ -1108,8 +1121,7 @@
     )
     across_chunks = [partner(d_proj, 2, count)]
     across, right, _ = lax.optimization_barrier((across, right, d_proj))
-    right = [right, partner(right, 1, count)] + across
-    right += [partner(item, 1, count) for item in across]
+    right = with_core(right, across, count)
     in_rows, attn_rows = shard_total * (inner // width), shard_total
     early_rows = in_rows + attn_rows
     terms = [
@@ -1127,8 +1139,7 @@
     far = jnp.concatenate([far, out_far])
     across_chunks, d_proj, _ = lax.optimization_barrier((across_chunks, d_proj, far))
     far = partner(far, 8, count)
-    right = [d_proj, partner(d_proj, 1, count)] + across_chunks
-    right += [partner(item, 1, count) for item in across_chunks]
+    right = with_core(d_proj, across_chunks, count)
     late_in = (group_pos[None], *right, *left)
     late = on_core(
         functools.partial(late_body, (0, shard_total)),

time: 332 us -> 332 us (level)
    ppermute x35 -> x32, waiting for transfers between devices: 88.2 us -> 89.4 us  [partner(): return lax.ppermute(rows, 'dp', [(i, i ^ apart) for i in range(count)])]
    ppermute x35 -> x32, starting transfers between devices: 32.1 us -> 32.8 us  [partner(): return lax.ppermute(rows, 'dp', [(i, i ^ apart) for i in range(count)])]
    unnamed x78 -> x82, local copies, waits for them, and re-layouts: 7.61 us -> 7.64 us
  transfers between devices with their start and end apart: 46 -> 43, of which waited for: 26 -> 23; matrix products, arithmetic and copies ran while one was open for 7% -> 7% of each run, Pallas kernels for 7% -> 7%
where the time goes in v15:
time: 332 us; the launch traced here: 331 us
  waiting for transfers between devices  131 us (39%)
  Pallas kernels  61.6 us (19%)
  starting transfers between devices  55.8 us (17%)
  blocking collectives  35.9 us (11%)
  local copies, waits for them, and re-layouts  27.1 us (8%)
  between operations  14.9 us (4%)
  other arithmetic  5.35 us (2%)
    ppermute x32, waiting for transfers between devices, partner(): return lax.ppermute(rows, 'dp', [(i, i ^ apart) for i in range(count)])  89.4 us
    pallas_call x17, Pallas kernels, on_core(): pl.pallas_call(body, out_shape=[jax.ShapeDtypeStruct(shape, dtype) for sh...  61.6 us
    all_to_all x2, blocking collectives, exchange(): return lax.all_to_all(blocks, 'dp', 0, 0, axis_index_groups=groups)  35.9 us
    ppermute x32, starting transfers between devices, partner(): return lax.ppermute(rows, 'dp', [(i, i ^ apart) for i in range(count)])  32.8 us
    all_gather x1, waiting for transfers between devices, on_device(): others = [lax.all_gather(stacked, 'dp', axis=0, tiled=True)]  25 us
    dynamic_update_slice x16, local copies, waits for them, and re-layouts, gather_rows(): whole = lax.dynamic_update_slice(whole, item[None], start)  11.5 us
    ppermute x4, waiting for transfers between devices, to_other_section(): return [lax.ppermute(rows, 'section', pairs) for rows in chunks]  9.81 us
    all_to_all x2, starting transfers between devices, exchange(): return lax.all_to_all(blocks, 'dp', 0, 0, axis_index_groups=groups)  7.78 us
  transfers between devices with their start and end apart: 43, of which 23 were waited for; matrix products, arithmetic and copies ran while one was open for 7% of the time, Pallas kernels for 7%

profile of v15, /device:TPU:0, one launch (start us, length us, event | category | flops | bytes accessed | tf_op | source)
XLA Modules:
  0.0 331.5 jit_solution(16797773201398930960)
XLA Ops:
  7.2 1.8 shard_map.153
  9.0 2.9 collective-permute-start.1
  12.0 1.6 collective-permute-start.2
  13.5 2.6 collective-permute-start.3
  18.8 1.8 shard_map.152
  20.9 2.2 broadcast_in_dim.105
  24.9 8.4 %collective-permute-done.3 = bf16[48,2432]{1,0:T(8,128)(2,1)S(1)} collective-permute-done((bf16[48,2432]{1,0:T(8,128)(2,1)}, bf16[48,2432]{1,0:T(8,128)(2,1)S(1)}, u32[]{:S(2)}, u32[]{:S(2)}) %collective-permute-start.3) | collective-permute-done | bytes 233504 | tf_op jit(solution)/shard_map/ppermute | solution.py:712
  38.9 4.5 %collective-permute-done.6 = bf16[48,2432]{1,0:T(8,128)(2,1)S(1)} collective-permute-done((bf16[48,2432]{1,0:T(8,128)(2,1)S(1)}, bf16[48,2432]{1,0:T(8,128)(2,1)S(1)}, u32[]{:S(2)}, u32[]{:S(2)}) %collective-permute-start.6) | collective-permute-done | bytes 233504 | tf_op jit(solution)/shard_map/ppermute | solution.py:712
  44.2 2.8 collective-permute-done.7
  54.4 3.6 %shard_map.154 = (f32[8,768]{1,0:T(8,128)S(1)}, bf16[128,768]{1,0:T(8,128)(2,1)S(1)}, bf16[128,768]{1,0:T(8,128)(2,1)S(1)}, bf16[128,1536]{1,0:T(8,128)(2,1)S(1)}) custom-call(bf16[768,2432]{1,0:T(8,128)(2,1)} %bitcast.23.first_ref, bf16[128,768]{1,0:T(8,128)(2,1)S(1)} %bitcast.90, f32[3,128,128]{2,1,0:T(8,128)S(1)} %tile.13.table_ref), custom_call_target="tpu_custom_call" | custom-call | flops 1024 | bytes 1024 | tf_op jit(solution)/shard_map/pallas_call | solution.py:65
  58.7 2.2 collective-permute-start.16
  64.6 3.7 %shard_map.155 = (bf16[128,768]{1,0:T(8,128)(2,1)S(1)}, f32[12,1,128]{2,1,0:T(1,128)S(1)}) custom-call(bf16[128,768]{1,0:T(8,128)(2,1)S(1)} %get-tuple-element.72.q_ref, bf16[128,1536]{1,0:T(8,128)(2,1)S(1)} %collective-permute-done.16.before_ref, bf16[128,1536]{1,0:T(8,128)(2,1)S(1)} %get-tuple-element.73.own_ref, ...), custom_call_target="tpu_custom_call" | custom-call | flops 1024 | bytes 1024 | tf_op jit(solution)/shard_map/pallas_call | solution.py:65
  68.9 25.0 %all-gather.2.cloned.1.call-done.refs_0_ = bf16[768,4352]{1,0:T(8,128)(2,1)} async-done(((bf16[48,4352]{1,0:T(8,128)(2,1)}), bf16[768,4352]{1,0:T(8,128)(2,1)}) %all-gather.2.cloned.1.call-update) | async-done | bytes 6684688 | tf_op jit(solution)/shard_map/all_gather | solution.py:896
  93.9 5.5 %shard_map.156 = (bf16[128,1920]{1,0:T(8,128)(2,1)}, f32[128,3072]{1,0:T(8,128)}, bf16[64,768]{1,0:T(8,128)(2,1)}, bf16[64,768]{1,0:T(8,128)(2,1)}) custom-call(bf16[768,4352]{1,0:T(8,128)(2,1)} %all-gather.2.cloned.1.call-done.refs_0_, bf16[128,768]{1,0:T(8,128)(2,1)} %bitcast.89, bf16[128,768]{1,0:T(8,128)(2,1)} %copy-done.20, ...), custom_call_target="tpu_custom_call" | custom-call | flops 1024 | bytes 1024 | tf_op jit(solution)/shard_map/pallas_call | solution.py:65
  99.5 3.5 %collective-permute-start.18 = (bf16[64,768]{1,0:T(8,128)(2,1)}, bf16[64,768]{1,0:T(8,128)(2,1)S(1)}, u32[]{:S(2)}, u32[]{:S(2)}) collective-permute-start(bf16[64,768]{1,0:T(8,128)(2,1)} %get-tuple-element.76), channel_id=1, source_target_pairs={{0,16},{1,17},{2,18},{3,19},{4,20},{5,21},{6,22},{7,23},{8,24},{9,... | collective-permute-start | bytes 294920 | tf_op jit(solution)/shard_map/ppermute | solution.py:708
  104.6 1.8 collective-permute-done.18.low_ref.refs_2_
  107.8 3.2 shard_map.157
  111.0 23.7 %all_to_all.20.got_ref = bf16[16,144,128]{2,1,0:T(8,128)(2,1)S(1)} all-to-all(bf16[16,144,128]{2,1,0:T(8,128)(2,1)S(1)} %get-tuple-element.78), channel_id=1, replica_groups={{0,1,2,3,4,5,6,7,8,9,10,11,12,13,14,15},{16,17,18,19,20,21,22,23,24,25,..., dimensions={0} | all-to-all | bytes 1179648 | tf_op jit(solution)/shard_map/all_to_all | solution.py:703
  136.3 6.0 %shard_map.158 = (bf16[16,48,128]{2,1,0:T(8,128)(2,1)S(1)}, f32[6,1,256]{2,1,0:T(1,128)S(1)}) custom-call(bf16[16,144,128]{2,1,0:T(8,128)(2,1)S(1)} %all_to_all.20.got_ref, bf16[16,64,128]{2,1,0:T(8,128)(2,1)S(1)} %collective-permute-done.20.other_ref, s32[1024,1]{1,0:T(8,128)S(1)} %copy.19.own_seg_ref, s32[1024,1]{1,0:T(8,128)S(1)} %copy.20.shared_seg_ref), custom_call_target="tpu_custom_call" | custom-call | flops 1024 | bytes 1024 | tf_op jit(solution)/shard_map/pallas_call | solution.py:65
  142.4 12.3 %all_to_all.21.refs_1_ = bf16[16,48,128]{2,1,0:T(8,128)(2,1)} all-to-all(bf16[16,48,128]{2,1,0:T(8,128)(2,1)S(1)} %get-tuple-element.79), channel_id=1, replica_groups={{0,1,2,3,4,5,6,7,8,9,10,11,12,13,14,15},{16,17,18,19,20,21,22,23,24,25,..., dimensions={0} | all-to-all | bytes 393216 | tf_op jit(solution)/shard_map/all_to_all | solution.py:703
  154.7 7.9 %shard_map.159 = (bf16[128,6528]{1,0:T(8,128)(2,1)}, f32[1,768]{1,0:T(1,128)}, f32[128,768]{1,0:T(8,128)}, bf16[16,48,128]{2,1,0:T(8,128)(2,1)}) custom-call(bf16[768,4352]{1,0:T(8,128)(2,1)} %all-gather.2.cloned.1.call-done.refs_0_, bf16[16,48,128]{2,1,0:T(8,128)(2,1)} %all_to_all.21.refs_1_, bf16[64,768]{1,0:T(8,128)(2,1)} %copy-done.16, ...), custom_call_target="tpu_custom_call" | custom-call | flops 1024 | bytes 1024 | tf_op jit(solution)/shard_map/pallas_call | solution.py:65
  162.6 3.5 %all-to-all-start.2 = ((bf16[16,48,128]{2,1,0:T(8,128)(2,1)}), bf16[16,48,128]{2,1,0:T(8,128)(2,1)S(1)}, u32[]{:S(2)}, u32[]{:S(2)}) async-start(bf16[16,48,128]{2,1,0:T(8,128)(2,1)} %get-tuple-element.85), calls=%async_computation.2 | async-start | bytes 393216 | tf_op jit(solution)/shard_map/all_to_all | solution.py:703
  170.8 4.3 %all-to-all-done.2.d_ref = bf16[16,48,128]{2,1,0:T(8,128)(2,1)S(1)} async-done(((bf16[16,48,128]{2,1,0:T(8,128)(2,1)}), bf16[16,48,128]{2,1,0:T(8,128)(2,1)S(1)}, u32[]{:S(2)}, u32[]{:S(2)}) %all-to-all-start.2) | async-done | bytes 196640 | tf_op jit(solution)/shard_map/all_to_all | solution.py:703
  175.1 7.3 %shard_map.161 = (bf16[16,144,128]{2,1,0:T(8,128)(2,1)S(1)}, bf16[16,64,128]{2,1,0:T(8,128)(2,1)S(1)}) custom-call(bf16[16,144,128]{2,1,0:T(8,128)(2,1)S(1)} %all_to_all.20.got_ref, bf16[16,64,128]{2,1,0:T(8,128)(2,1)S(1)} %collective-permute-done.20.other_ref, s32[1024,1]{1,0:T(8,128)S(1)} %copy.19.own_seg_ref, s32[1024,1]{1,0:T(8,128)S(1)} %copy.20.shared_seg_ref, ...), custom_call_target="tpu_custom_call" | custom-call | flops 1024 | bytes 1024 | tf_op jit(solution)/shard_map/pallas_call | solution.py:65
  185.1 4.3 %all-to-all-start.3 = ((bf16[16,144,128]{2,1,0:T(8,128)(2,1)}), bf16[16,144,128]{2,1,0:T(8,128)(2,1)}, u32[]{:S(2)}, u32[]{:S(2)}) async-start(bf16[16,144,128]{2,1,0:T(8,128)(2,1)} %add_convert_fusion), calls=%async_computation.3 | async-start | bytes 1179648 | tf_op jit(solution)/shard_map/all_to_all | solution.py:703
  189.7 1.7 collective-permute-start.23
  191.4 10.9 %collective-permute-done.23.refs_5_ = bf16[4,216,128]{2,1,0:T(8,128)(2,1)S(1)} collective-permute-done((bf16[4,216,128]{2,1,0:T(8,128)(2,1)S(1)}, bf16[4,216,128]{2,1,0:T(8,128)(2,1)S(1)}, u32[]{:S(2)}, u32[]{:S(2)}) %collective-permute-start.23) | collective-permute-done | bytes 221216 | tf_op jit(solution)/shard_map/ppermute | solution.py:712
  202.3 5.3 %collective-permute-done.24.refs_6_ = bf16[4,216,128]{2,1,0:T(8,128)(2,1)S(1)} collective-permute-done((bf16[4,216,128]{2,1,0:T(8,128)(2,1)S(1)}, bf16[4,216,128]{2,1,0:T(8,128)(2,1)S(1)}, u32[]{:S(2)}, u32[]{:S(2)}) %collective-permute-start.24) | collective-permute-done | bytes 221216 | tf_op jit(solution)/shard_map/ppermute | solution.py:712
  207.6 4.8 %shard_map.162 = (bf16[128,2304]{1,0:T(8,128)(2,1)}, f32[1,768]{1,0:T(1,128)}, bf16[64,768]{1,0:T(8,128)(2,1)}, bf16[64,768]{1,0:T(8,128)(2,1)}) custom-call(bf16[768,2432]{1,0:T(8,128)(2,1)} %bitcast.23.first_ref, bf16[16,144,128]{2,1,0:T(8,128)(2,1)} %all-to-all-done.3.got_ref, f32[128,768]{1,0:T(8,128)} %get-tuple-element.94.d_middle_ref, ...), custom_call_target="tpu_custom_call" | custom-call | flops 1024 | bytes 1024 | tf_op jit(solution)/shard_map/pallas_call | solution.py:65
  215.0 5.1 %collective-permute-done.25.refs_2_ = bf16[64,768]{1,0:T(8,128)(2,1)S(1)} collective-permute-done((bf16[64,768]{1,0:T(8,128)(2,1)}, bf16[64,768]{1,0:T(8,128)(2,1)S(1)}, u32[]{:S(2)}, u32[]{:S(2)}) %collective-permute-start.25) | collective-permute-done | bytes 98336 | tf_op jit(solution)/shard_map/ppermute | solution.py:708
  220.1 1.5 collective-permute-done.26.refs_3_
  223.5 6.1 %shard_map.163 = (f32[1,768]{1,0:T(1,128)S(1)}, f32[128,768]{1,0:T(8,128)S(1)}, bf16[128,768]{1,0:T(8,128)(2,1)S(1)}, bf16[128,3072]{1,0:T(8,128)(2,1)S(1)}) custom-call(bf16[768,4352]{1,0:T(8,128)(2,1)} %all-gather.2.cloned.1.call-done.refs_0_, s32[1]{0:T(128)} %bitcast.37.lower_ref.refs_1_, bf16[64,768]{1,0:T(8,128)(2,1)S(1)} %collective-permute-done.25.refs_2_, ...), custom_call_target="tpu_custom_call" | custom-call | flops 1024 | bytes 1024 | tf_op jit(solution)/shard_map/pallas_call | solution.py:65
  229.9 1.7 collective-permute-start.33
  232.0 1.7 collective-permute-start.30
  233.8 3.5 %shard_map.164 = (bf16[128,768]{1,0:T(8,128)(2,1)S(1)}, f32[128,1536]{1,0:T(8,128)S(1)}, bf16[128,1536]{1,0:T(8,128)(2,1)S(1)}, bf16[128,1536]{1,0:T(8,128)(2,1)S(1)}) custom-call(bf16[128,768]{1,0:T(8,128)(2,1)S(1)} %copy-done.19, bf16[128,1536]{1,0:T(8,128)(2,1)S(1)} %copy-done.12, bf16[128,1536]{1,0:T(8,128)(2,1)S(1)} %copy-done.10, ...), custom_call_target="tpu_custom_call" | custom-call | flops 1024 | bytes 1024 | tf_op jit(solution)/shard_map/pallas_call | solution.py:65
  238.6 3.1 collective-permute-start.31
  243.0 4.0 %shard_map.166 = (bf16[144,2304]{1,0:T(8,128)(2,1)S(1)}, bf16[128,768]{1,0:T(8,128)(2,1)S(1)}, f32[1,768]{1,0:T(1,128)}) custom-call(s32[1]{0:T(128)} %bitcast.37.lower_ref.refs_1_, bf16[768,2432]{1,0:T(8,128)(2,1)} %bitcast.23.first_ref, bf16[128,768]{1,0:T(8,128)(2,1)S(1)} %get-tuple-element.101.dq_ref, f32[128,1536]{1,0:T(8,128)S(1)} %get-tuple-element.102.own_ref, ...), custom_call_target="tpu_custom_call" | custom-call | flops 1024 | bytes 1024 | tf_op jit(solution)/shard_map/pallas_call | solution.py:65
  247.0 6.7 %collective-permute-done.33.refs_2_ = bf16[128,3072]{1,0:T(8,128)(2,1)S(1)} collective-permute-done((bf16[128,3072]{1,0:T(8,128)(2,1)S(1)}, bf16[128,3072]{1,0:T(8,128)(2,1)S(1)}, u32[]{:S(2)}, u32[]{:S(2)}) %collective-permute-start.33) | collective-permute-done | bytes 786464 | tf_op jit(solution)/shard_map/ppermute | solution.py:712
  253.8 8.0 %collective-permute-start.34 = (bf16[256,3072]{1,0:T(8,128)(2,1)S(1)}, bf16[256,3072]{1,0:T(8,128)(2,1)S(1)}, u32[]{:S(2)}, u32[]{:S(2)}) collective-permute-start(bf16[256,3072]{1,0:T(8,128)(2,1)S(1)} %pad_maximum_fusion), channel_id=1, source_target_pairs={{0,1},{1,0},{2,3},{3,2},{4,5},{5,4},{6,7},{7,6},{8,9},{9,8},{10,11... | collective-permute-start | bytes 4718600 | tf_op jit(solution)/shard_map/ppermute | solution.py:712
  261.8 3.0 collective-permute-done.34.refs_1_
  265.7 2.3 collective-permute-start.35
  268.0 2.0 collective-permute-start.32
  270.0 11.8 %collective-permute-done.35 = bf16[384,768]{1,0:T(8,128)(2,1)S(1)} collective-permute-done((bf16[384,768]{1,0:T(8,128)(2,1)S(1)}, bf16[384,768]{1,0:T(8,128)(2,1)S(1)}, u32[]{:S(2)}, u32[]{:S(2)}) %collective-permute-start.35) | collective-permute-done | bytes 589856 | tf_op jit(solution)/shard_map/ppermute | solution.py:712
  281.9 3.0 collective-permute-done.32.refs_2_
  285.1 2.4 collective-permute-start.39
  290.3 16.2 %collective-permute-done.39 = bf16[264,768]{1,0:T(8,128)(2,1)S(1)} collective-permute-done((bf16[264,768]{1,0:T(8,128)(2,1)S(1)}, bf16[264,768]{1,0:T(8,128)(2,1)S(1)}, u32[]{:S(2)}, u32[]{:S(2)}) %collective-permute-start.39) | collective-permute-done | bytes 405536 | tf_op jit(solution)/shard_map/ppermute | solution.py:712
  308.1 3.0 collective-permute-done.37
  312.0 11.1 %collective-permute-done.38 = bf16[48,2432]{1,0:T(8,128)(2,1)S(1)} collective-permute-done((bf16[48,2432]{1,0:T(8,128)(2,1)S(1)}, bf16[48,2432]{1,0:T(8,128)(2,1)S(1)}, u32[]{:S(2)}, u32[]{:S(2)}) %collective-permute-start.38) | collective-permute-done | bytes 233504 | tf_op jit(solution)/shard_map/ppermute | solution.py:712
  (221 shorter events, 51.2 us)
Async XLA Ops:
  7.2 86.7 %all-gather.2.cloned.1.call-start = ((), (), s32[]{:S(2)}) async-start(), calls=%async_computation.4 | async-start | bytes 7102464 | tf_op jit(solution)/shard_map/all_gather | solution.py:896
  9.0 11.7 %collective-permute-start.1 = (bf16[48,2432]{1,0:T(8,128)(2,1)}, bf16[48,2432]{1,0:T(8,128)(2,1)S(1)}, u32[]{:S(2)}, u32[]{:S(2)}) collective-permute-start(bf16[48,2432]{1,0:T(8,128)(2,1)} %shard_map.153), channel_id=1, source_target_pairs={{0,2},{1,3},{2,0},{3,1},{4,6},{5,7},{6,4},{7,5},{8,10},{9,11},{10,... | collective-permute-start | bytes 700424 | tf_op jit(solution)/shard_map/ppermute | solution.py:712
  12.0 12.6 %collective-permute-start.2 = (bf16[48,2432]{1,0:T(8,128)(2,1)}, bf16[48,2432]{1,0:T(8,128)(2,1)S(1)}, u32[]{:S(2)}, u32[]{:S(2)}) collective-permute-start(bf16[48,2432]{1,0:T(8,128)(2,1)} %shard_map.153), channel_id=1, source_target_pairs={{0,4},{1,5},{2,6},{3,7},{4,0},{5,1},{6,2},{7,3},{8,12},{9,13},{10,... | collective-permute-start | bytes 700424 | tf_op jit(solution)/shard_map/ppermute | solution.py:712
  13.5 19.7 %collective-permute-start.3 = (bf16[48,2432]{1,0:T(8,128)(2,1)}, bf16[48,2432]{1,0:T(8,128)(2,1)S(1)}, u32[]{:S(2)}, u32[]{:S(2)}) collective-permute-start(bf16[48,2432]{1,0:T(8,128)(2,1)} %shard_map.153), channel_id=1, source_target_pairs={{0,8},{1,9},{2,10},{3,11},{4,12},{5,13},{6,14},{7,15},{8,0},{9,1},... | collective-permute-start | bytes 700424 | tf_op jit(solution)/shard_map/ppermute | solution.py:712
  16.1 17.7 %collective-permute-start.4 = (bf16[48,2432]{1,0:T(8,128)(2,1)}, bf16[48,2432]{1,0:T(8,128)(2,1)S(1)}, u32[]{:S(2)}, u32[]{:S(2)}) collective-permute-start(bf16[48,2432]{1,0:T(8,128)(2,1)} %shard_map.153), channel_id=1, source_target_pairs={{0,12},{1,13},{2,14},{3,15},{4,8},{5,9},{6,10},{7,11},{8,4},{9,5},... | collective-permute-start | bytes 700424 | tf_op jit(solution)/shard_map/ppermute | solution.py:712
  17.1 1.2 collective-permute-start
  18.2 29.5 %collective-permute-start.8 = (bf16[48,2432]{1,0:T(8,128)(2,1)}, bf16[48,2432]{1,0:T(8,128)(2,1)S(1)}, u32[]{:S(2)}, u32[]{:S(2)}) collective-permute-start(bf16[48,2432]{1,0:T(8,128)(2,1)} %shard_map.153), channel_id=1, source_target_pairs={{0,1},{1,0},{2,3},{3,2},{4,5},{5,4},{6,7},{7,6},{8,9},{9,8},{10,11... | collective-permute-start | bytes 700424 | tf_op jit(solution)/shard_map/ppermute | solution.py:712
  24.3 24.6 %collective-permute-start.9 = (bf16[48,2432]{1,0:T(8,128)(2,1)S(1)}, bf16[48,2432]{1,0:T(8,128)(2,1)S(1)}, u32[]{:S(2)}, u32[]{:S(2)}) collective-permute-start(bf16[48,2432]{1,0:T(8,128)(2,1)S(1)} %collective-permute-done.1), channel_id=1, source_target_pairs={{0,1},{1,0},{2,3},{3,2},{4,5},{5,4},{6,7},{7,6},{8,9},{9,8},{10,11... | collective-permute-start | bytes 700424 | tf_op jit(solution)/shard_map/ppermute | solution.py:712
  24.6 13.6 %collective-permute-start.5 = (bf16[48,2432]{1,0:T(8,128)(2,1)S(1)}, bf16[48,2432]{1,0:T(8,128)(2,1)S(1)}, u32[]{:S(2)}, u32[]{:S(2)}) collective-permute-start(bf16[48,2432]{1,0:T(8,128)(2,1)S(1)} %collective-permute-done.2), channel_id=1, source_target_pairs={{0,2},{1,3},{2,0},{3,1},{4,6},{5,7},{6,4},{7,5},{8,10},{9,11},{10,... | collective-permute-start | bytes 700424 | tf_op jit(solution)/shard_map/ppermute | solution.py:712
  33.3 10.2 %collective-permute-start.6 = (bf16[48,2432]{1,0:T(8,128)(2,1)S(1)}, bf16[48,2432]{1,0:T(8,128)(2,1)S(1)}, u32[]{:S(2)}, u32[]{:S(2)}) collective-permute-start(bf16[48,2432]{1,0:T(8,128)(2,1)S(1)} %collective-permute-done.3), channel_id=1, source_target_pairs={{0,2},{1,3},{2,0},{3,1},{4,6},{5,7},{6,4},{7,5},{8,10},{9,11},{10,... | collective-permute-start | bytes 700424 | tf_op jit(solution)/shard_map/ppermute | solution.py:712
  33.8 13.2 %collective-permute-start.7 = (bf16[48,2432]{1,0:T(8,128)(2,1)S(1)}, bf16[48,2432]{1,0:T(8,128)(2,1)S(1)}, u32[]{:S(2)}, u32[]{:S(2)}) collective-permute-start(bf16[48,2432]{1,0:T(8,128)(2,1)S(1)} %collective-permute-done.4), channel_id=1, source_target_pairs={{0,2},{1,3},{2,0},{3,1},{4,6},{5,7},{6,4},{7,5},{8,10},{9,11},{10,... | collective-permute-start | bytes 700424 | tf_op jit(solution)/shard_map/ppermute | solution.py:712
  38.2 11.5 %collective-permute-start.10 = (bf16[48,2432]{1,0:T(8,128)(2,1)S(1)}, bf16[48,2432]{1,0:T(8,128)(2,1)S(1)}, u32[]{:S(2)}, u32[]{:S(2)}) collective-permute-start(bf16[48,2432]{1,0:T(8,128)(2,1)S(1)} %collective-permute-done.2), channel_id=1, source_target_pairs={{0,1},{1,0},{2,3},{3,2},{4,5},{5,4},{6,7},{7,6},{8,9},{9,8},{10,11... | collective-permute-start | bytes 700424 | tf_op jit(solution)/shard_map/ppermute | solution.py:712
  43.5 8.1 %collective-permute-start.12 = (bf16[48,2432]{1,0:T(8,128)(2,1)S(1)}, bf16[48,2432]{1,0:T(8,128)(2,1)S(1)}, u32[]{:S(2)}, u32[]{:S(2)}) collective-permute-start(bf16[48,2432]{1,0:T(8,128)(2,1)S(1)} %collective-permute-done.3), channel_id=1, source_target_pairs={{0,1},{1,0},{2,3},{3,2},{4,5},{5,4},{6,7},{7,6},{8,9},{9,8},{10,11... | collective-permute-start | bytes 700424 | tf_op jit(solution)/shard_map/ppermute | solution.py:712
  47.0 6.0 %collective-permute-start.14 = (bf16[48,2432]{1,0:T(8,128)(2,1)S(1)}, bf16[48,2432]{1,0:T(8,128)(2,1)S(1)}, u32[]{:S(2)}, u32[]{:S(2)}) collective-permute-start(bf16[48,2432]{1,0:T(8,128)(2,1)S(1)} %collective-permute-done.4), channel_id=1, source_target_pairs={{0,1},{1,0},{2,3},{3,2},{4,5},{5,4},{6,7},{7,6},{8,9},{9,8},{10,11... | collective-permute-start | bytes 700424 | tf_op jit(solution)/shard_map/ppermute | solution.py:712
  47.7 3.2 collective-permute-start.11
  48.9 3.4 %collective-permute-start.13 = (bf16[48,2432]{1,0:T(8,128)(2,1)S(1)}, bf16[48,2432]{1,0:T(8,128)(2,1)S(1)}, u32[]{:S(2)}, u32[]{:S(2)}) collective-permute-start(bf16[48,2432]{1,0:T(8,128)(2,1)S(1)} %collective-permute-done.6), channel_id=1, source_target_pairs={{0,1},{1,0},{2,3},{3,2},{4,5},{5,4},{6,7},{7,6},{8,9},{9,8},{10,11... | collective-permute-start | bytes 700424 | tf_op jit(solution)/shard_map/ppermute | solution.py:712
  49.7 4.0 %collective-permute-start.15 = (bf16[48,2432]{1,0:T(8,128)(2,1)S(1)}, bf16[48,2432]{1,0:T(8,128)(2,1)S(1)}, u32[]{:S(2)}, u32[]{:S(2)}) collective-permute-start(bf16[48,2432]{1,0:T(8,128)(2,1)S(1)} %collective-permute-done.7), channel_id=1, source_target_pairs={{0,1},{1,0},{2,3},{3,2},{4,5},{5,4},{6,7},{7,6},{8,9},{9,8},{10,11... | collective-permute-start | bytes 700424 | tf_op jit(solution)/shard_map/ppermute | solution.py:712
  58.7 40.7 %copy-start.9 = (bf16[128,1536]{1,0:T(8,128)(2,1)}, bf16[128,1536]{1,0:T(8,128)(2,1)S(1)}, u32[]{:S(2)}) copy-start(bf16[128,1536]{1,0:T(8,128)(2,1)S(1)} %get-tuple-element.73.own_ref) | copy-start | bytes 1179652
  58.7 40.7 %copy-start.18 = (bf16[128,768]{1,0:T(8,128)(2,1)}, bf16[128,768]{1,0:T(8,128)(2,1)S(1)}, u32[]{:S(2)}) copy-start(bf16[128,768]{1,0:T(8,128)(2,1)S(1)} %get-tuple-element.72.q_ref) | copy-start | bytes 589828
  58.7 4.8 %collective-permute-start.16 = (bf16[128,1536]{1,0:T(8,128)(2,1)S(1)}, bf16[128,1536]{1,0:T(8,128)(2,1)S(1)}, u32[]{:S(2)}, u32[]{:S(2)}) collective-permute-start(bf16[128,1536]{1,0:T(8,128)(2,1)S(1)} %get-tuple-element.73.own_ref), channel_id=1, source_target_pairs={{0,1},{1,2},{2,3},{3,4},{4,5},{5,6},{6,7},{7,8},{8,9},{9,10},{10,1... | collective-permute-start | bytes 1179656 | tf_op jit(solution)/shard_map/ppermute | solution.py:943
  60.9 3.6 %collective-permute-start.17 = (bf16[128,1536]{1,0:T(8,128)(2,1)S(1)}, bf16[128,1536]{1,0:T(8,128)(2,1)S(1)}, u32[]{:S(2)}, u32[]{:S(2)}) collective-permute-start(bf16[128,1536]{1,0:T(8,128)(2,1)S(1)} %get-tuple-element.73.own_ref), channel_id=1, source_target_pairs={{1,0},{2,1},{3,2},{4,3},{5,4},{6,5},{7,6},{8,7},{9,8},{10,9},{11,1... | collective-permute-start | bytes 1179656 | tf_op jit(solution)/shard_map/ppermute | solution.py:945
  62.9 36.6 %copy-start.6 = (f32[2,192,128]{2,1,0:T(8,128)}, f32[2,192,128]{2,1,0:T(8,128)S(1)}, u32[]{:S(2)}) copy-start(f32[2,192,128]{2,1,0:T(8,128)S(1)} %copy.18.bias_ref) | copy-start | bytes 589828
  63.5 44.3 %copy-start.29 = (f32[1,768]{1,0:T(1,128)}, f32[1,768]{1,0:T(1,128)S(1)}, u32[]{:S(2)}) copy-start(f32[1,768]{1,0:T(1,128)S(1)} %get-tuple-element.152.gain_ref) | copy-start | bytes 9220
  63.5 35.9 %copy-start.11 = (bf16[128,1536]{1,0:T(8,128)(2,1)}, bf16[128,1536]{1,0:T(8,128)(2,1)S(1)}, u32[]{:S(2)}) copy-start(bf16[128,1536]{1,0:T(8,128)(2,1)S(1)} %collective-permute-done.16.before_ref) | copy-start | bytes 1179652
  99.5 6.9 %collective-permute-start.18 = (bf16[64,768]{1,0:T(8,128)(2,1)}, bf16[64,768]{1,0:T(8,128)(2,1)S(1)}, u32[]{:S(2)}, u32[]{:S(2)}) collective-permute-start(bf16[64,768]{1,0:T(8,128)(2,1)} %get-tuple-element.76), channel_id=1, source_target_pairs={{0,16},{1,17},{2,18},{3,19},{4,20},{5,21},{6,22},{7,23},{8,24},{9,... | collective-permute-start | bytes 294920 | tf_op jit(solution)/shard_map/ppermute | solution.py:708
  102.9 4.9 %collective-permute-start.19 = (bf16[64,768]{1,0:T(8,128)(2,1)}, bf16[64,768]{1,0:T(8,128)(2,1)S(1)}, u32[]{:S(2)}, u32[]{:S(2)}) collective-permute-start(bf16[64,768]{1,0:T(8,128)(2,1)} %get-tuple-element.77), channel_id=1, source_target_pairs={{0,16},{1,17},{2,18},{3,19},{4,20},{5,21},{6,22},{7,23},{8,24},{9,... | collective-permute-start | bytes 294920 | tf_op jit(solution)/shard_map/ppermute | solution.py:708
  134.7 1.6 collective-permute-start.20
  162.6 12.5 %all-to-all-start.2 = ((bf16[16,48,128]{2,1,0:T(8,128)(2,1)}), bf16[16,48,128]{2,1,0:T(8,128)(2,1)S(1)}, u32[]{:S(2)}, u32[]{:S(2)}) async-start(bf16[16,48,128]{2,1,0:T(8,128)(2,1)} %get-tuple-element.85), calls=%async_computation.2 | async-start | bytes 393216 | tf_op jit(solution)/shard_map/all_to_all | solution.py:703
  182.4 1.6 collective-permute-start.21
  185.1 22.5 %all-to-all-start.3 = ((bf16[16,144,128]{2,1,0:T(8,128)(2,1)}), bf16[16,144,128]{2,1,0:T(8,128)(2,1)}, u32[]{:S(2)}, u32[]{:S(2)}) async-start(bf16[16,144,128]{2,1,0:T(8,128)(2,1)} %add_convert_fusion), calls=%async_computation.3 | async-start | bytes 1179648 | tf_op jit(solution)/shard_map/all_to_all | solution.py:703
  189.4 2.0 collective-permute-start.22
  189.7 12.6 %collective-permute-start.23 = (bf16[4,216,128]{2,1,0:T(8,128)(2,1)S(1)}, bf16[4,216,128]{2,1,0:T(8,128)(2,1)S(1)}, u32[]{:S(2)}, u32[]{:S(2)}) collective-permute-start(bf16[4,216,128]{2,1,0:T(8,128)(2,1)S(1)} %get-tuple-element.139), channel_id=1, source_target_pairs={{0,2},{1,3},{2,0},{3,1},{4,6},{5,7},{6,4},{7,5},{8,10},{9,11},{10,... | collective-permute-start | bytes 663560 | tf_op jit(solution)/shard_map/ppermute | solution.py:712
  191.4 16.2 %collective-permute-start.24 = (bf16[4,216,128]{2,1,0:T(8,128)(2,1)S(1)}, bf16[4,216,128]{2,1,0:T(8,128)(2,1)S(1)}, u32[]{:S(2)}, u32[]{:S(2)}) collective-permute-start(bf16[4,216,128]{2,1,0:T(8,128)(2,1)S(1)} %get-tuple-element.138), channel_id=1, source_target_pairs={{0,3},{1,2},{2,1},{3,0},{4,7},{5,6},{6,5},{7,4},{8,11},{9,10},{10,... | collective-permute-start | bytes 663560 | tf_op jit(solution)/shard_map/ppermute | solution.py:712
  212.4 7.7 %collective-permute-start.25 = (bf16[64,768]{1,0:T(8,128)(2,1)}, bf16[64,768]{1,0:T(8,128)(2,1)S(1)}, u32[]{:S(2)}, u32[]{:S(2)}) collective-permute-start(bf16[64,768]{1,0:T(8,128)(2,1)} %get-tuple-element.95), channel_id=1, source_target_pairs={{16,0},{17,1},{18,2},{19,3},{20,4},{21,5},{22,6},{23,7},{24,8},{25... | collective-permute-start | bytes 294920 | tf_op jit(solution)/shard_map/ppermute | solution.py:708
  213.7 7.9 %collective-permute-start.26 = (bf16[64,768]{1,0:T(8,128)(2,1)}, bf16[64,768]{1,0:T(8,128)(2,1)S(1)}, u32[]{:S(2)}, u32[]{:S(2)}) collective-permute-start(bf16[64,768]{1,0:T(8,128)(2,1)} %get-tuple-element.96), channel_id=1, source_target_pairs={{16,0},{17,1},{18,2},{19,3},{20,4},{21,5},{22,6},{23,7},{24,8},{25... | collective-permute-start | bytes 294920 | tf_op jit(solution)/shard_map/ppermute | solution.py:708
  221.7 8.1 %collective-permute-start.27 = (bf16[128,768]{1,0:T(8,128)(2,1)S(1)}, bf16[128,768]{1,0:T(8,128)(2,1)S(1)}, u32[]{:S(2)}, u32[]{:S(2)}) collective-permute-start(bf16[128,768]{1,0:T(8,128)(2,1)S(1)} %pad_maximum_fusion.5.refs_0_), channel_id=1, source_target_pairs={{0,2},{1,3},{2,0},{3,1},{4,6},{5,7},{6,4},{7,5},{8,10},{9,11},{10,... | collective-permute-start | bytes 589832 | tf_op jit(solution)/shard_map/ppermute | solution.py:712
  229.8 1.8 collective-permute-start.29
  229.9 23.8 %collective-permute-start.33 = (bf16[128,3072]{1,0:T(8,128)(2,1)S(1)}, bf16[128,3072]{1,0:T(8,128)(2,1)S(1)}, u32[]{:S(2)}, u32[]{:S(2)}) collective-permute-start(bf16[128,3072]{1,0:T(8,128)(2,1)S(1)} %get-tuple-element.121.refs_0_), channel_id=1, source_target_pairs={{0,2},{1,3},{2,0},{3,1},{4,6},{5,7},{6,4},{7,5},{8,10},{9,11},{10,... | collective-permute-start | bytes 2359304 | tf_op jit(solution)/shard_map/ppermute | solution.py:712
  232.0 9.6 %collective-permute-start.30 = (bf16[144,768]{1,0:T(8,128)(2,1)S(1)}, bf16[144,768]{1,0:T(8,128)(2,1)S(1)}, u32[]{:S(2)}, u32[]{:S(2)}) collective-permute-start(bf16[144,768]{1,0:T(8,128)(2,1)S(1)} %get-tuple-element.110), channel_id=1, source_target_pairs={{0,4},{1,5},{2,6},{3,7},{4,0},{5,1},{6,2},{7,3},{8,12},{9,13},{10,... | collective-permute-start | bytes 663560 | tf_op jit(solution)/shard_map/ppermute | solution.py:712
  237.3 4.4 %collective-permute-start.28 = (bf16[128,1536]{1,0:T(8,128)(2,1)S(1)}, bf16[128,1536]{1,0:T(8,128)(2,1)S(1)}, u32[]{:S(2)}, u32[]{:S(2)}) collective-permute-start(bf16[128,1536]{1,0:T(8,128)(2,1)S(1)} %get-tuple-element.103), channel_id=1, source_target_pairs={{1,0},{2,1},{3,2},{4,3},{5,4},{6,5},{7,6},{8,7},{9,8},{10,9},{11,1... | collective-permute-start | bytes 1179656 | tf_op jit(solution)/shard_map/ppermute | solution.py:1105
  238.6 4.4 %collective-permute-start.31 = (bf16[128,1536]{1,0:T(8,128)(2,1)S(1)}, bf16[128,1536]{1,0:T(8,128)(2,1)S(1)}, u32[]{:S(2)}, u32[]{:S(2)}) collective-permute-start(bf16[128,1536]{1,0:T(8,128)(2,1)S(1)} %get-tuple-element.112), channel_id=1, source_target_pairs={{0,1},{1,2},{2,3},{3,4},{4,5},{5,6},{6,7},{7,8},{8,9},{9,10},{10,1... | collective-permute-start | bytes 1179656 | tf_op jit(solution)/shard_map/ppermute | solution.py:1106
  253.8 11.0 %collective-permute-start.34 = (bf16[256,3072]{1,0:T(8,128)(2,1)S(1)}, bf16[256,3072]{1,0:T(8,128)(2,1)S(1)}, u32[]{:S(2)}, u32[]{:S(2)}) collective-permute-start(bf16[256,3072]{1,0:T(8,128)(2,1)S(1)} %pad_maximum_fusion), channel_id=1, source_target_pairs={{0,1},{1,0},{2,3},{3,2},{4,5},{5,4},{6,7},{7,6},{8,9},{9,8},{10,11... | collective-permute-start | bytes 4718600 | tf_op jit(solution)/shard_map/ppermute | solution.py:712
  265.7 16.1 %collective-permute-start.35 = (bf16[384,768]{1,0:T(8,128)(2,1)S(1)}, bf16[384,768]{1,0:T(8,128)(2,1)S(1)}, u32[]{:S(2)}, u32[]{:S(2)}) collective-permute-start(bf16[384,768]{1,0:T(8,128)(2,1)S(1)} %get-tuple-element.124), channel_id=1, source_target_pairs={{0,4},{1,5},{2,6},{3,7},{4,0},{5,1},{6,2},{7,3},{8,12},{9,13},{10,... | collective-permute-start | bytes 1769480 | tf_op jit(solution)/shard_map/ppermute | solution.py:712
  268.0 16.9 %collective-permute-start.32 = (bf16[144,2304]{1,0:T(8,128)(2,1)S(1)}, bf16[144,2304]{1,0:T(8,128)(2,1)S(1)}, u32[]{:S(2)}, u32[]{:S(2)}) collective-permute-start(bf16[144,2304]{1,0:T(8,128)(2,1)S(1)} %get-tuple-element.126.refs_0_), channel_id=1, source_target_pairs={{0,2},{1,3},{2,0},{3,1},{4,6},{5,7},{6,4},{7,5},{8,10},{9,11},{10,... | collective-permute-start | bytes 1990664 | tf_op jit(solution)/shard_map/ppermute | solution.py:712
  285.0 4.0 %collective-permute-start.36 = (bf16[288,2304]{1,0:T(8,128)(2,1)S(1)}, bf16[288,2304]{1,0:T(8,128)(2,1)S(1)}, u32[]{:S(2)}, u32[]{:S(2)}) collective-permute-start(bf16[288,2304]{1,0:T(8,128)(2,1)S(1)} %pad_maximum_fusion.1), channel_id=1, source_target_pairs={{0,1},{1,0},{2,3},{3,2},{4,5},{5,4},{6,7},{7,6},{8,9},{9,8},{10,11... | collective-permute-start | bytes 3981320 | tf_op jit(solution)/shard_map/ppermute | solution.py:712
  285.1 21.5 %collective-permute-start.39 = (bf16[264,768]{1,0:T(8,128)(2,1)S(1)}, bf16[264,768]{1,0:T(8,128)(2,1)S(1)}, u32[]{:S(2)}, u32[]{:S(2)}) collective-permute-start(bf16[264,768]{1,0:T(8,128)(2,1)S(1)} %pad_maximum_fusion.2), channel_id=1, source_target_pairs={{0,8},{1,9},{2,10},{3,11},{4,12},{5,13},{6,14},{7,15},{8,0},{9,1},... | collective-permute-start | bytes 1216520 | tf_op jit(solution)/shard_map/ppermute | solution.py:712
  289.7 21.4 %collective-permute-start.37 = (bf16[96,2432]{1,0:T(8,128)(2,1)S(1)}, bf16[96,2432]{1,0:T(8,128)(2,1)S(1)}, u32[]{:S(2)}, u32[]{:S(2)}) collective-permute-start(bf16[96,2432]{1,0:T(8,128)(2,1)S(1)} %get-tuple-element.129), channel_id=1, source_target_pairs={{0,4},{1,5},{2,6},{3,7},{4,0},{5,1},{6,2},{7,3},{8,12},{9,13},{10,... | collective-permute-start | bytes 1400840 | tf_op jit(solution)/shard_map/ppermute | solution.py:712
  311.2 11.9 %collective-permute-start.38 = (bf16[48,2432]{1,0:T(8,128)(2,1)S(1)}, bf16[48,2432]{1,0:T(8,128)(2,1)S(1)}, u32[]{:S(2)}, u32[]{:S(2)}) collective-permute-start(bf16[48,2432]{1,0:T(8,128)(2,1)S(1)} %add_convert_fusion.2), channel_id=1, source_target_pairs={{0,8},{1,9},{2,10},{3,11},{4,12},{5,13},{6,14},{7,15},{8,0},{9,1},... | collective-permute-start | bytes 700424 | tf_op jit(solution)/shard_map/ppermute | solution.py:712
  (36 other events, 574.0 us)
Sparse Core Ops, SparseCore 0:
  20.8 73.0 all-gather.1

commit v16 on v14

--- a/solution.py
+++ b/solution.py
@@ -13,7 +13,7 @@
 HALF_WIN = 64
 EXTRA = 16
 LANES = 128
-TILE = 256
+TILE = 512
 
 local_log_base = math.log(10000.0)
 global_log_base = math.log(160000.0)

time: 332 us -> 329 us (level)
  no operation moved by 1% of the time
where the time goes in v16:
time: 329 us
  waiting for transfers between devices  130 us (40%)
  Pallas kernels  60.1 us (18%)
  starting transfers between devices  55.9 us (17%)
  blocking collectives  35.9 us (11%)
  local copies, waits for them, and re-layouts  27 us (8%)
  between operations  14.8 us (4%)
  other arithmetic  5.12 us (2%)
    ppermute x35, waiting for transfers between devices, partner(): return lax.ppermute(rows, 'dp', [(i, i ^ apart) for i in range(count)])  88.2 us
    pallas_call x17, Pallas kernels, on_core(): pl.pallas_call(body, out_shape=[jax.ShapeDtypeStruct(shape, dtype) for sh...  60.1 us
    all_to_all x2, blocking collectives, exchange(): return lax.all_to_all(blocks, 'dp', 0, 0, axis_index_groups=groups)  35.9 us
    ppermute x35, starting transfers between devices, partner(): return lax.ppermute(rows, 'dp', [(i, i ^ apart) for i in range(count)])  32.1 us
    all_gather x1, waiting for transfers between devices, on_device(): others = [lax.all_gather(stacked, 'dp', axis=0, tiled=True)]  25 us
    dynamic_update_slice x16, local copies, waits for them, and re-layouts, gather_rows(): whole = lax.dynamic_update_slice(whole, item[None], start)  11.4 us
    ppermute x4, waiting for transfers between devices, to_other_section(): return [lax.ppermute(rows, 'section', pairs) for rows in chunks]  9.82 us
    all_to_all x2, starting transfers between devices, exchange(): return lax.all_to_all(blocks, 'dp', 0, 0, axis_index_groups=groups)  8.56 us
  transfers between devices with their start and end apart: 46, of which 26 were waited for; matrix products, arithmetic and copies ran while one was open for 7% of the time, Pallas kernels for 7%

profile of v16, /device:TPU:0, one launch (start us, length us, event | category | flops | bytes accessed | tf_op | source)
XLA Modules:
  0.0 328.6 jit_solution(16805242525895977248)
XLA Ops:
  7.2 1.8 shard_map.153
  9.0 2.9 collective-permute-start.1
  12.0 1.6 collective-permute-start.2
  13.5 2.6 collective-permute-start.3
  18.8 1.8 shard_map.152
  20.9 2.1 broadcast_in_dim.105
  24.9 8.4 %collective-permute-done.3 = bf16[48,2432]{1,0:T(8,128)(2,1)S(1)} collective-permute-done((bf16[48,2432]{1,0:T(8,128)(2,1)}, bf16[48,2432]{1,0:T(8,128)(2,1)S(1)}, u32[]{:S(2)}, u32[]{:S(2)}) %collective-permute-start.3) | collective-permute-done | bytes 233504 | tf_op jit(solution)/shard_map/ppermute | solution.py:712
  38.9 4.6 %collective-permute-done.6 = bf16[48,2432]{1,0:T(8,128)(2,1)S(1)} collective-permute-done((bf16[48,2432]{1,0:T(8,128)(2,1)S(1)}, bf16[48,2432]{1,0:T(8,128)(2,1)S(1)}, u32[]{:S(2)}, u32[]{:S(2)}) %collective-permute-start.6) | collective-permute-done | bytes 233504 | tf_op jit(solution)/shard_map/ppermute | solution.py:712
  44.2 2.8 collective-permute-done.7
  54.4 3.6 %shard_map.154 = (f32[8,768]{1,0:T(8,128)S(1)}, bf16[128,768]{1,0:T(8,128)(2,1)S(1)}, bf16[128,768]{1,0:T(8,128)(2,1)S(1)}, bf16[128,1536]{1,0:T(8,128)(2,1)S(1)}) custom-call(bf16[768,2432]{1,0:T(8,128)(2,1)} %bitcast.23.first_ref, bf16[128,768]{1,0:T(8,128)(2,1)S(1)} %bitcast.90, f32[3,128,128]{2,1,0:T(8,128)S(1)} %tile.13.table_ref), custom_call_target="tpu_custom_call" | custom-call | flops 1024 | bytes 1024 | tf_op jit(solution)/shard_map/pallas_call | solution.py:65
  58.7 2.2 collective-permute-start.16
  64.6 3.6 %shard_map.155 = (bf16[128,768]{1,0:T(8,128)(2,1)S(1)}, f32[12,1,128]{2,1,0:T(1,128)S(1)}) custom-call(bf16[128,768]{1,0:T(8,128)(2,1)S(1)} %get-tuple-element.72.q_ref, bf16[128,1536]{1,0:T(8,128)(2,1)S(1)} %collective-permute-done.16.before_ref, bf16[128,1536]{1,0:T(8,128)(2,1)S(1)} %get-tuple-element.73.own_ref, ...), custom_call_target="tpu_custom_call" | custom-call | flops 1024 | bytes 1024 | tf_op jit(solution)/shard_map/pallas_call | solution.py:65
  68.9 25.0 %all-gather.2.cloned.1.call-done.refs_0_ = bf16[768,4352]{1,0:T(8,128)(2,1)} async-done(((bf16[48,4352]{1,0:T(8,128)(2,1)}), bf16[768,4352]{1,0:T(8,128)(2,1)}) %all-gather.2.cloned.1.call-update) | async-done | bytes 6684688 | tf_op jit(solution)/shard_map/all_gather | solution.py:883
  93.9 5.5 %shard_map.156 = (bf16[128,1920]{1,0:T(8,128)(2,1)}, f32[128,3072]{1,0:T(8,128)}, bf16[64,768]{1,0:T(8,128)(2,1)}, bf16[64,768]{1,0:T(8,128)(2,1)}) custom-call(bf16[768,4352]{1,0:T(8,128)(2,1)} %all-gather.2.cloned.1.call-done.refs_0_, bf16[128,768]{1,0:T(8,128)(2,1)} %bitcast.89, bf16[128,768]{1,0:T(8,128)(2,1)} %copy-done.18, ...), custom_call_target="tpu_custom_call" | custom-call | flops 1024 | bytes 1024 | tf_op jit(solution)/shard_map/pallas_call | solution.py:65
  99.4 3.5 %collective-permute-start.18 = (bf16[64,768]{1,0:T(8,128)(2,1)}, bf16[64,768]{1,0:T(8,128)(2,1)S(1)}, u32[]{:S(2)}, u32[]{:S(2)}) collective-permute-start(bf16[64,768]{1,0:T(8,128)(2,1)} %get-tuple-element.76), channel_id=1, source_target_pairs={{0,16},{1,17},{2,18},{3,19},{4,20},{5,21},{6,22},{7,23},{8,24},{9,... | collective-permute-start | bytes 294920 | tf_op jit(solution)/shard_map/ppermute | solution.py:708
  104.6 1.8 collective-permute-done.18.low_ref.refs_2_
  107.8 3.2 shard_map.157
  111.0 23.6 %all_to_all.20.got_ref = bf16[16,144,128]{2,1,0:T(8,128)(2,1)S(1)} all-to-all(bf16[16,144,128]{2,1,0:T(8,128)(2,1)S(1)} %get-tuple-element.78), channel_id=1, replica_groups={{0,1,2,3,4,5,6,7,8,9,10,11,12,13,14,15},{16,17,18,19,20,21,22,23,24,25,..., dimensions={0} | all-to-all | bytes 1179648 | tf_op jit(solution)/shard_map/all_to_all | solution.py:703
  136.3 4.7 %shard_map.158 = (bf16[16,48,128]{2,1,0:T(8,128)(2,1)S(1)}, f32[3,1,512]{2,1,0:T(1,128)S(1)}) custom-call(bf16[16,144,128]{2,1,0:T(8,128)(2,1)S(1)} %all_to_all.20.got_ref, bf16[16,64,128]{2,1,0:T(8,128)(2,1)S(1)} %collective-permute-done.20.other_ref, s32[1024,1]{1,0:T(8,128)S(1)} %copy.19.own_seg_ref, s32[1024,1]{1,0:T(8,128)S(1)} %copy.20.shared_seg_ref), custom_call_target="tpu_custom_call" | custom-call | flops 1024 | bytes 1024 | tf_op jit(solution)/shard_map/pallas_call | solution.py:65
  141.0 12.3 %all_to_all.21.refs_1_ = bf16[16,48,128]{2,1,0:T(8,128)(2,1)} all-to-all(bf16[16,48,128]{2,1,0:T(8,128)(2,1)S(1)} %get-tuple-element.79), channel_id=1, replica_groups={{0,1,2,3,4,5,6,7,8,9,10,11,12,13,14,15},{16,17,18,19,20,21,22,23,24,25,..., dimensions={0} | all-to-all | bytes 393216 | tf_op jit(solution)/shard_map/all_to_all | solution.py:703
  153.3 7.9 %shard_map.159 = (bf16[128,6528]{1,0:T(8,128)(2,1)}, f32[1,768]{1,0:T(1,128)}, f32[128,768]{1,0:T(8,128)}, bf16[16,48,128]{2,1,0:T(8,128)(2,1)}) custom-call(bf16[768,4352]{1,0:T(8,128)(2,1)} %all-gather.2.cloned.1.call-done.refs_0_, bf16[16,48,128]{2,1,0:T(8,128)(2,1)} %all_to_all.21.refs_1_, bf16[64,768]{1,0:T(8,128)(2,1)} %copy-done.14, ...), custom_call_target="tpu_custom_call" | custom-call | flops 1024 | bytes 1024 | tf_op jit(solution)/shard_map/pallas_call | solution.py:65
  161.2 4.3 %all-to-all-start.2 = ((bf16[16,48,128]{2,1,0:T(8,128)(2,1)}), bf16[16,48,128]{2,1,0:T(8,128)(2,1)}, u32[]{:S(2)}, u32[]{:S(2)}) async-start(bf16[16,48,128]{2,1,0:T(8,128)(2,1)} %get-tuple-element.85), calls=%async_computation.2 | async-start | bytes 393216 | tf_op jit(solution)/shard_map/all_to_all | solution.py:703
  170.3 4.3 %all-to-all-done.2.d_ref = bf16[16,48,128]{2,1,0:T(8,128)(2,1)} async-done(((bf16[16,48,128]{2,1,0:T(8,128)(2,1)}), bf16[16,48,128]{2,1,0:T(8,128)(2,1)}, u32[]{:S(2)}, u32[]{:S(2)}) %all-to-all-start.2) | async-done | bytes 196640 | tf_op jit(solution)/shard_map/all_to_all | solution.py:703
  174.6 7.2 %shard_map.161 = (bf16[16,144,128]{2,1,0:T(8,128)(2,1)S(1)}, bf16[16,64,128]{2,1,0:T(8,128)(2,1)S(1)}) custom-call(bf16[16,144,128]{2,1,0:T(8,128)(2,1)S(1)} %all_to_all.20.got_ref, bf16[16,64,128]{2,1,0:T(8,128)(2,1)S(1)} %copy-done.13, s32[1024,1]{1,0:T(8,128)S(1)} %copy.19.own_seg_ref, s32[1024,1]{1,0:T(8,128)S(1)} %copy.20.shared_seg_ref, ...), custom_call_target="tpu_custom_call" | custom-call | flops 1024 | bytes 1024 | tf_op jit(solution)/shard_map/pallas_call | solution.py:65
  184.5 4.2 %all-to-all-start.3 = ((bf16[16,144,128]{2,1,0:T(8,128)(2,1)}), bf16[16,144,128]{2,1,0:T(8,128)(2,1)}, u32[]{:S(2)}, u32[]{:S(2)}) async-start(bf16[16,144,128]{2,1,0:T(8,128)(2,1)} %add_convert_fusion), calls=%async_computation.3 | async-start | bytes 1179648 | tf_op jit(solution)/shard_map/all_to_all | solution.py:703
  189.2 1.7 collective-permute-start.23
  190.9 10.9 %collective-permute-done.23.refs_6_ = bf16[4,216,128]{2,1,0:T(8,128)(2,1)S(1)} collective-permute-done((bf16[4,216,128]{2,1,0:T(8,128)(2,1)S(1)}, bf16[4,216,128]{2,1,0:T(8,128)(2,1)S(1)}, u32[]{:S(2)}, u32[]{:S(2)}) %collective-permute-start.23) | collective-permute-done | bytes 221216 | tf_op jit(solution)/shard_map/ppermute | solution.py:712
  201.8 5.3 %collective-permute-done.24.refs_7_ = bf16[4,216,128]{2,1,0:T(8,128)(2,1)S(1)} collective-permute-done((bf16[4,216,128]{2,1,0:T(8,128)(2,1)S(1)}, bf16[4,216,128]{2,1,0:T(8,128)(2,1)S(1)}, u32[]{:S(2)}, u32[]{:S(2)}) %collective-permute-start.24) | collective-permute-done | bytes 221216 | tf_op jit(solution)/shard_map/ppermute | solution.py:712
  207.1 4.7 %shard_map.162 = (bf16[128,2304]{1,0:T(8,128)(2,1)}, f32[1,768]{1,0:T(1,128)}, bf16[64,768]{1,0:T(8,128)(2,1)}, bf16[64,768]{1,0:T(8,128)(2,1)}) custom-call(bf16[768,2432]{1,0:T(8,128)(2,1)} %bitcast.23.first_ref, bf16[16,144,128]{2,1,0:T(8,128)(2,1)} %all-to-all-done.3.got_ref, f32[128,768]{1,0:T(8,128)} %get-tuple-element.94.d_middle_ref, ...), custom_call_target="tpu_custom_call" | custom-call | flops 1024 | bytes 1024 | tf_op jit(solution)/shard_map/pallas_call | solution.py:65
  214.4 5.1 %collective-permute-done.25.refs_2_ = bf16[64,768]{1,0:T(8,128)(2,1)S(1)} collective-permute-done((bf16[64,768]{1,0:T(8,128)(2,1)}, bf16[64,768]{1,0:T(8,128)(2,1)S(1)}, u32[]{:S(2)}, u32[]{:S(2)}) %collective-permute-start.25) | collective-permute-done | bytes 98336 | tf_op jit(solution)/shard_map/ppermute | solution.py:708
  219.5 1.5 collective-permute-done.26.refs_3_
  222.9 6.1 %shard_map.163 = (f32[1,768]{1,0:T(1,128)S(1)}, f32[128,768]{1,0:T(8,128)S(1)}, bf16[128,768]{1,0:T(8,128)(2,1)S(1)}, bf16[128,3072]{1,0:T(8,128)(2,1)S(1)}) custom-call(bf16[768,4352]{1,0:T(8,128)(2,1)} %all-gather.2.cloned.1.call-done.refs_0_, s32[1]{0:T(128)} %bitcast.37.lower_ref.refs_1_, bf16[64,768]{1,0:T(8,128)(2,1)S(1)} %collective-permute-done.25.refs_2_, ...), custom_call_target="tpu_custom_call" | custom-call | flops 1024 | bytes 1024 | tf_op jit(solution)/shard_map/pallas_call | solution.py:65
  229.1 1.7 collective-permute-start.34
  233.0 1.6 collective-permute-start.31
  234.5 3.5 %shard_map.164 = (bf16[128,768]{1,0:T(8,128)(2,1)S(1)}, f32[128,1536]{1,0:T(8,128)S(1)}, bf16[128,1536]{1,0:T(8,128)(2,1)S(1)}, bf16[128,1536]{1,0:T(8,128)(2,1)S(1)}) custom-call(bf16[128,768]{1,0:T(8,128)(2,1)S(1)} %copy-done.17, bf16[128,1536]{1,0:T(8,128)(2,1)S(1)} %copy-done.8, bf16[128,1536]{1,0:T(8,128)(2,1)S(1)} %copy-done.6, ...), custom_call_target="tpu_custom_call" | custom-call | flops 1024 | bytes 1024 | tf_op jit(solution)/shard_map/pallas_call | solution.py:65
  239.4 3.1 collective-permute-start.32
  243.8 4.0 %shard_map.166 = (bf16[144,2304]{1,0:T(8,128)(2,1)S(1)}, bf16[128,768]{1,0:T(8,128)(2,1)S(1)}, f32[1,768]{1,0:T(1,128)}) custom-call(s32[1]{0:T(128)} %bitcast.37.lower_ref.refs_1_, bf16[768,2432]{1,0:T(8,128)(2,1)} %bitcast.23.first_ref, bf16[128,768]{1,0:T(8,128)(2,1)S(1)} %get-tuple-element.101.dq_ref, f32[128,1536]{1,0:T(8,128)S(1)} %get-tuple-element.102.own_ref, ...), custom_call_target="tpu_custom_call" | custom-call | flops 1024 | bytes 1024 | tf_op jit(solution)/shard_map/pallas_call | solution.py:65
  247.8 5.2 %collective-permute-done.34.refs_2_ = bf16[128,3072]{1,0:T(8,128)(2,1)S(1)} collective-permute-done((bf16[128,3072]{1,0:T(8,128)(2,1)S(1)}, bf16[128,3072]{1,0:T(8,128)(2,1)S(1)}, u32[]{:S(2)}, u32[]{:S(2)}) %collective-permute-start.34) | collective-permute-done | bytes 786464 | tf_op jit(solution)/shard_map/ppermute | solution.py:712
  253.1 6.7 %collective-permute-start.35 = (bf16[128,3072]{1,0:T(8,128)(2,1)S(1)}, bf16[128,3072]{1,0:T(8,128)(2,1)S(1)}, u32[]{:S(2)}, u32[]{:S(2)}) collective-permute-start(bf16[128,3072]{1,0:T(8,128)(2,1)S(1)} %get-tuple-element.121.refs_0_), channel_id=1, source_target_pairs={{0,1},{1,0},{2,3},{3,2},{4,5},{5,4},{6,7},{7,6},{8,9},{9,8},{10,11... | collective-permute-start | bytes 2359304 | tf_op jit(solution)/shard_map/ppermute | solution.py:712
  259.8 1.8 collective-permute-done.35.refs_1_
  263.6 2.1 collective-permute-start.37
  265.7 2.2 collective-permute-start.33
  267.9 11.7 %collective-permute-done.37 = bf16[384,768]{1,0:T(8,128)(2,1)S(1)} collective-permute-done((bf16[384,768]{1,0:T(8,128)(2,1)S(1)}, bf16[384,768]{1,0:T(8,128)(2,1)S(1)}, u32[]{:S(2)}, u32[]{:S(2)}) %collective-permute-start.37) | collective-permute-done | bytes 589856 | tf_op jit(solution)/shard_map/ppermute | solution.py:712
  279.7 3.1 collective-permute-done.33.refs_2_
  283.3 2.3 collective-permute-start.42
  288.4 15.9 %collective-permute-done.42 = bf16[264,768]{1,0:T(8,128)(2,1)S(1)} collective-permute-done((bf16[264,768]{1,0:T(8,128)(2,1)S(1)}, bf16[264,768]{1,0:T(8,128)(2,1)S(1)}, u32[]{:S(2)}, u32[]{:S(2)}) %collective-permute-start.42) | collective-permute-done | bytes 405536 | tf_op jit(solution)/shard_map/ppermute | solution.py:712
  305.9 2.9 collective-permute-done.40
  309.6 10.6 %collective-permute-done.41 = bf16[48,2432]{1,0:T(8,128)(2,1)S(1)} collective-permute-done((bf16[48,2432]{1,0:T(8,128)(2,1)S(1)}, bf16[48,2432]{1,0:T(8,128)(2,1)S(1)}, u32[]{:S(2)}, u32[]{:S(2)}) %collective-permute-start.41) | collective-permute-done | bytes 233504 | tf_op jit(solution)/shard_map/ppermute | solution.py:712
  (220 shorter events, 54.2 us)
Async XLA Ops:
  7.2 86.7 %all-gather.2.cloned.1.call-start = ((), (), s32[]{:S(2)}) async-start(), calls=%async_computation.4 | async-start | bytes 7102464 | tf_op jit(solution)/shard_map/all_gather | solution.py:883
  9.0 11.7 %collective-permute-start.1 = (bf16[48,2432]{1,0:T(8,128)(2,1)}, bf16[48,2432]{1,0:T(8,128)(2,1)S(1)}, u32[]{:S(2)}, u32[]{:S(2)}) collective-permute-start(bf16[48,2432]{1,0:T(8,128)(2,1)} %shard_map.153), channel_id=1, source_target_pairs={{0,2},{1,3},{2,0},{3,1},{4,6},{5,7},{6,4},{7,5},{8,10},{9,11},{10,... | collective-permute-start | bytes 700424 | tf_op jit(solution)/shard_map/ppermute | solution.py:712
  12.0 12.6 %collective-permute-start.2 = (bf16[48,2432]{1,0:T(8,128)(2,1)}, bf16[48,2432]{1,0:T(8,128)(2,1)S(1)}, u32[]{:S(2)}, u32[]{:S(2)}) collective-permute-start(bf16[48,2432]{1,0:T(8,128)(2,1)} %shard_map.153), channel_id=1, source_target_pairs={{0,4},{1,5},{2,6},{3,7},{4,0},{5,1},{6,2},{7,3},{8,12},{9,13},{10,... | collective-permute-start | bytes 700424 | tf_op jit(solution)/shard_map/ppermute | solution.py:712
  13.5 19.7 %collective-permute-start.3 = (bf16[48,2432]{1,0:T(8,128)(2,1)}, bf16[48,2432]{1,0:T(8,128)(2,1)S(1)}, u32[]{:S(2)}, u32[]{:S(2)}) collective-permute-start(bf16[48,2432]{1,0:T(8,128)(2,1)} %shard_map.153), channel_id=1, source_target_pairs={{0,8},{1,9},{2,10},{3,11},{4,12},{5,13},{6,14},{7,15},{8,0},{9,1},... | collective-permute-start | bytes 700424 | tf_op jit(solution)/shard_map/ppermute | solution.py:712
  16.1 17.7 %collective-permute-start.4 = (bf16[48,2432]{1,0:T(8,128)(2,1)}, bf16[48,2432]{1,0:T(8,128)(2,1)S(1)}, u32[]{:S(2)}, u32[]{:S(2)}) collective-permute-start(bf16[48,2432]{1,0:T(8,128)(2,1)} %shard_map.153), channel_id=1, source_target_pairs={{0,12},{1,13},{2,14},{3,15},{4,8},{5,9},{6,10},{7,11},{8,4},{9,5},... | collective-permute-start | bytes 700424 | tf_op jit(solution)/shard_map/ppermute | solution.py:712
  17.1 1.2 collective-permute-start
  18.2 29.4 %collective-permute-start.8 = (bf16[48,2432]{1,0:T(8,128)(2,1)}, bf16[48,2432]{1,0:T(8,128)(2,1)S(1)}, u32[]{:S(2)}, u32[]{:S(2)}) collective-permute-start(bf16[48,2432]{1,0:T(8,128)(2,1)} %shard_map.153), channel_id=1, source_target_pairs={{0,1},{1,0},{2,3},{3,2},{4,5},{5,4},{6,7},{7,6},{8,9},{9,8},{10,11... | collective-permute-start | bytes 700424 | tf_op jit(solution)/shard_map/ppermute | solution.py:712
  24.3 24.6 %collective-permute-start.9 = (bf16[48,2432]{1,0:T(8,128)(2,1)S(1)}, bf16[48,2432]{1,0:T(8,128)(2,1)S(1)}, u32[]{:S(2)}, u32[]{:S(2)}) collective-permute-start(bf16[48,2432]{1,0:T(8,128)(2,1)S(1)} %collective-permute-done.1), channel_id=1, source_target_pairs={{0,1},{1,0},{2,3},{3,2},{4,5},{5,4},{6,7},{7,6},{8,9},{9,8},{10,11... | collective-permute-start | bytes 700424 | tf_op jit(solution)/shard_map/ppermute | solution.py:712
  24.5 13.6 %collective-permute-start.5 = (bf16[48,2432]{1,0:T(8,128)(2,1)S(1)}, bf16[48,2432]{1,0:T(8,128)(2,1)S(1)}, u32[]{:S(2)}, u32[]{:S(2)}) collective-permute-start(bf16[48,2432]{1,0:T(8,128)(2,1)S(1)} %collective-permute-done.2), channel_id=1, source_target_pairs={{0,2},{1,3},{2,0},{3,1},{4,6},{5,7},{6,4},{7,5},{8,10},{9,11},{10,... | collective-permute-start | bytes 700424 | tf_op jit(solution)/shard_map/ppermute | solution.py:712
  33.3 10.2 %collective-permute-start.6 = (bf16[48,2432]{1,0:T(8,128)(2,1)S(1)}, bf16[48,2432]{1,0:T(8,128)(2,1)S(1)}, u32[]{:S(2)}, u32[]{:S(2)}) collective-permute-start(bf16[48,2432]{1,0:T(8,128)(2,1)S(1)} %collective-permute-done.3), channel_id=1, source_target_pairs={{0,2},{1,3},{2,0},{3,1},{4,6},{5,7},{6,4},{7,5},{8,10},{9,11},{10,... | collective-permute-start | bytes 700424 | tf_op jit(solution)/shard_map/ppermute | solution.py:712
  33.8 13.2 %collective-permute-start.7 = (bf16[48,2432]{1,0:T(8,128)(2,1)S(1)}, bf16[48,2432]{1,0:T(8,128)(2,1)S(1)}, u32[]{:S(2)}, u32[]{:S(2)}) collective-permute-start(bf16[48,2432]{1,0:T(8,128)(2,1)S(1)} %collective-permute-done.4), channel_id=1, source_target_pairs={{0,2},{1,3},{2,0},{3,1},{4,6},{5,7},{6,4},{7,5},{8,10},{9,11},{10,... | collective-permute-start | bytes 700424 | tf_op jit(solution)/shard_map/ppermute | solution.py:712
  38.2 11.5 %collective-permute-start.10 = (bf16[48,2432]{1,0:T(8,128)(2,1)S(1)}, bf16[48,2432]{1,0:T(8,128)(2,1)S(1)}, u32[]{:S(2)}, u32[]{:S(2)}) collective-permute-start(bf16[48,2432]{1,0:T(8,128)(2,1)S(1)} %collective-permute-done.2), channel_id=1, source_target_pairs={{0,1},{1,0},{2,3},{3,2},{4,5},{5,4},{6,7},{7,6},{8,9},{9,8},{10,11... | collective-permute-start | bytes 700424 | tf_op jit(solution)/shard_map/ppermute | solution.py:712
  43.5 8.1 %collective-permute-start.12 = (bf16[48,2432]{1,0:T(8,128)(2,1)S(1)}, bf16[48,2432]{1,0:T(8,128)(2,1)S(1)}, u32[]{:S(2)}, u32[]{:S(2)}) collective-permute-start(bf16[48,2432]{1,0:T(8,128)(2,1)S(1)} %collective-permute-done.3), channel_id=1, source_target_pairs={{0,1},{1,0},{2,3},{3,2},{4,5},{5,4},{6,7},{7,6},{8,9},{9,8},{10,11... | collective-permute-start | bytes 700424 | tf_op jit(solution)/shard_map/ppermute | solution.py:712
  47.0 6.0 %collective-permute-start.14 = (bf16[48,2432]{1,0:T(8,128)(2,1)S(1)}, bf16[48,2432]{1,0:T(8,128)(2,1)S(1)}, u32[]{:S(2)}, u32[]{:S(2)}) collective-permute-start(bf16[48,2432]{1,0:T(8,128)(2,1)S(1)} %collective-permute-done.4), channel_id=1, source_target_pairs={{0,1},{1,0},{2,3},{3,2},{4,5},{5,4},{6,7},{7,6},{8,9},{9,8},{10,11... | collective-permute-start | bytes 700424 | tf_op jit(solution)/shard_map/ppermute | solution.py:712
  47.7 3.2 collective-permute-start.11
  48.9 3.4 %collective-permute-start.13 = (bf16[48,2432]{1,0:T(8,128)(2,1)S(1)}, bf16[48,2432]{1,0:T(8,128)(2,1)S(1)}, u32[]{:S(2)}, u32[]{:S(2)}) collective-permute-start(bf16[48,2432]{1,0:T(8,128)(2,1)S(1)} %collective-permute-done.6), channel_id=1, source_target_pairs={{0,1},{1,0},{2,3},{3,2},{4,5},{5,4},{6,7},{7,6},{8,9},{9,8},{10,11... | collective-permute-start | bytes 700424 | tf_op jit(solution)/shard_map/ppermute | solution.py:712
  49.7 4.1 %collective-permute-start.15 = (bf16[48,2432]{1,0:T(8,128)(2,1)S(1)}, bf16[48,2432]{1,0:T(8,128)(2,1)S(1)}, u32[]{:S(2)}, u32[]{:S(2)}) collective-permute-start(bf16[48,2432]{1,0:T(8,128)(2,1)S(1)} %collective-permute-done.7), channel_id=1, source_target_pairs={{0,1},{1,0},{2,3},{3,2},{4,5},{5,4},{6,7},{7,6},{8,9},{9,8},{10,11... | collective-permute-start | bytes 700424 | tf_op jit(solution)/shard_map/ppermute | solution.py:712
  58.7 40.7 %copy-start.16 = (bf16[128,768]{1,0:T(8,128)(2,1)}, bf16[128,768]{1,0:T(8,128)(2,1)S(1)}, u32[]{:S(2)}) copy-start(bf16[128,768]{1,0:T(8,128)(2,1)S(1)} %get-tuple-element.72.q_ref) | copy-start | bytes 589828
  58.7 4.8 %collective-permute-start.16 = (bf16[128,1536]{1,0:T(8,128)(2,1)S(1)}, bf16[128,1536]{1,0:T(8,128)(2,1)S(1)}, u32[]{:S(2)}, u32[]{:S(2)}) collective-permute-start(bf16[128,1536]{1,0:T(8,128)(2,1)S(1)} %get-tuple-element.73.own_ref), channel_id=1, source_target_pairs={{0,1},{1,2},{2,3},{3,4},{4,5},{5,6},{6,7},{7,8},{8,9},{9,10},{10,1... | collective-permute-start | bytes 1179656 | tf_op jit(solution)/shard_map/ppermute | solution.py:930
  60.9 3.6 %collective-permute-start.17 = (bf16[128,1536]{1,0:T(8,128)(2,1)S(1)}, bf16[128,1536]{1,0:T(8,128)(2,1)S(1)}, u32[]{:S(2)}, u32[]{:S(2)}) collective-permute-start(bf16[128,1536]{1,0:T(8,128)(2,1)S(1)} %get-tuple-element.73.own_ref), channel_id=1, source_target_pairs={{1,0},{2,1},{3,2},{4,3},{5,4},{6,5},{7,6},{8,7},{9,8},{10,9},{11,1... | collective-permute-start | bytes 1179656 | tf_op jit(solution)/shard_map/ppermute | solution.py:932
  63.5 44.3 %copy-start.27 = (f32[1,768]{1,0:T(1,128)}, f32[1,768]{1,0:T(1,128)S(1)}, u32[]{:S(2)}) copy-start(f32[1,768]{1,0:T(1,128)S(1)} %get-tuple-element.152.gain_ref) | copy-start | bytes 9220
  99.4 6.9 %collective-permute-start.18 = (bf16[64,768]{1,0:T(8,128)(2,1)}, bf16[64,768]{1,0:T(8,128)(2,1)S(1)}, u32[]{:S(2)}, u32[]{:S(2)}) collective-permute-start(bf16[64,768]{1,0:T(8,128)(2,1)} %get-tuple-element.76), channel_id=1, source_target_pairs={{0,16},{1,17},{2,18},{3,19},{4,20},{5,21},{6,22},{7,23},{8,24},{9,... | collective-permute-start | bytes 294920 | tf_op jit(solution)/shard_map/ppermute | solution.py:708
  102.9 4.9 %collective-permute-start.19 = (bf16[64,768]{1,0:T(8,128)(2,1)}, bf16[64,768]{1,0:T(8,128)(2,1)S(1)}, u32[]{:S(2)}, u32[]{:S(2)}) collective-permute-start(bf16[64,768]{1,0:T(8,128)(2,1)} %get-tuple-element.77), channel_id=1, source_target_pairs={{0,16},{1,17},{2,18},{3,19},{4,20},{5,21},{6,22},{7,23},{8,24},{9,... | collective-permute-start | bytes 294920 | tf_op jit(solution)/shard_map/ppermute | solution.py:708
  134.7 1.6 collective-permute-start.20
  161.2 13.3 %all-to-all-start.2 = ((bf16[16,48,128]{2,1,0:T(8,128)(2,1)}), bf16[16,48,128]{2,1,0:T(8,128)(2,1)}, u32[]{:S(2)}, u32[]{:S(2)}) async-start(bf16[16,48,128]{2,1,0:T(8,128)(2,1)} %get-tuple-element.85), calls=%async_computation.2 | async-start | bytes 393216 | tf_op jit(solution)/shard_map/all_to_all | solution.py:703
  181.8 1.6 collective-permute-start.21
  184.5 22.5 %all-to-all-start.3 = ((bf16[16,144,128]{2,1,0:T(8,128)(2,1)}), bf16[16,144,128]{2,1,0:T(8,128)(2,1)}, u32[]{:S(2)}, u32[]{:S(2)}) async-start(bf16[16,144,128]{2,1,0:T(8,128)(2,1)} %add_convert_fusion), calls=%async_computation.3 | async-start | bytes 1179648 | tf_op jit(solution)/shard_map/all_to_all | solution.py:703
  188.9 2.0 collective-permute-start.22
  189.2 12.6 %collective-permute-start.23 = (bf16[4,216,128]{2,1,0:T(8,128)(2,1)S(1)}, bf16[4,216,128]{2,1,0:T(8,128)(2,1)S(1)}, u32[]{:S(2)}, u32[]{:S(2)}) collective-permute-start(bf16[4,216,128]{2,1,0:T(8,128)(2,1)S(1)} %get-tuple-element.139), channel_id=1, source_target_pairs={{0,2},{1,3},{2,0},{3,1},{4,6},{5,7},{6,4},{7,5},{8,10},{9,11},{10,... | collective-permute-start | bytes 663560 | tf_op jit(solution)/shard_map/ppermute | solution.py:712
  190.9 16.2 %collective-permute-start.24 = (bf16[4,216,128]{2,1,0:T(8,128)(2,1)S(1)}, bf16[4,216,128]{2,1,0:T(8,128)(2,1)S(1)}, u32[]{:S(2)}, u32[]{:S(2)}) collective-permute-start(bf16[4,216,128]{2,1,0:T(8,128)(2,1)S(1)} %get-tuple-element.138), channel_id=1, source_target_pairs={{0,3},{1,2},{2,1},{3,0},{4,7},{5,6},{6,5},{7,4},{8,11},{9,10},{10,... | collective-permute-start | bytes 663560 | tf_op jit(solution)/shard_map/ppermute | solution.py:712
  211.8 7.7 %collective-permute-start.25 = (bf16[64,768]{1,0:T(8,128)(2,1)}, bf16[64,768]{1,0:T(8,128)(2,1)S(1)}, u32[]{:S(2)}, u32[]{:S(2)}) collective-permute-start(bf16[64,768]{1,0:T(8,128)(2,1)} %get-tuple-element.95), channel_id=1, source_target_pairs={{16,0},{17,1},{18,2},{19,3},{20,4},{21,5},{22,6},{23,7},{24,8},{25... | collective-permute-start | bytes 294920 | tf_op jit(solution)/shard_map/ppermute | solution.py:708
  213.1 7.9 %collective-permute-start.26 = (bf16[64,768]{1,0:T(8,128)(2,1)}, bf16[64,768]{1,0:T(8,128)(2,1)S(1)}, u32[]{:S(2)}, u32[]{:S(2)}) collective-permute-start(bf16[64,768]{1,0:T(8,128)(2,1)} %get-tuple-element.96), channel_id=1, source_target_pairs={{16,0},{17,1},{18,2},{19,3},{20,4},{21,5},{22,6},{23,7},{24,8},{25... | collective-permute-start | bytes 294920 | tf_op jit(solution)/shard_map/ppermute | solution.py:708
  221.1 8.0 %collective-permute-start.27 = (bf16[128,768]{1,0:T(8,128)(2,1)S(1)}, bf16[128,768]{1,0:T(8,128)(2,1)S(1)}, u32[]{:S(2)}, u32[]{:S(2)}) collective-permute-start(bf16[128,768]{1,0:T(8,128)(2,1)S(1)} %pad_maximum_fusion.2.refs_0_), channel_id=1, source_target_pairs={{0,2},{1,3},{2,0},{3,1},{4,6},{5,7},{6,4},{7,5},{8,10},{9,11},{10,... | collective-permute-start | bytes 589832 | tf_op jit(solution)/shard_map/ppermute | solution.py:712
  229.1 24.0 %collective-permute-start.34 = (bf16[128,3072]{1,0:T(8,128)(2,1)S(1)}, bf16[128,3072]{1,0:T(8,128)(2,1)S(1)}, u32[]{:S(2)}, u32[]{:S(2)}) collective-permute-start(bf16[128,3072]{1,0:T(8,128)(2,1)S(1)} %get-tuple-element.121.refs_0_), channel_id=1, source_target_pairs={{0,2},{1,3},{2,0},{3,1},{4,6},{5,7},{6,4},{7,5},{8,10},{9,11},{10,... | collective-permute-start | bytes 2359304 | tf_op jit(solution)/shard_map/ppermute | solution.py:712
  230.8 1.4 collective-permute-start.29
  230.8 1.7 collective-permute-start.30
  233.0 9.5 %collective-permute-start.31 = (bf16[144,768]{1,0:T(8,128)(2,1)S(1)}, bf16[144,768]{1,0:T(8,128)(2,1)S(1)}, u32[]{:S(2)}, u32[]{:S(2)}) collective-permute-start(bf16[144,768]{1,0:T(8,128)(2,1)S(1)} %get-tuple-element.110), channel_id=1, source_target_pairs={{0,4},{1,5},{2,6},{3,7},{4,0},{5,1},{6,2},{7,3},{8,12},{9,13},{10,... | collective-permute-start | bytes 663560 | tf_op jit(solution)/shard_map/ppermute | solution.py:712
  238.1 4.4 %collective-permute-start.28 = (bf16[128,1536]{1,0:T(8,128)(2,1)S(1)}, bf16[128,1536]{1,0:T(8,128)(2,1)S(1)}, u32[]{:S(2)}, u32[]{:S(2)}) collective-permute-start(bf16[128,1536]{1,0:T(8,128)(2,1)S(1)} %get-tuple-element.103), channel_id=1, source_target_pairs={{1,0},{2,1},{3,2},{4,3},{5,4},{6,5},{7,6},{8,7},{9,8},{10,9},{11,1... | collective-permute-start | bytes 1179656 | tf_op jit(solution)/shard_map/ppermute | solution.py:1092
  239.4 4.4 %collective-permute-start.32 = (bf16[128,1536]{1,0:T(8,128)(2,1)S(1)}, bf16[128,1536]{1,0:T(8,128)(2,1)S(1)}, u32[]{:S(2)}, u32[]{:S(2)}) collective-permute-start(bf16[128,1536]{1,0:T(8,128)(2,1)S(1)} %get-tuple-element.112), channel_id=1, source_target_pairs={{0,1},{1,2},{2,3},{3,4},{4,5},{5,6},{6,7},{7,8},{8,9},{9,10},{10,1... | collective-permute-start | bytes 1179656 | tf_op jit(solution)/shard_map/ppermute | solution.py:1093
  253.1 8.6 %collective-permute-start.35 = (bf16[128,3072]{1,0:T(8,128)(2,1)S(1)}, bf16[128,3072]{1,0:T(8,128)(2,1)S(1)}, u32[]{:S(2)}, u32[]{:S(2)}) collective-permute-start(bf16[128,3072]{1,0:T(8,128)(2,1)S(1)} %get-tuple-element.121.refs_0_), channel_id=1, source_target_pairs={{0,1},{1,0},{2,3},{3,2},{4,5},{5,4},{6,7},{7,6},{8,9},{9,8},{10,11... | collective-permute-start | bytes 2359304 | tf_op jit(solution)/shard_map/ppermute | solution.py:712
  259.7 3.0 collective-permute-start.36
  263.6 16.0 %collective-permute-start.37 = (bf16[384,768]{1,0:T(8,128)(2,1)S(1)}, bf16[384,768]{1,0:T(8,128)(2,1)S(1)}, u32[]{:S(2)}, u32[]{:S(2)}) collective-permute-start(bf16[384,768]{1,0:T(8,128)(2,1)S(1)} %get-tuple-element.124), channel_id=1, source_target_pairs={{0,4},{1,5},{2,6},{3,7},{4,0},{5,1},{6,2},{7,3},{8,12},{9,13},{10,... | collective-permute-start | bytes 1769480 | tf_op jit(solution)/shard_map/ppermute | solution.py:712
  265.7 17.1 %collective-permute-start.33 = (bf16[144,2304]{1,0:T(8,128)(2,1)S(1)}, bf16[144,2304]{1,0:T(8,128)(2,1)S(1)}, u32[]{:S(2)}, u32[]{:S(2)}) collective-permute-start(bf16[144,2304]{1,0:T(8,128)(2,1)S(1)} %get-tuple-element.126.refs_0_), channel_id=1, source_target_pairs={{0,2},{1,3},{2,0},{3,1},{4,6},{5,7},{6,4},{7,5},{8,10},{9,11},{10,... | collective-permute-start | bytes 1990664 | tf_op jit(solution)/shard_map/ppermute | solution.py:712
  282.8 4.3 %collective-permute-start.38 = (bf16[144,2304]{1,0:T(8,128)(2,1)S(1)}, bf16[144,2304]{1,0:T(8,128)(2,1)S(1)}, u32[]{:S(2)}, u32[]{:S(2)}) collective-permute-start(bf16[144,2304]{1,0:T(8,128)(2,1)S(1)} %get-tuple-element.126.refs_0_), channel_id=1, source_target_pairs={{0,1},{1,0},{2,3},{3,2},{4,5},{5,4},{6,7},{7,6},{8,9},{9,8},{10,11... | collective-permute-start | bytes 1990664 | tf_op jit(solution)/shard_map/ppermute | solution.py:712
  282.8 4.3 %collective-permute-start.39 = (bf16[144,2304]{1,0:T(8,128)(2,1)S(1)}, bf16[144,2304]{1,0:T(8,128)(2,1)S(1)}, u32[]{:S(2)}, u32[]{:S(2)}) collective-permute-start(bf16[144,2304]{1,0:T(8,128)(2,1)S(1)} %collective-permute-done.33.refs_2_), channel_id=1, source_target_pairs={{0,1},{1,0},{2,3},{3,2},{4,5},{5,4},{6,7},{7,6},{8,9},{9,8},{10,11... | collective-permute-start | bytes 1990664 | tf_op jit(solution)/shard_map/ppermute | solution.py:712
  283.3 21.0 %collective-permute-start.42 = (bf16[264,768]{1,0:T(8,128)(2,1)S(1)}, bf16[264,768]{1,0:T(8,128)(2,1)S(1)}, u32[]{:S(2)}, u32[]{:S(2)}) collective-permute-start(bf16[264,768]{1,0:T(8,128)(2,1)S(1)} %pad_maximum_fusion), channel_id=1, source_target_pairs={{0,8},{1,9},{2,10},{3,11},{4,12},{5,13},{6,14},{7,15},{8,0},{9,1},... | collective-permute-start | bytes 1216520 | tf_op jit(solution)/shard_map/ppermute | solution.py:712
  287.8 21.0 %collective-permute-start.40 = (bf16[96,2432]{1,0:T(8,128)(2,1)S(1)}, bf16[96,2432]{1,0:T(8,128)(2,1)S(1)}, u32[]{:S(2)}, u32[]{:S(2)}) collective-permute-start(bf16[96,2432]{1,0:T(8,128)(2,1)S(1)} %get-tuple-element.129), channel_id=1, source_target_pairs={{0,4},{1,5},{2,6},{3,7},{4,0},{5,1},{6,2},{7,3},{8,12},{9,13},{10,... | collective-permute-start | bytes 1400840 | tf_op jit(solution)/shard_map/ppermute | solution.py:712
  308.8 11.4 %collective-permute-start.41 = (bf16[48,2432]{1,0:T(8,128)(2,1)S(1)}, bf16[48,2432]{1,0:T(8,128)(2,1)S(1)}, u32[]{:S(2)}, u32[]{:S(2)}) collective-permute-start(bf16[48,2432]{1,0:T(8,128)(2,1)S(1)} %add_convert_fusion.2), channel_id=1, source_target_pairs={{0,8},{1,9},{2,10},{3,11},{4,12},{5,13},{6,14},{7,15},{8,0},{9,1},... | collective-permute-start | bytes 700424 | tf_op jit(solution)/shard_map/ppermute | solution.py:712
  (37 other events, 710.5 us)
Sparse Core Ops, SparseCore 0:
  20.8 73.0 all-gather.1
